TPU v7x, 32 devices: a whole 2x2x4 slice. The times are simulated.
32 devices in a mesh: groups: 2 (over x), replica: 8 (over z, y), tensor: 2 (over core).
Axes of the slice: x: 2, y: 2, z: 4, core: 2. Of those that a mesh axis runs over, the one named last changes fastest.
Arguments:
- normed_input_rows: bfloat16 [8192, 8192], P(('groups', 'replica'), 'tensor'), parts along dimension 0, may hold values from -6 to 6
- key_value_weight: bfloat16 [8192, 2048], P('tensor'), may hold values from -0.0625 to 0.0625
- lowrank_left_pieces: bfloat16 [48, 8192, 64], P('replica', 'tensor'), may hold values from -0.0625 to 0.0625
- adapter_up_factors: bfloat16 [48, 64, 2048], P('replica', None, 'tensor'), may hold values from -0.75 to 0.75
- segment_adapter_ids: int32 [256], P(('groups', 'replica')), parts along dimension 0, may hold values from 0 to 47, as said below
- residency: int32 [48], replicated, may hold values from 0 to 47, as said below
Outputs:
- projected: bfloat16 [8192, 2048], P(('groups', 'replica'), 'tensor'), parts along dimension 0
There are 2 independent parts, one for each index of `groups`. A program takes and returns all parts, laid end to end along the dimension named above; an argument that names none is the same for every part. Nothing has to cross between parts.
Inputs may be any that keep to these rules, and one draw needn't show every extreme that they name: `segment_adapter_ids`: among the 16 segments of one replica (aligned blocks of 16 entries), at most 2 name adapters with the same value of id // 6; in every draw some value of id // 6 is named by exactly 2 segments of every replica. A permutation; residency[a] // 6 equals a // 6.
All inputs are finite; a program needn't handle non-finite values.
Results may differ from a plain program's by a relative error of at most 0.005.
Values may be sent and summed in bfloat16 or wider, within the bound.
No kernel may reach another device: no remote copies, remote signals or barrier semaphores. Data moves between devices by JAX's collectives and lax.ppermute only.
A program may use at most 192 MiB of HBM per device.

v0:
```python
import jax
import jax.numpy as jnp
from jax import lax
from jax.sharding import PartitionSpec as P

CAP = 2
SEG = 32


def order_in_holder(seg_ids, each_owner):
    holder = seg_ids // each_owner
    seg_total = seg_ids.shape[-1]
    same_holder = holder[..., :, None] == holder[..., None, :]
    before = jnp.arange(seg_total)[None, :] < jnp.arange(seg_total)[:, None]
    position = jnp.sum(same_holder & before, axis=-1)
    return (holder, position)


def on_device(
    normed_input_rows,
    key_value_weight,
    lowrank_left_pieces,
    adapter_up_factors,
    segment_adapter_ids,
    residency,
):
    replicas = lax.axis_size("replica")
    my_index = lax.axis_index("replica")
    each_owner = lowrank_left_pieces.shape[0]
    partition_number = segment_adapter_ids.shape[0]
    midpoint_feature_count = normed_input_rows.shape[1]
    half_output = adapter_up_factors.shape[2]
    slot_count = replicas * CAP
    seg_table = lax.all_gather(segment_adapter_ids, "replica", axis=0, tiled=True).reshape(
        replicas, partition_number
    )
    holder_mine, position_mine = order_in_holder(segment_adapter_ids, each_owner)
    target = holder_mine * CAP + position_mine
    picker_matrix = (target[None, :] == jnp.arange(slot_count)[:, None]).astype(jnp.bfloat16)
    holder_all, position_all = order_in_holder(seg_table, each_owner)
    matched = (holder_all[:, None, :] == my_index) & (
        position_all[:, None, :] == jnp.arange(CAP)[None, :, None]
    )
    wanted = jnp.sum(jnp.where(matched, seg_table[:, None, :], 0), axis=-1)
    available_flag = jnp.any(matched, axis=-1)
    hit_table = wanted[..., None] == jnp.arange(residency.shape[0])
    stored = jnp.sum(jnp.where(hit_table, residency, 0), axis=-1) - my_index * each_owner
    responsible_device = (
        available_flag[..., None] & (stored[..., None] == jnp.arange(each_owner))
    ).astype(jnp.bfloat16)
    down_blocks = jnp.einsum(
        "yop,paf->yoaf", responsible_device, lowrank_left_pieces, preferred_element_type=jnp.float32
    ).astype(jnp.bfloat16)
    up_blocks = jnp.einsum(
        "mdy,ysb->mdsb", responsible_device, adapter_up_factors, preferred_element_type=jnp.float32
    ).astype(jnp.bfloat16)
    partial_value = jnp.dot(normed_input_rows, key_value_weight, preferred_element_type=jnp.float32)
    base_sum = lax.psum_scatter(partial_value, "tensor", scatter_dimension=1, tiled=True)
    blocked_rows = normed_input_rows.reshape(partition_number, SEG, midpoint_feature_count)
    outgoing = jnp.einsum(
        "cf,fxv->cxv", picker_matrix, blocked_rows, preferred_element_type=jnp.float32
    ).astype(jnp.bfloat16)
    outgoing = outgoing.reshape(replicas, CAP, SEG, midpoint_feature_count)
    arrived = lax.all_to_all(outgoing, "replica", split_axis=0, concat_axis=0, tiled=True)
    rank_reduced = jnp.einsum(
        "qcld,qcdr->qclr", arrived, down_blocks, preferred_element_type=jnp.float32
    )
    rank_reduced = lax.psum(rank_reduced, "tensor").astype(jnp.bfloat16)
    adapter_delta = jnp.einsum(
        "qclr,qcrv->qclv", rank_reduced, up_blocks, preferred_element_type=jnp.float32
    ).astype(jnp.bfloat16)
    gathered_result = lax.all_to_all(
        adapter_delta, "replica", split_axis=0, concat_axis=0, tiled=True
    )
    placed = jnp.einsum(
        "ps,plv->slv",
        picker_matrix,
        gathered_result.reshape(slot_count, SEG, half_output),
        preferred_element_type=jnp.float32,
    ).astype(jnp.bfloat16)
    placed = lax.optimization_barrier(placed)
    return (
        base_sum + placed.reshape(partition_number * SEG, half_output).astype(jnp.float32)
    ).astype(jnp.bfloat16)


def solution(mesh):
    placed = (
        P(("groups", "replica"), "tensor"),
        P("tensor", None),
        P("replica", "tensor", None),
        P("replica", None, "tensor"),
        P(("groups", "replica")),
        P(),
    )
    return jax.shard_map(
        on_device,
        mesh=mesh,
        in_specs=placed,
        out_specs=P(("groups", "replica"), "tensor"),
        check_vma=False,
    )
```

profile of v0, /device:TPU:0, one launch (start us, length us, event | category | flops | bytes accessed | tf_op | source)
XLA Modules:
  0.0 209.4 jit_solution(5790531606146346983)
XLA Ops:
  6.5 0.7 and_select_fusion
  7.2 0.2 convert_reduce_fusion.1
  7.4 0.7 multiply_add_fusion
  8.1 9.0 %convolution_convert_fusion.1 = bf16[16,32,4096]{2,0,1:T(8,128)(2,1)} fusion(bf16[16,32,4096]{2,1,0:T(8,128)(2,1)} %bitcast.30, s32[16]{0:T(128)S(1)} %multiply_add_fusion), kind=kOutput, calls=%fused_computation.3 | convolution fusion | flops 69206272 | bytes 8388672 | tf_op jit(solution)/shard_map/cf,fxv->cxv/dot_general | solution.py:60
  17.0 7.6 %reshape.83 = bf16[8,2,32,4096]{3,1,0,2:T(2,128)(2,1)} reshape(bf16[16,32,4096]{2,0,1:T(8,128)(2,1)} %convolution_convert_fusion.1) | data formatting | bytes 8388608 | tf_op jit(solution)/shard_map/reshape | solution.py:63
  24.6 9.9 %copy.18 = bf16[8,2,32,4096]{3,1,2,0:T(2,128)(2,1)} copy(bf16[8,2,32,4096]{3,1,0,2:T(2,128)(2,1)} %reshape.83) | data formatting | bytes 8388608 | tf_op jit(solution)/shard_map/reshape | solution.py:63
  34.6 7.3 %all-to-all-start = ((bf16[8,2,32,4096]{3,1,2,0:T(2,128)(2,1)}), bf16[8,2,32,4096]{3,1,2,0:T(2,128)(2,1)}, u32[]{:S(2)}, u32[]{:S(2)}) async-start(bf16[8,2,32,4096]{3,1,2,0:T(2,128)(2,1)} %copy.18), calls=%async_computation.1 | async-start | bytes 8388608 | tf_op jit(solution)/shard_map/all_to_all | solution.py:64
  41.8 0.2 reduce-scatter.2.cloned.1.call-start
  42.1 14.9 %fusion.32 = f32[512,2048]{1,0:T(8,128)} fusion(bf16[512,4096]{1,0:T(8,128)(2,1)} %param.6, bf16[4096,2048]{1,0:T(8,128)(2,1)} %param.7), kind=kOutput, calls=%fused_computation.47 | convolution fusion | flops 8589934592 | bytes 25165824 | tf_op jit(solution)/shard_map/dot_general | solution.py:57
  57.1 0.6 copy-done.3
  57.7 0.6 dynamic-slice
  58.9 0.2 dynamic-update-slice
  59.2 76.1 %all-reduce = s32[128]{0:T(128)S(1)} all-reduce(s32[128]{0:T(128)S(1)} %dynamic-update-slice), channel_id=1, replica_groups=mesh['groups'=2,'replica'=8,'tensor'=2] {'replica'}, use_global_device_ids=true, to_apply=%add | all-reduce | flops 128 | bytes 1024
  135.4 0.3 convert_reduce_fusion
  136.0 0.2 select_reduce_fusion
  136.2 0.8 convolution_convert_fusion.2
  137.0 9.0 %convolution_convert_fusion = bf16[8,2,4096,64]{2,0,3,1:T(8,128)(2,1)} fusion(bf16[6,4096,64]{1,2,0:T(8,128)(2,1)} %param.8, s32[8,2]{0,1:T(2,128)S(1)} %broadcast_subtract_fusion, pred[8,2]{0,1:T(4,128)(4,1)S(1)} %fusion.20), kind=kOutput, calls=%fused_computation.2 | convolution fusion | flops 54526144 | bytes 11534416 | tf_op jit(solution)/shard_map/yop,paf->yoaf/dot_general | solution.py:51
  146.0 15.8 %fusion = f32[8,2,32,64]{3,2,1,0:T(8,128)S(1)} fusion(bf16[8,2,4096,64]{2,0,3,1:T(8,128)(2,1)} %convolution_convert_fusion, bf16[8,2,32,4096]{3,1,2,0:T(2,128)(2,1)} %all-to-all-done), kind=kOutput, calls=%fused_computation | convolution fusion | flops 268435456 | bytes 12713984 | tf_op jit(solution)/shard_map/qcld,qcdr->qclr/dot_general | solution.py:65
  161.8 4.2 %all-reduce.2 = bf16[8,2,32,64]{3,2,1,0:T(8,128)(2,1)S(1)} all-reduce(f32[8,2,32,64]{3,2,1,0:T(8,128)S(1)} %fusion), channel_id=1, replica_groups=mesh['groups'=2,'replica'=8,'tensor'=2] {'tensor'}, use_global_device_ids=true, to_apply=%region_6.7 | all-reduce | flops 32768 | bytes 196608 | tf_op jit(solution)/shard_map/psum | solution.py:68
  166.0 2.6 %fusion.9 = bf16[8,2,32,1024]{3,2,1,0:T(8,128)(2,1)S(1)} fusion(bf16[8,2,64,1024]{3,0,2,1:T(8,128)(2,1)S(1)} %convolution_convert_fusion.2, bf16[8,2,32,64]{3,2,1,0:T(8,128)(2,1)S(1)} %all-reduce.2), kind=kOutput, calls=%fused_computation.13 | convolution fusion | flops 67633152 | bytes 3211264 | tf_op jit(solution)/shard_map/qclr,qcrv->qclv/dot_general | solution.py:69
  168.6 29.7 %all_to_all.10 = bf16[8,2,32,1024]{3,2,1,0:T(8,128)(2,1)S(1)} all-to-all(bf16[8,2,32,1024]{3,2,1,0:T(8,128)(2,1)S(1)} %fusion.9), channel_id=1, replica_groups=mesh['groups'=2,'replica'=8,'tensor'=2] {'replica'}, dimensions={0} | all-to-all | bytes 2097152 | tf_op jit(solution)/shard_map/all_to_all | solution.py:72
  198.3 0.8 convolution_convert_fusion.3
  199.1 0.6 copy.25
  199.7 2.9 %fusion.6 = bf16[512,1024]{1,0:T(8,128)(2,1)} fusion(f32[512,1024]{1,0:T(8,128)} %reduce-scatter.2.cloned.1.call-done, f32[16,32,1024]{2,1,0:T(8,128)S(1)} %copy.25), kind=kLoop, calls=%fused_computation.9 | loop fusion | flops 1048576 | bytes 5242880 | tf_op jit(solution)/shard_map/convert_element_type | solution.py:84
  (17 shorter events, 0.5 us)
Async XLA Ops:
  34.6 111.4 %all-to-all-start = ((bf16[8,2,32,4096]{3,1,2,0:T(2,128)(2,1)}), bf16[8,2,32,4096]{3,1,2,0:T(2,128)(2,1)}, u32[]{:S(2)}, u32[]{:S(2)}) async-start(bf16[8,2,32,4096]{3,1,2,0:T(2,128)(2,1)} %copy.18), calls=%async_computation.1 | async-start | bytes 8388608 | tf_op jit(solution)/shard_map/all_to_all | solution.py:64
  41.8 157.9 %reduce-scatter.2.cloned.1.call-start = ((), (), s32[]{:S(2)}) async-start(), calls=%async_computation.3 | async-start | bytes 6291456 | tf_op jit(solution)/shard_map/reduce_scatter | solution.py:58
  57.0 0.7 copy-start.3
  57.0 1.9 copy-start.2
  57.0 79.0 %copy-start.1 = (s32[48]{0:T(128)S(1)}, s32[48]{0:T(128)}, u32[]{:S(2)}) copy-start(s32[48]{0:T(128)} %param.11) | copy-start | bytes 580
  57.0 79.2 %copy-start = (bf16[6,64,1024]{2,1,0:T(8,128)(2,1)S(1)}, bf16[6,64,1024]{2,1,0:T(8,128)(2,1)}, u32[]{:S(2)}) copy-start(bf16[6,64,1024]{2,1,0:T(8,128)(2,1)} %param.9) | copy-start | bytes 2359300
Sparse Core Ops, SparseCore 0:
  57.2 13.2 reduce-scatter.1
where the time goes:
time: 210 us; the launch traced here: 209 us
  blocking collectives  110 us (52%)
  matrix products  52.9 us (25%)
  local copies, waits for them, and re-layouts  19.7 us (9%)
  between operations  14.2 us (7%)
  starting transfers between devices  7.5 us (4%)
  other arithmetic  5.21 us (2%)
    unnamed x1, blocking collectives  76.1 us
    all_to_all x1, blocking collectives, on_device(): lax.all_to_all(adapter_delta, 'replica', split_axis=0, concat_axis=0, til...  29.7 us
    reshape x2, local copies, waits for them, and re-layouts, on_device(): outgoing = outgoing.reshape(replicas, CAP, SEG, midpoint_feature_count)  17.6 us
    dot_general x1, matrix products, on_device(): jnp.einsum('qcld,qcdr->qclr', arrived, down_blocks, preferred_element_typ...  15.8 us
    dot_general x1, matrix products, on_device(): jnp.dot(normed_input_rows, key_value_weight, preferred_element_type=jnp.f...  14.9 us
    dot_general x1, matrix products, on_device(): jnp.einsum('yop,paf->yoaf', responsible_device, lowrank_left_pieces, pref...  8.99 us
    dot_general x1, matrix products, on_device(): jnp.einsum('cf,fxv->cxv', picker_matrix, blocked_rows, preferred_element_...  8.95 us
    all_to_all x1, starting transfers between devices, on_device(): lax.all_to_all(outgoing, 'replica', split_axis=0, concat_axis=0, tiled=True)  7.28 us
  transfers between devices with their start and end apart: 2, of which 0 were waited for; matrix products, arithmetic and copies ran while one was open for 22% of the time, Pallas kernels for 0%

commit v1 on v0

v1 whole, which is shorter than its diff:
```python
import functools

import jax
import jax.numpy as jnp
from jax import lax
from jax.experimental import pallas as pl
from jax.experimental.pallas import tpu as pltpu
from jax.sharding import PartitionSpec as P

CAP = 2
SEG = 32
LANES = 128
VMEM_LIMIT = 40 * 1024 * 1024
ANY = pl.BlockSpec(memory_space=pl.ANY)
SMEM = pl.BlockSpec(memory_space=pltpu.SMEM)


def params():
    return pltpu.CompilerParams(vmem_limit_bytes=VMEM_LIMIT)


def pick_kernel(count, seg_ref, x_ref, *rest):
    outs, sems = rest[:-1], rest[-1]
    copies = []
    for k in range(count):
        out, part = outs[k // CAP], k % CAP
        source = x_ref.at[pl.ds(pl.multiple_of(seg_ref[k] * SEG, SEG), SEG)]
        copies.append(
            pltpu.make_async_copy(source, out.at[pl.ds(part * SEG, SEG)], sems.at[k])
        )
    for copy in copies:
        copy.start()
    for copy in copies:
        copy.wait()


def pick_rows(seg_of, x):
    count = seg_of.shape[0]
    width = x.shape[1]
    return pl.pallas_call(
        functools.partial(pick_kernel, count),
        out_shape=[jax.ShapeDtypeStruct((CAP * SEG, width), x.dtype)] * (count // CAP),
        in_specs=[SMEM, ANY],
        out_specs=[ANY] * (count // CAP),
        scratch_shapes=[pltpu.SemaphoreType.DMA((count,))],
        compiler_params=params(),
        cost_estimate=pl.CostEstimate(
            flops=0, bytes_accessed=count * SEG * width * 4, transcendentals=0
        ),
        name="pick_rows",
    )(seg_of, x)


def slot_mask(slot, shape, first, slots, share, pieces):
    column = first + lax.broadcasted_iota(jnp.int32, shape, 1)
    mask = None
    for e in range(pieces):
        low = e * slots * share + slot * share
        here = (column >= low) & (column < low + share)
        mask = here if mask is None else mask | here
    return mask


def reduce_kernel(n_rows, n_left, slots, share, pieces, *refs):
    slot_ref = refs[0]
    rows = refs[1 : 1 + n_rows]
    lefts = refs[1 + n_rows : 1 + n_rows + n_left]
    out_ref, acc = refs[-2:]
    step = pl.program_id(0)
    rows_block = jnp.concatenate([ref[...] for ref in rows], axis=0)
    left_block = jnp.concatenate([ref[...] for ref in lefts], axis=0)
    product = lax.dot_general(
        rows_block, left_block, (((1,), (1,)), ((), ())), preferred_element_type=jnp.float32
    )

    @pl.when(step == 0)
    def _():
        acc[...] = product

    @pl.when(step > 0)
    def _():
        acc[...] += product

    @pl.when(step == pl.num_programs(0) - 1)
    def _():
        for i in range(n_rows * CAP):
            span = slice(i * SEG, (i + 1) * SEG)
            total = jnp.zeros((SEG, LANES), jnp.float32)
            for first in range(0, acc.shape[1], LANES):
                mask = slot_mask(slot_ref[i], (SEG, LANES), first, slots, share, pieces)
                total += jnp.where(mask, acc[span, first : first + LANES], 0.0)
            out_ref[span, :] = total


def reduce_rank(slot, rows, lefts, slots, share, name):
    width = rows[0].shape[1]
    block = min(width, 1024)
    height = len(rows) * CAP * SEG
    columns = sum(left.shape[0] for left in lefts)
    pieces = columns // (slots * share)
    specs = [pl.BlockSpec((ref.shape[0], block), lambda k: (0, k)) for ref in (*rows, *lefts)]
    return pl.pallas_call(
        functools.partial(reduce_kernel, len(rows), len(lefts), slots, share, pieces),
        grid=(width // block,),
        out_shape=jax.ShapeDtypeStruct((height, LANES), jnp.float32),
        in_specs=[SMEM, *specs],
        out_specs=pl.BlockSpec((height, LANES), lambda k: (0, 0)),
        scratch_shapes=[pltpu.VMEM((height, columns), jnp.float32)],
        compiler_params=params(),
        cost_estimate=pl.CostEstimate(
            flops=2 * height * width * columns,
            bytes_accessed=2 * width * (height + columns),
            transcendentals=0,
        ),
        name=name,
    )(slot, *rows, *lefts)


def expand_kernel(n_up, slots, share, pieces, slot_ref, mine_ref, other_ref, *refs):
    ups, outs = refs[:n_up], refs[n_up:]
    up = jnp.concatenate([ref[...] for ref in ups], axis=0)
    low = (mine_ref[...] + other_ref[...]).astype(jnp.bfloat16)
    spread = []
    for i in range(low.shape[0] // SEG):
        part = low[i * SEG : (i + 1) * SEG]
        blocks = [
            jnp.where(slot_mask(slot_ref[i], part.shape, first, slots, share, pieces), part, 0)
            for first in range(0, up.shape[0], LANES)
        ]
        spread.append(jnp.concatenate(blocks, axis=1))
    delta = jnp.dot(
        jnp.concatenate(spread, axis=0), up, preferred_element_type=jnp.float32
    ).astype(jnp.bfloat16)
    for i, out in enumerate(outs):
        out[...] = delta[i * CAP * SEG : (i + 1) * CAP * SEG]


def expand_rank(slot, mine, other, ups, slots, share, name):
    features = ups[0].shape[1]
    columns = sum(up.shape[0] for up in ups)
    pieces = columns // (slots * share)
    count = mine.shape[0] // (CAP * SEG)
    whole = pl.BlockSpec(memory_space=pltpu.VMEM)
    return pl.pallas_call(
        functools.partial(expand_kernel, len(ups), slots, share, pieces),
        out_shape=[jax.ShapeDtypeStruct((CAP * SEG, features), jnp.bfloat16)] * count,
        in_specs=[SMEM, whole, whole] + [whole] * len(ups),
        out_specs=[whole] * count,
        compiler_params=params(),
        cost_estimate=pl.CostEstimate(
            flops=2 * mine.shape[0] * columns * features,
            bytes_accessed=2 * features * (columns + mine.shape[0]) + 8 * mine.size,
            transcendentals=0,
        ),
        name=name,
    )(slot, mine, other, *ups)


def join_kernel(seg_ref, valid_ref, mine_ref, other_ref, *refs):
    deltas, out_ref = refs[:-1], refs[-1]
    for k in range(len(deltas) * CAP):
        part = k % CAP

        @pl.when(valid_ref[k] > 0)
        def _():
            span = pl.ds(pl.multiple_of(seg_ref[k] * SEG, SEG), SEG)
            base = mine_ref[span, :] + other_ref[span, :]
            delta = deltas[k // CAP][part * SEG : (part + 1) * SEG, :]
            out_ref[span, :] = (base + delta.astype(jnp.float32)).astype(out_ref.dtype)


def join(seg_of, valid, mine, other, deltas):
    height, features = mine.shape
    block = min(features, 256)
    tall = pl.BlockSpec((height, block), lambda j: (0, j))
    short = pl.BlockSpec((CAP * SEG, block), lambda j: (0, j))
    return pl.pallas_call(
        join_kernel,
        grid=(features // block,),
        out_shape=jax.ShapeDtypeStruct((height, features), jnp.bfloat16),
        in_specs=[SMEM, SMEM, tall, tall] + [short] * len(deltas),
        out_specs=tall,
        compiler_params=params(),
        cost_estimate=pl.CostEstimate(
            flops=2 * height * features, bytes_accessed=12 * height * features, transcendentals=0
        ),
        name="join",
    )(seg_of, valid, mine, other, *deltas)


def swap(value, axis, distance):
    count = lax.axis_size(axis)
    return lax.ppermute(value, axis, [(i, i ^ distance) for i in range(count)])


def on_device(x, weight, lefts, ups, ids, residency):
    replicas = lax.axis_size("replica")
    groups = lax.axis_size("groups")
    half = replicas // 2
    me = lax.axis_index("replica")
    group = lax.axis_index("groups")
    core = lax.axis_index("tensor")
    slots, _, rank = lefts.shape
    share = rank // groups
    width = x.shape[1]
    features = ups.shape[2]

    segs = ids.shape[0]
    holder = ids // slots
    earlier = jnp.arange(segs)[None, :] < jnp.arange(segs)[:, None]
    position = jnp.sum((holder[:, None] == holder[None, :]) & earlier, axis=1)
    stored = jnp.sum(
        jnp.where(ids[:, None] == jnp.arange(residency.shape[0])[None, :], residency[None, :], 0),
        axis=1,
    )
    stored = stored - holder * slots
    offset = jnp.arange(half)
    wanted = jnp.stack([me ^ offset, me ^ offset ^ half])
    match = (holder == wanted[..., None, None]) & (
        position == jnp.arange(CAP)[None, None, :, None]
    )
    seg_of = jnp.sum(jnp.where(match, jnp.arange(segs), 0), axis=-1).astype(jnp.int32)
    slot_of = jnp.sum(jnp.where(match, stored, 0), axis=-1).astype(jnp.int32)
    valid = jnp.any(match, axis=-1).astype(jnp.int32).reshape(-1)
    slot_in = [slot_of[:, 0]] + [swap(slot_of[:, d], "replica", d) for d in range(1, half)]
    slot_in = jnp.stack(slot_in, axis=1).reshape(2, half * CAP)

    left_rows = jnp.swapaxes(lefts, 1, 2)
    left_share = lax.dynamic_slice(left_rows, (0, group * share, 0), (slots, share, width))
    up_share = lax.dynamic_slice(ups, (0, group * share, 0), (slots, share, features))
    chunk = 2
    left_in = [
        swap(left_share[c : c + chunk].reshape(chunk * share, width), "replica", half)
        for c in range(0, slots, chunk)
    ]
    up_in = swap(up_share.reshape(slots * share, features), "replica", half)
    left_all = list(left_in)
    up_all = [up_in]
    for e in range(1, groups):
        left_all += [swap(piece, "groups", e) for piece in left_in]
        up_all.append(swap(up_in, "groups", e))

    picked = pick_rows(seg_of.reshape(-1), x)
    rows_in = [
        [picked[kind * half]]
        + [swap(picked[kind * half + d], "replica", d) for d in range(1, half)]
        for kind in range(2)
    ]

    def part(which):
        columns = lax.dynamic_slice(weight, (0, which * features), (weight.shape[0], features))
        return jnp.dot(x, columns, preferred_element_type=jnp.float32)

    base_other = swap(part(1 - core), "tensor", 1)
    base_mine = part(core)

    own_left = [left_rows.reshape(slots * rank, width)]
    own_up = [ups.reshape(slots * rank, features)]
    deltas = []
    for kind, (left, up, held, name) in enumerate(
        [(own_left, own_up, rank, "own"), (left_all, up_all, share, "taken")]
    ):
        low = reduce_rank(slot_in[kind], rows_in[kind], left, slots, held, "reduce_" + name)
        other = swap(low, "tensor", 1)
        terms = expand_rank(slot_in[kind], low, other, up, slots, held, "expand_" + name)
        deltas.append(terms[0])
        deltas += [swap(terms[d], "replica", d) for d in range(1, half)]
    return join(seg_of.reshape(-1), valid, base_mine, base_other, deltas)


def solution(mesh):
    placed = (
        P(("groups", "replica"), "tensor"),
        P("tensor", None),
        P("replica", "tensor", None),
        P("replica", None, "tensor"),
        P(("groups", "replica")),
        P(),
    )
    return jax.shard_map(
        on_device,
        mesh=mesh,
        in_specs=placed,
        out_specs=P(("groups", "replica"), "tensor"),
        check_vma=False,
    )
```

time: 210 us -> 189 us (0.900)
  blocking collectives: 110 us -> 0 us
  waiting for transfers between devices: 0.04 us -> 103 us
  matrix products: 52.9 us -> 18.7 us
  starting transfers between devices: 7.5 us -> 31.1 us
  Pallas kernels: 0 us -> 17.2 us
  between operations: 14.2 us -> 0.21 us
  local copies, waits for them, and re-layouts: 19.7 us -> 16.2 us
  other arithmetic: 5.21 us -> 2.41 us
    ppermute x0 -> x26, waiting for transfers between devices: none -> 103 us  [swap(): return lax.ppermute(value, axis, [(i, i ^ distance) for i in range(count)])]
    unnamed x1 -> x0, blocking collectives: 76.1 us -> none
    dot_general x7 -> x2, matrix products: 52.9 us -> 18.7 us  [part(): return jnp.dot(x, columns, preferred_element_type=jnp.float32)]
    ppermute x0 -> x26, starting transfers between devices: none -> 31.1 us  [swap(): return lax.ppermute(value, axis, [(i, i ^ distance) for i in range(count)])]
    all_to_all x1 -> x0, blocking collectives: 29.7 us -> none  [on_device(): lax.all_to_all(adapter_delta, 'replica', split_axis=0, concat_axis=0, til...]
    reshape x3 -> x1, local copies, waits for them, and re-layouts: 17.6 us -> 0.09 us  [on_device(): return join(seg_of.reshape(-1), valid, base_mine, base_other, deltas)]
    pallas_call x0 -> x6, Pallas kernels: none -> 17.2 us  [the longest x2 7.84 us: reduce_rank(): pl.pallas_call(functools.partial(reduce_kernel, len(rows), len(lefts), sl...]
    unnamed x11 -> x42, local copies, waits for them, and re-layouts: 1.44 us -> 13.6 us
  transfers between devices with their start and end apart: 2 -> 26, of which waited for: 0 -> 11; matrix products, arithmetic and copies ran while one was open for 22% -> 11% of each run, Pallas kernels for 0% -> 6%
where the time goes in v1:
time: 189 us; the launch traced here: 188 us
  waiting for transfers between devices  103 us (54%)
  starting transfers between devices  31.1 us (16%)
  matrix products  18.7 us (10%)
  Pallas kernels  17.2 us (9%)
  local copies, waits for them, and re-layouts  16.2 us (9%)
  other arithmetic  2.41 us (1%)
    ppermute x26, waiting for transfers between devices, swap(): return lax.ppermute(value, axis, [(i, i ^ distance) for i in range(count)])  103 us
    ppermute x26, starting transfers between devices, swap(): return lax.ppermute(value, axis, [(i, i ^ distance) for i in range(count)])  31.1 us
    dot_general x2, matrix products, part(): return jnp.dot(x, columns, preferred_element_type=jnp.float32)  18.7 us
    unnamed x42, local copies, waits for them, and re-layouts  13.6 us
    pallas_call x2, Pallas kernels, reduce_rank(): pl.pallas_call(functools.partial(reduce_kernel, len(rows), len(lefts), sl...  7.84 us
    pallas_call x1, Pallas kernels, join(): pl.pallas_call(join_kernel, grid=(features // block,), out_shape=jax.Shap...  4.17 us
  transfers between devices with their start and end apart: 26, of which 11 were waited for; matrix products, arithmetic and copies ran while one was open for 11% of the time, Pallas kernels for 6%

profile of v1, /device:TPU:0, one launch (start us, length us, event | category | flops | bytes accessed | tf_op | source)
XLA Modules:
  0.0 188.5 jit_solution(16922498822365822330)
XLA Ops:
  2.4 2.2 %copy-done.1 = bf16[512,4096]{1,0:T(8,128)(2,1)S(1)} copy-done((bf16[512,4096]{1,0:T(8,128)(2,1)S(1)}, bf16[512,4096]{1,0:T(8,128)(2,1)}, u32[]{:S(2)}) %copy-start.1) | copy-done | bytes 4194328
  4.6 2.1 %pick_rows.1 = (bf16[64,4096]{1,0:T(8,128)(2,1)S(1)}, bf16[64,4096]{1,0:T(8,128)(2,1)S(1)}, bf16[64,4096]{1,0:T(8,128)(2,1)S(1)}, bf16[64,4096]{1,0:T(8,128)(2,1...) custom-call(s32[16]{0:T(128)S(1)} %reshape.79.seg_ref, ...), custom_call_target="tpu_custom_call" | custom-call | bytes 8388608 | tf_op jit(solution)/shard_map/pick_rows/pallas_call | solution.py:40
  10.6 3.0 %collective-permute-start.11 = (bf16[64,4096]{1,0:T(8,128)(2,1)}, bf16[64,4096]{1,0:T(8,128)(2,1)}, u32[]{:S(2)}, u32[]{:S(2)}) collective-permute-start(bf16[64,4096]{1,0:T(8,128)(2,1)} %get-tuple-element.30), channel_id=1, source_target_pairs={{0,2},{2,0},{4,6},{6,4},{8,10},{10,8},{12,14},{14,12},{1,3},{3,1},... | collective-permute-start | bytes 1572872 | tf_op jit(solution)/shard_map/ppermute | solution.py:193
  16.5 3.0 %collective-permute-start.14 = (bf16[64,4096]{1,0:T(8,128)(2,1)}, bf16[64,4096]{1,0:T(8,128)(2,1)}, u32[]{:S(2)}, u32[]{:S(2)}) collective-permute-start(bf16[64,4096]{1,0:T(8,128)(2,1)} %bitcast.9), channel_id=1, source_target_pairs={{0,8},{2,10},{4,12},{6,14},{8,0},{10,2},{12,4},{14,6},{1,9},{3,11}... | collective-permute-start | bytes 1572872 | tf_op jit(solution)/shard_map/ppermute | solution.py:193
  21.3 4.5 %collective-permute-done.1 = s32[2,2]{1,0:T(2,128)S(1)} collective-permute-done((s32[2,2]{1,0:T(2,128)S(1)}, s32[2,2]{1,0:T(2,128)S(1)}, u32[]{:S(2)}, u32[]{:S(2)}) %collective-permute-start.1) | collective-permute-done | bytes 48 | tf_op jit(solution)/shard_map/ppermute | solution.py:193
  25.8 2.1 %collective-permute-start.2 = (s32[2,2]{1,0:T(2,128)S(1)}, s32[2,2]{1,0:T(2,128)S(1)}, u32[]{:S(2)}, u32[]{:S(2)}) collective-permute-start(s32[2,2]{1,0:T(2,128)S(1)} %get-tuple-element.39), channel_id=1, source_target_pairs={{0,4},{2,6},{4,0},{6,2},{8,12},{10,14},{12,8},{14,10},{1,5},{3,7},... | collective-permute-start | bytes 56 | tf_op jit(solution)/shard_map/ppermute | solution.py:193
  27.9 21.7 %collective-permute-done.2 = s32[2,2]{1,0:T(2,128)S(1)} collective-permute-done((s32[2,2]{1,0:T(2,128)S(1)}, s32[2,2]{1,0:T(2,128)S(1)}, u32[]{:S(2)}, u32[]{:S(2)}) %collective-permute-start.2) | collective-permute-done | bytes 48 | tf_op jit(solution)/shard_map/ppermute | solution.py:193
  51.2 2.9 %collective-permute-done.3 = s32[2,2]{1,0:T(2,128)S(1)} collective-permute-done((s32[2,2]{1,0:T(2,128)S(1)}, s32[2,2]{1,0:T(2,128)S(1)}, u32[]{:S(2)}, u32[]{:S(2)}) %collective-permute-start.3) | collective-permute-done | bytes 48 | tf_op jit(solution)/shard_map/ppermute | solution.py:193
  54.7 2.6 %collective-permute-start.21 = (bf16[192,1024]{1,0:T(8,128)(2,1)S(1)}, bf16[192,1024]{1,0:T(8,128)(2,1)}, u32[]{:S(2)}, u32[]{:S(2)}) collective-permute-start(bf16[192,1024]{1,0:T(8,128)(2,1)S(1)} %bitcast.23), channel_id=1, source_target_pairs={{0,8},{2,10},{4,12},{6,14},{8,0},{10,2},{12,4},{14,6},{1,9},{3,11}... | collective-permute-start | bytes 1179656 | tf_op jit(solution)/shard_map/ppermute | solution.py:193
  57.3 15.5 %collective-permute-done.21.refs_0_ = bf16[192,1024]{1,0:T(8,128)(2,1)} collective-permute-done((bf16[192,1024]{1,0:T(8,128)(2,1)S(1)}, bf16[192,1024]{1,0:T(8,128)(2,1)}, u32[]{:S(2)}, u32[]{:S(2)}) %collective-permute-start.21) | collective-permute-done | bytes 393248 | tf_op jit(solution)/shard_map/ppermute | solution.py:193
  72.7 2.9 %collective-permute-start.16 = (bf16[64,4096]{1,0:T(8,128)(2,1)}, bf16[64,4096]{1,0:T(8,128)(2,1)}, u32[]{:S(2)}, u32[]{:S(2)}) collective-permute-start(bf16[64,4096]{1,0:T(8,128)(2,1)} %bitcast.21), channel_id=1, source_target_pairs={{0,8},{2,10},{4,12},{6,14},{8,0},{10,2},{12,4},{14,6},{1,9},{3,11}... | collective-permute-start | bytes 1572872 | tf_op jit(solution)/shard_map/ppermute | solution.py:193
  79.2 10.5 %fusion.7 = f32[512,1024]{1,0:T(8,128)} fusion(bf16[512,4096]{1,0:T(8,128)(2,1)} %x_ref.1, bf16[4096,2048]{1,0:T(8,128)(2,1)} %param.7, s32[]{:T(128)S(6)} %select_n.29), kind=kOutput, calls=%fused_computation.5 | convolution fusion | flops 4294967296 | bytes 14680068 | tf_op jit(solution)/shard_map/dot_general | solution.py:252
  89.7 21.6 %collective-permute-done.15.refs_6_ = bf16[64,4096]{1,0:T(8,128)(2,1)} collective-permute-done((bf16[64,4096]{1,0:T(8,128)(2,1)}, bf16[64,4096]{1,0:T(8,128)(2,1)}, u32[]{:S(2)}, u32[]{:S(2)}) %collective-permute-start.15) | collective-permute-done | bytes 524320 | tf_op jit(solution)/shard_map/ppermute | solution.py:193
  111.4 9.1 %collective-permute-done.16.refs_7_ = bf16[64,4096]{1,0:T(8,128)(2,1)} collective-permute-done((bf16[64,4096]{1,0:T(8,128)(2,1)}, bf16[64,4096]{1,0:T(8,128)(2,1)}, u32[]{:S(2)}, u32[]{:S(2)}) %collective-permute-start.16) | collective-permute-done | bytes 524320 | tf_op jit(solution)/shard_map/ppermute | solution.py:193
  129.9 3.5 %reduce_own.1.mine_ref = f32[256,128]{1,0:T(8,128)S(1)} custom-call(s32[8]{0:T(128)S(1)} %squeeze.20.refs_0_.slot_ref, bf16[64,4096]{1,0:T(8,128)(2,1)S(1)} %copy-done.7, bf16[64,4096]{1,0:T(8,128)(2,1)S(1)} %copy-done.9, bf16[64,4096]{1,0:T(8,128)(2,1)S(1)} %copy-done.11, bf16[64,4096]{1,0:T(8,128)(2,1)} %collective-permute-done.6.refs_4_, ...), custom_call_target="tpu_custom_call" | custom-call | flops 805306368 | bytes 5242880 | tf_op jit(solution)/shard_map/reduce_own/pallas_call | solution.py:102
  133.4 2.3 %collective-permute-done.17.refs_8_ = bf16[64,4096]{1,0:T(8,128)(2,1)} collective-permute-done((bf16[64,4096]{1,0:T(8,128)(2,1)}, bf16[64,4096]{1,0:T(8,128)(2,1)}, u32[]{:S(2)}, u32[]{:S(2)}) %collective-permute-start.17) | collective-permute-done | bytes 524320 | tf_op jit(solution)/shard_map/ppermute | solution.py:193
  135.9 11.1 %collective-permute-done.18.refs_9_ = bf16[64,4096]{1,0:T(8,128)(2,1)} collective-permute-done((bf16[64,4096]{1,0:T(8,128)(2,1)}, bf16[64,4096]{1,0:T(8,128)(2,1)}, u32[]{:S(2)}, u32[]{:S(2)}) %collective-permute-start.18) | collective-permute-done | bytes 524320 | tf_op jit(solution)/shard_map/ppermute | solution.py:193
  146.9 11.2 %collective-permute-done.19.refs_10_ = bf16[64,4096]{1,0:T(8,128)(2,1)} collective-permute-done((bf16[64,4096]{1,0:T(8,128)(2,1)}, bf16[64,4096]{1,0:T(8,128)(2,1)}, u32[]{:S(2)}, u32[]{:S(2)}) %collective-permute-start.19) | collective-permute-done | bytes 524320 | tf_op jit(solution)/shard_map/ppermute | solution.py:193
  159.2 4.3 %reduce_taken.1.mine_ref = f32[256,128]{1,0:T(8,128)S(1)} custom-call(s32[8]{0:T(128)S(1)} %squeeze.21.refs_0_.slot_ref, bf16[64,4096]{1,0:T(8,128)(2,1)S(1)} %copy-done.5, bf16[64,4096]{1,0:T(8,128)(2,1)} %collective-permute-done.11.refs_2_, bf16[64,4096]{1,0:T(8,128)(2,1)} %collective-permute-done.12.refs_3_, ...), custom_call_target="tpu_custom_call" | custom-call | flops 805306368 | bytes 5242880 | tf_op jit(solution)/shard_map/reduce_taken/pallas_call | solution.py:102
  166.7 2.6 %collective-permute-start.9 = (bf16[64,1024]{1,0:T(8,128)(2,1)S(1)}, bf16[64,1024]{1,0:T(8,128)(2,1)S(1)}, u32[]{:S(2)}, u32[]{:S(2)}) collective-permute-start(bf16[64,1024]{1,0:T(8,128)(2,1)S(1)} %get-tuple-element.27), channel_id=1, source_target_pairs={{0,4},{2,6},{4,0},{6,2},{8,12},{10,14},{12,8},{14,10},{1,5},{3,7},... | collective-permute-start | bytes 393224 | tf_op jit(solution)/shard_map/ppermute | solution.py:193
  169.3 2.2 %expand_taken.1 = (bf16[64,1024]{1,0:T(8,128)(2,1)S(1)}, bf16[64,1024]{1,0:T(8,128)(2,1)}, bf16[64,1024]{1,0:T(8,128)(2,1)S(1)}, bf16[64,1024]{1,0:T(8,128)(2,1)S(1)}) custom-call(s32[8]{0:T(128)S(1)} %squeeze.21.refs_0_.slot_ref, f32[256,128]{1,0:T(8,128)S(1)} %reduce_taken.1.mine_ref, f32[256,128]{1,0:T(8,128)S(1)} %collective-permute-done.20.other_ref, ...), custom_call_target="tpu_custom_call" | custom-call | flops 201326592 | bytes 1572864 | tf_op jit(solution)/shard_map/expand_taken/pallas_call | solution.py:144
  173.0 1.9 %collective-permute-done.8.refs_1_ = bf16[64,1024]{1,0:T(8,128)(2,1)S(1)} collective-permute-done((bf16[64,1024]{1,0:T(8,128)(2,1)S(1)}, bf16[64,1024]{1,0:T(8,128)(2,1)S(1)}, u32[]{:S(2)}, u32[]{:S(2)}) %collective-permute-start.8) | collective-permute-done | bytes 131104 | tf_op jit(solution)/shard_map/ppermute | solution.py:193
  175.7 8.2 %fusion.4.mine_ref = f32[512,1024]{1,0:T(8,128)S(1)} fusion(bf16[512,4096]{1,0:T(8,128)(2,1)} %x_ref.1, bf16[4096,2048]{1,0:T(8,128)(2,1)} %param.7, s32[]{:T(128)S(6)} %select_n.28), kind=kOutput, calls=%fused_computation.4 | convolution fusion | flops 4294967296 | bytes 14680068 | tf_op jit(solution)/shard_map/dot_general | solution.py:252
  184.3 4.2 %join.1 = bf16[512,1024]{1,0:T(8,128)(2,1)} custom-call(s32[16]{0:T(128)S(1)} %reshape.79.seg_ref, s32[16]{0:T(128)S(1)} %reshape.86.valid_ref, f32[512,1024]{1,0:T(8,128)S(1)} %fusion.4.mine_ref, f32[512,1024]{1,0:T(8,128)} %collective-permute-done.other_ref, bf16[64,1024]{1,0:T(8,128)(2,1)S(1)} %get-tuple-element.25.refs_0_, ...), custom_call_target="tpu_custom_call" | custom-call | flops 1048576 | bytes 6291456 | tf_op jit(solution)/shard_map/join/pallas_call | solution.py:177
  (105 shorter events, 33.1 us)
Async XLA Ops:
  10.6 62.1 %collective-permute-start.11 = (bf16[64,4096]{1,0:T(8,128)(2,1)}, bf16[64,4096]{1,0:T(8,128)(2,1)}, u32[]{:S(2)}, u32[]{:S(2)}) collective-permute-start(bf16[64,4096]{1,0:T(8,128)(2,1)} %get-tuple-element.30), channel_id=1, source_target_pairs={{0,2},{2,0},{4,6},{6,4},{8,10},{10,8},{12,14},{14,12},{1,3},{3,1},... | collective-permute-start | bytes 1572872 | tf_op jit(solution)/shard_map/ppermute | solution.py:193
  13.6 62.1 %collective-permute-start.12 = (bf16[64,4096]{1,0:T(8,128)(2,1)}, bf16[64,4096]{1,0:T(8,128)(2,1)}, u32[]{:S(2)}, u32[]{:S(2)}) collective-permute-start(bf16[64,4096]{1,0:T(8,128)(2,1)} %get-tuple-element.31), channel_id=1, source_target_pairs={{0,4},{2,6},{4,0},{6,2},{8,12},{10,14},{12,8},{14,10},{1,5},{3,7},... | collective-permute-start | bytes 1572872 | tf_op jit(solution)/shard_map/ppermute | solution.py:193
  15.2 61.2 %collective-permute-start.13 = (bf16[64,4096]{1,0:T(8,128)(2,1)}, bf16[64,4096]{1,0:T(8,128)(2,1)}, u32[]{:S(2)}, u32[]{:S(2)}) collective-permute-start(bf16[64,4096]{1,0:T(8,128)(2,1)} %get-tuple-element.32), channel_id=1, source_target_pairs={{0,6},{2,4},{4,2},{6,0},{8,14},{10,12},{12,10},{14,8},{1,7},{3,5},... | collective-permute-start | bytes 1572872 | tf_op jit(solution)/shard_map/ppermute | solution.py:193
  16.5 60.9 %collective-permute-start.14 = (bf16[64,4096]{1,0:T(8,128)(2,1)}, bf16[64,4096]{1,0:T(8,128)(2,1)}, u32[]{:S(2)}, u32[]{:S(2)}) collective-permute-start(bf16[64,4096]{1,0:T(8,128)(2,1)} %bitcast.9), channel_id=1, source_target_pairs={{0,8},{2,10},{4,12},{6,14},{8,0},{10,2},{12,4},{14,6},{1,9},{3,11}... | collective-permute-start | bytes 1572872 | tf_op jit(solution)/shard_map/ppermute | solution.py:193
  19.7 6.1 %collective-permute-start.1 = (s32[2,2]{1,0:T(2,128)S(1)}, s32[2,2]{1,0:T(2,128)S(1)}, u32[]{:S(2)}, u32[]{:S(2)}) collective-permute-start(s32[2,2]{1,0:T(2,128)S(1)} %get-tuple-element.37), channel_id=1, source_target_pairs={{0,2},{2,0},{4,6},{6,4},{8,10},{10,8},{12,14},{14,12},{1,3},{3,1},... | collective-permute-start | bytes 56 | tf_op jit(solution)/shard_map/ppermute | solution.py:193
  25.8 23.8 %collective-permute-start.2 = (s32[2,2]{1,0:T(2,128)S(1)}, s32[2,2]{1,0:T(2,128)S(1)}, u32[]{:S(2)}, u32[]{:S(2)}) collective-permute-start(s32[2,2]{1,0:T(2,128)S(1)} %get-tuple-element.39), channel_id=1, source_target_pairs={{0,4},{2,6},{4,0},{6,2},{8,12},{10,14},{12,8},{14,10},{1,5},{3,7},... | collective-permute-start | bytes 56 | tf_op jit(solution)/shard_map/ppermute | solution.py:193
  54.7 18.1 %collective-permute-start.21 = (bf16[192,1024]{1,0:T(8,128)(2,1)S(1)}, bf16[192,1024]{1,0:T(8,128)(2,1)}, u32[]{:S(2)}, u32[]{:S(2)}) collective-permute-start(bf16[192,1024]{1,0:T(8,128)(2,1)S(1)} %bitcast.23), channel_id=1, source_target_pairs={{0,8},{2,10},{4,12},{6,14},{8,0},{10,2},{12,4},{14,6},{1,9},{3,11}... | collective-permute-start | bytes 1179656 | tf_op jit(solution)/shard_map/ppermute | solution.py:193
  72.7 38.6 %collective-permute-start.15 = (bf16[64,4096]{1,0:T(8,128)(2,1)}, bf16[64,4096]{1,0:T(8,128)(2,1)}, u32[]{:S(2)}, u32[]{:S(2)}) collective-permute-start(bf16[64,4096]{1,0:T(8,128)(2,1)} %bitcast.22), channel_id=1, source_target_pairs={{0,8},{2,10},{4,12},{6,14},{8,0},{10,2},{12,4},{14,6},{1,9},{3,11}... | collective-permute-start | bytes 1572872 | tf_op jit(solution)/shard_map/ppermute | solution.py:193
  72.7 47.8 %collective-permute-start.16 = (bf16[64,4096]{1,0:T(8,128)(2,1)}, bf16[64,4096]{1,0:T(8,128)(2,1)}, u32[]{:S(2)}, u32[]{:S(2)}) collective-permute-start(bf16[64,4096]{1,0:T(8,128)(2,1)} %bitcast.21), channel_id=1, source_target_pairs={{0,8},{2,10},{4,12},{6,14},{8,0},{10,2},{12,4},{14,6},{1,9},{3,11}... | collective-permute-start | bytes 1572872 | tf_op jit(solution)/shard_map/ppermute | solution.py:193
  75.7 46.3 %collective-permute-start.4 = (bf16[64,4096]{1,0:T(8,128)(2,1)}, bf16[64,4096]{1,0:T(8,128)(2,1)S(1)}, u32[]{:S(2)}, u32[]{:S(2)}) collective-permute-start(bf16[64,4096]{1,0:T(8,128)(2,1)} %copy-done.14), channel_id=1, source_target_pairs={{0,2},{2,0},{4,6},{6,4},{8,10},{10,8},{12,14},{14,12},{1,3},{3,1},... | collective-permute-start | bytes 1572872 | tf_op jit(solution)/shard_map/ppermute | solution.py:193
  76.3 47.0 %collective-permute-start.5 = (bf16[64,4096]{1,0:T(8,128)(2,1)}, bf16[64,4096]{1,0:T(8,128)(2,1)S(1)}, u32[]{:S(2)}, u32[]{:S(2)}) collective-permute-start(bf16[64,4096]{1,0:T(8,128)(2,1)} %copy-done.13), channel_id=1, source_target_pairs={{0,4},{2,6},{4,0},{6,2},{8,12},{10,14},{12,8},{14,10},{1,5},{3,7},... | collective-permute-start | bytes 1572872 | tf_op jit(solution)/shard_map/ppermute | solution.py:193
  77.4 48.6 %collective-permute-start.6 = (bf16[64,4096]{1,0:T(8,128)(2,1)}, bf16[64,4096]{1,0:T(8,128)(2,1)}, u32[]{:S(2)}, u32[]{:S(2)}) collective-permute-start(bf16[64,4096]{1,0:T(8,128)(2,1)} %copy-done.12), channel_id=1, source_target_pairs={{0,6},{2,4},{4,2},{6,0},{8,14},{10,12},{12,10},{14,8},{1,7},{3,5},... | collective-permute-start | bytes 1572872 | tf_op jit(solution)/shard_map/ppermute | solution.py:193
  111.4 72.9 %collective-permute-start = (f32[512,1024]{1,0:T(8,128)}, f32[512,1024]{1,0:T(8,128)}, u32[]{:S(2)}, u32[]{:S(2)}) collective-permute-start(f32[512,1024]{1,0:T(8,128)} %fusion.7), channel_id=1, source_target_pairs={{0,1},{1,0},{2,3},{3,2},{4,5},{5,4},{6,7},{7,6},{8,9},{9,8},{10,11... | collective-permute-start | bytes 6291464 | tf_op jit(solution)/shard_map/ppermute | solution.py:193
  120.5 15.2 %collective-permute-start.17 = (bf16[64,4096]{1,0:T(8,128)(2,1)}, bf16[64,4096]{1,0:T(8,128)(2,1)}, u32[]{:S(2)}, u32[]{:S(2)}) collective-permute-start(bf16[64,4096]{1,0:T(8,128)(2,1)} %collective-permute-done.14.refs_5_), channel_id=1, source_target_pairs={{0,16},{16,0},{1,17},{17,1},{2,18},{18,2},{3,19},{19,3},{4,20},{20... | collective-permute-start | bytes 1572872 | tf_op jit(solution)/shard_map/ppermute | solution.py:193
  122.8 24.1 %collective-permute-start.18 = (bf16[64,4096]{1,0:T(8,128)(2,1)}, bf16[64,4096]{1,0:T(8,128)(2,1)}, u32[]{:S(2)}, u32[]{:S(2)}) collective-permute-start(bf16[64,4096]{1,0:T(8,128)(2,1)} %collective-permute-done.15.refs_6_), channel_id=1, source_target_pairs={{0,16},{16,0},{1,17},{17,1},{2,18},{18,2},{3,19},{19,3},{4,20},{20... | collective-permute-start | bytes 1572872 | tf_op jit(solution)/shard_map/ppermute | solution.py:193
  124.2 34.0 %collective-permute-start.19 = (bf16[64,4096]{1,0:T(8,128)(2,1)}, bf16[64,4096]{1,0:T(8,128)(2,1)}, u32[]{:S(2)}, u32[]{:S(2)}) collective-permute-start(bf16[64,4096]{1,0:T(8,128)(2,1)} %collective-permute-done.16.refs_7_), channel_id=1, source_target_pairs={{0,16},{16,0},{1,17},{17,1},{2,18},{18,2},{3,19},{19,3},{4,20},{20... | collective-permute-start | bytes 1572872 | tf_op jit(solution)/shard_map/ppermute | solution.py:193
  126.0 40.7 %collective-permute-start.22 = (bf16[192,1024]{1,0:T(8,128)(2,1)}, bf16[192,1024]{1,0:T(8,128)(2,1)}, u32[]{:S(2)}, u32[]{:S(2)}) collective-permute-start(bf16[192,1024]{1,0:T(8,128)(2,1)} %collective-permute-done.21.refs_0_), channel_id=1, source_target_pairs={{0,16},{16,0},{1,17},{17,1},{2,18},{18,2},{3,19},{19,3},{4,20},{20... | collective-permute-start | bytes 1179656 | tf_op jit(solution)/shard_map/ppermute | solution.py:193
  135.7 27.9 %collective-permute-start.7 = (f32[256,128]{1,0:T(8,128)S(1)}, f32[256,128]{1,0:T(8,128)S(1)}, u32[]{:S(2)}, u32[]{:S(2)}) collective-permute-start(f32[256,128]{1,0:T(8,128)S(1)} %reduce_own.1.mine_ref), channel_id=1, source_target_pairs={{0,1},{1,0},{2,3},{3,2},{4,5},{5,4},{6,7},{7,6},{8,9},{9,8},{10,11... | collective-permute-start | bytes 393224 | tf_op jit(solution)/shard_map/ppermute | solution.py:193
  165.7 7.3 %collective-permute-start.10 = (bf16[64,1024]{1,0:T(8,128)(2,1)S(1)}, bf16[64,1024]{1,0:T(8,128)(2,1)S(1)}, u32[]{:S(2)}, u32[]{:S(2)}) collective-permute-start(bf16[64,1024]{1,0:T(8,128)(2,1)S(1)} %get-tuple-element.28), channel_id=1, source_target_pairs={{0,6},{2,4},{4,2},{6,0},{8,14},{10,12},{12,10},{14,8},{1,7},{3,5},... | collective-permute-start | bytes 393224 | tf_op jit(solution)/shard_map/ppermute | solution.py:193
  165.8 9.2 %collective-permute-start.8 = (bf16[64,1024]{1,0:T(8,128)(2,1)S(1)}, bf16[64,1024]{1,0:T(8,128)(2,1)S(1)}, u32[]{:S(2)}, u32[]{:S(2)}) collective-permute-start(bf16[64,1024]{1,0:T(8,128)(2,1)S(1)} %get-tuple-element.26), channel_id=1, source_target_pairs={{0,2},{2,0},{4,6},{6,4},{8,10},{10,8},{12,14},{14,12},{1,3},{3,1},... | collective-permute-start | bytes 393224 | tf_op jit(solution)/shard_map/ppermute | solution.py:193
  166.7 17.6 %collective-permute-start.9 = (bf16[64,1024]{1,0:T(8,128)(2,1)S(1)}, bf16[64,1024]{1,0:T(8,128)(2,1)S(1)}, u32[]{:S(2)}, u32[]{:S(2)}) collective-permute-start(bf16[64,1024]{1,0:T(8,128)(2,1)S(1)} %get-tuple-element.27), channel_id=1, source_target_pairs={{0,4},{2,6},{4,0},{6,2},{8,12},{10,14},{12,8},{14,10},{1,5},{3,7},... | collective-permute-start | bytes 393224 | tf_op jit(solution)/shard_map/ppermute | solution.py:193
  171.5 12.8 %collective-permute-start.23 = (bf16[64,1024]{1,0:T(8,128)(2,1)}, bf16[64,1024]{1,0:T(8,128)(2,1)S(1)}, u32[]{:S(2)}, u32[]{:S(2)}) collective-permute-start(bf16[64,1024]{1,0:T(8,128)(2,1)} %get-tuple-element.34), channel_id=1, source_target_pairs={{0,2},{2,0},{4,6},{6,4},{8,10},{10,8},{12,14},{14,12},{1,3},{3,1},... | collective-permute-start | bytes 393224 | tf_op jit(solution)/shard_map/ppermute | solution.py:193
  173.0 11.3 %collective-permute-start.24 = (bf16[64,1024]{1,0:T(8,128)(2,1)S(1)}, bf16[64,1024]{1,0:T(8,128)(2,1)S(1)}, u32[]{:S(2)}, u32[]{:S(2)}) collective-permute-start(bf16[64,1024]{1,0:T(8,128)(2,1)S(1)} %get-tuple-element.35), channel_id=1, source_target_pairs={{0,4},{2,6},{4,0},{6,2},{8,12},{10,14},{12,8},{14,10},{1,5},{3,7},... | collective-permute-start | bytes 393224 | tf_op jit(solution)/shard_map/ppermute | solution.py:193
  175.0 9.3 %collective-permute-start.25 = (bf16[64,1024]{1,0:T(8,128)(2,1)S(1)}, bf16[64,1024]{1,0:T(8,128)(2,1)S(1)}, u32[]{:S(2)}, u32[]{:S(2)}) collective-permute-start(bf16[64,1024]{1,0:T(8,128)(2,1)S(1)} %get-tuple-element.36), channel_id=1, source_target_pairs={{0,6},{2,4},{4,2},{6,0},{8,14},{10,12},{12,10},{14,8},{1,7},{3,5},... | collective-permute-start | bytes 393224 | tf_op jit(solution)/shard_map/ppermute | solution.py:193
  (23 other events, 223.0 us)

commit v2 on v1

v2 whole, which is shorter than its diff:
```python
import functools

import jax
import jax.numpy as jnp
from jax import lax
from jax.experimental import pallas as pl
from jax.experimental.pallas import tpu as pltpu
from jax.sharding import PartitionSpec as P

CAP = 2
SEG = 32
LANES = 128
PAIR = CAP * SEG
VMEM_LIMIT = 60 * 1024 * 1024
HBM = pl.BlockSpec(memory_space=pltpu.HBM)
SMEM = pl.BlockSpec(memory_space=pltpu.SMEM)


def params():
    return pltpu.CompilerParams(vmem_limit_bytes=VMEM_LIMIT)


def pick_kernel(replicas, half, slots, me_ref, ids_ref, residency_ref, x_ref, *rest):
    outs, seg_out = rest[:half], rest[half]
    seg_ref, slot_ref, count_ref, tags, sems = rest[half + 1 :]
    width = x_ref.shape[1]
    for h in range(replicas):
        count_ref[h] = 0
        for p in range(CAP):
            seg_ref[h * CAP + p] = -1
            slot_ref[h * CAP + p] = 0
    for s in range(ids_ref.shape[0]):
        adapter = ids_ref[s]
        holder = adapter // slots
        place = holder * CAP + count_ref[holder]
        count_ref[holder] = count_ref[holder] + 1
        seg_ref[place] = s
        slot_ref[place] = residency_ref[adapter] - holder * slots
    me = me_ref[0]
    copies = []
    for d in range(half):
        for kind in range(2):
            for p in range(CAP):
                place = (me ^ (d + kind * half)) * CAP + p
                seg = seg_ref[place]
                seg_out[(kind * half + d) * CAP + p] = seg
                span = pl.ds((kind * CAP + p) * SEG, SEG)
                start = pl.multiple_of(jnp.maximum(seg, 0) * SEG, SEG)
                copy = pltpu.make_async_copy(
                    x_ref.at[pl.ds(start, SEG)],
                    outs[d].at[span, pl.ds(0, width)],
                    sems.at[len(copies)],
                )
                copy.start()
                copies.append(copy)
                slot = slot_ref[place].astype(jnp.float32)
                tags[d, span, :] = jnp.full((SEG, LANES), slot, jnp.float32).astype(tags.dtype)
    for d in range(half):
        copy = pltpu.make_async_copy(
            tags.at[d], outs[d].at[:, pl.ds(width, LANES)], sems.at[len(copies)]
        )
        copy.start()
        copies.append(copy)
    for copy in copies:
        copy.wait()


def pick_rows(me, ids, residency, x, replicas, half, slots):
    width = x.shape[1]
    count = 2 * half * CAP
    return pl.pallas_call(
        functools.partial(pick_kernel, replicas, half, slots),
        out_shape=[jax.ShapeDtypeStruct((2 * PAIR, width + LANES), x.dtype)] * half
        + [jax.ShapeDtypeStruct((count,), jnp.int32)],
        in_specs=[SMEM, SMEM, SMEM, HBM],
        out_specs=[HBM] * half + [SMEM],
        scratch_shapes=[
            pltpu.SMEM((replicas * CAP,), jnp.int32),
            pltpu.SMEM((replicas * CAP,), jnp.int32),
            pltpu.SMEM((replicas,), jnp.int32),
            pltpu.VMEM((half, 2 * PAIR, LANES), x.dtype),
            pltpu.SemaphoreType.DMA((count + half,)),
        ],
        compiler_params=params(),
        cost_estimate=pl.CostEstimate(
            flops=0, bytes_accessed=count * SEG * width * 4, transcendentals=0
        ),
        name="pick_rows",
    )(me, ids, residency, x)


def slot_mask(tags, first, slots, share):
    lane = lax.broadcasted_iota(jnp.int32, (1, LANES), 1)
    column_slot = jnp.zeros((1, LANES), jnp.float32)
    for j in range(0, LANES, share):
        slot = ((first + j) // share) % slots
        column_slot = jnp.where(lane >= j, float(slot), column_slot)
    return tags == column_slot


def reduce_kernel(n_rows, n_left, slots, share, *refs):
    rows = refs[:n_rows]
    tags = refs[n_rows : 2 * n_rows]
    lefts = refs[2 * n_rows : 2 * n_rows + n_left]
    out_ref, acc = refs[-2:]
    step = pl.program_id(0)
    rows_block = jnp.concatenate([ref[...] for ref in rows], axis=0)
    left_block = jnp.concatenate([ref[...] for ref in lefts], axis=0)
    product = lax.dot_general(
        rows_block, left_block, (((1,), (1,)), ((), ())), preferred_element_type=jnp.float32
    )

    @pl.when(step == 0)
    def _():
        acc[...] = product

    @pl.when(step > 0)
    def _():
        acc[...] += product

    @pl.when(step == pl.num_programs(0) - 1)
    def _():
        tag = jnp.concatenate([ref[...] for ref in tags], axis=0).astype(jnp.float32)
        total = jnp.zeros(out_ref.shape, jnp.float32)
        for first in range(0, acc.shape[1], LANES):
            mask = slot_mask(tag, first, slots, share)
            total += jnp.where(mask, acc[:, first : first + LANES], 0.0)
        out_ref[...] = total


def reduce_rank(kind, rows, lefts, slots, share, name):
    width = lefts[0].shape[1]
    block = min(width, 1024)
    height = len(rows) * PAIR
    columns = sum(left.shape[0] for left in lefts)
    last = width // LANES
    return pl.pallas_call(
        functools.partial(reduce_kernel, len(rows), len(lefts), slots, share),
        grid=(width // block,),
        out_shape=jax.ShapeDtypeStruct((height, LANES), jnp.float32),
        in_specs=[pl.BlockSpec((PAIR, block), lambda k: (kind, k))] * len(rows)
        + [pl.BlockSpec((PAIR, LANES), lambda k: (kind, last))] * len(rows)
        + [pl.BlockSpec((left.shape[0], block), lambda k: (0, k)) for left in lefts],
        out_specs=pl.BlockSpec((height, LANES), lambda k: (0, 0)),
        scratch_shapes=[pltpu.VMEM((height, columns), jnp.float32)],
        compiler_params=params(),
        cost_estimate=pl.CostEstimate(
            flops=2 * height * width * columns,
            bytes_accessed=2 * width * (height + columns),
            transcendentals=0,
        ),
        name=name,
    )(*rows, *rows, *lefts)


def expand_kernel(n_rows, n_up, slots, share, mine_ref, other_ref, *refs):
    tags, ups, outs = refs[:n_rows], refs[n_rows : n_rows + n_up], refs[n_rows + n_up :]
    tag = jnp.concatenate([ref[...] for ref in tags], axis=0).astype(jnp.float32)
    up = jnp.concatenate([ref[...] for ref in ups], axis=0)
    low = (mine_ref[...] + other_ref[...]).astype(jnp.bfloat16).astype(jnp.float32)
    spread = [
        jnp.where(slot_mask(tag, first, slots, share), low, 0.0).astype(jnp.bfloat16)
        for first in range(0, up.shape[0], LANES)
    ]
    delta = jnp.dot(
        jnp.concatenate(spread, axis=1), up, preferred_element_type=jnp.float32
    ).astype(jnp.bfloat16)
    for i, out in enumerate(outs):
        out[...] = delta[i * PAIR : (i + 1) * PAIR]


def expand_rank(kind, rows, mine, other, ups, slots, share, name):
    features = ups[0].shape[1]
    block = min(features, 512)
    columns = sum(up.shape[0] for up in ups)
    last = rows[0].shape[1] // LANES - 1
    low = pl.BlockSpec(mine.shape, lambda j: (0, 0))
    return pl.pallas_call(
        functools.partial(expand_kernel, len(rows), len(ups), slots, share),
        grid=(features // block,),
        out_shape=[jax.ShapeDtypeStruct((PAIR, features), jnp.bfloat16)] * len(rows),
        in_specs=[low, low]
        + [pl.BlockSpec((PAIR, LANES), lambda j: (kind, last))] * len(rows)
        + [pl.BlockSpec((up.shape[0], block), lambda j: (0, j)) for up in ups],
        out_specs=[pl.BlockSpec((PAIR, block), lambda j: (0, j))] * len(rows),
        compiler_params=params(),
        cost_estimate=pl.CostEstimate(
            flops=2 * mine.shape[0] * columns * features,
            bytes_accessed=2 * features * (columns + mine.shape[0]) + 8 * mine.size,
            transcendentals=0,
        ),
        name=name,
    )(mine, other, *rows, *ups)


def join_kernel(seg_ref, base_ref, *refs):
    deltas, out_ref = refs[:-1], refs[-1]
    for k in range(len(deltas) * CAP):
        part = k % CAP

        @pl.when(seg_ref[k] >= 0)
        def _():
            span = pl.ds(pl.multiple_of(seg_ref[k] * SEG, SEG), SEG)
            delta = deltas[k // CAP][part * SEG : (part + 1) * SEG, :]
            out_ref[span, :] = (base_ref[span, :] + delta.astype(jnp.float32)).astype(
                out_ref.dtype
            )


def join(seg_of, base, deltas):
    height, features = base.shape
    block = min(features, 256)
    tall = pl.BlockSpec((height, block), lambda j: (0, j))
    short = pl.BlockSpec((PAIR, block), lambda j: (0, j))
    return pl.pallas_call(
        join_kernel,
        grid=(features // block,),
        out_shape=jax.ShapeDtypeStruct((height, features), jnp.bfloat16),
        in_specs=[SMEM, tall] + [short] * len(deltas),
        out_specs=tall,
        compiler_params=params(),
        cost_estimate=pl.CostEstimate(
            flops=height * features, bytes_accessed=8 * height * features, transcendentals=0
        ),
        name="join",
    )(seg_of, base, *deltas)


def swap(value, axis, distance):
    count = lax.axis_size(axis)
    return lax.ppermute(value, axis, [(i, i ^ distance) for i in range(count)])


def on_device(x, weight, lefts, ups, ids, residency):
    replicas = lax.axis_size("replica")
    groups = lax.axis_size("groups")
    half = replicas // 2
    me = lax.axis_index("replica").astype(jnp.int32)
    group = lax.axis_index("groups")
    core = lax.axis_index("tensor")
    slots, width, rank = lefts.shape
    share = rank // groups
    features = ups.shape[2]

    *picked, seg_of = pick_rows(me.reshape(1), ids, residency, x, replicas, half, slots)
    rows = [picked[0]] + [swap(picked[d], "replica", d) for d in range(1, half)]

    left_rows = jnp.swapaxes(lefts, 1, 2)
    late_left_rows, _ = lax.optimization_barrier((left_rows, picked[0]))
    left_share = lax.dynamic_slice(late_left_rows, (0, group * share, 0), (slots, share, width))
    x, left_share = lax.optimization_barrier((x, left_share))
    late_ups, rows[1] = lax.optimization_barrier((ups, rows[1]))
    up_share = lax.dynamic_slice(late_ups, (0, group * share, 0), (slots, share, features))
    chunk = 2
    left_in = [
        swap(left_share[c : c + chunk].reshape(chunk * share, width), "replica", half)
        for c in range(0, slots, chunk)
    ]
    up_in = swap(up_share.reshape(slots * share, features), "replica", half)
    left_all = list(left_in)
    up_all = [up_in]
    for e in range(1, groups):
        left_all += [swap(piece, "groups", e) for piece in left_in]
        up_all.append(swap(up_in, "groups", e))

    def part(which):
        columns = lax.dynamic_slice(weight, (0, which * features), (weight.shape[0], features))
        return jnp.dot(x, columns, preferred_element_type=jnp.float32)

    base = part(core) + swap(part(1 - core), "tensor", 1)

    own_left = [left_rows.reshape(slots * rank, width)]
    own_up = [ups.reshape(slots * rank, features)]
    deltas = []
    for kind, (left, up, held, name) in enumerate(
        [(own_left, own_up, rank, "own"), (left_all, up_all, share, "taken")]
    ):
        low = reduce_rank(kind, rows, left, slots, held, "reduce_" + name)
        if kind:
            low, base = lax.optimization_barrier((low, base))
        other = swap(low, "tensor", 1)
        terms = expand_rank(kind, rows, low, other, up, slots, held, "expand_" + name)
        deltas.append(terms[0])
        deltas += [swap(terms[d], "replica", d) for d in range(1, half)]
    return join(seg_of, base, deltas)


def solution(mesh):
    placed = (
        P(("groups", "replica"), "tensor"),
        P("tensor", None),
        P("replica", "tensor", None),
        P("replica", None, "tensor"),
        P(("groups", "replica")),
        P(),
    )
    return jax.shard_map(
        on_device,
        mesh=mesh,
        in_specs=placed,
        out_specs=P(("groups", "replica"), "tensor"),
        check_vma=False,
    )
```

time: 189 us -> 307 us (1.62)
  Pallas kernels: 17.2 us -> 149 us
  local copies, waits for them, and re-layouts: 16.2 us -> 4.92 us
    pallas_call x3, Pallas kernels: 5.22 us -> 135 us  [the longest x1 130 us: pick_rows(): pl.pallas_call(functools.partial(pick_kernel, replicas, half, slots), out...]
    unnamed x42 -> x38, local copies, waits for them, and re-layouts: 13.6 us -> 2.71 us
    ppermute x26 -> x20, starting transfers between devices: 31.1 us -> 28.5 us  [swap(): return lax.ppermute(value, axis, [(i, i ^ distance) for i in range(count)])]
    ppermute x26 -> x20, waiting for transfers between devices: 103 us -> 102 us  [swap(): return lax.ppermute(value, axis, [(i, i ^ distance) for i in range(count)])]
  transfers between devices with their start and end apart: 26 -> 20, of which waited for: 11 -> 9; matrix products, arithmetic and copies ran while one was open for 11% -> 4% of each run, Pallas kernels for 6% -> 5%
where the time goes in v2:
time: 307 us; the launch traced here: 306 us
  Pallas kernels  149 us (49%)
  waiting for transfers between devices  102 us (33%)
  starting transfers between devices  28.5 us (9%)
  matrix products  21.7 us (7%)
  local copies, waits for them, and re-layouts  4.92 us (2%)
    pallas_call x1, Pallas kernels, pick_rows(): pl.pallas_call(functools.partial(pick_kernel, replicas, half, slots), out...  130 us
    ppermute x20, waiting for transfers between devices, swap(): return lax.ppermute(value, axis, [(i, i ^ distance) for i in range(count)])  102 us
    ppermute x20, starting transfers between devices, swap(): return lax.ppermute(value, axis, [(i, i ^ distance) for i in range(count)])  28.5 us
    dot_general x2, matrix products, part(): return jnp.dot(x, columns, preferred_element_type=jnp.float32)  21.7 us
    pallas_call x2, Pallas kernels, reduce_rank(): pl.pallas_call(functools.partial(reduce_kernel, len(rows), len(lefts), sl...  10.2 us
  transfers between devices with their start and end apart: 20, of which 9 were waited for; matrix products, arithmetic and copies ran while one was open for 4% of the time, Pallas kernels for 5%

profile of v2, /device:TPU:0, one launch (start us, length us, event | category | flops | bytes accessed | tf_op | source)
XLA Modules:
  0.0 306.3 jit_solution(14031739268911450971)
XLA Ops:
  0.0 129.8 %pick_rows.1 = (bf16[128,4224]{1,0:T(8,128)(2,1)}, bf16[128,4224]{1,0:T(8,128)(2,1)}, bf16[128,4224]{1,0:T(8,128)(2,1)}, bf16[128,4224]{1,0:T(8,128)(2,1)}, s32[16]{0:T(128)}) custom-call(s32[1]{0:T(128)} %bitcast.me_ref, s32[16]{0:T(128)} %ids_ref.1, s32[48]{0:T(128)} %residency_ref.1, bf16[512,4096]{1,0:T(8,128)(2,1)} %x_ref.1), custom_call_target="tpu_custom_call" | custom-call | bytes 8388608 | tf_op jit(solution)/shard_map/pick_rows/pallas_call | solution.py:71
  131.1 10.6 %fusion = f32[512,1024]{1,0:T(8,128)} fusion(bf16[512,4096]{1,0:T(8,128)(2,1)} %x_ref.1, bf16[4096,2048]{1,0:T(8,128)(2,1)} %param.7, s32[]{:T(128)S(6)} %select_n.12), kind=kOutput, calls=%fused_computation | convolution fusion | flops 4294967296 | bytes 14680068 | tf_op jit(solution)/shard_map/dot_general | solution.py:268
  142.4 3.7 %collective-permute-start.3 = (bf16[64,4096]{1,0:T(8,128)(2,1)S(1)}, bf16[64,4096]{1,0:T(8,128)(2,1)}, u32[]{:S(2)}, u32[]{:S(2)}) collective-permute-start(bf16[64,4096]{1,0:T(8,128)(2,1)S(1)} %bitcast.16), channel_id=1, source_target_pairs={{0,8},{2,10},{4,12},{6,14},{8,0},{10,2},{12,4},{14,6},{1,9},{3,11}... | collective-permute-start | bytes 1572872 | tf_op jit(solution)/shard_map/ppermute | solution.py:231
  147.6 1.6 collective-permute-start.1
  149.5 20.8 %collective-permute-done.3.refs_8_ = bf16[64,4096]{1,0:T(8,128)(2,1)} collective-permute-done((bf16[64,4096]{1,0:T(8,128)(2,1)S(1)}, bf16[64,4096]{1,0:T(8,128)(2,1)}, u32[]{:S(2)}, u32[]{:S(2)}) %collective-permute-start.3) | collective-permute-done | bytes 524320 | tf_op jit(solution)/shard_map/ppermute | solution.py:231
  171.6 21.1 %collective-permute-done.4.refs_9_ = bf16[64,4096]{1,0:T(8,128)(2,1)} collective-permute-done((bf16[64,4096]{1,0:T(8,128)(2,1)S(1)}, bf16[64,4096]{1,0:T(8,128)(2,1)}, u32[]{:S(2)}, u32[]{:S(2)}) %collective-permute-start.4) | collective-permute-done | bytes 524320 | tf_op jit(solution)/shard_map/ppermute | solution.py:231
  192.8 3.5 %collective-permute-start.5 = (bf16[64,4096]{1,0:T(8,128)(2,1)S(1)}, bf16[64,4096]{1,0:T(8,128)(2,1)}, u32[]{:S(2)}, u32[]{:S(2)}) collective-permute-start(bf16[64,4096]{1,0:T(8,128)(2,1)S(1)} %bitcast.14), channel_id=1, source_target_pairs={{0,8},{2,10},{4,12},{6,14},{8,0},{10,2},{12,4},{14,6},{1,9},{3,11}... | collective-permute-start | bytes 1572872 | tf_op jit(solution)/shard_map/ppermute | solution.py:231
  196.2 30.5 %collective-permute-done.5.refs_10_ = bf16[64,4096]{1,0:T(8,128)(2,1)} collective-permute-done((bf16[64,4096]{1,0:T(8,128)(2,1)S(1)}, bf16[64,4096]{1,0:T(8,128)(2,1)}, u32[]{:S(2)}, u32[]{:S(2)}) %collective-permute-start.5) | collective-permute-done | bytes 524320 | tf_op jit(solution)/shard_map/ppermute | solution.py:231
  231.1 3.5 %collective-permute-start.15 = (bf16[192,1024]{1,0:T(8,128)(2,1)}, bf16[192,1024]{1,0:T(8,128)(2,1)}, u32[]{:S(2)}, u32[]{:S(2)}) collective-permute-start(bf16[192,1024]{1,0:T(8,128)(2,1)} %bitcast.7), channel_id=1, source_target_pairs={{0,8},{2,10},{4,12},{6,14},{8,0},{10,2},{12,4},{14,6},{1,9},{3,11}... | collective-permute-start | bytes 1179656 | tf_op jit(solution)/shard_map/ppermute | solution.py:231
  234.6 5.1 %reduce_own.1.mine_ref = f32[256,128]{1,0:T(8,128)} custom-call(bf16[128,4224]{1,0:T(8,128)(2,1)} %get-tuple-element.26.refs_0_.refs_4_, bf16[128,4224]{1,0:T(8,128)(2,1)} %copy-done, bf16[128,4224]{1,0:T(8,128)(2,1)} %copy-done.1, bf16[128,4224]{1,0:T(8,128)(2,1)} %copy-done.2, bf16[128,4224]{1,0:T(8,128)(2,1)} %get-tuple-element.26.refs_0_.refs_4_, ...), custom_call_target="tpu_custom_call" | custom-call | flops 805306368 | bytes 5242880 | tf_op jit(solution)/shard_map/reduce_own/pallas_call | solution.py:137
  239.7 2.2 collective-permute-done.6.refs_11_
  241.9 11.2 %collective-permute-done.7.refs_12_ = bf16[64,4096]{1,0:T(8,128)(2,1)} collective-permute-done((bf16[64,4096]{1,0:T(8,128)(2,1)}, bf16[64,4096]{1,0:T(8,128)(2,1)}, u32[]{:S(2)}, u32[]{:S(2)}) %collective-permute-start.7) | collective-permute-done | bytes 524320 | tf_op jit(solution)/shard_map/ppermute | solution.py:231
  253.1 9.9 %collective-permute-done.8.refs_13_ = bf16[64,4096]{1,0:T(8,128)(2,1)} collective-permute-done((bf16[64,4096]{1,0:T(8,128)(2,1)}, bf16[64,4096]{1,0:T(8,128)(2,1)}, u32[]{:S(2)}, u32[]{:S(2)}) %collective-permute-start.8) | collective-permute-done | bytes 524320 | tf_op jit(solution)/shard_map/ppermute | solution.py:231
  263.1 5.1 %reduce_taken.1.mine_ref = f32[256,128]{1,0:T(8,128)} custom-call(bf16[128,4224]{1,0:T(8,128)(2,1)} %get-tuple-element.26.refs_0_.refs_4_, bf16[128,4224]{1,0:T(8,128)(2,1)} %copy-done, bf16[128,4224]{1,0:T(8,128)(2,1)} %copy-done.1, bf16[128,4224]{1,0:T(8,128)(2,1)} %copy-done.2, bf16[128,4224]{1,0:T(8,128)(2,1)} %get-tuple-element.26.refs_0_.refs_4_, ...), custom_call_target="tpu_custom_call" | custom-call | flops 805306368 | bytes 5242880 | tf_op jit(solution)/shard_map/reduce_taken/pallas_call | solution.py:137
  268.2 1.6 collective-permute-start.16
  269.7 11.0 %fusion.4.base_ref = f32[512,1024]{1,0:T(8,128)} fusion(f32[512,1024]{1,0:T(8,128)} %collective-permute-done.9, bf16[512,4096]{1,0:T(8,128)(2,1)} %x_ref.1, bf16[4096,2048]{1,0:T(8,128)(2,1)} %param.7, s32[]{:T(128)S(6)} %select_n.11), kind=kOutput, calls=%fused_computation.4 | convolution fusion | flops 4295491584 | bytes 16777220 | tf_op jit(solution)/shard_map/dot_general | solution.py:268
  281.4 2.4 expand_own.1
  283.9 1.6 collective-permute-start.11
  285.4 2.5 collective-permute-start.12
  289.3 2.5 expand_taken.1
  293.3 2.0 collective-permute-start.18
  295.4 2.1 collective-permute-done.17.refs_5_
  297.5 2.4 collective-permute-done.18.refs_6_
  302.1 4.2 %join.1 = bf16[512,1024]{1,0:T(8,128)(2,1)} custom-call(s32[16]{0:T(128)} %get-tuple-element.25.seg_ref, f32[512,1024]{1,0:T(8,128)} %fusion.4.base_ref, bf16[64,1024]{1,0:T(8,128)(2,1)} %get-tuple-element.35.refs_0_, bf16[64,1024]{1,0:T(8,128)(2,1)} %copy-done.8, bf16[64,1024]{1,0:T(8,128)(2,1)} %copy-done.9, bf16[64,1024]{1,0:T(8,128)(2,1)} %copy-done.10, ...), custom_call_target="tpu_custom_call" | custom-call | flops 524288 | bytes 4194304 | tf_op jit(solution)/shard_map/join/pallas_call | solution.py:215
  (65 shorter events, 15.1 us)
Async XLA Ops:
  0.0 129.8 %copy-start.3 = (bf16[6,4096,64]{1,2,0:T(8,128)(2,1)S(1)}, bf16[6,4096,64]{1,2,0:T(8,128)(2,1)}, u32[]{:S(2)}) copy-start(bf16[6,4096,64]{1,2,0:T(8,128)(2,1)} %param.8) | copy-start | bytes 9437188
  131.1 14.9 %copy-start.18 = (bf16[128,4224]{1,0:T(8,128)(2,1)S(1)}, bf16[128,4224]{1,0:T(8,128)(2,1)}, u32[]{:S(2)}) copy-start(bf16[128,4224]{1,0:T(8,128)(2,1)} %get-tuple-element.27) | copy-start | bytes 3244036
  141.8 28.5 %copy-start.16 = (bf16[128,4224]{1,0:T(8,128)(2,1)S(1)}, bf16[128,4224]{1,0:T(8,128)(2,1)}, u32[]{:S(2)}) copy-start(bf16[128,4224]{1,0:T(8,128)(2,1)} %get-tuple-element.30) | copy-start | bytes 3244036
  141.8 88.5 %copy-start.5 = (bf16[6,64,1024]{2,1,0:T(8,128)(2,1)S(1)}, bf16[6,64,1024]{2,1,0:T(8,128)(2,1)}, u32[]{:S(2)}) copy-start(bf16[6,64,1024]{2,1,0:T(8,128)(2,1)} %param.9) | copy-start | bytes 2359300
  141.8 127.9 %collective-permute-start.9 = (f32[512,1024]{1,0:T(8,128)}, f32[512,1024]{1,0:T(8,128)}, u32[]{:S(2)}, u32[]{:S(2)}) collective-permute-start(f32[512,1024]{1,0:T(8,128)} %fusion), channel_id=1, source_target_pairs={{0,1},{1,0},{2,3},{3,2},{4,5},{5,4},{6,7},{7,6},{8,9},{9,8},{10,11... | collective-permute-start | bytes 6291464 | tf_op jit(solution)/shard_map/ppermute | solution.py:231
  142.4 27.9 %collective-permute-start.3 = (bf16[64,4096]{1,0:T(8,128)(2,1)S(1)}, bf16[64,4096]{1,0:T(8,128)(2,1)}, u32[]{:S(2)}, u32[]{:S(2)}) collective-permute-start(bf16[64,4096]{1,0:T(8,128)(2,1)S(1)} %bitcast.16), channel_id=1, source_target_pairs={{0,8},{2,10},{4,12},{6,14},{8,0},{10,2},{12,4},{14,6},{1,9},{3,11}... | collective-permute-start | bytes 1572872 | tf_op jit(solution)/shard_map/ppermute | solution.py:231
  146.1 82.2 %collective-permute-start = (bf16[128,4224]{1,0:T(8,128)(2,1)S(1)}, bf16[128,4224]{1,0:T(8,128)(2,1)S(1)}, u32[]{:S(2)}, u32[]{:S(2)}) collective-permute-start(bf16[128,4224]{1,0:T(8,128)(2,1)S(1)} %copy-done.18), channel_id=1, source_target_pairs={{0,2},{2,0},{4,6},{6,4},{8,10},{10,8},{12,14},{14,12},{1,3},{3,1},... | collective-permute-start | bytes 3244040 | tf_op jit(solution)/shard_map/ppermute | solution.py:231
  147.6 81.2 %collective-permute-start.1 = (bf16[128,4224]{1,0:T(8,128)(2,1)S(1)}, bf16[128,4224]{1,0:T(8,128)(2,1)S(1)}, u32[]{:S(2)}, u32[]{:S(2)}) collective-permute-start(bf16[128,4224]{1,0:T(8,128)(2,1)S(1)} %copy-done.17), channel_id=1, source_target_pairs={{0,4},{2,6},{4,0},{6,2},{8,12},{10,14},{12,8},{14,10},{1,5},{3,7},... | collective-permute-start | bytes 3244040 | tf_op jit(solution)/shard_map/ppermute | solution.py:231
  149.2 43.6 %collective-permute-start.4 = (bf16[64,4096]{1,0:T(8,128)(2,1)S(1)}, bf16[64,4096]{1,0:T(8,128)(2,1)}, u32[]{:S(2)}, u32[]{:S(2)}) collective-permute-start(bf16[64,4096]{1,0:T(8,128)(2,1)S(1)} %bitcast.15), channel_id=1, source_target_pairs={{0,8},{2,10},{4,12},{6,14},{8,0},{10,2},{12,4},{14,6},{1,9},{3,11}... | collective-permute-start | bytes 1572872 | tf_op jit(solution)/shard_map/ppermute | solution.py:231
  170.3 60.8 %collective-permute-start.2 = (bf16[128,4224]{1,0:T(8,128)(2,1)S(1)}, bf16[128,4224]{1,0:T(8,128)(2,1)S(1)}, u32[]{:S(2)}, u32[]{:S(2)}) collective-permute-start(bf16[128,4224]{1,0:T(8,128)(2,1)S(1)} %copy-done.16), channel_id=1, source_target_pairs={{0,6},{2,4},{4,2},{6,0},{8,14},{10,12},{12,10},{14,8},{1,7},{3,5},... | collective-permute-start | bytes 3244040 | tf_op jit(solution)/shard_map/ppermute | solution.py:231
  192.8 34.0 %collective-permute-start.5 = (bf16[64,4096]{1,0:T(8,128)(2,1)S(1)}, bf16[64,4096]{1,0:T(8,128)(2,1)}, u32[]{:S(2)}, u32[]{:S(2)}) collective-permute-start(bf16[64,4096]{1,0:T(8,128)(2,1)S(1)} %bitcast.14), channel_id=1, source_target_pairs={{0,8},{2,10},{4,12},{6,14},{8,0},{10,2},{12,4},{14,6},{1,9},{3,11}... | collective-permute-start | bytes 1572872 | tf_op jit(solution)/shard_map/ppermute | solution.py:231
  226.8 15.1 %collective-permute-start.6 = (bf16[64,4096]{1,0:T(8,128)(2,1)}, bf16[64,4096]{1,0:T(8,128)(2,1)}, u32[]{:S(2)}, u32[]{:S(2)}) collective-permute-start(bf16[64,4096]{1,0:T(8,128)(2,1)} %collective-permute-done.3.refs_8_), channel_id=1, source_target_pairs={{0,16},{16,0},{1,17},{17,1},{2,18},{18,2},{3,19},{19,3},{4,20},{20... | collective-permute-start | bytes 1572872 | tf_op jit(solution)/shard_map/ppermute | solution.py:231
  228.3 24.9 %collective-permute-start.7 = (bf16[64,4096]{1,0:T(8,128)(2,1)}, bf16[64,4096]{1,0:T(8,128)(2,1)}, u32[]{:S(2)}, u32[]{:S(2)}) collective-permute-start(bf16[64,4096]{1,0:T(8,128)(2,1)} %collective-permute-done.4.refs_9_), channel_id=1, source_target_pairs={{0,16},{16,0},{1,17},{17,1},{2,18},{18,2},{3,19},{19,3},{4,20},{20... | collective-permute-start | bytes 1572872 | tf_op jit(solution)/shard_map/ppermute | solution.py:231
  228.8 34.3 %collective-permute-start.8 = (bf16[64,4096]{1,0:T(8,128)(2,1)}, bf16[64,4096]{1,0:T(8,128)(2,1)}, u32[]{:S(2)}, u32[]{:S(2)}) collective-permute-start(bf16[64,4096]{1,0:T(8,128)(2,1)} %collective-permute-done.5.refs_10_), channel_id=1, source_target_pairs={{0,16},{16,0},{1,17},{17,1},{2,18},{18,2},{3,19},{19,3},{4,20},{20... | collective-permute-start | bytes 1572872 | tf_op jit(solution)/shard_map/ppermute | solution.py:231
  231.1 37.1 %collective-permute-start.15 = (bf16[192,1024]{1,0:T(8,128)(2,1)}, bf16[192,1024]{1,0:T(8,128)(2,1)}, u32[]{:S(2)}, u32[]{:S(2)}) collective-permute-start(bf16[192,1024]{1,0:T(8,128)(2,1)} %bitcast.7), channel_id=1, source_target_pairs={{0,8},{2,10},{4,12},{6,14},{8,0},{10,2},{12,4},{14,6},{1,9},{3,11}... | collective-permute-start | bytes 1179656 | tf_op jit(solution)/shard_map/ppermute | solution.py:231
  241.9 38.9 %collective-permute-start.10 = (f32[256,128]{1,0:T(8,128)}, f32[256,128]{1,0:T(8,128)S(1)}, u32[]{:S(2)}, u32[]{:S(2)}) collective-permute-start(f32[256,128]{1,0:T(8,128)} %reduce_own.1.mine_ref), channel_id=1, source_target_pairs={{0,1},{1,0},{2,3},{3,2},{4,5},{5,4},{6,7},{7,6},{8,9},{9,8},{10,11... | collective-permute-start | bytes 393224 | tf_op jit(solution)/shard_map/ppermute | solution.py:231
  268.2 19.7 %collective-permute-start.16 = (bf16[192,1024]{1,0:T(8,128)(2,1)}, bf16[192,1024]{1,0:T(8,128)(2,1)S(1)}, u32[]{:S(2)}, u32[]{:S(2)}) collective-permute-start(bf16[192,1024]{1,0:T(8,128)(2,1)} %collective-permute-done.15.refs_4_), channel_id=1, source_target_pairs={{0,16},{16,0},{1,17},{17,1},{2,18},{18,2},{3,19},{19,3},{4,20},{20... | collective-permute-start | bytes 1179656 | tf_op jit(solution)/shard_map/ppermute | solution.py:231
  280.8 7.1 %collective-permute-start.14 = (f32[256,128]{1,0:T(8,128)S(1)}, f32[256,128]{1,0:T(8,128)S(1)}, u32[]{:S(2)}, u32[]{:S(2)}) collective-permute-start(f32[256,128]{1,0:T(8,128)S(1)} %copy-done.6), channel_id=1, source_target_pairs={{0,1},{1,0},{2,3},{3,2},{4,5},{5,4},{6,7},{7,6},{8,9},{9,8},{10,11... | collective-permute-start | bytes 393224 | tf_op jit(solution)/shard_map/ppermute | solution.py:231
  283.9 11.5 %collective-permute-start.11 = (bf16[64,1024]{1,0:T(8,128)(2,1)}, bf16[64,1024]{1,0:T(8,128)(2,1)S(1)}, u32[]{:S(2)}, u32[]{:S(2)}) collective-permute-start(bf16[64,1024]{1,0:T(8,128)(2,1)} %get-tuple-element.36), channel_id=1, source_target_pairs={{0,2},{2,0},{4,6},{6,4},{8,10},{10,8},{12,14},{14,12},{1,3},{3,1},... | collective-permute-start | bytes 393224 | tf_op jit(solution)/shard_map/ppermute | solution.py:231
  285.4 10.0 %collective-permute-start.12 = (bf16[64,1024]{1,0:T(8,128)(2,1)}, bf16[64,1024]{1,0:T(8,128)(2,1)S(1)}, u32[]{:S(2)}, u32[]{:S(2)}) collective-permute-start(bf16[64,1024]{1,0:T(8,128)(2,1)} %get-tuple-element.37), channel_id=1, source_target_pairs={{0,4},{2,6},{4,0},{6,2},{8,12},{10,14},{12,8},{14,10},{1,5},{3,7},... | collective-permute-start | bytes 393224 | tf_op jit(solution)/shard_map/ppermute | solution.py:231
  287.9 7.5 %collective-permute-start.13 = (bf16[64,1024]{1,0:T(8,128)(2,1)}, bf16[64,1024]{1,0:T(8,128)(2,1)S(1)}, u32[]{:S(2)}, u32[]{:S(2)}) collective-permute-start(bf16[64,1024]{1,0:T(8,128)(2,1)} %get-tuple-element.38), channel_id=1, source_target_pairs={{0,6},{2,4},{4,2},{6,0},{8,14},{10,12},{12,10},{14,8},{1,7},{3,5},... | collective-permute-start | bytes 393224 | tf_op jit(solution)/shard_map/ppermute | solution.py:231
  291.8 5.7 %collective-permute-start.17 = (bf16[64,1024]{1,0:T(8,128)(2,1)}, bf16[64,1024]{1,0:T(8,128)(2,1)S(1)}, u32[]{:S(2)}, u32[]{:S(2)}) collective-permute-start(bf16[64,1024]{1,0:T(8,128)(2,1)} %get-tuple-element.42), channel_id=1, source_target_pairs={{0,2},{2,0},{4,6},{6,4},{8,10},{10,8},{12,14},{14,12},{1,3},{3,1},... | collective-permute-start | bytes 393224 | tf_op jit(solution)/shard_map/ppermute | solution.py:231
  293.3 6.6 %collective-permute-start.18 = (bf16[64,1024]{1,0:T(8,128)(2,1)}, bf16[64,1024]{1,0:T(8,128)(2,1)S(1)}, u32[]{:S(2)}, u32[]{:S(2)}) collective-permute-start(bf16[64,1024]{1,0:T(8,128)(2,1)} %get-tuple-element.43), channel_id=1, source_target_pairs={{0,4},{2,6},{4,0},{6,2},{8,12},{10,14},{12,8},{14,10},{1,5},{3,7},... | collective-permute-start | bytes 393224 | tf_op jit(solution)/shard_map/ppermute | solution.py:231
  295.4 6.1 %collective-permute-start.19 = (bf16[64,1024]{1,0:T(8,128)(2,1)}, bf16[64,1024]{1,0:T(8,128)(2,1)S(1)}, u32[]{:S(2)}, u32[]{:S(2)}) collective-permute-start(bf16[64,1024]{1,0:T(8,128)(2,1)} %get-tuple-element.44), channel_id=1, source_target_pairs={{0,6},{2,4},{4,2},{6,0},{8,14},{10,12},{12,10},{14,8},{1,7},{3,5},... | collective-permute-start | bytes 393224 | tf_op jit(solution)/shard_map/ppermute | solution.py:231
  (15 other events, 71.4 us)

commit v3 on v2

--- a/solution.py
+++ b/solution.py
@@ -22,14 +22,20 @@
 
 def pick_kernel(replicas, half, slots, me_ref, ids_ref, residency_ref, x_ref, *rest):
     outs, seg_out = rest[:half], rest[half]
-    seg_ref, slot_ref, count_ref, tags, sems = rest[half + 1 :]
+    seg_ref, slot_ref, count_ref, staged, tags, in_sems, sems = rest[half + 1 :]
     width = x_ref.shape[1]
+    segs = ids_ref.shape[0]
+    arrivals = []
+    for s in range(segs):
+        span = pl.ds(s * SEG, SEG)
+        arrivals.append(pltpu.make_async_copy(x_ref.at[span], staged.at[span], in_sems.at[s]))
+        arrivals[-1].start()
     for h in range(replicas):
         count_ref[h] = 0
         for p in range(CAP):
             seg_ref[h * CAP + p] = -1
             slot_ref[h * CAP + p] = 0
-    for s in range(ids_ref.shape[0]):
+    for s in range(segs):
         adapter = ids_ref[s]
         holder = adapter // slots
         place = holder * CAP + count_ref[holder]
@@ -37,6 +43,8 @@
         seg_ref[place] = s
         slot_ref[place] = residency_ref[adapter] - holder * slots
     me = me_ref[0]
+    for arrival in arrivals:
+        arrival.wait()
     copies = []
     for d in range(half):
         for kind in range(2):
@@ -47,7 +55,7 @@
                 span = pl.ds((kind * CAP + p) * SEG, SEG)
                 start = pl.multiple_of(jnp.maximum(seg, 0) * SEG, SEG)
                 copy = pltpu.make_async_copy(
-                    x_ref.at[pl.ds(start, SEG)],
+                    staged.at[pl.ds(start, SEG)],
                     outs[d].at[span, pl.ds(0, width)],
                     sems.at[len(copies)],
                 )
@@ -78,7 +86,9 @@
             pltpu.SMEM((replicas * CAP,), jnp.int32),
             pltpu.SMEM((replicas * CAP,), jnp.int32),
             pltpu.SMEM((replicas,), jnp.int32),
+            pltpu.VMEM(x.shape, x.dtype),
             pltpu.VMEM((half, 2 * PAIR, LANES), x.dtype),
+            pltpu.SemaphoreType.DMA((ids.shape[0],)),
             pltpu.SemaphoreType.DMA((count + half,)),
         ],
         compiler_params=params(),
@@ -98,14 +108,23 @@
     return tags == column_slot
 
 
-def reduce_kernel(n_rows, n_left, slots, share, *refs):
+def gather_parts(refs, counts):
+    total, at = None, 0
+    for count in counts:
+        whole = jnp.concatenate([ref[...] for ref in refs[at : at + count]], axis=0)
+        total = whole if total is None else total + whole
+        at += count
+    return total
+
+
+def reduce_kernel(n_rows, counts, slots, share, *refs):
     rows = refs[:n_rows]
     tags = refs[n_rows : 2 * n_rows]
-    lefts = refs[2 * n_rows : 2 * n_rows + n_left]
+    lefts = refs[2 * n_rows : -2]
     out_ref, acc = refs[-2:]
     step = pl.program_id(0)
     rows_block = jnp.concatenate([ref[...] for ref in rows], axis=0)
-    left_block = jnp.concatenate([ref[...] for ref in lefts], axis=0)
+    left_block = gather_parts(lefts, counts)
     product = lax.dot_general(
         rows_block, left_block, (((1,), (1,)), ((), ())), preferred_element_type=jnp.float32
     )
@@ -128,14 +147,16 @@
         out_ref[...] = total
 
 
-def reduce_rank(kind, rows, lefts, slots, share, name):
-    width = lefts[0].shape[1]
+def reduce_rank(kind, rows, sources, slots, share, name):
+    counts = [len(source) for source in sources]
+    lefts = [left for source in sources for left in source]
+    width = rows[0].shape[1] - LANES
     block = min(width, 1024)
     height = len(rows) * PAIR
-    columns = sum(left.shape[0] for left in lefts)
+    columns = sum(left.shape[0] for left in sources[0])
     last = width // LANES
     return pl.pallas_call(
-        functools.partial(reduce_kernel, len(rows), len(lefts), slots, share),
+        functools.partial(reduce_kernel, len(rows), counts, slots, share),
         grid=(width // block,),
         out_shape=jax.ShapeDtypeStruct((height, LANES), jnp.float32),
         in_specs=[pl.BlockSpec((PAIR, block), lambda k: (kind, k))] * len(rows)
@@ -153,10 +174,11 @@
     )(*rows, *rows, *lefts)
 
 
-def expand_kernel(n_rows, n_up, slots, share, mine_ref, other_ref, *refs):
+def expand_kernel(n_rows, counts, slots, share, mine_ref, other_ref, *refs):
+    n_up = sum(counts)
     tags, ups, outs = refs[:n_rows], refs[n_rows : n_rows + n_up], refs[n_rows + n_up :]
     tag = jnp.concatenate([ref[...] for ref in tags], axis=0).astype(jnp.float32)
-    up = jnp.concatenate([ref[...] for ref in ups], axis=0)
+    up = gather_parts(ups, counts)
     low = (mine_ref[...] + other_ref[...]).astype(jnp.bfloat16).astype(jnp.float32)
     spread = [
         jnp.where(slot_mask(tag, first, slots, share), low, 0.0).astype(jnp.bfloat16)
@@ -169,19 +191,25 @@
         out[...] = delta[i * PAIR : (i + 1) * PAIR]
 
 
-def expand_rank(kind, rows, mine, other, ups, slots, share, name):
-    features = ups[0].shape[1]
+def expand_rank(kind, rows, mine, other, sources, features, slots, share, name):
+    counts = [len(source) for source in sources]
+    ups = [up for source in sources for up in source]
     block = min(features, 512)
-    columns = sum(up.shape[0] for up in ups)
+    columns = sum(up.shape[0] for up in sources[0])
+
+    def up_spec(up):
+        first = (up.shape[1] - features) // block
+        return pl.BlockSpec((up.shape[0], block), lambda j: (0, first + j))
+
     last = rows[0].shape[1] // LANES - 1
     low = pl.BlockSpec(mine.shape, lambda j: (0, 0))
     return pl.pallas_call(
-        functools.partial(expand_kernel, len(rows), len(ups), slots, share),
+        functools.partial(expand_kernel, len(rows), counts, slots, share),
         grid=(features // block,),
         out_shape=[jax.ShapeDtypeStruct((PAIR, features), jnp.bfloat16)] * len(rows),
         in_specs=[low, low]
         + [pl.BlockSpec((PAIR, LANES), lambda j: (kind, last))] * len(rows)
-        + [pl.BlockSpec((up.shape[0], block), lambda j: (0, j)) for up in ups],
+        + [up_spec(up) for up in ups],
         out_specs=[pl.BlockSpec((PAIR, block), lambda j: (0, j))] * len(rows),
         compiler_params=params(),
         cost_estimate=pl.CostEstimate(
@@ -231,55 +259,81 @@
     return lax.ppermute(value, axis, [(i, i ^ distance) for i in range(count)])
 
 
+def swap_some(value, senders, group_distance, replica_distance):
+    groups, replicas = lax.axis_size("groups"), lax.axis_size("replica")
+    pairs = [
+        (g * replicas + r, (g ^ group_distance) * replicas + (r ^ replica_distance))
+        for g in range(groups)
+        for r in senders
+    ]
+    return lax.ppermute(value, ("groups", "replica"), pairs)
+
+
 def on_device(x, weight, lefts, ups, ids, residency):
     replicas = lax.axis_size("replica")
     groups = lax.axis_size("groups")
     half = replicas // 2
     me = lax.axis_index("replica").astype(jnp.int32)
     group = lax.axis_index("groups")
-    core = lax.axis_index("tensor")
     slots, width, rank = lefts.shape
     share = rank // groups
     features = ups.shape[2]
+    inner = range(replicas // 4, 3 * replicas // 4)
+    outer = [r for r in range(replicas) if r not in inner]
 
     *picked, seg_of = pick_rows(me.reshape(1), ids, residency, x, replicas, half, slots)
     rows = [picked[0]] + [swap(picked[d], "replica", d) for d in range(1, half)]
 
     left_rows = jnp.swapaxes(lefts, 1, 2)
-    late_left_rows, _ = lax.optimization_barrier((left_rows, picked[0]))
-    left_share = lax.dynamic_slice(late_left_rows, (0, group * share, 0), (slots, share, width))
-    x, left_share = lax.optimization_barrier((x, left_share))
-    late_ups, rows[1] = lax.optimization_barrier((ups, rows[1]))
-    up_share = lax.dynamic_slice(late_ups, (0, group * share, 0), (slots, share, features))
+
+    def shares(left, up):
+        return (
+            lax.dynamic_slice(left, (0, group * share, 0), (slots, share, width)),
+            lax.dynamic_slice(up, (0, group * share, 0), (slots, share, features)),
+        )
+
+    left_share, up_share = shares(left_rows, ups)
+    early_up = swap_some(up_share.reshape(slots * share, features), inner, 0, half)
+    early_left = swap_some(left_share.reshape(slots * share, width), inner, 0, half)
+
+    late_x, early_up, _ = lax.optimization_barrier((x, early_up, picked[0]))
+    partial_sum = jnp.dot(late_x, weight, preferred_element_type=jnp.float32)
+
+    rows, early_left, early_up, left_rows, ups, partial_sum = lax.optimization_barrier(
+        (rows, early_left, early_up, left_rows, ups, partial_sum)
+    )
+    left_share, up_share = shares(left_rows, ups)
     chunk = 2
     left_in = [
-        swap(left_share[c : c + chunk].reshape(chunk * share, width), "replica", half)
+        swap_some(left_share[c : c + chunk].reshape(chunk * share, width), outer, 0, half)
         for c in range(0, slots, chunk)
     ]
-    up_in = swap(up_share.reshape(slots * share, features), "replica", half)
-    left_all = list(left_in)
-    up_all = [up_in]
+    up_in = swap_some(up_share.reshape(slots * share, features), outer, 0, half)
+    early_lefts, early_ups = [early_left], [early_up]
+    late_lefts, late_ups = list(left_in), [up_in]
     for e in range(1, groups):
-        left_all += [swap(piece, "groups", e) for piece in left_in]
-        up_all.append(swap(up_in, "groups", e))
-
-    def part(which):
-        columns = lax.dynamic_slice(weight, (0, which * features), (weight.shape[0], features))
-        return jnp.dot(x, columns, preferred_element_type=jnp.float32)
-
-    base = part(core) + swap(part(1 - core), "tensor", 1)
-
-    own_left = [left_rows.reshape(slots * rank, width)]
-    own_up = [ups.reshape(slots * rank, features)]
+        early_lefts.append(swap_some(early_left, outer, e, 0))
+        early_ups.append(swap_some(early_up, outer, e, 0))
+        late_lefts += [swap_some(piece, inner, e, 0) for piece in left_in]
+        late_ups.append(swap_some(up_in, inner, e, 0))
+    base = lax.psum_scatter(partial_sum, "tensor", scatter_dimension=1, tiled=True)
+
+    own_left = [[left_rows.reshape(slots * rank, width)]]
+    own_up = [[ups.reshape(slots * rank, features)]]
     deltas = []
     for kind, (left, up, held, name) in enumerate(
-        [(own_left, own_up, rank, "own"), (left_all, up_all, share, "taken")]
+        [
+            (own_left, own_up, rank, "own"),
+            ([early_lefts, late_lefts], [early_ups, late_ups], share, "taken"),
+        ]
     ):
         low = reduce_rank(kind, rows, left, slots, held, "reduce_" + name)
         if kind:
             low, base = lax.optimization_barrier((low, base))
         other = swap(low, "tensor", 1)
-        terms = expand_rank(kind, rows, low, other, up, slots, held, "expand_" + name)
+        terms = expand_rank(
+            kind, rows, low, other, up, features, slots, held, "expand_" + name
+        )
         deltas.append(terms[0])
         deltas += [swap(terms[d], "replica", d) for d in range(1, half)]
     return join(seg_of, base, deltas)

time: 307 us -> 203 us (0.66)
  Pallas kernels: 149 us -> 25.8 us
  starting transfers between devices: 28.5 us -> 43.1 us
  between operations: 0.14 us -> 13.7 us
  matrix products: 21.7 us -> 14.9 us
  waiting for transfers between devices: 102 us -> 95.8 us
  local copies, waits for them, and re-layouts: 4.92 us -> 8.94 us
    pallas_call x1, Pallas kernels: 130 us -> 5.69 us  [pick_rows(): pl.pallas_call(functools.partial(pick_kernel, replicas, half, slots), out...]
    ppermute x20 -> x11, waiting for transfers between devices: 102 us -> 66.3 us  [swap(): return lax.ppermute(value, axis, [(i, i ^ distance) for i in range(count)])]
    ppermute x0 -> x12, waiting for transfers between devices: none -> 29.5 us  [swap_some(): return lax.ppermute(value, ('groups', 'replica'), pairs)]
    ppermute x0 -> x12, starting transfers between devices: none -> 24.8 us  [swap_some(): return lax.ppermute(value, ('groups', 'replica'), pairs)]
    ppermute x20 -> x11, starting transfers between devices: 28.5 us -> 18.4 us  [swap(): return lax.ppermute(value, axis, [(i, i ^ distance) for i in range(count)])]
    dot_general x2 -> x1, matrix products: 21.7 us -> 14.9 us  [on_device(): partial_sum = jnp.dot(late_x, weight, preferred_element_type=jnp.float32)]
  transfers between devices with their start and end apart: 20 -> 24, of which waited for: 9 -> 10; matrix products, arithmetic and copies ran while one was open for 4% -> 10% of each run, Pallas kernels for 5% -> 11%
where the time goes in v3:
time: 203 us; the launch traced here: 202 us
  waiting for transfers between devices  95.8 us (47%)
  starting transfers between devices  43.1 us (21%)
  Pallas kernels  25.8 us (13%)
  matrix products  14.9 us (7%)
  between operations  13.7 us (7%)
  local copies, waits for them, and re-layouts  8.94 us (4%)
    ppermute x11, waiting for transfers between devices, swap(): return lax.ppermute(value, axis, [(i, i ^ distance) for i in range(count)])  66.3 us
    ppermute x12, waiting for transfers between devices, swap_some(): return lax.ppermute(value, ('groups', 'replica'), pairs)  29.5 us
    ppermute x12, starting transfers between devices, swap_some(): return lax.ppermute(value, ('groups', 'replica'), pairs)  24.8 us
    ppermute x11, starting transfers between devices, swap(): return lax.ppermute(value, axis, [(i, i ^ distance) for i in range(count)])  18.4 us
    dot_general x1, matrix products, on_device(): partial_sum = jnp.dot(late_x, weight, preferred_element_type=jnp.float32)  14.9 us
    pallas_call x2, Pallas kernels, reduce_rank(): pl.pallas_call(functools.partial(reduce_kernel, len(rows), counts, slots,...  10.8 us
    pallas_call x1, Pallas kernels, pick_rows(): pl.pallas_call(functools.partial(pick_kernel, replicas, half, slots), out...  5.69 us
    pallas_call x2, Pallas kernels, expand_rank(): pl.pallas_call(functools.partial(expand_kernel, len(rows), counts, slots,...  5.17 us
  transfers between devices with their start and end apart: 24, of which 10 were waited for; matrix products, arithmetic and copies ran while one was open for 10% of the time, Pallas kernels for 11%

profile of v3, /device:TPU:0, one launch (start us, length us, event | category | flops | bytes accessed | tf_op | source)
XLA Modules:
  0.0 202.4 jit_solution(9276614724627700545)
XLA Ops:
  6.5 1.8 constant_dynamic-slice_fusion.4
  9.6 2.8 %constant_dynamic-slice_fusion.5 = bf16[6,4096,32]{1,2,0:T(8,128)(2,1)} fusion(bf16[6,4096,64]{1,2,0:T(8,128)(2,1)} %param.8, s32[]{:T(128)S(6)} %select_n.2), kind=kLoop, calls=%fused_computation.5 | loop fusion | bytes 3145732 | tf_op jit(solution)/shard_map/dynamic-slice
  13.6 5.7 %pick_rows.1 = (bf16[128,4224]{1,0:T(8,128)(2,1)}, bf16[128,4224]{1,0:T(8,128)(2,1)}, bf16[128,4224]{1,0:T(8,128)(2,1)}, bf16[128,4224]{1,0:T(8,128)(2,1)}, s32[16]{0:T(128)}) custom-call(s32[1]{0:T(128)} %bitcast.me_ref, s32[16]{0:T(128)} %ids_ref.1, s32[48]{0:T(128)} %residency_ref.1, bf16[512,4096]{1,0:T(8,128)(2,1)} %x_ref.1), custom_call_target="tpu_custom_call" | custom-call | bytes 8388608 | tf_op jit(solution)/shard_map/pick_rows/pallas_call | solution.py:79
  19.3 3.0 %collective-permute-start = (bf16[128,4224]{1,0:T(8,128)(2,1)}, bf16[128,4224]{1,0:T(8,128)(2,1)S(1)}, u32[]{:S(2)}, u32[]{:S(2)}) collective-permute-start(bf16[128,4224]{1,0:T(8,128)(2,1)} %get-tuple-element.33), channel_id=1, source_target_pairs={{0,2},{2,0},{4,6},{6,4},{8,10},{10,8},{12,14},{14,12},{1,3},{3,1},... | collective-permute-start | bytes 3244040 | tf_op jit(solution)/shard_map/ppermute | solution.py:259
  22.4 6.7 %collective-permute-start.1 = (bf16[128,4224]{1,0:T(8,128)(2,1)}, bf16[128,4224]{1,0:T(8,128)(2,1)S(1)}, u32[]{:S(2)}, u32[]{:S(2)}) collective-permute-start(bf16[128,4224]{1,0:T(8,128)(2,1)} %get-tuple-element.34), channel_id=1, source_target_pairs={{0,4},{2,6},{4,0},{6,2},{8,12},{10,14},{12,8},{14,10},{1,5},{3,7},... | collective-permute-start | bytes 3244040 | tf_op jit(solution)/shard_map/ppermute | solution.py:259
  29.1 14.9 %fusion = f32[512,2048]{1,0:T(8,128)} fusion(bf16[512,4096]{1,0:T(8,128)(2,1)} %x_ref.1, bf16[4096,2048]{1,0:T(8,128)(2,1)} %param.7), kind=kOutput, calls=%fused_computation.6 | convolution fusion | flops 8589934592 | bytes 25165824 | tf_op jit(solution)/shard_map/dot_general | solution.py:300
  44.0 2.4 %collective-permute-done.refs_1_.refs_5_ = bf16[128,4224]{1,0:T(8,128)(2,1)S(1)} collective-permute-done((bf16[128,4224]{1,0:T(8,128)(2,1)}, bf16[128,4224]{1,0:T(8,128)(2,1)S(1)}, u32[]{:S(2)}, u32[]{:S(2)}) %collective-permute-start) | collective-permute-done | bytes 1081376 | tf_op jit(solution)/shard_map/ppermute | solution.py:259
  46.4 33.5 %collective-permute-done.1.refs_2_.refs_6_ = bf16[128,4224]{1,0:T(8,128)(2,1)S(1)} collective-permute-done((bf16[128,4224]{1,0:T(8,128)(2,1)}, bf16[128,4224]{1,0:T(8,128)(2,1)S(1)}, u32[]{:S(2)}, u32[]{:S(2)}) %collective-permute-start.1) | collective-permute-done | bytes 1081376 | tf_op jit(solution)/shard_map/ppermute | solution.py:259
  79.9 24.7 %collective-permute-done.2.refs_3_.refs_7_ = bf16[128,4224]{1,0:T(8,128)(2,1)S(1)} collective-permute-done((bf16[128,4224]{1,0:T(8,128)(2,1)}, bf16[128,4224]{1,0:T(8,128)(2,1)S(1)}, u32[]{:S(2)}, u32[]{:S(2)}) %collective-permute-start.2) | collective-permute-done | bytes 1081376 | tf_op jit(solution)/shard_map/ppermute | solution.py:259
  104.7 3.5 %collective-permute-start.5 = (bf16[192,4096]{1,0:T(8,128)(2,1)}, bf16[192,4096]{1,0:T(8,128)(2,1)}, u32[]{:S(2)}, u32[]{:S(2)}) collective-permute-start(bf16[192,4096]{1,0:T(8,128)(2,1)} %collective-permute-done.3.refs_8_), channel_id=1, source_target_pairs={{0,16},{2,18},{12,28},{14,30},{16,0},{18,2},{28,12},{30,14},{1,17}... | collective-permute-start | bytes 4718600 | tf_op jit(solution)/shard_map/ppermute | solution.py:269
  113.7 9.6 %collective-permute-done.7.refs_11_ = bf16[64,4096]{1,0:T(8,128)(2,1)S(1)} collective-permute-done((bf16[64,4096]{1,0:T(8,128)(2,1)S(1)}, bf16[64,4096]{1,0:T(8,128)(2,1)S(1)}, u32[]{:S(2)}, u32[]{:S(2)}) %collective-permute-start.7) | collective-permute-done | bytes 524320 | tf_op jit(solution)/shard_map/ppermute | solution.py:269
  124.1 7.9 %collective-permute-start.18 = (bf16[192,1024]{1,0:T(8,128)(2,1)S(1)}, bf16[192,1024]{1,0:T(8,128)(2,1)S(1)}, u32[]{:S(2)}, u32[]{:S(2)}) collective-permute-start(bf16[192,1024]{1,0:T(8,128)(2,1)S(1)} %bitcast.20), channel_id=1, source_target_pairs={{0,8},{2,10},{12,4},{14,6},{16,24},{18,26},{28,20},{30,22},{1,9},{... | collective-permute-start | bytes 1179656 | tf_op jit(solution)/shard_map/ppermute | solution.py:269
  132.0 2.6 %collective-permute-done.8.refs_12_ = bf16[64,4096]{1,0:T(8,128)(2,1)S(1)} collective-permute-done((bf16[64,4096]{1,0:T(8,128)(2,1)S(1)}, bf16[64,4096]{1,0:T(8,128)(2,1)S(1)}, u32[]{:S(2)}, u32[]{:S(2)}) %collective-permute-start.8) | collective-permute-done | bytes 524320 | tf_op jit(solution)/shard_map/ppermute | solution.py:269
  135.3 10.5 %collective-permute-done.6.refs_10_ = bf16[64,4096]{1,0:T(8,128)(2,1)S(1)} collective-permute-done((bf16[64,4096]{1,0:T(8,128)(2,1)S(1)}, bf16[64,4096]{1,0:T(8,128)(2,1)S(1)}, u32[]{:S(2)}, u32[]{:S(2)}) %collective-permute-start.6) | collective-permute-done | bytes 524320 | tf_op jit(solution)/shard_map/ppermute | solution.py:269
  146.5 6.8 %collective-permute-done.18.refs_6_ = bf16[192,1024]{1,0:T(8,128)(2,1)S(1)} collective-permute-done((bf16[192,1024]{1,0:T(8,128)(2,1)S(1)}, bf16[192,1024]{1,0:T(8,128)(2,1)S(1)}, u32[]{:S(2)}, u32[]{:S(2)}) %collective-permute-start.18) | collective-permute-done | bytes 393248 | tf_op jit(solution)/shard_map/ppermute | solution.py:269
  153.3 3.3 %collective-permute-start.17 = (bf16[192,1024]{1,0:T(8,128)(2,1)}, bf16[192,1024]{1,0:T(8,128)(2,1)S(1)}, u32[]{:S(2)}, u32[]{:S(2)}) collective-permute-start(bf16[192,1024]{1,0:T(8,128)(2,1)} %collective-permute-done.4.refs_4_), channel_id=1, source_target_pairs={{0,16},{2,18},{12,28},{14,30},{16,0},{18,2},{28,12},{30,14},{1,17}... | collective-permute-start | bytes 1179656 | tf_op jit(solution)/shard_map/ppermute | solution.py:269
  158.1 5.1 %reduce_own.1.mine_ref = f32[256,128]{1,0:T(8,128)} custom-call(bf16[128,4224]{1,0:T(8,128)(2,1)} %get-tuple-element.38.refs_0_.refs_4_, bf16[128,4224]{1,0:T(8,128)(2,1)} %copy-done, bf16[128,4224]{1,0:T(8,128)(2,1)} %copy-done.1, bf16[128,4224]{1,0:T(8,128)(2,1)} %copy-done.2, bf16[128,4224]{1,0:T(8,128)(2,1)} %get-tuple-element.38.refs_0_.refs_4_, ...), custom_call_target="tpu_custom_call" | custom-call | flops 805306368 | bytes 5242880 | tf_op jit(solution)/shard_map/reduce_own/pallas_call | solution.py:158
  164.2 5.7 %reduce_taken.1.mine_ref = f32[256,128]{1,0:T(8,128)} custom-call(bf16[128,4224]{1,0:T(8,128)(2,1)} %get-tuple-element.38.refs_0_.refs_4_, bf16[128,4224]{1,0:T(8,128)(2,1)} %copy-done, bf16[128,4224]{1,0:T(8,128)(2,1)} %copy-done.1, bf16[128,4224]{1,0:T(8,128)(2,1)} %copy-done.2, bf16[128,4224]{1,0:T(8,128)(2,1)} %get-tuple-element.38.refs_0_.refs_4_, ...), custom_call_target="tpu_custom_call" | custom-call | flops 805306368 | bytes 5242880 | tf_op jit(solution)/shard_map/reduce_taken/pallas_call | solution.py:158
  171.0 2.4 %expand_own.1 = (bf16[64,1024]{1,0:T(8,128)(2,1)}, bf16[64,1024]{1,0:T(8,128)(2,1)}, bf16[64,1024]{1,0:T(8,128)(2,1)}, bf16[64,1024]{1,0:T(8,128)(2,1)}) custom-call(f32[256,128]{1,0:T(8,128)} %reduce_own.1.mine_ref, f32[256,128]{1,0:T(8,128)} %copy-done.19, bf16[128,4224]{1,0:T(8,128)(2,1)} %get-tuple-element.38.refs_0_.refs_4_, bf16[128,4224]{1,0:T(8,128)(2,1)} %copy-done, ...), custom_call_target="tpu_custom_call" | custom-call | flops 201326592 | bytes 1572864 | tf_op jit(solution)/shard_map/expand_own/pallas_call | solution.py:206
  173.5 1.5 collective-permute-start.13
  175.0 2.0 collective-permute-start.14
  178.7 2.7 %expand_taken.1 = (bf16[64,1024]{1,0:T(8,128)(2,1)}, bf16[64,1024]{1,0:T(8,128)(2,1)}, bf16[64,1024]{1,0:T(8,128)(2,1)}, bf16[64,1024]{1,0:T(8,128)(2,1)}) custom-call(f32[256,128]{1,0:T(8,128)} %reduce_taken.1.mine_ref, f32[256,128]{1,0:T(8,128)} %copy-done.15, bf16[128,4224]{1,0:T(8,128)(2,1)} %get-tuple-element.38.refs_0_.refs_4_, ...), custom_call_target="tpu_custom_call" | custom-call | flops 201326592 | bytes 1572864 | tf_op jit(solution)/shard_map/expand_taken/pallas_call | solution.py:206
  185.0 3.5 %collective-permute-done.20.refs_5_ = bf16[64,1024]{1,0:T(8,128)(2,1)S(1)} collective-permute-done((bf16[64,1024]{1,0:T(8,128)(2,1)}, bf16[64,1024]{1,0:T(8,128)(2,1)S(1)}, u32[]{:S(2)}, u32[]{:S(2)}) %collective-permute-start.20) | collective-permute-done | bytes 131104 | tf_op jit(solution)/shard_map/ppermute | solution.py:259
  191.3 4.2 %join.1 = bf16[512,1024]{1,0:T(8,128)(2,1)} custom-call(s32[16]{0:T(128)} %get-tuple-element.31.seg_ref, f32[512,1024]{1,0:T(8,128)} %reduce-scatter.2.cloned.1.call-done.base_ref, bf16[64,1024]{1,0:T(8,128)(2,1)} %get-tuple-element.47.refs_0_, bf16[64,1024]{1,0:T(8,128)(2,1)} %copy-done.12, bf16[64,1024]{1,0:T(8,128)(2,1)} %copy-done.13, ...), custom_call_target="tpu_custom_call" | custom-call | flops 524288 | bytes 4194304 | tf_op jit(solution)/shard_map/join/pallas_call | solution.py:243
  (76 shorter events, 21.8 us)
Async XLA Ops:
  6.5 163.4 %reduce-scatter.2.cloned.1.call-start = ((), (), s32[]{:S(2)}) async-start(), calls=%async_computation.1 | async-start | bytes 6291456 | tf_op jit(solution)/shard_map/reduce_scatter | solution.py:319
  8.3 20.8 %collective-permute-start.4 = (bf16[192,1024]{1,0:T(8,128)(2,1)}, bf16[192,1024]{1,0:T(8,128)(2,1)}, u32[]{:S(2)}, u32[]{:S(2)}) collective-permute-start(bf16[192,1024]{1,0:T(8,128)(2,1)} %bitcast.3), channel_id=1, source_target_pairs={{4,12},{6,14},{8,0},{10,2},{20,28},{22,30},{24,16},{26,18},{5,13},... | collective-permute-start | bytes 1179656 | tf_op jit(solution)/shard_map/ppermute | solution.py:269
  12.4 92.3 %collective-permute-start.3 = (bf16[192,4096]{1,0:T(8,128)(2,1)}, bf16[192,4096]{1,0:T(8,128)(2,1)}, u32[]{:S(2)}, u32[]{:S(2)}) collective-permute-start(bf16[192,4096]{1,0:T(8,128)(2,1)} %bitcast.2), channel_id=1, source_target_pairs={{4,12},{6,14},{8,0},{10,2},{20,28},{22,30},{24,16},{26,18},{5,13},... | collective-permute-start | bytes 4718600 | tf_op jit(solution)/shard_map/ppermute | solution.py:269
  19.3 27.1 %collective-permute-start = (bf16[128,4224]{1,0:T(8,128)(2,1)}, bf16[128,4224]{1,0:T(8,128)(2,1)S(1)}, u32[]{:S(2)}, u32[]{:S(2)}) collective-permute-start(bf16[128,4224]{1,0:T(8,128)(2,1)} %get-tuple-element.33), channel_id=1, source_target_pairs={{0,2},{2,0},{4,6},{6,4},{8,10},{10,8},{12,14},{14,12},{1,3},{3,1},... | collective-permute-start | bytes 3244040 | tf_op jit(solution)/shard_map/ppermute | solution.py:259
  22.4 57.5 %collective-permute-start.1 = (bf16[128,4224]{1,0:T(8,128)(2,1)}, bf16[128,4224]{1,0:T(8,128)(2,1)S(1)}, u32[]{:S(2)}, u32[]{:S(2)}) collective-permute-start(bf16[128,4224]{1,0:T(8,128)(2,1)} %get-tuple-element.34), channel_id=1, source_target_pairs={{0,4},{2,6},{4,0},{6,2},{8,12},{10,14},{12,8},{14,10},{1,5},{3,7},... | collective-permute-start | bytes 3244040 | tf_op jit(solution)/shard_map/ppermute | solution.py:259
  29.1 75.6 %collective-permute-start.2 = (bf16[128,4224]{1,0:T(8,128)(2,1)}, bf16[128,4224]{1,0:T(8,128)(2,1)S(1)}, u32[]{:S(2)}, u32[]{:S(2)}) collective-permute-start(bf16[128,4224]{1,0:T(8,128)(2,1)} %get-tuple-element.35), channel_id=1, source_target_pairs={{0,6},{2,4},{4,2},{6,0},{8,14},{10,12},{12,10},{14,8},{1,7},{3,5},... | collective-permute-start | bytes 3244040 | tf_op jit(solution)/shard_map/ppermute | solution.py:259
  104.7 58.6 %collective-permute-start.5 = (bf16[192,4096]{1,0:T(8,128)(2,1)}, bf16[192,4096]{1,0:T(8,128)(2,1)}, u32[]{:S(2)}, u32[]{:S(2)}) collective-permute-start(bf16[192,4096]{1,0:T(8,128)(2,1)} %collective-permute-done.3.refs_8_), channel_id=1, source_target_pairs={{0,16},{2,18},{12,28},{14,30},{16,0},{18,2},{28,12},{30,14},{1,17}... | collective-permute-start | bytes 4718600 | tf_op jit(solution)/shard_map/ppermute | solution.py:269
  109.8 13.6 %collective-permute-start.7 = (bf16[64,4096]{1,0:T(8,128)(2,1)S(1)}, bf16[64,4096]{1,0:T(8,128)(2,1)S(1)}, u32[]{:S(2)}, u32[]{:S(2)}) collective-permute-start(bf16[64,4096]{1,0:T(8,128)(2,1)S(1)} %bitcast.19), channel_id=1, source_target_pairs={{0,8},{2,10},{12,4},{14,6},{16,24},{18,26},{28,20},{30,22},{1,9},{... | collective-permute-start | bytes 1572872 | tf_op jit(solution)/shard_map/ppermute | solution.py:269
  111.1 23.5 %collective-permute-start.8 = (bf16[64,4096]{1,0:T(8,128)(2,1)S(1)}, bf16[64,4096]{1,0:T(8,128)(2,1)S(1)}, u32[]{:S(2)}, u32[]{:S(2)}) collective-permute-start(bf16[64,4096]{1,0:T(8,128)(2,1)S(1)} %bitcast.18), channel_id=1, source_target_pairs={{0,8},{2,10},{12,4},{14,6},{16,24},{18,26},{28,20},{30,22},{1,9},{... | collective-permute-start | bytes 1572872 | tf_op jit(solution)/shard_map/ppermute | solution.py:269
  112.4 33.4 %collective-permute-start.6 = (bf16[64,4096]{1,0:T(8,128)(2,1)S(1)}, bf16[64,4096]{1,0:T(8,128)(2,1)S(1)}, u32[]{:S(2)}, u32[]{:S(2)}) collective-permute-start(bf16[64,4096]{1,0:T(8,128)(2,1)S(1)} %bitcast.17), channel_id=1, source_target_pairs={{0,8},{2,10},{12,4},{14,6},{16,24},{18,26},{28,20},{30,22},{1,9},{... | collective-permute-start | bytes 1572872 | tf_op jit(solution)/shard_map/ppermute | solution.py:269
  123.3 33.3 %collective-permute-start.10 = (bf16[64,4096]{1,0:T(8,128)(2,1)S(1)}, bf16[64,4096]{1,0:T(8,128)(2,1)S(1)}, u32[]{:S(2)}, u32[]{:S(2)}) collective-permute-start(bf16[64,4096]{1,0:T(8,128)(2,1)S(1)} %collective-permute-done.7.refs_11_), channel_id=1, source_target_pairs={{4,20},{6,22},{8,24},{10,26},{20,4},{22,6},{24,8},{26,10},{5,21},{... | collective-permute-start | bytes 1572872 | tf_op jit(solution)/shard_map/ppermute | solution.py:269
  124.1 29.2 %collective-permute-start.18 = (bf16[192,1024]{1,0:T(8,128)(2,1)S(1)}, bf16[192,1024]{1,0:T(8,128)(2,1)S(1)}, u32[]{:S(2)}, u32[]{:S(2)}) collective-permute-start(bf16[192,1024]{1,0:T(8,128)(2,1)S(1)} %bitcast.20), channel_id=1, source_target_pairs={{0,8},{2,10},{12,4},{14,6},{16,24},{18,26},{28,20},{30,22},{1,9},{... | collective-permute-start | bytes 1179656 | tf_op jit(solution)/shard_map/ppermute | solution.py:269
  134.6 28.6 %collective-permute-start.11 = (bf16[64,4096]{1,0:T(8,128)(2,1)S(1)}, bf16[64,4096]{1,0:T(8,128)(2,1)S(1)}, u32[]{:S(2)}, u32[]{:S(2)}) collective-permute-start(bf16[64,4096]{1,0:T(8,128)(2,1)S(1)} %collective-permute-done.8.refs_12_), channel_id=1, source_target_pairs={{4,20},{6,22},{8,24},{10,26},{20,4},{22,6},{24,8},{26,10},{5,21},{... | collective-permute-start | bytes 1572872 | tf_op jit(solution)/shard_map/ppermute | solution.py:269
  145.8 17.5 %collective-permute-start.9 = (bf16[64,4096]{1,0:T(8,128)(2,1)S(1)}, bf16[64,4096]{1,0:T(8,128)(2,1)S(1)}, u32[]{:S(2)}, u32[]{:S(2)}) collective-permute-start(bf16[64,4096]{1,0:T(8,128)(2,1)S(1)} %collective-permute-done.6.refs_10_), channel_id=1, source_target_pairs={{4,20},{6,22},{8,24},{10,26},{20,4},{22,6},{24,8},{26,10},{5,21},{... | collective-permute-start | bytes 1572872 | tf_op jit(solution)/shard_map/ppermute | solution.py:269
  153.3 23.7 %collective-permute-start.17 = (bf16[192,1024]{1,0:T(8,128)(2,1)}, bf16[192,1024]{1,0:T(8,128)(2,1)S(1)}, u32[]{:S(2)}, u32[]{:S(2)}) collective-permute-start(bf16[192,1024]{1,0:T(8,128)(2,1)} %collective-permute-done.4.refs_4_), channel_id=1, source_target_pairs={{0,16},{2,18},{12,28},{14,30},{16,0},{18,2},{28,12},{30,14},{1,17}... | collective-permute-start | bytes 1179656 | tf_op jit(solution)/shard_map/ppermute | solution.py:269
  156.6 21.5 %collective-permute-start.19 = (bf16[192,1024]{1,0:T(8,128)(2,1)S(1)}, bf16[192,1024]{1,0:T(8,128)(2,1)}, u32[]{:S(2)}, u32[]{:S(2)}) collective-permute-start(bf16[192,1024]{1,0:T(8,128)(2,1)S(1)} %collective-permute-done.18.refs_6_), channel_id=1, source_target_pairs={{4,20},{6,22},{8,24},{10,26},{20,4},{22,6},{24,8},{26,10},{5,21},{... | collective-permute-start | bytes 1179656 | tf_op jit(solution)/shard_map/ppermute | solution.py:269
  163.2 7.2 %collective-permute-start.12 = (f32[256,128]{1,0:T(8,128)}, f32[256,128]{1,0:T(8,128)S(1)}, u32[]{:S(2)}, u32[]{:S(2)}) collective-permute-start(f32[256,128]{1,0:T(8,128)} %reduce_own.1.mine_ref), channel_id=1, source_target_pairs={{0,1},{1,0},{2,3},{3,2},{4,5},{5,4},{6,7},{7,6},{8,9},{9,8},{10,11... | collective-permute-start | bytes 393224 | tf_op jit(solution)/shard_map/ppermute | solution.py:259
  169.9 8.1 %collective-permute-start.16 = (f32[256,128]{1,0:T(8,128)}, f32[256,128]{1,0:T(8,128)S(1)}, u32[]{:S(2)}, u32[]{:S(2)}) collective-permute-start(f32[256,128]{1,0:T(8,128)} %reduce_taken.1.mine_ref), channel_id=1, source_target_pairs={{0,1},{1,0},{2,3},{3,2},{4,5},{5,4},{6,7},{7,6},{8,9},{9,8},{10,11... | collective-permute-start | bytes 393224 | tf_op jit(solution)/shard_map/ppermute | solution.py:259
  173.5 10.5 %collective-permute-start.13 = (bf16[64,1024]{1,0:T(8,128)(2,1)}, bf16[64,1024]{1,0:T(8,128)(2,1)S(1)}, u32[]{:S(2)}, u32[]{:S(2)}) collective-permute-start(bf16[64,1024]{1,0:T(8,128)(2,1)} %get-tuple-element.48), channel_id=1, source_target_pairs={{0,2},{2,0},{4,6},{6,4},{8,10},{10,8},{12,14},{14,12},{1,3},{3,1},... | collective-permute-start | bytes 393224 | tf_op jit(solution)/shard_map/ppermute | solution.py:259
  175.0 10.0 %collective-permute-start.14 = (bf16[64,1024]{1,0:T(8,128)(2,1)}, bf16[64,1024]{1,0:T(8,128)(2,1)S(1)}, u32[]{:S(2)}, u32[]{:S(2)}) collective-permute-start(bf16[64,1024]{1,0:T(8,128)(2,1)} %get-tuple-element.49), channel_id=1, source_target_pairs={{0,4},{2,6},{4,0},{6,2},{8,12},{10,14},{12,8},{14,10},{1,5},{3,7},... | collective-permute-start | bytes 393224 | tf_op jit(solution)/shard_map/ppermute | solution.py:259
  177.0 8.0 %collective-permute-start.15 = (bf16[64,1024]{1,0:T(8,128)(2,1)}, bf16[64,1024]{1,0:T(8,128)(2,1)S(1)}, u32[]{:S(2)}, u32[]{:S(2)}) collective-permute-start(bf16[64,1024]{1,0:T(8,128)(2,1)} %get-tuple-element.50), channel_id=1, source_target_pairs={{0,6},{2,4},{4,2},{6,0},{8,14},{10,12},{12,10},{14,8},{1,7},{3,5},... | collective-permute-start | bytes 393224 | tf_op jit(solution)/shard_map/ppermute | solution.py:259
  181.5 7.0 %collective-permute-start.20 = (bf16[64,1024]{1,0:T(8,128)(2,1)}, bf16[64,1024]{1,0:T(8,128)(2,1)S(1)}, u32[]{:S(2)}, u32[]{:S(2)}) collective-permute-start(bf16[64,1024]{1,0:T(8,128)(2,1)} %get-tuple-element.54), channel_id=1, source_target_pairs={{0,2},{2,0},{4,6},{6,4},{8,10},{10,8},{12,14},{14,12},{1,3},{3,1},... | collective-permute-start | bytes 393224 | tf_op jit(solution)/shard_map/ppermute | solution.py:259
  182.8 6.5 %collective-permute-start.21 = (bf16[64,1024]{1,0:T(8,128)(2,1)}, bf16[64,1024]{1,0:T(8,128)(2,1)S(1)}, u32[]{:S(2)}, u32[]{:S(2)}) collective-permute-start(bf16[64,1024]{1,0:T(8,128)(2,1)} %get-tuple-element.55), channel_id=1, source_target_pairs={{0,4},{2,6},{4,0},{6,2},{8,12},{10,14},{12,8},{14,10},{1,5},{3,7},... | collective-permute-start | bytes 393224 | tf_op jit(solution)/shard_map/ppermute | solution.py:259
  184.0 6.7 %collective-permute-start.22 = (bf16[64,1024]{1,0:T(8,128)(2,1)}, bf16[64,1024]{1,0:T(8,128)(2,1)S(1)}, u32[]{:S(2)}, u32[]{:S(2)}) collective-permute-start(bf16[64,1024]{1,0:T(8,128)(2,1)} %get-tuple-element.56), channel_id=1, source_target_pairs={{0,6},{2,4},{4,2},{6,0},{8,14},{10,12},{12,10},{14,8},{1,7},{3,5},... | collective-permute-start | bytes 393224 | tf_op jit(solution)/shard_map/ppermute | solution.py:259
  (20 other events, 246.2 us)
Sparse Core Ops, SparseCore 0:
  104.8 12.3 reduce-scatter.1

commit v4 on v0

v4 whole, which is shorter than its diff:
```python
import functools

import jax
import jax.numpy as jnp
from jax import lax
from jax.experimental import pallas as pl
from jax.experimental.pallas import tpu as pltpu
from jax.sharding import PartitionSpec as P

CAP = 2
SEG = 32
LANES = 128
PAIR = CAP * SEG
VMEM_LIMIT = 60 * 1024 * 1024
HBM = pl.BlockSpec(memory_space=pltpu.HBM)
SMEM = pl.BlockSpec(memory_space=pltpu.SMEM)
VMEM = pl.BlockSpec(memory_space=pltpu.VMEM)


class Plan:
    def __init__(self, replicas, groups, slots, rank, width, features):
        self.replicas, self.groups, self.slots, self.rank = replicas, groups, slots, rank
        self.width, self.features = width, features
        self.half = replicas // 2
        self.turn = self.half // 2
        self.near = [d for d in range(self.half) if not d & self.turn]
        self.cross = [d for d in range(self.half) if d & self.turn]
        self.share = rank // groups
        self.left_rows = slots * self.share
        beside = width // features
        self.up_rows = -(-self.left_rows // (beside * 16)) * 16
        self.up_piece = self.left_rows // PAIR
        self.up_first = self.left_rows % PAIR
        assert self.up_first + self.up_rows <= PAIR
        self.pieces = self.up_piece + 1
        self.wide = max(len(self.cross), -(-self.pieces // 2))
        self.narrow = max(2 * len(self.cross), self.pieces)
        self.outer = [r for r in range(replicas) if self.is_outer(r)]
        self.inner = [r for r in range(replicas) if not self.is_outer(r)]

    def is_outer(self, r):
        return (r < self.turn) or (r >= self.replicas - self.turn)

    def up_columns(self):
        for j, row in enumerate(range(0, self.left_rows, self.up_rows)):
            yield row, min(self.up_rows, self.left_rows - row), j * self.features

    def left_spans(self):
        for piece in range(self.pieces):
            rows = min(PAIR, self.left_rows - piece * PAIR)
            if rows > 0:
                yield piece, rows


def params():
    return pltpu.CompilerParams(vmem_limit_bytes=VMEM_LIMIT)


def am_outer(plan):
    me = lax.axis_index("replica")
    return (me < plan.turn) | (me >= plan.replicas - plan.turn)


def of_wide(refs, piece):
    return refs[piece // 2].at[pl.ds((piece % 2) * PAIR, PAIR)]


def lay_kernel(plan, ids_ref, residency_ref, x_ref, left_ref, up_ref, *rest):
    n_near, n_wide, n_narrow = len(plan.near), plan.wide, plan.narrow
    near, rest = rest[:n_near], rest[n_near:]
    wide, rest = rest[:n_wide], rest[n_wide:]
    narrow, rest = rest[:n_narrow], rest[n_narrow:]
    seg_out, seg_ref, slot_ref, count_ref, staged, tags, left, up, in_sems, sems = rest
    half, slots, width, share = plan.half, plan.slots, plan.width, plan.share
    segs = ids_ref.shape[0]
    me = lax.axis_index("replica")
    first = pl.multiple_of(lax.axis_index("groups") * share, share)

    arrivals = []

    def arrive(source, target):
        arrivals.append(pltpu.make_async_copy(source, target, in_sems.at[len(arrivals)]))
        arrivals[-1].start()

    for s in range(segs):
        span = pl.ds(s * SEG, SEG)
        arrive(x_ref.at[span], staged.at[span])
    for slot in range(slots):
        span = pl.ds(slot * share, share)
        arrive(left_ref.at[slot, pl.ds(first, share)], left.at[span])
        arrive(up_ref.at[slot, pl.ds(first, share)], up.at[span])

    for h in range(plan.replicas):
        count_ref[h] = 0
        for p in range(CAP):
            seg_ref[h * CAP + p] = -1
            slot_ref[h * CAP + p] = 0
    for s in range(segs):
        adapter = ids_ref[s]
        holder = adapter // slots
        place = holder * CAP + count_ref[holder]
        count_ref[holder] = count_ref[holder] + 1
        seg_ref[place] = s
        slot_ref[place] = residency_ref[adapter] - holder * slots
    for d in range(half):
        for kind in range(2):
            for p in range(CAP):
                place = (me ^ (d + kind * half)) * CAP + p
                seg_out[(kind * half + d) * CAP + p] = seg_ref[place]
                slot = slot_ref[place].astype(jnp.float32)
                tags[d, pl.ds((kind * CAP + p) * SEG, SEG), :] = jnp.full(
                    (SEG, LANES), slot, jnp.float32
                ).astype(tags.dtype)
    for arrival in arrivals:
        arrival.wait()

    def send_rows(d, kind, target, copies):
        def send(source, part):
            copies.append(pltpu.make_async_copy(source, part, sems.at[len(copies)]))
            copies[-1].start()

        for p in range(CAP):
            seg = jnp.maximum(seg_out[(kind * half + d) * CAP + p], 0)
            source = staged.at[pl.ds(pl.multiple_of(seg * SEG, SEG), SEG)]
            send(source, target.at[pl.ds(p * SEG, SEG), pl.ds(0, width)])
        send(tags.at[d, pl.ds(kind * PAIR, PAIR)], target.at[:, pl.ds(width, LANES)])

    def send_adapters(target_of, copies):
        def send(source, part):
            copies.append(pltpu.make_async_copy(source, part, sems.at[len(copies)]))
            copies[-1].start()

        for piece, rows in plan.left_spans():
            send(
                left.at[pl.ds(piece * PAIR, rows)],
                target_of(piece).at[pl.ds(0, rows), pl.ds(0, width)],
            )
        for row, rows, column in plan.up_columns():
            send(
                up.at[pl.ds(row, rows)],
                target_of(plan.up_piece).at[
                    pl.ds(plan.up_first, rows), pl.ds(column, plan.features)
                ],
            )

    def by_role(rows_of, adapters_of):
        copies = []
        for i, d in enumerate(plan.near):
            for kind in range(2):
                send_rows(d, kind, near[i].at[pl.ds(kind * PAIR, PAIR)], copies)
        for i, d in enumerate(plan.cross):
            for kind in range(2):
                send_rows(d, kind, rows_of(2 * i + kind), copies)
        send_adapters(adapters_of, copies)
        for copy in copies:
            copy.wait()

    outer = am_outer(plan)
    pl.when(outer)(lambda: by_role(lambda k: of_wide(wide, k), lambda k: narrow[k]))
    pl.when(jnp.logical_not(outer))(
        lambda: by_role(lambda k: narrow[k], lambda k: of_wide(wide, k))
    )


def lay_out(plan, ids, residency, x, left_rows, ups):
    count = 2 * plan.half * CAP
    wide = jax.ShapeDtypeStruct((2 * PAIR, plan.width + LANES), x.dtype)
    narrow = jax.ShapeDtypeStruct((PAIR, plan.width + LANES), x.dtype)
    n_out = len(plan.near) + plan.wide + plan.narrow
    n_sems = 3 * 2 * plan.half + plan.pieces + len(list(plan.up_columns()))
    out = pl.pallas_call(
        functools.partial(lay_kernel, plan),
        out_shape=[wide] * (len(plan.near) + plan.wide)
        + [narrow] * plan.narrow
        + [jax.ShapeDtypeStruct((count,), jnp.int32)],
        in_specs=[SMEM, SMEM, HBM, HBM, HBM],
        out_specs=[HBM] * n_out + [SMEM],
        scratch_shapes=[
            pltpu.SMEM((plan.replicas * CAP,), jnp.int32),
            pltpu.SMEM((plan.replicas * CAP,), jnp.int32),
            pltpu.SMEM((plan.replicas,), jnp.int32),
            pltpu.VMEM(x.shape, x.dtype),
            pltpu.VMEM((plan.half, 2 * PAIR, LANES), x.dtype),
            pltpu.VMEM((plan.left_rows, plan.width), x.dtype),
            pltpu.VMEM((plan.left_rows, plan.features), x.dtype),
            pltpu.SemaphoreType.DMA((ids.shape[0] + 2 * plan.slots,)),
            pltpu.SemaphoreType.DMA((n_sems,)),
        ],
        compiler_params=params(),
        cost_estimate=pl.CostEstimate(
            flops=0, bytes_accessed=6 * x.size, transcendentals=0
        ),
        name="lay_out",
    )(ids, residency, x, left_rows, ups)
    n_near = len(plan.near)
    return out[:n_near], out[n_near : n_near + plan.wide], out[n_near + plan.wide : -1], out[-1]


def slot_mask(tags, first, slots, share):
    lane = lax.broadcasted_iota(jnp.int32, (1, LANES), 1)
    column_slot = jnp.zeros((1, LANES), jnp.float32)
    for j in range(0, LANES, share):
        slot = ((first + j) // share) % slots
        column_slot = jnp.where(lane >= j, float(slot), column_slot)
    return tags == column_slot


class Copies:
    def __init__(self, outer, sems):
        self.outer, self.sems, self.waits = outer, sems, []

    def start(self, target, outer_source, inner_source=None):
        sem = self.sems.at[len(self.waits)]
        copy = pltpu.make_async_copy(outer_source, target, sem)
        if inner_source is None:
            copy.start()
        else:
            pl.when(self.outer)(copy.start)
            pl.when(jnp.logical_not(self.outer))(
                pltpu.make_async_copy(inner_source, target, sem).start
            )
        self.waits.append(copy)

    def wait(self):
        for copy in self.waits:
            copy.wait()


def reduce_kernel(plan, kind, n_steps, near, wide, narrow, lefts, low_ref, tag_ref, *scratch):
    rows, left, acc, tag, sems = scratch
    block = plan.width // n_steps
    outer = am_outer(plan)
    steps = []
    used = 0
    for k in range(n_steps + 1):
        copies = Copies(outer, sems.at[pl.ds(used, sems.shape[0] - used)])
        columns = pl.ds(k * block, block)
        if k == n_steps:
            columns = pl.ds(plan.width, LANES)
        span = pl.ds(kind * PAIR, PAIR)
        target = tag if k == n_steps else rows.at[:, columns]
        for i, d in enumerate(plan.near):
            copies.start(target.at[pl.ds(d * PAIR, PAIR)], near[i].at[span, columns])
        for i, d in enumerate(plan.cross):
            copies.start(
                target.at[pl.ds(d * PAIR, PAIR)],
                narrow[2 * i + kind].at[:, columns],
                wide[i].at[span, columns],
            )
        if k < n_steps:
            if kind == 0:
                copies.start(left.at[:, columns], lefts[0].at[:, columns])
            else:
                for e, (wide_left, narrow_left) in enumerate(lefts):
                    for piece, count in plan.left_spans():
                        first = e * plan.left_rows + piece * PAIR
                        copies.start(
                            left.at[pl.ds(first, count), columns],
                            of_wide(wide_left, piece).at[pl.ds(0, count), columns],
                            narrow_left[piece].at[pl.ds(0, count), columns],
                        )
        used += len(copies.waits)
        steps.append(copies)
    for k in range(n_steps):
        steps[k].wait()
        columns = pl.ds(k * block, block)
        product = lax.dot_general(
            rows[:, columns],
            left[:, columns],
            (((1,), (1,)), ((), ())),
            preferred_element_type=jnp.float32,
        )
        if k:
            acc[...] += product
        else:
            acc[...] = product
    steps[n_steps].wait()
    tags = tag[...].astype(jnp.float32)
    tag_ref[...] = tags
    share = plan.rank if kind == 0 else plan.share
    total = jnp.zeros(low_ref.shape, jnp.float32)
    for first in range(0, acc.shape[1], LANES):
        total += jnp.where(
            slot_mask(tags, first, plan.slots, share), acc[:, first : first + LANES], 0.0
        )
    low_ref[...] = total


def blocks_call(kernel, plan, blocks, out_shape, out_specs, scratch, flops, moved, name, extra=()):
    flat, tree = jax.tree.flatten(blocks)
    n_extra = len(extra)

    def body(*refs):
        head, rest = refs[:n_extra], refs[n_extra:]
        nested = jax.tree.unflatten(tree, rest[: len(flat)])
        kernel(*head, *nested, *rest[len(flat) :])

    return pl.pallas_call(
        body,
        out_shape=out_shape,
        in_specs=[VMEM] * n_extra + [HBM] * len(flat),
        out_specs=out_specs,
        scratch_shapes=scratch,
        compiler_params=params(),
        cost_estimate=pl.CostEstimate(flops=flops, bytes_accessed=moved, transcendentals=0),
        name=name,
    )(*extra, *flat)


def reduce_rank(plan, kind, near, wide, narrow, lefts, name):
    height = plan.half * PAIR
    columns = plan.slots * plan.rank
    n_steps = 4
    n_copies = (n_steps + 1) * (plan.half + plan.groups * plan.pieces)
    dtype = near[0].dtype
    return blocks_call(
        functools.partial(reduce_kernel, plan, kind, n_steps),
        plan,
        [near, wide, narrow, lefts],
        [jax.ShapeDtypeStruct((height, LANES), jnp.float32)] * 2,
        [VMEM, VMEM],
        [
            pltpu.VMEM((height, plan.width), dtype),
            pltpu.VMEM((columns, plan.width), dtype),
            pltpu.VMEM((height, columns), jnp.float32),
            pltpu.VMEM((height, LANES), dtype),
            pltpu.SemaphoreType.DMA((n_copies,)),
        ],
        2 * height * plan.width * columns,
        2 * plan.width * (height + columns),
        name,
    )


def expand_kernel(plan, kind, mine_ref, other_ref, tag_ref, ups, *rest):
    outs, (up, sems) = rest[:-2], rest[-2:]
    copies = Copies(am_outer(plan), sems)
    if kind == 0:
        copies.start(up, ups[0])
    else:
        for e, (wide, narrow) in enumerate(ups):
            for row, rows, column in plan.up_columns():
                part = pl.ds(plan.up_first, rows), pl.ds(column, plan.features)
                copies.start(
                    up.at[pl.ds(e * plan.left_rows + row, rows)],
                    of_wide(wide, plan.up_piece).at[part],
                    narrow[plan.up_piece].at[part],
                )
    share = plan.rank if kind == 0 else plan.share
    low = (mine_ref[...] + other_ref[...]).astype(jnp.bfloat16).astype(jnp.float32)
    tags = tag_ref[...]
    spread = [
        jnp.where(slot_mask(tags, first, plan.slots, share), low, 0.0).astype(jnp.bfloat16)
        for first in range(0, up.shape[0], LANES)
    ]
    spread = jnp.concatenate(spread, axis=1)
    copies.wait()
    delta = jnp.dot(spread, up[...], preferred_element_type=jnp.float32).astype(jnp.bfloat16)
    for i, out in enumerate(outs):
        out[...] = delta[i * PAIR : (i + 1) * PAIR]


def expand_rank(plan, kind, low, other, tag, ups, name):
    columns = plan.slots * plan.rank
    height = low.shape[0]
    return blocks_call(
        functools.partial(expand_kernel, plan, kind),
        plan,
        [ups],
        [jax.ShapeDtypeStruct((PAIR, plan.features), jnp.bfloat16)] * plan.half,
        [VMEM] * plan.half,
        [
            pltpu.VMEM((columns, plan.features), jnp.bfloat16),
            pltpu.SemaphoreType.DMA((plan.groups * len(list(plan.up_columns())),)),
        ],
        2 * height * columns * plan.features,
        2 * plan.features * (columns + height) + 12 * low.size,
        name,
        extra=(low, other, tag),
    )


def join_kernel(seg_ref, base_ref, *refs):
    deltas, out_ref = refs[:-1], refs[-1]
    for k in range(len(deltas) * CAP):
        part = k % CAP

        @pl.when(seg_ref[k] >= 0)
        def _():
            span = pl.ds(pl.multiple_of(seg_ref[k] * SEG, SEG), SEG)
            delta = deltas[k // CAP][part * SEG : (part + 1) * SEG, :]
            out_ref[span, :] = (base_ref[span, :] + delta.astype(jnp.float32)).astype(
                out_ref.dtype
            )


def join(seg_of, base, deltas):
    height, features = base.shape
    block = min(features, 512)
    tall = pl.BlockSpec((height, block), lambda j: (0, j))
    short = pl.BlockSpec((PAIR, block), lambda j: (0, j))
    return pl.pallas_call(
        join_kernel,
        grid=(features // block,),
        out_shape=jax.ShapeDtypeStruct((height, features), jnp.bfloat16),
        in_specs=[SMEM, tall] + [short] * len(deltas),
        out_specs=tall,
        compiler_params=params(),
        cost_estimate=pl.CostEstimate(
            flops=height * features, bytes_accessed=8 * height * features, transcendentals=0
        ),
        name="join",
    )(seg_of, base, *deltas)


def swap(value, axis, distance):
    count = lax.axis_size(axis)
    return lax.ppermute(value, axis, [(i, i ^ distance) for i in range(count)])


def send(plan, value, moves):
    pairs = [
        (g * plan.replicas + r, (g ^ group_distance) * plan.replicas + (r ^ replica_distance))
        for senders, group_distance, replica_distance in moves
        for g in range(plan.groups)
        for r in senders
    ]
    return lax.ppermute(value, ("groups", "replica"), pairs)


def on_device(x, weight, lefts, ups, ids, residency):
    slots, width, rank = lefts.shape
    features = ups.shape[2]
    plan = Plan(
        lax.axis_size("replica"), lax.axis_size("groups"), slots, rank, width, features
    )
    half, pieces = plan.half, plan.pieces
    left_rows = jnp.swapaxes(lefts, 1, 2)
    near, wide, narrow, seg_of = lay_out(plan, ids, residency, x, left_rows, ups)

    near = [near[0]] + [swap(near[i], "replica", d) for i, d in enumerate(plan.near) if d]
    wide_in = []
    for i in range(plan.wide):
        moves = []
        if i < len(plan.cross):
            moves.append((plan.outer, 0, plan.cross[i]))
        if 2 * i < pieces:
            moves.append((plan.inner, 0, half))
        wide_in.append(send(plan, wide[i], moves))

    partial_sum = jnp.dot(x, weight, preferred_element_type=jnp.float32)
    near, wide_in, narrow, partial_sum = lax.optimization_barrier(
        (near, wide_in, narrow, partial_sum)
    )
    narrow_in = []
    for j in range(plan.narrow):
        moves = []
        if j < 2 * len(plan.cross):
            moves.append((plan.inner, 0, plan.cross[j // 2]))
        if j < pieces:
            moves.append((plan.outer, 0, half))
        narrow_in.append(send(plan, narrow[j], moves))
    base = lax.psum_scatter(partial_sum, "tensor", scatter_dimension=1, tiled=True)

    shares = [(wide_in, narrow_in)]
    for e in range(1, plan.groups):
        shares.append(
            (
                [send(plan, block, [(plan.outer, e, 0)]) for block in wide_in[: -(-pieces // 2)]],
                [send(plan, block, [(plan.inner, e, 0)]) for block in narrow_in[:pieces]],
            )
        )

    deltas = []
    for kind, (left, up, name) in enumerate(
        [
            ([left_rows.reshape(slots * rank, width)], [ups.reshape(slots * rank, features)], "own"),
            (shares, shares, "taken"),
        ]
    ):
        if kind:
            left = [(w, n[: len(list(plan.left_spans()))]) for w, n in left]
        low, tag = reduce_rank(plan, kind, near, wide_in, narrow_in, left, "reduce_" + name)
        if kind:
            low, base = lax.optimization_barrier((low, base))
        other = swap(low, "tensor", 1)
        terms = expand_rank(plan, kind, low, other, tag, up, "expand_" + name)
        deltas.append(terms[0])
        deltas += [swap(terms[d], "replica", d) for d in range(1, half)]
    return join(seg_of, base, deltas)


def solution(mesh):
    placed = (
        P(("groups", "replica"), "tensor"),
        P("tensor", None),
        P("replica", "tensor", None),
        P("replica", None, "tensor"),
        P(("groups", "replica")),
        P(),
    )
    return jax.shard_map(
        on_device,
        mesh=mesh,
        in_specs=placed,
        out_specs=P(("groups", "replica"), "tensor"),
        check_vma=False,
    )
```

time: 210 us -> 168 us (0.80)
  blocking collectives: 110 us -> 0 us
  waiting for transfers between devices: 0.04 us -> 70.8 us
  matrix products: 52.9 us -> 14.9 us
  starting transfers between devices: 7.5 us -> 40.4 us
  Pallas kernels: 0 us -> 25.6 us
  local copies, waits for them, and re-layouts: 19.7 us -> 2.76 us
  other arithmetic: 5.21 us -> 0 us
    unnamed x1 -> x0, blocking collectives: 76.1 us -> none
    ppermute x0 -> x21, waiting for transfers between devices: none -> 70.8 us  [the longest x12 59.8 us: send(): return lax.ppermute(value, ('groups', 'replica'), pairs)]
    ppermute x0 -> x21, starting transfers between devices: none -> 40.4 us  [the longest x12 20.9 us: send(): return lax.ppermute(value, ('groups', 'replica'), pairs)]
    dot_general x7 -> x1, matrix products: 52.9 us -> 14.9 us  [on_device(): partial_sum = jnp.dot(x, weight, preferred_element_type=jnp.float32)]
    all_to_all x1 -> x0, blocking collectives: 29.7 us -> none  [on_device(): lax.all_to_all(adapter_delta, 'replica', split_axis=0, concat_axis=0, til...]
    pallas_call x0 -> x6, Pallas kernels: none -> 25.6 us  [the longest x4 15.6 us: blocks_call(): pl.pallas_call(body, out_shape=out_shape, in_specs=[VMEM] * n_extra + [HB...]
    reshape x3 -> x0, local copies, waits for them, and re-layouts: 17.6 us -> none  [the longest x2 17.6 us: on_device(): outgoing = outgoing.reshape(replicas, CAP, SEG, midpoint_feature_count)]
    all_to_all x1 -> x0, starting transfers between devices: 7.28 us -> none  [on_device(): lax.all_to_all(outgoing, 'replica', split_axis=0, concat_axis=0, tiled=True)]
  transfers between devices with their start and end apart: 2 -> 22, of which waited for: 0 -> 10; matrix products, arithmetic and copies ran while one was open for 22% -> 9% of each run, Pallas kernels for 0% -> 9%
where the time goes in v4:
time: 168 us
  waiting for transfers between devices  70.8 us (42%)
  starting transfers between devices  40.4 us (24%)
  Pallas kernels  25.6 us (15%)
  matrix products  14.9 us (9%)
  between operations  13.6 us (8%)
  local copies, waits for them, and re-layouts  2.76 us (2%)
    ppermute x12, waiting for transfers between devices, send(): return lax.ppermute(value, ('groups', 'replica'), pairs)  59.8 us
    ppermute x12, starting transfers between devices, send(): return lax.ppermute(value, ('groups', 'replica'), pairs)  20.9 us
    ppermute x9, starting transfers between devices, swap(): return lax.ppermute(value, axis, [(i, i ^ distance) for i in range(count)])  19.5 us
    pallas_call x4, Pallas kernels, blocks_call(): pl.pallas_call(body, out_shape=out_shape, in_specs=[VMEM] * n_extra + [HB...  15.6 us
    dot_general x1, matrix products, on_device(): partial_sum = jnp.dot(x, weight, preferred_element_type=jnp.float32)  14.9 us
    ppermute x9, waiting for transfers between devices, swap(): return lax.ppermute(value, axis, [(i, i ^ distance) for i in range(count)])  11 us
    pallas_call x1, Pallas kernels, lay_out(): pl.pallas_call(functools.partial(lay_kernel, plan), out_shape=[wide] * (l...  7.1 us
  transfers between devices with their start and end apart: 22, of which 10 were waited for; matrix products, arithmetic and copies ran while one was open for 9% of the time, Pallas kernels for 9%

profile of v4, /device:TPU:0, one launch (start us, length us, event | category | flops | bytes accessed | tf_op | source)
XLA Modules:
  0.0 168.1 jit_solution(17701684964467382008)
XLA Ops:
  6.5 7.1 %lay_out.1 = (bf16[128,4224]{1,0:T(8,128)(2,1)}, bf16[128,4224]{1,0:T(8,128)(2,1)}, bf16[128,4224]{1,0:T(8,128)(2,1)}, bf16[128,4224]{1,0:T(8,128)(2,1)}, bf16[6...) custom-call(s32[16]{0:T(128)} %ids_ref.1, ...), custom_call_target="tpu_custom_call" | custom-call | bytes 12582912 | tf_op jit(solution)/shard_map/lay_out/pallas_call | solution.py:171
  13.6 3.0 %collective-permute-start = (bf16[128,4224]{1,0:T(8,128)(2,1)}, bf16[128,4224]{1,0:T(8,128)(2,1)S(1)}, u32[]{:S(2)}, u32[]{:S(2)}) collective-permute-start(bf16[128,4224]{1,0:T(8,128)(2,1)} %get-tuple-element.39), channel_id=1, source_target_pairs={{0,2},{2,0},{4,6},{6,4},{8,10},{10,8},{12,14},{14,12},{1,3},{3,1},... | collective-permute-start | bytes 3244040 | tf_op jit(solution)/shard_map/ppermute | solution.py:418
  18.2 2.5 %collective-permute-start.2 = (bf16[128,4224]{1,0:T(8,128)(2,1)}, bf16[128,4224]{1,0:T(8,128)(2,1)S(1)}, u32[]{:S(2)}, u32[]{:S(2)}) collective-permute-start(bf16[128,4224]{1,0:T(8,128)(2,1)} %get-tuple-element.41), channel_id=1, source_target_pairs={{0,6},{2,4},{12,10},{14,8},{16,22},{18,20},{28,26},{30,24},{4,12},... | collective-permute-start | bytes 3244040 | tf_op jit(solution)/shard_map/ppermute | solution.py:428
  20.8 14.9 %fusion = f32[512,2048]{1,0:T(8,128)} fusion(bf16[512,4096]{1,0:T(8,128)(2,1)} %x_ref.1, bf16[4096,2048]{1,0:T(8,128)(2,1)} %param.7), kind=kOutput, calls=%fused_computation | convolution fusion | flops 8589934592 | bytes 25165824 | tf_op jit(solution)/shard_map/dot_general | solution.py:451
  35.7 5.0 %collective-permute-done.refs_1_ = bf16[128,4224]{1,0:T(8,128)(2,1)S(1)} collective-permute-done((bf16[128,4224]{1,0:T(8,128)(2,1)}, bf16[128,4224]{1,0:T(8,128)(2,1)S(1)}, u32[]{:S(2)}, u32[]{:S(2)}) %collective-permute-start) | collective-permute-done | bytes 1081376 | tf_op jit(solution)/shard_map/ppermute | solution.py:418
  40.7 3.8 %collective-permute-done.1.refs_2_.refs_8_.refs_3_ = bf16[128,4224]{1,0:T(8,128)(2,1)S(1)} collective-permute-done((bf16[128,4224]{1,0:T(8,128)(2,1)}, bf16[128,4224]{1,0:T(8,128)(2,1)S(1)}, u32[]{:S(2)}, u32[]{:S(2)}) %collective-permute-start.1) | collective-permute-done | bytes 1081376 | tf_op jit(solution)/shard_map/ppermute | solution.py:428
  44.6 21.7 %collective-permute-done.2.refs_3_.refs_9_.refs_4_ = bf16[128,4224]{1,0:T(8,128)(2,1)S(1)} collective-permute-done((bf16[128,4224]{1,0:T(8,128)(2,1)}, bf16[128,4224]{1,0:T(8,128)(2,1)S(1)}, u32[]{:S(2)}, u32[]{:S(2)}) %collective-permute-start.2) | collective-permute-done | bytes 1081376 | tf_op jit(solution)/shard_map/ppermute | solution.py:428
  66.3 1.7 collective-permute-start.3
  68.0 2.5 %collective-permute-start.4 = (bf16[64,4224]{1,0:T(8,128)(2,1)}, bf16[64,4224]{1,0:T(8,128)(2,1)S(1)}, u32[]{:S(2)}, u32[]{:S(2)}) collective-permute-start(bf16[64,4224]{1,0:T(8,128)(2,1)} %get-tuple-element.51), channel_id=1, source_target_pairs={{4,0},{6,2},{8,12},{10,14},{20,16},{22,18},{24,28},{26,30},{0,8},{... | collective-permute-start | bytes 1622024 | tf_op jit(solution)/shard_map/ppermute | solution.py:428
  71.2 3.5 %collective-permute-start.7 = (bf16[128,4224]{1,0:T(8,128)(2,1)S(1)}, bf16[128,4224]{1,0:T(8,128)(2,1)}, u32[]{:S(2)}, u32[]{:S(2)}) collective-permute-start(bf16[128,4224]{1,0:T(8,128)(2,1)S(1)} %collective-permute-done.1.refs_2_.refs_8_.refs_3_), channel_id=1, source_target_pairs={{0,16},{2,18},{12,28},{14,30},{16,0},{18,2},{28,12},{30,14},{1,17}... | collective-permute-start | bytes 3244040 | tf_op jit(solution)/shard_map/ppermute | solution.py:428
  74.7 7.1 %collective-permute-done.3.refs_4_.refs_10_.refs_5_ = bf16[64,4224]{1,0:T(8,128)(2,1)S(1)} collective-permute-done((bf16[64,4224]{1,0:T(8,128)(2,1)}, bf16[64,4224]{1,0:T(8,128)(2,1)S(1)}, u32[]{:S(2)}, u32[]{:S(2)}) %collective-permute-start.3) | collective-permute-done | bytes 540704 | tf_op jit(solution)/shard_map/ppermute | solution.py:428
  81.8 3.4 %collective-permute-start.8 = (bf16[128,4224]{1,0:T(8,128)(2,1)S(1)}, bf16[128,4224]{1,0:T(8,128)(2,1)}, u32[]{:S(2)}, u32[]{:S(2)}) collective-permute-start(bf16[128,4224]{1,0:T(8,128)(2,1)S(1)} %collective-permute-done.2.refs_3_.refs_9_.refs_4_), channel_id=1, source_target_pairs={{0,16},{2,18},{12,28},{14,30},{16,0},{18,2},{28,12},{30,14},{1,17}... | collective-permute-start | bytes 3244040 | tf_op jit(solution)/shard_map/ppermute | solution.py:428
  85.2 8.2 %collective-permute-done.4.refs_5_.refs_11_.refs_6_ = bf16[64,4224]{1,0:T(8,128)(2,1)S(1)} collective-permute-done((bf16[64,4224]{1,0:T(8,128)(2,1)}, bf16[64,4224]{1,0:T(8,128)(2,1)S(1)}, u32[]{:S(2)}, u32[]{:S(2)}) %collective-permute-start.4) | collective-permute-done | bytes 540704 | tf_op jit(solution)/shard_map/ppermute | solution.py:428
  94.1 10.8 %collective-permute-done.5.refs_6_.refs_12_.refs_7_ = bf16[64,4224]{1,0:T(8,128)(2,1)S(1)} collective-permute-done((bf16[64,4224]{1,0:T(8,128)(2,1)}, bf16[64,4224]{1,0:T(8,128)(2,1)S(1)}, u32[]{:S(2)}, u32[]{:S(2)}) %collective-permute-start.5) | collective-permute-done | bytes 540704 | tf_op jit(solution)/shard_map/ppermute | solution.py:428
  106.3 8.2 %collective-permute-done.6.refs_7_.refs_8_ = bf16[64,4224]{1,0:T(8,128)(2,1)} collective-permute-done((bf16[64,4224]{1,0:T(8,128)(2,1)}, bf16[64,4224]{1,0:T(8,128)(2,1)}, u32[]{:S(2)}, u32[]{:S(2)}) %collective-permute-start.6) | collective-permute-done | bytes 540704 | tf_op jit(solution)/shard_map/ppermute | solution.py:428
  118.2 4.3 %reduce_own.1 = (f32[256,128]{1,0:T(8,128)}, f32[256,128]{1,0:T(8,128)}) custom-call(bf16[128,4224]{1,0:T(8,128)(2,1)} %get-tuple-element.46.refs_0_, bf16[128,4224]{1,0:T(8,128)(2,1)} %copy-done.5, bf16[128,4224]{1,0:T(8,128)(2,1)} %copy-done, bf16[128,4224]{1,0:T(8,128)(2,1)} %copy-done.1, bf16[64,4224]{1,0:T(8,128)(2,1)} %copy-done.2, ...), custom_call_target="tpu_custom_call" | custom-call | flops 805306368 | bytes 5242880 | tf_op jit(solution)/shard_map/reduce_own/pallas_call | solution.py:298
  122.7 4.3 %reduce_taken.1 = (f32[256,128]{1,0:T(8,128)}, f32[256,128]{1,0:T(8,128)}) custom-call(bf16[128,4224]{1,0:T(8,128)(2,1)} %get-tuple-element.46.refs_0_, bf16[128,4224]{1,0:T(8,128)(2,1)} %copy-done.5, bf16[128,4224]{1,0:T(8,128)(2,1)} %copy-done, bf16[128,4224]{1,0:T(8,128)(2,1)} %copy-done.1, bf16[64,4224]{1,0:T(8,128)(2,1)} %copy-done.2, ...), custom_call_target="tpu_custom_call" | custom-call | flops 805306368 | bytes 5242880 | tf_op jit(solution)/shard_map/reduce_taken/pallas_call | solution.py:298
  128.2 3.4 %expand_own.1 = (bf16[64,1024]{1,0:T(8,128)(2,1)}, bf16[64,1024]{1,0:T(8,128)(2,1)}, bf16[64,1024]{1,0:T(8,128)(2,1)}, bf16[64,1024]{1,0:T(8,128)(2,1)}) custom-call(f32[256,128]{1,0:T(8,128)} %get-tuple-element.57.refs_0_, f32[256,128]{1,0:T(8,128)} %copy-done.13, f32[256,128]{1,0:T(8,128)} %get-tuple-element.58.refs_2_, bf16[384,1024]{1,0:T(8,128)(2,1)} %bitcast.8), custom_call_target="tpu_custom_call" | custom-call | flops 201326592 | bytes 1703936 | tf_op jit(solution)/shard_map/expand_own/pallas_call | solution.py:298
  133.0 10.1 %collective-permute-start.14 = (bf16[64,1024]{1,0:T(8,128)(2,1)}, bf16[64,1024]{1,0:T(8,128)(2,1)S(1)}, u32[]{:S(2)}, u32[]{:S(2)}) collective-permute-start(bf16[64,1024]{1,0:T(8,128)(2,1)} %get-tuple-element.61), channel_id=1, source_target_pairs={{0,4},{2,6},{4,0},{6,2},{8,12},{10,14},{12,8},{14,10},{1,5},{3,7},... | collective-permute-start | bytes 393224 | tf_op jit(solution)/shard_map/ppermute | solution.py:418
  144.6 3.5 %expand_taken.1 = (bf16[64,1024]{1,0:T(8,128)(2,1)}, bf16[64,1024]{1,0:T(8,128)(2,1)}, bf16[64,1024]{1,0:T(8,128)(2,1)}, bf16[64,1024]{1,0:T(8,128)(2,1)}) custom-call(f32[256,128]{1,0:T(8,128)} %get-tuple-element.63.refs_0_, f32[256,128]{1,0:T(8,128)} %copy-done.7, f32[256,128]{1,0:T(8,128)} %get-tuple-element.64.refs_2_, bf16[128,4224]{1,0:T(8,128)(2,1)} %copy-done, ...), custom_call_target="tpu_custom_call" | custom-call | flops 201326592 | bytes 1703936 | tf_op jit(solution)/shard_map/expand_taken/pallas_call | solution.py:298
  148.8 2.0 %collective-permute-start.19 = (bf16[64,1024]{1,0:T(8,128)(2,1)}, bf16[64,1024]{1,0:T(8,128)(2,1)S(1)}, u32[]{:S(2)}, u32[]{:S(2)}) collective-permute-start(bf16[64,1024]{1,0:T(8,128)(2,1)} %get-tuple-element.67), channel_id=1, source_target_pairs={{0,4},{2,6},{4,0},{6,2},{8,12},{10,14},{12,8},{14,10},{1,5},{3,7},... | collective-permute-start | bytes 393224 | tf_op jit(solution)/shard_map/ppermute | solution.py:418
  151.7 2.0 %collective-permute-done.18.refs_5_ = bf16[64,1024]{1,0:T(8,128)(2,1)S(1)} collective-permute-done((bf16[64,1024]{1,0:T(8,128)(2,1)}, bf16[64,1024]{1,0:T(8,128)(2,1)S(1)}, u32[]{:S(2)}, u32[]{:S(2)}) %collective-permute-start.18) | collective-permute-done | bytes 131104 | tf_op jit(solution)/shard_map/ppermute | solution.py:418
  154.8 2.9 %collective-permute-done.20.refs_7_ = bf16[64,1024]{1,0:T(8,128)(2,1)S(1)} collective-permute-done((bf16[64,1024]{1,0:T(8,128)(2,1)}, bf16[64,1024]{1,0:T(8,128)(2,1)S(1)}, u32[]{:S(2)}, u32[]{:S(2)}) %collective-permute-start.20) | collective-permute-done | bytes 131104 | tf_op jit(solution)/shard_map/ppermute | solution.py:418
  158.3 2.9 %join.1 = bf16[512,1024]{1,0:T(8,128)(2,1)} custom-call(s32[16]{0:T(128)} %get-tuple-element.37.seg_ref, f32[512,1024]{1,0:T(8,128)} %reduce-scatter.2.cloned.1.call-done.base_ref, bf16[64,1024]{1,0:T(8,128)(2,1)} %get-tuple-element.59.refs_0_, bf16[64,1024]{1,0:T(8,128)(2,1)} %copy-done.8, bf16[64,1024]{1,0:T(8,128)(2,1)} %copy-done.9, ...), custom_call_target="tpu_custom_call" | custom-call | flops 524288 | bytes 4194304 | tf_op jit(solution)/shard_map/join/pallas_call | solution.py:402
  (58 shorter events, 15.5 us)
Async XLA Ops:
  6.5 120.5 %reduce-scatter.2.cloned.1.call-start = ((), (), s32[]{:S(2)}) async-start(), calls=%async_computation.1 | async-start | bytes 6291456 | tf_op jit(solution)/shard_map/reduce_scatter | solution.py:463
  13.6 27.1 %collective-permute-start = (bf16[128,4224]{1,0:T(8,128)(2,1)}, bf16[128,4224]{1,0:T(8,128)(2,1)S(1)}, u32[]{:S(2)}, u32[]{:S(2)}) collective-permute-start(bf16[128,4224]{1,0:T(8,128)(2,1)} %get-tuple-element.39), channel_id=1, source_target_pairs={{0,2},{2,0},{4,6},{6,4},{8,10},{10,8},{12,14},{14,12},{1,3},{3,1},... | collective-permute-start | bytes 3244040 | tf_op jit(solution)/shard_map/ppermute | solution.py:418
  16.7 27.9 %collective-permute-start.1 = (bf16[128,4224]{1,0:T(8,128)(2,1)}, bf16[128,4224]{1,0:T(8,128)(2,1)S(1)}, u32[]{:S(2)}, u32[]{:S(2)}) collective-permute-start(bf16[128,4224]{1,0:T(8,128)(2,1)} %get-tuple-element.40), channel_id=1, source_target_pairs={{0,4},{2,6},{12,8},{14,10},{16,20},{18,22},{28,24},{30,26},{4,12},... | collective-permute-start | bytes 3244040 | tf_op jit(solution)/shard_map/ppermute | solution.py:428
  18.2 48.0 %collective-permute-start.2 = (bf16[128,4224]{1,0:T(8,128)(2,1)}, bf16[128,4224]{1,0:T(8,128)(2,1)S(1)}, u32[]{:S(2)}, u32[]{:S(2)}) collective-permute-start(bf16[128,4224]{1,0:T(8,128)(2,1)} %get-tuple-element.41), channel_id=1, source_target_pairs={{0,6},{2,4},{12,10},{14,8},{16,22},{18,20},{28,26},{30,24},{4,12},... | collective-permute-start | bytes 3244040 | tf_op jit(solution)/shard_map/ppermute | solution.py:428
  44.6 73.6 %copy-start = (bf16[128,4224]{1,0:T(8,128)(2,1)}, bf16[128,4224]{1,0:T(8,128)(2,1)S(1)}, u32[]{:S(2)}) copy-start(bf16[128,4224]{1,0:T(8,128)(2,1)S(1)} %collective-permute-done.1.refs_2_.refs_8_.refs_3_) | copy-start | bytes 3244036
  66.3 51.9 %copy-start.1 = (bf16[128,4224]{1,0:T(8,128)(2,1)}, bf16[128,4224]{1,0:T(8,128)(2,1)S(1)}, u32[]{:S(2)}) copy-start(bf16[128,4224]{1,0:T(8,128)(2,1)S(1)} %collective-permute-done.2.refs_3_.refs_9_.refs_4_) | copy-start | bytes 3244036
  66.3 15.5 %collective-permute-start.3 = (bf16[64,4224]{1,0:T(8,128)(2,1)}, bf16[64,4224]{1,0:T(8,128)(2,1)S(1)}, u32[]{:S(2)}, u32[]{:S(2)}) collective-permute-start(bf16[64,4224]{1,0:T(8,128)(2,1)} %get-tuple-element.50), channel_id=1, source_target_pairs={{4,0},{6,2},{8,12},{10,14},{20,16},{22,18},{24,28},{26,30},{0,8},{... | collective-permute-start | bytes 1622024 | tf_op jit(solution)/shard_map/ppermute | solution.py:428
  68.0 25.4 %collective-permute-start.4 = (bf16[64,4224]{1,0:T(8,128)(2,1)}, bf16[64,4224]{1,0:T(8,128)(2,1)S(1)}, u32[]{:S(2)}, u32[]{:S(2)}) collective-permute-start(bf16[64,4224]{1,0:T(8,128)(2,1)} %get-tuple-element.51), channel_id=1, source_target_pairs={{4,0},{6,2},{8,12},{10,14},{20,16},{22,18},{24,28},{26,30},{0,8},{... | collective-permute-start | bytes 1622024 | tf_op jit(solution)/shard_map/ppermute | solution.py:428
  70.5 34.3 %collective-permute-start.5 = (bf16[64,4224]{1,0:T(8,128)(2,1)}, bf16[64,4224]{1,0:T(8,128)(2,1)S(1)}, u32[]{:S(2)}, u32[]{:S(2)}) collective-permute-start(bf16[64,4224]{1,0:T(8,128)(2,1)} %get-tuple-element.52), channel_id=1, source_target_pairs={{4,2},{6,0},{8,14},{10,12},{20,18},{22,16},{24,30},{26,28},{0,8},{... | collective-permute-start | bytes 1622024 | tf_op jit(solution)/shard_map/ppermute | solution.py:428
  70.6 43.9 %collective-permute-start.6 = (bf16[64,4224]{1,0:T(8,128)(2,1)}, bf16[64,4224]{1,0:T(8,128)(2,1)}, u32[]{:S(2)}, u32[]{:S(2)}) collective-permute-start(bf16[64,4224]{1,0:T(8,128)(2,1)} %get-tuple-element.53), channel_id=1, source_target_pairs={{4,2},{6,0},{8,14},{10,12},{20,18},{22,16},{24,30},{26,28},{0,8},{... | collective-permute-start | bytes 1622024 | tf_op jit(solution)/shard_map/ppermute | solution.py:428
  71.2 51.5 %collective-permute-start.7 = (bf16[128,4224]{1,0:T(8,128)(2,1)S(1)}, bf16[128,4224]{1,0:T(8,128)(2,1)}, u32[]{:S(2)}, u32[]{:S(2)}) collective-permute-start(bf16[128,4224]{1,0:T(8,128)(2,1)S(1)} %collective-permute-done.1.refs_2_.refs_8_.refs_3_), channel_id=1, source_target_pairs={{0,16},{2,18},{12,28},{14,30},{16,0},{18,2},{28,12},{30,14},{1,17}... | collective-permute-start | bytes 3244040 | tf_op jit(solution)/shard_map/ppermute | solution.py:428
  81.8 40.9 %collective-permute-start.8 = (bf16[128,4224]{1,0:T(8,128)(2,1)S(1)}, bf16[128,4224]{1,0:T(8,128)(2,1)}, u32[]{:S(2)}, u32[]{:S(2)}) collective-permute-start(bf16[128,4224]{1,0:T(8,128)(2,1)S(1)} %collective-permute-done.2.refs_3_.refs_9_.refs_4_), channel_id=1, source_target_pairs={{0,16},{2,18},{12,28},{14,30},{16,0},{18,2},{28,12},{30,14},{1,17}... | collective-permute-start | bytes 3244040 | tf_op jit(solution)/shard_map/ppermute | solution.py:428
  93.4 22.6 %collective-permute-start.9 = (bf16[64,4224]{1,0:T(8,128)(2,1)S(1)}, bf16[64,4224]{1,0:T(8,128)(2,1)S(1)}, u32[]{:S(2)}, u32[]{:S(2)}) collective-permute-start(bf16[64,4224]{1,0:T(8,128)(2,1)S(1)} %collective-permute-done.3.refs_4_.refs_10_.refs_5_), channel_id=1, source_target_pairs={{4,20},{6,22},{8,24},{10,26},{20,4},{22,6},{24,8},{26,10},{5,21},{... | collective-permute-start | bytes 1622024 | tf_op jit(solution)/shard_map/ppermute | solution.py:428
  104.8 17.7 %collective-permute-start.10 = (bf16[64,4224]{1,0:T(8,128)(2,1)S(1)}, bf16[64,4224]{1,0:T(8,128)(2,1)}, u32[]{:S(2)}, u32[]{:S(2)}) collective-permute-start(bf16[64,4224]{1,0:T(8,128)(2,1)S(1)} %collective-permute-done.4.refs_5_.refs_11_.refs_6_), channel_id=1, source_target_pairs={{4,20},{6,22},{8,24},{10,26},{20,4},{22,6},{24,8},{26,10},{5,21},{... | collective-permute-start | bytes 1622024 | tf_op jit(solution)/shard_map/ppermute | solution.py:428
  114.5 8.2 %collective-permute-start.11 = (bf16[64,4224]{1,0:T(8,128)(2,1)S(1)}, bf16[64,4224]{1,0:T(8,128)(2,1)}, u32[]{:S(2)}, u32[]{:S(2)}) collective-permute-start(bf16[64,4224]{1,0:T(8,128)(2,1)S(1)} %collective-permute-done.5.refs_6_.refs_12_.refs_7_), channel_id=1, source_target_pairs={{4,20},{6,22},{8,24},{10,26},{20,4},{22,6},{24,8},{26,10},{5,21},{... | collective-permute-start | bytes 1622024 | tf_op jit(solution)/shard_map/ppermute | solution.py:428
  116.8 27.2 %collective-permute-start.17 = (bf16[64,4224]{1,0:T(8,128)(2,1)}, bf16[64,4224]{1,0:T(8,128)(2,1)}, u32[]{:S(2)}, u32[]{:S(2)}) collective-permute-start(bf16[64,4224]{1,0:T(8,128)(2,1)} %collective-permute-done.6.refs_7_.refs_8_), channel_id=1, source_target_pairs={{4,20},{6,22},{8,24},{10,26},{20,4},{22,6},{24,8},{26,10},{5,21},{... | collective-permute-start | bytes 1622024 | tf_op jit(solution)/shard_map/ppermute | solution.py:428
  122.6 5.0 %collective-permute-start.12 = (f32[256,128]{1,0:T(8,128)}, f32[256,128]{1,0:T(8,128)S(1)}, u32[]{:S(2)}, u32[]{:S(2)}) collective-permute-start(f32[256,128]{1,0:T(8,128)} %get-tuple-element.57.refs_0_), channel_id=1, source_target_pairs={{0,1},{1,0},{2,3},{3,2},{4,5},{5,4},{6,7},{7,6},{8,9},{9,8},{10,11... | collective-permute-start | bytes 393224 | tf_op jit(solution)/shard_map/ppermute | solution.py:418
  127.0 16.9 %collective-permute-start.16 = (f32[256,128]{1,0:T(8,128)}, f32[256,128]{1,0:T(8,128)S(1)}, u32[]{:S(2)}, u32[]{:S(2)}) collective-permute-start(f32[256,128]{1,0:T(8,128)} %get-tuple-element.63.refs_0_), channel_id=1, source_target_pairs={{0,1},{1,0},{2,3},{3,2},{4,5},{5,4},{6,7},{7,6},{8,9},{9,8},{10,11... | collective-permute-start | bytes 393224 | tf_op jit(solution)/shard_map/ppermute | solution.py:418
  131.6 19.1 %collective-permute-start.13 = (bf16[64,1024]{1,0:T(8,128)(2,1)}, bf16[64,1024]{1,0:T(8,128)(2,1)S(1)}, u32[]{:S(2)}, u32[]{:S(2)}) collective-permute-start(bf16[64,1024]{1,0:T(8,128)(2,1)} %get-tuple-element.60), channel_id=1, source_target_pairs={{0,2},{2,0},{4,6},{6,4},{8,10},{10,8},{12,14},{14,12},{1,3},{3,1},... | collective-permute-start | bytes 393224 | tf_op jit(solution)/shard_map/ppermute | solution.py:418
  133.0 18.7 %collective-permute-start.14 = (bf16[64,1024]{1,0:T(8,128)(2,1)}, bf16[64,1024]{1,0:T(8,128)(2,1)S(1)}, u32[]{:S(2)}, u32[]{:S(2)}) collective-permute-start(bf16[64,1024]{1,0:T(8,128)(2,1)} %get-tuple-element.61), channel_id=1, source_target_pairs={{0,4},{2,6},{4,0},{6,2},{8,12},{10,14},{12,8},{14,10},{1,5},{3,7},... | collective-permute-start | bytes 393224 | tf_op jit(solution)/shard_map/ppermute | solution.py:418
  143.1 8.7 %collective-permute-start.15 = (bf16[64,1024]{1,0:T(8,128)(2,1)}, bf16[64,1024]{1,0:T(8,128)(2,1)S(1)}, u32[]{:S(2)}, u32[]{:S(2)}) collective-permute-start(bf16[64,1024]{1,0:T(8,128)(2,1)} %get-tuple-element.62), channel_id=1, source_target_pairs={{0,6},{2,4},{4,2},{6,0},{8,14},{10,12},{12,10},{14,8},{1,7},{3,5},... | collective-permute-start | bytes 393224 | tf_op jit(solution)/shard_map/ppermute | solution.py:418
  148.1 5.7 %collective-permute-start.18 = (bf16[64,1024]{1,0:T(8,128)(2,1)}, bf16[64,1024]{1,0:T(8,128)(2,1)S(1)}, u32[]{:S(2)}, u32[]{:S(2)}) collective-permute-start(bf16[64,1024]{1,0:T(8,128)(2,1)} %get-tuple-element.66), channel_id=1, source_target_pairs={{0,2},{2,0},{4,6},{6,4},{8,10},{10,8},{12,14},{14,12},{1,3},{3,1},... | collective-permute-start | bytes 393224 | tf_op jit(solution)/shard_map/ppermute | solution.py:418
  148.8 6.0 %collective-permute-start.19 = (bf16[64,1024]{1,0:T(8,128)(2,1)}, bf16[64,1024]{1,0:T(8,128)(2,1)S(1)}, u32[]{:S(2)}, u32[]{:S(2)}) collective-permute-start(bf16[64,1024]{1,0:T(8,128)(2,1)} %get-tuple-element.67), channel_id=1, source_target_pairs={{0,4},{2,6},{4,0},{6,2},{8,12},{10,14},{12,8},{14,10},{1,5},{3,7},... | collective-permute-start | bytes 393224 | tf_op jit(solution)/shard_map/ppermute | solution.py:418
  150.8 6.9 %collective-permute-start.20 = (bf16[64,1024]{1,0:T(8,128)(2,1)}, bf16[64,1024]{1,0:T(8,128)(2,1)S(1)}, u32[]{:S(2)}, u32[]{:S(2)}) collective-permute-start(bf16[64,1024]{1,0:T(8,128)(2,1)} %get-tuple-element.68), channel_id=1, source_target_pairs={{0,6},{2,4},{4,2},{6,0},{8,14},{10,12},{12,10},{14,8},{1,7},{3,5},... | collective-permute-start | bytes 393224 | tf_op jit(solution)/shard_map/ppermute | solution.py:418
  (13 other events, 128.6 us)
Sparse Core Ops, SparseCore 0:
  66.4 12.3 reduce-scatter.1

commit v5 on v4

v5 whole, which is shorter than its diff:
```python
import functools

import jax
import jax.numpy as jnp
from jax import lax
from jax.experimental import pallas as pl
from jax.experimental.pallas import tpu as pltpu
from jax.sharding import PartitionSpec as P

CAP = 2
SEG = 32
LANES = 128
PAIR = CAP * SEG
VMEM_LIMIT = 24 * 1024 * 1024
HBM = pl.BlockSpec(memory_space=pltpu.HBM)
SMEM = pl.BlockSpec(memory_space=pltpu.SMEM)
VMEM = pl.BlockSpec(memory_space=pltpu.VMEM)


class Plan:
    def __init__(self, replicas, groups, slots, rank, width, features):
        self.replicas, self.groups, self.slots, self.rank = replicas, groups, slots, rank
        self.width, self.features = width, features
        self.half = replicas // 2
        self.turn = self.half // 2
        self.near = [d for d in range(self.half) if not d & self.turn]
        self.cross = [d for d in range(self.half) if d & self.turn]
        self.share = rank // groups
        self.left_rows = slots * self.share
        self.padded = -(-self.left_rows // LANES) * LANES
        beside = width // features
        self.up_rows = -(-self.left_rows // (beside * 16)) * 16
        self.left_pieces = -(-self.left_rows // PAIR)
        self.pieces = self.left_pieces + 1
        assert self.up_rows <= PAIR
        self.adapter_wide = -(-self.pieces // 2)
        self.wide = max(len(self.cross), self.adapter_wide)
        self.narrow = max(2 * len(self.cross), self.pieces)
        self.outer = [r for r in range(replicas) if self.is_outer(r)]
        self.inner = [r for r in range(replicas) if not self.is_outer(r)]

    def is_outer(self, r):
        return (r < self.turn) or (r >= self.replicas - self.turn)

    def up_columns(self):
        for j, row in enumerate(range(0, self.left_rows, self.up_rows)):
            yield row, min(self.up_rows, self.left_rows - row), j * self.features

    def left_spans(self):
        for piece in range(self.left_pieces):
            yield piece, min(PAIR, self.left_rows - piece * PAIR)

    def narrow_rows(self, i, kind):
        return kind * len(self.cross) + i


def params(limit=VMEM_LIMIT):
    return pltpu.CompilerParams(vmem_limit_bytes=limit)


def am_outer(plan):
    me = lax.axis_index("replica")
    return (me < plan.turn) | (me >= plan.replicas - plan.turn)


def of_wide(refs, piece):
    return refs[piece // 2].at[pl.ds((piece % 2) * PAIR, PAIR)]


def narrow_adapters(narrow, piece, plan):
    return narrow[0] if piece == plan.left_pieces else narrow[1 + piece]


def lay_kernel(plan, first_call, ids_ref, residency_ref, x_ref, left_ref, up_ref, *rest):
    n_near = len(plan.near) - 1 if first_call else 1
    n_blocks = plan.wide if first_call else plan.narrow
    near, rest = rest[:n_near], rest[n_near:]
    blocks, rest = rest[:n_blocks], rest[n_blocks:]
    seg_out, seg_ref, slot_ref, count_ref, staged, tags, left, up, in_sems, sems = rest
    half, slots, width, share = plan.half, plan.slots, plan.width, plan.share
    me = lax.axis_index("replica")
    first = pl.multiple_of(lax.axis_index("groups") * share, share)
    outer = am_outer(plan)
    rows_outer = outer if first_call else jnp.logical_not(outer)

    for h in range(plan.replicas):
        count_ref[h] = 0
        for p in range(CAP):
            seg_ref[h * CAP + p] = -1
            slot_ref[h * CAP + p] = 0
    for s in range(ids_ref.shape[0]):
        adapter = ids_ref[s]
        holder = adapter // slots
        place = holder * CAP + count_ref[holder]
        count_ref[holder] = count_ref[holder] + 1
        seg_ref[place] = s
        slot_ref[place] = residency_ref[adapter] - holder * slots
    for d in range(half):
        for kind in range(2):
            for p in range(CAP):
                seg_out[(kind * half + d) * CAP + p] = seg_ref[
                    (me ^ (d + kind * half)) * CAP + p
                ]

    def move(moves, tagged):
        arrivals = []
        for source, stage, _ in moves:
            arrivals.append(pltpu.make_async_copy(source, stage, in_sems.at[len(arrivals)]))
            arrivals[-1].start()
        departures = []

        def depart(source, target):
            departures.append(pltpu.make_async_copy(source, target, sems.at[len(departures)]))
            departures[-1].start()

        for d, kind, target in tagged:
            for p in range(CAP):
                slot = slot_ref[(me ^ (d + kind * half)) * CAP + p].astype(jnp.float32)
                tags[d, pl.ds((kind * CAP + p) * SEG, SEG), :] = jnp.full(
                    (SEG, LANES), slot, jnp.float32
                ).astype(tags.dtype)
        for d, kind, target in tagged:
            depart(tags.at[d, pl.ds(kind * PAIR, PAIR)], target.at[:, pl.ds(width, LANES)])
        for arrival, (_, stage, target) in zip(arrivals, moves):
            arrival.wait()
            if target is not None:
                for part, place in target:
                    depart(part, place)
        for departure in departures:
            departure.wait()

    def row_moves(targets):
        moves = []
        for d, kind, target in targets:
            for p in range(CAP):
                seg = jnp.maximum(seg_out[(kind * half + d) * CAP + p], 0)
                stage = staged.at[pl.ds(((kind * half + d) * CAP + p) * SEG, SEG)]
                moves.append(
                    (
                        x_ref.at[pl.ds(pl.multiple_of(seg * SEG, SEG), SEG)],
                        stage,
                        [(stage, target.at[pl.ds(p * SEG, SEG), pl.ds(0, width)])],
                    )
                )
        return moves

    def adapter_moves(target_of):
        moves = []
        for slot in range(slots):
            span = pl.ds(slot * share, share)
            source = pl.ds(first, share)
            moves.append((up_ref.at[slot, source], up.at[span], None))
            moves.append((left_ref.at[slot, source], left.at[span], None))
        outs = [
            (
                up.at[pl.ds(row, rows)],
                target_of(plan.left_pieces).at[pl.ds(0, rows), pl.ds(column, plan.features)],
            )
            for row, rows, column in plan.up_columns()
        ]
        outs += [
            (
                left.at[pl.ds(piece * PAIR, rows)],
                target_of(piece).at[pl.ds(0, rows), pl.ds(0, width)],
            )
            for piece, rows in plan.left_spans()
        ]
        source, stage, _ = moves[-1]
        moves[-1] = (source, stage, outs)
        return moves

    near_d = plan.near[1:] if first_call else plan.near[:1]
    near_targets = [
        (d, kind, near[i].at[pl.ds(kind * PAIR, PAIR)])
        for i, d in enumerate(near_d)
        for kind in range(2)
    ]
    if first_call:
        cross_targets = [
            (d, kind, of_wide(blocks, 2 * i + kind))
            for i, d in enumerate(plan.cross)
            for kind in range(2)
        ]
    else:
        cross_targets = [
            (d, kind, blocks[plan.narrow_rows(i, kind)])
            for i, d in enumerate(plan.cross)
            for kind in range(2)
        ]

    @pl.when(rows_outer)
    def _():
        targets = cross_targets + near_targets
        move(row_moves(targets), targets)

    @pl.when(jnp.logical_not(rows_outer))
    def _():
        if first_call:
            adapters = adapter_moves(lambda piece: of_wide(blocks, piece))
        else:
            adapters = adapter_moves(lambda piece: narrow_adapters(blocks, piece, plan))
        move(adapters + row_moves(near_targets), near_targets)


def lay_out(plan, first_call, ids, residency, x, left_rows, ups):
    count = 2 * plan.half * CAP
    wide = jax.ShapeDtypeStruct((2 * PAIR, plan.width + LANES), x.dtype)
    narrow = jax.ShapeDtypeStruct((PAIR, plan.width + LANES), x.dtype)
    near = [wide] * (len(plan.near) - 1 if first_call else 1)
    blocks = [wide] * plan.wide if first_call else [narrow] * plan.narrow
    out = pl.pallas_call(
        functools.partial(lay_kernel, plan, first_call),
        out_shape=near + blocks + [jax.ShapeDtypeStruct((count,), jnp.int32)],
        in_specs=[SMEM, SMEM, HBM, HBM, HBM],
        out_specs=[HBM] * (len(near) + len(blocks)) + [SMEM],
        scratch_shapes=[
            pltpu.SMEM((plan.replicas * CAP,), jnp.int32),
            pltpu.SMEM((plan.replicas * CAP,), jnp.int32),
            pltpu.SMEM((plan.replicas,), jnp.int32),
            pltpu.VMEM((count * SEG, plan.width), x.dtype),
            pltpu.VMEM((plan.half, 2 * PAIR, LANES), x.dtype),
            pltpu.VMEM((plan.left_rows, plan.width), x.dtype),
            pltpu.VMEM((plan.left_rows, plan.features), x.dtype),
            pltpu.SemaphoreType.DMA((count + 2 * plan.slots,)),
            pltpu.SemaphoreType.DMA((2 * count + 2 * plan.pieces,)),
        ],
        compiler_params=params(60 * 1024 * 1024),
        cost_estimate=pl.CostEstimate(
            flops=0, bytes_accessed=3 * x.size, transcendentals=0
        ),
        name="lay_out_first" if first_call else "lay_out_second",
    )(ids, residency, x, left_rows, ups)
    return list(out[: len(near)]), list(out[len(near) : -1]), out[-1]


def slot_mask(tags, first, columns, slots, share):
    lane = lax.broadcasted_iota(jnp.int32, (1, LANES), 1)
    column_slot = jnp.zeros((1, LANES), jnp.float32)
    for j in range(0, LANES, share):
        slot = (first + j) // share if first + j < columns else -1
        column_slot = jnp.where(lane >= j, float(slot), column_slot)
    return tags == column_slot


class Copies:
    def __init__(self, outer, sems):
        self.outer, self.sems, self.waits = outer, sems, []

    def both(self, target, outer_source, inner_source=None):
        sem = self.sems.at[len(self.waits)]
        copy = pltpu.make_async_copy(outer_source, target, sem)
        if inner_source is None:
            copy.start()
        else:
            pl.when(self.outer)(copy.start)
            pl.when(jnp.logical_not(self.outer))(
                pltpu.make_async_copy(inner_source, target, sem).start
            )
        self.waits.append((None, copy))

    def one(self, wanted, target, source):
        copy = pltpu.make_async_copy(source, target, self.sems.at[len(self.waits)])
        pl.when(wanted)(copy.start)
        self.waits.append((wanted, copy))

    def wait(self):
        for wanted, copy in self.waits:
            if wanted is None:
                copy.wait()
            else:
                pl.when(wanted)(copy.wait)


def fold(product, tags, columns, slots, share):
    total = jnp.zeros(tags.shape, jnp.float32)
    for first in range(0, product.shape[1], LANES):
        mask = slot_mask(tags, first, columns, slots, share)
        total += jnp.where(mask, product[:, first : first + LANES], 0.0)
    return total


def copy_rows(copies, plan, kind, target, columns, near, wide, narrow):
    span = pl.ds(kind * PAIR, PAIR)
    for i, d in enumerate(plan.near):
        copies.both(target.at[pl.ds(d * PAIR, PAIR)], near[i].at[span, columns])
    for i, d in enumerate(plan.cross):
        copies.both(
            target.at[pl.ds(d * PAIR, PAIR)],
            narrow[plan.narrow_rows(i, kind)].at[:, columns],
            wide[i].at[span, columns],
        )


def product_of(rows, left):
    return lax.dot_general(
        rows, left, (((1,), (1,)), ((), ())), preferred_element_type=jnp.float32
    )


def reduce_own_kernel(plan, n_steps, near, wide, narrow, own, low_ref, tag_ref, *scratch):
    rows, left, acc, tag, sems = scratch
    block = plan.width // n_steps
    outer = am_outer(plan)
    each = plan.half + 1
    steps = []
    for k in range(n_steps + 1):
        copies = Copies(outer, sems.at[pl.ds(k * each, each)])
        columns = pl.ds(k * block, block) if k < n_steps else pl.ds(plan.width, LANES)
        target = rows.at[:, columns] if k < n_steps else tag
        copy_rows(copies, plan, 0, target, columns, near, wide, narrow)
        if k < n_steps:
            copies.both(left.at[:, columns], own.at[:, columns])
        steps.append(copies)
    for k in range(n_steps):
        steps[k].wait()
        columns = pl.ds(k * block, block)
        product = product_of(rows[:, columns], left[:, columns])
        acc[...] = acc[...] + product if k else product
    steps[n_steps].wait()
    tags = tag[...].astype(jnp.float32)
    tag_ref[...] = tags
    low_ref[...] = fold(acc, tags, acc.shape[1], plan.slots, plan.rank)


def reduce_taken_kernel(plan, n_steps, near, wide, narrow, across, *rest):
    lows, tag_ref = rest[: plan.groups], rest[plan.groups]
    rows, left, acc, tag, sems = rest[plan.groups + 1 :]
    block = plan.width // n_steps
    outer = am_outer(plan)
    inner = jnp.logical_not(outer)
    more = plan.groups - 1
    each = plan.half + plan.left_pieces + more * (plan.half + plan.left_pieces)
    steps = []
    for k in range(n_steps + 1):
        copies = Copies(outer, sems.at[pl.ds(k * each, each)])
        columns = pl.ds(k * block, block) if k < n_steps else pl.ds(plan.width, LANES)
        target = rows.at[0, :, columns] if k < n_steps else tag.at[0]
        copy_rows(copies, plan, 1, target, columns, near, wide, narrow)
        for e in range(1, plan.groups):
            for i, d in enumerate(plan.near + plan.cross):
                target = rows.at[e, :, columns] if k < n_steps else tag.at[e]
                copies.one(
                    inner,
                    target.at[pl.ds(d * PAIR, PAIR)],
                    of_wide(across[e - 1], i).at[:, columns],
                )
        if k < n_steps:
            for piece, count in plan.left_spans():
                span = pl.ds(0, count), columns
                copies.both(
                    left.at[0, pl.ds(piece * PAIR, count), columns],
                    of_wide(wide, piece).at[span],
                    narrow_adapters(narrow, piece, plan).at[span],
                )
                for e in range(1, plan.groups):
                    copies.one(
                        outer,
                        left.at[e, pl.ds(piece * PAIR, count), columns],
                        of_wide(across[e - 1], piece).at[span],
                    )
        steps.append(copies)
    for k in range(n_steps):
        steps[k].wait()
        columns = pl.ds(k * block, block)
        for e in range(plan.groups):
            rows_at = jnp.where(inner, e, 0)
            left_at = jnp.where(outer, e, 0)
            product = product_of(rows[rows_at, :, columns], left[left_at, :, columns])
            acc[e] = acc[e] + product if k else product
    steps[n_steps].wait()
    tag_ref[...] = tag[0].astype(jnp.float32)
    for e in range(plan.groups):
        tags = tag[jnp.where(inner, e, 0)].astype(jnp.float32)
        lows[e][...] = fold(acc.at[e], tags, plan.left_rows, plan.slots, plan.share)


def blocks_call(kernel, blocks, out_shape, out_specs, scratch, flops, moved, name, extra=()):
    flat, tree = jax.tree.flatten(blocks)
    n_extra = len(extra)

    def body(*refs):
        head, rest = refs[:n_extra], refs[n_extra:]
        nested = jax.tree.unflatten(tree, rest[: len(flat)])
        kernel(*head, *nested, *rest[len(flat) :])

    return pl.pallas_call(
        body,
        out_shape=out_shape,
        in_specs=[VMEM] * n_extra + [HBM] * len(flat),
        out_specs=out_specs,
        scratch_shapes=scratch,
        compiler_params=params(),
        cost_estimate=pl.CostEstimate(flops=flops, bytes_accessed=moved, transcendentals=0),
        name=name,
    )(*extra, *flat)


def reduce_own(plan, near, wide, narrow, own):
    height = plan.half * PAIR
    columns = own.shape[0]
    n_steps = 4
    dtype = own.dtype
    return blocks_call(
        functools.partial(reduce_own_kernel, plan, n_steps),
        [near, wide, narrow, own],
        [jax.ShapeDtypeStruct((height, LANES), jnp.float32)] * 2,
        [VMEM] * 2,
        [
            pltpu.VMEM((height, plan.width), dtype),
            pltpu.VMEM((columns, plan.width), dtype),
            pltpu.VMEM((height, columns), jnp.float32),
            pltpu.VMEM((height, LANES), dtype),
            pltpu.SemaphoreType.DMA(((n_steps + 1) * (plan.half + 1),)),
        ],
        2 * height * plan.width * columns,
        2 * plan.width * (height + columns),
        "reduce_own",
    )


def reduce_taken(plan, near, wide, narrow, across):
    height = plan.half * PAIR
    n_steps = 4
    dtype = near[0].dtype
    groups, padded = plan.groups, plan.padded
    *lows, tag = blocks_call(
        functools.partial(reduce_taken_kernel, plan, n_steps),
        [near, wide, narrow, across],
        [jax.ShapeDtypeStruct((height, LANES), jnp.float32)] * (groups + 1),
        [VMEM] * (groups + 1),
        [
            pltpu.VMEM((groups, height, plan.width), dtype),
            pltpu.VMEM((groups, padded, plan.width), dtype),
            pltpu.VMEM((groups, height, padded), jnp.float32),
            pltpu.VMEM((groups, height, LANES), dtype),
            pltpu.SemaphoreType.DMA(((n_steps + 1) * groups * (plan.half + plan.left_pieces),)),
        ],
        2 * height * plan.width * groups * padded,
        2 * plan.width * (height + padded) * groups,
        "reduce_taken",
    )
    return lows, tag


def add_low(mine_ref, other_ref):
    return (mine_ref[...] + other_ref[...]).astype(jnp.bfloat16).astype(jnp.float32)


def spread(low, tags, columns, slots, share):
    blocks = [
        jnp.where(slot_mask(tags, first, columns, slots, share), low, 0.0).astype(jnp.bfloat16)
        for first in range(0, columns, LANES)
    ]
    return jnp.concatenate(blocks, axis=1)


def write_deltas(delta, outs):
    delta = delta.astype(jnp.bfloat16)
    for i, out in enumerate(outs):
        out[...] = delta[i * PAIR : (i + 1) * PAIR]


def expand_own_kernel(plan, mine_ref, other_ref, tag_ref, own, *rest):
    outs, (up, sem) = rest[:-2], rest[-2:]
    copy = pltpu.make_async_copy(own, up, sem)
    copy.start()
    low = add_low(mine_ref, other_ref)
    wide_low = spread(low, tag_ref[...], up.shape[0], plan.slots, plan.rank)
    copy.wait()
    write_deltas(jnp.dot(wide_low, up[...], preferred_element_type=jnp.float32), outs)


def expand_own(plan, mine, other, tag, own):
    columns, features = own.shape
    return blocks_call(
        functools.partial(expand_own_kernel, plan),
        [own],
        [jax.ShapeDtypeStruct((PAIR, features), jnp.bfloat16)] * plan.half,
        [VMEM] * plan.half,
        [pltpu.VMEM(own.shape, own.dtype), pltpu.SemaphoreType.DMA(())],
        2 * mine.shape[0] * columns * features,
        2 * features * (columns + mine.shape[0]),
        "expand_own",
        extra=(mine, other, tag),
    )


def expand_taken_kernel(plan, *refs):
    lows, tag_ref, refs = refs[: 2 * plan.groups], refs[2 * plan.groups], refs[2 * plan.groups + 1 :]
    wide, narrow, across_wide, across_narrow = refs[:4]
    outs, (up, sems) = refs[4:-2], refs[-2:]
    copies = Copies(am_outer(plan), sems)
    for row, rows, column in plan.up_columns():
        part = pl.ds(0, rows), pl.ds(column, plan.features)
        for e in range(plan.groups):
            copies.both(
                up.at[e, pl.ds(row, rows)],
                of_wide(wide if e == 0 else across_wide[e - 1], plan.left_pieces).at[part],
                (narrow if e == 0 else across_narrow[e - 1]).at[part],
            )
    if plan.padded > plan.left_rows:
        up[:, plan.left_rows :, :] = jnp.zeros(
            (plan.groups, plan.padded - plan.left_rows, plan.features), up.dtype
        )
    tags = tag_ref[...]
    wides = [
        spread(
            add_low(lows[2 * e], lows[2 * e + 1]), tags, plan.left_rows, plan.slots, plan.share
        )
        for e in range(plan.groups)
    ]
    copies.wait()
    delta = None
    for e in range(plan.groups):
        product = jnp.dot(wides[e], up[e], preferred_element_type=jnp.float32)
        delta = product if delta is None else delta + product
    write_deltas(delta, outs)


def expand_taken(plan, lows, tag, wide, narrow, across_wide, across_narrow):
    height, features = lows[0].shape[0], plan.features
    return blocks_call(
        functools.partial(expand_taken_kernel, plan),
        [wide, narrow, across_wide, across_narrow],
        [jax.ShapeDtypeStruct((PAIR, features), jnp.bfloat16)] * plan.half,
        [VMEM] * plan.half,
        [
            pltpu.VMEM((plan.groups, plan.padded, features), jnp.bfloat16),
            pltpu.SemaphoreType.DMA((plan.groups * len(list(plan.up_columns())),)),
        ],
        2 * height * plan.groups * plan.padded * features,
        2 * features * (plan.groups * plan.padded + height),
        "expand_taken",
        extra=(*lows, tag),
    )


def join_kernel(seg_ref, base_ref, *refs):
    deltas, out_ref = refs[:-1], refs[-1]
    for k in range(len(deltas) * CAP):
        part = k % CAP

        @pl.when(seg_ref[k] >= 0)
        def _():
            span = pl.ds(pl.multiple_of(seg_ref[k] * SEG, SEG), SEG)
            delta = deltas[k // CAP][part * SEG : (part + 1) * SEG, :]
            out_ref[span, :] = (base_ref[span, :] + delta.astype(jnp.float32)).astype(
                out_ref.dtype
            )


def join(seg_of, base, deltas):
    height, features = base.shape
    block = min(features, 512)
    tall = pl.BlockSpec((height, block), lambda j: (0, j))
    short = pl.BlockSpec((PAIR, block), lambda j: (0, j))
    return pl.pallas_call(
        join_kernel,
        grid=(features // block,),
        out_shape=jax.ShapeDtypeStruct((height, features), jnp.bfloat16),
        in_specs=[SMEM, tall] + [short] * len(deltas),
        out_specs=tall,
        compiler_params=params(),
        cost_estimate=pl.CostEstimate(
            flops=height * features, bytes_accessed=8 * height * features, transcendentals=0
        ),
        name="join",
    )(seg_of, base, *deltas)


def swap(value, axis, distance):
    count = lax.axis_size(axis)
    return lax.ppermute(value, axis, [(i, i ^ distance) for i in range(count)])


def send(plan, value, moves):
    shape = (plan.groups, plan.replicas, lax.axis_size("tensor"))

    def place(g, r, c):
        return (g * shape[1] + r) * shape[2] + c

    pairs = [
        (place(g, r, c), place(g ^ flips[0], r ^ flips[1], c ^ flips[2]))
        for senders, *flips in moves
        for g in range(shape[0])
        for r in senders
        for c in range(shape[2])
    ]
    return lax.ppermute(value, ("groups", "replica", "tensor"), pairs)


def on_device(x, weight, lefts, ups, ids, residency):
    slots, width, rank = lefts.shape
    features = ups.shape[2]
    plan = Plan(
        lax.axis_size("replica"), lax.axis_size("groups"), slots, rank, width, features
    )
    half, n_cross = plan.half, len(plan.cross)
    core = lax.axis_index("tensor")
    outer = am_outer(plan)
    left_rows = jnp.swapaxes(lefts, 1, 2)
    near, wide, seg_of = lay_out(plan, True, ids, residency, x, left_rows, ups)

    near = [swap(block, "replica", d) for block, d in zip(near, plan.near[1:])]
    wide_in = []
    for i in range(plan.wide):
        moves = []
        if i < n_cross:
            moves.append((plan.outer, 0, plan.cross[i], 0))
        if i < plan.adapter_wide:
            moves.append((plan.inner, 0, half, 0))
        wide_in.append(send(plan, wide[i], moves))

    def part(which):
        columns = lax.dynamic_slice(weight, (0, which * features), (weight.shape[0], features))
        return jnp.dot(x, columns, preferred_element_type=jnp.float32)

    base_other = part(1 - core)
    late_ids, _ = lax.optimization_barrier((ids, seg_of))
    own_rows, narrow, _ = lay_out(plan, False, late_ids, residency, x, left_rows, ups)
    near = own_rows + near
    near, wide_in[0], narrow[:2], base_other = lax.optimization_barrier(
        (near, wide_in[0], narrow[:2], base_other)
    )

    def narrow_send(j):
        moves = []
        if j < 2 * n_cross:
            moves.append((plan.inner, 0, plan.cross[j % n_cross], 0))
        if j < plan.pieces:
            moves.append((plan.outer, 0, half, 0))
        return send(plan, narrow[j], moves)

    def taken_rows(i):
        return near[i][PAIR:] if i < len(plan.near) else wide_in[i - len(plan.near)][PAIR:]

    def across_send(i):
        value = jnp.concatenate([taken_rows(2 * i), taken_rows(2 * i + 1)], axis=0)
        if i < plan.adapter_wide:
            value = jnp.where(outer, wide_in[i], value)
        return [
            send(plan, value, [(plan.outer, e, 0, 0), (plan.inner, e, 0, 0)])
            for e in range(1, plan.groups)
        ]

    across = [across_send(0)]
    narrow_in = [narrow_send(0), narrow_send(1)]
    wide_in, narrow[2:] = lax.optimization_barrier((wide_in, narrow[2:]))
    across += [across_send(i) for i in range(1, half // 2)]
    narrow_in += [narrow_send(j) for j in range(2, plan.narrow)]
    across = [[blocks[e] for blocks in across] for e in range(plan.groups - 1)]
    across_up = [send(plan, narrow_in[0], [(plan.inner, e, 0, 0)]) for e in range(1, plan.groups)]
    base = part(core) + swap(base_other, "tensor", 1)

    own_left = left_rows.reshape(slots * rank, width)
    low, tag = reduce_own(plan, near, wide_in[:n_cross], narrow_in[:n_cross], own_left)
    other = swap(low, "tensor", 1)
    terms = expand_own(plan, low, other, tag, ups.reshape(slots * rank, features))
    deltas = [terms[0]] + [swap(terms[d], "replica", d) for d in range(1, half)]

    narrow_in[-1], base, deltas[0] = lax.optimization_barrier((narrow_in[-1], base, deltas[0]))
    lows, tag = reduce_taken(plan, near, wide_in, narrow_in, across)
    pairs = [lows[0], swap(lows[0], "tensor", 1)]
    for e in range(1, plan.groups):
        pairs.append(send(plan, lows[e], [(plan.outer, 0, 0, 0), (plan.inner, e, 0, 0)]))
        pairs.append(send(plan, lows[e], [(plan.outer, 0, 0, 1), (plan.inner, e, 0, 1)]))
    pairs, deltas = lax.optimization_barrier((pairs, deltas))
    across_wide = [blocks[: plan.adapter_wide] for blocks in across]
    terms = expand_taken(
        plan, pairs, tag, wide_in[: plan.adapter_wide], narrow_in[0], across_wide, across_up
    )
    deltas += [terms[0]] + [swap(terms[d], "replica", d) for d in range(1, half)]
    return join(seg_of, base, deltas)


def solution(mesh):
    placed = (
        P(("groups", "replica"), "tensor"),
        P("tensor", None),
        P("replica", "tensor", None),
        P("replica", None, "tensor"),
        P(("groups", "replica")),
        P(),
    )
    return jax.shard_map(
        on_device,
        mesh=mesh,
        in_specs=placed,
        out_specs=P(("groups", "replica"), "tensor"),
        check_vma=False,
    )
```

time: 168 us -> 159 us (0.946)
  waiting for transfers between devices: 70.8 us -> 86.8 us
  between operations: 13.6 us -> 0.27 us
  Pallas kernels: 25.6 us -> 18.5 us
  starting transfers between devices: 40.4 us -> 36.9 us
  local copies, waits for them, and re-layouts: 2.76 us -> 0.2 us
    ppermute x12 -> x11, waiting for transfers between devices: 59.8 us -> 72.7 us  [send(): return lax.ppermute(value, ('groups', 'replica', 'tensor'), pairs)]
    pallas_call x4, Pallas kernels: 15.6 us -> 6.79 us  [blocks_call(): pl.pallas_call(body, out_shape=out_shape, in_specs=[VMEM] * n_extra + [HB...]
    ppermute x12 -> x11, starting transfers between devices: 20.9 us -> 14.8 us  [send(): return lax.ppermute(value, ('groups', 'replica', 'tensor'), pairs)]
    ppermute x9 -> x10, waiting for transfers between devices: 11 us -> 14.1 us  [swap(): return lax.ppermute(value, axis, [(i, i ^ distance) for i in range(count)])]
    unnamed x30 -> x18, local copies, waits for them, and re-layouts: 2.76 us -> 0.04 us
    pallas_call x1 -> x2, Pallas kernels: 7.1 us -> 9.69 us  [lay_out(): pl.pallas_call(functools.partial(lay_kernel, plan, first_call), out_shape...]
    ppermute x9 -> x10, starting transfers between devices: 19.5 us -> 22.1 us  [swap(): return lax.ppermute(value, axis, [(i, i ^ distance) for i in range(count)])]
    dot_general x1 -> x2, matrix products: 14.9 us -> 15.2 us  [part(): return jnp.dot(x, columns, preferred_element_type=jnp.float32)]
  transfers between devices with their start and end apart: 22 -> 21, of which waited for: 10 -> 11; matrix products, arithmetic and copies ran while one was open for 9% -> 10% of each run, Pallas kernels for 9% -> 7%
where the time goes in v5:
time: 159 us
  waiting for transfers between devices  86.8 us (55%)
  starting transfers between devices  36.9 us (23%)
  Pallas kernels  18.5 us (12%)
  matrix products  15.2 us (10%)
    ppermute x11, waiting for transfers between devices, send(): return lax.ppermute(value, ('groups', 'replica', 'tensor'), pairs)  72.7 us
    ppermute x10, starting transfers between devices, swap(): return lax.ppermute(value, axis, [(i, i ^ distance) for i in range(count)])  22.1 us
    dot_general x2, matrix products, part(): return jnp.dot(x, columns, preferred_element_type=jnp.float32)  15.2 us
    ppermute x11, starting transfers between devices, send(): return lax.ppermute(value, ('groups', 'replica', 'tensor'), pairs)  14.8 us
    ppermute x10, waiting for transfers between devices, swap(): return lax.ppermute(value, axis, [(i, i ^ distance) for i in range(count)])  14.1 us
    pallas_call x2, Pallas kernels, lay_out(): pl.pallas_call(functools.partial(lay_kernel, plan, first_call), out_shape...  9.69 us
    pallas_call x4, Pallas kernels, blocks_call(): pl.pallas_call(body, out_shape=out_shape, in_specs=[VMEM] * n_extra + [HB...  6.79 us
  transfers between devices with their start and end apart: 21, of which 11 were waited for; matrix products, arithmetic and copies ran while one was open for 10% of the time, Pallas kernels for 7%

profile of v5, /device:TPU:0, one launch (start us, length us, event | category | flops | bytes accessed | tf_op | source)
XLA Modules:
  0.0 158.7 jit_solution(15597611252568174259)
XLA Ops:
  0.0 4.6 %lay_out_first.1 = (bf16[128,4224]{1,0:T(8,128)(2,1)}, bf16[128,4224]{1,0:T(8,128)(2,1)}, bf16[128,4224]{1,0:T(8,128)(2,1)}, s32[16]{0:T(128)}) custom-call(s32[16]{0:T(128)} %ids_ref.2, s32[48]{0:T(128)} %residency_ref.3, bf16[512,4096]{1,0:T(8,128)(2,1)} %x_ref.3, bf16[6,64,4096]{2,1,0:T(8,128)(2,1)} %bitcast.10, bf16[6,64,1024]{2,1,0:T(8,128)(2,1)} %up_ref.3), custom_call_target="tpu_custom_call" | custom-call | bytes 6291456 | tf_op jit(solution)/shard_map/lay_out_first/pallas_call | solution.py:211
  4.6 3.0 %collective-permute-start = (bf16[128,4224]{1,0:T(8,128)(2,1)}, bf16[128,4224]{1,0:T(8,128)(2,1)S(1)}, u32[]{:S(2)}, u32[]{:S(2)}) collective-permute-start(bf16[128,4224]{1,0:T(8,128)(2,1)} %get-tuple-element.52), channel_id=1, source_target_pairs={{0,2},{2,0},{4,6},{6,4},{8,10},{10,8},{12,14},{14,12},{1,3},{3,1},... | collective-permute-start | bytes 3244040 | tf_op jit(solution)/shard_map/ppermute | solution.py:573
  7.6 2.1 %collective-permute-start.1 = (bf16[128,4224]{1,0:T(8,128)(2,1)}, bf16[128,4224]{1,0:T(8,128)(2,1)S(1)}, u32[]{:S(2)}, u32[]{:S(2)}) collective-permute-start(bf16[128,4224]{1,0:T(8,128)(2,1)} %get-tuple-element.53), channel_id=1, source_target_pairs={{0,4},{1,5},{2,6},{3,7},{12,8},{13,9},{14,10},{15,11},{16,20},{17,... | collective-permute-start | bytes 3244040 | tf_op jit(solution)/shard_map/ppermute | solution.py:589
  9.7 2.0 %collective-permute-start.2 = (bf16[128,4224]{1,0:T(8,128)(2,1)}, bf16[128,4224]{1,0:T(8,128)(2,1)S(1)}, u32[]{:S(2)}, u32[]{:S(2)}) collective-permute-start(bf16[128,4224]{1,0:T(8,128)(2,1)} %get-tuple-element.57), channel_id=1, source_target_pairs={{0,6},{1,7},{2,4},{3,5},{12,10},{13,11},{14,8},{15,9},{16,22},{17,... | collective-permute-start | bytes 3244040 | tf_op jit(solution)/shard_map/ppermute | solution.py:589
  11.8 5.1 %lay_out_second.1 = (bf16[128,4224]{1,0:T(8,128)(2,1)}, bf16[64,4224]{1,0:T(8,128)(2,1)}, bf16[64,4224]{1,0:T(8,128)(2,1)}, bf16[64,4224]{1,0:T(8,128)(2,1)}, bf16[64,4224]{1,0:T(8,128)(2,1)}, /*index=5*/s32[16]{0:T(128)}) custom-call(s32[16]{0:T(128)} %ids_ref.2, s32[48]{0:T(128)} %residency_ref.3, bf16[512,4096]{1,0:T(8,128)(2,1)} %x_ref.3, ...), custom_call_target="tpu_custom_call" | custom-call | bytes 6291456 | tf_op jit(solution)/shard_map/lay_out_second/pallas_call | solution.py:211
  16.9 8.3 %fusion.4 = f32[512,1024]{1,0:T(8,128)S(1)} fusion(bf16[512,4096]{1,0:T(8,128)(2,1)} %x_ref.3, bf16[4096,2048]{1,0:T(8,128)(2,1)} %param.7, s32[]{:T(128)S(6)} %select_n.18), kind=kOutput, calls=%fused_computation.5 | convolution fusion | flops 4294967296 | bytes 14680068 | tf_op jit(solution)/shard_map/dot_general | solution.py:616
  25.2 6.5 %collective-permute-done.refs_1_ = bf16[128,4224]{1,0:T(8,128)(2,1)S(1)} collective-permute-done((bf16[128,4224]{1,0:T(8,128)(2,1)}, bf16[128,4224]{1,0:T(8,128)(2,1)S(1)}, u32[]{:S(2)}, u32[]{:S(2)}) %collective-permute-start) | collective-permute-done | bytes 1081376 | tf_op jit(solution)/shard_map/ppermute | solution.py:573
  31.7 3.9 %collective-permute-done.1.refs_2_.refs_5_ = bf16[128,4224]{1,0:T(8,128)(2,1)S(1)} collective-permute-done((bf16[128,4224]{1,0:T(8,128)(2,1)}, bf16[128,4224]{1,0:T(8,128)(2,1)S(1)}, u32[]{:S(2)}, u32[]{:S(2)}) %collective-permute-start.1) | collective-permute-done | bytes 1081376 | tf_op jit(solution)/shard_map/ppermute | solution.py:589
  35.7 22.0 %collective-permute-done.2.refs_3_.refs_6_ = bf16[128,4224]{1,0:T(8,128)(2,1)S(1)} collective-permute-done((bf16[128,4224]{1,0:T(8,128)(2,1)}, bf16[128,4224]{1,0:T(8,128)(2,1)S(1)}, u32[]{:S(2)}, u32[]{:S(2)}) %collective-permute-start.2) | collective-permute-done | bytes 1081376 | tf_op jit(solution)/shard_map/ppermute | solution.py:589
  57.7 1.7 %collective-permute-start.3 = (bf16[64,4224]{1,0:T(8,128)(2,1)S(1)}, bf16[64,4224]{1,0:T(8,128)(2,1)S(1)}, u32[]{:S(2)}, u32[]{:S(2)}) collective-permute-start(bf16[64,4224]{1,0:T(8,128)(2,1)S(1)} %copy-done.6), channel_id=1, source_target_pairs={{4,2},{5,3},{6,0},{7,1},{8,14},{9,15},{10,12},{11,13},{20,18},{21,... | collective-permute-start | bytes 1622024 | tf_op jit(solution)/shard_map/ppermute | solution.py:589
  59.4 2.0 %collective-permute-start.5 = (bf16[64,4224]{1,0:T(8,128)(2,1)S(1)}, bf16[64,4224]{1,0:T(8,128)(2,1)S(1)}, u32[]{:S(2)}, u32[]{:S(2)}) collective-permute-start(bf16[64,4224]{1,0:T(8,128)(2,1)S(1)} %copy-done.8), channel_id=1, source_target_pairs={{4,0},{5,1},{6,2},{7,3},{8,12},{9,13},{10,14},{11,15},{20,16},{21,... | collective-permute-start | bytes 1622024 | tf_op jit(solution)/shard_map/ppermute | solution.py:589
  61.5 2.0 %collective-permute-start.8 = (bf16[64,4224]{1,0:T(8,128)(2,1)S(1)}, bf16[64,4224]{1,0:T(8,128)(2,1)S(1)}, u32[]{:S(2)}, u32[]{:S(2)}) collective-permute-start(bf16[64,4224]{1,0:T(8,128)(2,1)S(1)} %copy-done.5), channel_id=1, source_target_pairs={{4,0},{5,1},{6,2},{7,3},{8,12},{9,13},{10,14},{11,15},{20,16},{21,... | collective-permute-start | bytes 1622024 | tf_op jit(solution)/shard_map/ppermute | solution.py:589
  64.0 20.4 %collective-permute-done.5.refs_4_.refs_7_ = bf16[64,4224]{1,0:T(8,128)(2,1)S(1)} collective-permute-done((bf16[64,4224]{1,0:T(8,128)(2,1)S(1)}, bf16[64,4224]{1,0:T(8,128)(2,1)S(1)}, u32[]{:S(2)}, u32[]{:S(2)}) %collective-permute-start.5) | collective-permute-done | bytes 540704 | tf_op jit(solution)/shard_map/ppermute | solution.py:589
  85.9 11.1 %collective-permute-done.6.refs_5_ = bf16[64,4224]{1,0:T(8,128)(2,1)S(1)} collective-permute-done((bf16[64,4224]{1,0:T(8,128)(2,1)S(1)}, bf16[64,4224]{1,0:T(8,128)(2,1)S(1)}, u32[]{:S(2)}, u32[]{:S(2)}) %collective-permute-start.6) | collective-permute-done | bytes 540704 | tf_op jit(solution)/shard_map/ppermute | solution.py:589
  97.0 2.4 %reduce_own.1 = (f32[256,128]{1,0:T(8,128)S(1)}, f32[256,128]{1,0:T(8,128)S(1)}) custom-call(bf16[128,4224]{1,0:T(8,128)(2,1)S(1)} %copy-done.2, bf16[128,4224]{1,0:T(8,128)(2,1)S(1)} %collective-permute-done.refs_1_, bf16[128,4224]{1,0:T(8,128)(2,1)S(1)} %collective-permute-done.1.refs_2_.refs_5_, ...), custom_call_target="tpu_custom_call" | custom-call | flops 805306368 | bytes 5242880 | tf_op jit(solution)/shard_map/reduce_own/pallas_call | solution.py:386
  102.3 6.9 %fusion = f32[1024,512]{0,1:T(8,128)S(1)} fusion(bf16[512,4096]{1,0:T(8,128)(2,1)S(1)} %copy-done.4, bf16[4096,2048]{1,0:T(8,128)(2,1)} %param.7, s32[]{:T(128)S(6)} %select_n.19), kind=kOutput, calls=%fused_computation | convolution fusion | flops 4294967296 | bytes 14680068 | tf_op jit(solution)/shard_map/dot_general | solution.py:616
  111.0 3.4 %collective-permute-start.15 = (bf16[64,1024]{1,0:T(8,128)(2,1)S(1)}, bf16[64,1024]{1,0:T(8,128)(2,1)S(1)}, u32[]{:S(2)}, u32[]{:S(2)}) collective-permute-start(bf16[64,1024]{1,0:T(8,128)(2,1)S(1)} %get-tuple-element.78), channel_id=1, source_target_pairs={{0,4},{2,6},{4,0},{6,2},{8,12},{10,14},{12,8},{14,10},{1,5},{3,7},... | collective-permute-start | bytes 393224 | tf_op jit(solution)/shard_map/ppermute | solution.py:573
  115.0 14.4 %collective-permute-done.10.refs_9_ = bf16[128,4224]{1,0:T(8,128)(2,1)S(1)} collective-permute-done((bf16[128,4224]{1,0:T(8,128)(2,1)S(1)}, bf16[128,4224]{1,0:T(8,128)(2,1)S(1)}, u32[]{:S(2)}, u32[]{:S(2)}) %collective-permute-start.10) | collective-permute-done | bytes 1081376 | tf_op jit(solution)/shard_map/ppermute | solution.py:589
  129.3 3.2 %reduce_taken.1 = (f32[256,128]{1,0:T(8,128)S(1)}, f32[256,128]{1,0:T(8,128)S(1)}, f32[256,128]{1,0:T(8,128)S(1)}) custom-call(bf16[128,4224]{1,0:T(8,128)(2,1)S(1)} %copy-done.2, bf16[128,4224]{1,0:T(8,128)(2,1)S(1)} %collective-permute-done.refs_1_, bf16[128,4224]{1,0:T(8,128)(2,1)S(1)} %collective-permute-done.1.refs_2_.refs_5_, ...), custom_call_target="tpu_custom_call" | custom-call | flops 1073741824 | bytes 8388608 | tf_op jit(solution)/shard_map/reduce_taken/pallas_call | solution.py:386
  135.6 1.6 %collective-permute-start.18 = (bf16[64,1024]{1,0:T(8,128)(2,1)S(1)}, bf16[64,1024]{1,0:T(8,128)(2,1)S(1)}, u32[]{:S(2)}, u32[]{:S(2)}) collective-permute-start(bf16[64,1024]{1,0:T(8,128)(2,1)S(1)} %get-tuple-element.90), channel_id=1, source_target_pairs={{0,2},{2,0},{4,6},{6,4},{8,10},{10,8},{12,14},{14,12},{1,3},{3,1},... | collective-permute-start | bytes 393224 | tf_op jit(solution)/shard_map/ppermute | solution.py:573
  137.2 12.4 %collective-permute-start.19 = (bf16[64,1024]{1,0:T(8,128)(2,1)S(1)}, bf16[64,1024]{1,0:T(8,128)(2,1)S(1)}, u32[]{:S(2)}, u32[]{:S(2)}) collective-permute-start(bf16[64,1024]{1,0:T(8,128)(2,1)S(1)} %get-tuple-element.91), channel_id=1, source_target_pairs={{0,4},{2,6},{4,0},{6,2},{8,12},{10,14},{12,8},{14,10},{1,5},{3,7},... | collective-permute-start | bytes 393224 | tf_op jit(solution)/shard_map/ppermute | solution.py:573
  150.3 3.2 %collective-permute-done.19.refs_6_ = bf16[64,1024]{1,0:T(8,128)(2,1)S(1)} collective-permute-done((bf16[64,1024]{1,0:T(8,128)(2,1)S(1)}, bf16[64,1024]{1,0:T(8,128)(2,1)S(1)}, u32[]{:S(2)}, u32[]{:S(2)}) %collective-permute-start.19) | collective-permute-done | bytes 131104 | tf_op jit(solution)/shard_map/ppermute | solution.py:573
  153.5 3.2 %collective-permute-done.20.refs_7_ = bf16[64,1024]{1,0:T(8,128)(2,1)S(1)} collective-permute-done((bf16[64,1024]{1,0:T(8,128)(2,1)S(1)}, bf16[64,1024]{1,0:T(8,128)(2,1)S(1)}, u32[]{:S(2)}, u32[]{:S(2)}) %collective-permute-start.20) | collective-permute-done | bytes 131104 | tf_op jit(solution)/shard_map/ppermute | solution.py:573
  156.7 2.0 %join.1 = bf16[512,1024]{1,0:T(8,128)(2,1)} custom-call(s32[16]{0:T(128)S(1)} %copy-done.3, f32[512,1024]{1,0:T(8,128)S(1)} %bitcast_add_fusion.base_ref, bf16[64,1024]{1,0:T(8,128)(2,1)S(1)} %get-tuple-element.80.refs_0_, bf16[64,1024]{1,0:T(8,128)(2,1)S(1)} %collective-permute-done.14.refs_1_, bf16[64,1024]{1,0:T(8,128)(2,1)S(1)} %collective-permute-done.15.refs_2_, ...), custom_call_target="tpu_custom_call" | custom-call | flops 524288 | bytes 4194304 | tf_op jit(solution)/shard_map/join/pallas_call | solution.py:557
  (52 shorter events, 11.0 us)
Async XLA Ops:
  4.6 27.1 %collective-permute-start = (bf16[128,4224]{1,0:T(8,128)(2,1)}, bf16[128,4224]{1,0:T(8,128)(2,1)S(1)}, u32[]{:S(2)}, u32[]{:S(2)}) collective-permute-start(bf16[128,4224]{1,0:T(8,128)(2,1)} %get-tuple-element.52), channel_id=1, source_target_pairs={{0,2},{2,0},{4,6},{6,4},{8,10},{10,8},{12,14},{14,12},{1,3},{3,1},... | collective-permute-start | bytes 3244040 | tf_op jit(solution)/shard_map/ppermute | solution.py:573
  7.6 28.0 %collective-permute-start.1 = (bf16[128,4224]{1,0:T(8,128)(2,1)}, bf16[128,4224]{1,0:T(8,128)(2,1)S(1)}, u32[]{:S(2)}, u32[]{:S(2)}) collective-permute-start(bf16[128,4224]{1,0:T(8,128)(2,1)} %get-tuple-element.53), channel_id=1, source_target_pairs={{0,4},{1,5},{2,6},{3,7},{12,8},{13,9},{14,10},{15,11},{16,20},{17,... | collective-permute-start | bytes 3244040 | tf_op jit(solution)/shard_map/ppermute | solution.py:589
  9.7 48.0 %collective-permute-start.2 = (bf16[128,4224]{1,0:T(8,128)(2,1)}, bf16[128,4224]{1,0:T(8,128)(2,1)S(1)}, u32[]{:S(2)}, u32[]{:S(2)}) collective-permute-start(bf16[128,4224]{1,0:T(8,128)(2,1)} %get-tuple-element.57), channel_id=1, source_target_pairs={{0,6},{1,7},{2,4},{3,5},{12,10},{13,11},{14,8},{15,9},{16,22},{17,... | collective-permute-start | bytes 3244040 | tf_op jit(solution)/shard_map/ppermute | solution.py:589
  16.9 44.5 %copy-start.7 = (bf16[64,4224]{1,0:T(8,128)(2,1)S(1)}, bf16[64,4224]{1,0:T(8,128)(2,1)}, u32[]{:S(2)}) copy-start(bf16[64,4224]{1,0:T(8,128)(2,1)} %get-tuple-element.67) | copy-start | bytes 1622020
  16.9 44.6 %copy-start.5 = (bf16[64,4224]{1,0:T(8,128)(2,1)S(1)}, bf16[64,4224]{1,0:T(8,128)(2,1)}, u32[]{:S(2)}) copy-start(bf16[64,4224]{1,0:T(8,128)(2,1)} %get-tuple-element.72) | copy-start | bytes 1622020
  16.9 46.7 %copy-start.2 = (bf16[128,4224]{1,0:T(8,128)(2,1)S(1)}, bf16[128,4224]{1,0:T(8,128)(2,1)}, u32[]{:S(2)}) copy-start(bf16[128,4224]{1,0:T(8,128)(2,1)} %get-tuple-element.62.refs_0_) | copy-start | bytes 3244036
  57.7 52.0 %collective-permute-start.3 = (bf16[64,4224]{1,0:T(8,128)(2,1)S(1)}, bf16[64,4224]{1,0:T(8,128)(2,1)S(1)}, u32[]{:S(2)}, u32[]{:S(2)}) collective-permute-start(bf16[64,4224]{1,0:T(8,128)(2,1)S(1)} %copy-done.6), channel_id=1, source_target_pairs={{4,2},{5,3},{6,0},{7,1},{8,14},{9,15},{10,12},{11,13},{20,18},{21,... | collective-permute-start | bytes 1622024 | tf_op jit(solution)/shard_map/ppermute | solution.py:589
  59.4 51.6 %collective-permute-start.4 = (f32[512,1024]{1,0:T(8,128)S(1)}, f32[512,1024]{1,0:T(8,128)S(1)}, u32[]{:S(2)}, u32[]{:S(2)}) collective-permute-start(f32[512,1024]{1,0:T(8,128)S(1)} %fusion.4), channel_id=1, source_target_pairs={{0,1},{1,0},{2,3},{3,2},{4,5},{5,4},{6,7},{7,6},{8,9},{9,8},{10,11... | collective-permute-start | bytes 6291464 | tf_op jit(solution)/shard_map/ppermute | solution.py:573
  59.4 25.0 %collective-permute-start.5 = (bf16[64,4224]{1,0:T(8,128)(2,1)S(1)}, bf16[64,4224]{1,0:T(8,128)(2,1)S(1)}, u32[]{:S(2)}, u32[]{:S(2)}) collective-permute-start(bf16[64,4224]{1,0:T(8,128)(2,1)S(1)} %copy-done.8), channel_id=1, source_target_pairs={{4,0},{5,1},{6,2},{7,3},{8,12},{9,13},{10,14},{11,15},{20,16},{21,... | collective-permute-start | bytes 1622024 | tf_op jit(solution)/shard_map/ppermute | solution.py:589
  61.4 35.6 %collective-permute-start.6 = (bf16[64,4224]{1,0:T(8,128)(2,1)S(1)}, bf16[64,4224]{1,0:T(8,128)(2,1)S(1)}, u32[]{:S(2)}, u32[]{:S(2)}) collective-permute-start(bf16[64,4224]{1,0:T(8,128)(2,1)S(1)} %copy-done.7), channel_id=1, source_target_pairs={{4,2},{5,3},{6,0},{7,1},{8,14},{9,15},{10,12},{11,13},{20,18},{21,... | collective-permute-start | bytes 1622024 | tf_op jit(solution)/shard_map/ppermute | solution.py:589
  61.5 48.9 %collective-permute-start.8 = (bf16[64,4224]{1,0:T(8,128)(2,1)S(1)}, bf16[64,4224]{1,0:T(8,128)(2,1)S(1)}, u32[]{:S(2)}, u32[]{:S(2)}) collective-permute-start(bf16[64,4224]{1,0:T(8,128)(2,1)S(1)} %copy-done.5), channel_id=1, source_target_pairs={{4,0},{5,1},{6,2},{7,3},{8,12},{9,13},{10,14},{11,15},{20,16},{21,... | collective-permute-start | bytes 1622024 | tf_op jit(solution)/shard_map/ppermute | solution.py:589
  84.4 30.4 %collective-permute-start.9 = (bf16[128,4224]{1,0:T(8,128)(2,1)S(1)}, bf16[128,4224]{1,0:T(8,128)(2,1)S(1)}, u32[]{:S(2)}, u32[]{:S(2)}) collective-permute-start(bf16[128,4224]{1,0:T(8,128)(2,1)S(1)} %maximum_select_fusion), channel_id=1, source_target_pairs={{0,16},{1,17},{2,18},{3,19},{12,28},{13,29},{14,30},{15,31},{16,0}... | collective-permute-start | bytes 3244040 | tf_op jit(solution)/shard_map/ppermute | solution.py:589
  99.3 1.4 collective-permute-start.7
  100.8 28.6 %collective-permute-start.10 = (bf16[128,4224]{1,0:T(8,128)(2,1)S(1)}, bf16[128,4224]{1,0:T(8,128)(2,1)S(1)}, u32[]{:S(2)}, u32[]{:S(2)}) collective-permute-start(bf16[128,4224]{1,0:T(8,128)(2,1)S(1)} %maximum_select_fusion.1), channel_id=1, source_target_pairs={{0,16},{1,17},{2,18},{3,19},{12,28},{13,29},{14,30},{15,31},{16,0}... | collective-permute-start | bytes 3244040 | tf_op jit(solution)/shard_map/ppermute | solution.py:589
  109.7 25.1 %collective-permute-start.17 = (bf16[64,4224]{1,0:T(8,128)(2,1)S(1)}, bf16[64,4224]{1,0:T(8,128)(2,1)S(1)}, u32[]{:S(2)}, u32[]{:S(2)}) collective-permute-start(bf16[64,4224]{1,0:T(8,128)(2,1)S(1)} %collective-permute-done.5.refs_4_.refs_7_), channel_id=1, source_target_pairs={{4,20},{5,21},{6,22},{7,23},{8,24},{9,25},{10,26},{11,27},{20,4},{... | collective-permute-start | bytes 1622024 | tf_op jit(solution)/shard_map/ppermute | solution.py:589
  110.4 22.2 %collective-permute-start.14 = (bf16[64,1024]{1,0:T(8,128)(2,1)S(1)}, bf16[64,1024]{1,0:T(8,128)(2,1)S(1)}, u32[]{:S(2)}, u32[]{:S(2)}) collective-permute-start(bf16[64,1024]{1,0:T(8,128)(2,1)S(1)} %get-tuple-element.77), channel_id=1, source_target_pairs={{0,2},{2,0},{4,6},{6,4},{8,10},{10,8},{12,14},{14,12},{1,3},{3,1},... | collective-permute-start | bytes 393224 | tf_op jit(solution)/shard_map/ppermute | solution.py:573
  111.0 22.3 %collective-permute-start.15 = (bf16[64,1024]{1,0:T(8,128)(2,1)S(1)}, bf16[64,1024]{1,0:T(8,128)(2,1)S(1)}, u32[]{:S(2)}, u32[]{:S(2)}) collective-permute-start(bf16[64,1024]{1,0:T(8,128)(2,1)S(1)} %get-tuple-element.78), channel_id=1, source_target_pairs={{0,4},{2,6},{4,0},{6,2},{8,12},{10,14},{12,8},{14,10},{1,5},{3,7},... | collective-permute-start | bytes 393224 | tf_op jit(solution)/shard_map/ppermute | solution.py:573
  114.8 19.0 %collective-permute-start.16 = (bf16[64,1024]{1,0:T(8,128)(2,1)S(1)}, bf16[64,1024]{1,0:T(8,128)(2,1)S(1)}, u32[]{:S(2)}, u32[]{:S(2)}) collective-permute-start(bf16[64,1024]{1,0:T(8,128)(2,1)S(1)} %get-tuple-element.79), channel_id=1, source_target_pairs={{0,6},{2,4},{4,2},{6,0},{8,14},{10,12},{12,10},{14,8},{1,7},{3,5},... | collective-permute-start | bytes 393224 | tf_op jit(solution)/shard_map/ppermute | solution.py:573
  132.5 1.4 collective-permute-start.11
  132.6 1.3 collective-permute-start.12
  133.3 1.5 collective-permute-start.13
  135.6 14.7 %collective-permute-start.18 = (bf16[64,1024]{1,0:T(8,128)(2,1)S(1)}, bf16[64,1024]{1,0:T(8,128)(2,1)S(1)}, u32[]{:S(2)}, u32[]{:S(2)}) collective-permute-start(bf16[64,1024]{1,0:T(8,128)(2,1)S(1)} %get-tuple-element.90), channel_id=1, source_target_pairs={{0,2},{2,0},{4,6},{6,4},{8,10},{10,8},{12,14},{14,12},{1,3},{3,1},... | collective-permute-start | bytes 393224 | tf_op jit(solution)/shard_map/ppermute | solution.py:573
  137.2 16.4 %collective-permute-start.19 = (bf16[64,1024]{1,0:T(8,128)(2,1)S(1)}, bf16[64,1024]{1,0:T(8,128)(2,1)S(1)}, u32[]{:S(2)}, u32[]{:S(2)}) collective-permute-start(bf16[64,1024]{1,0:T(8,128)(2,1)S(1)} %get-tuple-element.91), channel_id=1, source_target_pairs={{0,4},{2,6},{4,0},{6,2},{8,12},{10,14},{12,8},{14,10},{1,5},{3,7},... | collective-permute-start | bytes 393224 | tf_op jit(solution)/shard_map/ppermute | solution.py:573
  149.6 7.1 %collective-permute-start.20 = (bf16[64,1024]{1,0:T(8,128)(2,1)S(1)}, bf16[64,1024]{1,0:T(8,128)(2,1)S(1)}, u32[]{:S(2)}, u32[]{:S(2)}) collective-permute-start(bf16[64,1024]{1,0:T(8,128)(2,1)S(1)} %get-tuple-element.92), channel_id=1, source_target_pairs={{0,6},{2,4},{4,2},{6,0},{8,14},{10,12},{12,10},{14,8},{1,7},{3,5},... | collective-permute-start | bytes 393224 | tf_op jit(solution)/shard_map/ppermute | solution.py:573
  (6 other events, 153.3 us)

commit v6 on v5

--- a/solution.py
+++ b/solution.py
@@ -271,6 +271,36 @@
                 pl.when(wanted)(copy.wait)
 
 
+def lane_group(share):
+    return lax.broadcasted_iota(jnp.int32, (1, LANES), 1) // share
+
+
+def spread_lanes(value, share):
+    total = value
+    for shift in range(share, LANES, share):
+        total += pltpu.roll(value, shift, 1)
+    return total
+
+
+def pack(low, share):
+    count = LANES // share
+    height = low.shape[0] // count
+    everywhere = spread_lanes(low, share)
+    packed = jnp.zeros((height, LANES), jnp.float32)
+    for i in range(count):
+        rows = everywhere[i * height : (i + 1) * height]
+        packed = jnp.where(lane_group(share) == i, rows, packed)
+    return packed
+
+
+def unpack(packed, share):
+    rows = [
+        spread_lanes(jnp.where(lane_group(share) == i, packed, 0.0), share)
+        for i in range(LANES // share)
+    ]
+    return jnp.concatenate(rows, axis=0)
+
+
 def fold(product, tags, columns, slots, share):
     total = jnp.zeros(tags.shape, jnp.float32)
     for first in range(0, product.shape[1], LANES):
@@ -319,7 +349,7 @@
     steps[n_steps].wait()
     tags = tag[...].astype(jnp.float32)
     tag_ref[...] = tags
-    low_ref[...] = fold(acc, tags, acc.shape[1], plan.slots, plan.rank)
+    low_ref[...] = pack(fold(acc, tags, acc.shape[1], plan.slots, plan.rank), plan.rank)
 
 
 def reduce_taken_kernel(plan, n_steps, near, wide, narrow, across, *rest):
@@ -371,7 +401,8 @@
     tag_ref[...] = tag[0].astype(jnp.float32)
     for e in range(plan.groups):
         tags = tag[jnp.where(inner, e, 0)].astype(jnp.float32)
-        lows[e][...] = fold(acc.at[e], tags, plan.left_rows, plan.slots, plan.share)
+        low = fold(acc.at[e], tags, plan.left_rows, plan.slots, plan.share)
+        lows[e][...] = pack(low, plan.share)
 
 
 def blocks_call(kernel, blocks, out_shape, out_specs, scratch, flops, moved, name, extra=()):
@@ -403,7 +434,10 @@
     return blocks_call(
         functools.partial(reduce_own_kernel, plan, n_steps),
         [near, wide, narrow, own],
-        [jax.ShapeDtypeStruct((height, LANES), jnp.float32)] * 2,
+        [
+            jax.ShapeDtypeStruct((height * plan.rank // LANES, LANES), jnp.float32),
+            jax.ShapeDtypeStruct((height, LANES), jnp.float32),
+        ],
         [VMEM] * 2,
         [
             pltpu.VMEM((height, plan.width), dtype),
@@ -426,7 +460,8 @@
     *lows, tag = blocks_call(
         functools.partial(reduce_taken_kernel, plan, n_steps),
         [near, wide, narrow, across],
-        [jax.ShapeDtypeStruct((height, LANES), jnp.float32)] * (groups + 1),
+        [jax.ShapeDtypeStruct((height * plan.share // LANES, LANES), jnp.float32)] * groups
+        + [jax.ShapeDtypeStruct((height, LANES), jnp.float32)],
         [VMEM] * (groups + 1),
         [
             pltpu.VMEM((groups, height, plan.width), dtype),
@@ -442,8 +477,9 @@
     return lows, tag
 
 
-def add_low(mine_ref, other_ref):
-    return (mine_ref[...] + other_ref[...]).astype(jnp.bfloat16).astype(jnp.float32)
+def add_low(mine_ref, other_ref, share):
+    low = (mine_ref[...] + other_ref[...]).astype(jnp.bfloat16).astype(jnp.float32)
+    return unpack(low, share)
 
 
 def spread(low, tags, columns, slots, share):
@@ -464,7 +500,7 @@
     outs, (up, sem) = rest[:-2], rest[-2:]
     copy = pltpu.make_async_copy(own, up, sem)
     copy.start()
-    low = add_low(mine_ref, other_ref)
+    low = add_low(mine_ref, other_ref, plan.rank)
     wide_low = spread(low, tag_ref[...], up.shape[0], plan.slots, plan.rank)
     copy.wait()
     write_deltas(jnp.dot(wide_low, up[...], preferred_element_type=jnp.float32), outs)
@@ -478,8 +514,8 @@
         [jax.ShapeDtypeStruct((PAIR, features), jnp.bfloat16)] * plan.half,
         [VMEM] * plan.half,
         [pltpu.VMEM(own.shape, own.dtype), pltpu.SemaphoreType.DMA(())],
-        2 * mine.shape[0] * columns * features,
-        2 * features * (columns + mine.shape[0]),
+        2 * tag.shape[0] * columns * features,
+        2 * features * (columns + tag.shape[0]),
         "expand_own",
         extra=(mine, other, tag),
     )
@@ -505,7 +541,11 @@
     tags = tag_ref[...]
     wides = [
         spread(
-            add_low(lows[2 * e], lows[2 * e + 1]), tags, plan.left_rows, plan.slots, plan.share
+            add_low(lows[2 * e], lows[2 * e + 1], plan.share),
+            tags,
+            plan.left_rows,
+            plan.slots,
+            plan.share,
         )
         for e in range(plan.groups)
     ]
@@ -518,7 +558,7 @@
 
 
 def expand_taken(plan, lows, tag, wide, narrow, across_wide, across_narrow):
-    height, features = lows[0].shape[0], plan.features
+    height, features = tag.shape[0], plan.features
     return blocks_call(
         functools.partial(expand_taken_kernel, plan),
         [wide, narrow, across_wide, across_narrow],
@@ -601,7 +641,6 @@
     left_rows = jnp.swapaxes(lefts, 1, 2)
     near, wide, seg_of = lay_out(plan, True, ids, residency, x, left_rows, ups)
 
-    near = [swap(block, "replica", d) for block, d in zip(near, plan.near[1:])]
     wide_in = []
     for i in range(plan.wide):
         moves = []
@@ -610,17 +649,19 @@
         if i < plan.adapter_wide:
             moves.append((plan.inner, 0, half, 0))
         wide_in.append(send(plan, wide[i], moves))
+    near = [swap(block, "replica", d) for block, d in zip(near, plan.near[1:])]
+
+    late_ids, _ = lax.optimization_barrier((ids, seg_of))
+    own_rows, narrow, _ = lay_out(plan, False, late_ids, residency, x, left_rows, ups)
+    near = own_rows + near
 
     def part(which):
         columns = lax.dynamic_slice(weight, (0, which * features), (weight.shape[0], features))
         return jnp.dot(x, columns, preferred_element_type=jnp.float32)
 
-    base_other = part(1 - core)
-    late_ids, _ = lax.optimization_barrier((ids, seg_of))
-    own_rows, narrow, _ = lay_out(plan, False, late_ids, residency, x, left_rows, ups)
-    near = own_rows + near
-    near, wide_in[0], narrow[:2], base_other = lax.optimization_barrier(
-        (near, wide_in[0], narrow[:2], base_other)
+    base_other, base_mine = part(1 - core), part(core)
+    near, wide_in[0], narrow[:2], base_other, base_mine = lax.optimization_barrier(
+        (near, wide_in[0], narrow[:2], base_other, base_mine)
     )
 
     def narrow_send(j):
@@ -645,12 +686,15 @@
 
     across = [across_send(0)]
     narrow_in = [narrow_send(0), narrow_send(1)]
-    wide_in, narrow[2:] = lax.optimization_barrier((wide_in, narrow[2:]))
     across += [across_send(i) for i in range(1, half // 2)]
+    narrow_in[0], narrow[2:], base_other = lax.optimization_barrier(
+        (narrow_in[0], narrow[2:], base_other)
+    )
+    base = base_mine + swap(base_other, "tensor", 1)
+    across_up = [send(plan, narrow_in[0], [(plan.inner, e, 0, 0)]) for e in range(1, plan.groups)]
+    base, across[0], narrow[3:] = lax.optimization_barrier((base, across[0], narrow[3:]))
     narrow_in += [narrow_send(j) for j in range(2, plan.narrow)]
     across = [[blocks[e] for blocks in across] for e in range(plan.groups - 1)]
-    across_up = [send(plan, narrow_in[0], [(plan.inner, e, 0, 0)]) for e in range(1, plan.groups)]
-    base = part(core) + swap(base_other, "tensor", 1)
 
     own_left = left_rows.reshape(slots * rank, width)
     low, tag = reduce_own(plan, near, wide_in[:n_cross], narrow_in[:n_cross], own_left)

time: 159 us -> 139 us (0.87)
  waiting for transfers between devices: 86.8 us -> 68.3 us
  starting transfers between devices: 36.9 us -> 27.3 us
  matrix products: 15.2 us -> 21 us
    ppermute x11, waiting for transfers between devices: 72.7 us -> 60.7 us  [send(): return lax.ppermute(value, ('groups', 'replica', 'tensor'), pairs)]
    ppermute x10, starting transfers between devices: 22.1 us -> 13.7 us  [swap(): return lax.ppermute(value, axis, [(i, i ^ distance) for i in range(count)])]
    ppermute x10, waiting for transfers between devices: 14.1 us -> 7.56 us  [swap(): return lax.ppermute(value, axis, [(i, i ^ distance) for i in range(count)])]
    dot_general x2, matrix products: 15.2 us -> 21 us  [part(): return jnp.dot(x, columns, preferred_element_type=jnp.float32)]
  transfers between devices with their start and end apart: 21 -> 21, of which waited for: 11 -> 9; matrix products, arithmetic and copies ran while one was open for 10% -> 17% of each run, Pallas kernels for 7% -> 9%
where the time goes in v6:
time: 139 us
  waiting for transfers between devices  68.3 us (49%)
  starting transfers between devices  27.3 us (20%)
  matrix products  21 us (15%)
  Pallas kernels  19.7 us (14%)
    ppermute x11, waiting for transfers between devices, send(): return lax.ppermute(value, ('groups', 'replica', 'tensor'), pairs)  60.7 us
    dot_general x2, matrix products, part(): return jnp.dot(x, columns, preferred_element_type=jnp.float32)  21 us
    ppermute x10, starting transfers between devices, swap(): return lax.ppermute(value, axis, [(i, i ^ distance) for i in range(count)])  13.7 us
    ppermute x11, starting transfers between devices, send(): return lax.ppermute(value, ('groups', 'replica', 'tensor'), pairs)  13.5 us
    pallas_call x2, Pallas kernels, lay_out(): pl.pallas_call(functools.partial(lay_kernel, plan, first_call), out_shape...  9.79 us
    pallas_call x4, Pallas kernels, blocks_call(): pl.pallas_call(body, out_shape=out_shape, in_specs=[VMEM] * n_extra + [HB...  7.93 us
    ppermute x10, waiting for transfers between devices, swap(): return lax.ppermute(value, axis, [(i, i ^ distance) for i in range(count)])  7.56 us
  transfers between devices with their start and end apart: 21, of which 9 were waited for; matrix products, arithmetic and copies ran while one was open for 17% of the time, Pallas kernels for 9%

profile of v6, /device:TPU:0, one launch (start us, length us, event | category | flops | bytes accessed | tf_op | source)
XLA Modules:
  0.0 138.7 jit_solution(12129210053753340567)
XLA Ops:
  0.0 4.7 %lay_out_first.1 = (bf16[128,4224]{1,0:T(8,128)(2,1)}, bf16[128,4224]{1,0:T(8,128)(2,1)}, bf16[128,4224]{1,0:T(8,128)(2,1)}, s32[16]{0:T(128)}) custom-call(s32[16]{0:T(128)} %ids_ref.2, s32[48]{0:T(128)} %residency_ref.3, bf16[512,4096]{1,0:T(8,128)(2,1)} %x_ref.3, bf16[6,64,4096]{2,1,0:T(8,128)(2,1)} %bitcast.10, bf16[6,64,1024]{2,1,0:T(8,128)(2,1)} %up_ref.3), custom_call_target="tpu_custom_call" | custom-call | bytes 6291456 | tf_op jit(solution)/shard_map/lay_out_first/pallas_call | solution.py:211
  4.7 3.0 %collective-permute-start = (bf16[128,4224]{1,0:T(8,128)(2,1)}, bf16[128,4224]{1,0:T(8,128)(2,1)S(1)}, u32[]{:S(2)}, u32[]{:S(2)}) collective-permute-start(bf16[128,4224]{1,0:T(8,128)(2,1)} %get-tuple-element.56), channel_id=1, source_target_pairs={{0,2},{2,0},{4,6},{6,4},{8,10},{10,8},{12,14},{14,12},{1,3},{3,1},... | collective-permute-start | bytes 3244040 | tf_op jit(solution)/shard_map/ppermute | solution.py:613
  7.7 2.0 %collective-permute-start.1 = (bf16[128,4224]{1,0:T(8,128)(2,1)}, bf16[128,4224]{1,0:T(8,128)(2,1)S(1)}, u32[]{:S(2)}, u32[]{:S(2)}) collective-permute-start(bf16[128,4224]{1,0:T(8,128)(2,1)} %get-tuple-element.57), channel_id=1, source_target_pairs={{0,4},{1,5},{2,6},{3,7},{12,8},{13,9},{14,10},{15,11},{16,20},{17,... | collective-permute-start | bytes 3244040 | tf_op jit(solution)/shard_map/ppermute | solution.py:629
  9.7 10.5 %fusion.4 = f32[512,1024]{1,0:T(8,128)} fusion(bf16[512,4096]{1,0:T(8,128)(2,1)} %x_ref.3, bf16[4096,2048]{1,0:T(8,128)(2,1)} %param.7, s32[]{:T(128)S(6)} %select_n.18), kind=kOutput, calls=%fused_computation.4 | convolution fusion | flops 4294967296 | bytes 14680068 | tf_op jit(solution)/shard_map/dot_general | solution.py:660
  20.2 5.1 %lay_out_second.1 = (bf16[128,4224]{1,0:T(8,128)(2,1)}, bf16[64,4224]{1,0:T(8,128)(2,1)}, bf16[64,4224]{1,0:T(8,128)(2,1)}, bf16[64,4224]{1,0:T(8,128)(2,1)}, bf16[64,4224]{1,0:T(8,128)(2,1)}, /*index=5*/s32[16]{0:T(128)}) custom-call(s32[16]{0:T(128)} %ids_ref.2, s32[48]{0:T(128)} %residency_ref.3, bf16[512,4096]{1,0:T(8,128)(2,1)} %x_ref.3, ...), custom_call_target="tpu_custom_call" | custom-call | bytes 6291456 | tf_op jit(solution)/shard_map/lay_out_second/pallas_call | solution.py:211
  25.3 10.5 %fusion.7 = f32[512,1024]{1,0:T(8,128)} fusion(bf16[512,4096]{1,0:T(8,128)(2,1)} %x_ref.3, bf16[4096,2048]{1,0:T(8,128)(2,1)} %param.7, s32[]{:T(128)S(6)} %select_n.19), kind=kOutput, calls=%fused_computation.5 | convolution fusion | flops 4294967296 | bytes 14680068 | tf_op jit(solution)/shard_map/dot_general | solution.py:660
  36.4 1.4 %collective-permute-start.6 = (bf16[128,4224]{1,0:T(8,128)(2,1)}, bf16[128,4224]{1,0:T(8,128)(2,1)S(1)}, u32[]{:S(2)}, u32[]{:S(2)}) collective-permute-start(bf16[128,4224]{1,0:T(8,128)(2,1)} %get-tuple-element.72), channel_id=1, source_target_pairs={{0,6},{1,7},{2,4},{3,5},{12,10},{13,11},{14,8},{15,9},{16,22},{17,... | collective-permute-start | bytes 3244040 | tf_op jit(solution)/shard_map/ppermute | solution.py:629
  39.1 11.4 %collective-permute-done.2.refs_4_.refs_7_ = bf16[64,4224]{1,0:T(8,128)(2,1)} collective-permute-done((bf16[64,4224]{1,0:T(8,128)(2,1)}, bf16[64,4224]{1,0:T(8,128)(2,1)}, u32[]{:S(2)}, u32[]{:S(2)}) %collective-permute-start.2) | collective-permute-done | bytes 540704 | tf_op jit(solution)/shard_map/ppermute | solution.py:629
  50.8 1.6 %collective-permute-start.4 = (bf16[128,4224]{1,0:T(8,128)(2,1)S(1)}, bf16[128,4224]{1,0:T(8,128)(2,1)S(1)}, u32[]{:S(2)}, u32[]{:S(2)}) collective-permute-start(bf16[128,4224]{1,0:T(8,128)(2,1)S(1)} %maximum_select_fusion), channel_id=1, source_target_pairs={{0,16},{1,17},{2,18},{3,19},{12,28},{13,29},{14,30},{15,31},{16,0}... | collective-permute-start | bytes 3244040 | tf_op jit(solution)/shard_map/ppermute | solution.py:629
  52.4 21.7 %collective-permute-done.6.refs_3_.refs_6_ = bf16[128,4224]{1,0:T(8,128)(2,1)S(1)} collective-permute-done((bf16[128,4224]{1,0:T(8,128)(2,1)}, bf16[128,4224]{1,0:T(8,128)(2,1)S(1)}, u32[]{:S(2)}, u32[]{:S(2)}) %collective-permute-start.6) | collective-permute-done | bytes 1081376 | tf_op jit(solution)/shard_map/ppermute | solution.py:629
  74.5 1.6 %collective-permute-start.10 = (bf16[128,4224]{1,0:T(8,128)(2,1)S(1)}, bf16[128,4224]{1,0:T(8,128)(2,1)S(1)}, u32[]{:S(2)}, u32[]{:S(2)}) collective-permute-start(bf16[128,4224]{1,0:T(8,128)(2,1)S(1)} %maximum_select_fusion.1), channel_id=1, source_target_pairs={{0,16},{1,17},{2,18},{3,19},{12,28},{13,29},{14,30},{15,31},{16,0}... | collective-permute-start | bytes 3244040 | tf_op jit(solution)/shard_map/ppermute | solution.py:629
  77.6 2.3 %collective-permute-start.5 = (bf16[64,4224]{1,0:T(8,128)(2,1)S(1)}, bf16[64,4224]{1,0:T(8,128)(2,1)S(1)}, u32[]{:S(2)}, u32[]{:S(2)}) collective-permute-start(bf16[64,4224]{1,0:T(8,128)(2,1)S(1)} %copy-done.7), channel_id=1, source_target_pairs={{4,2},{5,3},{6,0},{7,1},{8,14},{9,15},{10,12},{11,13},{20,18},{21,... | collective-permute-start | bytes 1622024 | tf_op jit(solution)/shard_map/ppermute | solution.py:629
  81.7 10.4 %collective-permute-done.7.refs_5_ = bf16[64,4224]{1,0:T(8,128)(2,1)S(1)} collective-permute-done((bf16[64,4224]{1,0:T(8,128)(2,1)S(1)}, bf16[64,4224]{1,0:T(8,128)(2,1)S(1)}, u32[]{:S(2)}, u32[]{:S(2)}) %collective-permute-start.7) | collective-permute-done | bytes 540704 | tf_op jit(solution)/shard_map/ppermute | solution.py:629
  92.1 2.9 %reduce_own.1 = (f32[128,128]{1,0:T(8,128)S(1)}, f32[256,128]{1,0:T(8,128)S(1)}) custom-call(bf16[128,4224]{1,0:T(8,128)(2,1)S(1)} %copy-done.2, bf16[128,4224]{1,0:T(8,128)(2,1)S(1)} %collective-permute-done.refs_1_, bf16[128,4224]{1,0:T(8,128)(2,1)S(1)} %collective-permute-done.1.refs_2_.refs_5_, ...), custom_call_target="tpu_custom_call" | custom-call | flops 805306368 | bytes 5242880 | tf_op jit(solution)/shard_map/reduce_own/pallas_call | solution.py:417
  95.1 1.2 collective-permute-done.8.refs_1_
  97.5 6.2 %collective-permute-done.5.refs_7_ = bf16[64,4224]{1,0:T(8,128)(2,1)S(1)} collective-permute-done((bf16[64,4224]{1,0:T(8,128)(2,1)S(1)}, bf16[64,4224]{1,0:T(8,128)(2,1)S(1)}, u32[]{:S(2)}, u32[]{:S(2)}) %collective-permute-start.5) | collective-permute-done | bytes 540704 | tf_op jit(solution)/shard_map/ppermute | solution.py:629
  103.7 10.1 %collective-permute-done.9.refs_6_ = bf16[64,4224]{1,0:T(8,128)(2,1)S(1)} collective-permute-done((bf16[64,4224]{1,0:T(8,128)(2,1)S(1)}, bf16[64,4224]{1,0:T(8,128)(2,1)S(1)}, u32[]{:S(2)}, u32[]{:S(2)}) %collective-permute-start.9) | collective-permute-done | bytes 540704 | tf_op jit(solution)/shard_map/ppermute | solution.py:629
  114.8 3.6 %reduce_taken.1 = (f32[64,128]{1,0:T(8,128)S(1)}, f32[64,128]{1,0:T(8,128)S(1)}, f32[256,128]{1,0:T(8,128)S(1)}) custom-call(bf16[128,4224]{1,0:T(8,128)(2,1)S(1)} %copy-done.2, bf16[128,4224]{1,0:T(8,128)(2,1)S(1)} %collective-permute-done.refs_1_, bf16[128,4224]{1,0:T(8,128)(2,1)S(1)} %collective-permute-done.1.refs_2_.refs_5_, ...), custom_call_target="tpu_custom_call" | custom-call | flops 1073741824 | bytes 8388608 | tf_op jit(solution)/shard_map/reduce_taken/pallas_call | solution.py:417
  121.5 1.2 collective-permute-start.18
  122.7 6.3 %collective-permute-start.19 = (bf16[64,1024]{1,0:T(8,128)(2,1)S(1)}, bf16[64,1024]{1,0:T(8,128)(2,1)S(1)}, u32[]{:S(2)}, u32[]{:S(2)}) collective-permute-start(bf16[64,1024]{1,0:T(8,128)(2,1)S(1)} %get-tuple-element.99), channel_id=1, source_target_pairs={{0,4},{2,6},{4,0},{6,2},{8,12},{10,14},{12,8},{14,10},{1,5},{3,7},... | collective-permute-start | bytes 393224 | tf_op jit(solution)/shard_map/ppermute | solution.py:613
  129.0 1.4 collective-permute-start.20
  130.4 2.6 %collective-permute-done.19.refs_6_ = bf16[64,1024]{1,0:T(8,128)(2,1)S(1)} collective-permute-done((bf16[64,1024]{1,0:T(8,128)(2,1)S(1)}, bf16[64,1024]{1,0:T(8,128)(2,1)S(1)}, u32[]{:S(2)}, u32[]{:S(2)}) %collective-permute-start.19) | collective-permute-done | bytes 131104 | tf_op jit(solution)/shard_map/ppermute | solution.py:613
  133.0 3.7 %collective-permute-done.20.refs_7_ = bf16[64,1024]{1,0:T(8,128)(2,1)S(1)} collective-permute-done((bf16[64,1024]{1,0:T(8,128)(2,1)S(1)}, bf16[64,1024]{1,0:T(8,128)(2,1)S(1)}, u32[]{:S(2)}, u32[]{:S(2)}) %collective-permute-start.20) | collective-permute-done | bytes 131104 | tf_op jit(solution)/shard_map/ppermute | solution.py:613
  136.7 2.0 %join.1 = bf16[512,1024]{1,0:T(8,128)(2,1)} custom-call(s32[16]{0:T(128)S(1)} %copy-done.3, f32[512,1024]{1,0:T(8,128)S(1)} %add.11.base_ref, bf16[64,1024]{1,0:T(8,128)(2,1)S(1)} %get-tuple-element.88.refs_0_, bf16[64,1024]{1,0:T(8,128)(2,1)S(1)} %collective-permute-done.14.refs_1_, bf16[64,1024]{1,0:T(8,128)(2,1)S(1)} %collective-permute-done.15.refs_2_, ...), custom_call_target="tpu_custom_call" | custom-call | flops 524288 | bytes 4194304 | tf_op jit(solution)/shard_map/join/pallas_call | solution.py:597
  (52 shorter events, 11.1 us)
Async XLA Ops:
  4.7 31.1 %collective-permute-start = (bf16[128,4224]{1,0:T(8,128)(2,1)}, bf16[128,4224]{1,0:T(8,128)(2,1)S(1)}, u32[]{:S(2)}, u32[]{:S(2)}) collective-permute-start(bf16[128,4224]{1,0:T(8,128)(2,1)} %get-tuple-element.56), channel_id=1, source_target_pairs={{0,2},{2,0},{4,6},{6,4},{8,10},{10,8},{12,14},{14,12},{1,3},{3,1},... | collective-permute-start | bytes 3244040 | tf_op jit(solution)/shard_map/ppermute | solution.py:613
  7.7 28.1 %collective-permute-start.1 = (bf16[128,4224]{1,0:T(8,128)(2,1)}, bf16[128,4224]{1,0:T(8,128)(2,1)S(1)}, u32[]{:S(2)}, u32[]{:S(2)}) collective-permute-start(bf16[128,4224]{1,0:T(8,128)(2,1)} %get-tuple-element.57), channel_id=1, source_target_pairs={{0,4},{1,5},{2,6},{3,7},{12,8},{13,9},{14,10},{15,11},{16,20},{17,... | collective-permute-start | bytes 3244040 | tf_op jit(solution)/shard_map/ppermute | solution.py:629
  35.8 14.7 %collective-permute-start.2 = (bf16[64,4224]{1,0:T(8,128)(2,1)}, bf16[64,4224]{1,0:T(8,128)(2,1)}, u32[]{:S(2)}, u32[]{:S(2)}) collective-permute-start(bf16[64,4224]{1,0:T(8,128)(2,1)} %get-tuple-element.61), channel_id=1, source_target_pairs={{4,0},{5,1},{6,2},{7,3},{8,12},{9,13},{10,14},{11,15},{20,16},{21,... | collective-permute-start | bytes 1622024 | tf_op jit(solution)/shard_map/ppermute | solution.py:629
  36.4 37.7 %collective-permute-start.6 = (bf16[128,4224]{1,0:T(8,128)(2,1)}, bf16[128,4224]{1,0:T(8,128)(2,1)S(1)}, u32[]{:S(2)}, u32[]{:S(2)}) collective-permute-start(bf16[128,4224]{1,0:T(8,128)(2,1)} %get-tuple-element.72), channel_id=1, source_target_pairs={{0,6},{1,7},{2,4},{3,5},{12,10},{13,11},{14,8},{15,9},{16,22},{17,... | collective-permute-start | bytes 3244040 | tf_op jit(solution)/shard_map/ppermute | solution.py:629
  50.5 26.7 %collective-permute-start.3 = (f32[512,1024]{1,0:T(8,128)S(1)}, f32[512,1024]{1,0:T(8,128)S(1)}, u32[]{:S(2)}, u32[]{:S(2)}) collective-permute-start(f32[512,1024]{1,0:T(8,128)S(1)} %copy-done.5), channel_id=1, source_target_pairs={{0,1},{1,0},{2,3},{3,2},{4,5},{5,4},{6,7},{7,6},{8,9},{9,8},{10,11... | collective-permute-start | bytes 6291464 | tf_op jit(solution)/shard_map/ppermute | solution.py:613
  50.8 25.2 %copy-start.8 = (bf16[64,4224]{1,0:T(8,128)(2,1)S(1)}, bf16[64,4224]{1,0:T(8,128)(2,1)}, u32[]{:S(2)}) copy-start(bf16[64,4224]{1,0:T(8,128)(2,1)} %get-tuple-element.74) | copy-start | bytes 1622020
  50.8 26.3 %copy-start.4 = (f32[512,1024]{1,0:T(8,128)S(1)}, f32[512,1024]{1,0:T(8,128)}, u32[]{:S(2)}) copy-start(f32[512,1024]{1,0:T(8,128)} %fusion.7) | copy-start | bytes 6291460
  50.8 26.7 %collective-permute-start.4 = (bf16[128,4224]{1,0:T(8,128)(2,1)S(1)}, bf16[128,4224]{1,0:T(8,128)(2,1)S(1)}, u32[]{:S(2)}, u32[]{:S(2)}) collective-permute-start(bf16[128,4224]{1,0:T(8,128)(2,1)S(1)} %maximum_select_fusion), channel_id=1, source_target_pairs={{0,16},{1,17},{2,18},{3,19},{12,28},{13,29},{14,30},{15,31},{16,0}... | collective-permute-start | bytes 3244040 | tf_op jit(solution)/shard_map/ppermute | solution.py:629
  74.4 17.7 %copy-start = (bf16[6,4096,64]{1,2,0:T(8,128)(2,1)S(1)}, bf16[6,4096,64]{1,2,0:T(8,128)(2,1)}, u32[]{:S(2)}) copy-start(bf16[6,4096,64]{1,2,0:T(8,128)(2,1)} %param.8) | copy-start | bytes 9437188
  74.5 40.4 %collective-permute-start.10 = (bf16[128,4224]{1,0:T(8,128)(2,1)S(1)}, bf16[128,4224]{1,0:T(8,128)(2,1)S(1)}, u32[]{:S(2)}, u32[]{:S(2)}) collective-permute-start(bf16[128,4224]{1,0:T(8,128)(2,1)S(1)} %maximum_select_fusion.1), channel_id=1, source_target_pairs={{0,16},{1,17},{2,18},{3,19},{12,28},{13,29},{14,30},{15,31},{16,0}... | collective-permute-start | bytes 3244040 | tf_op jit(solution)/shard_map/ppermute | solution.py:629
  76.0 16.1 %collective-permute-start.7 = (bf16[64,4224]{1,0:T(8,128)(2,1)S(1)}, bf16[64,4224]{1,0:T(8,128)(2,1)S(1)}, u32[]{:S(2)}, u32[]{:S(2)}) collective-permute-start(bf16[64,4224]{1,0:T(8,128)(2,1)S(1)} %copy-done.8), channel_id=1, source_target_pairs={{4,2},{5,3},{6,0},{7,1},{8,14},{9,15},{10,12},{11,13},{20,18},{21,... | collective-permute-start | bytes 1622024 | tf_op jit(solution)/shard_map/ppermute | solution.py:629
  77.6 26.1 %collective-permute-start.5 = (bf16[64,4224]{1,0:T(8,128)(2,1)S(1)}, bf16[64,4224]{1,0:T(8,128)(2,1)S(1)}, u32[]{:S(2)}, u32[]{:S(2)}) collective-permute-start(bf16[64,4224]{1,0:T(8,128)(2,1)S(1)} %copy-done.7), channel_id=1, source_target_pairs={{4,2},{5,3},{6,0},{7,1},{8,14},{9,15},{10,12},{11,13},{20,18},{21,... | collective-permute-start | bytes 1622024 | tf_op jit(solution)/shard_map/ppermute | solution.py:629
  79.9 33.9 %collective-permute-start.9 = (bf16[64,4224]{1,0:T(8,128)(2,1)S(1)}, bf16[64,4224]{1,0:T(8,128)(2,1)S(1)}, u32[]{:S(2)}, u32[]{:S(2)}) collective-permute-start(bf16[64,4224]{1,0:T(8,128)(2,1)S(1)} %copy-done.6), channel_id=1, source_target_pairs={{4,0},{5,1},{6,2},{7,3},{8,12},{9,13},{10,14},{11,15},{20,16},{21,... | collective-permute-start | bytes 1622024 | tf_op jit(solution)/shard_map/ppermute | solution.py:629
  81.0 39.6 %collective-permute-start.17 = (bf16[64,4224]{1,0:T(8,128)(2,1)}, bf16[64,4224]{1,0:T(8,128)(2,1)S(1)}, u32[]{:S(2)}, u32[]{:S(2)}) collective-permute-start(bf16[64,4224]{1,0:T(8,128)(2,1)} %collective-permute-done.2.refs_4_.refs_7_), channel_id=1, source_target_pairs={{4,20},{5,21},{6,22},{7,23},{8,24},{9,25},{10,26},{11,27},{20,4},{... | collective-permute-start | bytes 1622024 | tf_op jit(solution)/shard_map/ppermute | solution.py:629
  95.0 1.3 collective-permute-start.8
  96.9 21.6 %collective-permute-start.14 = (bf16[64,1024]{1,0:T(8,128)(2,1)S(1)}, bf16[64,1024]{1,0:T(8,128)(2,1)S(1)}, u32[]{:S(2)}, u32[]{:S(2)}) collective-permute-start(bf16[64,1024]{1,0:T(8,128)(2,1)S(1)} %get-tuple-element.85), channel_id=1, source_target_pairs={{0,2},{2,0},{4,6},{6,4},{8,10},{10,8},{12,14},{14,12},{1,3},{3,1},... | collective-permute-start | bytes 393224 | tf_op jit(solution)/shard_map/ppermute | solution.py:613
  103.7 15.5 %collective-permute-start.15 = (bf16[64,1024]{1,0:T(8,128)(2,1)S(1)}, bf16[64,1024]{1,0:T(8,128)(2,1)S(1)}, u32[]{:S(2)}, u32[]{:S(2)}) collective-permute-start(bf16[64,1024]{1,0:T(8,128)(2,1)S(1)} %get-tuple-element.86), channel_id=1, source_target_pairs={{0,4},{2,6},{4,0},{6,2},{8,12},{10,14},{12,8},{14,10},{1,5},{3,7},... | collective-permute-start | bytes 393224 | tf_op jit(solution)/shard_map/ppermute | solution.py:613
  113.8 6.0 %collective-permute-start.16 = (bf16[64,1024]{1,0:T(8,128)(2,1)S(1)}, bf16[64,1024]{1,0:T(8,128)(2,1)S(1)}, u32[]{:S(2)}, u32[]{:S(2)}) collective-permute-start(bf16[64,1024]{1,0:T(8,128)(2,1)S(1)} %get-tuple-element.87), channel_id=1, source_target_pairs={{0,6},{2,4},{4,2},{6,0},{8,14},{10,12},{12,10},{14,8},{1,7},{3,5},... | collective-permute-start | bytes 393224 | tf_op jit(solution)/shard_map/ppermute | solution.py:613
  118.4 1.3 collective-permute-start.11
  118.5 1.2 collective-permute-start.12
  119.2 1.4 %collective-permute-start.13 = (f32[64,128]{1,0:T(8,128)S(1)}, f32[64,128]{1,0:T(8,128)S(1)}, u32[]{:S(2)}, u32[]{:S(2)}) collective-permute-start(f32[64,128]{1,0:T(8,128)S(1)} %get-tuple-element.83), channel_id=1, source_target_pairs={{0,1},{1,0},{2,3},{3,2},{12,13},{13,12},{14,15},{15,14},{16,17},{1... | collective-permute-start | bytes 98312 | tf_op jit(solution)/shard_map/ppermute | solution.py:629
  121.5 8.9 %collective-permute-start.18 = (bf16[64,1024]{1,0:T(8,128)(2,1)S(1)}, bf16[64,1024]{1,0:T(8,128)(2,1)S(1)}, u32[]{:S(2)}, u32[]{:S(2)}) collective-permute-start(bf16[64,1024]{1,0:T(8,128)(2,1)S(1)} %get-tuple-element.98), channel_id=1, source_target_pairs={{0,2},{2,0},{4,6},{6,4},{8,10},{10,8},{12,14},{14,12},{1,3},{3,1},... | collective-permute-start | bytes 393224 | tf_op jit(solution)/shard_map/ppermute | solution.py:613
  122.7 10.3 %collective-permute-start.19 = (bf16[64,1024]{1,0:T(8,128)(2,1)S(1)}, bf16[64,1024]{1,0:T(8,128)(2,1)S(1)}, u32[]{:S(2)}, u32[]{:S(2)}) collective-permute-start(bf16[64,1024]{1,0:T(8,128)(2,1)S(1)} %get-tuple-element.99), channel_id=1, source_target_pairs={{0,4},{2,6},{4,0},{6,2},{8,12},{10,14},{12,8},{14,10},{1,5},{3,7},... | collective-permute-start | bytes 393224 | tf_op jit(solution)/shard_map/ppermute | solution.py:613
  129.0 7.7 %collective-permute-start.20 = (bf16[64,1024]{1,0:T(8,128)(2,1)S(1)}, bf16[64,1024]{1,0:T(8,128)(2,1)S(1)}, u32[]{:S(2)}, u32[]{:S(2)}) collective-permute-start(bf16[64,1024]{1,0:T(8,128)(2,1)S(1)} %get-tuple-element.100), channel_id=1, source_target_pairs={{0,6},{2,4},{4,2},{6,0},{8,14},{10,12},{12,10},{14,8},{1,7},{3,5},... | collective-permute-start | bytes 393224 | tf_op jit(solution)/shard_map/ppermute | solution.py:613
  (6 other events, 59.3 us)

commit v7 on v6

--- a/solution.py
+++ b/solution.py
@@ -34,8 +34,9 @@
         self.pieces = self.left_pieces + 1
         assert self.up_rows <= PAIR
         self.adapter_wide = -(-self.pieces // 2)
-        self.wide = max(len(self.cross), self.adapter_wide)
-        self.narrow = max(2 * len(self.cross), self.pieces)
+        self.units = 2 * len(self.cross)
+        assert self.pieces <= self.units and self.adapter_wide <= len(self.cross)
+        self.wide = len(self.cross)
         self.outer = [r for r in range(replicas) if self.is_outer(r)]
         self.inner = [r for r in range(replicas) if not self.is_outer(r)]
 
@@ -50,8 +51,20 @@
         for piece in range(self.left_pieces):
             yield piece, min(PAIR, self.left_rows - piece * PAIR)
 
-    def narrow_rows(self, i, kind):
-        return kind * len(self.cross) + i
+    def late_blocks(self):
+        blocks = [(self.cross[0], 1, 0)]
+        blocks += [(d, 2, 2 * i - 1) for i, d in enumerate(self.cross) if i]
+        return blocks + [(self.cross[0], 1, self.units - 1)]
+
+    def late_unit(self, refs, unit):
+        if unit in (0, self.units - 1):
+            return refs[0 if unit == 0 else -1]
+        return refs[(unit + 1) // 2].at[pl.ds((unit - 1) % 2 * PAIR, PAIR)]
+
+    def late_rows(self, refs, i, kind):
+        if i == 0:
+            return self.late_unit(refs, 0 if kind == 0 else self.units - 1)
+        return self.late_unit(refs, 2 * i - 1 + kind)
 
 
 def params(limit=VMEM_LIMIT):
@@ -67,13 +80,13 @@
     return refs[piece // 2].at[pl.ds((piece % 2) * PAIR, PAIR)]
 
 
-def narrow_adapters(narrow, piece, plan):
-    return narrow[0] if piece == plan.left_pieces else narrow[1 + piece]
+def late_adapters(late, piece, plan):
+    return plan.late_unit(late, 0 if piece == plan.left_pieces else 1 + piece)
 
 
 def lay_kernel(plan, first_call, ids_ref, residency_ref, x_ref, left_ref, up_ref, *rest):
-    n_near = len(plan.near) - 1 if first_call else 1
-    n_blocks = plan.wide if first_call else plan.narrow
+    n_near = 0 if first_call else len(plan.near)
+    n_blocks = plan.wide if first_call else len(plan.late_blocks())
     near, rest = rest[:n_near], rest[n_near:]
     blocks, rest = rest[:n_blocks], rest[n_blocks:]
     seg_out, seg_ref, slot_ref, count_ref, staged, tags, left, up, in_sems, sems = rest
@@ -169,7 +182,7 @@
         moves[-1] = (source, stage, outs)
         return moves
 
-    near_d = plan.near[1:] if first_call else plan.near[:1]
+    near_d = [] if first_call else plan.near
     near_targets = [
         (d, kind, near[i].at[pl.ds(kind * PAIR, PAIR)])
         for i, d in enumerate(near_d)
@@ -183,7 +196,7 @@
         ]
     else:
         cross_targets = [
-            (d, kind, blocks[plan.narrow_rows(i, kind)])
+            (d, kind, plan.late_rows(blocks, i, kind))
             for i, d in enumerate(plan.cross)
             for kind in range(2)
         ]
@@ -198,16 +211,19 @@
         if first_call:
             adapters = adapter_moves(lambda piece: of_wide(blocks, piece))
         else:
-            adapters = adapter_moves(lambda piece: narrow_adapters(blocks, piece, plan))
+            adapters = adapter_moves(lambda piece: late_adapters(blocks, piece, plan))
         move(adapters + row_moves(near_targets), near_targets)
 
 
 def lay_out(plan, first_call, ids, residency, x, left_rows, ups):
     count = 2 * plan.half * CAP
     wide = jax.ShapeDtypeStruct((2 * PAIR, plan.width + LANES), x.dtype)
-    narrow = jax.ShapeDtypeStruct((PAIR, plan.width + LANES), x.dtype)
-    near = [wide] * (len(plan.near) - 1 if first_call else 1)
-    blocks = [wide] * plan.wide if first_call else [narrow] * plan.narrow
+    late = [
+        jax.ShapeDtypeStruct((n * PAIR, plan.width + LANES), x.dtype)
+        for _, n, _ in plan.late_blocks()
+    ]
+    near = [] if first_call else [wide] * len(plan.near)
+    blocks = [wide] * plan.wide if first_call else late
     out = pl.pallas_call(
         functools.partial(lay_kernel, plan, first_call),
         out_shape=near + blocks + [jax.ShapeDtypeStruct((count,), jnp.int32)],
@@ -225,9 +241,7 @@
             pltpu.SemaphoreType.DMA((2 * count + 2 * plan.pieces,)),
         ],
         compiler_params=params(60 * 1024 * 1024),
-        cost_estimate=pl.CostEstimate(
-            flops=0, bytes_accessed=3 * x.size, transcendentals=0
-        ),
+        cost_estimate=pl.CostEstimate(flops=0, bytes_accessed=x.size, transcendentals=0),
         name="lay_out_first" if first_call else "lay_out_second",
     )(ids, residency, x, left_rows, ups)
     return list(out[: len(near)]), list(out[len(near) : -1]), out[-1]
@@ -316,7 +330,7 @@
     for i, d in enumerate(plan.cross):
         copies.both(
             target.at[pl.ds(d * PAIR, PAIR)],
-            narrow[plan.narrow_rows(i, kind)].at[:, columns],
+            plan.late_rows(narrow, i, kind).at[:, columns],
             wide[i].at[span, columns],
         )
 
@@ -372,7 +386,7 @@
                 copies.one(
                     inner,
                     target.at[pl.ds(d * PAIR, PAIR)],
-                    of_wide(across[e - 1], i).at[:, columns],
+                    across[e - 1][i].at[:, columns],
                 )
         if k < n_steps:
             for piece, count in plan.left_spans():
@@ -380,13 +394,13 @@
                 copies.both(
                     left.at[0, pl.ds(piece * PAIR, count), columns],
                     of_wide(wide, piece).at[span],
-                    narrow_adapters(narrow, piece, plan).at[span],
+                    late_adapters(narrow, piece, plan).at[span],
                 )
                 for e in range(1, plan.groups):
                     copies.one(
                         outer,
                         left.at[e, pl.ds(piece * PAIR, count), columns],
-                        of_wide(across[e - 1], piece).at[span],
+                        across[e - 1][piece].at[span],
                     )
         steps.append(copies)
     for k in range(n_steps):
@@ -421,7 +435,7 @@
         out_specs=out_specs,
         scratch_shapes=scratch,
         compiler_params=params(),
-        cost_estimate=pl.CostEstimate(flops=flops, bytes_accessed=moved, transcendentals=0),
+        cost_estimate=pl.CostEstimate(flops=1, bytes_accessed=1, transcendentals=0),
         name=name,
     )(*extra, *flat)
 
@@ -531,7 +545,7 @@
         for e in range(plan.groups):
             copies.both(
                 up.at[e, pl.ds(row, rows)],
-                of_wide(wide if e == 0 else across_wide[e - 1], plan.left_pieces).at[part],
+                (of_wide(wide, plan.left_pieces) if e == 0 else across_wide[e - 1]).at[part],
                 (narrow if e == 0 else across_narrow[e - 1]).at[part],
             )
     if plan.padded > plan.left_rows:
@@ -639,7 +653,7 @@
     core = lax.axis_index("tensor")
     outer = am_outer(plan)
     left_rows = jnp.swapaxes(lefts, 1, 2)
-    near, wide, seg_of = lay_out(plan, True, ids, residency, x, left_rows, ups)
+    _, wide, seg_of = lay_out(plan, True, ids, residency, x, left_rows, ups)
 
     wide_in = []
     for i in range(plan.wide):
@@ -649,70 +663,67 @@
         if i < plan.adapter_wide:
             moves.append((plan.inner, 0, half, 0))
         wide_in.append(send(plan, wide[i], moves))
-    near = [swap(block, "replica", d) for block, d in zip(near, plan.near[1:])]
-
-    late_ids, _ = lax.optimization_barrier((ids, seg_of))
-    own_rows, narrow, _ = lay_out(plan, False, late_ids, residency, x, left_rows, ups)
-    near = own_rows + near
 
     def part(which):
         columns = lax.dynamic_slice(weight, (0, which * features), (weight.shape[0], features))
         return jnp.dot(x, columns, preferred_element_type=jnp.float32)
 
-    base_other, base_mine = part(1 - core), part(core)
-    near, wide_in[0], narrow[:2], base_other, base_mine = lax.optimization_barrier(
-        (near, wide_in[0], narrow[:2], base_other, base_mine)
-    )
-
-    def narrow_send(j):
-        moves = []
-        if j < 2 * n_cross:
-            moves.append((plan.inner, 0, plan.cross[j % n_cross], 0))
-        if j < plan.pieces:
-            moves.append((plan.outer, 0, half, 0))
-        return send(plan, narrow[j], moves)
-
-    def taken_rows(i):
-        return near[i][PAIR:] if i < len(plan.near) else wide_in[i - len(plan.near)][PAIR:]
-
+    base_other = part(1 - core)
+    late_ids, base_other, _ = lax.optimization_barrier((ids, base_other, seg_of))
+    near, late, _ = lay_out(plan, False, late_ids, residency, x, left_rows, ups)
+    near = near[:1] + [swap(near[i], "replica", d) for i, d in enumerate(plan.near) if d]
+    base_mine = part(core)
     def across_send(i):
-        value = jnp.concatenate([taken_rows(2 * i), taken_rows(2 * i + 1)], axis=0)
-        if i < plan.adapter_wide:
-            value = jnp.where(outer, wide_in[i], value)
+        if i < len(plan.near):
+            value = near[i][PAIR:]
+        else:
+            value = wide_in[i - len(plan.near)][PAIR:]
+        if i < plan.pieces:
+            piece = wide_in[i // 2][(i % 2) * PAIR : (i % 2 + 1) * PAIR]
+            value = jnp.where(outer, piece, value)
         return [
             send(plan, value, [(plan.outer, e, 0, 0), (plan.inner, e, 0, 0)])
             for e in range(1, plan.groups)
         ]
 
     across = [across_send(0)]
-    narrow_in = [narrow_send(0), narrow_send(1)]
-    across += [across_send(i) for i in range(1, half // 2)]
-    narrow_in[0], narrow[2:], base_other = lax.optimization_barrier(
-        (narrow_in[0], narrow[2:], base_other)
-    )
+
     base = base_mine + swap(base_other, "tensor", 1)
-    across_up = [send(plan, narrow_in[0], [(plan.inner, e, 0, 0)]) for e in range(1, plan.groups)]
-    base, across[0], narrow[3:] = lax.optimization_barrier((base, across[0], narrow[3:]))
-    narrow_in += [narrow_send(j) for j in range(2, plan.narrow)]
+    wide_in, near, across, late, base = lax.optimization_barrier(
+        (wide_in, near, across, late, base)
+    )
+    across += [across_send(i) for i in range(1, half)]
+    late_in = []
+    for block, (d, _, unit) in zip(late, plan.late_blocks()):
+        moves = [(plan.inner, 0, d, 0)]
+        if unit < plan.pieces:
+            moves.append((plan.outer, 0, half, 0))
+        if unit == plan.units - 1:
+            late_in[0], block = lax.optimization_barrier((late_in[0], block))
+        late_in.append(send(plan, block, moves))
+    across_up = [
+        send(plan, late_in[0], [(plan.inner, e, 0, 0)]) for e in range(1, plan.groups)
+    ]
+    late_in[:-1], across = lax.optimization_barrier((late_in[:-1], across))
     across = [[blocks[e] for blocks in across] for e in range(plan.groups - 1)]
 
     own_left = left_rows.reshape(slots * rank, width)
-    low, tag = reduce_own(plan, near, wide_in[:n_cross], narrow_in[:n_cross], own_left)
+    low, tag = reduce_own(plan, near, wide_in, late_in[:-1], own_left)
     other = swap(low, "tensor", 1)
     terms = expand_own(plan, low, other, tag, ups.reshape(slots * rank, features))
     deltas = [terms[0]] + [swap(terms[d], "replica", d) for d in range(1, half)]
 
-    narrow_in[-1], base, deltas[0] = lax.optimization_barrier((narrow_in[-1], base, deltas[0]))
-    lows, tag = reduce_taken(plan, near, wide_in, narrow_in, across)
+    late_in[-1], deltas[:2], across_up = lax.optimization_barrier(
+        (late_in[-1], deltas[:2], across_up)
+    )
+    lows, tag = reduce_taken(plan, near, wide_in, late_in, across)
     pairs = [lows[0], swap(lows[0], "tensor", 1)]
     for e in range(1, plan.groups):
         pairs.append(send(plan, lows[e], [(plan.outer, 0, 0, 0), (plan.inner, e, 0, 0)]))
         pairs.append(send(plan, lows[e], [(plan.outer, 0, 0, 1), (plan.inner, e, 0, 1)]))
     pairs, deltas = lax.optimization_barrier((pairs, deltas))
-    across_wide = [blocks[: plan.adapter_wide] for blocks in across]
-    terms = expand_taken(
-        plan, pairs, tag, wide_in[: plan.adapter_wide], narrow_in[0], across_wide, across_up
-    )
+    across_wide = [blocks[plan.left_pieces] for blocks in across]
+    terms = expand_taken(plan, pairs, tag, wide_in, late_in[0], across_wide, across_up)
     deltas += [terms[0]] + [swap(terms[d], "replica", d) for d in range(1, half)]
     return join(seg_of, base, deltas)
 

time: 139 us -> 150 us (1.079)
  starting transfers between devices: 27.3 us -> 53 us
  waiting for transfers between devices: 68.3 us -> 55.3 us
    ppermute x11 -> x12, starting transfers between devices: 13.5 us -> 36.8 us  [send(): return lax.ppermute(value, ('groups', 'replica', 'tensor'), pairs)]
    ppermute x11 -> x12, waiting for transfers between devices: 60.7 us -> 46.3 us  [send(): return lax.ppermute(value, ('groups', 'replica', 'tensor'), pairs)]
    ppermute x10, starting transfers between devices: 13.7 us -> 16.3 us  [swap(): return lax.ppermute(value, axis, [(i, i ^ distance) for i in range(count)])]
    ppermute x10, waiting for transfers between devices: 7.56 us -> 9.06 us  [swap(): return lax.ppermute(value, axis, [(i, i ^ distance) for i in range(count)])]
  transfers between devices with their start and end apart: 21 -> 22, of which waited for: 9 -> 10; matrix products, arithmetic and copies ran while one was open for 17% -> 14% of each run, Pallas kernels for 9% -> 8%
where the time goes in v7:
time: 150 us; the launch traced here: 149 us
  waiting for transfers between devices  55.3 us (37%)
  starting transfers between devices  53 us (35%)
  matrix products  20.2 us (13%)
  Pallas kernels  19.4 us (13%)
    ppermute x12, waiting for transfers between devices, send(): return lax.ppermute(value, ('groups', 'replica', 'tensor'), pairs)  46.3 us
    ppermute x12, starting transfers between devices, send(): return lax.ppermute(value, ('groups', 'replica', 'tensor'), pairs)  36.8 us
    dot_general x2, matrix products, part(): return jnp.dot(x, columns, preferred_element_type=jnp.float32)  20.2 us
    ppermute x10, starting transfers between devices, swap(): return lax.ppermute(value, axis, [(i, i ^ distance) for i in range(count)])  16.3 us
    pallas_call x2, Pallas kernels, lay_out(): pl.pallas_call(functools.partial(lay_kernel, plan, first_call), out_shape...  9.78 us
    ppermute x10, waiting for transfers between devices, swap(): return lax.ppermute(value, axis, [(i, i ^ distance) for i in range(count)])  9.06 us
    pallas_call x4, Pallas kernels, blocks_call(): pl.pallas_call(body, out_shape=out_shape, in_specs=[VMEM] * n_extra + [HB...  7.67 us
  transfers between devices with their start and end apart: 22, of which 10 were waited for; matrix products, arithmetic and copies ran while one was open for 14% of the time, Pallas kernels for 8%

profile of v7, /device:TPU:0, one launch (start us, length us, event | category | flops | bytes accessed | tf_op | source)
XLA Modules:
  0.0 149.5 jit_solution(17386513411806385444)
XLA Ops:
  0.0 4.3 %lay_out_first.1 = (bf16[128,4224]{1,0:T(8,128)(2,1)}, bf16[128,4224]{1,0:T(8,128)(2,1)}, s32[16]{0:T(128)}) custom-call(s32[16]{0:T(128)} %ids_ref.2, s32[48]{0:T(128)} %residency_ref.3, bf16[512,4096]{1,0:T(8,128)(2,1)} %x_ref.3, bf16[6,64,4096]{2,1,0:T(8,128)(2,1)} %bitcast.10, bf16[6,64,1024]{2,1,0:T(8,128)(2,1)} %up_ref.3), custom_call_target="tpu_custom_call" | custom-call | bytes 2097152 | tf_op jit(solution)/shard_map/lay_out_first/pallas_call | solution.py:227
  4.3 3.5 %collective-permute-start = (bf16[128,4224]{1,0:T(8,128)(2,1)}, bf16[128,4224]{1,0:T(8,128)(2,1)S(1)}, u32[]{:S(2)}, u32[]{:S(2)}) collective-permute-start(bf16[128,4224]{1,0:T(8,128)(2,1)} %get-tuple-element.58), channel_id=1, source_target_pairs={{0,4},{1,5},{2,6},{3,7},{12,8},{13,9},{14,10},{15,11},{16,20},{17,... | collective-permute-start | bytes 3244040 | tf_op jit(solution)/shard_map/ppermute | solution.py:643
  7.9 10.5 %fusion.4 = f32[512,1024]{1,0:T(8,128)} fusion(bf16[512,4096]{1,0:T(8,128)(2,1)} %x_ref.3, bf16[4096,2048]{1,0:T(8,128)(2,1)} %param.7, s32[]{:T(128)S(6)} %select_n.24), kind=kOutput, calls=%fused_computation.5 | convolution fusion | flops 4294967296 | bytes 14680068 | tf_op jit(solution)/shard_map/dot_general | solution.py:669
  18.4 3.1 %collective-permute-start.1 = (bf16[128,4224]{1,0:T(8,128)(2,1)}, bf16[128,4224]{1,0:T(8,128)(2,1)S(1)}, u32[]{:S(2)}, u32[]{:S(2)}) collective-permute-start(bf16[128,4224]{1,0:T(8,128)(2,1)} %get-tuple-element.59), channel_id=1, source_target_pairs={{0,6},{1,7},{2,4},{3,5},{12,10},{13,11},{14,8},{15,9},{16,22},{17,... | collective-permute-start | bytes 3244040 | tf_op jit(solution)/shard_map/ppermute | solution.py:643
  21.4 5.5 %lay_out_second.1 = (bf16[128,4224]{1,0:T(8,128)(2,1)}, bf16[128,4224]{1,0:T(8,128)(2,1)}, bf16[64,4224]{1,0:T(8,128)(2,1)}, bf16[128,4224]{1,0:T(8,128)(2,1)}, bf16[64,4224]{1,0:T(8,128)(2,1)}, /*index=5*/s32[16]{0:T(128)}) custom-call(s32[16]{0:T(128)} %ids_ref.2, s32[48]{0:T(128)} %residency_ref.3, bf16[512,4096]{1,0:T(8,128)(2,1)} %x_ref.3, ...), custom_call_target="tpu_custom_call" | custom-call | bytes 2097152 | tf_op jit(solution)/shard_map/lay_out_second/pallas_call | solution.py:227
  27.5 6.3 %collective-permute-done.refs_2_.refs_5_ = bf16[128,4224]{1,0:T(8,128)(2,1)S(1)} collective-permute-done((bf16[128,4224]{1,0:T(8,128)(2,1)}, bf16[128,4224]{1,0:T(8,128)(2,1)S(1)}, u32[]{:S(2)}, u32[]{:S(2)}) %collective-permute-start) | collective-permute-done | bytes 1081376 | tf_op jit(solution)/shard_map/ppermute | solution.py:643
  34.9 1.6 %collective-permute-start.3 = (bf16[64,4224]{1,0:T(8,128)(2,1)S(1)}, bf16[64,4224]{1,0:T(8,128)(2,1)S(1)}, u32[]{:S(2)}, u32[]{:S(2)}) collective-permute-start(bf16[64,4224]{1,0:T(8,128)(2,1)S(1)} %slice_select_fusion), channel_id=1, source_target_pairs={{0,16},{1,17},{2,18},{3,19},{12,28},{13,29},{14,30},{15,31},{16,0}... | collective-permute-start | bytes 1622024 | tf_op jit(solution)/shard_map/ppermute | solution.py:643
  36.5 9.7 %bitcast_add_fusion.base_ref = f32[512,1024]{1,0:T(8,128)S(1)} fusion(f32[512,1024]{1,0:T(8,128)} %collective-permute-done.4, bf16[512,4096]{1,0:T(8,128)(2,1)} %x_ref.3, bf16[4096,2048]{1,0:T(8,128)(2,1)} %param.7, s32[]{:T(128)S(6)} %select_n.27), kind=kOutput, calls=%fused_computation.4 | convolution fusion | flops 4295491584 | bytes 16777220 | tf_op jit(solution)/shard_map/dot_general | solution.py:669
  46.2 9.9 %collective-permute-done.1.refs_3_.refs_6_ = bf16[128,4224]{1,0:T(8,128)(2,1)S(1)} collective-permute-done((bf16[128,4224]{1,0:T(8,128)(2,1)}, bf16[128,4224]{1,0:T(8,128)(2,1)S(1)}, u32[]{:S(2)}, u32[]{:S(2)}) %collective-permute-start.1) | collective-permute-done | bytes 1081376 | tf_op jit(solution)/shard_map/ppermute | solution.py:643
  56.1 20.2 %collective-permute-start.5 = (bf16[64,4224]{1,0:T(8,128)(2,1)S(1)}, bf16[64,4224]{1,0:T(8,128)(2,1)S(1)}, u32[]{:S(2)}, u32[]{:S(2)}) collective-permute-start(bf16[64,4224]{1,0:T(8,128)(2,1)S(1)} %copy-done.6), channel_id=1, source_target_pairs={{4,0},{5,1},{6,2},{7,3},{8,12},{9,13},{10,14},{11,15},{20,16},{21,... | collective-permute-start | bytes 1622024 | tf_op jit(solution)/shard_map/ppermute | solution.py:643
  76.6 1.6 %collective-permute-start.7 = (bf16[64,4224]{1,0:T(8,128)(2,1)S(1)}, bf16[64,4224]{1,0:T(8,128)(2,1)S(1)}, u32[]{:S(2)}, u32[]{:S(2)}) collective-permute-start(bf16[64,4224]{1,0:T(8,128)(2,1)S(1)} %get-tuple-element.111), channel_id=1, source_target_pairs={{0,16},{1,17},{2,18},{3,19},{12,28},{13,29},{14,30},{15,31},{16,0}... | collective-permute-start | bytes 1622024 | tf_op jit(solution)/shard_map/ppermute | solution.py:643
  78.7 1.5 collective-permute-start.9
  80.1 9.5 %collective-permute-done.5.refs_4_.refs_7_ = bf16[64,4224]{1,0:T(8,128)(2,1)S(1)} collective-permute-done((bf16[64,4224]{1,0:T(8,128)(2,1)S(1)}, bf16[64,4224]{1,0:T(8,128)(2,1)S(1)}, u32[]{:S(2)}, u32[]{:S(2)}) %collective-permute-start.5) | collective-permute-done | bytes 540704 | tf_op jit(solution)/shard_map/ppermute | solution.py:643
  89.6 2.8 %collective-permute-start.10 = (bf16[64,4224]{1,0:T(8,128)(2,1)S(1)}, bf16[64,4224]{1,0:T(8,128)(2,1)S(1)}, u32[]{:S(2)}, u32[]{:S(2)}) collective-permute-start(bf16[64,4224]{1,0:T(8,128)(2,1)S(1)} %copy-done.5), channel_id=1, source_target_pairs={{4,0},{5,1},{6,2},{7,3},{8,12},{9,13},{10,14},{11,15},{20,16},{21,... | collective-permute-start | bytes 1622024 | tf_op jit(solution)/shard_map/ppermute | solution.py:643
  93.2 10.3 %collective-permute-done.8.refs_9_ = bf16[64,4224]{1,0:T(8,128)(2,1)S(1)} collective-permute-done((bf16[64,4224]{1,0:T(8,128)(2,1)S(1)}, bf16[64,4224]{1,0:T(8,128)(2,1)S(1)}, u32[]{:S(2)}, u32[]{:S(2)}) %collective-permute-start.8) | collective-permute-done | bytes 540704 | tf_op jit(solution)/shard_map/ppermute | solution.py:643
  103.4 9.7 %collective-permute-done.9.refs_10_.refs_8_ = bf16[64,4224]{1,0:T(8,128)(2,1)S(1)} collective-permute-done((bf16[64,4224]{1,0:T(8,128)(2,1)S(1)}, bf16[64,4224]{1,0:T(8,128)(2,1)S(1)}, u32[]{:S(2)}, u32[]{:S(2)}) %collective-permute-start.9) | collective-permute-done | bytes 540704 | tf_op jit(solution)/shard_map/ppermute | solution.py:643
  113.8 2.6 %reduce_own.1 = (f32[128,128]{1,0:T(8,128)S(1)}, f32[256,128]{1,0:T(8,128)S(1)}) custom-call(bf16[128,4224]{1,0:T(8,128)(2,1)S(1)} %copy-done.2, bf16[128,4224]{1,0:T(8,128)(2,1)S(1)} %collective-permute-done.2.refs_1_, bf16[128,4224]{1,0:T(8,128)(2,1)S(1)} %collective-permute-done.refs_2_.refs_5_, ...), custom_call_target="tpu_custom_call" | custom-call | flops 1 | bytes 1 | tf_op jit(solution)/shard_map/reduce_own/pallas_call | solution.py:431
  119.2 3.8 %collective-permute-start.17 = (bf16[64,1024]{1,0:T(8,128)(2,1)S(1)}, bf16[64,1024]{1,0:T(8,128)(2,1)S(1)}, u32[]{:S(2)}, u32[]{:S(2)}) collective-permute-start(bf16[64,1024]{1,0:T(8,128)(2,1)S(1)} %get-tuple-element.93), channel_id=1, source_target_pairs={{0,4},{2,6},{4,0},{6,2},{8,12},{10,14},{12,8},{14,10},{1,5},{3,7},... | collective-permute-start | bytes 393224 | tf_op jit(solution)/shard_map/ppermute | solution.py:627
  124.0 3.6 %reduce_taken.1 = (f32[64,128]{1,0:T(8,128)S(1)}, f32[64,128]{1,0:T(8,128)S(1)}, f32[256,128]{1,0:T(8,128)S(1)}) custom-call(bf16[128,4224]{1,0:T(8,128)(2,1)S(1)} %copy-done.2, bf16[128,4224]{1,0:T(8,128)(2,1)S(1)} %collective-permute-done.2.refs_1_, bf16[128,4224]{1,0:T(8,128)(2,1)S(1)} %collective-permute-done.refs_2_.refs_5_, ...), custom_call_target="tpu_custom_call" | custom-call | flops 1 | bytes 1 | tf_op jit(solution)/shard_map/reduce_taken/pallas_call | solution.py:431
  128.9 1.4 collective-permute-done.18.refs_3_
  131.8 8.3 %collective-permute-start.20 = (bf16[64,1024]{1,0:T(8,128)(2,1)S(1)}, bf16[64,1024]{1,0:T(8,128)(2,1)S(1)}, u32[]{:S(2)}, u32[]{:S(2)}) collective-permute-start(bf16[64,1024]{1,0:T(8,128)(2,1)S(1)} %get-tuple-element.107), channel_id=1, source_target_pairs={{0,4},{2,6},{4,0},{6,2},{8,12},{10,14},{12,8},{14,10},{1,5},{3,7},... | collective-permute-start | bytes 393224 | tf_op jit(solution)/shard_map/ppermute | solution.py:627
  141.1 2.9 %collective-permute-done.20.refs_6_ = bf16[64,1024]{1,0:T(8,128)(2,1)S(1)} collective-permute-done((bf16[64,1024]{1,0:T(8,128)(2,1)S(1)}, bf16[64,1024]{1,0:T(8,128)(2,1)S(1)}, u32[]{:S(2)}, u32[]{:S(2)}) %collective-permute-start.20) | collective-permute-done | bytes 131104 | tf_op jit(solution)/shard_map/ppermute | solution.py:627
  144.0 3.4 %collective-permute-done.21.refs_7_ = bf16[64,1024]{1,0:T(8,128)(2,1)S(1)} collective-permute-done((bf16[64,1024]{1,0:T(8,128)(2,1)S(1)}, bf16[64,1024]{1,0:T(8,128)(2,1)S(1)}, u32[]{:S(2)}, u32[]{:S(2)}) %collective-permute-start.21) | collective-permute-done | bytes 131104 | tf_op jit(solution)/shard_map/ppermute | solution.py:627
  147.5 2.0 %join.1 = bf16[512,1024]{1,0:T(8,128)(2,1)} custom-call(s32[16]{0:T(128)S(1)} %copy-done.3, f32[512,1024]{1,0:T(8,128)S(1)} %bitcast_add_fusion.base_ref, bf16[64,1024]{1,0:T(8,128)(2,1)S(1)} %get-tuple-element.95.refs_0_, bf16[64,1024]{1,0:T(8,128)(2,1)S(1)} %collective-permute-done.12.refs_1_, bf16[64,1024]{1,0:T(8,128)(2,1)S(1)} %collective-permute-done.17.refs_2_, ...), custom_call_target="tpu_custom_call" | custom-call | flops 524288 | bytes 4194304 | tf_op jit(solution)/shard_map/join/pallas_call | solution.py:611
  (45 shorter events, 11.4 us)
Async XLA Ops:
  4.3 29.4 %collective-permute-start = (bf16[128,4224]{1,0:T(8,128)(2,1)}, bf16[128,4224]{1,0:T(8,128)(2,1)S(1)}, u32[]{:S(2)}, u32[]{:S(2)}) collective-permute-start(bf16[128,4224]{1,0:T(8,128)(2,1)} %get-tuple-element.58), channel_id=1, source_target_pairs={{0,4},{1,5},{2,6},{3,7},{12,8},{13,9},{14,10},{15,11},{16,20},{17,... | collective-permute-start | bytes 3244040 | tf_op jit(solution)/shard_map/ppermute | solution.py:643
  18.3 18.1 %collective-permute-start.4 = (f32[512,1024]{1,0:T(8,128)}, f32[512,1024]{1,0:T(8,128)}, u32[]{:S(2)}, u32[]{:S(2)}) collective-permute-start(f32[512,1024]{1,0:T(8,128)} %fusion.4), channel_id=1, source_target_pairs={{0,1},{1,0},{2,3},{3,2},{4,5},{5,4},{6,7},{7,6},{8,9},{9,8},{10,11... | collective-permute-start | bytes 6291464 | tf_op jit(solution)/shard_map/ppermute | solution.py:627
  18.4 37.8 %collective-permute-start.1 = (bf16[128,4224]{1,0:T(8,128)(2,1)}, bf16[128,4224]{1,0:T(8,128)(2,1)S(1)}, u32[]{:S(2)}, u32[]{:S(2)}) collective-permute-start(bf16[128,4224]{1,0:T(8,128)(2,1)} %get-tuple-element.59), channel_id=1, source_target_pairs={{0,6},{1,7},{2,4},{3,5},{12,10},{13,11},{14,8},{15,9},{16,22},{17,... | collective-permute-start | bytes 3244040 | tf_op jit(solution)/shard_map/ppermute | solution.py:643
  26.9 29.2 %collective-permute-start.2 = (bf16[128,4224]{1,0:T(8,128)(2,1)}, bf16[128,4224]{1,0:T(8,128)(2,1)S(1)}, u32[]{:S(2)}, u32[]{:S(2)}) collective-permute-start(bf16[128,4224]{1,0:T(8,128)(2,1)} %get-tuple-element.62), channel_id=1, source_target_pairs={{0,2},{2,0},{4,6},{6,4},{8,10},{10,8},{12,14},{14,12},{1,3},{3,1},... | collective-permute-start | bytes 3244040 | tf_op jit(solution)/shard_map/ppermute | solution.py:627
  34.9 21.2 %collective-permute-start.3 = (bf16[64,4224]{1,0:T(8,128)(2,1)S(1)}, bf16[64,4224]{1,0:T(8,128)(2,1)S(1)}, u32[]{:S(2)}, u32[]{:S(2)}) collective-permute-start(bf16[64,4224]{1,0:T(8,128)(2,1)S(1)} %slice_select_fusion), channel_id=1, source_target_pairs={{0,16},{1,17},{2,18},{3,19},{12,28},{13,29},{14,30},{15,31},{16,0}... | collective-permute-start | bytes 1622024 | tf_op jit(solution)/shard_map/ppermute | solution.py:643
  36.5 77.3 %copy-start.2 = (bf16[128,4224]{1,0:T(8,128)(2,1)S(1)}, bf16[128,4224]{1,0:T(8,128)(2,1)}, u32[]{:S(2)}) copy-start(bf16[128,4224]{1,0:T(8,128)(2,1)} %get-tuple-element.68.refs_0_) | copy-start | bytes 3244036
  46.2 67.5 %copy-start = (bf16[6,4096,64]{1,2,0:T(8,128)(2,1)S(1)}, bf16[6,4096,64]{1,2,0:T(8,128)(2,1)}, u32[]{:S(2)}) copy-start(bf16[6,4096,64]{1,2,0:T(8,128)(2,1)} %param.8) | copy-start | bytes 9437188
  56.1 33.5 %collective-permute-start.5 = (bf16[64,4224]{1,0:T(8,128)(2,1)S(1)}, bf16[64,4224]{1,0:T(8,128)(2,1)S(1)}, u32[]{:S(2)}, u32[]{:S(2)}) collective-permute-start(bf16[64,4224]{1,0:T(8,128)(2,1)S(1)} %copy-done.6), channel_id=1, source_target_pairs={{4,0},{5,1},{6,2},{7,3},{8,12},{9,13},{10,14},{11,15},{20,16},{21,... | collective-permute-start | bytes 1622024 | tf_op jit(solution)/shard_map/ppermute | solution.py:643
  76.4 37.4 %collective-permute-start.6 = (bf16[128,4224]{1,0:T(8,128)(2,1)S(1)}, bf16[128,4224]{1,0:T(8,128)(2,1)S(1)}, u32[]{:S(2)}, u32[]{:S(2)}) collective-permute-start(bf16[128,4224]{1,0:T(8,128)(2,1)S(1)} %copy-done.4), channel_id=1, source_target_pairs={{4,2},{5,3},{6,0},{7,1},{8,14},{9,15},{10,12},{11,13},{20,18},{21,... | collective-permute-start | bytes 3244040 | tf_op jit(solution)/shard_map/ppermute | solution.py:643
  76.6 15.9 %collective-permute-start.7 = (bf16[64,4224]{1,0:T(8,128)(2,1)S(1)}, bf16[64,4224]{1,0:T(8,128)(2,1)S(1)}, u32[]{:S(2)}, u32[]{:S(2)}) collective-permute-start(bf16[64,4224]{1,0:T(8,128)(2,1)S(1)} %get-tuple-element.111), channel_id=1, source_target_pairs={{0,16},{1,17},{2,18},{3,19},{12,28},{13,29},{14,30},{15,31},{16,0}... | collective-permute-start | bytes 1622024 | tf_op jit(solution)/shard_map/ppermute | solution.py:643
  78.1 25.3 %collective-permute-start.8 = (bf16[64,4224]{1,0:T(8,128)(2,1)S(1)}, bf16[64,4224]{1,0:T(8,128)(2,1)S(1)}, u32[]{:S(2)}, u32[]{:S(2)}) collective-permute-start(bf16[64,4224]{1,0:T(8,128)(2,1)S(1)} %get-tuple-element.110), channel_id=1, source_target_pairs={{0,16},{1,17},{2,18},{3,19},{12,28},{13,29},{14,30},{15,31},{16,0}... | collective-permute-start | bytes 1622024 | tf_op jit(solution)/shard_map/ppermute | solution.py:643
  78.7 34.5 %collective-permute-start.9 = (bf16[64,4224]{1,0:T(8,128)(2,1)S(1)}, bf16[64,4224]{1,0:T(8,128)(2,1)S(1)}, u32[]{:S(2)}, u32[]{:S(2)}) collective-permute-start(bf16[64,4224]{1,0:T(8,128)(2,1)S(1)} %get-tuple-element.109), channel_id=1, source_target_pairs={{0,16},{1,17},{2,18},{3,19},{12,28},{13,29},{14,30},{15,31},{16,0}... | collective-permute-start | bytes 1622024 | tf_op jit(solution)/shard_map/ppermute | solution.py:643
  89.6 34.4 %collective-permute-start.10 = (bf16[64,4224]{1,0:T(8,128)(2,1)S(1)}, bf16[64,4224]{1,0:T(8,128)(2,1)S(1)}, u32[]{:S(2)}, u32[]{:S(2)}) collective-permute-start(bf16[64,4224]{1,0:T(8,128)(2,1)S(1)} %copy-done.5), channel_id=1, source_target_pairs={{4,0},{5,1},{6,2},{7,3},{8,12},{9,13},{10,14},{11,15},{20,16},{21,... | collective-permute-start | bytes 1622024 | tf_op jit(solution)/shard_map/ppermute | solution.py:643
  92.5 31.5 %collective-permute-start.13 = (bf16[64,4224]{1,0:T(8,128)(2,1)S(1)}, bf16[64,4224]{1,0:T(8,128)(2,1)S(1)}, u32[]{:S(2)}, u32[]{:S(2)}) collective-permute-start(bf16[64,4224]{1,0:T(8,128)(2,1)S(1)} %collective-permute-done.5.refs_4_.refs_7_), channel_id=1, source_target_pairs={{4,20},{5,21},{6,22},{7,23},{8,24},{9,25},{10,26},{11,27},{20,4},{... | collective-permute-start | bytes 1622024 | tf_op jit(solution)/shard_map/ppermute | solution.py:643
  116.3 1.3 collective-permute-start.11
  118.3 5.7 %collective-permute-start.12 = (bf16[64,1024]{1,0:T(8,128)(2,1)S(1)}, bf16[64,1024]{1,0:T(8,128)(2,1)S(1)}, u32[]{:S(2)}, u32[]{:S(2)}) collective-permute-start(bf16[64,1024]{1,0:T(8,128)(2,1)S(1)} %get-tuple-element.83), channel_id=1, source_target_pairs={{0,2},{2,0},{4,6},{6,4},{8,10},{10,8},{12,14},{14,12},{1,3},{3,1},... | collective-permute-start | bytes 393224 | tf_op jit(solution)/shard_map/ppermute | solution.py:627
  119.2 9.7 %collective-permute-start.17 = (bf16[64,1024]{1,0:T(8,128)(2,1)S(1)}, bf16[64,1024]{1,0:T(8,128)(2,1)S(1)}, u32[]{:S(2)}, u32[]{:S(2)}) collective-permute-start(bf16[64,1024]{1,0:T(8,128)(2,1)S(1)} %get-tuple-element.93), channel_id=1, source_target_pairs={{0,4},{2,6},{4,0},{6,2},{8,12},{10,14},{12,8},{14,10},{1,5},{3,7},... | collective-permute-start | bytes 393224 | tf_op jit(solution)/shard_map/ppermute | solution.py:627
  123.0 7.3 %collective-permute-start.18 = (bf16[64,1024]{1,0:T(8,128)(2,1)S(1)}, bf16[64,1024]{1,0:T(8,128)(2,1)S(1)}, u32[]{:S(2)}, u32[]{:S(2)}) collective-permute-start(bf16[64,1024]{1,0:T(8,128)(2,1)S(1)} %get-tuple-element.94), channel_id=1, source_target_pairs={{0,6},{2,4},{4,2},{6,0},{8,14},{10,12},{12,10},{14,8},{1,7},{3,5},... | collective-permute-start | bytes 393224 | tf_op jit(solution)/shard_map/ppermute | solution.py:627
  127.6 2.7 %collective-permute-start.14 = (f32[64,128]{1,0:T(8,128)S(1)}, f32[64,128]{1,0:T(8,128)S(1)}, u32[]{:S(2)}, u32[]{:S(2)}) collective-permute-start(f32[64,128]{1,0:T(8,128)S(1)} %get-tuple-element.99.refs_0_), channel_id=1, source_target_pairs={{0,1},{1,0},{2,3},{3,2},{4,5},{5,4},{6,7},{7,6},{8,9},{9,8},{10,11... | collective-permute-start | bytes 98312 | tf_op jit(solution)/shard_map/ppermute | solution.py:627
  127.7 2.6 %collective-permute-start.15 = (f32[64,128]{1,0:T(8,128)S(1)}, f32[64,128]{1,0:T(8,128)S(1)}, u32[]{:S(2)}, u32[]{:S(2)}) collective-permute-start(f32[64,128]{1,0:T(8,128)S(1)} %get-tuple-element.90), channel_id=1, source_target_pairs={{0,0},{1,1},{2,2},{3,3},{12,12},{13,13},{14,14},{15,15},{16,16},{1... | collective-permute-start | bytes 98312 | tf_op jit(solution)/shard_map/ppermute | solution.py:643
  128.4 2.0 %collective-permute-start.16 = (f32[64,128]{1,0:T(8,128)S(1)}, f32[64,128]{1,0:T(8,128)S(1)}, u32[]{:S(2)}, u32[]{:S(2)}) collective-permute-start(f32[64,128]{1,0:T(8,128)S(1)} %get-tuple-element.90), channel_id=1, source_target_pairs={{0,1},{1,0},{2,3},{3,2},{12,13},{13,12},{14,15},{15,14},{16,17},{1... | collective-permute-start | bytes 98312 | tf_op jit(solution)/shard_map/ppermute | solution.py:643
  131.3 9.8 %collective-permute-start.19 = (bf16[64,1024]{1,0:T(8,128)(2,1)S(1)}, bf16[64,1024]{1,0:T(8,128)(2,1)S(1)}, u32[]{:S(2)}, u32[]{:S(2)}) collective-permute-start(bf16[64,1024]{1,0:T(8,128)(2,1)S(1)} %get-tuple-element.106), channel_id=1, source_target_pairs={{0,2},{2,0},{4,6},{6,4},{8,10},{10,8},{12,14},{14,12},{1,3},{3,1},... | collective-permute-start | bytes 393224 | tf_op jit(solution)/shard_map/ppermute | solution.py:627
  131.8 12.2 %collective-permute-start.20 = (bf16[64,1024]{1,0:T(8,128)(2,1)S(1)}, bf16[64,1024]{1,0:T(8,128)(2,1)S(1)}, u32[]{:S(2)}, u32[]{:S(2)}) collective-permute-start(bf16[64,1024]{1,0:T(8,128)(2,1)S(1)} %get-tuple-element.107), channel_id=1, source_target_pairs={{0,4},{2,6},{4,0},{6,2},{8,12},{10,14},{12,8},{14,10},{1,5},{3,7},... | collective-permute-start | bytes 393224 | tf_op jit(solution)/shard_map/ppermute | solution.py:627
  140.1 7.3 %collective-permute-start.21 = (bf16[64,1024]{1,0:T(8,128)(2,1)S(1)}, bf16[64,1024]{1,0:T(8,128)(2,1)S(1)}, u32[]{:S(2)}, u32[]{:S(2)}) collective-permute-start(bf16[64,1024]{1,0:T(8,128)(2,1)S(1)} %get-tuple-element.108), channel_id=1, source_target_pairs={{0,6},{2,4},{4,2},{6,0},{8,14},{10,12},{12,10},{14,8},{1,7},{3,5},... | collective-permute-start | bytes 393224 | tf_op jit(solution)/shard_map/ppermute | solution.py:627
  (5 other events, 129.9 us)

commit v8 on v7

--- a/solution.py
+++ b/solution.py
@@ -25,6 +25,7 @@
         self.turn = self.half // 2
         self.near = [d for d in range(self.half) if not d & self.turn]
         self.cross = [d for d in range(self.half) if d & self.turn]
+        self.across = self.near[1:] + self.near[:1] + self.cross
         self.share = rank // groups
         self.left_rows = slots * self.share
         self.padded = -(-self.left_rows // LANES) * LANES
@@ -85,7 +86,7 @@
 
 
 def lay_kernel(plan, first_call, ids_ref, residency_ref, x_ref, left_ref, up_ref, *rest):
-    n_near = 0 if first_call else len(plan.near)
+    n_near = len(plan.near) - 1 if first_call else 1
     n_blocks = plan.wide if first_call else len(plan.late_blocks())
     near, rest = rest[:n_near], rest[n_near:]
     blocks, rest = rest[:n_blocks], rest[n_blocks:]
@@ -182,7 +183,7 @@
         moves[-1] = (source, stage, outs)
         return moves
 
-    near_d = [] if first_call else plan.near
+    near_d = plan.near[1:] if first_call else plan.near[:1]
     near_targets = [
         (d, kind, near[i].at[pl.ds(kind * PAIR, PAIR)])
         for i, d in enumerate(near_d)
@@ -222,7 +223,7 @@
         jax.ShapeDtypeStruct((n * PAIR, plan.width + LANES), x.dtype)
         for _, n, _ in plan.late_blocks()
     ]
-    near = [] if first_call else [wide] * len(plan.near)
+    near = [wide] * (len(plan.near) - 1 if first_call else 1)
     blocks = [wide] * plan.wide if first_call else late
     out = pl.pallas_call(
         functools.partial(lay_kernel, plan, first_call),
@@ -381,7 +382,7 @@
         target = rows.at[0, :, columns] if k < n_steps else tag.at[0]
         copy_rows(copies, plan, 1, target, columns, near, wide, narrow)
         for e in range(1, plan.groups):
-            for i, d in enumerate(plan.near + plan.cross):
+            for i, d in enumerate(plan.across):
                 target = rows.at[e, :, columns] if k < n_steps else tag.at[e]
                 copies.one(
                     inner,
@@ -653,8 +654,9 @@
     core = lax.axis_index("tensor")
     outer = am_outer(plan)
     left_rows = jnp.swapaxes(lefts, 1, 2)
-    _, wide, seg_of = lay_out(plan, True, ids, residency, x, left_rows, ups)
-
+    near, wide, seg_of = lay_out(plan, True, ids, residency, x, left_rows, ups)
+
+    near = [swap(block, "replica", d) for block, d in zip(near, plan.near[1:])]
     wide_in = []
     for i in range(plan.wide):
         moves = []
@@ -670,14 +672,13 @@
 
     base_other = part(1 - core)
     late_ids, base_other, _ = lax.optimization_barrier((ids, base_other, seg_of))
-    near, late, _ = lay_out(plan, False, late_ids, residency, x, left_rows, ups)
-    near = near[:1] + [swap(near[i], "replica", d) for i, d in enumerate(plan.near) if d]
+    own_rows, late, _ = lay_out(plan, False, late_ids, residency, x, left_rows, ups)
+    near = own_rows + near
     base_mine = part(core)
     def across_send(i):
-        if i < len(plan.near):
-            value = near[i][PAIR:]
-        else:
-            value = wide_in[i - len(plan.near)][PAIR:]
+        d = plan.across[i]
+        block = near[plan.near.index(d)] if d in plan.near else wide_in[plan.cross.index(d)]
+        value = block[PAIR:]
         if i < plan.pieces:
             piece = wide_in[i // 2][(i % 2) * PAIR : (i % 2 + 1) * PAIR]
             value = jnp.where(outer, piece, value)

time: 150 us -> 144 us (0.960)
  starting transfers between devices: 53 us -> 30.1 us
  waiting for transfers between devices: 55.3 us -> 72.7 us
    ppermute x12, starting transfers between devices: 36.8 us -> 16.5 us  [send(): return lax.ppermute(value, ('groups', 'replica', 'tensor'), pairs)]
    ppermute x12, waiting for transfers between devices: 46.3 us -> 63.1 us  [send(): return lax.ppermute(value, ('groups', 'replica', 'tensor'), pairs)]
    ppermute x10, starting transfers between devices: 16.3 us -> 13.6 us  [swap(): return lax.ppermute(value, axis, [(i, i ^ distance) for i in range(count)])]
  transfers between devices with their start and end apart: 22 -> 22, of which waited for: 10 -> 11; matrix products, arithmetic and copies ran while one was open for 14% -> 14% of each run, Pallas kernels for 8% -> 8%
where the time goes in v8:
time: 144 us; the launch traced here: 143 us
  waiting for transfers between devices  72.7 us (50%)
  starting transfers between devices  30.1 us (21%)
  matrix products  20.1 us (14%)
  Pallas kernels  19.4 us (13%)
    ppermute x12, waiting for transfers between devices, send(): return lax.ppermute(value, ('groups', 'replica', 'tensor'), pairs)  63.1 us
    dot_general x2, matrix products, part(): return jnp.dot(x, columns, preferred_element_type=jnp.float32)  20.1 us
    ppermute x12, starting transfers between devices, send(): return lax.ppermute(value, ('groups', 'replica', 'tensor'), pairs)  16.5 us
    ppermute x10, starting transfers between devices, swap(): return lax.ppermute(value, axis, [(i, i ^ distance) for i in range(count)])  13.6 us
    pallas_call x2, Pallas kernels, lay_out(): pl.pallas_call(functools.partial(lay_kernel, plan, first_call), out_shape...  9.79 us
    ppermute x10, waiting for transfers between devices, swap(): return lax.ppermute(value, axis, [(i, i ^ distance) for i in range(count)])  9.51 us
    pallas_call x4, Pallas kernels, blocks_call(): pl.pallas_call(body, out_shape=out_shape, in_specs=[VMEM] * n_extra + [HB...  7.6 us
  transfers between devices with their start and end apart: 22, of which 11 were waited for; matrix products, arithmetic and copies ran while one was open for 14% of the time, Pallas kernels for 8%

profile of v8, /device:TPU:0, one launch (start us, length us, event | category | flops | bytes accessed | tf_op | source)
XLA Modules:
  0.0 142.7 jit_solution(5623471882769858617)
XLA Ops:
  0.0 4.7 %lay_out_first.1 = (bf16[128,4224]{1,0:T(8,128)(2,1)}, bf16[128,4224]{1,0:T(8,128)(2,1)}, bf16[128,4224]{1,0:T(8,128)(2,1)}, s32[16]{0:T(128)}) custom-call(s32[16]{0:T(128)} %ids_ref.2, s32[48]{0:T(128)} %residency_ref.3, bf16[512,4096]{1,0:T(8,128)(2,1)} %x_ref.3, bf16[6,64,4096]{2,1,0:T(8,128)(2,1)} %bitcast.10, bf16[6,64,1024]{2,1,0:T(8,128)(2,1)} %up_ref.3), custom_call_target="tpu_custom_call" | custom-call | bytes 2097152 | tf_op jit(solution)/shard_map/lay_out_first/pallas_call | solution.py:228
  4.7 3.5 %collective-permute-start = (bf16[128,4224]{1,0:T(8,128)(2,1)}, bf16[128,4224]{1,0:T(8,128)(2,1)S(1)}, u32[]{:S(2)}, u32[]{:S(2)}) collective-permute-start(bf16[128,4224]{1,0:T(8,128)(2,1)} %get-tuple-element.58), channel_id=1, source_target_pairs={{0,4},{1,5},{2,6},{3,7},{12,8},{13,9},{14,10},{15,11},{16,20},{17,... | collective-permute-start | bytes 3244040 | tf_op jit(solution)/shard_map/ppermute | solution.py:644
  8.2 1.5 %collective-permute-start.2 = (bf16[128,4224]{1,0:T(8,128)(2,1)}, bf16[128,4224]{1,0:T(8,128)(2,1)S(1)}, u32[]{:S(2)}, u32[]{:S(2)}) collective-permute-start(bf16[128,4224]{1,0:T(8,128)(2,1)} %get-tuple-element.62), channel_id=1, source_target_pairs={{0,2},{2,0},{4,6},{6,4},{8,10},{10,8},{12,14},{14,12},{1,3},{3,1},... | collective-permute-start | bytes 3244040 | tf_op jit(solution)/shard_map/ppermute | solution.py:628
  9.7 10.5 %fusion.4 = f32[512,1024]{1,0:T(8,128)} fusion(bf16[512,4096]{1,0:T(8,128)(2,1)} %x_ref.3, bf16[4096,2048]{1,0:T(8,128)(2,1)} %param.7, s32[]{:T(128)S(6)} %select_n.24), kind=kOutput, calls=%fused_computation.5 | convolution fusion | flops 4294967296 | bytes 14680068 | tf_op jit(solution)/shard_map/dot_general | solution.py:671
  20.2 2.1 %collective-permute-start.1 = (bf16[128,4224]{1,0:T(8,128)(2,1)}, bf16[128,4224]{1,0:T(8,128)(2,1)S(1)}, u32[]{:S(2)}, u32[]{:S(2)}) collective-permute-start(bf16[128,4224]{1,0:T(8,128)(2,1)} %get-tuple-element.59), channel_id=1, source_target_pairs={{0,6},{1,7},{2,4},{3,5},{12,10},{13,11},{14,8},{15,9},{16,22},{17,... | collective-permute-start | bytes 3244040 | tf_op jit(solution)/shard_map/ppermute | solution.py:644
  22.3 5.1 %lay_out_second.1 = (bf16[128,4224]{1,0:T(8,128)(2,1)}, bf16[64,4224]{1,0:T(8,128)(2,1)}, bf16[128,4224]{1,0:T(8,128)(2,1)}, bf16[64,4224]{1,0:T(8,128)(2,1)}, s32[16]{0:T(128)}) custom-call(s32[16]{0:T(128)} %ids_ref.2, s32[48]{0:T(128)} %residency_ref.3, bf16[512,4096]{1,0:T(8,128)(2,1)} %x_ref.3, bf16[6,64,4096]{2,1,0:T(8,128)(2,1)} %bitcast.11, ...), custom_call_target="tpu_custom_call" | custom-call | bytes 2097152 | tf_op jit(solution)/shard_map/lay_out_second/pallas_call | solution.py:228
  27.4 6.7 %collective-permute-done.refs_2_.refs_5_ = bf16[128,4224]{1,0:T(8,128)(2,1)S(1)} collective-permute-done((bf16[128,4224]{1,0:T(8,128)(2,1)}, bf16[128,4224]{1,0:T(8,128)(2,1)S(1)}, u32[]{:S(2)}, u32[]{:S(2)}) %collective-permute-start) | collective-permute-done | bytes 1081376 | tf_op jit(solution)/shard_map/ppermute | solution.py:644
  34.2 1.6 %collective-permute-start.3 = (bf16[64,4224]{1,0:T(8,128)(2,1)S(1)}, bf16[64,4224]{1,0:T(8,128)(2,1)S(1)}, u32[]{:S(2)}, u32[]{:S(2)}) collective-permute-start(bf16[64,4224]{1,0:T(8,128)(2,1)S(1)} %slice_select_fusion), channel_id=1, source_target_pairs={{0,16},{1,17},{2,18},{3,19},{12,28},{13,29},{14,30},{15,31},{16,0}... | collective-permute-start | bytes 1622024 | tf_op jit(solution)/shard_map/ppermute | solution.py:644
  35.8 9.7 %bitcast_add_fusion.base_ref = f32[512,1024]{1,0:T(8,128)S(1)} fusion(f32[512,1024]{1,0:T(8,128)} %collective-permute-done.4, bf16[512,4096]{1,0:T(8,128)(2,1)} %x_ref.3, bf16[4096,2048]{1,0:T(8,128)(2,1)} %param.7, s32[]{:T(128)S(6)} %select_n.27), kind=kOutput, calls=%fused_computation.4 | convolution fusion | flops 4295491584 | bytes 16777220 | tf_op jit(solution)/shard_map/dot_general | solution.py:671
  45.4 11.0 %collective-permute-done.1.refs_3_.refs_6_ = bf16[128,4224]{1,0:T(8,128)(2,1)S(1)} collective-permute-done((bf16[128,4224]{1,0:T(8,128)(2,1)}, bf16[128,4224]{1,0:T(8,128)(2,1)S(1)}, u32[]{:S(2)}, u32[]{:S(2)}) %collective-permute-start.1) | collective-permute-done | bytes 1081376 | tf_op jit(solution)/shard_map/ppermute | solution.py:644
  56.5 2.7 %collective-permute-start.5 = (bf16[64,4224]{1,0:T(8,128)(2,1)S(1)}, bf16[64,4224]{1,0:T(8,128)(2,1)S(1)}, u32[]{:S(2)}, u32[]{:S(2)}) collective-permute-start(bf16[64,4224]{1,0:T(8,128)(2,1)S(1)} %copy-done.6), channel_id=1, source_target_pairs={{4,0},{5,1},{6,2},{7,3},{8,12},{9,13},{10,14},{11,15},{20,16},{21,... | collective-permute-start | bytes 1622024 | tf_op jit(solution)/shard_map/ppermute | solution.py:644
  60.4 1.6 %collective-permute-start.7 = (bf16[64,4224]{1,0:T(8,128)(2,1)S(1)}, bf16[64,4224]{1,0:T(8,128)(2,1)S(1)}, u32[]{:S(2)}, u32[]{:S(2)}) collective-permute-start(bf16[64,4224]{1,0:T(8,128)(2,1)S(1)} %get-tuple-element.111), channel_id=1, source_target_pairs={{0,16},{1,17},{2,18},{3,19},{12,28},{13,29},{14,30},{15,31},{16,0}... | collective-permute-start | bytes 1622024 | tf_op jit(solution)/shard_map/ppermute | solution.py:644
  64.0 20.4 %collective-permute-done.5.refs_4_.refs_7_ = bf16[64,4224]{1,0:T(8,128)(2,1)S(1)} collective-permute-done((bf16[64,4224]{1,0:T(8,128)(2,1)S(1)}, bf16[64,4224]{1,0:T(8,128)(2,1)S(1)}, u32[]{:S(2)}, u32[]{:S(2)}) %collective-permute-start.5) | collective-permute-done | bytes 540704 | tf_op jit(solution)/shard_map/ppermute | solution.py:644
  85.1 2.1 %collective-permute-done.8.refs_9_ = bf16[64,4224]{1,0:T(8,128)(2,1)S(1)} collective-permute-done((bf16[64,4224]{1,0:T(8,128)(2,1)S(1)}, bf16[64,4224]{1,0:T(8,128)(2,1)S(1)}, u32[]{:S(2)}, u32[]{:S(2)}) %collective-permute-start.8) | collective-permute-done | bytes 540704 | tf_op jit(solution)/shard_map/ppermute | solution.py:644
  87.3 9.0 %collective-permute-done.9.refs_10_.refs_8_ = bf16[64,4224]{1,0:T(8,128)(2,1)S(1)} collective-permute-done((bf16[64,4224]{1,0:T(8,128)(2,1)S(1)}, bf16[64,4224]{1,0:T(8,128)(2,1)S(1)}, u32[]{:S(2)}, u32[]{:S(2)}) %collective-permute-start.9) | collective-permute-done | bytes 540704 | tf_op jit(solution)/shard_map/ppermute | solution.py:644
  96.3 13.1 %collective-permute-done.6.refs_5_ = bf16[128,4224]{1,0:T(8,128)(2,1)S(1)} collective-permute-done((bf16[128,4224]{1,0:T(8,128)(2,1)S(1)}, bf16[128,4224]{1,0:T(8,128)(2,1)S(1)}, u32[]{:S(2)}, u32[]{:S(2)}) %collective-permute-start.6) | collective-permute-done | bytes 1081376 | tf_op jit(solution)/shard_map/ppermute | solution.py:644
  109.4 2.6 %reduce_own.1 = (f32[128,128]{1,0:T(8,128)S(1)}, f32[256,128]{1,0:T(8,128)S(1)}) custom-call(bf16[128,4224]{1,0:T(8,128)(2,1)S(1)} %copy-done.2, bf16[128,4224]{1,0:T(8,128)(2,1)S(1)} %collective-permute-done.2.refs_1_, bf16[128,4224]{1,0:T(8,128)(2,1)S(1)} %collective-permute-done.refs_2_.refs_5_, ...), custom_call_target="tpu_custom_call" | custom-call | flops 1 | bytes 1 | tf_op jit(solution)/shard_map/reduce_own/pallas_call | solution.py:432
  114.0 3.5 %collective-permute-start.17 = (bf16[64,1024]{1,0:T(8,128)(2,1)S(1)}, bf16[64,1024]{1,0:T(8,128)(2,1)S(1)}, u32[]{:S(2)}, u32[]{:S(2)}) collective-permute-start(bf16[64,1024]{1,0:T(8,128)(2,1)S(1)} %get-tuple-element.93), channel_id=1, source_target_pairs={{0,4},{2,6},{4,0},{6,2},{8,12},{10,14},{12,8},{14,10},{1,5},{3,7},... | collective-permute-start | bytes 393224 | tf_op jit(solution)/shard_map/ppermute | solution.py:628
  117.4 2.1 %collective-permute-done.12.refs_1_ = bf16[64,1024]{1,0:T(8,128)(2,1)S(1)} collective-permute-done((bf16[64,1024]{1,0:T(8,128)(2,1)S(1)}, bf16[64,1024]{1,0:T(8,128)(2,1)S(1)}, u32[]{:S(2)}, u32[]{:S(2)}) %collective-permute-start.12) | collective-permute-done | bytes 131104 | tf_op jit(solution)/shard_map/ppermute | solution.py:628
  119.5 3.6 %reduce_taken.1 = (f32[64,128]{1,0:T(8,128)S(1)}, f32[64,128]{1,0:T(8,128)S(1)}, f32[256,128]{1,0:T(8,128)S(1)}) custom-call(bf16[128,4224]{1,0:T(8,128)(2,1)S(1)} %copy-done.2, bf16[128,4224]{1,0:T(8,128)(2,1)S(1)} %collective-permute-done.2.refs_1_, bf16[128,4224]{1,0:T(8,128)(2,1)S(1)} %collective-permute-done.refs_2_.refs_5_, ...), custom_call_target="tpu_custom_call" | custom-call | flops 1 | bytes 1 | tf_op jit(solution)/shard_map/reduce_taken/pallas_call | solution.py:432
  126.5 8.0 %collective-permute-start.20 = (bf16[64,1024]{1,0:T(8,128)(2,1)S(1)}, bf16[64,1024]{1,0:T(8,128)(2,1)S(1)}, u32[]{:S(2)}, u32[]{:S(2)}) collective-permute-start(bf16[64,1024]{1,0:T(8,128)(2,1)S(1)} %get-tuple-element.107), channel_id=1, source_target_pairs={{0,4},{2,6},{4,0},{6,2},{8,12},{10,14},{12,8},{14,10},{1,5},{3,7},... | collective-permute-start | bytes 393224 | tf_op jit(solution)/shard_map/ppermute | solution.py:628
  134.5 4.3 %collective-permute-done.20.refs_6_ = bf16[64,1024]{1,0:T(8,128)(2,1)S(1)} collective-permute-done((bf16[64,1024]{1,0:T(8,128)(2,1)S(1)}, bf16[64,1024]{1,0:T(8,128)(2,1)S(1)}, u32[]{:S(2)}, u32[]{:S(2)}) %collective-permute-start.20) | collective-permute-done | bytes 131104 | tf_op jit(solution)/shard_map/ppermute | solution.py:628
  138.8 1.9 %collective-permute-done.21.refs_7_ = bf16[64,1024]{1,0:T(8,128)(2,1)S(1)} collective-permute-done((bf16[64,1024]{1,0:T(8,128)(2,1)S(1)}, bf16[64,1024]{1,0:T(8,128)(2,1)S(1)}, u32[]{:S(2)}, u32[]{:S(2)}) %collective-permute-start.21) | collective-permute-done | bytes 131104 | tf_op jit(solution)/shard_map/ppermute | solution.py:628
  140.7 2.0 %join.1 = bf16[512,1024]{1,0:T(8,128)(2,1)} custom-call(s32[16]{0:T(128)S(1)} %copy-done.3, f32[512,1024]{1,0:T(8,128)S(1)} %bitcast_add_fusion.base_ref, bf16[64,1024]{1,0:T(8,128)(2,1)S(1)} %get-tuple-element.95.refs_0_, bf16[64,1024]{1,0:T(8,128)(2,1)S(1)} %collective-permute-done.12.refs_1_, bf16[64,1024]{1,0:T(8,128)(2,1)S(1)} %collective-permute-done.17.refs_2_, ...), custom_call_target="tpu_custom_call" | custom-call | flops 524288 | bytes 4194304 | tf_op jit(solution)/shard_map/join/pallas_call | solution.py:612
  (45 shorter events, 9.5 us)
Async XLA Ops:
  4.7 29.4 %collective-permute-start = (bf16[128,4224]{1,0:T(8,128)(2,1)}, bf16[128,4224]{1,0:T(8,128)(2,1)S(1)}, u32[]{:S(2)}, u32[]{:S(2)}) collective-permute-start(bf16[128,4224]{1,0:T(8,128)(2,1)} %get-tuple-element.58), channel_id=1, source_target_pairs={{0,4},{1,5},{2,6},{3,7},{12,8},{13,9},{14,10},{15,11},{16,20},{17,... | collective-permute-start | bytes 3244040 | tf_op jit(solution)/shard_map/ppermute | solution.py:644
  8.2 25.9 %collective-permute-start.2 = (bf16[128,4224]{1,0:T(8,128)(2,1)}, bf16[128,4224]{1,0:T(8,128)(2,1)S(1)}, u32[]{:S(2)}, u32[]{:S(2)}) collective-permute-start(bf16[128,4224]{1,0:T(8,128)(2,1)} %get-tuple-element.62), channel_id=1, source_target_pairs={{0,2},{2,0},{4,6},{6,4},{8,10},{10,8},{12,14},{14,12},{1,3},{3,1},... | collective-permute-start | bytes 3244040 | tf_op jit(solution)/shard_map/ppermute | solution.py:628
  20.2 15.6 %collective-permute-start.4 = (f32[512,1024]{1,0:T(8,128)}, f32[512,1024]{1,0:T(8,128)}, u32[]{:S(2)}, u32[]{:S(2)}) collective-permute-start(f32[512,1024]{1,0:T(8,128)} %fusion.4), channel_id=1, source_target_pairs={{0,1},{1,0},{2,3},{3,2},{4,5},{5,4},{6,7},{7,6},{8,9},{9,8},{10,11... | collective-permute-start | bytes 6291464 | tf_op jit(solution)/shard_map/ppermute | solution.py:628
  20.2 36.2 %collective-permute-start.1 = (bf16[128,4224]{1,0:T(8,128)(2,1)}, bf16[128,4224]{1,0:T(8,128)(2,1)S(1)}, u32[]{:S(2)}, u32[]{:S(2)}) collective-permute-start(bf16[128,4224]{1,0:T(8,128)(2,1)} %get-tuple-element.59), channel_id=1, source_target_pairs={{0,6},{1,7},{2,4},{3,5},{12,10},{13,11},{14,8},{15,9},{16,22},{17,... | collective-permute-start | bytes 3244040 | tf_op jit(solution)/shard_map/ppermute | solution.py:644
  34.2 22.2 %collective-permute-start.3 = (bf16[64,4224]{1,0:T(8,128)(2,1)S(1)}, bf16[64,4224]{1,0:T(8,128)(2,1)S(1)}, u32[]{:S(2)}, u32[]{:S(2)}) collective-permute-start(bf16[64,4224]{1,0:T(8,128)(2,1)S(1)} %slice_select_fusion), channel_id=1, source_target_pairs={{0,16},{1,17},{2,18},{3,19},{12,28},{13,29},{14,30},{15,31},{16,0}... | collective-permute-start | bytes 1622024 | tf_op jit(solution)/shard_map/ppermute | solution.py:644
  45.4 39.0 %copy-start.5 = (bf16[64,4224]{1,0:T(8,128)(2,1)S(1)}, bf16[64,4224]{1,0:T(8,128)(2,1)}, u32[]{:S(2)}) copy-start(bf16[64,4224]{1,0:T(8,128)(2,1)} %get-tuple-element.79) | copy-start | bytes 1622020
  45.4 63.9 %copy-start = (bf16[6,4096,64]{1,2,0:T(8,128)(2,1)S(1)}, bf16[6,4096,64]{1,2,0:T(8,128)(2,1)}, u32[]{:S(2)}) copy-start(bf16[6,4096,64]{1,2,0:T(8,128)(2,1)} %param.8) | copy-start | bytes 9437188
  56.5 28.0 %collective-permute-start.5 = (bf16[64,4224]{1,0:T(8,128)(2,1)S(1)}, bf16[64,4224]{1,0:T(8,128)(2,1)S(1)}, u32[]{:S(2)}, u32[]{:S(2)}) collective-permute-start(bf16[64,4224]{1,0:T(8,128)(2,1)S(1)} %copy-done.6), channel_id=1, source_target_pairs={{4,0},{5,1},{6,2},{7,3},{8,12},{9,13},{10,14},{11,15},{20,16},{21,... | collective-permute-start | bytes 1622024 | tf_op jit(solution)/shard_map/ppermute | solution.py:644
  59.2 50.2 %collective-permute-start.6 = (bf16[128,4224]{1,0:T(8,128)(2,1)S(1)}, bf16[128,4224]{1,0:T(8,128)(2,1)S(1)}, u32[]{:S(2)}, u32[]{:S(2)}) collective-permute-start(bf16[128,4224]{1,0:T(8,128)(2,1)S(1)} %copy-done.4), channel_id=1, source_target_pairs={{4,2},{5,3},{6,0},{7,1},{8,14},{9,15},{10,12},{11,13},{20,18},{21,... | collective-permute-start | bytes 3244040 | tf_op jit(solution)/shard_map/ppermute | solution.py:644
  60.4 24.0 %collective-permute-start.7 = (bf16[64,4224]{1,0:T(8,128)(2,1)S(1)}, bf16[64,4224]{1,0:T(8,128)(2,1)S(1)}, u32[]{:S(2)}, u32[]{:S(2)}) collective-permute-start(bf16[64,4224]{1,0:T(8,128)(2,1)S(1)} %get-tuple-element.111), channel_id=1, source_target_pairs={{0,16},{1,17},{2,18},{3,19},{12,28},{13,29},{14,30},{15,31},{16,0}... | collective-permute-start | bytes 1622024 | tf_op jit(solution)/shard_map/ppermute | solution.py:644
  62.0 25.3 %collective-permute-start.8 = (bf16[64,4224]{1,0:T(8,128)(2,1)S(1)}, bf16[64,4224]{1,0:T(8,128)(2,1)S(1)}, u32[]{:S(2)}, u32[]{:S(2)}) collective-permute-start(bf16[64,4224]{1,0:T(8,128)(2,1)S(1)} %get-tuple-element.110), channel_id=1, source_target_pairs={{0,16},{1,17},{2,18},{3,19},{12,28},{13,29},{14,30},{15,31},{16,0}... | collective-permute-start | bytes 1622024 | tf_op jit(solution)/shard_map/ppermute | solution.py:644
  62.5 33.7 %collective-permute-start.9 = (bf16[64,4224]{1,0:T(8,128)(2,1)S(1)}, bf16[64,4224]{1,0:T(8,128)(2,1)S(1)}, u32[]{:S(2)}, u32[]{:S(2)}) collective-permute-start(bf16[64,4224]{1,0:T(8,128)(2,1)S(1)} %get-tuple-element.109), channel_id=1, source_target_pairs={{0,16},{1,17},{2,18},{3,19},{12,28},{13,29},{14,30},{15,31},{16,0}... | collective-permute-start | bytes 1622024 | tf_op jit(solution)/shard_map/ppermute | solution.py:644
  84.4 33.0 %collective-permute-start.10 = (bf16[64,4224]{1,0:T(8,128)(2,1)S(1)}, bf16[64,4224]{1,0:T(8,128)(2,1)S(1)}, u32[]{:S(2)}, u32[]{:S(2)}) collective-permute-start(bf16[64,4224]{1,0:T(8,128)(2,1)S(1)} %copy-done.5), channel_id=1, source_target_pairs={{4,0},{5,1},{6,2},{7,3},{8,12},{9,13},{10,14},{11,15},{20,16},{21,... | collective-permute-start | bytes 1622024 | tf_op jit(solution)/shard_map/ppermute | solution.py:644
  84.4 33.0 %collective-permute-start.13 = (bf16[64,4224]{1,0:T(8,128)(2,1)S(1)}, bf16[64,4224]{1,0:T(8,128)(2,1)S(1)}, u32[]{:S(2)}, u32[]{:S(2)}) collective-permute-start(bf16[64,4224]{1,0:T(8,128)(2,1)S(1)} %collective-permute-done.5.refs_4_.refs_7_), channel_id=1, source_target_pairs={{4,20},{5,21},{6,22},{7,23},{8,24},{9,25},{10,26},{11,27},{20,4},{... | collective-permute-start | bytes 1622024 | tf_op jit(solution)/shard_map/ppermute | solution.py:644
  111.9 1.3 collective-permute-start.11
  113.9 5.6 %collective-permute-start.12 = (bf16[64,1024]{1,0:T(8,128)(2,1)S(1)}, bf16[64,1024]{1,0:T(8,128)(2,1)S(1)}, u32[]{:S(2)}, u32[]{:S(2)}) collective-permute-start(bf16[64,1024]{1,0:T(8,128)(2,1)S(1)} %get-tuple-element.83), channel_id=1, source_target_pairs={{0,2},{2,0},{4,6},{6,4},{8,10},{10,8},{12,14},{14,12},{1,3},{3,1},... | collective-permute-start | bytes 393224 | tf_op jit(solution)/shard_map/ppermute | solution.py:628
  114.0 10.4 %collective-permute-start.17 = (bf16[64,1024]{1,0:T(8,128)(2,1)S(1)}, bf16[64,1024]{1,0:T(8,128)(2,1)S(1)}, u32[]{:S(2)}, u32[]{:S(2)}) collective-permute-start(bf16[64,1024]{1,0:T(8,128)(2,1)S(1)} %get-tuple-element.93), channel_id=1, source_target_pairs={{0,4},{2,6},{4,0},{6,2},{8,12},{10,14},{12,8},{14,10},{1,5},{3,7},... | collective-permute-start | bytes 393224 | tf_op jit(solution)/shard_map/ppermute | solution.py:628
  117.4 7.0 %collective-permute-start.18 = (bf16[64,1024]{1,0:T(8,128)(2,1)S(1)}, bf16[64,1024]{1,0:T(8,128)(2,1)S(1)}, u32[]{:S(2)}, u32[]{:S(2)}) collective-permute-start(bf16[64,1024]{1,0:T(8,128)(2,1)S(1)} %get-tuple-element.94), channel_id=1, source_target_pairs={{0,6},{2,4},{4,2},{6,0},{8,14},{10,12},{12,10},{14,8},{1,7},{3,5},... | collective-permute-start | bytes 393224 | tf_op jit(solution)/shard_map/ppermute | solution.py:628
  123.1 1.3 collective-permute-start.14
  123.2 1.2 collective-permute-start.15
  123.8 1.4 collective-permute-start.16
  126.1 8.4 %collective-permute-start.19 = (bf16[64,1024]{1,0:T(8,128)(2,1)S(1)}, bf16[64,1024]{1,0:T(8,128)(2,1)S(1)}, u32[]{:S(2)}, u32[]{:S(2)}) collective-permute-start(bf16[64,1024]{1,0:T(8,128)(2,1)S(1)} %get-tuple-element.106), channel_id=1, source_target_pairs={{0,2},{2,0},{4,6},{6,4},{8,10},{10,8},{12,14},{14,12},{1,3},{3,1},... | collective-permute-start | bytes 393224 | tf_op jit(solution)/shard_map/ppermute | solution.py:628
  126.5 12.3 %collective-permute-start.20 = (bf16[64,1024]{1,0:T(8,128)(2,1)S(1)}, bf16[64,1024]{1,0:T(8,128)(2,1)S(1)}, u32[]{:S(2)}, u32[]{:S(2)}) collective-permute-start(bf16[64,1024]{1,0:T(8,128)(2,1)S(1)} %get-tuple-element.107), channel_id=1, source_target_pairs={{0,4},{2,6},{4,0},{6,2},{8,12},{10,14},{12,8},{14,10},{1,5},{3,7},... | collective-permute-start | bytes 393224 | tf_op jit(solution)/shard_map/ppermute | solution.py:628
  134.5 6.2 %collective-permute-start.21 = (bf16[64,1024]{1,0:T(8,128)(2,1)S(1)}, bf16[64,1024]{1,0:T(8,128)(2,1)S(1)}, u32[]{:S(2)}, u32[]{:S(2)}) collective-permute-start(bf16[64,1024]{1,0:T(8,128)(2,1)S(1)} %get-tuple-element.108), channel_id=1, source_target_pairs={{0,6},{2,4},{4,2},{6,0},{8,14},{10,12},{12,10},{14,8},{1,7},{3,5},... | collective-permute-start | bytes 393224 | tf_op jit(solution)/shard_map/ppermute | solution.py:628
  (5 other events, 94.8 us)

commit v9 on v8

--- a/solution.py
+++ b/solution.py
@@ -670,11 +670,11 @@
         columns = lax.dynamic_slice(weight, (0, which * features), (weight.shape[0], features))
         return jnp.dot(x, columns, preferred_element_type=jnp.float32)
 
-    base_other = part(1 - core)
-    late_ids, base_other, _ = lax.optimization_barrier((ids, base_other, seg_of))
+    late_ids, near = lax.optimization_barrier((ids, near))
     own_rows, late, _ = lay_out(plan, False, late_ids, residency, x, left_rows, ups)
     near = own_rows + near
-    base_mine = part(core)
+    base_other, base_mine = part(1 - core), part(core)
+
     def across_send(i):
         d = plan.across[i]
         block = near[plan.near.index(d)] if d in plan.near else wide_in[plan.cross.index(d)]
@@ -689,9 +689,8 @@
 
     across = [across_send(0)]
 
-    base = base_mine + swap(base_other, "tensor", 1)
-    wide_in, near, across, late, base = lax.optimization_barrier(
-        (wide_in, near, across, late, base)
+    wide_in, near, across, late, base_other, base_mine = lax.optimization_barrier(
+        (wide_in, near, across, late, base_other, base_mine)
     )
     across += [across_send(i) for i in range(1, half)]
     late_in = []
@@ -705,6 +704,7 @@
     across_up = [
         send(plan, late_in[0], [(plan.inner, e, 0, 0)]) for e in range(1, plan.groups)
     ]
+    base = base_mine + swap(base_other, "tensor", 1)
     late_in[:-1], across = lax.optimization_barrier((late_in[:-1], across))
     across = [[blocks[e] for blocks in across] for e in range(plan.groups - 1)]
 
@@ -714,8 +714,8 @@
     terms = expand_own(plan, low, other, tag, ups.reshape(slots * rank, features))
     deltas = [terms[0]] + [swap(terms[d], "replica", d) for d in range(1, half)]
 
-    late_in[-1], deltas[:2], across_up = lax.optimization_barrier(
-        (late_in[-1], deltas[:2], across_up)
+    late_in[-1], deltas[:2], across_up, base = lax.optimization_barrier(
+        (late_in[-1], deltas[:2], across_up, base)
     )
     lows, tag = reduce_taken(plan, near, wide_in, late_in, across)
     pairs = [lows[0], swap(lows[0], "tensor", 1)]

time: 144 us -> 135 us (0.938)
  waiting for transfers between devices: 72.7 us -> 64.3 us
  matrix products: 20.1 us -> 16.5 us
  other arithmetic: 0.23 us -> 2.48 us
    ppermute x12, waiting for transfers between devices: 63.1 us -> 45.7 us  [send(): return lax.ppermute(value, ('groups', 'replica', 'tensor'), pairs)]
    ppermute x10, waiting for transfers between devices: 9.51 us -> 18.6 us  [swap(): return lax.ppermute(value, axis, [(i, i ^ distance) for i in range(count)])]
    dot_general x2, matrix products: 20.1 us -> 16.5 us  [part(): return jnp.dot(x, columns, preferred_element_type=jnp.float32)]
    ppermute x10, starting transfers between devices: 13.6 us -> 15 us  [swap(): return lax.ppermute(value, axis, [(i, i ^ distance) for i in range(count)])]
  transfers between devices with their start and end apart: 22 -> 22, of which waited for: 11 -> 12; matrix products, arithmetic and copies ran while one was open for 14% -> 14% of each run, Pallas kernels for 8% -> 9%
where the time goes in v9:
time: 135 us
  waiting for transfers between devices  64.3 us (48%)
  starting transfers between devices  30.7 us (23%)
  Pallas kernels  19.2 us (14%)
  matrix products  16.5 us (12%)
  other arithmetic  2.48 us (2%)
    ppermute x12, waiting for transfers between devices, send(): return lax.ppermute(value, ('groups', 'replica', 'tensor'), pairs)  45.7 us
    ppermute x10, waiting for transfers between devices, swap(): return lax.ppermute(value, axis, [(i, i ^ distance) for i in range(count)])  18.6 us
    dot_general x2, matrix products, part(): return jnp.dot(x, columns, preferred_element_type=jnp.float32)  16.5 us
    ppermute x12, starting transfers between devices, send(): return lax.ppermute(value, ('groups', 'replica', 'tensor'), pairs)  15.6 us
    ppermute x10, starting transfers between devices, swap(): return lax.ppermute(value, axis, [(i, i ^ distance) for i in range(count)])  15 us
    pallas_call x2, Pallas kernels, lay_out(): pl.pallas_call(functools.partial(lay_kernel, plan, first_call), out_shape...  9.76 us
    pallas_call x4, Pallas kernels, blocks_call(): pl.pallas_call(body, out_shape=out_shape, in_specs=[VMEM] * n_extra + [HB...  7.48 us
  transfers between devices with their start and end apart: 22, of which 12 were waited for; matrix products, arithmetic and copies ran while one was open for 14% of the time, Pallas kernels for 9%

profile of v9, /device:TPU:0, one launch (start us, length us, event | category | flops | bytes accessed | tf_op | source)
XLA Modules:
  0.0 134.6 jit_solution(11604172636250499599)
XLA Ops:
  0.0 4.7 %lay_out_first.1 = (bf16[128,4224]{1,0:T(8,128)(2,1)}, bf16[128,4224]{1,0:T(8,128)(2,1)}, bf16[128,4224]{1,0:T(8,128)(2,1)}, s32[16]{0:T(128)}) custom-call(s32[16]{0:T(128)} %ids_ref.2, s32[48]{0:T(128)} %residency_ref.3, bf16[512,4096]{1,0:T(8,128)(2,1)} %x_ref.3, bf16[6,64,4096]{2,1,0:T(8,128)(2,1)} %bitcast.10, bf16[6,64,1024]{2,1,0:T(8,128)(2,1)} %up_ref.3), custom_call_target="tpu_custom_call" | custom-call | bytes 2097152 | tf_op jit(solution)/shard_map/lay_out_first/pallas_call | solution.py:228
  4.7 3.0 %collective-permute-start.2 = (bf16[128,4224]{1,0:T(8,128)(2,1)}, bf16[128,4224]{1,0:T(8,128)(2,1)S(1)}, u32[]{:S(2)}, u32[]{:S(2)}) collective-permute-start(bf16[128,4224]{1,0:T(8,128)(2,1)} %get-tuple-element.62), channel_id=1, source_target_pairs={{0,2},{2,0},{4,6},{6,4},{8,10},{10,8},{12,14},{14,12},{1,3},{3,1},... | collective-permute-start | bytes 3244040 | tf_op jit(solution)/shard_map/ppermute | solution.py:628
  7.7 2.0 %collective-permute-start = (bf16[128,4224]{1,0:T(8,128)(2,1)}, bf16[128,4224]{1,0:T(8,128)(2,1)S(1)}, u32[]{:S(2)}, u32[]{:S(2)}) collective-permute-start(bf16[128,4224]{1,0:T(8,128)(2,1)} %get-tuple-element.60), channel_id=1, source_target_pairs={{0,4},{1,5},{2,6},{3,7},{12,8},{13,9},{14,10},{15,11},{16,20},{17,... | collective-permute-start | bytes 3244040 | tf_op jit(solution)/shard_map/ppermute | solution.py:644
  9.8 2.1 %collective-permute-start.1 = (bf16[128,4224]{1,0:T(8,128)(2,1)}, bf16[128,4224]{1,0:T(8,128)(2,1)S(1)}, u32[]{:S(2)}, u32[]{:S(2)}) collective-permute-start(bf16[128,4224]{1,0:T(8,128)(2,1)} %get-tuple-element.61), channel_id=1, source_target_pairs={{0,6},{1,7},{2,4},{3,5},{12,10},{13,11},{14,8},{15,9},{16,22},{17,... | collective-permute-start | bytes 3244040 | tf_op jit(solution)/shard_map/ppermute | solution.py:644
  11.8 10.6 %fusion.4 = f32[512,1024]{1,0:T(8,128)} fusion(bf16[512,4096]{1,0:T(8,128)(2,1)} %x_ref.3, bf16[4096,2048]{1,0:T(8,128)(2,1)} %param.7, s32[]{:T(128)S(6)} %select_n.26), kind=kOutput, calls=%fused_computation.4 | convolution fusion | flops 4294967296 | bytes 14680068 | tf_op jit(solution)/shard_map/dot_general | solution.py:671
  22.5 9.3 %collective-permute-done.2.refs_1_ = bf16[128,4224]{1,0:T(8,128)(2,1)S(1)} collective-permute-done((bf16[128,4224]{1,0:T(8,128)(2,1)}, bf16[128,4224]{1,0:T(8,128)(2,1)S(1)}, u32[]{:S(2)}, u32[]{:S(2)}) %collective-permute-start.2) | collective-permute-done | bytes 1081376 | tf_op jit(solution)/shard_map/ppermute | solution.py:628
  31.8 3.9 %collective-permute-done.refs_2_.refs_5_ = bf16[128,4224]{1,0:T(8,128)(2,1)S(1)} collective-permute-done((bf16[128,4224]{1,0:T(8,128)(2,1)}, bf16[128,4224]{1,0:T(8,128)(2,1)S(1)}, u32[]{:S(2)}, u32[]{:S(2)}) %collective-permute-start) | collective-permute-done | bytes 1081376 | tf_op jit(solution)/shard_map/ppermute | solution.py:644
  38.1 5.9 %fusion.7 = f32[512,1024]{1,0:T(8,128)} fusion(bf16[512,4096]{1,0:T(8,128)(2,1)S(1)} %copy-done.5, bf16[4096,2048]{1,0:T(8,128)(2,1)S(1)} %copy-done.7, s32[]{:T(128)S(6)} %select_n.27), kind=kOutput, calls=%fused_computation.5 | convolution fusion | flops 4294967296 | bytes 14680068 | tf_op jit(solution)/shard_map/dot_general | solution.py:671
  44.0 5.1 %lay_out_second.1 = (bf16[128,4224]{1,0:T(8,128)(2,1)}, bf16[64,4224]{1,0:T(8,128)(2,1)}, bf16[128,4224]{1,0:T(8,128)(2,1)}, bf16[64,4224]{1,0:T(8,128)(2,1)}, s32[16]{0:T(128)}) custom-call(s32[16]{0:T(128)} %ids_ref.2, s32[48]{0:T(128)} %residency_ref.3, bf16[512,4096]{1,0:T(8,128)(2,1)} %x_ref.3, bf16[6,64,4096]{2,1,0:T(8,128)(2,1)} %bitcast.11, ...), custom_call_target="tpu_custom_call" | custom-call | bytes 2097152 | tf_op jit(solution)/shard_map/lay_out_second/pallas_call | solution.py:228
  49.1 8.6 %collective-permute-done.1.refs_3_.refs_6_ = bf16[128,4224]{1,0:T(8,128)(2,1)S(1)} collective-permute-done((bf16[128,4224]{1,0:T(8,128)(2,1)}, bf16[128,4224]{1,0:T(8,128)(2,1)S(1)}, u32[]{:S(2)}, u32[]{:S(2)}) %collective-permute-start.1) | collective-permute-done | bytes 1081376 | tf_op jit(solution)/shard_map/ppermute | solution.py:644
  57.7 1.7 %collective-permute-start.4 = (bf16[64,4224]{1,0:T(8,128)(2,1)}, bf16[64,4224]{1,0:T(8,128)(2,1)S(1)}, u32[]{:S(2)}, u32[]{:S(2)}) collective-permute-start(bf16[64,4224]{1,0:T(8,128)(2,1)} %get-tuple-element.69), channel_id=1, source_target_pairs={{4,0},{5,1},{6,2},{7,3},{8,12},{9,13},{10,14},{11,15},{20,16},{21,... | collective-permute-start | bytes 1622024 | tf_op jit(solution)/shard_map/ppermute | solution.py:644
  59.4 2.1 %collective-permute-start.6 = (bf16[128,4224]{1,0:T(8,128)(2,1)}, bf16[128,4224]{1,0:T(8,128)(2,1)S(1)}, u32[]{:S(2)}, u32[]{:S(2)}) collective-permute-start(bf16[128,4224]{1,0:T(8,128)(2,1)} %get-tuple-element.77), channel_id=1, source_target_pairs={{4,2},{5,3},{6,0},{7,1},{8,14},{9,15},{10,12},{11,13},{20,18},{21,... | collective-permute-start | bytes 3244040 | tf_op jit(solution)/shard_map/ppermute | solution.py:644
  64.8 8.3 %collective-permute-done.4.refs_4_.refs_7_ = bf16[64,4224]{1,0:T(8,128)(2,1)S(1)} collective-permute-done((bf16[64,4224]{1,0:T(8,128)(2,1)}, bf16[64,4224]{1,0:T(8,128)(2,1)S(1)}, u32[]{:S(2)}, u32[]{:S(2)}) %collective-permute-start.4) | collective-permute-done | bytes 540704 | tf_op jit(solution)/shard_map/ppermute | solution.py:644
  74.5 3.4 %collective-permute-done.7.refs_8_ = bf16[64,4224]{1,0:T(8,128)(2,1)S(1)} collective-permute-done((bf16[64,4224]{1,0:T(8,128)(2,1)S(1)}, bf16[64,4224]{1,0:T(8,128)(2,1)S(1)}, u32[]{:S(2)}, u32[]{:S(2)}) %collective-permute-start.7) | collective-permute-done | bytes 540704 | tf_op jit(solution)/shard_map/ppermute | solution.py:644
  78.6 10.9 %collective-permute-done.8.refs_9_ = bf16[64,4224]{1,0:T(8,128)(2,1)S(1)} collective-permute-done((bf16[64,4224]{1,0:T(8,128)(2,1)S(1)}, bf16[64,4224]{1,0:T(8,128)(2,1)S(1)}, u32[]{:S(2)}, u32[]{:S(2)}) %collective-permute-start.8) | collective-permute-done | bytes 540704 | tf_op jit(solution)/shard_map/ppermute | solution.py:644
  90.3 9.8 %collective-permute-done.9.refs_10_.refs_8_ = bf16[64,4224]{1,0:T(8,128)(2,1)S(1)} collective-permute-done((bf16[64,4224]{1,0:T(8,128)(2,1)S(1)}, bf16[64,4224]{1,0:T(8,128)(2,1)S(1)}, u32[]{:S(2)}, u32[]{:S(2)}) %collective-permute-start.9) | collective-permute-done | bytes 540704 | tf_op jit(solution)/shard_map/ppermute | solution.py:644
  101.3 2.4 %reduce_own.1 = (f32[128,128]{1,0:T(8,128)S(1)}, f32[256,128]{1,0:T(8,128)S(1)}) custom-call(bf16[128,4224]{1,0:T(8,128)(2,1)S(1)} %copy-done.2, bf16[128,4224]{1,0:T(8,128)(2,1)S(1)} %collective-permute-done.2.refs_1_, bf16[128,4224]{1,0:T(8,128)(2,1)S(1)} %collective-permute-done.refs_2_.refs_5_, ...), custom_call_target="tpu_custom_call" | custom-call | flops 1 | bytes 1 | tf_op jit(solution)/shard_map/reduce_own/pallas_call | solution.py:432
  106.2 1.9 %collective-permute-start.17 = (bf16[64,1024]{1,0:T(8,128)(2,1)S(1)}, bf16[64,1024]{1,0:T(8,128)(2,1)S(1)}, u32[]{:S(2)}, u32[]{:S(2)}) collective-permute-start(bf16[64,1024]{1,0:T(8,128)(2,1)S(1)} %get-tuple-element.97), channel_id=1, source_target_pairs={{0,4},{2,6},{4,0},{6,2},{8,12},{10,14},{12,8},{14,10},{1,5},{3,7},... | collective-permute-start | bytes 393224 | tf_op jit(solution)/shard_map/ppermute | solution.py:628
  109.7 1.6 %collective-permute-done.11.refs_1_ = bf16[64,1024]{1,0:T(8,128)(2,1)S(1)} collective-permute-done((bf16[64,1024]{1,0:T(8,128)(2,1)S(1)}, bf16[64,1024]{1,0:T(8,128)(2,1)S(1)}, u32[]{:S(2)}, u32[]{:S(2)}) %collective-permute-start.11) | collective-permute-done | bytes 131104 | tf_op jit(solution)/shard_map/ppermute | solution.py:628
  111.3 3.6 %reduce_taken.1 = (f32[64,128]{1,0:T(8,128)S(1)}, f32[64,128]{1,0:T(8,128)S(1)}, f32[256,128]{1,0:T(8,128)S(1)}) custom-call(bf16[128,4224]{1,0:T(8,128)(2,1)S(1)} %copy-done.3, bf16[128,4224]{1,0:T(8,128)(2,1)S(1)} %collective-permute-done.2.refs_1_, bf16[128,4224]{1,0:T(8,128)(2,1)S(1)} %collective-permute-done.refs_2_.refs_5_, ...), custom_call_target="tpu_custom_call" | custom-call | flops 1 | bytes 1 | tf_op jit(solution)/shard_map/reduce_taken/pallas_call | solution.py:432
  118.5 6.8 %collective-permute-start.20 = (bf16[64,1024]{1,0:T(8,128)(2,1)S(1)}, bf16[64,1024]{1,0:T(8,128)(2,1)S(1)}, u32[]{:S(2)}, u32[]{:S(2)}) collective-permute-start(bf16[64,1024]{1,0:T(8,128)(2,1)S(1)} %get-tuple-element.111), channel_id=1, source_target_pairs={{0,4},{2,6},{4,0},{6,2},{8,12},{10,14},{12,8},{14,10},{1,5},{3,7},... | collective-permute-start | bytes 393224 | tf_op jit(solution)/shard_map/ppermute | solution.py:628
  126.2 2.9 %collective-permute-done.20.refs_6_ = bf16[64,1024]{1,0:T(8,128)(2,1)S(1)} collective-permute-done((bf16[64,1024]{1,0:T(8,128)(2,1)S(1)}, bf16[64,1024]{1,0:T(8,128)(2,1)S(1)}, u32[]{:S(2)}, u32[]{:S(2)}) %collective-permute-start.20) | collective-permute-done | bytes 131104 | tf_op jit(solution)/shard_map/ppermute | solution.py:628
  129.2 3.4 %collective-permute-done.21.refs_7_ = bf16[64,1024]{1,0:T(8,128)(2,1)S(1)} collective-permute-done((bf16[64,1024]{1,0:T(8,128)(2,1)S(1)}, bf16[64,1024]{1,0:T(8,128)(2,1)S(1)}, u32[]{:S(2)}, u32[]{:S(2)}) %collective-permute-start.21) | collective-permute-done | bytes 131104 | tf_op jit(solution)/shard_map/ppermute | solution.py:628
  132.6 2.0 %join.1 = bf16[512,1024]{1,0:T(8,128)(2,1)} custom-call(s32[16]{0:T(128)S(1)} %copy-done.4, f32[512,1024]{1,0:T(8,128)S(1)} %add.11.base_ref, bf16[64,1024]{1,0:T(8,128)(2,1)S(1)} %get-tuple-element.99.refs_0_, bf16[64,1024]{1,0:T(8,128)(2,1)S(1)} %collective-permute-done.11.refs_1_, bf16[64,1024]{1,0:T(8,128)(2,1)S(1)} %collective-permute-done.17.refs_2_, ...), custom_call_target="tpu_custom_call" | custom-call | flops 524288 | bytes 4194304 | tf_op jit(solution)/shard_map/join/pallas_call | solution.py:612
  (50 shorter events, 18.4 us)
Async XLA Ops:
  4.7 27.1 %collective-permute-start.2 = (bf16[128,4224]{1,0:T(8,128)(2,1)}, bf16[128,4224]{1,0:T(8,128)(2,1)S(1)}, u32[]{:S(2)}, u32[]{:S(2)}) collective-permute-start(bf16[128,4224]{1,0:T(8,128)(2,1)} %get-tuple-element.62), channel_id=1, source_target_pairs={{0,2},{2,0},{4,6},{6,4},{8,10},{10,8},{12,14},{14,12},{1,3},{3,1},... | collective-permute-start | bytes 3244040 | tf_op jit(solution)/shard_map/ppermute | solution.py:628
  7.7 28.0 %collective-permute-start = (bf16[128,4224]{1,0:T(8,128)(2,1)}, bf16[128,4224]{1,0:T(8,128)(2,1)S(1)}, u32[]{:S(2)}, u32[]{:S(2)}) collective-permute-start(bf16[128,4224]{1,0:T(8,128)(2,1)} %get-tuple-element.60), channel_id=1, source_target_pairs={{0,4},{1,5},{2,6},{3,7},{12,8},{13,9},{14,10},{15,11},{16,20},{17,... | collective-permute-start | bytes 3244040 | tf_op jit(solution)/shard_map/ppermute | solution.py:644
  9.8 48.0 %collective-permute-start.1 = (bf16[128,4224]{1,0:T(8,128)(2,1)}, bf16[128,4224]{1,0:T(8,128)(2,1)S(1)}, u32[]{:S(2)}, u32[]{:S(2)}) collective-permute-start(bf16[128,4224]{1,0:T(8,128)(2,1)} %get-tuple-element.61), channel_id=1, source_target_pairs={{0,6},{1,7},{2,4},{3,5},{12,10},{13,11},{14,8},{15,9},{16,22},{17,... | collective-permute-start | bytes 3244040 | tf_op jit(solution)/shard_map/ppermute | solution.py:644
  36.6 21.1 %collective-permute-start.3 = (bf16[64,4224]{1,0:T(8,128)(2,1)}, bf16[64,4224]{1,0:T(8,128)(2,1)S(1)}, u32[]{:S(2)}, u32[]{:S(2)}) collective-permute-start(bf16[64,4224]{1,0:T(8,128)(2,1)} %slice_select_fusion), channel_id=1, source_target_pairs={{0,16},{1,17},{2,18},{3,19},{12,28},{13,29},{14,30},{15,31},{16,0}... | collective-permute-start | bytes 1622024 | tf_op jit(solution)/shard_map/ppermute | solution.py:644
  49.1 40.4 %copy-start.8 = (bf16[64,4224]{1,0:T(8,128)(2,1)S(1)}, bf16[64,4224]{1,0:T(8,128)(2,1)}, u32[]{:S(2)}) copy-start(bf16[64,4224]{1,0:T(8,128)(2,1)} %get-tuple-element.71) | copy-start | bytes 1622020
  49.1 51.0 %copy-start = (bf16[6,4096,64]{1,2,0:T(8,128)(2,1)S(1)}, bf16[6,4096,64]{1,2,0:T(8,128)(2,1)}, u32[]{:S(2)}) copy-start(bf16[6,4096,64]{1,2,0:T(8,128)(2,1)} %param.8) | copy-start | bytes 9437188
  57.7 50.4 %collective-permute-start.13 = (f32[512,1024]{1,0:T(8,128)}, f32[512,1024]{1,0:T(8,128)S(1)}, u32[]{:S(2)}, u32[]{:S(2)}) collective-permute-start(f32[512,1024]{1,0:T(8,128)} %fusion.4), channel_id=1, source_target_pairs={{0,1},{1,0},{2,3},{3,2},{4,5},{5,4},{6,7},{7,6},{8,9},{9,8},{10,11... | collective-permute-start | bytes 6291464 | tf_op jit(solution)/shard_map/ppermute | solution.py:628
  57.7 15.3 %collective-permute-start.4 = (bf16[64,4224]{1,0:T(8,128)(2,1)}, bf16[64,4224]{1,0:T(8,128)(2,1)S(1)}, u32[]{:S(2)}, u32[]{:S(2)}) collective-permute-start(bf16[64,4224]{1,0:T(8,128)(2,1)} %get-tuple-element.69), channel_id=1, source_target_pairs={{4,0},{5,1},{6,2},{7,3},{8,12},{9,13},{10,14},{11,15},{20,16},{21,... | collective-permute-start | bytes 1622024 | tf_op jit(solution)/shard_map/ppermute | solution.py:644
  59.4 40.6 %collective-permute-start.6 = (bf16[128,4224]{1,0:T(8,128)(2,1)}, bf16[128,4224]{1,0:T(8,128)(2,1)S(1)}, u32[]{:S(2)}, u32[]{:S(2)}) collective-permute-start(bf16[128,4224]{1,0:T(8,128)(2,1)} %get-tuple-element.77), channel_id=1, source_target_pairs={{4,2},{5,3},{6,0},{7,1},{8,14},{9,15},{10,12},{11,13},{20,18},{21,... | collective-permute-start | bytes 3244040 | tf_op jit(solution)/shard_map/ppermute | solution.py:644
  62.7 15.2 %collective-permute-start.7 = (bf16[64,4224]{1,0:T(8,128)(2,1)S(1)}, bf16[64,4224]{1,0:T(8,128)(2,1)S(1)}, u32[]{:S(2)}, u32[]{:S(2)}) collective-permute-start(bf16[64,4224]{1,0:T(8,128)(2,1)S(1)} %get-tuple-element.115), channel_id=1, source_target_pairs={{0,16},{1,17},{2,18},{3,19},{12,28},{13,29},{14,30},{15,31},{16,0}... | collective-permute-start | bytes 1622024 | tf_op jit(solution)/shard_map/ppermute | solution.py:644
  64.2 25.2 %collective-permute-start.8 = (bf16[64,4224]{1,0:T(8,128)(2,1)S(1)}, bf16[64,4224]{1,0:T(8,128)(2,1)S(1)}, u32[]{:S(2)}, u32[]{:S(2)}) collective-permute-start(bf16[64,4224]{1,0:T(8,128)(2,1)S(1)} %get-tuple-element.114), channel_id=1, source_target_pairs={{0,16},{1,17},{2,18},{3,19},{12,28},{13,29},{14,30},{15,31},{16,0}... | collective-permute-start | bytes 1622024 | tf_op jit(solution)/shard_map/ppermute | solution.py:644
  73.0 27.0 %collective-permute-start.9 = (bf16[64,4224]{1,0:T(8,128)(2,1)S(1)}, bf16[64,4224]{1,0:T(8,128)(2,1)S(1)}, u32[]{:S(2)}, u32[]{:S(2)}) collective-permute-start(bf16[64,4224]{1,0:T(8,128)(2,1)S(1)} %get-tuple-element.113), channel_id=1, source_target_pairs={{0,16},{1,17},{2,18},{3,19},{12,28},{13,29},{14,30},{15,31},{16,0}... | collective-permute-start | bytes 1622024 | tf_op jit(solution)/shard_map/ppermute | solution.py:644
  77.9 31.7 %collective-permute-start.12 = (bf16[64,4224]{1,0:T(8,128)(2,1)S(1)}, bf16[64,4224]{1,0:T(8,128)(2,1)S(1)}, u32[]{:S(2)}, u32[]{:S(2)}) collective-permute-start(bf16[64,4224]{1,0:T(8,128)(2,1)S(1)} %collective-permute-done.4.refs_4_.refs_7_), channel_id=1, source_target_pairs={{4,20},{5,21},{6,22},{7,23},{8,24},{9,25},{10,26},{11,27},{20,4},{... | collective-permute-start | bytes 1622024 | tf_op jit(solution)/shard_map/ppermute | solution.py:644
  89.5 20.2 %collective-permute-start.5 = (bf16[64,4224]{1,0:T(8,128)(2,1)S(1)}, bf16[64,4224]{1,0:T(8,128)(2,1)S(1)}, u32[]{:S(2)}, u32[]{:S(2)}) collective-permute-start(bf16[64,4224]{1,0:T(8,128)(2,1)S(1)} %copy-done.8), channel_id=1, source_target_pairs={{4,0},{5,1},{6,2},{7,3},{8,12},{9,13},{10,14},{11,15},{20,16},{21,... | collective-permute-start | bytes 1622024 | tf_op jit(solution)/shard_map/ppermute | solution.py:644
  103.7 1.3 collective-permute-start.10
  105.7 5.6 %collective-permute-start.11 = (bf16[64,1024]{1,0:T(8,128)(2,1)S(1)}, bf16[64,1024]{1,0:T(8,128)(2,1)S(1)}, u32[]{:S(2)}, u32[]{:S(2)}) collective-permute-start(bf16[64,1024]{1,0:T(8,128)(2,1)S(1)} %get-tuple-element.84), channel_id=1, source_target_pairs={{0,2},{2,0},{4,6},{6,4},{8,10},{10,8},{12,14},{14,12},{1,3},{3,1},... | collective-permute-start | bytes 393224 | tf_op jit(solution)/shard_map/ppermute | solution.py:628
  106.2 9.9 %collective-permute-start.17 = (bf16[64,1024]{1,0:T(8,128)(2,1)S(1)}, bf16[64,1024]{1,0:T(8,128)(2,1)S(1)}, u32[]{:S(2)}, u32[]{:S(2)}) collective-permute-start(bf16[64,1024]{1,0:T(8,128)(2,1)S(1)} %get-tuple-element.97), channel_id=1, source_target_pairs={{0,4},{2,6},{4,0},{6,2},{8,12},{10,14},{12,8},{14,10},{1,5},{3,7},... | collective-permute-start | bytes 393224 | tf_op jit(solution)/shard_map/ppermute | solution.py:628
  108.2 8.0 %collective-permute-start.18 = (bf16[64,1024]{1,0:T(8,128)(2,1)S(1)}, bf16[64,1024]{1,0:T(8,128)(2,1)S(1)}, u32[]{:S(2)}, u32[]{:S(2)}) collective-permute-start(bf16[64,1024]{1,0:T(8,128)(2,1)S(1)} %get-tuple-element.98), channel_id=1, source_target_pairs={{0,6},{2,4},{4,2},{6,0},{8,14},{10,12},{12,10},{14,8},{1,7},{3,5},... | collective-permute-start | bytes 393224 | tf_op jit(solution)/shard_map/ppermute | solution.py:628
  114.9 1.3 collective-permute-start.14
  115.0 1.2 collective-permute-start.15
  115.6 1.4 %collective-permute-start.16 = (f32[64,128]{1,0:T(8,128)S(1)}, f32[64,128]{1,0:T(8,128)S(1)}, u32[]{:S(2)}, u32[]{:S(2)}) collective-permute-start(f32[64,128]{1,0:T(8,128)S(1)} %get-tuple-element.94), channel_id=1, source_target_pairs={{0,1},{1,0},{2,3},{3,2},{12,13},{13,12},{14,15},{15,14},{16,17},{1... | collective-permute-start | bytes 98312 | tf_op jit(solution)/shard_map/ppermute | solution.py:644
  117.9 8.3 %collective-permute-start.19 = (bf16[64,1024]{1,0:T(8,128)(2,1)S(1)}, bf16[64,1024]{1,0:T(8,128)(2,1)S(1)}, u32[]{:S(2)}, u32[]{:S(2)}) collective-permute-start(bf16[64,1024]{1,0:T(8,128)(2,1)S(1)} %get-tuple-element.110), channel_id=1, source_target_pairs={{0,2},{2,0},{4,6},{6,4},{8,10},{10,8},{12,14},{14,12},{1,3},{3,1},... | collective-permute-start | bytes 393224 | tf_op jit(solution)/shard_map/ppermute | solution.py:628
  118.5 10.7 %collective-permute-start.20 = (bf16[64,1024]{1,0:T(8,128)(2,1)S(1)}, bf16[64,1024]{1,0:T(8,128)(2,1)S(1)}, u32[]{:S(2)}, u32[]{:S(2)}) collective-permute-start(bf16[64,1024]{1,0:T(8,128)(2,1)S(1)} %get-tuple-element.111), channel_id=1, source_target_pairs={{0,4},{2,6},{4,0},{6,2},{8,12},{10,14},{12,8},{14,10},{1,5},{3,7},... | collective-permute-start | bytes 393224 | tf_op jit(solution)/shard_map/ppermute | solution.py:628
  125.3 7.3 %collective-permute-start.21 = (bf16[64,1024]{1,0:T(8,128)(2,1)S(1)}, bf16[64,1024]{1,0:T(8,128)(2,1)S(1)}, u32[]{:S(2)}, u32[]{:S(2)}) collective-permute-start(bf16[64,1024]{1,0:T(8,128)(2,1)S(1)} %get-tuple-element.112), channel_id=1, source_target_pairs={{0,6},{2,4},{4,2},{6,0},{8,14},{10,12},{12,10},{14,8},{1,7},{3,5},... | collective-permute-start | bytes 393224 | tf_op jit(solution)/shard_map/ppermute | solution.py:628
  (7 other events, 86.4 us)

commit v10 on v9

--- a/solution.py
+++ b/solution.py
@@ -36,6 +36,7 @@
         assert self.up_rows <= PAIR
         self.adapter_wide = -(-self.pieces // 2)
         self.units = 2 * len(self.cross)
+        self.last_piece = self.units - 2 if self.units - 2 < self.left_pieces else None
         assert self.pieces <= self.units and self.adapter_wide <= len(self.cross)
         self.wide = len(self.cross)
         self.outer = [r for r in range(replicas) if self.is_outer(r)]
@@ -329,11 +330,13 @@
     for i, d in enumerate(plan.near):
         copies.both(target.at[pl.ds(d * PAIR, PAIR)], near[i].at[span, columns])
     for i, d in enumerate(plan.cross):
-        copies.both(
-            target.at[pl.ds(d * PAIR, PAIR)],
-            plan.late_rows(narrow, i, kind).at[:, columns],
-            wide[i].at[span, columns],
-        )
+        place = target.at[pl.ds(d * PAIR, PAIR)]
+        if i == 0 and kind == 1:
+            copies.one(jnp.logical_not(copies.outer), place, wide[i].at[span, columns])
+        else:
+            copies.both(
+                place, plan.late_rows(narrow, i, kind).at[:, columns], wide[i].at[span, columns]
+            )
 
 
 def product_of(rows, left):
@@ -375,6 +378,21 @@
     inner = jnp.logical_not(outer)
     more = plan.groups - 1
     each = plan.half + plan.left_pieces + more * (plan.half + plan.left_pieces)
+    missing = pl.ds(plan.cross[0] * PAIR, PAIR)
+
+    @pl.when(outer)
+    def _():
+        rows[0, missing, :] = jnp.zeros((PAIR, plan.width), rows.dtype)
+        tag[0, missing, :] = jnp.zeros((PAIR, LANES), tag.dtype)
+
+    if plan.last_piece is not None:
+
+        @pl.when(inner)
+        def _():
+            left[0, pl.ds(plan.last_piece * PAIR, PAIR), :] = jnp.zeros(
+                (PAIR, plan.width), left.dtype
+            )
+
     steps = []
     for k in range(n_steps + 1):
         copies = Copies(outer, sems.at[pl.ds(k * each, each)])
@@ -392,11 +410,15 @@
         if k < n_steps:
             for piece, count in plan.left_spans():
                 span = pl.ds(0, count), columns
-                copies.both(
-                    left.at[0, pl.ds(piece * PAIR, count), columns],
-                    of_wide(wide, piece).at[span],
-                    late_adapters(narrow, piece, plan).at[span],
-                )
+                place = left.at[0, pl.ds(piece * PAIR, count), columns]
+                if piece == plan.last_piece:
+                    copies.one(outer, place, of_wide(wide, piece).at[span])
+                else:
+                    copies.both(
+                        place,
+                        of_wide(wide, piece).at[span],
+                        late_adapters(narrow, piece, plan).at[span],
+                    )
                 for e in range(1, plan.groups):
                     copies.one(
                         outer,
@@ -420,6 +442,89 @@
         lows[e][...] = pack(low, plan.share)
 
 
+def reduce_last_kernel(plan, *refs):
+    groups, width = plan.groups, plan.width
+    before, tag_ref, refs = refs[:groups], refs[groups], refs[groups + 1 :]
+    near, wide, last, across = refs[:4]
+    lows, tag_out = refs[4 : 4 + groups], refs[4 + groups]
+    outer = am_outer(plan)
+    inner = jnp.logical_not(outer)
+    first_row = plan.cross[0] * PAIR
+
+    def padded(parts, height):
+        rows = sum(part.shape[0] for part in parts)
+        if rows < height:
+            parts = parts + [jnp.zeros((height - rows, width), last.dtype)]
+        return jnp.concatenate(parts, axis=0)
+
+    @pl.when(outer)
+    def _():
+        tags = last[:, width:].astype(jnp.float32)
+        tag_out[...] = tag_ref[...]
+        tag_out[first_row : first_row + PAIR, :] = tags
+        rows = last[:, :width]
+        for e in range(groups):
+            total = jnp.zeros((PAIR, LANES), jnp.float32)
+            for first in range(0, plan.padded, LANES):
+                parts = []
+                for piece, count in plan.left_spans():
+                    if first <= piece * PAIR < first + LANES:
+                        source = of_wide(wide, piece) if e == 0 else across[e - 1][piece]
+                        parts.append(source[:count, :width])
+                product = product_of(rows, padded(parts, LANES))
+                mask = slot_mask(tags, first, plan.left_rows, plan.slots, plan.share)
+                total += jnp.where(mask, product, 0.0)
+            whole = [jnp.zeros((PAIR, LANES), jnp.float32)] * plan.half
+            whole[plan.cross[0]] = total
+            lows[e][...] = before[e][...] + pack(jnp.concatenate(whole, axis=0), plan.share)
+
+    @pl.when(inner)
+    def _():
+        tag_out[...] = tag_ref[...]
+        if plan.last_piece is None:
+            for e in range(groups):
+                lows[e][...] = before[e][...]
+            return
+        at = plan.last_piece * PAIR
+        first = at // LANES * LANES
+        count = min(PAIR, plan.left_rows - at)
+        parts = [jnp.zeros((at - first, width), last.dtype)] if at > first else []
+        left = padded(parts + [last[:count, :width]], LANES)
+        for e in range(groups):
+            if e == 0:
+                blocks = {d: near[i][PAIR:] for i, d in enumerate(plan.near)}
+                blocks.update({d: wide[i][PAIR:] for i, d in enumerate(plan.cross)})
+            else:
+                blocks = {d: across[e - 1][i][...] for i, d in enumerate(plan.across)}
+            whole = jnp.concatenate([blocks[d] for d in range(plan.half)], axis=0)
+            product = product_of(whole[:, :width], left)
+            tags = whole[:, width:].astype(jnp.float32)
+            mask = slot_mask(tags, first, plan.left_rows, plan.slots, plan.share)
+            low = pack(jnp.where(mask, product, 0.0), plan.share)
+            lows[e][...] = before[e][...] + low
+
+
+def reduce_last(plan, lows, tag, near, wide, last, across):
+    flat, tree = jax.tree.flatten([near, wide, last, across])
+    n_head = plan.groups + 1
+
+    def body(*refs):
+        nested = jax.tree.unflatten(tree, refs[n_head : n_head + len(flat)])
+        reduce_last_kernel(plan, *refs[:n_head], *nested, *refs[n_head + len(flat) :])
+
+    shapes = [jax.ShapeDtypeStruct(a.shape, a.dtype) for a in (*lows, tag)]
+    *lows, tag = pl.pallas_call(
+        body,
+        out_shape=shapes,
+        in_specs=[VMEM] * (n_head + len(flat)),
+        out_specs=[VMEM] * n_head,
+        compiler_params=params(),
+        cost_estimate=pl.CostEstimate(flops=1, bytes_accessed=1, transcendentals=0),
+        name="reduce_last",
+    )(*lows, tag, *flat)
+    return lows, tag
+
+
 def blocks_call(kernel, blocks, out_shape, out_specs, scratch, flops, moved, name, extra=()):
     flat, tree = jax.tree.flatten(blocks)
     n_extra = len(extra)
@@ -444,7 +549,7 @@
 def reduce_own(plan, near, wide, narrow, own):
     height = plan.half * PAIR
     columns = own.shape[0]
-    n_steps = 4
+    n_steps = 2
     dtype = own.dtype
     return blocks_call(
         functools.partial(reduce_own_kernel, plan, n_steps),
@@ -469,7 +574,7 @@
 
 def reduce_taken(plan, near, wide, narrow, across):
     height = plan.half * PAIR
-    n_steps = 4
+    n_steps = 2
     dtype = near[0].dtype
     groups, padded = plan.groups, plan.padded
     *lows, tag = blocks_call(
@@ -606,15 +711,11 @@
 
 def join(seg_of, base, deltas):
     height, features = base.shape
-    block = min(features, 512)
-    tall = pl.BlockSpec((height, block), lambda j: (0, j))
-    short = pl.BlockSpec((PAIR, block), lambda j: (0, j))
     return pl.pallas_call(
         join_kernel,
-        grid=(features // block,),
         out_shape=jax.ShapeDtypeStruct((height, features), jnp.bfloat16),
-        in_specs=[SMEM, tall] + [short] * len(deltas),
-        out_specs=tall,
+        in_specs=[SMEM, VMEM] + [VMEM] * len(deltas),
+        out_specs=VMEM,
         compiler_params=params(),
         cost_estimate=pl.CostEstimate(
             flops=height * features, bytes_accessed=8 * height * features, transcendentals=0
@@ -666,13 +767,13 @@
             moves.append((plan.inner, 0, half, 0))
         wide_in.append(send(plan, wide[i], moves))
 
+    late_ids, near, late_x = lax.optimization_barrier((ids, near, x))
+    own_rows, late, _ = lay_out(plan, False, late_ids, residency, x, left_rows, ups)
+    near = own_rows + near
     def part(which):
         columns = lax.dynamic_slice(weight, (0, which * features), (weight.shape[0], features))
-        return jnp.dot(x, columns, preferred_element_type=jnp.float32)
-
-    late_ids, near = lax.optimization_barrier((ids, near))
-    own_rows, late, _ = lay_out(plan, False, late_ids, residency, x, left_rows, ups)
-    near = own_rows + near
+        return jnp.dot(late_x, columns, preferred_element_type=jnp.float32)
+
     base_other, base_mine = part(1 - core), part(core)
 
     def across_send(i):
@@ -714,10 +815,11 @@
     terms = expand_own(plan, low, other, tag, ups.reshape(slots * rank, features))
     deltas = [terms[0]] + [swap(terms[d], "replica", d) for d in range(1, half)]
 
-    late_in[-1], deltas[:2], across_up, base = lax.optimization_barrier(
-        (late_in[-1], deltas[:2], across_up, base)
-    )
-    lows, tag = reduce_taken(plan, near, wide_in, late_in, across)
+    lows, tag = reduce_taken(plan, near, wide_in, late_in[:-1], across)
+    late_in[-1], deltas[:2], across_up, base, lows = lax.optimization_barrier(
+        (late_in[-1], deltas[:2], across_up, base, lows)
+    )
+    lows, tag = reduce_last(plan, lows, tag, near, wide_in, late_in[-1], across)
     pairs = [lows[0], swap(lows[0], "tensor", 1)]
     for e in range(1, plan.groups):
         pairs.append(send(plan, lows[e], [(plan.outer, 0, 0, 0), (plan.inner, e, 0, 0)]))

time: 135 us -> 134 us (level)
  starting transfers between devices: 30.7 us -> 27.9 us
  matrix products: 16.5 us -> 18.8 us
  waiting for transfers between devices: 64.3 us -> 66.2 us
    ppermute x10, waiting for transfers between devices: 18.6 us -> 27.6 us  [swap(): return lax.ppermute(value, axis, [(i, i ^ distance) for i in range(count)])]
    ppermute x12, waiting for transfers between devices: 45.7 us -> 38.6 us  [send(): return lax.ppermute(value, ('groups', 'replica', 'tensor'), pairs)]
    dot_general x2, matrix products: 16.5 us -> 18.8 us  [part(): return jnp.dot(late_x, columns, preferred_element_type=jnp.float32)]
    pallas_call x4, Pallas kernels: 7.48 us -> 5.98 us  [blocks_call(): pl.pallas_call(body, out_shape=out_shape, in_specs=[VMEM] * n_extra + [HB...]
    ppermute x12, starting transfers between devices: 15.6 us -> 14.2 us  [send(): return lax.ppermute(value, ('groups', 'replica', 'tensor'), pairs)]
    pallas_call x1 -> x2, Pallas kernels: 2 us -> 3.18 us  [the longest x1 1.81 us: join(): pl.pallas_call(join_kernel, out_shape=jax.ShapeDtypeStruct((height, featu...]
  transfers between devices with their start and end apart: 22 -> 22, of which waited for: 12 -> 10; matrix products, arithmetic and copies ran while one was open for 14% -> 15% of each run, Pallas kernels for 9% -> 9%
where the time goes in v10:
time: 134 us; the launch traced here: 133 us
  waiting for transfers between devices  66.2 us (49%)
  starting transfers between devices  27.9 us (21%)
  Pallas kernels  18.9 us (14%)
  matrix products  18.8 us (14%)
  other arithmetic  1.41 us (1%)
    ppermute x12, waiting for transfers between devices, send(): return lax.ppermute(value, ('groups', 'replica', 'tensor'), pairs)  38.6 us
    ppermute x10, waiting for transfers between devices, swap(): return lax.ppermute(value, axis, [(i, i ^ distance) for i in range(count)])  27.6 us
    dot_general x2, matrix products, part(): return jnp.dot(late_x, columns, preferred_element_type=jnp.float32)  18.8 us
    ppermute x12, starting transfers between devices, send(): return lax.ppermute(value, ('groups', 'replica', 'tensor'), pairs)  14.2 us
    ppermute x10, starting transfers between devices, swap(): return lax.ppermute(value, axis, [(i, i ^ distance) for i in range(count)])  13.8 us
    pallas_call x2, Pallas kernels, lay_out(): pl.pallas_call(functools.partial(lay_kernel, plan, first_call), out_shape...  9.7 us
    pallas_call x4, Pallas kernels, blocks_call(): pl.pallas_call(body, out_shape=out_shape, in_specs=[VMEM] * n_extra + [HB...  5.98 us
  transfers between devices with their start and end apart: 22, of which 10 were waited for; matrix products, arithmetic and copies ran while one was open for 15% of the time, Pallas kernels for 9%

profile of v10, /device:TPU:0, one launch (start us, length us, event | category | flops | bytes accessed | tf_op | source)
XLA Modules:
  0.0 133.5 jit_solution(17618686388861837645)
XLA Ops:
  0.0 4.6 %lay_out_first.1 = (bf16[128,4224]{1,0:T(8,128)(2,1)}, bf16[128,4224]{1,0:T(8,128)(2,1)}, bf16[128,4224]{1,0:T(8,128)(2,1)}, s32[16]{0:T(128)}) custom-call(s32[16]{0:T(128)} %ids_ref.2, s32[48]{0:T(128)} %residency_ref.3, bf16[512,4096]{1,0:T(8,128)(2,1)} %x_ref.3, bf16[6,64,4096]{2,1,0:T(8,128)(2,1)} %bitcast.6, bf16[6,64,1024]{2,1,0:T(8,128)(2,1)} %up_ref.3), custom_call_target="tpu_custom_call" | custom-call | bytes 2097152 | tf_op jit(solution)/shard_map/lay_out_first/pallas_call | solution.py:229
  4.6 3.0 %collective-permute-start.2 = (bf16[128,4224]{1,0:T(8,128)(2,1)}, bf16[128,4224]{1,0:T(8,128)(2,1)S(1)}, u32[]{:S(2)}, u32[]{:S(2)}) collective-permute-start(bf16[128,4224]{1,0:T(8,128)(2,1)} %get-tuple-element.68), channel_id=1, source_target_pairs={{0,2},{2,0},{4,6},{6,4},{8,10},{10,8},{12,14},{14,12},{1,3},{3,1},... | collective-permute-start | bytes 3244040 | tf_op jit(solution)/shard_map/ppermute | solution.py:729
  7.6 2.1 %collective-permute-start = (bf16[128,4224]{1,0:T(8,128)(2,1)}, bf16[128,4224]{1,0:T(8,128)(2,1)S(1)}, u32[]{:S(2)}, u32[]{:S(2)}) collective-permute-start(bf16[128,4224]{1,0:T(8,128)(2,1)} %get-tuple-element.66), channel_id=1, source_target_pairs={{0,4},{1,5},{2,6},{3,7},{12,8},{13,9},{14,10},{15,11},{16,20},{17,... | collective-permute-start | bytes 3244040 | tf_op jit(solution)/shard_map/ppermute | solution.py:745
  9.7 2.0 %collective-permute-start.1 = (bf16[128,4224]{1,0:T(8,128)(2,1)}, bf16[128,4224]{1,0:T(8,128)(2,1)S(1)}, u32[]{:S(2)}, u32[]{:S(2)}) collective-permute-start(bf16[128,4224]{1,0:T(8,128)(2,1)} %get-tuple-element.67), channel_id=1, source_target_pairs={{0,6},{1,7},{2,4},{3,5},{12,10},{13,11},{14,8},{15,9},{16,22},{17,... | collective-permute-start | bytes 3244040 | tf_op jit(solution)/shard_map/ppermute | solution.py:745
  11.7 20.0 %collective-permute-done.2.refs_1_.refs_4_ = bf16[128,4224]{1,0:T(8,128)(2,1)S(1)} collective-permute-done((bf16[128,4224]{1,0:T(8,128)(2,1)}, bf16[128,4224]{1,0:T(8,128)(2,1)S(1)}, u32[]{:S(2)}, u32[]{:S(2)}) %collective-permute-start.2) | collective-permute-done | bytes 1081376 | tf_op jit(solution)/shard_map/ppermute | solution.py:729
  31.7 4.0 %collective-permute-done.refs_2_.refs_5_ = bf16[128,4224]{1,0:T(8,128)(2,1)S(1)} collective-permute-done((bf16[128,4224]{1,0:T(8,128)(2,1)}, bf16[128,4224]{1,0:T(8,128)(2,1)S(1)}, u32[]{:S(2)}, u32[]{:S(2)}) %collective-permute-start) | collective-permute-done | bytes 1081376 | tf_op jit(solution)/shard_map/ppermute | solution.py:745
  36.5 1.5 %collective-permute-start.3 = (bf16[64,4224]{1,0:T(8,128)(2,1)}, bf16[64,4224]{1,0:T(8,128)(2,1)S(1)}, u32[]{:S(2)}, u32[]{:S(2)}) collective-permute-start(bf16[64,4224]{1,0:T(8,128)(2,1)} %slice_select_fusion), channel_id=1, source_target_pairs={{0,16},{1,17},{2,18},{3,19},{12,28},{13,29},{14,30},{15,31},{16,0}... | collective-permute-start | bytes 1622024 | tf_op jit(solution)/shard_map/ppermute | solution.py:745
  38.0 10.5 %fusion = f32[512,1024]{1,0:T(8,128)} fusion(bf16[512,4096]{1,0:T(8,128)(2,1)} %x_ref.3, bf16[4096,2048]{1,0:T(8,128)(2,1)} %param.7, s32[]{:T(128)S(6)} %select_n.27), kind=kOutput, calls=%fused_computation | convolution fusion | flops 4294967296 | bytes 14680068 | tf_op jit(solution)/shard_map/dot_general | solution.py:775
  48.5 5.1 %lay_out_second.1 = (bf16[128,4224]{1,0:T(8,128)(2,1)}, bf16[64,4224]{1,0:T(8,128)(2,1)}, bf16[128,4224]{1,0:T(8,128)(2,1)}, bf16[64,4224]{1,0:T(8,128)(2,1)}, s32[16]{0:T(128)}) custom-call(s32[16]{0:T(128)} %ids_ref.2, s32[48]{0:T(128)} %residency_ref.3, bf16[512,4096]{1,0:T(8,128)(2,1)} %x_ref.3, bf16[6,64,4096]{2,1,0:T(8,128)(2,1)} %bitcast.7, ...), custom_call_target="tpu_custom_call" | custom-call | bytes 2097152 | tf_op jit(solution)/shard_map/lay_out_second/pallas_call | solution.py:229
  53.7 8.3 %fusion.2 = f32[512,1024]{1,0:T(8,128)S(1)} fusion(bf16[512,4096]{1,0:T(8,128)(2,1)} %x_ref.3, bf16[4096,2048]{1,0:T(8,128)(2,1)} %param.7, s32[]{:T(128)S(6)} %select_n.26), kind=kOutput, calls=%fused_computation.2 | convolution fusion | flops 4294967296 | bytes 14680068 | tf_op jit(solution)/shard_map/dot_general | solution.py:775
  62.0 1.6 %collective-permute-start.4 = (bf16[64,4224]{1,0:T(8,128)(2,1)S(1)}, bf16[64,4224]{1,0:T(8,128)(2,1)S(1)}, u32[]{:S(2)}, u32[]{:S(2)}) collective-permute-start(bf16[64,4224]{1,0:T(8,128)(2,1)S(1)} %copy-done.7), channel_id=1, source_target_pairs={{4,0},{5,1},{6,2},{7,3},{8,12},{9,13},{10,14},{11,15},{20,16},{21,... | collective-permute-start | bytes 1622024 | tf_op jit(solution)/shard_map/ppermute | solution.py:745
  63.7 2.4 %collective-permute-start.6 = (bf16[128,4224]{1,0:T(8,128)(2,1)S(1)}, bf16[128,4224]{1,0:T(8,128)(2,1)S(1)}, u32[]{:S(2)}, u32[]{:S(2)}) collective-permute-start(bf16[128,4224]{1,0:T(8,128)(2,1)S(1)} %copy-done.5), channel_id=1, source_target_pairs={{4,2},{5,3},{6,0},{7,1},{8,14},{9,15},{10,12},{11,13},{20,18},{21,... | collective-permute-start | bytes 3244040 | tf_op jit(solution)/shard_map/ppermute | solution.py:745
  66.9 1.5 %collective-permute-start.8 = (bf16[64,4224]{1,0:T(8,128)(2,1)S(1)}, bf16[64,4224]{1,0:T(8,128)(2,1)S(1)}, u32[]{:S(2)}, u32[]{:S(2)}) collective-permute-start(bf16[64,4224]{1,0:T(8,128)(2,1)S(1)} %get-tuple-element.126), channel_id=1, source_target_pairs={{0,16},{1,17},{2,18},{3,19},{12,28},{13,29},{14,30},{15,31},{16,0}... | collective-permute-start | bytes 1622024 | tf_op jit(solution)/shard_map/ppermute | solution.py:745
  68.4 8.9 %collective-permute-done.4.refs_4_.refs_7_ = bf16[64,4224]{1,0:T(8,128)(2,1)S(1)} collective-permute-done((bf16[64,4224]{1,0:T(8,128)(2,1)S(1)}, bf16[64,4224]{1,0:T(8,128)(2,1)S(1)}, u32[]{:S(2)}, u32[]{:S(2)}) %collective-permute-start.4) | collective-permute-done | bytes 540704 | tf_op jit(solution)/shard_map/ppermute | solution.py:745
  77.8 3.6 %collective-permute-done.9.refs_9_.refs_11_.refs_8_ = bf16[64,4224]{1,0:T(8,128)(2,1)S(1)} collective-permute-done((bf16[64,4224]{1,0:T(8,128)(2,1)S(1)}, bf16[64,4224]{1,0:T(8,128)(2,1)S(1)}, u32[]{:S(2)}, u32[]{:S(2)}) %collective-permute-start.9) | collective-permute-done | bytes 540704 | tf_op jit(solution)/shard_map/ppermute | solution.py:745
  81.4 11.6 %collective-permute-done.8.refs_8_.refs_10_ = bf16[64,4224]{1,0:T(8,128)(2,1)S(1)} collective-permute-done((bf16[64,4224]{1,0:T(8,128)(2,1)S(1)}, bf16[64,4224]{1,0:T(8,128)(2,1)S(1)}, u32[]{:S(2)}, u32[]{:S(2)}) %collective-permute-start.8) | collective-permute-done | bytes 540704 | tf_op jit(solution)/shard_map/ppermute | solution.py:745
  93.7 10.5 %collective-permute-done.7.refs_7_.refs_9_ = bf16[64,4224]{1,0:T(8,128)(2,1)S(1)} collective-permute-done((bf16[64,4224]{1,0:T(8,128)(2,1)S(1)}, bf16[64,4224]{1,0:T(8,128)(2,1)S(1)}, u32[]{:S(2)}, u32[]{:S(2)}) %collective-permute-start.7) | collective-permute-done | bytes 540704 | tf_op jit(solution)/shard_map/ppermute | solution.py:745
  104.2 2.0 %reduce_own.1 = (f32[128,128]{1,0:T(8,128)S(1)}, f32[256,128]{1,0:T(8,128)S(1)}) custom-call(bf16[128,4224]{1,0:T(8,128)(2,1)S(1)} %copy-done.1, bf16[128,4224]{1,0:T(8,128)(2,1)S(1)} %collective-permute-done.2.refs_1_.refs_4_, bf16[128,4224]{1,0:T(8,128)(2,1)S(1)} %collective-permute-done.refs_2_.refs_5_, ...), custom_call_target="tpu_custom_call" | custom-call | flops 1 | bytes 1 | tf_op jit(solution)/shard_map/reduce_own/pallas_call | solution.py:537
  109.7 2.1 %collective-permute-start.18 = (bf16[64,1024]{1,0:T(8,128)(2,1)S(1)}, bf16[64,1024]{1,0:T(8,128)(2,1)S(1)}, u32[]{:S(2)}, u32[]{:S(2)}) collective-permute-start(bf16[64,1024]{1,0:T(8,128)(2,1)S(1)} %get-tuple-element.110), channel_id=1, source_target_pairs={{0,6},{2,4},{4,2},{6,0},{8,14},{10,12},{12,10},{14,8},{1,7},{3,5},... | collective-permute-start | bytes 393224 | tf_op jit(solution)/shard_map/ppermute | solution.py:729
  111.7 2.5 %reduce_taken.1 = (f32[64,128]{1,0:T(8,128)S(1)}, f32[64,128]{1,0:T(8,128)S(1)}, f32[256,128]{1,0:T(8,128)S(1)}) custom-call(bf16[128,4224]{1,0:T(8,128)(2,1)S(1)} %copy-done.1, bf16[128,4224]{1,0:T(8,128)(2,1)S(1)} %collective-permute-done.2.refs_1_.refs_4_, bf16[128,4224]{1,0:T(8,128)(2,1)S(1)} %collective-permute-done.refs_2_.refs_5_, ...), custom_call_target="tpu_custom_call" | custom-call | flops 1 | bytes 1 | tf_op jit(solution)/shard_map/reduce_taken/pallas_call | solution.py:537
  119.3 6.5 %collective-permute-start.20 = (bf16[64,1024]{1,0:T(8,128)(2,1)S(1)}, bf16[64,1024]{1,0:T(8,128)(2,1)S(1)}, u32[]{:S(2)}, u32[]{:S(2)}) collective-permute-start(bf16[64,1024]{1,0:T(8,128)(2,1)S(1)} %get-tuple-element.123), channel_id=1, source_target_pairs={{0,4},{2,6},{4,0},{6,2},{8,12},{10,14},{12,8},{14,10},{1,5},{3,7},... | collective-permute-start | bytes 393224 | tf_op jit(solution)/shard_map/ppermute | solution.py:729
  125.8 3.7 %collective-permute-done.20.refs_6_ = bf16[64,1024]{1,0:T(8,128)(2,1)S(1)} collective-permute-done((bf16[64,1024]{1,0:T(8,128)(2,1)S(1)}, bf16[64,1024]{1,0:T(8,128)(2,1)S(1)}, u32[]{:S(2)}, u32[]{:S(2)}) %collective-permute-start.20) | collective-permute-done | bytes 131104 | tf_op jit(solution)/shard_map/ppermute | solution.py:729
  129.5 2.2 %collective-permute-done.21.refs_7_ = bf16[64,1024]{1,0:T(8,128)(2,1)S(1)} collective-permute-done((bf16[64,1024]{1,0:T(8,128)(2,1)S(1)}, bf16[64,1024]{1,0:T(8,128)(2,1)S(1)}, u32[]{:S(2)}, u32[]{:S(2)}) %collective-permute-start.21) | collective-permute-done | bytes 131104 | tf_op jit(solution)/shard_map/ppermute | solution.py:729
  131.7 1.8 %join.1 = bf16[512,1024]{1,0:T(8,128)(2,1)} custom-call(s32[16]{0:T(128)S(1)} %copy-done.3, f32[512,1024]{1,0:T(8,128)S(1)} %add.11.base_ref, bf16[64,1024]{1,0:T(8,128)(2,1)S(1)} %get-tuple-element.111.refs_0_, bf16[64,1024]{1,0:T(8,128)(2,1)S(1)} %collective-permute-done.11.refs_1_, bf16[64,1024]{1,0:T(8,128)(2,1)S(1)} %collective-permute-done.17.refs_2_, ...), custom_call_target="tpu_custom_call" | custom-call | flops 524288 | bytes 4194304 | tf_op jit(solution)/shard_map/join/pallas_call | solution.py:714
  (49 shorter events, 11.3 us)
Async XLA Ops:
  4.6 27.1 %collective-permute-start.2 = (bf16[128,4224]{1,0:T(8,128)(2,1)}, bf16[128,4224]{1,0:T(8,128)(2,1)S(1)}, u32[]{:S(2)}, u32[]{:S(2)}) collective-permute-start(bf16[128,4224]{1,0:T(8,128)(2,1)} %get-tuple-element.68), channel_id=1, source_target_pairs={{0,2},{2,0},{4,6},{6,4},{8,10},{10,8},{12,14},{14,12},{1,3},{3,1},... | collective-permute-start | bytes 3244040 | tf_op jit(solution)/shard_map/ppermute | solution.py:729
  7.6 28.0 %collective-permute-start = (bf16[128,4224]{1,0:T(8,128)(2,1)}, bf16[128,4224]{1,0:T(8,128)(2,1)S(1)}, u32[]{:S(2)}, u32[]{:S(2)}) collective-permute-start(bf16[128,4224]{1,0:T(8,128)(2,1)} %get-tuple-element.66), channel_id=1, source_target_pairs={{0,4},{1,5},{2,6},{3,7},{12,8},{13,9},{14,10},{15,11},{16,20},{17,... | collective-permute-start | bytes 3244040 | tf_op jit(solution)/shard_map/ppermute | solution.py:745
  9.7 52.3 %collective-permute-start.1 = (bf16[128,4224]{1,0:T(8,128)(2,1)}, bf16[128,4224]{1,0:T(8,128)(2,1)S(1)}, u32[]{:S(2)}, u32[]{:S(2)}) collective-permute-start(bf16[128,4224]{1,0:T(8,128)(2,1)} %get-tuple-element.67), channel_id=1, source_target_pairs={{0,6},{1,7},{2,4},{3,5},{12,10},{13,11},{14,8},{15,9},{16,22},{17,... | collective-permute-start | bytes 3244040 | tf_op jit(solution)/shard_map/ppermute | solution.py:745
  36.5 25.5 %collective-permute-start.3 = (bf16[64,4224]{1,0:T(8,128)(2,1)}, bf16[64,4224]{1,0:T(8,128)(2,1)S(1)}, u32[]{:S(2)}, u32[]{:S(2)}) collective-permute-start(bf16[64,4224]{1,0:T(8,128)(2,1)} %slice_select_fusion), channel_id=1, source_target_pairs={{0,16},{1,17},{2,18},{3,19},{12,28},{13,29},{14,30},{15,31},{16,0}... | collective-permute-start | bytes 1622024 | tf_op jit(solution)/shard_map/ppermute | solution.py:745
  62.0 19.4 %copy-start.6 = (bf16[64,4224]{1,0:T(8,128)(2,1)S(1)}, bf16[64,4224]{1,0:T(8,128)(2,1)}, u32[]{:S(2)}) copy-start(bf16[64,4224]{1,0:T(8,128)(2,1)} %get-tuple-element.78) | copy-start | bytes 1622020
  62.0 42.2 %copy-start = (bf16[6,4096,64]{1,2,0:T(8,128)(2,1)S(1)}, bf16[6,4096,64]{1,2,0:T(8,128)(2,1)}, u32[]{:S(2)}) copy-start(bf16[6,4096,64]{1,2,0:T(8,128)(2,1)} %param.8) | copy-start | bytes 9437188
  62.0 15.3 %collective-permute-start.4 = (bf16[64,4224]{1,0:T(8,128)(2,1)S(1)}, bf16[64,4224]{1,0:T(8,128)(2,1)S(1)}, u32[]{:S(2)}, u32[]{:S(2)}) collective-permute-start(bf16[64,4224]{1,0:T(8,128)(2,1)S(1)} %copy-done.7), channel_id=1, source_target_pairs={{4,0},{5,1},{6,2},{7,3},{8,12},{9,13},{10,14},{11,15},{20,16},{21,... | collective-permute-start | bytes 1622024 | tf_op jit(solution)/shard_map/ppermute | solution.py:745
  63.7 40.5 %collective-permute-start.6 = (bf16[128,4224]{1,0:T(8,128)(2,1)S(1)}, bf16[128,4224]{1,0:T(8,128)(2,1)S(1)}, u32[]{:S(2)}, u32[]{:S(2)}) collective-permute-start(bf16[128,4224]{1,0:T(8,128)(2,1)S(1)} %copy-done.5), channel_id=1, source_target_pairs={{4,2},{5,3},{6,0},{7,1},{8,14},{9,15},{10,12},{11,13},{20,18},{21,... | collective-permute-start | bytes 3244040 | tf_op jit(solution)/shard_map/ppermute | solution.py:745
  66.1 43.6 %collective-permute-start.13 = (f32[512,1024]{1,0:T(8,128)S(1)}, f32[512,1024]{1,0:T(8,128)S(1)}, u32[]{:S(2)}, u32[]{:S(2)}) collective-permute-start(f32[512,1024]{1,0:T(8,128)S(1)} %fusion.2), channel_id=1, source_target_pairs={{0,1},{1,0},{2,3},{3,2},{4,5},{5,4},{6,7},{7,6},{8,9},{9,8},{10,11... | collective-permute-start | bytes 6291464 | tf_op jit(solution)/shard_map/ppermute | solution.py:729
  66.3 15.1 %collective-permute-start.9 = (bf16[64,4224]{1,0:T(8,128)(2,1)S(1)}, bf16[64,4224]{1,0:T(8,128)(2,1)S(1)}, u32[]{:S(2)}, u32[]{:S(2)}) collective-permute-start(bf16[64,4224]{1,0:T(8,128)(2,1)S(1)} %get-tuple-element.125), channel_id=1, source_target_pairs={{0,16},{1,17},{2,18},{3,19},{12,28},{13,29},{14,30},{15,31},{16,0}... | collective-permute-start | bytes 1622024 | tf_op jit(solution)/shard_map/ppermute | solution.py:745
  66.9 26.1 %collective-permute-start.8 = (bf16[64,4224]{1,0:T(8,128)(2,1)S(1)}, bf16[64,4224]{1,0:T(8,128)(2,1)S(1)}, u32[]{:S(2)}, u32[]{:S(2)}) collective-permute-start(bf16[64,4224]{1,0:T(8,128)(2,1)S(1)} %get-tuple-element.126), channel_id=1, source_target_pairs={{0,16},{1,17},{2,18},{3,19},{12,28},{13,29},{14,30},{15,31},{16,0}... | collective-permute-start | bytes 1622024 | tf_op jit(solution)/shard_map/ppermute | solution.py:745
  77.3 26.9 %collective-permute-start.7 = (bf16[64,4224]{1,0:T(8,128)(2,1)S(1)}, bf16[64,4224]{1,0:T(8,128)(2,1)S(1)}, u32[]{:S(2)}, u32[]{:S(2)}) collective-permute-start(bf16[64,4224]{1,0:T(8,128)(2,1)S(1)} %get-tuple-element.127), channel_id=1, source_target_pairs={{0,16},{1,17},{2,18},{3,19},{12,28},{13,29},{14,30},{15,31},{16,0}... | collective-permute-start | bytes 1622024 | tf_op jit(solution)/shard_map/ppermute | solution.py:745
  81.4 33.2 %collective-permute-start.5 = (bf16[64,4224]{1,0:T(8,128)(2,1)S(1)}, bf16[64,4224]{1,0:T(8,128)(2,1)S(1)}, u32[]{:S(2)}, u32[]{:S(2)}) collective-permute-start(bf16[64,4224]{1,0:T(8,128)(2,1)S(1)} %copy-done.6), channel_id=1, source_target_pairs={{4,0},{5,1},{6,2},{7,3},{8,12},{9,13},{10,14},{11,15},{20,16},{21,... | collective-permute-start | bytes 1622024 | tf_op jit(solution)/shard_map/ppermute | solution.py:745
  93.0 21.6 %collective-permute-start.12 = (bf16[64,4224]{1,0:T(8,128)(2,1)S(1)}, bf16[64,4224]{1,0:T(8,128)(2,1)S(1)}, u32[]{:S(2)}, u32[]{:S(2)}) collective-permute-start(bf16[64,4224]{1,0:T(8,128)(2,1)S(1)} %collective-permute-done.4.refs_4_.refs_7_), channel_id=1, source_target_pairs={{4,20},{5,21},{6,22},{7,23},{8,24},{9,25},{10,26},{11,27},{20,4},{... | collective-permute-start | bytes 1622024 | tf_op jit(solution)/shard_map/ppermute | solution.py:745
  106.2 1.3 collective-permute-start.10
  108.2 6.5 %collective-permute-start.11 = (bf16[64,1024]{1,0:T(8,128)(2,1)S(1)}, bf16[64,1024]{1,0:T(8,128)(2,1)S(1)}, u32[]{:S(2)}, u32[]{:S(2)}) collective-permute-start(bf16[64,1024]{1,0:T(8,128)(2,1)S(1)} %get-tuple-element.91), channel_id=1, source_target_pairs={{0,2},{2,0},{4,6},{6,4},{8,10},{10,8},{12,14},{14,12},{1,3},{3,1},... | collective-permute-start | bytes 393224 | tf_op jit(solution)/shard_map/ppermute | solution.py:729
  108.7 8.5 %collective-permute-start.17 = (bf16[64,1024]{1,0:T(8,128)(2,1)S(1)}, bf16[64,1024]{1,0:T(8,128)(2,1)S(1)}, u32[]{:S(2)}, u32[]{:S(2)}) collective-permute-start(bf16[64,1024]{1,0:T(8,128)(2,1)S(1)} %get-tuple-element.109), channel_id=1, source_target_pairs={{0,4},{2,6},{4,0},{6,2},{8,12},{10,14},{12,8},{14,10},{1,5},{3,7},... | collective-permute-start | bytes 393224 | tf_op jit(solution)/shard_map/ppermute | solution.py:729
  109.7 8.1 %collective-permute-start.18 = (bf16[64,1024]{1,0:T(8,128)(2,1)S(1)}, bf16[64,1024]{1,0:T(8,128)(2,1)S(1)}, u32[]{:S(2)}, u32[]{:S(2)}) collective-permute-start(bf16[64,1024]{1,0:T(8,128)(2,1)S(1)} %get-tuple-element.110), channel_id=1, source_target_pairs={{0,6},{2,4},{4,2},{6,0},{8,14},{10,12},{12,10},{14,8},{1,7},{3,5},... | collective-permute-start | bytes 393224 | tf_op jit(solution)/shard_map/ppermute | solution.py:729
  116.0 1.8 %collective-permute-start.14 = (f32[64,128]{1,0:T(8,128)S(1)}, f32[64,128]{1,0:T(8,128)S(1)}, u32[]{:S(2)}, u32[]{:S(2)}) collective-permute-start(f32[64,128]{1,0:T(8,128)S(1)} %get-tuple-element.115.refs_0_), channel_id=1, source_target_pairs={{0,1},{1,0},{2,3},{3,2},{4,5},{5,4},{6,7},{7,6},{8,9},{9,8},{10,11... | collective-permute-start | bytes 98312 | tf_op jit(solution)/shard_map/ppermute | solution.py:729
  116.1 1.7 %collective-permute-start.16 = (f32[64,128]{1,0:T(8,128)S(1)}, f32[64,128]{1,0:T(8,128)S(1)}, u32[]{:S(2)}, u32[]{:S(2)}) collective-permute-start(f32[64,128]{1,0:T(8,128)S(1)} %get-tuple-element.106), channel_id=1, source_target_pairs={{0,1},{1,0},{2,3},{3,2},{12,13},{13,12},{14,15},{15,14},{16,17},{1... | collective-permute-start | bytes 98312 | tf_op jit(solution)/shard_map/ppermute | solution.py:745
  116.6 1.2 collective-permute-start.15
  118.7 7.1 %collective-permute-start.19 = (bf16[64,1024]{1,0:T(8,128)(2,1)S(1)}, bf16[64,1024]{1,0:T(8,128)(2,1)S(1)}, u32[]{:S(2)}, u32[]{:S(2)}) collective-permute-start(bf16[64,1024]{1,0:T(8,128)(2,1)S(1)} %get-tuple-element.122), channel_id=1, source_target_pairs={{0,2},{2,0},{4,6},{6,4},{8,10},{10,8},{12,14},{14,12},{1,3},{3,1},... | collective-permute-start | bytes 393224 | tf_op jit(solution)/shard_map/ppermute | solution.py:729
  119.3 10.2 %collective-permute-start.20 = (bf16[64,1024]{1,0:T(8,128)(2,1)S(1)}, bf16[64,1024]{1,0:T(8,128)(2,1)S(1)}, u32[]{:S(2)}, u32[]{:S(2)}) collective-permute-start(bf16[64,1024]{1,0:T(8,128)(2,1)S(1)} %get-tuple-element.123), channel_id=1, source_target_pairs={{0,4},{2,6},{4,0},{6,2},{8,12},{10,14},{12,8},{14,10},{1,5},{3,7},... | collective-permute-start | bytes 393224 | tf_op jit(solution)/shard_map/ppermute | solution.py:729
  125.8 5.9 %collective-permute-start.21 = (bf16[64,1024]{1,0:T(8,128)(2,1)S(1)}, bf16[64,1024]{1,0:T(8,128)(2,1)S(1)}, u32[]{:S(2)}, u32[]{:S(2)}) collective-permute-start(bf16[64,1024]{1,0:T(8,128)(2,1)S(1)} %get-tuple-element.124), channel_id=1, source_target_pairs={{0,6},{2,4},{4,2},{6,0},{8,14},{10,12},{12,10},{14,8},{1,7},{3,5},... | collective-permute-start | bytes 393224 | tf_op jit(solution)/shard_map/ppermute | solution.py:729
  (6 other events, 54.4 us)

commit v11 on v10

--- a/solution.py
+++ b/solution.py
@@ -745,6 +745,11 @@
     return lax.ppermute(value, ("groups", "replica", "tensor"), pairs)
 
 
+def return_terms(terms):
+    back = {d: swap(terms[d], "replica", d) for d in reversed(range(1, len(terms)))}
+    return [back[d] for d in range(1, len(terms))]
+
+
 def on_device(x, weight, lefts, ups, ids, residency):
     slots, width, rank = lefts.shape
     features = ups.shape[2]
@@ -767,14 +772,15 @@
             moves.append((plan.inner, 0, half, 0))
         wide_in.append(send(plan, wide[i], moves))
 
-    late_ids, near, late_x = lax.optimization_barrier((ids, near, x))
+    late_ids, _ = lax.optimization_barrier((ids, seg_of))
+    near, late_x = lax.optimization_barrier((near, x))
     own_rows, late, _ = lay_out(plan, False, late_ids, residency, x, left_rows, ups)
     near = own_rows + near
-    def part(which):
+    def part(which, rows):
         columns = lax.dynamic_slice(weight, (0, which * features), (weight.shape[0], features))
-        return jnp.dot(late_x, columns, preferred_element_type=jnp.float32)
-
-    base_other, base_mine = part(1 - core), part(core)
+        return jnp.dot(rows, columns, preferred_element_type=jnp.float32)
+
+    base_other, base_mine = part(1 - core, late_x), part(core, late_x)
 
     def across_send(i):
         d = plan.across[i]
@@ -806,14 +812,14 @@
         send(plan, late_in[0], [(plan.inner, e, 0, 0)]) for e in range(1, plan.groups)
     ]
     base = base_mine + swap(base_other, "tensor", 1)
-    late_in[:-1], across = lax.optimization_barrier((late_in[:-1], across))
+    late_in[:-1], across[:-1] = lax.optimization_barrier((late_in[:-1], across[:-1]))
     across = [[blocks[e] for blocks in across] for e in range(plan.groups - 1)]
 
     own_left = left_rows.reshape(slots * rank, width)
     low, tag = reduce_own(plan, near, wide_in, late_in[:-1], own_left)
     other = swap(low, "tensor", 1)
     terms = expand_own(plan, low, other, tag, ups.reshape(slots * rank, features))
-    deltas = [terms[0]] + [swap(terms[d], "replica", d) for d in range(1, half)]
+    deltas = [terms[0]] + return_terms(terms)
 
     lows, tag = reduce_taken(plan, near, wide_in, late_in[:-1], across)
     late_in[-1], deltas[:2], across_up, base, lows = lax.optimization_barrier(
@@ -827,7 +833,7 @@
     pairs, deltas = lax.optimization_barrier((pairs, deltas))
     across_wide = [blocks[plan.left_pieces] for blocks in across]
     terms = expand_taken(plan, pairs, tag, wide_in, late_in[0], across_wide, across_up)
-    deltas += [terms[0]] + [swap(terms[d], "replica", d) for d in range(1, half)]
+    deltas += [terms[0]] + return_terms(terms)
     return join(seg_of, base, deltas)
 
 

time: 134 us -> 131 us (0.978)
  starting transfers between devices: 27.9 us -> 33.5 us
  waiting for transfers between devices: 66.2 us -> 62.3 us
  matrix products: 18.8 us -> 15 us
    ppermute x10, waiting for transfers between devices: 27.6 us -> 22.8 us  [swap(): return lax.ppermute(value, axis, [(i, i ^ distance) for i in range(count)])]
    ppermute x10, starting transfers between devices: 13.8 us -> 17.8 us  [swap(): return lax.ppermute(value, axis, [(i, i ^ distance) for i in range(count)])]
    dot_general x2, matrix products: 18.8 us -> 15 us  [part(): return jnp.dot(rows, columns, preferred_element_type=jnp.float32)]
    ppermute x12, starting transfers between devices: 14.2 us -> 15.6 us  [send(): return lax.ppermute(value, ('groups', 'replica', 'tensor'), pairs)]
  transfers between devices with their start and end apart: 22 -> 22, of which waited for: 10 -> 13; matrix products, arithmetic and copies ran while one was open for 15% -> 12% of each run, Pallas kernels for 9% -> 9%
where the time goes in v11:
time: 131 us; the launch traced here: 130 us
  waiting for transfers between devices  62.3 us (48%)
  starting transfers between devices  33.5 us (26%)
  Pallas kernels  18.7 us (14%)
  matrix products  15 us (11%)
    ppermute x12, waiting for transfers between devices, send(): return lax.ppermute(value, ('groups', 'replica', 'tensor'), pairs)  39.5 us
    ppermute x10, waiting for transfers between devices, swap(): return lax.ppermute(value, axis, [(i, i ^ distance) for i in range(count)])  22.8 us
    ppermute x10, starting transfers between devices, swap(): return lax.ppermute(value, axis, [(i, i ^ distance) for i in range(count)])  17.8 us
    ppermute x12, starting transfers between devices, send(): return lax.ppermute(value, ('groups', 'replica', 'tensor'), pairs)  15.6 us
    dot_general x2, matrix products, part(): return jnp.dot(rows, columns, preferred_element_type=jnp.float32)  15 us
    pallas_call x2, Pallas kernels, lay_out(): pl.pallas_call(functools.partial(lay_kernel, plan, first_call), out_shape...  9.74 us
    pallas_call x4, Pallas kernels, blocks_call(): pl.pallas_call(body, out_shape=out_shape, in_specs=[VMEM] * n_extra + [HB...  5.95 us
  transfers between devices with their start and end apart: 22, of which 13 were waited for; matrix products, arithmetic and copies ran while one was open for 12% of the time, Pallas kernels for 9%

profile of v11, /device:TPU:0, one launch (start us, length us, event | category | flops | bytes accessed | tf_op | source)
XLA Modules:
  0.0 130.3 jit_solution(1527829272566973270)
XLA Ops:
  0.0 4.6 %lay_out_first.1 = (bf16[128,4224]{1,0:T(8,128)(2,1)}, bf16[128,4224]{1,0:T(8,128)(2,1)}, bf16[128,4224]{1,0:T(8,128)(2,1)}, s32[16]{0:T(128)}) custom-call(s32[16]{0:T(128)} %ids_ref.2, s32[48]{0:T(128)} %residency_ref.3, bf16[512,4096]{1,0:T(8,128)(2,1)} %x_ref.3, bf16[6,64,4096]{2,1,0:T(8,128)(2,1)} %bitcast.6, bf16[6,64,1024]{2,1,0:T(8,128)(2,1)} %up_ref.3), custom_call_target="tpu_custom_call" | custom-call | bytes 2097152 | tf_op jit(solution)/shard_map/lay_out_first/pallas_call | solution.py:229
  4.6 3.0 %collective-permute-start.2 = (bf16[128,4224]{1,0:T(8,128)(2,1)}, bf16[128,4224]{1,0:T(8,128)(2,1)S(1)}, u32[]{:S(2)}, u32[]{:S(2)}) collective-permute-start(bf16[128,4224]{1,0:T(8,128)(2,1)} %get-tuple-element.69), channel_id=1, source_target_pairs={{0,2},{2,0},{4,6},{6,4},{8,10},{10,8},{12,14},{14,12},{1,3},{3,1},... | collective-permute-start | bytes 3244040 | tf_op jit(solution)/shard_map/ppermute | solution.py:729
  7.7 2.0 %collective-permute-start = (bf16[128,4224]{1,0:T(8,128)(2,1)}, bf16[128,4224]{1,0:T(8,128)(2,1)S(1)}, u32[]{:S(2)}, u32[]{:S(2)}) collective-permute-start(bf16[128,4224]{1,0:T(8,128)(2,1)} %get-tuple-element.65), channel_id=1, source_target_pairs={{0,4},{1,5},{2,6},{3,7},{12,8},{13,9},{14,10},{15,11},{16,20},{17,... | collective-permute-start | bytes 3244040 | tf_op jit(solution)/shard_map/ppermute | solution.py:745
  9.7 2.1 %collective-permute-start.1 = (bf16[128,4224]{1,0:T(8,128)(2,1)}, bf16[128,4224]{1,0:T(8,128)(2,1)S(1)}, u32[]{:S(2)}, u32[]{:S(2)}) collective-permute-start(bf16[128,4224]{1,0:T(8,128)(2,1)} %get-tuple-element.66), channel_id=1, source_target_pairs={{0,6},{1,7},{2,4},{3,5},{12,10},{13,11},{14,8},{15,9},{16,22},{17,... | collective-permute-start | bytes 3244040 | tf_op jit(solution)/shard_map/ppermute | solution.py:745
  11.8 5.1 %lay_out_second.1 = (bf16[128,4224]{1,0:T(8,128)(2,1)}, bf16[64,4224]{1,0:T(8,128)(2,1)}, bf16[128,4224]{1,0:T(8,128)(2,1)}, bf16[64,4224]{1,0:T(8,128)(2,1)}, s32[16]{0:T(128)}) custom-call(s32[16]{0:T(128)} %ids_ref.2, s32[48]{0:T(128)} %residency_ref.3, bf16[512,4096]{1,0:T(8,128)(2,1)} %x_ref.3, bf16[6,64,4096]{2,1,0:T(8,128)(2,1)} %bitcast.7, ...), custom_call_target="tpu_custom_call" | custom-call | bytes 2097152 | tf_op jit(solution)/shard_map/lay_out_second/pallas_call | solution.py:229
  16.9 14.8 %collective-permute-done.2.refs_1_.refs_4_ = bf16[128,4224]{1,0:T(8,128)(2,1)S(1)} collective-permute-done((bf16[128,4224]{1,0:T(8,128)(2,1)}, bf16[128,4224]{1,0:T(8,128)(2,1)S(1)}, u32[]{:S(2)}, u32[]{:S(2)}) %collective-permute-start.2) | collective-permute-done | bytes 1081376 | tf_op jit(solution)/shard_map/ppermute | solution.py:729
  31.7 3.9 %collective-permute-done.refs_2_.refs_5_ = bf16[128,4224]{1,0:T(8,128)(2,1)S(1)} collective-permute-done((bf16[128,4224]{1,0:T(8,128)(2,1)}, bf16[128,4224]{1,0:T(8,128)(2,1)S(1)}, u32[]{:S(2)}, u32[]{:S(2)}) %collective-permute-start) | collective-permute-done | bytes 1081376 | tf_op jit(solution)/shard_map/ppermute | solution.py:745
  37.3 9.1 %fusion = f32[512,1024]{1,0:T(8,128)S(1)} fusion(bf16[512,4096]{1,0:T(8,128)(2,1)} %x_ref.3, bf16[4096,2048]{1,0:T(8,128)(2,1)} %param.7, s32[]{:T(128)S(6)} %select_n.27), kind=kOutput, calls=%fused_computation | convolution fusion | flops 4294967296 | bytes 14680068 | tf_op jit(solution)/shard_map/dot_general | solution.py:781
  46.5 5.9 %fusion.2 = f32[512,1024]{1,0:T(8,128)} fusion(bf16[512,4096]{1,0:T(8,128)(2,1)S(1)} %copy-done.4, bf16[4096,2048]{1,0:T(8,128)(2,1)S(1)} %bitcast.11, s32[]{:T(128)S(6)} %select_n.26), kind=kOutput, calls=%fused_computation.2 | convolution fusion | flops 4294967296 | bytes 14680068 | tf_op jit(solution)/shard_map/dot_general | solution.py:781
  52.4 5.3 %collective-permute-done.1.refs_3_.refs_6_ = bf16[128,4224]{1,0:T(8,128)(2,1)S(1)} collective-permute-done((bf16[128,4224]{1,0:T(8,128)(2,1)}, bf16[128,4224]{1,0:T(8,128)(2,1)S(1)}, u32[]{:S(2)}, u32[]{:S(2)}) %collective-permute-start.1) | collective-permute-done | bytes 1081376 | tf_op jit(solution)/shard_map/ppermute | solution.py:745
  57.7 1.7 %collective-permute-start.4 = (bf16[64,4224]{1,0:T(8,128)(2,1)}, bf16[64,4224]{1,0:T(8,128)(2,1)S(1)}, u32[]{:S(2)}, u32[]{:S(2)}) collective-permute-start(bf16[64,4224]{1,0:T(8,128)(2,1)} %get-tuple-element.75), channel_id=1, source_target_pairs={{4,0},{5,1},{6,2},{7,3},{8,12},{9,13},{10,14},{11,15},{20,16},{21,... | collective-permute-start | bytes 1622024 | tf_op jit(solution)/shard_map/ppermute | solution.py:745
  59.4 2.1 %collective-permute-start.6 = (bf16[128,4224]{1,0:T(8,128)(2,1)}, bf16[128,4224]{1,0:T(8,128)(2,1)S(1)}, u32[]{:S(2)}, u32[]{:S(2)}) collective-permute-start(bf16[128,4224]{1,0:T(8,128)(2,1)} %get-tuple-element.83), channel_id=1, source_target_pairs={{4,2},{5,3},{6,0},{7,1},{8,14},{9,15},{10,12},{11,13},{20,18},{21,... | collective-permute-start | bytes 3244040 | tf_op jit(solution)/shard_map/ppermute | solution.py:745
  63.7 9.4 %collective-permute-done.4.refs_4_.refs_7_ = bf16[64,4224]{1,0:T(8,128)(2,1)S(1)} collective-permute-done((bf16[64,4224]{1,0:T(8,128)(2,1)}, bf16[64,4224]{1,0:T(8,128)(2,1)S(1)}, u32[]{:S(2)}, u32[]{:S(2)}) %collective-permute-start.4) | collective-permute-done | bytes 540704 | tf_op jit(solution)/shard_map/ppermute | solution.py:745
  74.6 2.1 %collective-permute-done.8.refs_8_.refs_10_ = bf16[64,4224]{1,0:T(8,128)(2,1)S(1)} collective-permute-done((bf16[64,4224]{1,0:T(8,128)(2,1)S(1)}, bf16[64,4224]{1,0:T(8,128)(2,1)S(1)}, u32[]{:S(2)}, u32[]{:S(2)}) %collective-permute-start.8) | collective-permute-done | bytes 540704 | tf_op jit(solution)/shard_map/ppermute | solution.py:745
  77.5 10.8 %collective-permute-done.7.refs_7_.refs_9_ = bf16[64,4224]{1,0:T(8,128)(2,1)S(1)} collective-permute-done((bf16[64,4224]{1,0:T(8,128)(2,1)S(1)}, bf16[64,4224]{1,0:T(8,128)(2,1)S(1)}, u32[]{:S(2)}, u32[]{:S(2)}) %collective-permute-start.7) | collective-permute-done | bytes 540704 | tf_op jit(solution)/shard_map/ppermute | solution.py:745
  89.0 7.2 %collective-permute-done.6.refs_5_ = bf16[128,4224]{1,0:T(8,128)(2,1)S(1)} collective-permute-done((bf16[128,4224]{1,0:T(8,128)(2,1)}, bf16[128,4224]{1,0:T(8,128)(2,1)S(1)}, u32[]{:S(2)}, u32[]{:S(2)}) %collective-permute-start.6) | collective-permute-done | bytes 1081376 | tf_op jit(solution)/shard_map/ppermute | solution.py:745
  96.2 2.0 %reduce_own.1 = (f32[128,128]{1,0:T(8,128)S(1)}, f32[256,128]{1,0:T(8,128)S(1)}) custom-call(bf16[128,4224]{1,0:T(8,128)(2,1)S(1)} %copy-done.1, bf16[128,4224]{1,0:T(8,128)(2,1)S(1)} %collective-permute-done.2.refs_1_.refs_4_, bf16[128,4224]{1,0:T(8,128)(2,1)S(1)} %collective-permute-done.refs_2_.refs_5_, ...), custom_call_target="tpu_custom_call" | custom-call | flops 1 | bytes 1 | tf_op jit(solution)/shard_map/reduce_own/pallas_call | solution.py:537
  101.8 1.6 %collective-permute-start.17 = (bf16[64,1024]{1,0:T(8,128)(2,1)S(1)}, bf16[64,1024]{1,0:T(8,128)(2,1)S(1)}, u32[]{:S(2)}, u32[]{:S(2)}) collective-permute-start(bf16[64,1024]{1,0:T(8,128)(2,1)S(1)} %get-tuple-element.107), channel_id=1, source_target_pairs={{0,4},{2,6},{4,0},{6,2},{8,12},{10,14},{12,8},{14,10},{1,5},{3,7},... | collective-permute-start | bytes 393224 | tf_op jit(solution)/shard_map/ppermute | solution.py:729
  103.7 2.5 %reduce_taken.1 = (f32[64,128]{1,0:T(8,128)S(1)}, f32[64,128]{1,0:T(8,128)S(1)}, f32[256,128]{1,0:T(8,128)S(1)}) custom-call(bf16[128,4224]{1,0:T(8,128)(2,1)S(1)} %copy-done.1, bf16[128,4224]{1,0:T(8,128)(2,1)S(1)} %collective-permute-done.2.refs_1_.refs_4_, bf16[128,4224]{1,0:T(8,128)(2,1)S(1)} %collective-permute-done.refs_2_.refs_5_, ...), custom_call_target="tpu_custom_call" | custom-call | flops 1 | bytes 1 | tf_op jit(solution)/shard_map/reduce_taken/pallas_call | solution.py:537
  112.3 1.6 %collective-permute-start.19 = (bf16[64,1024]{1,0:T(8,128)(2,1)S(1)}, bf16[64,1024]{1,0:T(8,128)(2,1)S(1)}, u32[]{:S(2)}, u32[]{:S(2)}) collective-permute-start(bf16[64,1024]{1,0:T(8,128)(2,1)S(1)} %get-tuple-element.120), channel_id=1, source_target_pairs={{0,2},{2,0},{4,6},{6,4},{8,10},{10,8},{12,14},{14,12},{1,3},{3,1},... | collective-permute-start | bytes 393224 | tf_op jit(solution)/shard_map/ppermute | solution.py:729
  113.9 8.6 %collective-permute-start.20 = (bf16[64,1024]{1,0:T(8,128)(2,1)S(1)}, bf16[64,1024]{1,0:T(8,128)(2,1)S(1)}, u32[]{:S(2)}, u32[]{:S(2)}) collective-permute-start(bf16[64,1024]{1,0:T(8,128)(2,1)S(1)} %get-tuple-element.121), channel_id=1, source_target_pairs={{0,4},{2,6},{4,0},{6,2},{8,12},{10,14},{12,8},{14,10},{1,5},{3,7},... | collective-permute-start | bytes 393224 | tf_op jit(solution)/shard_map/ppermute | solution.py:729
  123.4 3.1 %collective-permute-done.20.refs_6_ = bf16[64,1024]{1,0:T(8,128)(2,1)S(1)} collective-permute-done((bf16[64,1024]{1,0:T(8,128)(2,1)S(1)}, bf16[64,1024]{1,0:T(8,128)(2,1)S(1)}, u32[]{:S(2)}, u32[]{:S(2)}) %collective-permute-start.20) | collective-permute-done | bytes 131104 | tf_op jit(solution)/shard_map/ppermute | solution.py:729
  126.5 2.0 %collective-permute-done.21.refs_7_ = bf16[64,1024]{1,0:T(8,128)(2,1)S(1)} collective-permute-done((bf16[64,1024]{1,0:T(8,128)(2,1)S(1)}, bf16[64,1024]{1,0:T(8,128)(2,1)S(1)}, u32[]{:S(2)}, u32[]{:S(2)}) %collective-permute-start.21) | collective-permute-done | bytes 131104 | tf_op jit(solution)/shard_map/ppermute | solution.py:729
  128.5 1.8 %join.1 = bf16[512,1024]{1,0:T(8,128)(2,1)} custom-call(s32[16]{0:T(128)S(1)} %copy-done.3, f32[512,1024]{1,0:T(8,128)S(1)} %add.11.base_ref, bf16[64,1024]{1,0:T(8,128)(2,1)S(1)} %get-tuple-element.109.refs_0_, bf16[64,1024]{1,0:T(8,128)(2,1)S(1)} %collective-permute-done.10.refs_1_, bf16[64,1024]{1,0:T(8,128)(2,1)S(1)} %collective-permute-done.17.refs_2_, ...), custom_call_target="tpu_custom_call" | custom-call | flops 524288 | bytes 4194304 | tf_op jit(solution)/shard_map/join/pallas_call | solution.py:714
  (54 shorter events, 17.7 us)
Async XLA Ops:
  4.6 27.1 %collective-permute-start.2 = (bf16[128,4224]{1,0:T(8,128)(2,1)}, bf16[128,4224]{1,0:T(8,128)(2,1)S(1)}, u32[]{:S(2)}, u32[]{:S(2)}) collective-permute-start(bf16[128,4224]{1,0:T(8,128)(2,1)} %get-tuple-element.69), channel_id=1, source_target_pairs={{0,2},{2,0},{4,6},{6,4},{8,10},{10,8},{12,14},{14,12},{1,3},{3,1},... | collective-permute-start | bytes 3244040 | tf_op jit(solution)/shard_map/ppermute | solution.py:729
  7.7 28.0 %collective-permute-start = (bf16[128,4224]{1,0:T(8,128)(2,1)}, bf16[128,4224]{1,0:T(8,128)(2,1)S(1)}, u32[]{:S(2)}, u32[]{:S(2)}) collective-permute-start(bf16[128,4224]{1,0:T(8,128)(2,1)} %get-tuple-element.65), channel_id=1, source_target_pairs={{0,4},{1,5},{2,6},{3,7},{12,8},{13,9},{14,10},{15,11},{16,20},{17,... | collective-permute-start | bytes 3244040 | tf_op jit(solution)/shard_map/ppermute | solution.py:745
  9.7 48.0 %collective-permute-start.1 = (bf16[128,4224]{1,0:T(8,128)(2,1)}, bf16[128,4224]{1,0:T(8,128)(2,1)S(1)}, u32[]{:S(2)}, u32[]{:S(2)}) collective-permute-start(bf16[128,4224]{1,0:T(8,128)(2,1)} %get-tuple-element.66), channel_id=1, source_target_pairs={{0,6},{1,7},{2,4},{3,5},{12,10},{13,11},{14,8},{15,9},{16,22},{17,... | collective-permute-start | bytes 3244040 | tf_op jit(solution)/shard_map/ppermute | solution.py:745
  35.8 21.9 %collective-permute-start.3 = (bf16[64,4224]{1,0:T(8,128)(2,1)S(1)}, bf16[64,4224]{1,0:T(8,128)(2,1)S(1)}, u32[]{:S(2)}, u32[]{:S(2)}) collective-permute-start(bf16[64,4224]{1,0:T(8,128)(2,1)S(1)} %slice_select_fusion), channel_id=1, source_target_pairs={{0,16},{1,17},{2,18},{3,19},{12,28},{13,29},{14,30},{15,31},{16,0}... | collective-permute-start | bytes 1622024 | tf_op jit(solution)/shard_map/ppermute | solution.py:745
  52.4 24.3 %copy-start.5 = (bf16[64,4224]{1,0:T(8,128)(2,1)S(1)}, bf16[64,4224]{1,0:T(8,128)(2,1)}, u32[]{:S(2)}) copy-start(bf16[64,4224]{1,0:T(8,128)(2,1)} %get-tuple-element.77) | copy-start | bytes 1622020
  52.4 43.8 %copy-start = (bf16[6,4096,64]{1,2,0:T(8,128)(2,1)S(1)}, bf16[6,4096,64]{1,2,0:T(8,128)(2,1)}, u32[]{:S(2)}) copy-start(bf16[6,4096,64]{1,2,0:T(8,128)(2,1)} %param.8) | copy-start | bytes 9437188
  57.7 15.4 %collective-permute-start.4 = (bf16[64,4224]{1,0:T(8,128)(2,1)}, bf16[64,4224]{1,0:T(8,128)(2,1)S(1)}, u32[]{:S(2)}, u32[]{:S(2)}) collective-permute-start(bf16[64,4224]{1,0:T(8,128)(2,1)} %get-tuple-element.75), channel_id=1, source_target_pairs={{4,0},{5,1},{6,2},{7,3},{8,12},{9,13},{10,14},{11,15},{20,16},{21,... | collective-permute-start | bytes 1622024 | tf_op jit(solution)/shard_map/ppermute | solution.py:745
  59.4 36.9 %collective-permute-start.6 = (bf16[128,4224]{1,0:T(8,128)(2,1)}, bf16[128,4224]{1,0:T(8,128)(2,1)S(1)}, u32[]{:S(2)}, u32[]{:S(2)}) collective-permute-start(bf16[128,4224]{1,0:T(8,128)(2,1)} %get-tuple-element.83), channel_id=1, source_target_pairs={{4,2},{5,3},{6,0},{7,1},{8,14},{9,15},{10,12},{11,13},{20,18},{21,... | collective-permute-start | bytes 3244040 | tf_op jit(solution)/shard_map/ppermute | solution.py:745
  61.5 41.9 %collective-permute-start.12 = (f32[512,1024]{1,0:T(8,128)}, f32[512,1024]{1,0:T(8,128)S(1)}, u32[]{:S(2)}, u32[]{:S(2)}) collective-permute-start(f32[512,1024]{1,0:T(8,128)} %fusion.2), channel_id=1, source_target_pairs={{0,1},{1,0},{2,3},{3,2},{4,5},{5,4},{6,7},{7,6},{8,9},{9,8},{10,11... | collective-permute-start | bytes 6291464 | tf_op jit(solution)/shard_map/ppermute | solution.py:729
  61.6 15.1 %collective-permute-start.8 = (bf16[64,4224]{1,0:T(8,128)(2,1)S(1)}, bf16[64,4224]{1,0:T(8,128)(2,1)S(1)}, u32[]{:S(2)}, u32[]{:S(2)}) collective-permute-start(bf16[64,4224]{1,0:T(8,128)(2,1)S(1)} %get-tuple-element.124), channel_id=1, source_target_pairs={{0,16},{1,17},{2,18},{3,19},{12,28},{13,29},{14,30},{15,31},{16,0}... | collective-permute-start | bytes 1622024 | tf_op jit(solution)/shard_map/ppermute | solution.py:745
  63.2 25.2 %collective-permute-start.7 = (bf16[64,4224]{1,0:T(8,128)(2,1)S(1)}, bf16[64,4224]{1,0:T(8,128)(2,1)S(1)}, u32[]{:S(2)}, u32[]{:S(2)}) collective-permute-start(bf16[64,4224]{1,0:T(8,128)(2,1)S(1)} %get-tuple-element.125), channel_id=1, source_target_pairs={{0,16},{1,17},{2,18},{3,19},{12,28},{13,29},{14,30},{15,31},{16,0}... | collective-permute-start | bytes 1622024 | tf_op jit(solution)/shard_map/ppermute | solution.py:745
  73.1 28.6 %collective-permute-start.13 = (bf16[64,4224]{1,0:T(8,128)(2,1)S(1)}, bf16[64,4224]{1,0:T(8,128)(2,1)S(1)}, u32[]{:S(2)}, u32[]{:S(2)}) collective-permute-start(bf16[64,4224]{1,0:T(8,128)(2,1)S(1)} %get-tuple-element.123), channel_id=1, source_target_pairs={{0,16},{1,17},{2,18},{3,19},{12,28},{13,29},{14,30},{15,31},{16,0}... | collective-permute-start | bytes 1622024 | tf_op jit(solution)/shard_map/ppermute | solution.py:745
  76.8 30.6 %collective-permute-start.5 = (bf16[64,4224]{1,0:T(8,128)(2,1)S(1)}, bf16[64,4224]{1,0:T(8,128)(2,1)S(1)}, u32[]{:S(2)}, u32[]{:S(2)}) collective-permute-start(bf16[64,4224]{1,0:T(8,128)(2,1)S(1)} %copy-done.5), channel_id=1, source_target_pairs={{4,0},{5,1},{6,2},{7,3},{8,12},{9,13},{10,14},{11,15},{20,16},{21,... | collective-permute-start | bytes 1622024 | tf_op jit(solution)/shard_map/ppermute | solution.py:745
  88.3 19.0 %collective-permute-start.11 = (bf16[64,4224]{1,0:T(8,128)(2,1)S(1)}, bf16[64,4224]{1,0:T(8,128)(2,1)S(1)}, u32[]{:S(2)}, u32[]{:S(2)}) collective-permute-start(bf16[64,4224]{1,0:T(8,128)(2,1)S(1)} %collective-permute-done.4.refs_4_.refs_7_), channel_id=1, source_target_pairs={{4,20},{5,21},{6,22},{7,23},{8,24},{9,25},{10,26},{11,27},{20,4},{... | collective-permute-start | bytes 1622024 | tf_op jit(solution)/shard_map/ppermute | solution.py:745
  98.2 1.3 %collective-permute-start.9 = (f32[128,128]{1,0:T(8,128)S(1)}, f32[128,128]{1,0:T(8,128)S(1)}, u32[]{:S(2)}, u32[]{:S(2)}) collective-permute-start(f32[128,128]{1,0:T(8,128)S(1)} %get-tuple-element.87.refs_0_), channel_id=1, source_target_pairs={{0,1},{1,0},{2,3},{3,2},{4,5},{5,4},{6,7},{7,6},{8,9},{9,8},{10,11... | collective-permute-start | bytes 196616 | tf_op jit(solution)/shard_map/ppermute | solution.py:729
  100.2 7.2 %collective-permute-start.10 = (bf16[64,1024]{1,0:T(8,128)(2,1)S(1)}, bf16[64,1024]{1,0:T(8,128)(2,1)S(1)}, u32[]{:S(2)}, u32[]{:S(2)}) collective-permute-start(bf16[64,1024]{1,0:T(8,128)(2,1)S(1)} %get-tuple-element.90), channel_id=1, source_target_pairs={{0,2},{2,0},{4,6},{6,4},{8,10},{10,8},{12,14},{14,12},{1,3},{3,1},... | collective-permute-start | bytes 393224 | tf_op jit(solution)/shard_map/ppermute | solution.py:729
  101.8 8.3 %collective-permute-start.17 = (bf16[64,1024]{1,0:T(8,128)(2,1)S(1)}, bf16[64,1024]{1,0:T(8,128)(2,1)S(1)}, u32[]{:S(2)}, u32[]{:S(2)}) collective-permute-start(bf16[64,1024]{1,0:T(8,128)(2,1)S(1)} %get-tuple-element.107), channel_id=1, source_target_pairs={{0,4},{2,6},{4,0},{6,2},{8,12},{10,14},{12,8},{14,10},{1,5},{3,7},... | collective-permute-start | bytes 393224 | tf_op jit(solution)/shard_map/ppermute | solution.py:729
  103.4 8.0 %collective-permute-start.18 = (bf16[64,1024]{1,0:T(8,128)(2,1)S(1)}, bf16[64,1024]{1,0:T(8,128)(2,1)S(1)}, u32[]{:S(2)}, u32[]{:S(2)}) collective-permute-start(bf16[64,1024]{1,0:T(8,128)(2,1)S(1)} %get-tuple-element.108), channel_id=1, source_target_pairs={{0,6},{2,4},{4,2},{6,0},{8,14},{10,12},{12,10},{14,8},{1,7},{3,5},... | collective-permute-start | bytes 393224 | tf_op jit(solution)/shard_map/ppermute | solution.py:729
  108.5 2.9 %collective-permute-start.14 = (f32[64,128]{1,0:T(8,128)S(1)}, f32[64,128]{1,0:T(8,128)S(1)}, u32[]{:S(2)}, u32[]{:S(2)}) collective-permute-start(f32[64,128]{1,0:T(8,128)S(1)} %get-tuple-element.113.refs_0_), channel_id=1, source_target_pairs={{0,1},{1,0},{2,3},{3,2},{4,5},{5,4},{6,7},{7,6},{8,9},{9,8},{10,11... | collective-permute-start | bytes 98312 | tf_op jit(solution)/shard_map/ppermute | solution.py:729
  108.6 2.8 %collective-permute-start.16 = (f32[64,128]{1,0:T(8,128)S(1)}, f32[64,128]{1,0:T(8,128)S(1)}, u32[]{:S(2)}, u32[]{:S(2)}) collective-permute-start(f32[64,128]{1,0:T(8,128)S(1)} %get-tuple-element.104), channel_id=1, source_target_pairs={{0,1},{1,0},{2,3},{3,2},{12,13},{13,12},{14,15},{15,14},{16,17},{1... | collective-permute-start | bytes 98312 | tf_op jit(solution)/shard_map/ppermute | solution.py:745
  109.1 2.3 %collective-permute-start.15 = (f32[64,128]{1,0:T(8,128)S(1)}, f32[64,128]{1,0:T(8,128)S(1)}, u32[]{:S(2)}, u32[]{:S(2)}) collective-permute-start(f32[64,128]{1,0:T(8,128)S(1)} %get-tuple-element.104), channel_id=1, source_target_pairs={{0,0},{1,1},{2,2},{3,3},{12,12},{13,13},{14,14},{15,15},{16,16},{1... | collective-permute-start | bytes 98312 | tf_op jit(solution)/shard_map/ppermute | solution.py:745
  112.3 11.1 %collective-permute-start.19 = (bf16[64,1024]{1,0:T(8,128)(2,1)S(1)}, bf16[64,1024]{1,0:T(8,128)(2,1)S(1)}, u32[]{:S(2)}, u32[]{:S(2)}) collective-permute-start(bf16[64,1024]{1,0:T(8,128)(2,1)S(1)} %get-tuple-element.120), channel_id=1, source_target_pairs={{0,2},{2,0},{4,6},{6,4},{8,10},{10,8},{12,14},{14,12},{1,3},{3,1},... | collective-permute-start | bytes 393224 | tf_op jit(solution)/shard_map/ppermute | solution.py:729
  113.9 12.6 %collective-permute-start.20 = (bf16[64,1024]{1,0:T(8,128)(2,1)S(1)}, bf16[64,1024]{1,0:T(8,128)(2,1)S(1)}, u32[]{:S(2)}, u32[]{:S(2)}) collective-permute-start(bf16[64,1024]{1,0:T(8,128)(2,1)S(1)} %get-tuple-element.121), channel_id=1, source_target_pairs={{0,4},{2,6},{4,0},{6,2},{8,12},{10,14},{12,8},{14,10},{1,5},{3,7},... | collective-permute-start | bytes 393224 | tf_op jit(solution)/shard_map/ppermute | solution.py:729
  122.4 6.0 %collective-permute-start.21 = (bf16[64,1024]{1,0:T(8,128)(2,1)S(1)}, bf16[64,1024]{1,0:T(8,128)(2,1)S(1)}, u32[]{:S(2)}, u32[]{:S(2)}) collective-permute-start(bf16[64,1024]{1,0:T(8,128)(2,1)S(1)} %get-tuple-element.122), channel_id=1, source_target_pairs={{0,6},{2,4},{4,2},{6,0},{8,14},{10,12},{12,10},{14,8},{1,7},{3,5},... | collective-permute-start | bytes 393224 | tf_op jit(solution)/shard_map/ppermute | solution.py:729
  (8 other events, 92.1 us)

commit v12 on v11

--- a/solution.py
+++ b/solution.py
@@ -808,9 +808,8 @@
         if unit == plan.units - 1:
             late_in[0], block = lax.optimization_barrier((late_in[0], block))
         late_in.append(send(plan, block, moves))
-    across_up = [
-        send(plan, late_in[0], [(plan.inner, e, 0, 0)]) for e in range(1, plan.groups)
-    ]
+    late_up = late_in[0][: plan.up_rows, :width]
+    across_up = [send(plan, late_up, [(plan.inner, e, 0, 0)]) for e in range(1, plan.groups)]
     base = base_mine + swap(base_other, "tensor", 1)
     late_in[:-1], across[:-1] = lax.optimization_barrier((late_in[:-1], across[:-1]))
     across = [[blocks[e] for blocks in across] for e in range(plan.groups - 1)]

time: 131 us -> 128 us (0.977)
  starting transfers between devices: 33.5 us -> 30.3 us
  waiting for transfers between devices: 62.3 us -> 64.2 us
    ppermute x10, starting transfers between devices: 17.8 us -> 14.7 us  [swap(): return lax.ppermute(value, axis, [(i, i ^ distance) for i in range(count)])]
    dot_general x2, matrix products: 15 us -> 13.7 us  [part(): return jnp.dot(rows, columns, preferred_element_type=jnp.float32)]
    ppermute x12, waiting for transfers between devices: 39.5 us -> 40.8 us  [send(): return lax.ppermute(value, ('groups', 'replica', 'tensor'), pairs)]
  transfers between devices with their start and end apart: 22 -> 22, of which waited for: 13 -> 13; matrix products, arithmetic and copies ran while one was open for 12% -> 11% of each run, Pallas kernels for 9% -> 9%
where the time goes in v12:
time: 128 us
  waiting for transfers between devices  64.2 us (50%)
  starting transfers between devices  30.3 us (24%)
  Pallas kernels  18.7 us (15%)
  matrix products  13.7 us (11%)
    ppermute x12, waiting for transfers between devices, send(): return lax.ppermute(value, ('groups', 'replica', 'tensor'), pairs)  40.8 us
    ppermute x10, waiting for transfers between devices, swap(): return lax.ppermute(value, axis, [(i, i ^ distance) for i in range(count)])  23.4 us
    ppermute x12, starting transfers between devices, send(): return lax.ppermute(value, ('groups', 'replica', 'tensor'), pairs)  15.6 us
    ppermute x10, starting transfers between devices, swap(): return lax.ppermute(value, axis, [(i, i ^ distance) for i in range(count)])  14.7 us
    dot_general x2, matrix products, part(): return jnp.dot(rows, columns, preferred_element_type=jnp.float32)  13.7 us
    pallas_call x2, Pallas kernels, lay_out(): pl.pallas_call(functools.partial(lay_kernel, plan, first_call), out_shape...  9.72 us
    pallas_call x4, Pallas kernels, blocks_call(): pl.pallas_call(body, out_shape=out_shape, in_specs=[VMEM] * n_extra + [HB...  5.95 us
  transfers between devices with their start and end apart: 22, of which 13 were waited for; matrix products, arithmetic and copies ran while one was open for 11% of the time, Pallas kernels for 9%

profile of v12, /device:TPU:0, one launch (start us, length us, event | category | flops | bytes accessed | tf_op | source)
XLA Modules:
  0.0 127.8 jit_solution(3422550887308064762)
XLA Ops:
  0.0 4.6 %lay_out_first.1 = (bf16[128,4224]{1,0:T(8,128)(2,1)}, bf16[128,4224]{1,0:T(8,128)(2,1)}, bf16[128,4224]{1,0:T(8,128)(2,1)}, s32[16]{0:T(128)}) custom-call(s32[16]{0:T(128)} %ids_ref.2, s32[48]{0:T(128)} %residency_ref.3, bf16[512,4096]{1,0:T(8,128)(2,1)} %x_ref.3, bf16[6,64,4096]{2,1,0:T(8,128)(2,1)} %bitcast.6, bf16[6,64,1024]{2,1,0:T(8,128)(2,1)} %up_ref.3), custom_call_target="tpu_custom_call" | custom-call | bytes 2097152 | tf_op jit(solution)/shard_map/lay_out_first/pallas_call | solution.py:229
  4.6 3.0 %collective-permute-start.2 = (bf16[128,4224]{1,0:T(8,128)(2,1)}, bf16[128,4224]{1,0:T(8,128)(2,1)S(1)}, u32[]{:S(2)}, u32[]{:S(2)}) collective-permute-start(bf16[128,4224]{1,0:T(8,128)(2,1)} %get-tuple-element.69), channel_id=1, source_target_pairs={{0,2},{2,0},{4,6},{6,4},{8,10},{10,8},{12,14},{14,12},{1,3},{3,1},... | collective-permute-start | bytes 3244040 | tf_op jit(solution)/shard_map/ppermute | solution.py:729
  7.7 2.1 %collective-permute-start = (bf16[128,4224]{1,0:T(8,128)(2,1)}, bf16[128,4224]{1,0:T(8,128)(2,1)S(1)}, u32[]{:S(2)}, u32[]{:S(2)}) collective-permute-start(bf16[128,4224]{1,0:T(8,128)(2,1)} %get-tuple-element.65), channel_id=1, source_target_pairs={{0,4},{1,5},{2,6},{3,7},{12,8},{13,9},{14,10},{15,11},{16,20},{17,... | collective-permute-start | bytes 3244040 | tf_op jit(solution)/shard_map/ppermute | solution.py:745
  9.7 2.1 %collective-permute-start.1 = (bf16[128,4224]{1,0:T(8,128)(2,1)}, bf16[128,4224]{1,0:T(8,128)(2,1)S(1)}, u32[]{:S(2)}, u32[]{:S(2)}) collective-permute-start(bf16[128,4224]{1,0:T(8,128)(2,1)} %get-tuple-element.66), channel_id=1, source_target_pairs={{0,6},{1,7},{2,4},{3,5},{12,10},{13,11},{14,8},{15,9},{16,22},{17,... | collective-permute-start | bytes 3244040 | tf_op jit(solution)/shard_map/ppermute | solution.py:745
  11.8 5.1 %lay_out_second.1 = (bf16[128,4224]{1,0:T(8,128)(2,1)}, bf16[64,4224]{1,0:T(8,128)(2,1)}, bf16[128,4224]{1,0:T(8,128)(2,1)}, bf16[64,4224]{1,0:T(8,128)(2,1)}, s32[16]{0:T(128)}) custom-call(s32[16]{0:T(128)} %ids_ref.2, s32[48]{0:T(128)} %residency_ref.3, bf16[512,4096]{1,0:T(8,128)(2,1)} %x_ref.3, bf16[6,64,4096]{2,1,0:T(8,128)(2,1)} %bitcast.7, ...), custom_call_target="tpu_custom_call" | custom-call | bytes 2097152 | tf_op jit(solution)/shard_map/lay_out_second/pallas_call | solution.py:229
  16.9 14.8 %collective-permute-done.2.refs_1_.refs_4_ = bf16[128,4224]{1,0:T(8,128)(2,1)S(1)} collective-permute-done((bf16[128,4224]{1,0:T(8,128)(2,1)}, bf16[128,4224]{1,0:T(8,128)(2,1)S(1)}, u32[]{:S(2)}, u32[]{:S(2)}) %collective-permute-start.2) | collective-permute-done | bytes 1081376 | tf_op jit(solution)/shard_map/ppermute | solution.py:729
  31.7 3.9 %collective-permute-done.refs_2_.refs_5_ = bf16[128,4224]{1,0:T(8,128)(2,1)S(1)} collective-permute-done((bf16[128,4224]{1,0:T(8,128)(2,1)}, bf16[128,4224]{1,0:T(8,128)(2,1)S(1)}, u32[]{:S(2)}, u32[]{:S(2)}) %collective-permute-start) | collective-permute-done | bytes 1081376 | tf_op jit(solution)/shard_map/ppermute | solution.py:745
  37.3 9.1 %fusion = f32[512,1024]{1,0:T(8,128)S(1)} fusion(bf16[512,4096]{1,0:T(8,128)(2,1)} %x_ref.3, bf16[4096,2048]{1,0:T(8,128)(2,1)} %param.7, s32[]{:T(128)S(6)} %select_n.27), kind=kOutput, calls=%fused_computation | convolution fusion | flops 4294967296 | bytes 14680068 | tf_op jit(solution)/shard_map/dot_general | solution.py:781
  46.6 4.5 %fusion.2 = f32[512,1024]{1,0:T(8,128)S(1)} fusion(bf16[512,4096]{1,0:T(8,128)(2,1)S(1)} %copy-done.4, bf16[4096,2048]{1,0:T(8,128)(2,1)S(1)} %bitcast.11, s32[]{:T(128)S(6)} %select_n.26), kind=kOutput, calls=%fused_computation.2 | convolution fusion | flops 4294967296 | bytes 14680068 | tf_op jit(solution)/shard_map/dot_general | solution.py:781
  51.1 6.6 %collective-permute-done.1.refs_3_.refs_6_ = bf16[128,4224]{1,0:T(8,128)(2,1)S(1)} collective-permute-done((bf16[128,4224]{1,0:T(8,128)(2,1)}, bf16[128,4224]{1,0:T(8,128)(2,1)S(1)}, u32[]{:S(2)}, u32[]{:S(2)}) %collective-permute-start.1) | collective-permute-done | bytes 1081376 | tf_op jit(solution)/shard_map/ppermute | solution.py:745
  57.7 1.7 %collective-permute-start.4 = (bf16[64,4224]{1,0:T(8,128)(2,1)}, bf16[64,4224]{1,0:T(8,128)(2,1)S(1)}, u32[]{:S(2)}, u32[]{:S(2)}) collective-permute-start(bf16[64,4224]{1,0:T(8,128)(2,1)} %get-tuple-element.75), channel_id=1, source_target_pairs={{4,0},{5,1},{6,2},{7,3},{8,12},{9,13},{10,14},{11,15},{20,16},{21,... | collective-permute-start | bytes 1622024 | tf_op jit(solution)/shard_map/ppermute | solution.py:745
  59.4 2.1 %collective-permute-start.6 = (bf16[128,4224]{1,0:T(8,128)(2,1)S(1)}, bf16[128,4224]{1,0:T(8,128)(2,1)S(1)}, u32[]{:S(2)}, u32[]{:S(2)}) collective-permute-start(bf16[128,4224]{1,0:T(8,128)(2,1)S(1)} %copy-done.5), channel_id=1, source_target_pairs={{4,2},{5,3},{6,0},{7,1},{8,14},{9,15},{10,12},{11,13},{20,18},{21,... | collective-permute-start | bytes 3244040 | tf_op jit(solution)/shard_map/ppermute | solution.py:745
  63.7 9.4 %collective-permute-done.4.refs_4_.refs_7_ = bf16[64,4224]{1,0:T(8,128)(2,1)S(1)} collective-permute-done((bf16[64,4224]{1,0:T(8,128)(2,1)}, bf16[64,4224]{1,0:T(8,128)(2,1)S(1)}, u32[]{:S(2)}, u32[]{:S(2)}) %collective-permute-start.4) | collective-permute-done | bytes 540704 | tf_op jit(solution)/shard_map/ppermute | solution.py:745
  74.6 2.1 %collective-permute-done.8.refs_8_.refs_10_ = bf16[64,4224]{1,0:T(8,128)(2,1)S(1)} collective-permute-done((bf16[64,4224]{1,0:T(8,128)(2,1)S(1)}, bf16[64,4224]{1,0:T(8,128)(2,1)S(1)}, u32[]{:S(2)}, u32[]{:S(2)}) %collective-permute-start.8) | collective-permute-done | bytes 540704 | tf_op jit(solution)/shard_map/ppermute | solution.py:745
  77.6 10.7 %collective-permute-done.7.refs_7_.refs_9_ = bf16[64,4224]{1,0:T(8,128)(2,1)S(1)} collective-permute-done((bf16[64,4224]{1,0:T(8,128)(2,1)S(1)}, bf16[64,4224]{1,0:T(8,128)(2,1)S(1)}, u32[]{:S(2)}, u32[]{:S(2)}) %collective-permute-start.7) | collective-permute-done | bytes 540704 | tf_op jit(solution)/shard_map/ppermute | solution.py:745
  89.0 7.2 %collective-permute-done.6.refs_5_ = bf16[128,4224]{1,0:T(8,128)(2,1)S(1)} collective-permute-done((bf16[128,4224]{1,0:T(8,128)(2,1)S(1)}, bf16[128,4224]{1,0:T(8,128)(2,1)S(1)}, u32[]{:S(2)}, u32[]{:S(2)}) %collective-permute-start.6) | collective-permute-done | bytes 1081376 | tf_op jit(solution)/shard_map/ppermute | solution.py:745
  96.2 2.0 %reduce_own.1 = (f32[128,128]{1,0:T(8,128)S(1)}, f32[256,128]{1,0:T(8,128)S(1)}) custom-call(bf16[128,4224]{1,0:T(8,128)(2,1)S(1)} %copy-done.1, bf16[128,4224]{1,0:T(8,128)(2,1)S(1)} %collective-permute-done.2.refs_1_.refs_4_, bf16[128,4224]{1,0:T(8,128)(2,1)S(1)} %collective-permute-done.refs_2_.refs_5_, ...), custom_call_target="tpu_custom_call" | custom-call | flops 1 | bytes 1 | tf_op jit(solution)/shard_map/reduce_own/pallas_call | solution.py:537
  101.8 1.6 %collective-permute-start.17 = (bf16[64,1024]{1,0:T(8,128)(2,1)S(1)}, bf16[64,1024]{1,0:T(8,128)(2,1)S(1)}, u32[]{:S(2)}, u32[]{:S(2)}) collective-permute-start(bf16[64,1024]{1,0:T(8,128)(2,1)S(1)} %get-tuple-element.107), channel_id=1, source_target_pairs={{0,4},{2,6},{4,0},{6,2},{8,12},{10,14},{12,8},{14,10},{1,5},{3,7},... | collective-permute-start | bytes 393224 | tf_op jit(solution)/shard_map/ppermute | solution.py:729
  103.7 2.5 %reduce_taken.1 = (f32[64,128]{1,0:T(8,128)S(1)}, f32[64,128]{1,0:T(8,128)S(1)}, f32[256,128]{1,0:T(8,128)S(1)}) custom-call(bf16[128,4224]{1,0:T(8,128)(2,1)S(1)} %copy-done.1, bf16[128,4224]{1,0:T(8,128)(2,1)S(1)} %collective-permute-done.2.refs_1_.refs_4_, bf16[128,4224]{1,0:T(8,128)(2,1)S(1)} %collective-permute-done.refs_2_.refs_5_, ...), custom_call_target="tpu_custom_call" | custom-call | flops 1 | bytes 1 | tf_op jit(solution)/shard_map/reduce_taken/pallas_call | solution.py:537
  112.3 1.6 %collective-permute-start.19 = (bf16[64,1024]{1,0:T(8,128)(2,1)S(1)}, bf16[64,1024]{1,0:T(8,128)(2,1)S(1)}, u32[]{:S(2)}, u32[]{:S(2)}) collective-permute-start(bf16[64,1024]{1,0:T(8,128)(2,1)S(1)} %get-tuple-element.120), channel_id=1, source_target_pairs={{0,2},{2,0},{4,6},{6,4},{8,10},{10,8},{12,14},{14,12},{1,3},{3,1},... | collective-permute-start | bytes 393224 | tf_op jit(solution)/shard_map/ppermute | solution.py:729
  113.9 6.0 %collective-permute-start.20 = (bf16[64,1024]{1,0:T(8,128)(2,1)S(1)}, bf16[64,1024]{1,0:T(8,128)(2,1)S(1)}, u32[]{:S(2)}, u32[]{:S(2)}) collective-permute-start(bf16[64,1024]{1,0:T(8,128)(2,1)S(1)} %get-tuple-element.121), channel_id=1, source_target_pairs={{0,4},{2,6},{4,0},{6,2},{8,12},{10,14},{12,8},{14,10},{1,5},{3,7},... | collective-permute-start | bytes 393224 | tf_op jit(solution)/shard_map/ppermute | solution.py:729
  120.3 3.8 %collective-permute-done.20.refs_6_ = bf16[64,1024]{1,0:T(8,128)(2,1)S(1)} collective-permute-done((bf16[64,1024]{1,0:T(8,128)(2,1)S(1)}, bf16[64,1024]{1,0:T(8,128)(2,1)S(1)}, u32[]{:S(2)}, u32[]{:S(2)}) %collective-permute-start.20) | collective-permute-done | bytes 131104 | tf_op jit(solution)/shard_map/ppermute | solution.py:729
  124.0 2.0 %collective-permute-done.21.refs_7_ = bf16[64,1024]{1,0:T(8,128)(2,1)S(1)} collective-permute-done((bf16[64,1024]{1,0:T(8,128)(2,1)S(1)}, bf16[64,1024]{1,0:T(8,128)(2,1)S(1)}, u32[]{:S(2)}, u32[]{:S(2)}) %collective-permute-start.21) | collective-permute-done | bytes 131104 | tf_op jit(solution)/shard_map/ppermute | solution.py:729
  126.0 1.8 %join.1 = bf16[512,1024]{1,0:T(8,128)(2,1)} custom-call(s32[16]{0:T(128)S(1)} %copy-done.3, f32[512,1024]{1,0:T(8,128)S(1)} %add.11.base_ref, bf16[64,1024]{1,0:T(8,128)(2,1)S(1)} %get-tuple-element.109.refs_0_, bf16[64,1024]{1,0:T(8,128)(2,1)S(1)} %collective-permute-done.10.refs_1_, bf16[64,1024]{1,0:T(8,128)(2,1)S(1)} %collective-permute-done.17.refs_2_, ...), custom_call_target="tpu_custom_call" | custom-call | flops 524288 | bytes 4194304 | tf_op jit(solution)/shard_map/join/pallas_call | solution.py:714
  (57 shorter events, 17.1 us)
Async XLA Ops:
  4.6 27.1 %collective-permute-start.2 = (bf16[128,4224]{1,0:T(8,128)(2,1)}, bf16[128,4224]{1,0:T(8,128)(2,1)S(1)}, u32[]{:S(2)}, u32[]{:S(2)}) collective-permute-start(bf16[128,4224]{1,0:T(8,128)(2,1)} %get-tuple-element.69), channel_id=1, source_target_pairs={{0,2},{2,0},{4,6},{6,4},{8,10},{10,8},{12,14},{14,12},{1,3},{3,1},... | collective-permute-start | bytes 3244040 | tf_op jit(solution)/shard_map/ppermute | solution.py:729
  7.7 28.0 %collective-permute-start = (bf16[128,4224]{1,0:T(8,128)(2,1)}, bf16[128,4224]{1,0:T(8,128)(2,1)S(1)}, u32[]{:S(2)}, u32[]{:S(2)}) collective-permute-start(bf16[128,4224]{1,0:T(8,128)(2,1)} %get-tuple-element.65), channel_id=1, source_target_pairs={{0,4},{1,5},{2,6},{3,7},{12,8},{13,9},{14,10},{15,11},{16,20},{17,... | collective-permute-start | bytes 3244040 | tf_op jit(solution)/shard_map/ppermute | solution.py:745
  9.7 48.0 %collective-permute-start.1 = (bf16[128,4224]{1,0:T(8,128)(2,1)}, bf16[128,4224]{1,0:T(8,128)(2,1)S(1)}, u32[]{:S(2)}, u32[]{:S(2)}) collective-permute-start(bf16[128,4224]{1,0:T(8,128)(2,1)} %get-tuple-element.66), channel_id=1, source_target_pairs={{0,6},{1,7},{2,4},{3,5},{12,10},{13,11},{14,8},{15,9},{16,22},{17,... | collective-permute-start | bytes 3244040 | tf_op jit(solution)/shard_map/ppermute | solution.py:745
  35.8 21.9 %collective-permute-start.3 = (bf16[64,4224]{1,0:T(8,128)(2,1)S(1)}, bf16[64,4224]{1,0:T(8,128)(2,1)S(1)}, u32[]{:S(2)}, u32[]{:S(2)}) collective-permute-start(bf16[64,4224]{1,0:T(8,128)(2,1)S(1)} %slice_select_fusion), channel_id=1, source_target_pairs={{0,16},{1,17},{2,18},{3,19},{12,28},{13,29},{14,30},{15,31},{16,0}... | collective-permute-start | bytes 1622024 | tf_op jit(solution)/shard_map/ppermute | solution.py:745
  51.1 25.6 %copy-start.6 = (bf16[64,4224]{1,0:T(8,128)(2,1)S(1)}, bf16[64,4224]{1,0:T(8,128)(2,1)}, u32[]{:S(2)}) copy-start(bf16[64,4224]{1,0:T(8,128)(2,1)} %get-tuple-element.77) | copy-start | bytes 1622020
  57.7 38.5 %copy-start = (bf16[6,4096,64]{1,2,0:T(8,128)(2,1)S(1)}, bf16[6,4096,64]{1,2,0:T(8,128)(2,1)}, u32[]{:S(2)}) copy-start(bf16[6,4096,64]{1,2,0:T(8,128)(2,1)} %param.8) | copy-start | bytes 9437188
  57.7 15.4 %collective-permute-start.4 = (bf16[64,4224]{1,0:T(8,128)(2,1)}, bf16[64,4224]{1,0:T(8,128)(2,1)S(1)}, u32[]{:S(2)}, u32[]{:S(2)}) collective-permute-start(bf16[64,4224]{1,0:T(8,128)(2,1)} %get-tuple-element.75), channel_id=1, source_target_pairs={{4,0},{5,1},{6,2},{7,3},{8,12},{9,13},{10,14},{11,15},{20,16},{21,... | collective-permute-start | bytes 1622024 | tf_op jit(solution)/shard_map/ppermute | solution.py:745
  59.4 36.8 %collective-permute-start.6 = (bf16[128,4224]{1,0:T(8,128)(2,1)S(1)}, bf16[128,4224]{1,0:T(8,128)(2,1)S(1)}, u32[]{:S(2)}, u32[]{:S(2)}) collective-permute-start(bf16[128,4224]{1,0:T(8,128)(2,1)S(1)} %copy-done.5), channel_id=1, source_target_pairs={{4,2},{5,3},{6,0},{7,1},{8,14},{9,15},{10,12},{11,13},{20,18},{21,... | collective-permute-start | bytes 3244040 | tf_op jit(solution)/shard_map/ppermute | solution.py:745
  61.4 41.9 %collective-permute-start.12 = (f32[512,1024]{1,0:T(8,128)S(1)}, f32[512,1024]{1,0:T(8,128)S(1)}, u32[]{:S(2)}, u32[]{:S(2)}) collective-permute-start(f32[512,1024]{1,0:T(8,128)S(1)} %fusion.2), channel_id=1, source_target_pairs={{0,1},{1,0},{2,3},{3,2},{4,5},{5,4},{6,7},{7,6},{8,9},{9,8},{10,11... | collective-permute-start | bytes 6291464 | tf_op jit(solution)/shard_map/ppermute | solution.py:729
  61.6 15.1 %collective-permute-start.8 = (bf16[64,4224]{1,0:T(8,128)(2,1)S(1)}, bf16[64,4224]{1,0:T(8,128)(2,1)S(1)}, u32[]{:S(2)}, u32[]{:S(2)}) collective-permute-start(bf16[64,4224]{1,0:T(8,128)(2,1)S(1)} %get-tuple-element.124), channel_id=1, source_target_pairs={{0,16},{1,17},{2,18},{3,19},{12,28},{13,29},{14,30},{15,31},{16,0}... | collective-permute-start | bytes 1622024 | tf_op jit(solution)/shard_map/ppermute | solution.py:745
  63.2 25.2 %collective-permute-start.7 = (bf16[64,4224]{1,0:T(8,128)(2,1)S(1)}, bf16[64,4224]{1,0:T(8,128)(2,1)S(1)}, u32[]{:S(2)}, u32[]{:S(2)}) collective-permute-start(bf16[64,4224]{1,0:T(8,128)(2,1)S(1)} %get-tuple-element.125), channel_id=1, source_target_pairs={{0,16},{1,17},{2,18},{3,19},{12,28},{13,29},{14,30},{15,31},{16,0}... | collective-permute-start | bytes 1622024 | tf_op jit(solution)/shard_map/ppermute | solution.py:745
  73.1 28.6 %collective-permute-start.13 = (bf16[64,4224]{1,0:T(8,128)(2,1)S(1)}, bf16[64,4224]{1,0:T(8,128)(2,1)S(1)}, u32[]{:S(2)}, u32[]{:S(2)}) collective-permute-start(bf16[64,4224]{1,0:T(8,128)(2,1)S(1)} %get-tuple-element.123), channel_id=1, source_target_pairs={{0,16},{1,17},{2,18},{3,19},{12,28},{13,29},{14,30},{15,31},{16,0}... | collective-permute-start | bytes 1622024 | tf_op jit(solution)/shard_map/ppermute | solution.py:745
  76.7 30.6 %collective-permute-start.5 = (bf16[64,4224]{1,0:T(8,128)(2,1)S(1)}, bf16[64,4224]{1,0:T(8,128)(2,1)S(1)}, u32[]{:S(2)}, u32[]{:S(2)}) collective-permute-start(bf16[64,4224]{1,0:T(8,128)(2,1)S(1)} %copy-done.6), channel_id=1, source_target_pairs={{4,0},{5,1},{6,2},{7,3},{8,12},{9,13},{10,14},{11,15},{20,16},{21,... | collective-permute-start | bytes 1622024 | tf_op jit(solution)/shard_map/ppermute | solution.py:745
  88.3 18.3 %collective-permute-start.11 = (bf16[48,4096]{1,0:T(8,128)(2,1)S(1)}, bf16[48,4096]{1,0:T(8,128)(2,1)S(1)}, u32[]{:S(2)}, u32[]{:S(2)}) collective-permute-start(bf16[48,4096]{1,0:T(8,128)(2,1)S(1)} %slice.28), channel_id=1, source_target_pairs={{4,20},{5,21},{6,22},{7,23},{8,24},{9,25},{10,26},{11,27},{20,4},{... | collective-permute-start | bytes 1179656 | tf_op jit(solution)/shard_map/ppermute | solution.py:745
  98.2 1.3 %collective-permute-start.9 = (f32[128,128]{1,0:T(8,128)S(1)}, f32[128,128]{1,0:T(8,128)S(1)}, u32[]{:S(2)}, u32[]{:S(2)}) collective-permute-start(f32[128,128]{1,0:T(8,128)S(1)} %get-tuple-element.87.refs_0_), channel_id=1, source_target_pairs={{0,1},{1,0},{2,3},{3,2},{4,5},{5,4},{6,7},{7,6},{8,9},{9,8},{10,11... | collective-permute-start | bytes 196616 | tf_op jit(solution)/shard_map/ppermute | solution.py:729
  100.2 7.2 %collective-permute-start.10 = (bf16[64,1024]{1,0:T(8,128)(2,1)S(1)}, bf16[64,1024]{1,0:T(8,128)(2,1)S(1)}, u32[]{:S(2)}, u32[]{:S(2)}) collective-permute-start(bf16[64,1024]{1,0:T(8,128)(2,1)S(1)} %get-tuple-element.90), channel_id=1, source_target_pairs={{0,2},{2,0},{4,6},{6,4},{8,10},{10,8},{12,14},{14,12},{1,3},{3,1},... | collective-permute-start | bytes 393224 | tf_op jit(solution)/shard_map/ppermute | solution.py:729
  101.8 8.3 %collective-permute-start.17 = (bf16[64,1024]{1,0:T(8,128)(2,1)S(1)}, bf16[64,1024]{1,0:T(8,128)(2,1)S(1)}, u32[]{:S(2)}, u32[]{:S(2)}) collective-permute-start(bf16[64,1024]{1,0:T(8,128)(2,1)S(1)} %get-tuple-element.107), channel_id=1, source_target_pairs={{0,4},{2,6},{4,0},{6,2},{8,12},{10,14},{12,8},{14,10},{1,5},{3,7},... | collective-permute-start | bytes 393224 | tf_op jit(solution)/shard_map/ppermute | solution.py:729
  103.4 8.0 %collective-permute-start.18 = (bf16[64,1024]{1,0:T(8,128)(2,1)S(1)}, bf16[64,1024]{1,0:T(8,128)(2,1)S(1)}, u32[]{:S(2)}, u32[]{:S(2)}) collective-permute-start(bf16[64,1024]{1,0:T(8,128)(2,1)S(1)} %get-tuple-element.108), channel_id=1, source_target_pairs={{0,6},{2,4},{4,2},{6,0},{8,14},{10,12},{12,10},{14,8},{1,7},{3,5},... | collective-permute-start | bytes 393224 | tf_op jit(solution)/shard_map/ppermute | solution.py:729
  108.5 2.8 %collective-permute-start.14 = (f32[64,128]{1,0:T(8,128)S(1)}, f32[64,128]{1,0:T(8,128)S(1)}, u32[]{:S(2)}, u32[]{:S(2)}) collective-permute-start(f32[64,128]{1,0:T(8,128)S(1)} %get-tuple-element.113.refs_0_), channel_id=1, source_target_pairs={{0,1},{1,0},{2,3},{3,2},{4,5},{5,4},{6,7},{7,6},{8,9},{9,8},{10,11... | collective-permute-start | bytes 98312 | tf_op jit(solution)/shard_map/ppermute | solution.py:729
  108.6 2.8 %collective-permute-start.16 = (f32[64,128]{1,0:T(8,128)S(1)}, f32[64,128]{1,0:T(8,128)S(1)}, u32[]{:S(2)}, u32[]{:S(2)}) collective-permute-start(f32[64,128]{1,0:T(8,128)S(1)} %get-tuple-element.104), channel_id=1, source_target_pairs={{0,1},{1,0},{2,3},{3,2},{12,13},{13,12},{14,15},{15,14},{16,17},{1... | collective-permute-start | bytes 98312 | tf_op jit(solution)/shard_map/ppermute | solution.py:745
  109.1 2.3 %collective-permute-start.15 = (f32[64,128]{1,0:T(8,128)S(1)}, f32[64,128]{1,0:T(8,128)S(1)}, u32[]{:S(2)}, u32[]{:S(2)}) collective-permute-start(f32[64,128]{1,0:T(8,128)S(1)} %get-tuple-element.104), channel_id=1, source_target_pairs={{0,0},{1,1},{2,2},{3,3},{12,12},{13,13},{14,14},{15,15},{16,16},{1... | collective-permute-start | bytes 98312 | tf_op jit(solution)/shard_map/ppermute | solution.py:745
  112.3 7.9 %collective-permute-start.19 = (bf16[64,1024]{1,0:T(8,128)(2,1)S(1)}, bf16[64,1024]{1,0:T(8,128)(2,1)S(1)}, u32[]{:S(2)}, u32[]{:S(2)}) collective-permute-start(bf16[64,1024]{1,0:T(8,128)(2,1)S(1)} %get-tuple-element.120), channel_id=1, source_target_pairs={{0,2},{2,0},{4,6},{6,4},{8,10},{10,8},{12,14},{14,12},{1,3},{3,1},... | collective-permute-start | bytes 393224 | tf_op jit(solution)/shard_map/ppermute | solution.py:729
  113.9 10.1 %collective-permute-start.20 = (bf16[64,1024]{1,0:T(8,128)(2,1)S(1)}, bf16[64,1024]{1,0:T(8,128)(2,1)S(1)}, u32[]{:S(2)}, u32[]{:S(2)}) collective-permute-start(bf16[64,1024]{1,0:T(8,128)(2,1)S(1)} %get-tuple-element.121), channel_id=1, source_target_pairs={{0,4},{2,6},{4,0},{6,2},{8,12},{10,14},{12,8},{14,10},{1,5},{3,7},... | collective-permute-start | bytes 393224 | tf_op jit(solution)/shard_map/ppermute | solution.py:729
  119.9 6.1 %collective-permute-start.21 = (bf16[64,1024]{1,0:T(8,128)(2,1)S(1)}, bf16[64,1024]{1,0:T(8,128)(2,1)S(1)}, u32[]{:S(2)}, u32[]{:S(2)}) collective-permute-start(bf16[64,1024]{1,0:T(8,128)(2,1)S(1)} %get-tuple-element.122), channel_id=1, source_target_pairs={{0,6},{2,4},{4,2},{6,0},{8,14},{10,12},{12,10},{14,8},{1,7},{3,5},... | collective-permute-start | bytes 393224 | tf_op jit(solution)/shard_map/ppermute | solution.py:729
  (9 other events, 102.4 us)

commit v13 on v12

--- a/solution.py
+++ b/solution.py
@@ -89,8 +89,10 @@
 def lay_kernel(plan, first_call, ids_ref, residency_ref, x_ref, left_ref, up_ref, *rest):
     n_near = len(plan.near) - 1 if first_call else 1
     n_blocks = plan.wide if first_call else len(plan.late_blocks())
+    n_tags = len(plan.cross) if first_call else 0
     near, rest = rest[:n_near], rest[n_near:]
     blocks, rest = rest[:n_blocks], rest[n_blocks:]
+    tag_outs, rest = rest[:n_tags], rest[n_tags:]
     seg_out, seg_ref, slot_ref, count_ref, staged, tags, left, up, in_sems, sems = rest
     half, slots, width, share = plan.half, plan.slots, plan.width, plan.share
     me = lax.axis_index("replica")
@@ -128,7 +130,10 @@
             departures.append(pltpu.make_async_copy(source, target, sems.at[len(departures)]))
             departures[-1].start()
 
-        for d, kind, target in tagged:
+        written = [(d, kind) for d, kind, _ in tagged]
+        if first_call:
+            written += [(d, kind) for d in plan.cross for kind in range(2)]
+        for d, kind in written:
             for p in range(CAP):
                 slot = slot_ref[(me ^ (d + kind * half)) * CAP + p].astype(jnp.float32)
                 tags[d, pl.ds((kind * CAP + p) * SEG, SEG), :] = jnp.full(
@@ -136,6 +141,8 @@
                 ).astype(tags.dtype)
         for d, kind, target in tagged:
             depart(tags.at[d, pl.ds(kind * PAIR, PAIR)], target.at[:, pl.ds(width, LANES)])
+        for d, tag_out in zip(plan.cross, tag_outs):
+            depart(tags.at[d], tag_out)
         for arrival, (_, stage, target) in zip(arrivals, moves):
             arrival.wait()
             if target is not None:
@@ -205,8 +212,7 @@
 
     @pl.when(rows_outer)
     def _():
-        targets = cross_targets + near_targets
-        move(row_moves(targets), targets)
+        move(row_moves(cross_targets + near_targets), near_targets)
 
     @pl.when(jnp.logical_not(rows_outer))
     def _():
@@ -219,13 +225,12 @@
 
 def lay_out(plan, first_call, ids, residency, x, left_rows, ups):
     count = 2 * plan.half * CAP
-    wide = jax.ShapeDtypeStruct((2 * PAIR, plan.width + LANES), x.dtype)
-    late = [
-        jax.ShapeDtypeStruct((n * PAIR, plan.width + LANES), x.dtype)
-        for _, n, _ in plan.late_blocks()
-    ]
-    near = [wide] * (len(plan.near) - 1 if first_call else 1)
-    blocks = [wide] * plan.wide if first_call else late
+    tagged = jax.ShapeDtypeStruct((2 * PAIR, plan.width + LANES), x.dtype)
+    near = [tagged] * (len(plan.near) - 1 if first_call else 1)
+    heights = [2] * plan.wide if first_call else [n for _, n, _ in plan.late_blocks()]
+    blocks = [jax.ShapeDtypeStruct((n * PAIR, plan.width), x.dtype) for n in heights]
+    if first_call:
+        blocks += [jax.ShapeDtypeStruct((2 * PAIR, LANES), x.dtype)] * len(plan.cross)
     out = pl.pallas_call(
         functools.partial(lay_kernel, plan, first_call),
         out_shape=near + blocks + [jax.ShapeDtypeStruct((count,), jnp.int32)],
@@ -325,7 +330,7 @@
     return total
 
 
-def copy_rows(copies, plan, kind, target, columns, near, wide, narrow):
+def copy_rows(copies, plan, kind, target, columns, near, wide, late):
     span = pl.ds(kind * PAIR, PAIR)
     for i, d in enumerate(plan.near):
         copies.both(target.at[pl.ds(d * PAIR, PAIR)], near[i].at[span, columns])
@@ -335,8 +340,16 @@
             copies.one(jnp.logical_not(copies.outer), place, wide[i].at[span, columns])
         else:
             copies.both(
-                place, plan.late_rows(narrow, i, kind).at[:, columns], wide[i].at[span, columns]
+                place, plan.late_rows(late, i, kind).at[:, columns], wide[i].at[span, columns]
             )
+
+
+def copy_tags(copies, plan, kind, target, near, tags):
+    span = pl.ds(kind * PAIR, PAIR)
+    for i, d in enumerate(plan.near):
+        copies.both(target.at[pl.ds(d * PAIR, PAIR)], near[i].at[span, pl.ds(plan.width, LANES)])
+    for i, d in enumerate(plan.cross):
+        copies.both(target.at[pl.ds(d * PAIR, PAIR)], tags[i].at[span])
 
 
 def product_of(rows, left):
@@ -345,7 +358,7 @@
     )
 
 
-def reduce_own_kernel(plan, n_steps, near, wide, narrow, own, low_ref, tag_ref, *scratch):
+def reduce_own_kernel(plan, n_steps, near, wide, late, tags, own, low_ref, tag_ref, *scratch):
     rows, left, acc, tag, sems = scratch
     block = plan.width // n_steps
     outer = am_outer(plan)
@@ -353,11 +366,12 @@
     steps = []
     for k in range(n_steps + 1):
         copies = Copies(outer, sems.at[pl.ds(k * each, each)])
-        columns = pl.ds(k * block, block) if k < n_steps else pl.ds(plan.width, LANES)
-        target = rows.at[:, columns] if k < n_steps else tag
-        copy_rows(copies, plan, 0, target, columns, near, wide, narrow)
         if k < n_steps:
+            columns = pl.ds(k * block, block)
+            copy_rows(copies, plan, 0, rows.at[:, columns], columns, near, wide, late)
             copies.both(left.at[:, columns], own.at[:, columns])
+        else:
+            copy_tags(copies, plan, 0, tag, near, tags)
         steps.append(copies)
     for k in range(n_steps):
         steps[k].wait()
@@ -370,7 +384,7 @@
     low_ref[...] = pack(fold(acc, tags, acc.shape[1], plan.slots, plan.rank), plan.rank)
 
 
-def reduce_taken_kernel(plan, n_steps, near, wide, narrow, across, *rest):
+def reduce_taken_kernel(plan, n_steps, near, wide, late, tags, across, *rest):
     lows, tag_ref = rest[: plan.groups], rest[plan.groups]
     rows, left, acc, tag, sems = rest[plan.groups + 1 :]
     block = plan.width // n_steps
@@ -383,7 +397,6 @@
     @pl.when(outer)
     def _():
         rows[0, missing, :] = jnp.zeros((PAIR, plan.width), rows.dtype)
-        tag[0, missing, :] = jnp.zeros((PAIR, LANES), tag.dtype)
 
     if plan.last_piece is not None:
 
@@ -397,8 +410,10 @@
     for k in range(n_steps + 1):
         copies = Copies(outer, sems.at[pl.ds(k * each, each)])
         columns = pl.ds(k * block, block) if k < n_steps else pl.ds(plan.width, LANES)
-        target = rows.at[0, :, columns] if k < n_steps else tag.at[0]
-        copy_rows(copies, plan, 1, target, columns, near, wide, narrow)
+        if k < n_steps:
+            copy_rows(copies, plan, 1, rows.at[0, :, columns], columns, near, wide, late)
+        else:
+            copy_tags(copies, plan, 1, tag.at[0], near, tags)
         for e in range(1, plan.groups):
             for i, d in enumerate(plan.across):
                 target = rows.at[e, :, columns] if k < n_steps else tag.at[e]
@@ -417,7 +432,7 @@
                     copies.both(
                         place,
                         of_wide(wide, piece).at[span],
-                        late_adapters(narrow, piece, plan).at[span],
+                        late_adapters(late, piece, plan).at[span],
                     )
                 for e in range(1, plan.groups):
                     copies.one(
@@ -446,7 +461,7 @@
     groups, width = plan.groups, plan.width
     before, tag_ref, refs = refs[:groups], refs[groups], refs[groups + 1 :]
     near, wide, last, across = refs[:4]
-    lows, tag_out = refs[4 : 4 + groups], refs[4 + groups]
+    lows = refs[4:]
     outer = am_outer(plan)
     inner = jnp.logical_not(outer)
     first_row = plan.cross[0] * PAIR
@@ -459,10 +474,8 @@
 
     @pl.when(outer)
     def _():
-        tags = last[:, width:].astype(jnp.float32)
-        tag_out[...] = tag_ref[...]
-        tag_out[first_row : first_row + PAIR, :] = tags
-        rows = last[:, :width]
+        tags = tag_ref[first_row : first_row + PAIR, :]
+        rows = last[...]
         for e in range(groups):
             total = jnp.zeros((PAIR, LANES), jnp.float32)
             for first in range(0, plan.padded, LANES):
@@ -480,7 +493,6 @@
 
     @pl.when(inner)
     def _():
-        tag_out[...] = tag_ref[...]
         if plan.last_piece is None:
             for e in range(groups):
                 lows[e][...] = before[e][...]
@@ -489,16 +501,18 @@
         first = at // LANES * LANES
         count = min(PAIR, plan.left_rows - at)
         parts = [jnp.zeros((at - first, width), last.dtype)] if at > first else []
-        left = padded(parts + [last[:count, :width]], LANES)
+        left = padded(parts + [last[:count, :]], LANES)
         for e in range(groups):
             if e == 0:
-                blocks = {d: near[i][PAIR:] for i, d in enumerate(plan.near)}
-                blocks.update({d: wide[i][PAIR:] for i, d in enumerate(plan.cross)})
+                blocks = {d: near[i].at[PAIR:] for i, d in enumerate(plan.near)}
+                blocks.update({d: wide[i].at[PAIR:] for i, d in enumerate(plan.cross)})
+                tags = tag_ref[...]
             else:
-                blocks = {d: across[e - 1][i][...] for i, d in enumerate(plan.across)}
-            whole = jnp.concatenate([blocks[d] for d in range(plan.half)], axis=0)
-            product = product_of(whole[:, :width], left)
-            tags = whole[:, width:].astype(jnp.float32)
+                blocks = {d: across[e - 1][i] for i, d in enumerate(plan.across)}
+                tags = [blocks[d][:, width:] for d in range(plan.half)]
+                tags = jnp.concatenate(tags, axis=0).astype(jnp.float32)
+            whole = jnp.concatenate([blocks[d][:, :width] for d in range(plan.half)], axis=0)
+            product = product_of(whole, left)
             mask = slot_mask(tags, first, plan.left_rows, plan.slots, plan.share)
             low = pack(jnp.where(mask, product, 0.0), plan.share)
             lows[e][...] = before[e][...] + low
@@ -512,17 +526,16 @@
         nested = jax.tree.unflatten(tree, refs[n_head : n_head + len(flat)])
         reduce_last_kernel(plan, *refs[:n_head], *nested, *refs[n_head + len(flat) :])
 
-    shapes = [jax.ShapeDtypeStruct(a.shape, a.dtype) for a in (*lows, tag)]
-    *lows, tag = pl.pallas_call(
+    shapes = [jax.ShapeDtypeStruct(a.shape, a.dtype) for a in lows]
+    return pl.pallas_call(
         body,
         out_shape=shapes,
         in_specs=[VMEM] * (n_head + len(flat)),
-        out_specs=[VMEM] * n_head,
+        out_specs=[VMEM] * len(lows),
         compiler_params=params(),
         cost_estimate=pl.CostEstimate(flops=1, bytes_accessed=1, transcendentals=0),
         name="reduce_last",
     )(*lows, tag, *flat)
-    return lows, tag
 
 
 def blocks_call(kernel, blocks, out_shape, out_specs, scratch, flops, moved, name, extra=()):
@@ -546,14 +559,14 @@
     )(*extra, *flat)
 
 
-def reduce_own(plan, near, wide, narrow, own):
+def reduce_own(plan, near, wide, late, tags, own):
     height = plan.half * PAIR
     columns = own.shape[0]
     n_steps = 2
     dtype = own.dtype
     return blocks_call(
         functools.partial(reduce_own_kernel, plan, n_steps),
-        [near, wide, narrow, own],
+        [near, wide, late, tags, own],
         [
             jax.ShapeDtypeStruct((height * plan.rank // LANES, LANES), jnp.float32),
             jax.ShapeDtypeStruct((height, LANES), jnp.float32),
@@ -572,14 +585,14 @@
     )
 
 
-def reduce_taken(plan, near, wide, narrow, across):
+def reduce_taken(plan, near, wide, late, tags, across):
     height = plan.half * PAIR
     n_steps = 2
     dtype = near[0].dtype
     groups, padded = plan.groups, plan.padded
     *lows, tag = blocks_call(
         functools.partial(reduce_taken_kernel, plan, n_steps),
-        [near, wide, narrow, across],
+        [near, wide, late, tags, across],
         [jax.ShapeDtypeStruct((height * plan.share // LANES, LANES), jnp.float32)] * groups
         + [jax.ShapeDtypeStruct((height, LANES), jnp.float32)],
         [VMEM] * (groups + 1),
@@ -761,6 +774,7 @@
     outer = am_outer(plan)
     left_rows = jnp.swapaxes(lefts, 1, 2)
     near, wide, seg_of = lay_out(plan, True, ids, residency, x, left_rows, ups)
+    wide, tags = wide[: plan.wide], wide[plan.wide :]
 
     near = [swap(block, "replica", d) for block, d in zip(near, plan.near[1:])]
     wide_in = []
@@ -784,20 +798,26 @@
 
     def across_send(i):
         d = plan.across[i]
-        block = near[plan.near.index(d)] if d in plan.near else wide_in[plan.cross.index(d)]
-        value = block[PAIR:]
+        if d in plan.near:
+            block = near[plan.near.index(d)][PAIR:]
+            value, tag = block[:, :width], block[:, width:]
+        else:
+            j = plan.cross.index(d)
+            value, tag = wide_in[j][PAIR:], tags_in[j][PAIR:]
         if i < plan.pieces:
             piece = wide_in[i // 2][(i % 2) * PAIR : (i % 2 + 1) * PAIR]
             value = jnp.where(outer, piece, value)
+        value = jnp.concatenate([value, tag], axis=1)
         return [
             send(plan, value, [(plan.outer, e, 0, 0), (plan.inner, e, 0, 0)])
             for e in range(1, plan.groups)
         ]
 
     across = [across_send(0)]
-
-    wide_in, near, across, late, base_other, base_mine = lax.optimization_barrier(
-        (wide_in, near, across, late, base_other, base_mine)
+    tags_in = [swap(tag, "replica", d) for tag, d in zip(tags, plan.cross)]
+
+    wide_in, near, across, late, tags_in, base_other, base_mine = lax.optimization_barrier(
+        (wide_in, near, across, late, tags_in, base_other, base_mine)
     )
     across += [across_send(i) for i in range(1, half)]
     late_in = []
@@ -808,23 +828,23 @@
         if unit == plan.units - 1:
             late_in[0], block = lax.optimization_barrier((late_in[0], block))
         late_in.append(send(plan, block, moves))
-    late_up = late_in[0][: plan.up_rows, :width]
+    late_up = late_in[0][: plan.up_rows]
     across_up = [send(plan, late_up, [(plan.inner, e, 0, 0)]) for e in range(1, plan.groups)]
     base = base_mine + swap(base_other, "tensor", 1)
     late_in[:-1], across[:-1] = lax.optimization_barrier((late_in[:-1], across[:-1]))
     across = [[blocks[e] for blocks in across] for e in range(plan.groups - 1)]
 
     own_left = left_rows.reshape(slots * rank, width)
-    low, tag = reduce_own(plan, near, wide_in, late_in[:-1], own_left)
+    low, tag = reduce_own(plan, near, wide_in, late_in[:-1], tags_in, own_left)
     other = swap(low, "tensor", 1)
     terms = expand_own(plan, low, other, tag, ups.reshape(slots * rank, features))
     deltas = [terms[0]] + return_terms(terms)
 
-    lows, tag = reduce_taken(plan, near, wide_in, late_in[:-1], across)
+    lows, tag = reduce_taken(plan, near, wide_in, late_in[:-1], tags_in, across)
     late_in[-1], deltas[:2], across_up, base, lows = lax.optimization_barrier(
         (late_in[-1], deltas[:2], across_up, base, lows)
     )
-    lows, tag = reduce_last(plan, lows, tag, near, wide_in, late_in[-1], across)
+    lows = reduce_last(plan, lows, tag, near, wide_in, late_in[-1], across)
     pairs = [lows[0], swap(lows[0], "tensor", 1)]
     for e in range(1, plan.groups):
         pairs.append(send(plan, lows[e], [(plan.outer, 0, 0, 0), (plan.inner, e, 0, 0)]))

time: 128 us -> 128 us (level)
  waiting for transfers between devices: 64.2 us -> 60.6 us
  starting transfers between devices: 30.3 us -> 32.9 us
    ppermute x12, waiting for transfers between devices: 40.8 us -> 32.5 us  [send(): return lax.ppermute(value, ('groups', 'replica', 'tensor'), pairs)]
    ppermute x10 -> x12, waiting for transfers between devices: 23.4 us -> 28.1 us  [swap(): return lax.ppermute(value, axis, [(i, i ^ distance) for i in range(count)])]
    ppermute x10 -> x12, starting transfers between devices: 14.7 us -> 16.2 us  [swap(): return lax.ppermute(value, axis, [(i, i ^ distance) for i in range(count)])]
  transfers between devices with their start and end apart: 22 -> 24, of which waited for: 13 -> 12; matrix products, arithmetic and copies ran while one was open for 11% -> 11% of each run, Pallas kernels for 9% -> 9%
where the time goes in v13:
time: 128 us; the launch traced here: 127 us
  waiting for transfers between devices  60.6 us (47%)
  starting transfers between devices  32.9 us (26%)
  Pallas kernels  19 us (15%)
  matrix products  13.7 us (11%)
    ppermute x12, waiting for transfers between devices, send(): return lax.ppermute(value, ('groups', 'replica', 'tensor'), pairs)  32.5 us
    ppermute x12, waiting for transfers between devices, swap(): return lax.ppermute(value, axis, [(i, i ^ distance) for i in range(count)])  28.1 us
    ppermute x12, starting transfers between devices, send(): return lax.ppermute(value, ('groups', 'replica', 'tensor'), pairs)  16.7 us
    ppermute x12, starting transfers between devices, swap(): return lax.ppermute(value, axis, [(i, i ^ distance) for i in range(count)])  16.2 us
    dot_general x2, matrix products, part(): return jnp.dot(rows, columns, preferred_element_type=jnp.float32)  13.7 us
    pallas_call x2, Pallas kernels, lay_out(): pl.pallas_call(functools.partial(lay_kernel, plan, first_call), out_shape...  9.73 us
    pallas_call x4, Pallas kernels, blocks_call(): pl.pallas_call(body, out_shape=out_shape, in_specs=[VMEM] * n_extra + [HB...  6.2 us
  transfers between devices with their start and end apart: 24, of which 12 were waited for; matrix products, arithmetic and copies ran while one was open for 11% of the time, Pallas kernels for 9%

profile of v13, /device:TPU:0, one launch (start us, length us, event | category | flops | bytes accessed | tf_op | source)
XLA Modules:
  0.0 127.4 jit_solution(5464425204124147508)
XLA Ops:
  0.0 4.6 %lay_out_first.1 = (bf16[128,4224]{1,0:T(8,128)(2,1)}, bf16[128,4096]{1,0:T(8,128)(2,1)}, bf16[128,4096]{1,0:T(8,128)(2,1)}, bf16[128,128]{1,0:T(8,128)(2,1)}, bf16[128,128]{1,0:T(8,128)(2,1)}, /*index=5*/s32[16]{0:T(128)}) custom-call(s32[16]{0:T(128)} %ids_ref.2, s32[48]{0:T(128)} %residency_ref.3, bf16[512,4096]{1,0:T(8,128)(2,1)} %x_ref.3, ...), custom_call_target="tpu_custom_call" | custom-call | bytes 2097152 | tf_op jit(solution)/shard_map/lay_out_first/pallas_call | solution.py:234
  4.6 3.0 %collective-permute-start.2 = (bf16[128,4224]{1,0:T(8,128)(2,1)}, bf16[128,4224]{1,0:T(8,128)(2,1)S(1)}, u32[]{:S(2)}, u32[]{:S(2)}) collective-permute-start(bf16[128,4224]{1,0:T(8,128)(2,1)} %get-tuple-element.72), channel_id=1, source_target_pairs={{0,2},{2,0},{4,6},{6,4},{8,10},{10,8},{12,14},{14,12},{1,3},{3,1},... | collective-permute-start | bytes 3244040 | tf_op jit(solution)/shard_map/ppermute | solution.py:742
  7.7 2.1 %collective-permute-start = (bf16[128,4096]{1,0:T(8,128)(2,1)}, bf16[128,4096]{1,0:T(8,128)(2,1)S(1)}, u32[]{:S(2)}, u32[]{:S(2)}) collective-permute-start(bf16[128,4096]{1,0:T(8,128)(2,1)} %get-tuple-element.68), channel_id=1, source_target_pairs={{0,4},{1,5},{2,6},{3,7},{12,8},{13,9},{14,10},{15,11},{16,20},{17,... | collective-permute-start | bytes 3145736 | tf_op jit(solution)/shard_map/ppermute | solution.py:758
  9.7 2.1 %collective-permute-start.4 = (bf16[128,128]{1,0:T(8,128)(2,1)}, bf16[128,128]{1,0:T(8,128)(2,1)S(1)}, u32[]{:S(2)}, u32[]{:S(2)}) collective-permute-start(bf16[128,128]{1,0:T(8,128)(2,1)} %get-tuple-element.77), channel_id=1, source_target_pairs={{0,4},{2,6},{4,0},{6,2},{8,12},{10,14},{12,8},{14,10},{1,5},{3,7},... | collective-permute-start | bytes 98312 | tf_op jit(solution)/shard_map/ppermute | solution.py:742
  11.8 2.9 %collective-permute-start.1 = (bf16[128,4096]{1,0:T(8,128)(2,1)}, bf16[128,4096]{1,0:T(8,128)(2,1)S(1)}, u32[]{:S(2)}, u32[]{:S(2)}) collective-permute-start(bf16[128,4096]{1,0:T(8,128)(2,1)} %get-tuple-element.69), channel_id=1, source_target_pairs={{0,6},{1,7},{2,4},{3,5},{12,10},{13,11},{14,8},{15,9},{16,22},{17,... | collective-permute-start | bytes 3145736 | tf_op jit(solution)/shard_map/ppermute | solution.py:758
  14.8 5.1 %lay_out_second.1 = (bf16[128,4224]{1,0:T(8,128)(2,1)}, bf16[64,4096]{1,0:T(8,128)(2,1)}, bf16[128,4096]{1,0:T(8,128)(2,1)}, bf16[64,4096]{1,0:T(8,128)(2,1)}, s32[16]{0:T(128)}) custom-call(s32[16]{0:T(128)} %ids_ref.2, s32[48]{0:T(128)} %residency_ref.3, bf16[512,4096]{1,0:T(8,128)(2,1)} %x_ref.3, bf16[6,64,4096]{2,1,0:T(8,128)(2,1)} %bitcast.7, ...), custom_call_target="tpu_custom_call" | custom-call | bytes 2097152 | tf_op jit(solution)/shard_map/lay_out_second/pallas_call | solution.py:234
  19.9 11.8 %collective-permute-done.2.refs_1_.refs_4_ = bf16[128,4224]{1,0:T(8,128)(2,1)S(1)} collective-permute-done((bf16[128,4224]{1,0:T(8,128)(2,1)}, bf16[128,4224]{1,0:T(8,128)(2,1)S(1)}, u32[]{:S(2)}, u32[]{:S(2)}) %collective-permute-start.2) | collective-permute-done | bytes 1081376 | tf_op jit(solution)/shard_map/ppermute | solution.py:742
  31.7 3.3 %collective-permute-done.refs_2_.refs_5_ = bf16[128,4096]{1,0:T(8,128)(2,1)S(1)} collective-permute-done((bf16[128,4096]{1,0:T(8,128)(2,1)}, bf16[128,4096]{1,0:T(8,128)(2,1)S(1)}, u32[]{:S(2)}, u32[]{:S(2)}) %collective-permute-start) | collective-permute-done | bytes 1048608 | tf_op jit(solution)/shard_map/ppermute | solution.py:758
  36.8 9.1 %fusion = f32[512,1024]{1,0:T(8,128)S(1)} fusion(bf16[512,4096]{1,0:T(8,128)(2,1)} %x_ref.3, bf16[4096,2048]{1,0:T(8,128)(2,1)} %param.7, s32[]{:T(128)S(6)} %select_n.27), kind=kOutput, calls=%fused_computation | convolution fusion | flops 4294967296 | bytes 14680068 | tf_op jit(solution)/shard_map/dot_general | solution.py:795
  46.0 4.5 %fusion.2 = f32[512,1024]{1,0:T(8,128)S(1)} fusion(bf16[512,4096]{1,0:T(8,128)(2,1)S(1)} %copy-done.4, bf16[4096,2048]{1,0:T(8,128)(2,1)S(1)} %bitcast.11, s32[]{:T(128)S(6)} %select_n.26), kind=kOutput, calls=%fused_computation.2 | convolution fusion | flops 4294967296 | bytes 14680068 | tf_op jit(solution)/shard_map/dot_general | solution.py:795
  50.6 6.5 %collective-permute-done.4.refs_6_ = bf16[128,128]{1,0:T(8,128)(2,1)S(1)} collective-permute-done((bf16[128,128]{1,0:T(8,128)(2,1)}, bf16[128,128]{1,0:T(8,128)(2,1)S(1)}, u32[]{:S(2)}, u32[]{:S(2)}) %collective-permute-start.4) | collective-permute-done | bytes 32800 | tf_op jit(solution)/shard_map/ppermute | solution.py:742
  57.7 1.8 %collective-permute-start.6 = (bf16[64,4096]{1,0:T(8,128)(2,1)}, bf16[64,4096]{1,0:T(8,128)(2,1)S(1)}, u32[]{:S(2)}, u32[]{:S(2)}) collective-permute-start(bf16[64,4096]{1,0:T(8,128)(2,1)} %get-tuple-element.80), channel_id=1, source_target_pairs={{4,0},{5,1},{6,2},{7,3},{8,12},{9,13},{10,14},{11,15},{20,16},{21,... | collective-permute-start | bytes 1572872 | tf_op jit(solution)/shard_map/ppermute | solution.py:758
  59.5 1.8 %collective-permute-start.8 = (bf16[128,4096]{1,0:T(8,128)(2,1)S(1)}, bf16[128,4096]{1,0:T(8,128)(2,1)S(1)}, u32[]{:S(2)}, u32[]{:S(2)}) collective-permute-start(bf16[128,4096]{1,0:T(8,128)(2,1)S(1)} %copy-done.5), channel_id=1, source_target_pairs={{4,2},{5,3},{6,0},{7,1},{8,14},{9,15},{10,12},{11,13},{20,18},{21,... | collective-permute-start | bytes 3145736 | tf_op jit(solution)/shard_map/ppermute | solution.py:758
  63.7 9.0 %collective-permute-done.6.refs_4_.refs_7_ = bf16[64,4096]{1,0:T(8,128)(2,1)S(1)} collective-permute-done((bf16[64,4096]{1,0:T(8,128)(2,1)}, bf16[64,4096]{1,0:T(8,128)(2,1)S(1)}, u32[]{:S(2)}, u32[]{:S(2)}) %collective-permute-start.6) | collective-permute-done | bytes 524320 | tf_op jit(solution)/shard_map/ppermute | solution.py:758
  74.2 2.4 %collective-permute-done.9.refs_9_ = bf16[64,4224]{1,0:T(8,128)(2,1)S(1)} collective-permute-done((bf16[64,4224]{1,0:T(8,128)(2,1)S(1)}, bf16[64,4224]{1,0:T(8,128)(2,1)S(1)}, u32[]{:S(2)}, u32[]{:S(2)}) %collective-permute-start.9) | collective-permute-done | bytes 540704 | tf_op jit(solution)/shard_map/ppermute | solution.py:758
  77.7 10.4 %collective-permute-done.10.refs_10_ = bf16[64,4224]{1,0:T(8,128)(2,1)S(1)} collective-permute-done((bf16[64,4224]{1,0:T(8,128)(2,1)S(1)}, bf16[64,4224]{1,0:T(8,128)(2,1)S(1)}, u32[]{:S(2)}, u32[]{:S(2)}) %collective-permute-start.10) | collective-permute-done | bytes 540704 | tf_op jit(solution)/shard_map/ppermute | solution.py:758
  88.9 7.3 %collective-permute-done.8.refs_5_ = bf16[128,4096]{1,0:T(8,128)(2,1)S(1)} collective-permute-done((bf16[128,4096]{1,0:T(8,128)(2,1)S(1)}, bf16[128,4096]{1,0:T(8,128)(2,1)S(1)}, u32[]{:S(2)}, u32[]{:S(2)}) %collective-permute-start.8) | collective-permute-done | bytes 1048608 | tf_op jit(solution)/shard_map/ppermute | solution.py:758
  96.2 2.0 %reduce_own.1 = (f32[128,128]{1,0:T(8,128)S(1)}, f32[256,128]{1,0:T(8,128)S(1)}) custom-call(bf16[128,4224]{1,0:T(8,128)(2,1)S(1)} %copy-done.1, bf16[128,4224]{1,0:T(8,128)(2,1)S(1)} %collective-permute-done.2.refs_1_.refs_4_, bf16[128,4096]{1,0:T(8,128)(2,1)S(1)} %collective-permute-done.refs_2_.refs_5_, ...), custom_call_target="tpu_custom_call" | custom-call | flops 1 | bytes 1 | tf_op jit(solution)/shard_map/reduce_own/pallas_call | solution.py:550
  103.7 2.7 %reduce_taken.1 = (f32[64,128]{1,0:T(8,128)S(1)}, f32[64,128]{1,0:T(8,128)S(1)}, f32[256,128]{1,0:T(8,128)S(1)}) custom-call(bf16[128,4224]{1,0:T(8,128)(2,1)S(1)} %copy-done.1, bf16[128,4224]{1,0:T(8,128)(2,1)S(1)} %collective-permute-done.2.refs_1_.refs_4_, bf16[128,4096]{1,0:T(8,128)(2,1)S(1)} %collective-permute-done.refs_2_.refs_5_, ...), custom_call_target="tpu_custom_call" | custom-call | flops 1 | bytes 1 | tf_op jit(solution)/shard_map/reduce_taken/pallas_call | solution.py:550
  109.3 2.8 %collective-permute-done.20.refs_3_ = bf16[64,1024]{1,0:T(8,128)(2,1)S(1)} collective-permute-done((bf16[64,1024]{1,0:T(8,128)(2,1)S(1)}, bf16[64,1024]{1,0:T(8,128)(2,1)S(1)}, u32[]{:S(2)}, u32[]{:S(2)}) %collective-permute-start.20) | collective-permute-done | bytes 131104 | tf_op jit(solution)/shard_map/ppermute | solution.py:742
  113.6 5.9 %collective-permute-start.22 = (bf16[64,1024]{1,0:T(8,128)(2,1)S(1)}, bf16[64,1024]{1,0:T(8,128)(2,1)S(1)}, u32[]{:S(2)}, u32[]{:S(2)}) collective-permute-start(bf16[64,1024]{1,0:T(8,128)(2,1)S(1)} %get-tuple-element.127), channel_id=1, source_target_pairs={{0,4},{2,6},{4,0},{6,2},{8,12},{10,14},{12,8},{14,10},{1,5},{3,7},... | collective-permute-start | bytes 393224 | tf_op jit(solution)/shard_map/ppermute | solution.py:742
  120.4 3.1 %collective-permute-done.22.refs_6_ = bf16[64,1024]{1,0:T(8,128)(2,1)S(1)} collective-permute-done((bf16[64,1024]{1,0:T(8,128)(2,1)S(1)}, bf16[64,1024]{1,0:T(8,128)(2,1)S(1)}, u32[]{:S(2)}, u32[]{:S(2)}) %collective-permute-start.22) | collective-permute-done | bytes 131104 | tf_op jit(solution)/shard_map/ppermute | solution.py:742
  123.5 2.0 %collective-permute-done.23.refs_7_ = bf16[64,1024]{1,0:T(8,128)(2,1)S(1)} collective-permute-done((bf16[64,1024]{1,0:T(8,128)(2,1)S(1)}, bf16[64,1024]{1,0:T(8,128)(2,1)S(1)}, u32[]{:S(2)}, u32[]{:S(2)}) %collective-permute-start.23) | collective-permute-done | bytes 131104 | tf_op jit(solution)/shard_map/ppermute | solution.py:742
  125.6 1.8 %join.1 = bf16[512,1024]{1,0:T(8,128)(2,1)} custom-call(s32[16]{0:T(128)S(1)} %copy-done.3, f32[512,1024]{1,0:T(8,128)S(1)} %add.11.base_ref, bf16[64,1024]{1,0:T(8,128)(2,1)S(1)} %get-tuple-element.116.refs_0_, bf16[64,1024]{1,0:T(8,128)(2,1)S(1)} %collective-permute-done.12.refs_1_, bf16[64,1024]{1,0:T(8,128)(2,1)S(1)} %collective-permute-done.19.refs_2_, ...), custom_call_target="tpu_custom_call" | custom-call | flops 524288 | bytes 4194304 | tf_op jit(solution)/shard_map/join/pallas_call | solution.py:727
  (69 shorter events, 18.7 us)
Async XLA Ops:
  4.6 27.1 %collective-permute-start.2 = (bf16[128,4224]{1,0:T(8,128)(2,1)}, bf16[128,4224]{1,0:T(8,128)(2,1)S(1)}, u32[]{:S(2)}, u32[]{:S(2)}) collective-permute-start(bf16[128,4224]{1,0:T(8,128)(2,1)} %get-tuple-element.72), channel_id=1, source_target_pairs={{0,2},{2,0},{4,6},{6,4},{8,10},{10,8},{12,14},{14,12},{1,3},{3,1},... | collective-permute-start | bytes 3244040 | tf_op jit(solution)/shard_map/ppermute | solution.py:742
  7.7 27.4 %collective-permute-start = (bf16[128,4096]{1,0:T(8,128)(2,1)}, bf16[128,4096]{1,0:T(8,128)(2,1)S(1)}, u32[]{:S(2)}, u32[]{:S(2)}) collective-permute-start(bf16[128,4096]{1,0:T(8,128)(2,1)} %get-tuple-element.68), channel_id=1, source_target_pairs={{0,4},{1,5},{2,6},{3,7},{12,8},{13,9},{14,10},{15,11},{16,20},{17,... | collective-permute-start | bytes 3145736 | tf_op jit(solution)/shard_map/ppermute | solution.py:758
  9.7 47.4 %collective-permute-start.4 = (bf16[128,128]{1,0:T(8,128)(2,1)}, bf16[128,128]{1,0:T(8,128)(2,1)S(1)}, u32[]{:S(2)}, u32[]{:S(2)}) collective-permute-start(bf16[128,128]{1,0:T(8,128)(2,1)} %get-tuple-element.77), channel_id=1, source_target_pairs={{0,4},{2,6},{4,0},{6,2},{8,12},{10,14},{12,8},{14,10},{1,5},{3,7},... | collective-permute-start | bytes 98312 | tf_op jit(solution)/shard_map/ppermute | solution.py:742
  11.8 45.8 %collective-permute-start.5 = (bf16[128,128]{1,0:T(8,128)(2,1)}, bf16[128,128]{1,0:T(8,128)(2,1)S(1)}, u32[]{:S(2)}, u32[]{:S(2)}) collective-permute-start(bf16[128,128]{1,0:T(8,128)(2,1)} %get-tuple-element.78), channel_id=1, source_target_pairs={{0,6},{2,4},{4,2},{6,0},{8,14},{10,12},{12,10},{14,8},{1,7},{3,5},... | collective-permute-start | bytes 98312 | tf_op jit(solution)/shard_map/ppermute | solution.py:742
  11.8 45.8 %collective-permute-start.1 = (bf16[128,4096]{1,0:T(8,128)(2,1)}, bf16[128,4096]{1,0:T(8,128)(2,1)S(1)}, u32[]{:S(2)}, u32[]{:S(2)}) collective-permute-start(bf16[128,4096]{1,0:T(8,128)(2,1)} %get-tuple-element.69), channel_id=1, source_target_pairs={{0,6},{1,7},{2,4},{3,5},{12,10},{13,11},{14,8},{15,9},{16,22},{17,... | collective-permute-start | bytes 3145736 | tf_op jit(solution)/shard_map/ppermute | solution.py:758
  35.2 22.4 %collective-permute-start.3 = (bf16[64,4224]{1,0:T(8,128)(2,1)S(1)}, bf16[64,4224]{1,0:T(8,128)(2,1)S(1)}, u32[]{:S(2)}, u32[]{:S(2)}) collective-permute-start(bf16[64,4224]{1,0:T(8,128)(2,1)S(1)} %pad_maximum_fusion), channel_id=1, source_target_pairs={{0,16},{1,17},{2,18},{3,19},{12,28},{13,29},{14,30},{15,31},{16,0}... | collective-permute-start | bytes 1622024 | tf_op jit(solution)/shard_map/ppermute | solution.py:758
  57.7 15.0 %collective-permute-start.6 = (bf16[64,4096]{1,0:T(8,128)(2,1)}, bf16[64,4096]{1,0:T(8,128)(2,1)S(1)}, u32[]{:S(2)}, u32[]{:S(2)}) collective-permute-start(bf16[64,4096]{1,0:T(8,128)(2,1)} %get-tuple-element.80), channel_id=1, source_target_pairs={{4,0},{5,1},{6,2},{7,3},{8,12},{9,13},{10,14},{11,15},{20,16},{21,... | collective-permute-start | bytes 1572872 | tf_op jit(solution)/shard_map/ppermute | solution.py:758
  59.5 36.7 %collective-permute-start.8 = (bf16[128,4096]{1,0:T(8,128)(2,1)S(1)}, bf16[128,4096]{1,0:T(8,128)(2,1)S(1)}, u32[]{:S(2)}, u32[]{:S(2)}) collective-permute-start(bf16[128,4096]{1,0:T(8,128)(2,1)S(1)} %copy-done.5), channel_id=1, source_target_pairs={{4,2},{5,3},{6,0},{7,1},{8,14},{9,15},{10,12},{11,13},{20,18},{21,... | collective-permute-start | bytes 3145736 | tf_op jit(solution)/shard_map/ppermute | solution.py:758
  61.2 41.2 %collective-permute-start.14 = (f32[512,1024]{1,0:T(8,128)S(1)}, f32[512,1024]{1,0:T(8,128)S(1)}, u32[]{:S(2)}, u32[]{:S(2)}) collective-permute-start(f32[512,1024]{1,0:T(8,128)S(1)} %fusion.2), channel_id=1, source_target_pairs={{0,1},{1,0},{2,3},{3,2},{4,5},{5,4},{6,7},{7,6},{8,9},{9,8},{10,11... | collective-permute-start | bytes 6291464 | tf_op jit(solution)/shard_map/ppermute | solution.py:742
  61.5 15.1 %collective-permute-start.9 = (bf16[64,4224]{1,0:T(8,128)(2,1)S(1)}, bf16[64,4224]{1,0:T(8,128)(2,1)S(1)}, u32[]{:S(2)}, u32[]{:S(2)}) collective-permute-start(bf16[64,4224]{1,0:T(8,128)(2,1)S(1)} %pad_maximum_fusion.1), channel_id=1, source_target_pairs={{0,16},{1,17},{2,18},{3,19},{12,28},{13,29},{14,30},{15,31},{16,0}... | collective-permute-start | bytes 1622024 | tf_op jit(solution)/shard_map/ppermute | solution.py:758
  63.1 25.1 %collective-permute-start.10 = (bf16[64,4224]{1,0:T(8,128)(2,1)S(1)}, bf16[64,4224]{1,0:T(8,128)(2,1)S(1)}, u32[]{:S(2)}, u32[]{:S(2)}) collective-permute-start(bf16[64,4224]{1,0:T(8,128)(2,1)S(1)} %pad_maximum_fusion.2), channel_id=1, source_target_pairs={{0,16},{1,17},{2,18},{3,19},{12,28},{13,29},{14,30},{15,31},{16,0}... | collective-permute-start | bytes 1622024 | tf_op jit(solution)/shard_map/ppermute | solution.py:758
  72.7 28.0 %collective-permute-start.15 = (bf16[64,4224]{1,0:T(8,128)(2,1)S(1)}, bf16[64,4224]{1,0:T(8,128)(2,1)S(1)}, u32[]{:S(2)}, u32[]{:S(2)}) collective-permute-start(bf16[64,4224]{1,0:T(8,128)(2,1)S(1)} %pad_maximum_fusion.3), channel_id=1, source_target_pairs={{0,16},{1,17},{2,18},{3,19},{12,28},{13,29},{14,30},{15,31},{16,0}... | collective-permute-start | bytes 1622024 | tf_op jit(solution)/shard_map/ppermute | solution.py:758
  76.6 30.2 %collective-permute-start.7 = (bf16[64,4096]{1,0:T(8,128)(2,1)S(1)}, bf16[64,4096]{1,0:T(8,128)(2,1)S(1)}, u32[]{:S(2)}, u32[]{:S(2)}) collective-permute-start(bf16[64,4096]{1,0:T(8,128)(2,1)S(1)} %copy-done.6), channel_id=1, source_target_pairs={{4,0},{5,1},{6,2},{7,3},{8,12},{9,13},{10,14},{11,15},{20,16},{21,... | collective-permute-start | bytes 1572872 | tf_op jit(solution)/shard_map/ppermute | solution.py:758
  88.2 18.6 %collective-permute-start.13 = (bf16[48,4096]{1,0:T(8,128)(2,1)S(1)}, bf16[48,4096]{1,0:T(8,128)(2,1)S(1)}, u32[]{:S(2)}, u32[]{:S(2)}) collective-permute-start(bf16[48,4096]{1,0:T(8,128)(2,1)S(1)} %slice.49), channel_id=1, source_target_pairs={{4,20},{5,21},{6,22},{7,23},{8,24},{9,25},{10,26},{11,27},{20,4},{... | collective-permute-start | bytes 1179656 | tf_op jit(solution)/shard_map/ppermute | solution.py:758
  98.2 1.3 %collective-permute-start.11 = (f32[128,128]{1,0:T(8,128)S(1)}, f32[128,128]{1,0:T(8,128)S(1)}, u32[]{:S(2)}, u32[]{:S(2)}) collective-permute-start(f32[128,128]{1,0:T(8,128)S(1)} %get-tuple-element.94.refs_0_), channel_id=1, source_target_pairs={{0,1},{1,0},{2,3},{3,2},{4,5},{5,4},{6,7},{7,6},{8,9},{9,8},{10,11... | collective-permute-start | bytes 196616 | tf_op jit(solution)/shard_map/ppermute | solution.py:742
  100.1 6.7 %collective-permute-start.12 = (bf16[64,1024]{1,0:T(8,128)(2,1)S(1)}, bf16[64,1024]{1,0:T(8,128)(2,1)S(1)}, u32[]{:S(2)}, u32[]{:S(2)}) collective-permute-start(bf16[64,1024]{1,0:T(8,128)(2,1)S(1)} %get-tuple-element.97), channel_id=1, source_target_pairs={{0,2},{2,0},{4,6},{6,4},{8,10},{10,8},{12,14},{14,12},{1,3},{3,1},... | collective-permute-start | bytes 393224 | tf_op jit(solution)/shard_map/ppermute | solution.py:742
  100.7 8.6 %collective-permute-start.19 = (bf16[64,1024]{1,0:T(8,128)(2,1)S(1)}, bf16[64,1024]{1,0:T(8,128)(2,1)S(1)}, u32[]{:S(2)}, u32[]{:S(2)}) collective-permute-start(bf16[64,1024]{1,0:T(8,128)(2,1)S(1)} %get-tuple-element.114), channel_id=1, source_target_pairs={{0,4},{2,6},{4,0},{6,2},{8,12},{10,14},{12,8},{14,10},{1,5},{3,7},... | collective-permute-start | bytes 393224 | tf_op jit(solution)/shard_map/ppermute | solution.py:742
  102.4 9.7 %collective-permute-start.20 = (bf16[64,1024]{1,0:T(8,128)(2,1)S(1)}, bf16[64,1024]{1,0:T(8,128)(2,1)S(1)}, u32[]{:S(2)}, u32[]{:S(2)}) collective-permute-start(bf16[64,1024]{1,0:T(8,128)(2,1)S(1)} %get-tuple-element.115), channel_id=1, source_target_pairs={{0,6},{2,4},{4,2},{6,0},{8,14},{10,12},{12,10},{14,8},{1,7},{3,5},... | collective-permute-start | bytes 393224 | tf_op jit(solution)/shard_map/ppermute | solution.py:742
  108.0 4.1 %collective-permute-start.16 = (f32[64,128]{1,0:T(8,128)S(1)}, f32[64,128]{1,0:T(8,128)S(1)}, u32[]{:S(2)}, u32[]{:S(2)}) collective-permute-start(f32[64,128]{1,0:T(8,128)S(1)} %get-tuple-element.120.refs_0_), channel_id=1, source_target_pairs={{0,1},{1,0},{2,3},{3,2},{4,5},{5,4},{6,7},{7,6},{8,9},{9,8},{10,11... | collective-permute-start | bytes 98312 | tf_op jit(solution)/shard_map/ppermute | solution.py:742
  108.1 4.0 %collective-permute-start.18 = (f32[64,128]{1,0:T(8,128)S(1)}, f32[64,128]{1,0:T(8,128)S(1)}, u32[]{:S(2)}, u32[]{:S(2)}) collective-permute-start(f32[64,128]{1,0:T(8,128)S(1)} %get-tuple-element.111), channel_id=1, source_target_pairs={{0,1},{1,0},{2,3},{3,2},{12,13},{13,12},{14,15},{15,14},{16,17},{1... | collective-permute-start | bytes 98312 | tf_op jit(solution)/shard_map/ppermute | solution.py:758
  108.6 3.5 %collective-permute-start.17 = (f32[64,128]{1,0:T(8,128)S(1)}, f32[64,128]{1,0:T(8,128)S(1)}, u32[]{:S(2)}, u32[]{:S(2)}) collective-permute-start(f32[64,128]{1,0:T(8,128)S(1)} %get-tuple-element.111), channel_id=1, source_target_pairs={{0,0},{1,1},{2,2},{3,3},{12,12},{13,13},{14,14},{15,15},{16,16},{1... | collective-permute-start | bytes 98312 | tf_op jit(solution)/shard_map/ppermute | solution.py:758
  113.0 7.4 %collective-permute-start.21 = (bf16[64,1024]{1,0:T(8,128)(2,1)S(1)}, bf16[64,1024]{1,0:T(8,128)(2,1)S(1)}, u32[]{:S(2)}, u32[]{:S(2)}) collective-permute-start(bf16[64,1024]{1,0:T(8,128)(2,1)S(1)} %get-tuple-element.126), channel_id=1, source_target_pairs={{0,2},{2,0},{4,6},{6,4},{8,10},{10,8},{12,14},{14,12},{1,3},{3,1},... | collective-permute-start | bytes 393224 | tf_op jit(solution)/shard_map/ppermute | solution.py:742
  113.6 9.9 %collective-permute-start.22 = (bf16[64,1024]{1,0:T(8,128)(2,1)S(1)}, bf16[64,1024]{1,0:T(8,128)(2,1)S(1)}, u32[]{:S(2)}, u32[]{:S(2)}) collective-permute-start(bf16[64,1024]{1,0:T(8,128)(2,1)S(1)} %get-tuple-element.127), channel_id=1, source_target_pairs={{0,4},{2,6},{4,0},{6,2},{8,12},{10,14},{12,8},{14,10},{1,5},{3,7},... | collective-permute-start | bytes 393224 | tf_op jit(solution)/shard_map/ppermute | solution.py:742
  119.5 6.1 %collective-permute-start.23 = (bf16[64,1024]{1,0:T(8,128)(2,1)S(1)}, bf16[64,1024]{1,0:T(8,128)(2,1)S(1)}, u32[]{:S(2)}, u32[]{:S(2)}) collective-permute-start(bf16[64,1024]{1,0:T(8,128)(2,1)S(1)} %get-tuple-element.128), channel_id=1, source_target_pairs={{0,6},{2,4},{4,2},{6,0},{8,14},{10,12},{12,10},{14,8},{1,7},{3,5},... | collective-permute-start | bytes 393224 | tf_op jit(solution)/shard_map/ppermute | solution.py:742
  (11 other events, 150.0 us)

commit v14 on v13

--- a/solution.py
+++ b/solution.py
@@ -841,14 +841,16 @@
     deltas = [terms[0]] + return_terms(terms)
 
     lows, tag = reduce_taken(plan, near, wide_in, late_in[:-1], tags_in, across)
-    late_in[-1], deltas[:2], across_up, base, lows = lax.optimization_barrier(
-        (late_in[-1], deltas[:2], across_up, base, lows)
+    late_in[-1], deltas[:2], base, lows = lax.optimization_barrier(
+        (late_in[-1], deltas[:2], base, lows)
     )
     lows = reduce_last(plan, lows, tag, near, wide_in, late_in[-1], across)
-    pairs = [lows[0], swap(lows[0], "tensor", 1)]
-    for e in range(1, plan.groups):
-        pairs.append(send(plan, lows[e], [(plan.outer, 0, 0, 0), (plan.inner, e, 0, 0)]))
-        pairs.append(send(plan, lows[e], [(plan.outer, 0, 0, 1), (plan.inner, e, 0, 1)]))
+    pairs = []
+    for e in range(plan.groups):
+        low = lows[e]
+        if e:
+            low = send(plan, low, [(plan.outer, 0, 0, 0), (plan.inner, e, 0, 0)])
+        pairs += [low, swap(low, "tensor", 1)]
     pairs, deltas = lax.optimization_barrier((pairs, deltas))
     across_wide = [blocks[plan.left_pieces] for blocks in across]
     terms = expand_taken(plan, pairs, tag, wide_in, late_in[0], across_wide, across_up)

time: 128 us -> 127 us (level)
  starting transfers between devices: 32.9 us -> 31.5 us
    ppermute x12 -> x13, waiting for transfers between devices: 28.1 us -> 29.3 us  [swap(): return lax.ppermute(value, axis, [(i, i ^ distance) for i in range(count)])]
    ppermute x12 -> x13, starting transfers between devices: 16.2 us -> 15.3 us  [swap(): return lax.ppermute(value, axis, [(i, i ^ distance) for i in range(count)])]
    ppermute x12 -> x11, starting transfers between devices: 16.7 us -> 16.2 us  [send(): return lax.ppermute(value, ('groups', 'replica', 'tensor'), pairs)]
    ppermute x12 -> x11, waiting for transfers between devices: 32.5 us -> 32.5 us  [send(): return lax.ppermute(value, ('groups', 'replica', 'tensor'), pairs)]
where the time goes in v14:
time: 127 us
  waiting for transfers between devices  61.8 us (49%)
  starting transfers between devices  31.5 us (25%)
  Pallas kernels  18.9 us (15%)
  matrix products  13.7 us (11%)
    ppermute x11, waiting for transfers between devices, send(): return lax.ppermute(value, ('groups', 'replica', 'tensor'), pairs)  32.5 us
    ppermute x13, waiting for transfers between devices, swap(): return lax.ppermute(value, axis, [(i, i ^ distance) for i in range(count)])  29.3 us
    ppermute x11, starting transfers between devices, send(): return lax.ppermute(value, ('groups', 'replica', 'tensor'), pairs)  16.2 us
    ppermute x13, starting transfers between devices, swap(): return lax.ppermute(value, axis, [(i, i ^ distance) for i in range(count)])  15.3 us
    dot_general x2, matrix products, part(): return jnp.dot(rows, columns, preferred_element_type=jnp.float32)  13.7 us
    pallas_call x2, Pallas kernels, lay_out(): pl.pallas_call(functools.partial(lay_kernel, plan, first_call), out_shape...  9.73 us
    pallas_call x4, Pallas kernels, blocks_call(): pl.pallas_call(body, out_shape=out_shape, in_specs=[VMEM] * n_extra + [HB...  6.2 us
  transfers between devices with their start and end apart: 24, of which 12 were waited for; matrix products, arithmetic and copies ran while one was open for 11% of the time, Pallas kernels for 9%

profile of v14, /device:TPU:0, one launch (start us, length us, event | category | flops | bytes accessed | tf_op | source)
XLA Modules:
  0.0 127.1 jit_solution(6717287076403093447)
XLA Ops:
  0.0 4.6 %lay_out_first.1 = (bf16[128,4224]{1,0:T(8,128)(2,1)}, bf16[128,4096]{1,0:T(8,128)(2,1)}, bf16[128,4096]{1,0:T(8,128)(2,1)}, bf16[128,128]{1,0:T(8,128)(2,1)}, bf16[128,128]{1,0:T(8,128)(2,1)}, /*index=5*/s32[16]{0:T(128)}) custom-call(s32[16]{0:T(128)} %ids_ref.2, s32[48]{0:T(128)} %residency_ref.3, bf16[512,4096]{1,0:T(8,128)(2,1)} %x_ref.3, ...), custom_call_target="tpu_custom_call" | custom-call | bytes 2097152 | tf_op jit(solution)/shard_map/lay_out_first/pallas_call | solution.py:234
  4.6 3.0 %collective-permute-start.2 = (bf16[128,4224]{1,0:T(8,128)(2,1)}, bf16[128,4224]{1,0:T(8,128)(2,1)S(1)}, u32[]{:S(2)}, u32[]{:S(2)}) collective-permute-start(bf16[128,4224]{1,0:T(8,128)(2,1)} %get-tuple-element.71), channel_id=1, source_target_pairs={{0,2},{2,0},{4,6},{6,4},{8,10},{10,8},{12,14},{14,12},{1,3},{3,1},... | collective-permute-start | bytes 3244040 | tf_op jit(solution)/shard_map/ppermute | solution.py:742
  7.7 2.1 %collective-permute-start = (bf16[128,4096]{1,0:T(8,128)(2,1)}, bf16[128,4096]{1,0:T(8,128)(2,1)S(1)}, u32[]{:S(2)}, u32[]{:S(2)}) collective-permute-start(bf16[128,4096]{1,0:T(8,128)(2,1)} %get-tuple-element.67), channel_id=1, source_target_pairs={{0,4},{1,5},{2,6},{3,7},{12,8},{13,9},{14,10},{15,11},{16,20},{17,... | collective-permute-start | bytes 3145736 | tf_op jit(solution)/shard_map/ppermute | solution.py:758
  9.7 2.1 %collective-permute-start.4 = (bf16[128,128]{1,0:T(8,128)(2,1)}, bf16[128,128]{1,0:T(8,128)(2,1)S(1)}, u32[]{:S(2)}, u32[]{:S(2)}) collective-permute-start(bf16[128,128]{1,0:T(8,128)(2,1)} %get-tuple-element.76), channel_id=1, source_target_pairs={{0,4},{2,6},{4,0},{6,2},{8,12},{10,14},{12,8},{14,10},{1,5},{3,7},... | collective-permute-start | bytes 98312 | tf_op jit(solution)/shard_map/ppermute | solution.py:742
  11.8 2.9 %collective-permute-start.1 = (bf16[128,4096]{1,0:T(8,128)(2,1)}, bf16[128,4096]{1,0:T(8,128)(2,1)S(1)}, u32[]{:S(2)}, u32[]{:S(2)}) collective-permute-start(bf16[128,4096]{1,0:T(8,128)(2,1)} %get-tuple-element.68), channel_id=1, source_target_pairs={{0,6},{1,7},{2,4},{3,5},{12,10},{13,11},{14,8},{15,9},{16,22},{17,... | collective-permute-start | bytes 3145736 | tf_op jit(solution)/shard_map/ppermute | solution.py:758
  14.8 5.1 %lay_out_second.1 = (bf16[128,4224]{1,0:T(8,128)(2,1)}, bf16[64,4096]{1,0:T(8,128)(2,1)}, bf16[128,4096]{1,0:T(8,128)(2,1)}, bf16[64,4096]{1,0:T(8,128)(2,1)}, s32[16]{0:T(128)}) custom-call(s32[16]{0:T(128)} %ids_ref.2, s32[48]{0:T(128)} %residency_ref.3, bf16[512,4096]{1,0:T(8,128)(2,1)} %x_ref.3, bf16[6,64,4096]{2,1,0:T(8,128)(2,1)} %bitcast.7, ...), custom_call_target="tpu_custom_call" | custom-call | bytes 2097152 | tf_op jit(solution)/shard_map/lay_out_second/pallas_call | solution.py:234
  19.9 11.8 %collective-permute-done.2.refs_1_.refs_4_ = bf16[128,4224]{1,0:T(8,128)(2,1)S(1)} collective-permute-done((bf16[128,4224]{1,0:T(8,128)(2,1)}, bf16[128,4224]{1,0:T(8,128)(2,1)S(1)}, u32[]{:S(2)}, u32[]{:S(2)}) %collective-permute-start.2) | collective-permute-done | bytes 1081376 | tf_op jit(solution)/shard_map/ppermute | solution.py:742
  31.7 3.3 %collective-permute-done.refs_2_.refs_5_ = bf16[128,4096]{1,0:T(8,128)(2,1)S(1)} collective-permute-done((bf16[128,4096]{1,0:T(8,128)(2,1)}, bf16[128,4096]{1,0:T(8,128)(2,1)S(1)}, u32[]{:S(2)}, u32[]{:S(2)}) %collective-permute-start) | collective-permute-done | bytes 1048608 | tf_op jit(solution)/shard_map/ppermute | solution.py:758
  36.8 9.1 %fusion = f32[512,1024]{1,0:T(8,128)S(1)} fusion(bf16[512,4096]{1,0:T(8,128)(2,1)} %x_ref.3, bf16[4096,2048]{1,0:T(8,128)(2,1)} %param.7, s32[]{:T(128)S(6)} %select_n.27), kind=kOutput, calls=%fused_computation | convolution fusion | flops 4294967296 | bytes 14680068 | tf_op jit(solution)/shard_map/dot_general | solution.py:795
  46.0 4.5 %fusion.2 = f32[512,1024]{1,0:T(8,128)S(1)} fusion(bf16[512,4096]{1,0:T(8,128)(2,1)S(1)} %copy-done.4, bf16[4096,2048]{1,0:T(8,128)(2,1)S(1)} %bitcast.11, s32[]{:T(128)S(6)} %select_n.26), kind=kOutput, calls=%fused_computation.2 | convolution fusion | flops 4294967296 | bytes 14680068 | tf_op jit(solution)/shard_map/dot_general | solution.py:795
  50.6 6.5 %collective-permute-done.4.refs_6_ = bf16[128,128]{1,0:T(8,128)(2,1)S(1)} collective-permute-done((bf16[128,128]{1,0:T(8,128)(2,1)}, bf16[128,128]{1,0:T(8,128)(2,1)S(1)}, u32[]{:S(2)}, u32[]{:S(2)}) %collective-permute-start.4) | collective-permute-done | bytes 32800 | tf_op jit(solution)/shard_map/ppermute | solution.py:742
  57.7 1.8 %collective-permute-start.6 = (bf16[64,4096]{1,0:T(8,128)(2,1)}, bf16[64,4096]{1,0:T(8,128)(2,1)S(1)}, u32[]{:S(2)}, u32[]{:S(2)}) collective-permute-start(bf16[64,4096]{1,0:T(8,128)(2,1)} %get-tuple-element.79), channel_id=1, source_target_pairs={{4,0},{5,1},{6,2},{7,3},{8,12},{9,13},{10,14},{11,15},{20,16},{21,... | collective-permute-start | bytes 1572872 | tf_op jit(solution)/shard_map/ppermute | solution.py:758
  59.5 1.8 %collective-permute-start.8 = (bf16[128,4096]{1,0:T(8,128)(2,1)S(1)}, bf16[128,4096]{1,0:T(8,128)(2,1)S(1)}, u32[]{:S(2)}, u32[]{:S(2)}) collective-permute-start(bf16[128,4096]{1,0:T(8,128)(2,1)S(1)} %copy-done.5), channel_id=1, source_target_pairs={{4,2},{5,3},{6,0},{7,1},{8,14},{9,15},{10,12},{11,13},{20,18},{21,... | collective-permute-start | bytes 3145736 | tf_op jit(solution)/shard_map/ppermute | solution.py:758
  63.7 9.0 %collective-permute-done.6.refs_4_.refs_7_ = bf16[64,4096]{1,0:T(8,128)(2,1)S(1)} collective-permute-done((bf16[64,4096]{1,0:T(8,128)(2,1)}, bf16[64,4096]{1,0:T(8,128)(2,1)S(1)}, u32[]{:S(2)}, u32[]{:S(2)}) %collective-permute-start.6) | collective-permute-done | bytes 524320 | tf_op jit(solution)/shard_map/ppermute | solution.py:758
  74.2 2.4 %collective-permute-done.9.refs_9_ = bf16[64,4224]{1,0:T(8,128)(2,1)S(1)} collective-permute-done((bf16[64,4224]{1,0:T(8,128)(2,1)S(1)}, bf16[64,4224]{1,0:T(8,128)(2,1)S(1)}, u32[]{:S(2)}, u32[]{:S(2)}) %collective-permute-start.9) | collective-permute-done | bytes 540704 | tf_op jit(solution)/shard_map/ppermute | solution.py:758
  77.7 10.4 %collective-permute-done.10.refs_10_ = bf16[64,4224]{1,0:T(8,128)(2,1)S(1)} collective-permute-done((bf16[64,4224]{1,0:T(8,128)(2,1)S(1)}, bf16[64,4224]{1,0:T(8,128)(2,1)S(1)}, u32[]{:S(2)}, u32[]{:S(2)}) %collective-permute-start.10) | collective-permute-done | bytes 540704 | tf_op jit(solution)/shard_map/ppermute | solution.py:758
  88.9 7.3 %collective-permute-done.8.refs_5_ = bf16[128,4096]{1,0:T(8,128)(2,1)S(1)} collective-permute-done((bf16[128,4096]{1,0:T(8,128)(2,1)S(1)}, bf16[128,4096]{1,0:T(8,128)(2,1)S(1)}, u32[]{:S(2)}, u32[]{:S(2)}) %collective-permute-start.8) | collective-permute-done | bytes 1048608 | tf_op jit(solution)/shard_map/ppermute | solution.py:758
  96.2 2.0 %reduce_own.1 = (f32[128,128]{1,0:T(8,128)S(1)}, f32[256,128]{1,0:T(8,128)S(1)}) custom-call(bf16[128,4224]{1,0:T(8,128)(2,1)S(1)} %copy-done.1, bf16[128,4224]{1,0:T(8,128)(2,1)S(1)} %collective-permute-done.2.refs_1_.refs_4_, bf16[128,4096]{1,0:T(8,128)(2,1)S(1)} %collective-permute-done.refs_2_.refs_5_, ...), custom_call_target="tpu_custom_call" | custom-call | flops 1 | bytes 1 | tf_op jit(solution)/shard_map/reduce_own/pallas_call | solution.py:550
  103.7 2.7 %reduce_taken.1 = (f32[64,128]{1,0:T(8,128)S(1)}, f32[64,128]{1,0:T(8,128)S(1)}, f32[256,128]{1,0:T(8,128)S(1)}) custom-call(bf16[128,4224]{1,0:T(8,128)(2,1)S(1)} %copy-done.1, bf16[128,4224]{1,0:T(8,128)(2,1)S(1)} %collective-permute-done.2.refs_1_.refs_4_, bf16[128,4096]{1,0:T(8,128)(2,1)S(1)} %collective-permute-done.refs_2_.refs_5_, ...), custom_call_target="tpu_custom_call" | custom-call | flops 1 | bytes 1 | tf_op jit(solution)/shard_map/reduce_taken/pallas_call | solution.py:550
  109.3 2.8 %collective-permute-done.19.refs_3_ = bf16[64,1024]{1,0:T(8,128)(2,1)S(1)} collective-permute-done((bf16[64,1024]{1,0:T(8,128)(2,1)S(1)}, bf16[64,1024]{1,0:T(8,128)(2,1)S(1)}, u32[]{:S(2)}, u32[]{:S(2)}) %collective-permute-start.19) | collective-permute-done | bytes 131104 | tf_op jit(solution)/shard_map/ppermute | solution.py:742
  113.6 5.4 %collective-permute-start.22 = (bf16[64,1024]{1,0:T(8,128)(2,1)S(1)}, bf16[64,1024]{1,0:T(8,128)(2,1)S(1)}, u32[]{:S(2)}, u32[]{:S(2)}) collective-permute-start(bf16[64,1024]{1,0:T(8,128)(2,1)S(1)} %get-tuple-element.125), channel_id=1, source_target_pairs={{0,4},{2,6},{4,0},{6,2},{8,12},{10,14},{12,8},{14,10},{1,5},{3,7},... | collective-permute-start | bytes 393224 | tf_op jit(solution)/shard_map/ppermute | solution.py:742
  119.0 4.3 %collective-permute-done.22.refs_6_ = bf16[64,1024]{1,0:T(8,128)(2,1)S(1)} collective-permute-done((bf16[64,1024]{1,0:T(8,128)(2,1)S(1)}, bf16[64,1024]{1,0:T(8,128)(2,1)S(1)}, u32[]{:S(2)}, u32[]{:S(2)}) %collective-permute-start.22) | collective-permute-done | bytes 131104 | tf_op jit(solution)/shard_map/ppermute | solution.py:742
  123.3 2.0 %collective-permute-done.23.refs_7_ = bf16[64,1024]{1,0:T(8,128)(2,1)S(1)} collective-permute-done((bf16[64,1024]{1,0:T(8,128)(2,1)S(1)}, bf16[64,1024]{1,0:T(8,128)(2,1)S(1)}, u32[]{:S(2)}, u32[]{:S(2)}) %collective-permute-start.23) | collective-permute-done | bytes 131104 | tf_op jit(solution)/shard_map/ppermute | solution.py:742
  125.3 1.8 %join.1 = bf16[512,1024]{1,0:T(8,128)(2,1)} custom-call(s32[16]{0:T(128)S(1)} %copy-done.3, f32[512,1024]{1,0:T(8,128)S(1)} %add.11.base_ref, bf16[64,1024]{1,0:T(8,128)(2,1)S(1)} %get-tuple-element.115.refs_0_, bf16[64,1024]{1,0:T(8,128)(2,1)S(1)} %collective-permute-done.12.refs_1_, bf16[64,1024]{1,0:T(8,128)(2,1)S(1)} %collective-permute-done.18.refs_2_, ...), custom_call_target="tpu_custom_call" | custom-call | flops 524288 | bytes 4194304 | tf_op jit(solution)/shard_map/join/pallas_call | solution.py:727
  (69 shorter events, 17.8 us)
Async XLA Ops:
  4.6 27.1 %collective-permute-start.2 = (bf16[128,4224]{1,0:T(8,128)(2,1)}, bf16[128,4224]{1,0:T(8,128)(2,1)S(1)}, u32[]{:S(2)}, u32[]{:S(2)}) collective-permute-start(bf16[128,4224]{1,0:T(8,128)(2,1)} %get-tuple-element.71), channel_id=1, source_target_pairs={{0,2},{2,0},{4,6},{6,4},{8,10},{10,8},{12,14},{14,12},{1,3},{3,1},... | collective-permute-start | bytes 3244040 | tf_op jit(solution)/shard_map/ppermute | solution.py:742
  7.7 27.4 %collective-permute-start = (bf16[128,4096]{1,0:T(8,128)(2,1)}, bf16[128,4096]{1,0:T(8,128)(2,1)S(1)}, u32[]{:S(2)}, u32[]{:S(2)}) collective-permute-start(bf16[128,4096]{1,0:T(8,128)(2,1)} %get-tuple-element.67), channel_id=1, source_target_pairs={{0,4},{1,5},{2,6},{3,7},{12,8},{13,9},{14,10},{15,11},{16,20},{17,... | collective-permute-start | bytes 3145736 | tf_op jit(solution)/shard_map/ppermute | solution.py:758
  9.7 47.4 %collective-permute-start.4 = (bf16[128,128]{1,0:T(8,128)(2,1)}, bf16[128,128]{1,0:T(8,128)(2,1)S(1)}, u32[]{:S(2)}, u32[]{:S(2)}) collective-permute-start(bf16[128,128]{1,0:T(8,128)(2,1)} %get-tuple-element.76), channel_id=1, source_target_pairs={{0,4},{2,6},{4,0},{6,2},{8,12},{10,14},{12,8},{14,10},{1,5},{3,7},... | collective-permute-start | bytes 98312 | tf_op jit(solution)/shard_map/ppermute | solution.py:742
  11.8 45.8 %collective-permute-start.5 = (bf16[128,128]{1,0:T(8,128)(2,1)}, bf16[128,128]{1,0:T(8,128)(2,1)S(1)}, u32[]{:S(2)}, u32[]{:S(2)}) collective-permute-start(bf16[128,128]{1,0:T(8,128)(2,1)} %get-tuple-element.77), channel_id=1, source_target_pairs={{0,6},{2,4},{4,2},{6,0},{8,14},{10,12},{12,10},{14,8},{1,7},{3,5},... | collective-permute-start | bytes 98312 | tf_op jit(solution)/shard_map/ppermute | solution.py:742
  11.8 45.8 %collective-permute-start.1 = (bf16[128,4096]{1,0:T(8,128)(2,1)}, bf16[128,4096]{1,0:T(8,128)(2,1)S(1)}, u32[]{:S(2)}, u32[]{:S(2)}) collective-permute-start(bf16[128,4096]{1,0:T(8,128)(2,1)} %get-tuple-element.68), channel_id=1, source_target_pairs={{0,6},{1,7},{2,4},{3,5},{12,10},{13,11},{14,8},{15,9},{16,22},{17,... | collective-permute-start | bytes 3145736 | tf_op jit(solution)/shard_map/ppermute | solution.py:758
  35.2 22.4 %collective-permute-start.3 = (bf16[64,4224]{1,0:T(8,128)(2,1)S(1)}, bf16[64,4224]{1,0:T(8,128)(2,1)S(1)}, u32[]{:S(2)}, u32[]{:S(2)}) collective-permute-start(bf16[64,4224]{1,0:T(8,128)(2,1)S(1)} %pad_maximum_fusion), channel_id=1, source_target_pairs={{0,16},{1,17},{2,18},{3,19},{12,28},{13,29},{14,30},{15,31},{16,0}... | collective-permute-start | bytes 1622024 | tf_op jit(solution)/shard_map/ppermute | solution.py:758
  57.7 15.0 %collective-permute-start.6 = (bf16[64,4096]{1,0:T(8,128)(2,1)}, bf16[64,4096]{1,0:T(8,128)(2,1)S(1)}, u32[]{:S(2)}, u32[]{:S(2)}) collective-permute-start(bf16[64,4096]{1,0:T(8,128)(2,1)} %get-tuple-element.79), channel_id=1, source_target_pairs={{4,0},{5,1},{6,2},{7,3},{8,12},{9,13},{10,14},{11,15},{20,16},{21,... | collective-permute-start | bytes 1572872 | tf_op jit(solution)/shard_map/ppermute | solution.py:758
  59.5 36.7 %collective-permute-start.8 = (bf16[128,4096]{1,0:T(8,128)(2,1)S(1)}, bf16[128,4096]{1,0:T(8,128)(2,1)S(1)}, u32[]{:S(2)}, u32[]{:S(2)}) collective-permute-start(bf16[128,4096]{1,0:T(8,128)(2,1)S(1)} %copy-done.5), channel_id=1, source_target_pairs={{4,2},{5,3},{6,0},{7,1},{8,14},{9,15},{10,12},{11,13},{20,18},{21,... | collective-permute-start | bytes 3145736 | tf_op jit(solution)/shard_map/ppermute | solution.py:758
  61.2 41.2 %collective-permute-start.13 = (f32[512,1024]{1,0:T(8,128)S(1)}, f32[512,1024]{1,0:T(8,128)S(1)}, u32[]{:S(2)}, u32[]{:S(2)}) collective-permute-start(f32[512,1024]{1,0:T(8,128)S(1)} %fusion.2), channel_id=1, source_target_pairs={{0,1},{1,0},{2,3},{3,2},{4,5},{5,4},{6,7},{7,6},{8,9},{9,8},{10,11... | collective-permute-start | bytes 6291464 | tf_op jit(solution)/shard_map/ppermute | solution.py:742
  61.5 15.1 %collective-permute-start.9 = (bf16[64,4224]{1,0:T(8,128)(2,1)S(1)}, bf16[64,4224]{1,0:T(8,128)(2,1)S(1)}, u32[]{:S(2)}, u32[]{:S(2)}) collective-permute-start(bf16[64,4224]{1,0:T(8,128)(2,1)S(1)} %pad_maximum_fusion.1), channel_id=1, source_target_pairs={{0,16},{1,17},{2,18},{3,19},{12,28},{13,29},{14,30},{15,31},{16,0}... | collective-permute-start | bytes 1622024 | tf_op jit(solution)/shard_map/ppermute | solution.py:758
  63.1 25.1 %collective-permute-start.10 = (bf16[64,4224]{1,0:T(8,128)(2,1)S(1)}, bf16[64,4224]{1,0:T(8,128)(2,1)S(1)}, u32[]{:S(2)}, u32[]{:S(2)}) collective-permute-start(bf16[64,4224]{1,0:T(8,128)(2,1)S(1)} %pad_maximum_fusion.2), channel_id=1, source_target_pairs={{0,16},{1,17},{2,18},{3,19},{12,28},{13,29},{14,30},{15,31},{16,0}... | collective-permute-start | bytes 1622024 | tf_op jit(solution)/shard_map/ppermute | solution.py:758
  72.7 28.0 %collective-permute-start.14 = (bf16[64,4224]{1,0:T(8,128)(2,1)S(1)}, bf16[64,4224]{1,0:T(8,128)(2,1)S(1)}, u32[]{:S(2)}, u32[]{:S(2)}) collective-permute-start(bf16[64,4224]{1,0:T(8,128)(2,1)S(1)} %pad_maximum_fusion.3), channel_id=1, source_target_pairs={{0,16},{1,17},{2,18},{3,19},{12,28},{13,29},{14,30},{15,31},{16,0}... | collective-permute-start | bytes 1622024 | tf_op jit(solution)/shard_map/ppermute | solution.py:758
  76.6 30.2 %collective-permute-start.7 = (bf16[64,4096]{1,0:T(8,128)(2,1)S(1)}, bf16[64,4096]{1,0:T(8,128)(2,1)S(1)}, u32[]{:S(2)}, u32[]{:S(2)}) collective-permute-start(bf16[64,4096]{1,0:T(8,128)(2,1)S(1)} %copy-done.6), channel_id=1, source_target_pairs={{4,0},{5,1},{6,2},{7,3},{8,12},{9,13},{10,14},{11,15},{20,16},{21,... | collective-permute-start | bytes 1572872 | tf_op jit(solution)/shard_map/ppermute | solution.py:758
  88.2 23.9 %collective-permute-start.20 = (bf16[48,4096]{1,0:T(8,128)(2,1)S(1)}, bf16[48,4096]{1,0:T(8,128)(2,1)S(1)}, u32[]{:S(2)}, u32[]{:S(2)}) collective-permute-start(bf16[48,4096]{1,0:T(8,128)(2,1)S(1)} %slice.51), channel_id=1, source_target_pairs={{4,20},{5,21},{6,22},{7,23},{8,24},{9,25},{10,26},{11,27},{20,4},{... | collective-permute-start | bytes 1179656 | tf_op jit(solution)/shard_map/ppermute | solution.py:758
  98.2 1.3 %collective-permute-start.11 = (f32[128,128]{1,0:T(8,128)S(1)}, f32[128,128]{1,0:T(8,128)S(1)}, u32[]{:S(2)}, u32[]{:S(2)}) collective-permute-start(f32[128,128]{1,0:T(8,128)S(1)} %get-tuple-element.93.refs_0_), channel_id=1, source_target_pairs={{0,1},{1,0},{2,3},{3,2},{4,5},{5,4},{6,7},{7,6},{8,9},{9,8},{10,11... | collective-permute-start | bytes 196616 | tf_op jit(solution)/shard_map/ppermute | solution.py:742
  100.1 6.7 %collective-permute-start.12 = (bf16[64,1024]{1,0:T(8,128)(2,1)S(1)}, bf16[64,1024]{1,0:T(8,128)(2,1)S(1)}, u32[]{:S(2)}, u32[]{:S(2)}) collective-permute-start(bf16[64,1024]{1,0:T(8,128)(2,1)S(1)} %get-tuple-element.96), channel_id=1, source_target_pairs={{0,2},{2,0},{4,6},{6,4},{8,10},{10,8},{12,14},{14,12},{1,3},{3,1},... | collective-permute-start | bytes 393224 | tf_op jit(solution)/shard_map/ppermute | solution.py:742
  100.7 8.6 %collective-permute-start.18 = (bf16[64,1024]{1,0:T(8,128)(2,1)S(1)}, bf16[64,1024]{1,0:T(8,128)(2,1)S(1)}, u32[]{:S(2)}, u32[]{:S(2)}) collective-permute-start(bf16[64,1024]{1,0:T(8,128)(2,1)S(1)} %get-tuple-element.113), channel_id=1, source_target_pairs={{0,4},{2,6},{4,0},{6,2},{8,12},{10,14},{12,8},{14,10},{1,5},{3,7},... | collective-permute-start | bytes 393224 | tf_op jit(solution)/shard_map/ppermute | solution.py:742
  102.4 9.7 %collective-permute-start.19 = (bf16[64,1024]{1,0:T(8,128)(2,1)S(1)}, bf16[64,1024]{1,0:T(8,128)(2,1)S(1)}, u32[]{:S(2)}, u32[]{:S(2)}) collective-permute-start(bf16[64,1024]{1,0:T(8,128)(2,1)S(1)} %get-tuple-element.114), channel_id=1, source_target_pairs={{0,6},{2,4},{4,2},{6,0},{8,14},{10,12},{12,10},{14,8},{1,7},{3,5},... | collective-permute-start | bytes 393224 | tf_op jit(solution)/shard_map/ppermute | solution.py:742
  108.0 0.8 collective-permute-start.16
  108.7 3.4 %collective-permute-start.15 = (f32[64,128]{1,0:T(8,128)S(1)}, f32[64,128]{1,0:T(8,128)S(1)}, u32[]{:S(2)}, u32[]{:S(2)}) collective-permute-start(f32[64,128]{1,0:T(8,128)S(1)} %get-tuple-element.119.refs_0_), channel_id=1, source_target_pairs={{0,1},{1,0},{2,3},{3,2},{4,5},{5,4},{6,7},{7,6},{8,9},{9,8},{10,11... | collective-permute-start | bytes 98312 | tf_op jit(solution)/shard_map/ppermute | solution.py:742
  108.8 3.3 %collective-permute-start.17 = (f32[64,128]{1,0:T(8,128)S(1)}, f32[64,128]{1,0:T(8,128)S(1)}, u32[]{:S(2)}, u32[]{:S(2)}) collective-permute-start(f32[64,128]{1,0:T(8,128)S(1)} %collective-permute-done.16.refs_2_), channel_id=1, source_target_pairs={{0,1},{1,0},{2,3},{3,2},{4,5},{5,4},{6,7},{7,6},{8,9},{9,8},{10,11... | collective-permute-start | bytes 98312 | tf_op jit(solution)/shard_map/ppermute | solution.py:742
  113.0 6.0 %collective-permute-start.21 = (bf16[64,1024]{1,0:T(8,128)(2,1)S(1)}, bf16[64,1024]{1,0:T(8,128)(2,1)S(1)}, u32[]{:S(2)}, u32[]{:S(2)}) collective-permute-start(bf16[64,1024]{1,0:T(8,128)(2,1)S(1)} %get-tuple-element.124), channel_id=1, source_target_pairs={{0,2},{2,0},{4,6},{6,4},{8,10},{10,8},{12,14},{14,12},{1,3},{3,1},... | collective-permute-start | bytes 393224 | tf_op jit(solution)/shard_map/ppermute | solution.py:742
  113.6 9.8 %collective-permute-start.22 = (bf16[64,1024]{1,0:T(8,128)(2,1)S(1)}, bf16[64,1024]{1,0:T(8,128)(2,1)S(1)}, u32[]{:S(2)}, u32[]{:S(2)}) collective-permute-start(bf16[64,1024]{1,0:T(8,128)(2,1)S(1)} %get-tuple-element.125), channel_id=1, source_target_pairs={{0,4},{2,6},{4,0},{6,2},{8,12},{10,14},{12,8},{14,10},{1,5},{3,7},... | collective-permute-start | bytes 393224 | tf_op jit(solution)/shard_map/ppermute | solution.py:742
  119.0 6.3 %collective-permute-start.23 = (bf16[64,1024]{1,0:T(8,128)(2,1)S(1)}, bf16[64,1024]{1,0:T(8,128)(2,1)S(1)}, u32[]{:S(2)}, u32[]{:S(2)}) collective-permute-start(bf16[64,1024]{1,0:T(8,128)(2,1)S(1)} %get-tuple-element.126), channel_id=1, source_target_pairs={{0,6},{2,4},{4,2},{6,0},{8,14},{10,12},{12,10},{14,8},{1,7},{3,5},... | collective-permute-start | bytes 393224 | tf_op jit(solution)/shard_map/ppermute | solution.py:742
  (11 other events, 149.8 us)

commit v15 on v14

--- a/solution.py
+++ b/solution.py
@@ -610,9 +610,8 @@
     return lows, tag
 
 
-def add_low(mine_ref, other_ref, share):
-    low = (mine_ref[...] + other_ref[...]).astype(jnp.bfloat16).astype(jnp.float32)
-    return unpack(low, share)
+def rounded(low, share):
+    return unpack(low.astype(jnp.bfloat16).astype(jnp.float32), share)
 
 
 def spread(low, tags, columns, slots, share):
@@ -633,7 +632,7 @@
     outs, (up, sem) = rest[:-2], rest[-2:]
     copy = pltpu.make_async_copy(own, up, sem)
     copy.start()
-    low = add_low(mine_ref, other_ref, plan.rank)
+    low = rounded(mine_ref[...] + other_ref[...], plan.rank)
     wide_low = spread(low, tag_ref[...], up.shape[0], plan.slots, plan.rank)
     copy.wait()
     write_deltas(jnp.dot(wide_low, up[...], preferred_element_type=jnp.float32), outs)
@@ -672,16 +671,12 @@
             (plan.groups, plan.padded - plan.left_rows, plan.features), up.dtype
         )
     tags = tag_ref[...]
-    wides = [
-        spread(
-            add_low(lows[2 * e], lows[2 * e + 1], plan.share),
-            tags,
-            plan.left_rows,
-            plan.slots,
-            plan.share,
-        )
-        for e in range(plan.groups)
-    ]
+    wides = []
+    for e in range(plan.groups):
+        mine, other = lows[2 * e][...], lows[2 * e + 1][...]
+        low = jnp.where(am_outer(plan), mine, other) if e else mine + other
+        low = rounded(low, plan.share)
+        wides.append(spread(low, tags, plan.left_rows, plan.slots, plan.share))
     copies.wait()
     delta = None
     for e in range(plan.groups):
@@ -708,24 +703,27 @@
     )
 
 
-def join_kernel(seg_ref, base_ref, *refs):
+def join_kernel(order, seg_ref, base_ref, *refs):
     deltas, out_ref = refs[:-1], refs[-1]
-    for k in range(len(deltas) * CAP):
-        part = k % CAP
+    for i in range(len(deltas) * CAP):
+        part = i % CAP
+        k = order[i // CAP] * CAP + part
 
         @pl.when(seg_ref[k] >= 0)
         def _():
             span = pl.ds(pl.multiple_of(seg_ref[k] * SEG, SEG), SEG)
-            delta = deltas[k // CAP][part * SEG : (part + 1) * SEG, :]
+            delta = deltas[i // CAP][part * SEG : (part + 1) * SEG, :]
             out_ref[span, :] = (base_ref[span, :] + delta.astype(jnp.float32)).astype(
                 out_ref.dtype
             )
 
 
-def join(seg_of, base, deltas):
+def join(plan, seg_of, base, deltas):
     height, features = base.shape
+    order = [kind * plan.half + d for kind in range(2) for d in plan.cross + plan.near]
+    deltas = [deltas[i] for i in order]
     return pl.pallas_call(
-        join_kernel,
+        functools.partial(join_kernel, order),
         out_shape=jax.ShapeDtypeStruct((height, features), jnp.bfloat16),
         in_specs=[SMEM, VMEM] + [VMEM] * len(deltas),
         out_specs=VMEM,
@@ -847,15 +845,17 @@
     lows = reduce_last(plan, lows, tag, near, wide_in, late_in[-1], across)
     pairs = []
     for e in range(plan.groups):
-        low = lows[e]
+        other = swap(lows[e], "tensor", 1)
         if e:
-            low = send(plan, low, [(plan.outer, 0, 0, 0), (plan.inner, e, 0, 0)])
-        pairs += [low, swap(low, "tensor", 1)]
+            total = lows[e] + other
+            pairs += [total, swap(total, "groups", e)]
+        else:
+            pairs += [lows[e], other]
     pairs, deltas = lax.optimization_barrier((pairs, deltas))
     across_wide = [blocks[plan.left_pieces] for blocks in across]
     terms = expand_taken(plan, pairs, tag, wide_in, late_in[0], across_wide, across_up)
     deltas += [terms[0]] + return_terms(terms)
-    return join(seg_of, base, deltas)
+    return join(plan, seg_of, base, deltas)
 
 
 def solution(mesh):

time: 127 us -> 126 us (level)
  starting transfers between devices: 31.5 us -> 29.9 us
    ppermute x13 -> x14, starting transfers between devices: 15.3 us -> 14.4 us  [swap(): return lax.ppermute(value, axis, [(i, i ^ distance) for i in range(count)])]
    ppermute x11 -> x10, starting transfers between devices: 16.2 us -> 15.5 us  [send(): return lax.ppermute(value, ('groups', 'replica', 'tensor'), pairs)]
    ppermute x13 -> x14, waiting for transfers between devices: 29.3 us -> 29.2 us  [swap(): return lax.ppermute(value, axis, [(i, i ^ distance) for i in range(count)])]
    ppermute x11 -> x10, waiting for transfers between devices: 32.5 us -> 32.5 us  [send(): return lax.ppermute(value, ('groups', 'replica', 'tensor'), pairs)]
  transfers between devices with their start and end apart: 24 -> 24, of which waited for: 12 -> 15; matrix products, arithmetic and copies ran while one was open for 11% -> 12% of each run, Pallas kernels for 9% -> 9%
where the time goes in v15:
time: 126 us; the launch traced here: 125 us
  waiting for transfers between devices  61.7 us (49%)
  starting transfers between devices  29.9 us (24%)
  Pallas kernels  18.9 us (15%)
  matrix products  13.7 us (11%)
    ppermute x10, waiting for transfers between devices, send(): return lax.ppermute(value, ('groups', 'replica', 'tensor'), pairs)  32.5 us
    ppermute x14, waiting for transfers between devices, swap(): return lax.ppermute(value, axis, [(i, i ^ distance) for i in range(count)])  29.2 us
    ppermute x10, starting transfers between devices, send(): return lax.ppermute(value, ('groups', 'replica', 'tensor'), pairs)  15.5 us
    ppermute x14, starting transfers between devices, swap(): return lax.ppermute(value, axis, [(i, i ^ distance) for i in range(count)])  14.4 us
    dot_general x2, matrix products, part(): return jnp.dot(rows, columns, preferred_element_type=jnp.float32)  13.7 us
    pallas_call x2, Pallas kernels, lay_out(): pl.pallas_call(functools.partial(lay_kernel, plan, first_call), out_shape...  9.73 us
    pallas_call x4, Pallas kernels, blocks_call(): pl.pallas_call(body, out_shape=out_shape, in_specs=[VMEM] * n_extra + [HB...  6.18 us
  transfers between devices with their start and end apart: 24, of which 15 were waited for; matrix products, arithmetic and copies ran while one was open for 12% of the time, Pallas kernels for 9%

profile of v15, /device:TPU:0, one launch (start us, length us, event | category | flops | bytes accessed | tf_op | source)
XLA Modules:
  0.0 125.4 jit_solution(15637499618459355596)
XLA Ops:
  0.0 4.6 %lay_out_first.1 = (bf16[128,4224]{1,0:T(8,128)(2,1)}, bf16[128,4096]{1,0:T(8,128)(2,1)}, bf16[128,4096]{1,0:T(8,128)(2,1)}, bf16[128,128]{1,0:T(8,128)(2,1)}, bf16[128,128]{1,0:T(8,128)(2,1)}, /*index=5*/s32[16]{0:T(128)}) custom-call(s32[16]{0:T(128)} %ids_ref.2, s32[48]{0:T(128)} %residency_ref.3, bf16[512,4096]{1,0:T(8,128)(2,1)} %x_ref.3, ...), custom_call_target="tpu_custom_call" | custom-call | bytes 2097152 | tf_op jit(solution)/shard_map/lay_out_first/pallas_call | solution.py:234
  4.6 3.0 %collective-permute-start.2 = (bf16[128,4224]{1,0:T(8,128)(2,1)}, bf16[128,4224]{1,0:T(8,128)(2,1)S(1)}, u32[]{:S(2)}, u32[]{:S(2)}) collective-permute-start(bf16[128,4224]{1,0:T(8,128)(2,1)} %get-tuple-element.71), channel_id=1, source_target_pairs={{0,2},{2,0},{4,6},{6,4},{8,10},{10,8},{12,14},{14,12},{1,3},{3,1},... | collective-permute-start | bytes 3244040 | tf_op jit(solution)/shard_map/ppermute | solution.py:740
  7.7 2.1 %collective-permute-start = (bf16[128,4096]{1,0:T(8,128)(2,1)}, bf16[128,4096]{1,0:T(8,128)(2,1)S(1)}, u32[]{:S(2)}, u32[]{:S(2)}) collective-permute-start(bf16[128,4096]{1,0:T(8,128)(2,1)} %get-tuple-element.67), channel_id=1, source_target_pairs={{0,4},{1,5},{2,6},{3,7},{12,8},{13,9},{14,10},{15,11},{16,20},{17,... | collective-permute-start | bytes 3145736 | tf_op jit(solution)/shard_map/ppermute | solution.py:756
  9.7 2.1 %collective-permute-start.4 = (bf16[128,128]{1,0:T(8,128)(2,1)}, bf16[128,128]{1,0:T(8,128)(2,1)S(1)}, u32[]{:S(2)}, u32[]{:S(2)}) collective-permute-start(bf16[128,128]{1,0:T(8,128)(2,1)} %get-tuple-element.76), channel_id=1, source_target_pairs={{0,4},{2,6},{4,0},{6,2},{8,12},{10,14},{12,8},{14,10},{1,5},{3,7},... | collective-permute-start | bytes 98312 | tf_op jit(solution)/shard_map/ppermute | solution.py:740
  11.8 2.9 %collective-permute-start.1 = (bf16[128,4096]{1,0:T(8,128)(2,1)}, bf16[128,4096]{1,0:T(8,128)(2,1)S(1)}, u32[]{:S(2)}, u32[]{:S(2)}) collective-permute-start(bf16[128,4096]{1,0:T(8,128)(2,1)} %get-tuple-element.68), channel_id=1, source_target_pairs={{0,6},{1,7},{2,4},{3,5},{12,10},{13,11},{14,8},{15,9},{16,22},{17,... | collective-permute-start | bytes 3145736 | tf_op jit(solution)/shard_map/ppermute | solution.py:756
  14.8 5.1 %lay_out_second.1 = (bf16[128,4224]{1,0:T(8,128)(2,1)}, bf16[64,4096]{1,0:T(8,128)(2,1)}, bf16[128,4096]{1,0:T(8,128)(2,1)}, bf16[64,4096]{1,0:T(8,128)(2,1)}, s32[16]{0:T(128)}) custom-call(s32[16]{0:T(128)} %ids_ref.2, s32[48]{0:T(128)} %residency_ref.3, bf16[512,4096]{1,0:T(8,128)(2,1)} %x_ref.3, bf16[6,64,4096]{2,1,0:T(8,128)(2,1)} %bitcast.7, ...), custom_call_target="tpu_custom_call" | custom-call | bytes 2097152 | tf_op jit(solution)/shard_map/lay_out_second/pallas_call | solution.py:234
  19.9 11.8 %collective-permute-done.2.refs_1_.refs_4_ = bf16[128,4224]{1,0:T(8,128)(2,1)S(1)} collective-permute-done((bf16[128,4224]{1,0:T(8,128)(2,1)}, bf16[128,4224]{1,0:T(8,128)(2,1)S(1)}, u32[]{:S(2)}, u32[]{:S(2)}) %collective-permute-start.2) | collective-permute-done | bytes 1081376 | tf_op jit(solution)/shard_map/ppermute | solution.py:740
  31.7 3.3 %collective-permute-done.refs_2_.refs_5_ = bf16[128,4096]{1,0:T(8,128)(2,1)S(1)} collective-permute-done((bf16[128,4096]{1,0:T(8,128)(2,1)}, bf16[128,4096]{1,0:T(8,128)(2,1)S(1)}, u32[]{:S(2)}, u32[]{:S(2)}) %collective-permute-start) | collective-permute-done | bytes 1048608 | tf_op jit(solution)/shard_map/ppermute | solution.py:756
  36.8 9.1 %fusion = f32[512,1024]{1,0:T(8,128)S(1)} fusion(bf16[512,4096]{1,0:T(8,128)(2,1)} %x_ref.3, bf16[4096,2048]{1,0:T(8,128)(2,1)} %param.7, s32[]{:T(128)S(6)} %select_n.27), kind=kOutput, calls=%fused_computation | convolution fusion | flops 4294967296 | bytes 14680068 | tf_op jit(solution)/shard_map/dot_general | solution.py:793
  46.0 4.5 %fusion.2 = f32[512,1024]{1,0:T(8,128)S(1)} fusion(bf16[512,4096]{1,0:T(8,128)(2,1)S(1)} %copy-done.4, bf16[4096,2048]{1,0:T(8,128)(2,1)S(1)} %bitcast.11, s32[]{:T(128)S(6)} %select_n.26), kind=kOutput, calls=%fused_computation.2 | convolution fusion | flops 4294967296 | bytes 14680068 | tf_op jit(solution)/shard_map/dot_general | solution.py:793
  50.6 6.5 %collective-permute-done.4.refs_6_ = bf16[128,128]{1,0:T(8,128)(2,1)S(1)} collective-permute-done((bf16[128,128]{1,0:T(8,128)(2,1)}, bf16[128,128]{1,0:T(8,128)(2,1)S(1)}, u32[]{:S(2)}, u32[]{:S(2)}) %collective-permute-start.4) | collective-permute-done | bytes 32800 | tf_op jit(solution)/shard_map/ppermute | solution.py:740
  57.7 1.8 %collective-permute-start.6 = (bf16[64,4096]{1,0:T(8,128)(2,1)}, bf16[64,4096]{1,0:T(8,128)(2,1)S(1)}, u32[]{:S(2)}, u32[]{:S(2)}) collective-permute-start(bf16[64,4096]{1,0:T(8,128)(2,1)} %get-tuple-element.79), channel_id=1, source_target_pairs={{4,0},{5,1},{6,2},{7,3},{8,12},{9,13},{10,14},{11,15},{20,16},{21,... | collective-permute-start | bytes 1572872 | tf_op jit(solution)/shard_map/ppermute | solution.py:756
  59.5 1.8 %collective-permute-start.8 = (bf16[128,4096]{1,0:T(8,128)(2,1)S(1)}, bf16[128,4096]{1,0:T(8,128)(2,1)S(1)}, u32[]{:S(2)}, u32[]{:S(2)}) collective-permute-start(bf16[128,4096]{1,0:T(8,128)(2,1)S(1)} %copy-done.5), channel_id=1, source_target_pairs={{4,2},{5,3},{6,0},{7,1},{8,14},{9,15},{10,12},{11,13},{20,18},{21,... | collective-permute-start | bytes 3145736 | tf_op jit(solution)/shard_map/ppermute | solution.py:756
  63.7 9.0 %collective-permute-done.6.refs_4_.refs_7_ = bf16[64,4096]{1,0:T(8,128)(2,1)S(1)} collective-permute-done((bf16[64,4096]{1,0:T(8,128)(2,1)}, bf16[64,4096]{1,0:T(8,128)(2,1)S(1)}, u32[]{:S(2)}, u32[]{:S(2)}) %collective-permute-start.6) | collective-permute-done | bytes 524320 | tf_op jit(solution)/shard_map/ppermute | solution.py:756
  74.2 2.4 %collective-permute-done.9.refs_9_ = bf16[64,4224]{1,0:T(8,128)(2,1)S(1)} collective-permute-done((bf16[64,4224]{1,0:T(8,128)(2,1)S(1)}, bf16[64,4224]{1,0:T(8,128)(2,1)S(1)}, u32[]{:S(2)}, u32[]{:S(2)}) %collective-permute-start.9) | collective-permute-done | bytes 540704 | tf_op jit(solution)/shard_map/ppermute | solution.py:756
  77.7 10.4 %collective-permute-done.10.refs_10_ = bf16[64,4224]{1,0:T(8,128)(2,1)S(1)} collective-permute-done((bf16[64,4224]{1,0:T(8,128)(2,1)S(1)}, bf16[64,4224]{1,0:T(8,128)(2,1)S(1)}, u32[]{:S(2)}, u32[]{:S(2)}) %collective-permute-start.10) | collective-permute-done | bytes 540704 | tf_op jit(solution)/shard_map/ppermute | solution.py:756
  88.9 7.3 %collective-permute-done.8.refs_5_ = bf16[128,4096]{1,0:T(8,128)(2,1)S(1)} collective-permute-done((bf16[128,4096]{1,0:T(8,128)(2,1)S(1)}, bf16[128,4096]{1,0:T(8,128)(2,1)S(1)}, u32[]{:S(2)}, u32[]{:S(2)}) %collective-permute-start.8) | collective-permute-done | bytes 1048608 | tf_op jit(solution)/shard_map/ppermute | solution.py:756
  96.2 2.0 %reduce_own.1 = (f32[128,128]{1,0:T(8,128)S(1)}, f32[256,128]{1,0:T(8,128)S(1)}) custom-call(bf16[128,4224]{1,0:T(8,128)(2,1)S(1)} %copy-done.1, bf16[128,4224]{1,0:T(8,128)(2,1)S(1)} %collective-permute-done.2.refs_1_.refs_4_, bf16[128,4096]{1,0:T(8,128)(2,1)S(1)} %collective-permute-done.refs_2_.refs_5_, ...), custom_call_target="tpu_custom_call" | custom-call | flops 1 | bytes 1 | tf_op jit(solution)/shard_map/reduce_own/pallas_call | solution.py:550
  100.7 1.7 %collective-permute-start.18 = (bf16[64,1024]{1,0:T(8,128)(2,1)S(1)}, bf16[64,1024]{1,0:T(8,128)(2,1)S(1)}, u32[]{:S(2)}, u32[]{:S(2)}) collective-permute-start(bf16[64,1024]{1,0:T(8,128)(2,1)S(1)} %get-tuple-element.113), channel_id=1, source_target_pairs={{0,4},{2,6},{4,0},{6,2},{8,12},{10,14},{12,8},{14,10},{1,5},{3,7},... | collective-permute-start | bytes 393224 | tf_op jit(solution)/shard_map/ppermute | solution.py:740
  103.7 2.7 %reduce_taken.1 = (f32[64,128]{1,0:T(8,128)S(1)}, f32[64,128]{1,0:T(8,128)S(1)}, f32[256,128]{1,0:T(8,128)S(1)}) custom-call(bf16[128,4224]{1,0:T(8,128)(2,1)S(1)} %copy-done.1, bf16[128,4224]{1,0:T(8,128)(2,1)S(1)} %collective-permute-done.2.refs_1_.refs_4_, bf16[128,4096]{1,0:T(8,128)(2,1)S(1)} %collective-permute-done.refs_2_.refs_5_, ...), custom_call_target="tpu_custom_call" | custom-call | flops 1 | bytes 1 | tf_op jit(solution)/shard_map/reduce_taken/pallas_call | solution.py:550
  114.1 1.6 %collective-permute-start.21 = (bf16[64,1024]{1,0:T(8,128)(2,1)S(1)}, bf16[64,1024]{1,0:T(8,128)(2,1)S(1)}, u32[]{:S(2)}, u32[]{:S(2)}) collective-permute-start(bf16[64,1024]{1,0:T(8,128)(2,1)S(1)} %get-tuple-element.123), channel_id=1, source_target_pairs={{0,4},{2,6},{4,0},{6,2},{8,12},{10,14},{12,8},{14,10},{1,5},{3,7},... | collective-permute-start | bytes 393224 | tf_op jit(solution)/shard_map/ppermute | solution.py:740
  117.7 2.6 %collective-permute-done.21.refs_4_ = bf16[64,1024]{1,0:T(8,128)(2,1)S(1)} collective-permute-done((bf16[64,1024]{1,0:T(8,128)(2,1)S(1)}, bf16[64,1024]{1,0:T(8,128)(2,1)S(1)}, u32[]{:S(2)}, u32[]{:S(2)}) %collective-permute-start.21) | collective-permute-done | bytes 131104 | tf_op jit(solution)/shard_map/ppermute | solution.py:740
  120.3 2.0 %collective-permute-done.22.refs_5_ = bf16[64,1024]{1,0:T(8,128)(2,1)S(1)} collective-permute-done((bf16[64,1024]{1,0:T(8,128)(2,1)S(1)}, bf16[64,1024]{1,0:T(8,128)(2,1)S(1)}, u32[]{:S(2)}, u32[]{:S(2)}) %collective-permute-start.22) | collective-permute-done | bytes 131104 | tf_op jit(solution)/shard_map/ppermute | solution.py:740
  123.5 1.8 %join.1 = bf16[512,1024]{1,0:T(8,128)(2,1)} custom-call(s32[16]{0:T(128)S(1)} %copy-done.3, f32[512,1024]{1,0:T(8,128)S(1)} %add.14.base_ref, bf16[64,1024]{1,0:T(8,128)(2,1)S(1)} %collective-permute-done.18.refs_0_, bf16[64,1024]{1,0:T(8,128)(2,1)S(1)} %collective-permute-done.19.refs_1_, bf16[64,1024]{1,0:T(8,128)(2,1)S(1)} %get-tuple-element.117.refs_2_, ...), custom_call_target="tpu_custom_call" | custom-call | flops 524288 | bytes 4194304 | tf_op jit(solution)/shard_map/join/pallas_call | solution.py:725
  (70 shorter events, 22.7 us)
Async XLA Ops:
  4.6 27.1 %collective-permute-start.2 = (bf16[128,4224]{1,0:T(8,128)(2,1)}, bf16[128,4224]{1,0:T(8,128)(2,1)S(1)}, u32[]{:S(2)}, u32[]{:S(2)}) collective-permute-start(bf16[128,4224]{1,0:T(8,128)(2,1)} %get-tuple-element.71), channel_id=1, source_target_pairs={{0,2},{2,0},{4,6},{6,4},{8,10},{10,8},{12,14},{14,12},{1,3},{3,1},... | collective-permute-start | bytes 3244040 | tf_op jit(solution)/shard_map/ppermute | solution.py:740
  7.7 27.4 %collective-permute-start = (bf16[128,4096]{1,0:T(8,128)(2,1)}, bf16[128,4096]{1,0:T(8,128)(2,1)S(1)}, u32[]{:S(2)}, u32[]{:S(2)}) collective-permute-start(bf16[128,4096]{1,0:T(8,128)(2,1)} %get-tuple-element.67), channel_id=1, source_target_pairs={{0,4},{1,5},{2,6},{3,7},{12,8},{13,9},{14,10},{15,11},{16,20},{17,... | collective-permute-start | bytes 3145736 | tf_op jit(solution)/shard_map/ppermute | solution.py:756
  9.7 47.4 %collective-permute-start.4 = (bf16[128,128]{1,0:T(8,128)(2,1)}, bf16[128,128]{1,0:T(8,128)(2,1)S(1)}, u32[]{:S(2)}, u32[]{:S(2)}) collective-permute-start(bf16[128,128]{1,0:T(8,128)(2,1)} %get-tuple-element.76), channel_id=1, source_target_pairs={{0,4},{2,6},{4,0},{6,2},{8,12},{10,14},{12,8},{14,10},{1,5},{3,7},... | collective-permute-start | bytes 98312 | tf_op jit(solution)/shard_map/ppermute | solution.py:740
  11.8 45.8 %collective-permute-start.5 = (bf16[128,128]{1,0:T(8,128)(2,1)}, bf16[128,128]{1,0:T(8,128)(2,1)S(1)}, u32[]{:S(2)}, u32[]{:S(2)}) collective-permute-start(bf16[128,128]{1,0:T(8,128)(2,1)} %get-tuple-element.77), channel_id=1, source_target_pairs={{0,6},{2,4},{4,2},{6,0},{8,14},{10,12},{12,10},{14,8},{1,7},{3,5},... | collective-permute-start | bytes 98312 | tf_op jit(solution)/shard_map/ppermute | solution.py:740
  11.8 45.8 %collective-permute-start.1 = (bf16[128,4096]{1,0:T(8,128)(2,1)}, bf16[128,4096]{1,0:T(8,128)(2,1)S(1)}, u32[]{:S(2)}, u32[]{:S(2)}) collective-permute-start(bf16[128,4096]{1,0:T(8,128)(2,1)} %get-tuple-element.68), channel_id=1, source_target_pairs={{0,6},{1,7},{2,4},{3,5},{12,10},{13,11},{14,8},{15,9},{16,22},{17,... | collective-permute-start | bytes 3145736 | tf_op jit(solution)/shard_map/ppermute | solution.py:756
  35.2 22.4 %collective-permute-start.3 = (bf16[64,4224]{1,0:T(8,128)(2,1)S(1)}, bf16[64,4224]{1,0:T(8,128)(2,1)S(1)}, u32[]{:S(2)}, u32[]{:S(2)}) collective-permute-start(bf16[64,4224]{1,0:T(8,128)(2,1)S(1)} %pad_maximum_fusion), channel_id=1, source_target_pairs={{0,16},{1,17},{2,18},{3,19},{12,28},{13,29},{14,30},{15,31},{16,0}... | collective-permute-start | bytes 1622024 | tf_op jit(solution)/shard_map/ppermute | solution.py:756
  57.7 15.0 %collective-permute-start.6 = (bf16[64,4096]{1,0:T(8,128)(2,1)}, bf16[64,4096]{1,0:T(8,128)(2,1)S(1)}, u32[]{:S(2)}, u32[]{:S(2)}) collective-permute-start(bf16[64,4096]{1,0:T(8,128)(2,1)} %get-tuple-element.79), channel_id=1, source_target_pairs={{4,0},{5,1},{6,2},{7,3},{8,12},{9,13},{10,14},{11,15},{20,16},{21,... | collective-permute-start | bytes 1572872 | tf_op jit(solution)/shard_map/ppermute | solution.py:756
  59.5 36.7 %collective-permute-start.8 = (bf16[128,4096]{1,0:T(8,128)(2,1)S(1)}, bf16[128,4096]{1,0:T(8,128)(2,1)S(1)}, u32[]{:S(2)}, u32[]{:S(2)}) collective-permute-start(bf16[128,4096]{1,0:T(8,128)(2,1)S(1)} %copy-done.5), channel_id=1, source_target_pairs={{4,2},{5,3},{6,0},{7,1},{8,14},{9,15},{10,12},{11,13},{20,18},{21,... | collective-permute-start | bytes 3145736 | tf_op jit(solution)/shard_map/ppermute | solution.py:756
  61.2 41.2 %collective-permute-start.13 = (f32[512,1024]{1,0:T(8,128)S(1)}, f32[512,1024]{1,0:T(8,128)S(1)}, u32[]{:S(2)}, u32[]{:S(2)}) collective-permute-start(f32[512,1024]{1,0:T(8,128)S(1)} %fusion.2), channel_id=1, source_target_pairs={{0,1},{1,0},{2,3},{3,2},{4,5},{5,4},{6,7},{7,6},{8,9},{9,8},{10,11... | collective-permute-start | bytes 6291464 | tf_op jit(solution)/shard_map/ppermute | solution.py:740
  61.5 15.1 %collective-permute-start.9 = (bf16[64,4224]{1,0:T(8,128)(2,1)S(1)}, bf16[64,4224]{1,0:T(8,128)(2,1)S(1)}, u32[]{:S(2)}, u32[]{:S(2)}) collective-permute-start(bf16[64,4224]{1,0:T(8,128)(2,1)S(1)} %pad_maximum_fusion.1), channel_id=1, source_target_pairs={{0,16},{1,17},{2,18},{3,19},{12,28},{13,29},{14,30},{15,31},{16,0}... | collective-permute-start | bytes 1622024 | tf_op jit(solution)/shard_map/ppermute | solution.py:756
  63.1 25.1 %collective-permute-start.10 = (bf16[64,4224]{1,0:T(8,128)(2,1)S(1)}, bf16[64,4224]{1,0:T(8,128)(2,1)S(1)}, u32[]{:S(2)}, u32[]{:S(2)}) collective-permute-start(bf16[64,4224]{1,0:T(8,128)(2,1)S(1)} %pad_maximum_fusion.2), channel_id=1, source_target_pairs={{0,16},{1,17},{2,18},{3,19},{12,28},{13,29},{14,30},{15,31},{16,0}... | collective-permute-start | bytes 1622024 | tf_op jit(solution)/shard_map/ppermute | solution.py:756
  72.7 28.0 %collective-permute-start.14 = (bf16[64,4224]{1,0:T(8,128)(2,1)S(1)}, bf16[64,4224]{1,0:T(8,128)(2,1)S(1)}, u32[]{:S(2)}, u32[]{:S(2)}) collective-permute-start(bf16[64,4224]{1,0:T(8,128)(2,1)S(1)} %pad_maximum_fusion.3), channel_id=1, source_target_pairs={{0,16},{1,17},{2,18},{3,19},{12,28},{13,29},{14,30},{15,31},{16,0}... | collective-permute-start | bytes 1622024 | tf_op jit(solution)/shard_map/ppermute | solution.py:756
  76.6 30.2 %collective-permute-start.7 = (bf16[64,4096]{1,0:T(8,128)(2,1)S(1)}, bf16[64,4096]{1,0:T(8,128)(2,1)S(1)}, u32[]{:S(2)}, u32[]{:S(2)}) collective-permute-start(bf16[64,4096]{1,0:T(8,128)(2,1)S(1)} %copy-done.6), channel_id=1, source_target_pairs={{4,0},{5,1},{6,2},{7,3},{8,12},{9,13},{10,14},{11,15},{20,16},{21,... | collective-permute-start | bytes 1572872 | tf_op jit(solution)/shard_map/ppermute | solution.py:756
  88.2 25.0 %collective-permute-start.20 = (bf16[48,4096]{1,0:T(8,128)(2,1)S(1)}, bf16[48,4096]{1,0:T(8,128)(2,1)S(1)}, u32[]{:S(2)}, u32[]{:S(2)}) collective-permute-start(bf16[48,4096]{1,0:T(8,128)(2,1)S(1)} %slice.51), channel_id=1, source_target_pairs={{4,20},{5,21},{6,22},{7,23},{8,24},{9,25},{10,26},{11,27},{20,4},{... | collective-permute-start | bytes 1179656 | tf_op jit(solution)/shard_map/ppermute | solution.py:756
  98.2 1.3 %collective-permute-start.11 = (f32[128,128]{1,0:T(8,128)S(1)}, f32[128,128]{1,0:T(8,128)S(1)}, u32[]{:S(2)}, u32[]{:S(2)}) collective-permute-start(f32[128,128]{1,0:T(8,128)S(1)} %get-tuple-element.93.refs_0_), channel_id=1, source_target_pairs={{0,1},{1,0},{2,3},{3,2},{4,5},{5,4},{6,7},{7,6},{8,9},{9,8},{10,11... | collective-permute-start | bytes 196616 | tf_op jit(solution)/shard_map/ppermute | solution.py:740
  100.1 6.7 %collective-permute-start.12 = (bf16[64,1024]{1,0:T(8,128)(2,1)S(1)}, bf16[64,1024]{1,0:T(8,128)(2,1)S(1)}, u32[]{:S(2)}, u32[]{:S(2)}) collective-permute-start(bf16[64,1024]{1,0:T(8,128)(2,1)S(1)} %get-tuple-element.96), channel_id=1, source_target_pairs={{0,2},{2,0},{4,6},{6,4},{8,10},{10,8},{12,14},{14,12},{1,3},{3,1},... | collective-permute-start | bytes 393224 | tf_op jit(solution)/shard_map/ppermute | solution.py:740
  100.7 10.1 %collective-permute-start.18 = (bf16[64,1024]{1,0:T(8,128)(2,1)S(1)}, bf16[64,1024]{1,0:T(8,128)(2,1)S(1)}, u32[]{:S(2)}, u32[]{:S(2)}) collective-permute-start(bf16[64,1024]{1,0:T(8,128)(2,1)S(1)} %get-tuple-element.113), channel_id=1, source_target_pairs={{0,4},{2,6},{4,0},{6,2},{8,12},{10,14},{12,8},{14,10},{1,5},{3,7},... | collective-permute-start | bytes 393224 | tf_op jit(solution)/shard_map/ppermute | solution.py:740
  102.4 9.7 %collective-permute-start.19 = (bf16[64,1024]{1,0:T(8,128)(2,1)S(1)}, bf16[64,1024]{1,0:T(8,128)(2,1)S(1)}, u32[]{:S(2)}, u32[]{:S(2)}) collective-permute-start(bf16[64,1024]{1,0:T(8,128)(2,1)S(1)} %get-tuple-element.114), channel_id=1, source_target_pairs={{0,6},{2,4},{4,2},{6,0},{8,14},{10,12},{12,10},{14,8},{1,7},{3,5},... | collective-permute-start | bytes 393224 | tf_op jit(solution)/shard_map/ppermute | solution.py:740
  108.0 1.3 %collective-permute-start.16 = (f32[64,128]{1,0:T(8,128)S(1)}, f32[64,128]{1,0:T(8,128)S(1)}, u32[]{:S(2)}, u32[]{:S(2)}) collective-permute-start(f32[64,128]{1,0:T(8,128)S(1)} %get-tuple-element.110), channel_id=1, source_target_pairs={{0,1},{1,0},{2,3},{3,2},{4,5},{5,4},{6,7},{7,6},{8,9},{9,8},{10,11... | collective-permute-start | bytes 98312 | tf_op jit(solution)/shard_map/ppermute | solution.py:740
  108.1 4.0 %collective-permute-start.15 = (f32[64,128]{1,0:T(8,128)S(1)}, f32[64,128]{1,0:T(8,128)S(1)}, u32[]{:S(2)}, u32[]{:S(2)}) collective-permute-start(f32[64,128]{1,0:T(8,128)S(1)} %get-tuple-element.119.refs_0_), channel_id=1, source_target_pairs={{0,1},{1,0},{2,3},{3,2},{4,5},{5,4},{6,7},{7,6},{8,9},{9,8},{10,11... | collective-permute-start | bytes 98312 | tf_op jit(solution)/shard_map/ppermute | solution.py:740
  109.3 3.9 %collective-permute-start.17 = (f32[64,128]{1,0:T(8,128)S(1)}, f32[64,128]{1,0:T(8,128)S(1)}, u32[]{:S(2)}, u32[]{:S(2)}) collective-permute-start(f32[64,128]{1,0:T(8,128)S(1)} %add.15.refs_2_), channel_id=1, source_target_pairs={{0,16},{16,0},{1,17},{17,1},{2,18},{18,2},{3,19},{19,3},{4,20},{20... | collective-permute-start | bytes 98312 | tf_op jit(solution)/shard_map/ppermute | solution.py:740
  114.1 6.2 %collective-permute-start.21 = (bf16[64,1024]{1,0:T(8,128)(2,1)S(1)}, bf16[64,1024]{1,0:T(8,128)(2,1)S(1)}, u32[]{:S(2)}, u32[]{:S(2)}) collective-permute-start(bf16[64,1024]{1,0:T(8,128)(2,1)S(1)} %get-tuple-element.123), channel_id=1, source_target_pairs={{0,4},{2,6},{4,0},{6,2},{8,12},{10,14},{12,8},{14,10},{1,5},{3,7},... | collective-permute-start | bytes 393224 | tf_op jit(solution)/shard_map/ppermute | solution.py:740
  115.7 6.6 %collective-permute-start.22 = (bf16[64,1024]{1,0:T(8,128)(2,1)S(1)}, bf16[64,1024]{1,0:T(8,128)(2,1)S(1)}, u32[]{:S(2)}, u32[]{:S(2)}) collective-permute-start(bf16[64,1024]{1,0:T(8,128)(2,1)S(1)} %get-tuple-element.124), channel_id=1, source_target_pairs={{0,6},{2,4},{4,2},{6,0},{8,14},{10,12},{12,10},{14,8},{1,7},{3,5},... | collective-permute-start | bytes 393224 | tf_op jit(solution)/shard_map/ppermute | solution.py:740
  116.8 6.8 %collective-permute-start.23 = (bf16[64,1024]{1,0:T(8,128)(2,1)S(1)}, bf16[64,1024]{1,0:T(8,128)(2,1)S(1)}, u32[]{:S(2)}, u32[]{:S(2)}) collective-permute-start(bf16[64,1024]{1,0:T(8,128)(2,1)S(1)} %get-tuple-element.126), channel_id=1, source_target_pairs={{0,2},{2,0},{4,6},{6,4},{8,10},{10,8},{12,14},{14,12},{1,3},{3,1},... | collective-permute-start | bytes 393224 | tf_op jit(solution)/shard_map/ppermute | solution.py:740
  (11 other events, 148.0 us)

commit v16 on v15

--- a/solution.py
+++ b/solution.py
@@ -54,19 +54,10 @@
             yield piece, min(PAIR, self.left_rows - piece * PAIR)
 
     def late_blocks(self):
-        blocks = [(self.cross[0], 1, 0)]
-        blocks += [(d, 2, 2 * i - 1) for i, d in enumerate(self.cross) if i]
-        return blocks + [(self.cross[0], 1, self.units - 1)]
-
-    def late_unit(self, refs, unit):
-        if unit in (0, self.units - 1):
-            return refs[0 if unit == 0 else -1]
-        return refs[(unit + 1) // 2].at[pl.ds((unit - 1) % 2 * PAIR, PAIR)]
+        return self.cross + self.cross[::-1]
 
     def late_rows(self, refs, i, kind):
-        if i == 0:
-            return self.late_unit(refs, 0 if kind == 0 else self.units - 1)
-        return self.late_unit(refs, 2 * i - 1 + kind)
+        return refs[i if kind == 0 else self.units - 1 - i]
 
 
 def params(limit=VMEM_LIMIT):
@@ -83,7 +74,7 @@
 
 
 def late_adapters(late, piece, plan):
-    return plan.late_unit(late, 0 if piece == plan.left_pieces else 1 + piece)
+    return late[0 if piece == plan.left_pieces else 1 + piece]
 
 
 def lay_kernel(plan, first_call, ids_ref, residency_ref, x_ref, left_ref, up_ref, *rest):
@@ -227,7 +218,7 @@
     count = 2 * plan.half * CAP
     tagged = jax.ShapeDtypeStruct((2 * PAIR, plan.width + LANES), x.dtype)
     near = [tagged] * (len(plan.near) - 1 if first_call else 1)
-    heights = [2] * plan.wide if first_call else [n for _, n, _ in plan.late_blocks()]
+    heights = [2] * plan.wide if first_call else [1] * plan.units
     blocks = [jax.ShapeDtypeStruct((n * PAIR, plan.width), x.dtype) for n in heights]
     if first_call:
         blocks += [jax.ShapeDtypeStruct((2 * PAIR, LANES), x.dtype)] * len(plan.cross)
@@ -811,36 +802,39 @@
             for e in range(1, plan.groups)
         ]
 
-    across = [across_send(0)]
+    across = [across_send(0), across_send(1)]
     tags_in = [swap(tag, "replica", d) for tag, d in zip(tags, plan.cross)]
 
-    wide_in, near, across, late, tags_in, base_other, base_mine = lax.optimization_barrier(
-        (wide_in, near, across, late, tags_in, base_other, base_mine)
-    )
-    across += [across_send(i) for i in range(1, half)]
+    wide_in, near, across[0], late, tags_in, base_other, base_mine = lax.optimization_barrier(
+        (wide_in, near, across[0], late, tags_in, base_other, base_mine)
+    )
+    across += [across_send(i) for i in range(2, half)]
     late_in = []
-    for block, (d, _, unit) in zip(late, plan.late_blocks()):
+    for unit, d in enumerate(plan.late_blocks()):
         moves = [(plan.inner, 0, d, 0)]
         if unit < plan.pieces:
             moves.append((plan.outer, 0, half, 0))
-        if unit == plan.units - 1:
-            late_in[0], block = lax.optimization_barrier((late_in[0], block))
+        block = late[unit]
+        if unit >= 2:
+            late_in[unit - 2], across[1], block = lax.optimization_barrier(
+                (late_in[unit - 2], across[1], block)
+            )
         late_in.append(send(plan, block, moves))
     late_up = late_in[0][: plan.up_rows]
     across_up = [send(plan, late_up, [(plan.inner, e, 0, 0)]) for e in range(1, plan.groups)]
     base = base_mine + swap(base_other, "tensor", 1)
-    late_in[:-1], across[:-1] = lax.optimization_barrier((late_in[:-1], across[:-1]))
+    late_in[:n_cross], across[:-1] = lax.optimization_barrier((late_in[:n_cross], across[:-1]))
     across = [[blocks[e] for blocks in across] for e in range(plan.groups - 1)]
 
     own_left = left_rows.reshape(slots * rank, width)
-    low, tag = reduce_own(plan, near, wide_in, late_in[:-1], tags_in, own_left)
+    low, tag = reduce_own(plan, near, wide_in, late_in[:n_cross], tags_in, own_left)
     other = swap(low, "tensor", 1)
     terms = expand_own(plan, low, other, tag, ups.reshape(slots * rank, features))
     deltas = [terms[0]] + return_terms(terms)
 
     lows, tag = reduce_taken(plan, near, wide_in, late_in[:-1], tags_in, across)
-    late_in[-1], deltas[:2], base, lows = lax.optimization_barrier(
-        (late_in[-1], deltas[:2], base, lows)
+    late_in[-1], deltas[:2], lows, base = lax.optimization_barrier(
+        (late_in[-1], deltas[:2], lows, base)
     )
     lows = reduce_last(plan, lows, tag, near, wide_in, late_in[-1], across)
     pairs = []

time: 126 us -> 127 us (level)
  starting transfers between devices: 29.9 us -> 31.5 us
  matrix products: 13.7 us -> 12.1 us
    ppermute x10 -> x11, starting transfers between devices: 15.5 us -> 17.1 us  [send(): return lax.ppermute(value, ('groups', 'replica', 'tensor'), pairs)]
    dot_general x2, matrix products: 13.7 us -> 12.1 us  [part(): return jnp.dot(rows, columns, preferred_element_type=jnp.float32)]
    ppermute x10 -> x11, waiting for transfers between devices: 32.5 us -> 31.7 us  [send(): return lax.ppermute(value, ('groups', 'replica', 'tensor'), pairs)]
  transfers between devices with their start and end apart: 24 -> 25, of which waited for: 15 -> 15; matrix products, arithmetic and copies ran while one was open for 12% -> 12% of each run, Pallas kernels for 9% -> 9%
where the time goes in v16:
time: 127 us
  waiting for transfers between devices  61.4 us (48%)
  starting transfers between devices  31.5 us (25%)
  Pallas kernels  18.9 us (15%)
  matrix products  12.1 us (10%)
  other arithmetic  1.79 us (1%)
    ppermute x11, waiting for transfers between devices, send(): return lax.ppermute(value, ('groups', 'replica', 'tensor'), pairs)  31.7 us
    ppermute x14, waiting for transfers between devices, swap(): return lax.ppermute(value, axis, [(i, i ^ distance) for i in range(count)])  29.7 us
    ppermute x11, starting transfers between devices, send(): return lax.ppermute(value, ('groups', 'replica', 'tensor'), pairs)  17.1 us
    ppermute x14, starting transfers between devices, swap(): return lax.ppermute(value, axis, [(i, i ^ distance) for i in range(count)])  14.4 us
    dot_general x2, matrix products, part(): return jnp.dot(rows, columns, preferred_element_type=jnp.float32)  12.1 us
    pallas_call x2, Pallas kernels, lay_out(): pl.pallas_call(functools.partial(lay_kernel, plan, first_call), out_shape...  9.73 us
    pallas_call x4, Pallas kernels, blocks_call(): pl.pallas_call(body, out_shape=out_shape, in_specs=[VMEM] * n_extra + [HB...  6.2 us
  transfers between devices with their start and end apart: 25, of which 15 were waited for; matrix products, arithmetic and copies ran while one was open for 12% of the time, Pallas kernels for 9%

profile of v16, /device:TPU:0, one launch (start us, length us, event | category | flops | bytes accessed | tf_op | source)
XLA Modules:
  0.0 127.0 jit_solution(17371260060586352888)
XLA Ops:
  0.0 4.6 %lay_out_first.1 = (bf16[128,4224]{1,0:T(8,128)(2,1)}, bf16[128,4096]{1,0:T(8,128)(2,1)}, bf16[128,4096]{1,0:T(8,128)(2,1)}, bf16[128,128]{1,0:T(8,128)(2,1)}, bf16[128,128]{1,0:T(8,128)(2,1)}, /*index=5*/s32[16]{0:T(128)}) custom-call(s32[16]{0:T(128)} %ids_ref.2, s32[48]{0:T(128)} %residency_ref.3, bf16[512,4096]{1,0:T(8,128)(2,1)} %x_ref.3, ...), custom_call_target="tpu_custom_call" | custom-call | bytes 2097152 | tf_op jit(solution)/shard_map/lay_out_first/pallas_call | solution.py:225
  4.6 3.0 %collective-permute-start.2 = (bf16[128,4224]{1,0:T(8,128)(2,1)}, bf16[128,4224]{1,0:T(8,128)(2,1)S(1)}, u32[]{:S(2)}, u32[]{:S(2)}) collective-permute-start(bf16[128,4224]{1,0:T(8,128)(2,1)} %get-tuple-element.77), channel_id=1, source_target_pairs={{0,2},{2,0},{4,6},{6,4},{8,10},{10,8},{12,14},{14,12},{1,3},{3,1},... | collective-permute-start | bytes 3244040 | tf_op jit(solution)/shard_map/ppermute | solution.py:731
  7.7 2.1 %collective-permute-start = (bf16[128,4096]{1,0:T(8,128)(2,1)}, bf16[128,4096]{1,0:T(8,128)(2,1)S(1)}, u32[]{:S(2)}, u32[]{:S(2)}) collective-permute-start(bf16[128,4096]{1,0:T(8,128)(2,1)} %get-tuple-element.73), channel_id=1, source_target_pairs={{0,4},{1,5},{2,6},{3,7},{12,8},{13,9},{14,10},{15,11},{16,20},{17,... | collective-permute-start | bytes 3145736 | tf_op jit(solution)/shard_map/ppermute | solution.py:747
  9.7 2.0 %collective-permute-start.1 = (bf16[128,4096]{1,0:T(8,128)(2,1)}, bf16[128,4096]{1,0:T(8,128)(2,1)S(1)}, u32[]{:S(2)}, u32[]{:S(2)}) collective-permute-start(bf16[128,4096]{1,0:T(8,128)(2,1)} %get-tuple-element.74), channel_id=1, source_target_pairs={{0,6},{1,7},{2,4},{3,5},{12,10},{13,11},{14,8},{15,9},{16,22},{17,... | collective-permute-start | bytes 3145736 | tf_op jit(solution)/shard_map/ppermute | solution.py:747
  12.8 2.0 %collective-permute-start.5 = (bf16[128,128]{1,0:T(8,128)(2,1)}, bf16[128,128]{1,0:T(8,128)(2,1)S(1)}, u32[]{:S(2)}, u32[]{:S(2)}) collective-permute-start(bf16[128,128]{1,0:T(8,128)(2,1)} %get-tuple-element.84), channel_id=1, source_target_pairs={{0,6},{2,4},{4,2},{6,0},{8,14},{10,12},{12,10},{14,8},{1,7},{3,5},... | collective-permute-start | bytes 98312 | tf_op jit(solution)/shard_map/ppermute | solution.py:731
  14.7 5.1 %lay_out_second.1 = (bf16[128,4224]{1,0:T(8,128)(2,1)}, bf16[64,4096]{1,0:T(8,128)(2,1)}, bf16[64,4096]{1,0:T(8,128)(2,1)}, bf16[64,4096]{1,0:T(8,128)(2,1)}, bf16[64,4096]{1,0:T(8,128)(2,1)}, /*index=5*/s32[16]{0:T(128)}) custom-call(s32[16]{0:T(128)} %ids_ref.2, s32[48]{0:T(128)} %residency_ref.3, bf16[512,4096]{1,0:T(8,128)(2,1)} %x_ref.3, ...), custom_call_target="tpu_custom_call" | custom-call | bytes 2097152 | tf_op jit(solution)/shard_map/lay_out_second/pallas_call | solution.py:225
  20.6 11.1 %collective-permute-done.2.refs_1_.refs_4_ = bf16[128,4224]{1,0:T(8,128)(2,1)S(1)} collective-permute-done((bf16[128,4224]{1,0:T(8,128)(2,1)}, bf16[128,4224]{1,0:T(8,128)(2,1)S(1)}, u32[]{:S(2)}, u32[]{:S(2)}) %collective-permute-start.2) | collective-permute-done | bytes 1081376 | tf_op jit(solution)/shard_map/ppermute | solution.py:731
  31.7 3.3 %collective-permute-done.refs_2_.refs_5_ = bf16[128,4096]{1,0:T(8,128)(2,1)S(1)} collective-permute-done((bf16[128,4096]{1,0:T(8,128)(2,1)}, bf16[128,4096]{1,0:T(8,128)(2,1)S(1)}, u32[]{:S(2)}, u32[]{:S(2)}) %collective-permute-start) | collective-permute-done | bytes 1048608 | tf_op jit(solution)/shard_map/ppermute | solution.py:747
  37.9 7.6 %fusion.2 = f32[512,1024]{1,0:T(8,128)S(1)} fusion(bf16[512,4096]{1,0:T(8,128)(2,1)S(1)} %copy-done.4, bf16[4096,2048]{1,0:T(8,128)(2,1)} %param.7, s32[]{:T(128)S(6)} %select_n.26), kind=kOutput, calls=%fused_computation.2 | convolution fusion | flops 4294967296 | bytes 14680068 | tf_op jit(solution)/shard_map/dot_general | solution.py:784
  45.5 4.5 %fusion = f32[512,1024]{1,0:T(8,128)S(1)} fusion(bf16[512,4096]{1,0:T(8,128)(2,1)S(1)} %copy-done.4, bf16[4096,2048]{1,0:T(8,128)(2,1)S(1)} %bitcast.11, s32[]{:T(128)S(6)} %select_n.27), kind=kOutput, calls=%fused_computation | convolution fusion | flops 4294967296 | bytes 14680068 | tf_op jit(solution)/shard_map/dot_general | solution.py:784
  50.7 6.3 %collective-permute-done.4.refs_6_.refs_7_ = bf16[128,128]{1,0:T(8,128)(2,1)S(1)} collective-permute-done((bf16[128,128]{1,0:T(8,128)(2,1)}, bf16[128,128]{1,0:T(8,128)(2,1)S(1)}, u32[]{:S(2)}, u32[]{:S(2)}) %collective-permute-start.4) | collective-permute-done | bytes 32800 | tf_op jit(solution)/shard_map/ppermute | solution.py:731
  61.2 2.0 %collective-permute-start.6 = (bf16[64,4096]{1,0:T(8,128)(2,1)S(1)}, bf16[64,4096]{1,0:T(8,128)(2,1)S(1)}, u32[]{:S(2)}, u32[]{:S(2)}) collective-permute-start(bf16[64,4096]{1,0:T(8,128)(2,1)S(1)} %copy-done.7), channel_id=1, source_target_pairs={{4,2},{5,3},{6,0},{7,1},{8,14},{9,15},{10,12},{11,13},{20,18},{21,... | collective-permute-start | bytes 1572872 | tf_op jit(solution)/shard_map/ppermute | solution.py:747
  63.9 10.4 %collective-permute-done.7.refs_4_.refs_7_ = bf16[64,4096]{1,0:T(8,128)(2,1)S(1)} collective-permute-done((bf16[64,4096]{1,0:T(8,128)(2,1)S(1)}, bf16[64,4096]{1,0:T(8,128)(2,1)S(1)}, u32[]{:S(2)}, u32[]{:S(2)}) %collective-permute-start.7) | collective-permute-done | bytes 524320 | tf_op jit(solution)/shard_map/ppermute | solution.py:747
  74.2 2.6 %collective-permute-start.13 = (bf16[64,4096]{1,0:T(8,128)(2,1)S(1)}, bf16[64,4096]{1,0:T(8,128)(2,1)S(1)}, u32[]{:S(2)}, u32[]{:S(2)}) collective-permute-start(bf16[64,4096]{1,0:T(8,128)(2,1)S(1)} %copy-done.6), channel_id=1, source_target_pairs={{4,2},{5,3},{6,0},{7,1},{8,14},{9,15},{10,12},{11,13},{20,18},{21,... | collective-permute-start | bytes 1572872 | tf_op jit(solution)/shard_map/ppermute | solution.py:747
  76.9 9.5 %collective-permute-done.6.refs_5_ = bf16[64,4096]{1,0:T(8,128)(2,1)S(1)} collective-permute-done((bf16[64,4096]{1,0:T(8,128)(2,1)S(1)}, bf16[64,4096]{1,0:T(8,128)(2,1)S(1)}, u32[]{:S(2)}, u32[]{:S(2)}) %collective-permute-start.6) | collective-permute-done | bytes 524320 | tf_op jit(solution)/shard_map/ppermute | solution.py:747
  88.1 2.0 %reduce_own.1 = (f32[128,128]{1,0:T(8,128)S(1)}, f32[256,128]{1,0:T(8,128)S(1)}) custom-call(bf16[128,4224]{1,0:T(8,128)(2,1)S(1)} %copy-done.1, bf16[128,4224]{1,0:T(8,128)(2,1)S(1)} %collective-permute-done.2.refs_1_.refs_4_, bf16[128,4096]{1,0:T(8,128)(2,1)S(1)} %collective-permute-done.refs_2_.refs_5_, ...), custom_call_target="tpu_custom_call" | custom-call | flops 1 | bytes 1 | tf_op jit(solution)/shard_map/reduce_own/pallas_call | solution.py:541
  94.4 3.3 %collective-permute-done.13.refs_6_ = bf16[64,4096]{1,0:T(8,128)(2,1)S(1)} collective-permute-done((bf16[64,4096]{1,0:T(8,128)(2,1)S(1)}, bf16[64,4096]{1,0:T(8,128)(2,1)S(1)}, u32[]{:S(2)}, u32[]{:S(2)}) %collective-permute-start.13) | collective-permute-done | bytes 524320 | tf_op jit(solution)/shard_map/ppermute | solution.py:747
  99.6 2.7 %reduce_taken.1 = (f32[64,128]{1,0:T(8,128)S(1)}, f32[64,128]{1,0:T(8,128)S(1)}, f32[256,128]{1,0:T(8,128)S(1)}) custom-call(bf16[128,4224]{1,0:T(8,128)(2,1)S(1)} %copy-done.1, bf16[128,4224]{1,0:T(8,128)(2,1)S(1)} %collective-permute-done.2.refs_1_.refs_4_, bf16[128,4096]{1,0:T(8,128)(2,1)S(1)} %collective-permute-done.refs_2_.refs_5_, ...), custom_call_target="tpu_custom_call" | custom-call | flops 1 | bytes 1 | tf_op jit(solution)/shard_map/reduce_taken/pallas_call | solution.py:541
  102.7 5.2 %collective-permute-done.9.refs_7_ = bf16[64,4096]{1,0:T(8,128)(2,1)S(1)} collective-permute-done((bf16[64,4096]{1,0:T(8,128)(2,1)S(1)}, bf16[64,4096]{1,0:T(8,128)(2,1)S(1)}, u32[]{:S(2)}, u32[]{:S(2)}) %collective-permute-start.9) | collective-permute-done | bytes 524320 | tf_op jit(solution)/shard_map/ppermute | solution.py:747
  111.0 2.8 %collective-permute-done.20.refs_1_ = bf16[64,1024]{1,0:T(8,128)(2,1)S(1)} collective-permute-done((bf16[64,1024]{1,0:T(8,128)(2,1)S(1)}, bf16[64,1024]{1,0:T(8,128)(2,1)S(1)}, u32[]{:S(2)}, u32[]{:S(2)}) %collective-permute-start.20) | collective-permute-done | bytes 131104 | tf_op jit(solution)/shard_map/ppermute | solution.py:731
  115.2 2.0 %collective-permute-start.22 = (bf16[64,1024]{1,0:T(8,128)(2,1)S(1)}, bf16[64,1024]{1,0:T(8,128)(2,1)S(1)}, u32[]{:S(2)}, u32[]{:S(2)}) collective-permute-start(bf16[64,1024]{1,0:T(8,128)(2,1)S(1)} %get-tuple-element.135), channel_id=1, source_target_pairs={{0,4},{2,6},{4,0},{6,2},{8,12},{10,14},{12,8},{14,10},{1,5},{3,7},... | collective-permute-start | bytes 393224 | tf_op jit(solution)/shard_map/ppermute | solution.py:731
  118.8 2.4 %collective-permute-done.22.refs_4_ = bf16[64,1024]{1,0:T(8,128)(2,1)S(1)} collective-permute-done((bf16[64,1024]{1,0:T(8,128)(2,1)S(1)}, bf16[64,1024]{1,0:T(8,128)(2,1)S(1)}, u32[]{:S(2)}, u32[]{:S(2)}) %collective-permute-start.22) | collective-permute-done | bytes 131104 | tf_op jit(solution)/shard_map/ppermute | solution.py:731
  121.2 2.9 %collective-permute-done.23.refs_5_ = bf16[64,1024]{1,0:T(8,128)(2,1)S(1)} collective-permute-done((bf16[64,1024]{1,0:T(8,128)(2,1)S(1)}, bf16[64,1024]{1,0:T(8,128)(2,1)S(1)}, u32[]{:S(2)}, u32[]{:S(2)}) %collective-permute-start.23) | collective-permute-done | bytes 131104 | tf_op jit(solution)/shard_map/ppermute | solution.py:731
  125.1 1.8 %join.1 = bf16[512,1024]{1,0:T(8,128)(2,1)} custom-call(s32[16]{0:T(128)S(1)} %copy-done.3, f32[512,1024]{1,0:T(8,128)S(1)} %add.14.base_ref, bf16[64,1024]{1,0:T(8,128)(2,1)S(1)} %collective-permute-done.19.refs_0_, bf16[64,1024]{1,0:T(8,128)(2,1)S(1)} %collective-permute-done.20.refs_1_, bf16[64,1024]{1,0:T(8,128)(2,1)S(1)} %get-tuple-element.129.refs_2_, ...), custom_call_target="tpu_custom_call" | custom-call | flops 524288 | bytes 4194304 | tf_op jit(solution)/shard_map/join/pallas_call | solution.py:716
  (76 shorter events, 25.2 us)
Async XLA Ops:
  4.6 27.1 %collective-permute-start.2 = (bf16[128,4224]{1,0:T(8,128)(2,1)}, bf16[128,4224]{1,0:T(8,128)(2,1)S(1)}, u32[]{:S(2)}, u32[]{:S(2)}) collective-permute-start(bf16[128,4224]{1,0:T(8,128)(2,1)} %get-tuple-element.77), channel_id=1, source_target_pairs={{0,2},{2,0},{4,6},{6,4},{8,10},{10,8},{12,14},{14,12},{1,3},{3,1},... | collective-permute-start | bytes 3244040 | tf_op jit(solution)/shard_map/ppermute | solution.py:731
  7.7 27.4 %collective-permute-start = (bf16[128,4096]{1,0:T(8,128)(2,1)}, bf16[128,4096]{1,0:T(8,128)(2,1)S(1)}, u32[]{:S(2)}, u32[]{:S(2)}) collective-permute-start(bf16[128,4096]{1,0:T(8,128)(2,1)} %get-tuple-element.73), channel_id=1, source_target_pairs={{0,4},{1,5},{2,6},{3,7},{12,8},{13,9},{14,10},{15,11},{16,20},{17,... | collective-permute-start | bytes 3145736 | tf_op jit(solution)/shard_map/ppermute | solution.py:747
  9.7 47.9 %collective-permute-start.1 = (bf16[128,4096]{1,0:T(8,128)(2,1)}, bf16[128,4096]{1,0:T(8,128)(2,1)S(1)}, u32[]{:S(2)}, u32[]{:S(2)}) collective-permute-start(bf16[128,4096]{1,0:T(8,128)(2,1)} %get-tuple-element.74), channel_id=1, source_target_pairs={{0,6},{1,7},{2,4},{3,5},{12,10},{13,11},{14,8},{15,9},{16,22},{17,... | collective-permute-start | bytes 3145736 | tf_op jit(solution)/shard_map/ppermute | solution.py:747
  11.8 45.3 %collective-permute-start.4 = (bf16[128,128]{1,0:T(8,128)(2,1)}, bf16[128,128]{1,0:T(8,128)(2,1)S(1)}, u32[]{:S(2)}, u32[]{:S(2)}) collective-permute-start(bf16[128,128]{1,0:T(8,128)(2,1)} %get-tuple-element.83), channel_id=1, source_target_pairs={{0,4},{2,6},{4,0},{6,2},{8,12},{10,14},{12,8},{14,10},{1,5},{3,7},... | collective-permute-start | bytes 98312 | tf_op jit(solution)/shard_map/ppermute | solution.py:731
  12.8 44.9 %collective-permute-start.5 = (bf16[128,128]{1,0:T(8,128)(2,1)}, bf16[128,128]{1,0:T(8,128)(2,1)S(1)}, u32[]{:S(2)}, u32[]{:S(2)}) collective-permute-start(bf16[128,128]{1,0:T(8,128)(2,1)} %get-tuple-element.84), channel_id=1, source_target_pairs={{0,6},{2,4},{4,2},{6,0},{8,14},{10,12},{12,10},{14,8},{1,7},{3,5},... | collective-permute-start | bytes 98312 | tf_op jit(solution)/shard_map/ppermute | solution.py:731
  36.3 21.3 %collective-permute-start.3 = (bf16[64,4224]{1,0:T(8,128)(2,1)S(1)}, bf16[64,4224]{1,0:T(8,128)(2,1)S(1)}, u32[]{:S(2)}, u32[]{:S(2)}) collective-permute-start(bf16[64,4224]{1,0:T(8,128)(2,1)S(1)} %pad_maximum_fusion), channel_id=1, source_target_pairs={{0,16},{1,17},{2,18},{3,19},{12,28},{13,29},{14,30},{15,31},{16,0}... | collective-permute-start | bytes 1622024 | tf_op jit(solution)/shard_map/ppermute | solution.py:747
  50.1 13.1 %collective-permute-start.8 = (bf16[64,4224]{1,0:T(8,128)(2,1)S(1)}, bf16[64,4224]{1,0:T(8,128)(2,1)S(1)}, u32[]{:S(2)}, u32[]{:S(2)}) collective-permute-start(bf16[64,4224]{1,0:T(8,128)(2,1)S(1)} %pad_maximum_fusion.1), channel_id=1, source_target_pairs={{0,16},{1,17},{2,18},{3,19},{12,28},{13,29},{14,30},{15,31},{16,0}... | collective-permute-start | bytes 1622024 | tf_op jit(solution)/shard_map/ppermute | solution.py:747
  57.7 40.7 %collective-permute-start.15 = (f32[512,1024]{1,0:T(8,128)S(1)}, f32[512,1024]{1,0:T(8,128)S(1)}, u32[]{:S(2)}, u32[]{:S(2)}) collective-permute-start(f32[512,1024]{1,0:T(8,128)S(1)} %fusion.2), channel_id=1, source_target_pairs={{0,1},{1,0},{2,3},{3,2},{4,5},{5,4},{6,7},{7,6},{8,9},{9,8},{10,11... | collective-permute-start | bytes 6291464 | tf_op jit(solution)/shard_map/ppermute | solution.py:731
  57.9 30.2 %collective-permute-start.10 = (bf16[64,4224]{1,0:T(8,128)(2,1)S(1)}, bf16[64,4224]{1,0:T(8,128)(2,1)S(1)}, u32[]{:S(2)}, u32[]{:S(2)}) collective-permute-start(bf16[64,4224]{1,0:T(8,128)(2,1)S(1)} %pad_maximum_fusion.2), channel_id=1, source_target_pairs={{0,16},{1,17},{2,18},{3,19},{12,28},{13,29},{14,30},{15,31},{16,0}... | collective-permute-start | bytes 1622024 | tf_op jit(solution)/shard_map/ppermute | solution.py:747
  59.5 14.8 %collective-permute-start.7 = (bf16[64,4096]{1,0:T(8,128)(2,1)S(1)}, bf16[64,4096]{1,0:T(8,128)(2,1)S(1)}, u32[]{:S(2)}, u32[]{:S(2)}) collective-permute-start(bf16[64,4096]{1,0:T(8,128)(2,1)S(1)} %copy-done.8), channel_id=1, source_target_pairs={{4,0},{5,1},{6,2},{7,3},{8,12},{9,13},{10,14},{11,15},{20,16},{21,... | collective-permute-start | bytes 1572872 | tf_op jit(solution)/shard_map/ppermute | solution.py:747
  61.2 25.2 %collective-permute-start.6 = (bf16[64,4096]{1,0:T(8,128)(2,1)S(1)}, bf16[64,4096]{1,0:T(8,128)(2,1)S(1)}, u32[]{:S(2)}, u32[]{:S(2)}) collective-permute-start(bf16[64,4096]{1,0:T(8,128)(2,1)S(1)} %copy-done.7), channel_id=1, source_target_pairs={{4,2},{5,3},{6,0},{7,1},{8,14},{9,15},{10,12},{11,13},{20,18},{21,... | collective-permute-start | bytes 1572872 | tf_op jit(solution)/shard_map/ppermute | solution.py:747
  63.3 29.6 %collective-permute-start.14 = (bf16[64,4224]{1,0:T(8,128)(2,1)S(1)}, bf16[64,4224]{1,0:T(8,128)(2,1)S(1)}, u32[]{:S(2)}, u32[]{:S(2)}) collective-permute-start(bf16[64,4224]{1,0:T(8,128)(2,1)S(1)} %pad_maximum_fusion.3), channel_id=1, source_target_pairs={{0,16},{1,17},{2,18},{3,19},{12,28},{13,29},{14,30},{15,31},{16,0}... | collective-permute-start | bytes 1622024 | tf_op jit(solution)/shard_map/ppermute | solution.py:747
  74.2 23.4 %collective-permute-start.13 = (bf16[64,4096]{1,0:T(8,128)(2,1)S(1)}, bf16[64,4096]{1,0:T(8,128)(2,1)S(1)}, u32[]{:S(2)}, u32[]{:S(2)}) collective-permute-start(bf16[64,4096]{1,0:T(8,128)(2,1)S(1)} %copy-done.6), channel_id=1, source_target_pairs={{4,2},{5,3},{6,0},{7,1},{8,14},{9,15},{10,12},{11,13},{20,18},{21,... | collective-permute-start | bytes 1572872 | tf_op jit(solution)/shard_map/ppermute | solution.py:747
  86.4 21.5 %collective-permute-start.9 = (bf16[64,4096]{1,0:T(8,128)(2,1)S(1)}, bf16[64,4096]{1,0:T(8,128)(2,1)S(1)}, u32[]{:S(2)}, u32[]{:S(2)}) collective-permute-start(bf16[64,4096]{1,0:T(8,128)(2,1)S(1)} %copy-done.5), channel_id=1, source_target_pairs={{4,0},{5,1},{6,2},{7,3},{8,12},{9,13},{10,14},{11,15},{20,16},{21,... | collective-permute-start | bytes 1572872 | tf_op jit(solution)/shard_map/ppermute | solution.py:747
  90.2 1.3 %collective-permute-start.11 = (f32[128,128]{1,0:T(8,128)S(1)}, f32[128,128]{1,0:T(8,128)S(1)}, u32[]{:S(2)}, u32[]{:S(2)}) collective-permute-start(f32[128,128]{1,0:T(8,128)S(1)} %get-tuple-element.104.refs_0_), channel_id=1, source_target_pairs={{0,1},{1,0},{2,3},{3,2},{4,5},{5,4},{6,7},{7,6},{8,9},{9,8},{10,11... | collective-permute-start | bytes 196616 | tf_op jit(solution)/shard_map/ppermute | solution.py:731
  91.5 22.8 %collective-permute-start.21 = (bf16[48,4096]{1,0:T(8,128)(2,1)S(1)}, bf16[48,4096]{1,0:T(8,128)(2,1)S(1)}, u32[]{:S(2)}, u32[]{:S(2)}) collective-permute-start(bf16[48,4096]{1,0:T(8,128)(2,1)S(1)} %slice.54), channel_id=1, source_target_pairs={{4,20},{5,21},{6,22},{7,23},{8,24},{9,25},{10,26},{11,27},{20,4},{... | collective-permute-start | bytes 1179656 | tf_op jit(solution)/shard_map/ppermute | solution.py:747
  92.8 9.9 %collective-permute-start.12 = (bf16[64,1024]{1,0:T(8,128)(2,1)S(1)}, bf16[64,1024]{1,0:T(8,128)(2,1)S(1)}, u32[]{:S(2)}, u32[]{:S(2)}) collective-permute-start(bf16[64,1024]{1,0:T(8,128)(2,1)S(1)} %get-tuple-element.107), channel_id=1, source_target_pairs={{0,2},{2,0},{4,6},{6,4},{8,10},{10,8},{12,14},{14,12},{1,3},{3,1},... | collective-permute-start | bytes 393224 | tf_op jit(solution)/shard_map/ppermute | solution.py:731
  97.7 13.3 %collective-permute-start.19 = (bf16[64,1024]{1,0:T(8,128)(2,1)S(1)}, bf16[64,1024]{1,0:T(8,128)(2,1)S(1)}, u32[]{:S(2)}, u32[]{:S(2)}) collective-permute-start(bf16[64,1024]{1,0:T(8,128)(2,1)S(1)} %get-tuple-element.125), channel_id=1, source_target_pairs={{0,4},{2,6},{4,0},{6,2},{8,12},{10,14},{12,8},{14,10},{1,5},{3,7},... | collective-permute-start | bytes 393224 | tf_op jit(solution)/shard_map/ppermute | solution.py:731
  98.4 15.4 %collective-permute-start.20 = (bf16[64,1024]{1,0:T(8,128)(2,1)S(1)}, bf16[64,1024]{1,0:T(8,128)(2,1)S(1)}, u32[]{:S(2)}, u32[]{:S(2)}) collective-permute-start(bf16[64,1024]{1,0:T(8,128)(2,1)S(1)} %get-tuple-element.126), channel_id=1, source_target_pairs={{0,6},{2,4},{4,2},{6,0},{8,14},{10,12},{12,10},{14,8},{1,7},{3,5},... | collective-permute-start | bytes 393224 | tf_op jit(solution)/shard_map/ppermute | solution.py:731
  109.2 4.6 %collective-permute-start.16 = (f32[64,128]{1,0:T(8,128)S(1)}, f32[64,128]{1,0:T(8,128)S(1)}, u32[]{:S(2)}, u32[]{:S(2)}) collective-permute-start(f32[64,128]{1,0:T(8,128)S(1)} %get-tuple-element.131.refs_0_), channel_id=1, source_target_pairs={{0,1},{1,0},{2,3},{3,2},{4,5},{5,4},{6,7},{7,6},{8,9},{9,8},{10,11... | collective-permute-start | bytes 98312 | tf_op jit(solution)/shard_map/ppermute | solution.py:731
  110.4 3.9 %collective-permute-start.18 = (f32[64,128]{1,0:T(8,128)S(1)}, f32[64,128]{1,0:T(8,128)S(1)}, u32[]{:S(2)}, u32[]{:S(2)}) collective-permute-start(f32[64,128]{1,0:T(8,128)S(1)} %add.15.refs_2_), channel_id=1, source_target_pairs={{0,16},{16,0},{1,17},{17,1},{2,18},{18,2},{3,19},{19,3},{4,20},{20... | collective-permute-start | bytes 98312 | tf_op jit(solution)/shard_map/ppermute | solution.py:731
  115.2 5.9 %collective-permute-start.22 = (bf16[64,1024]{1,0:T(8,128)(2,1)S(1)}, bf16[64,1024]{1,0:T(8,128)(2,1)S(1)}, u32[]{:S(2)}, u32[]{:S(2)}) collective-permute-start(bf16[64,1024]{1,0:T(8,128)(2,1)S(1)} %get-tuple-element.135), channel_id=1, source_target_pairs={{0,4},{2,6},{4,0},{6,2},{8,12},{10,14},{12,8},{14,10},{1,5},{3,7},... | collective-permute-start | bytes 393224 | tf_op jit(solution)/shard_map/ppermute | solution.py:731
  117.2 6.8 %collective-permute-start.23 = (bf16[64,1024]{1,0:T(8,128)(2,1)S(1)}, bf16[64,1024]{1,0:T(8,128)(2,1)S(1)}, u32[]{:S(2)}, u32[]{:S(2)}) collective-permute-start(bf16[64,1024]{1,0:T(8,128)(2,1)S(1)} %get-tuple-element.136), channel_id=1, source_target_pairs={{0,6},{2,4},{4,2},{6,0},{8,14},{10,12},{12,10},{14,8},{1,7},{3,5},... | collective-permute-start | bytes 393224 | tf_op jit(solution)/shard_map/ppermute | solution.py:731
  118.3 6.9 %collective-permute-start.24 = (bf16[64,1024]{1,0:T(8,128)(2,1)S(1)}, bf16[64,1024]{1,0:T(8,128)(2,1)S(1)}, u32[]{:S(2)}, u32[]{:S(2)}) collective-permute-start(bf16[64,1024]{1,0:T(8,128)(2,1)S(1)} %get-tuple-element.138), channel_id=1, source_target_pairs={{0,2},{2,0},{4,6},{6,4},{8,10},{10,8},{12,14},{14,12},{1,3},{3,1},... | collective-permute-start | bytes 393224 | tf_op jit(solution)/shard_map/ppermute | solution.py:731
  (14 other events, 203.4 us)

commit v17 on v16

--- a/solution.py
+++ b/solution.py
@@ -808,18 +808,20 @@
     wide_in, near, across[0], late, tags_in, base_other, base_mine = lax.optimization_barrier(
         (wide_in, near, across[0], late, tags_in, base_other, base_mine)
     )
-    across += [across_send(i) for i in range(2, half)]
     late_in = []
     for unit, d in enumerate(plan.late_blocks()):
         moves = [(plan.inner, 0, d, 0)]
         if unit < plan.pieces:
             moves.append((plan.outer, 0, half, 0))
         block = late[unit]
-        if unit >= 2:
-            late_in[unit - 2], across[1], block = lax.optimization_barrier(
-                (late_in[unit - 2], across[1], block)
+        if unit == 2:
+            late_in[0], across[1], tags_in, block = lax.optimization_barrier(
+                (late_in[0], across[1], tags_in, block)
             )
+        elif unit > 2:
+            late_in[unit - 2], block = lax.optimization_barrier((late_in[unit - 2], block))
         late_in.append(send(plan, block, moves))
+    across += [across_send(i) for i in range(2, half)]
     late_up = late_in[0][: plan.up_rows]
     across_up = [send(plan, late_up, [(plan.inner, e, 0, 0)]) for e in range(1, plan.groups)]
     base = base_mine + swap(base_other, "tensor", 1)

time: 127 us -> 126 us (level)
  waiting for transfers between devices: 61.4 us -> 57.3 us
  starting transfers between devices: 31.5 us -> 34 us
    ppermute x11, waiting for transfers between devices: 31.7 us -> 28.7 us  [send(): return lax.ppermute(value, ('groups', 'replica', 'tensor'), pairs)]
    ppermute x14, starting transfers between devices: 14.4 us -> 16.8 us  [swap(): return lax.ppermute(value, axis, [(i, i ^ distance) for i in range(count)])]
  transfers between devices with their start and end apart: 25 -> 25, of which waited for: 15 -> 18; matrix products, arithmetic and copies ran while one was open for 12% -> 12% of each run, Pallas kernels for 9% -> 9%
where the time goes in v17:
time: 126 us; the launch traced here: 125 us
  waiting for transfers between devices  57.3 us (45%)
  starting transfers between devices  34 us (27%)
  Pallas kernels  18.9 us (15%)
  matrix products  12.1 us (10%)
  other arithmetic  1.79 us (1%)
    ppermute x11, waiting for transfers between devices, send(): return lax.ppermute(value, ('groups', 'replica', 'tensor'), pairs)  28.7 us
    ppermute x14, waiting for transfers between devices, swap(): return lax.ppermute(value, axis, [(i, i ^ distance) for i in range(count)])  28.6 us
    ppermute x11, starting transfers between devices, send(): return lax.ppermute(value, ('groups', 'replica', 'tensor'), pairs)  17.2 us
    ppermute x14, starting transfers between devices, swap(): return lax.ppermute(value, axis, [(i, i ^ distance) for i in range(count)])  16.8 us
    dot_general x2, matrix products, part(): return jnp.dot(rows, columns, preferred_element_type=jnp.float32)  12.1 us
    pallas_call x2, Pallas kernels, lay_out(): pl.pallas_call(functools.partial(lay_kernel, plan, first_call), out_shape...  9.73 us
    pallas_call x4, Pallas kernels, blocks_call(): pl.pallas_call(body, out_shape=out_shape, in_specs=[VMEM] * n_extra + [HB...  6.21 us
  transfers between devices with their start and end apart: 25, of which 18 were waited for; matrix products, arithmetic and copies ran while one was open for 12% of the time, Pallas kernels for 9%

profile of v17, /device:TPU:0, one launch (start us, length us, event | category | flops | bytes accessed | tf_op | source)
XLA Modules:
  0.0 125.3 jit_solution(13918463519289828393)
XLA Ops:
  0.0 4.6 %lay_out_first.1 = (bf16[128,4224]{1,0:T(8,128)(2,1)}, bf16[128,4096]{1,0:T(8,128)(2,1)}, bf16[128,4096]{1,0:T(8,128)(2,1)}, bf16[128,128]{1,0:T(8,128)(2,1)}, bf16[128,128]{1,0:T(8,128)(2,1)}, /*index=5*/s32[16]{0:T(128)}) custom-call(s32[16]{0:T(128)} %ids_ref.2, s32[48]{0:T(128)} %residency_ref.3, bf16[512,4096]{1,0:T(8,128)(2,1)} %x_ref.3, ...), custom_call_target="tpu_custom_call" | custom-call | bytes 2097152 | tf_op jit(solution)/shard_map/lay_out_first/pallas_call | solution.py:225
  4.6 3.0 %collective-permute-start.2 = (bf16[128,4224]{1,0:T(8,128)(2,1)}, bf16[128,4224]{1,0:T(8,128)(2,1)S(1)}, u32[]{:S(2)}, u32[]{:S(2)}) collective-permute-start(bf16[128,4224]{1,0:T(8,128)(2,1)} %get-tuple-element.78), channel_id=1, source_target_pairs={{0,2},{2,0},{4,6},{6,4},{8,10},{10,8},{12,14},{14,12},{1,3},{3,1},... | collective-permute-start | bytes 3244040 | tf_op jit(solution)/shard_map/ppermute | solution.py:731
  7.7 2.1 %collective-permute-start = (bf16[128,4096]{1,0:T(8,128)(2,1)}, bf16[128,4096]{1,0:T(8,128)(2,1)S(1)}, u32[]{:S(2)}, u32[]{:S(2)}) collective-permute-start(bf16[128,4096]{1,0:T(8,128)(2,1)} %get-tuple-element.74), channel_id=1, source_target_pairs={{0,4},{1,5},{2,6},{3,7},{12,8},{13,9},{14,10},{15,11},{16,20},{17,... | collective-permute-start | bytes 3145736 | tf_op jit(solution)/shard_map/ppermute | solution.py:747
  9.7 2.0 %collective-permute-start.1 = (bf16[128,4096]{1,0:T(8,128)(2,1)}, bf16[128,4096]{1,0:T(8,128)(2,1)S(1)}, u32[]{:S(2)}, u32[]{:S(2)}) collective-permute-start(bf16[128,4096]{1,0:T(8,128)(2,1)} %get-tuple-element.75), channel_id=1, source_target_pairs={{0,6},{1,7},{2,4},{3,5},{12,10},{13,11},{14,8},{15,9},{16,22},{17,... | collective-permute-start | bytes 3145736 | tf_op jit(solution)/shard_map/ppermute | solution.py:747
  12.8 2.0 %collective-permute-start.5 = (bf16[128,128]{1,0:T(8,128)(2,1)}, bf16[128,128]{1,0:T(8,128)(2,1)S(1)}, u32[]{:S(2)}, u32[]{:S(2)}) collective-permute-start(bf16[128,128]{1,0:T(8,128)(2,1)} %get-tuple-element.85), channel_id=1, source_target_pairs={{0,6},{2,4},{4,2},{6,0},{8,14},{10,12},{12,10},{14,8},{1,7},{3,5},... | collective-permute-start | bytes 98312 | tf_op jit(solution)/shard_map/ppermute | solution.py:731
  14.7 5.1 %lay_out_second.1 = (bf16[128,4224]{1,0:T(8,128)(2,1)}, bf16[64,4096]{1,0:T(8,128)(2,1)}, bf16[64,4096]{1,0:T(8,128)(2,1)}, bf16[64,4096]{1,0:T(8,128)(2,1)}, bf16[64,4096]{1,0:T(8,128)(2,1)}, /*index=5*/s32[16]{0:T(128)}) custom-call(s32[16]{0:T(128)} %ids_ref.2, s32[48]{0:T(128)} %residency_ref.3, bf16[512,4096]{1,0:T(8,128)(2,1)} %x_ref.3, ...), custom_call_target="tpu_custom_call" | custom-call | bytes 2097152 | tf_op jit(solution)/shard_map/lay_out_second/pallas_call | solution.py:225
  20.6 11.1 %collective-permute-done.2.refs_1_.refs_4_ = bf16[128,4224]{1,0:T(8,128)(2,1)S(1)} collective-permute-done((bf16[128,4224]{1,0:T(8,128)(2,1)}, bf16[128,4224]{1,0:T(8,128)(2,1)S(1)}, u32[]{:S(2)}, u32[]{:S(2)}) %collective-permute-start.2) | collective-permute-done | bytes 1081376 | tf_op jit(solution)/shard_map/ppermute | solution.py:731
  31.7 3.3 %collective-permute-done.refs_2_.refs_5_ = bf16[128,4096]{1,0:T(8,128)(2,1)S(1)} collective-permute-done((bf16[128,4096]{1,0:T(8,128)(2,1)}, bf16[128,4096]{1,0:T(8,128)(2,1)S(1)}, u32[]{:S(2)}, u32[]{:S(2)}) %collective-permute-start) | collective-permute-done | bytes 1048608 | tf_op jit(solution)/shard_map/ppermute | solution.py:747
  37.9 7.6 %fusion.2 = f32[512,1024]{1,0:T(8,128)S(1)} fusion(bf16[512,4096]{1,0:T(8,128)(2,1)S(1)} %copy-done.4, bf16[4096,2048]{1,0:T(8,128)(2,1)} %param.7, s32[]{:T(128)S(6)} %select_n.26), kind=kOutput, calls=%fused_computation.2 | convolution fusion | flops 4294967296 | bytes 14680068 | tf_op jit(solution)/shard_map/dot_general | solution.py:784
  45.5 4.5 %fusion = f32[512,1024]{1,0:T(8,128)S(1)} fusion(bf16[512,4096]{1,0:T(8,128)(2,1)S(1)} %copy-done.4, bf16[4096,2048]{1,0:T(8,128)(2,1)S(1)} %bitcast.11, s32[]{:T(128)S(6)} %select_n.27), kind=kOutput, calls=%fused_computation | convolution fusion | flops 4294967296 | bytes 14680068 | tf_op jit(solution)/shard_map/dot_general | solution.py:784
  50.7 6.4 %collective-permute-done.4.refs_6_.refs_7_ = bf16[128,128]{1,0:T(8,128)(2,1)S(1)} collective-permute-done((bf16[128,128]{1,0:T(8,128)(2,1)}, bf16[128,128]{1,0:T(8,128)(2,1)S(1)}, u32[]{:S(2)}, u32[]{:S(2)}) %collective-permute-start.4) | collective-permute-done | bytes 32800 | tf_op jit(solution)/shard_map/ppermute | solution.py:731
  59.6 2.0 %collective-permute-start.6 = (bf16[64,4096]{1,0:T(8,128)(2,1)S(1)}, bf16[64,4096]{1,0:T(8,128)(2,1)S(1)}, u32[]{:S(2)}, u32[]{:S(2)}) collective-permute-start(bf16[64,4096]{1,0:T(8,128)(2,1)S(1)} %copy-done.7), channel_id=1, source_target_pairs={{4,2},{5,3},{6,0},{7,1},{8,14},{9,15},{10,12},{11,13},{20,18},{21,... | collective-permute-start | bytes 1572872 | tf_op jit(solution)/shard_map/ppermute | solution.py:747
  61.8 10.8 %collective-permute-done.8.refs_4_.refs_7_ = bf16[64,4096]{1,0:T(8,128)(2,1)S(1)} collective-permute-done((bf16[64,4096]{1,0:T(8,128)(2,1)S(1)}, bf16[64,4096]{1,0:T(8,128)(2,1)S(1)}, u32[]{:S(2)}, u32[]{:S(2)}) %collective-permute-start.8) | collective-permute-done | bytes 524320 | tf_op jit(solution)/shard_map/ppermute | solution.py:747
  74.2 2.6 %collective-permute-start.13 = (bf16[64,4096]{1,0:T(8,128)(2,1)S(1)}, bf16[64,4096]{1,0:T(8,128)(2,1)S(1)}, u32[]{:S(2)}, u32[]{:S(2)}) collective-permute-start(bf16[64,4096]{1,0:T(8,128)(2,1)S(1)} %copy-done.6), channel_id=1, source_target_pairs={{4,2},{5,3},{6,0},{7,1},{8,14},{9,15},{10,12},{11,13},{20,18},{21,... | collective-permute-start | bytes 1572872 | tf_op jit(solution)/shard_map/ppermute | solution.py:747
  77.4 7.3 %collective-permute-done.6.refs_5_ = bf16[64,4096]{1,0:T(8,128)(2,1)S(1)} collective-permute-done((bf16[64,4096]{1,0:T(8,128)(2,1)S(1)}, bf16[64,4096]{1,0:T(8,128)(2,1)S(1)}, u32[]{:S(2)}, u32[]{:S(2)}) %collective-permute-start.6) | collective-permute-done | bytes 524320 | tf_op jit(solution)/shard_map/ppermute | solution.py:747
  87.9 2.0 %reduce_own.1 = (f32[128,128]{1,0:T(8,128)S(1)}, f32[256,128]{1,0:T(8,128)S(1)}) custom-call(bf16[128,4224]{1,0:T(8,128)(2,1)S(1)} %copy-done.1, bf16[128,4224]{1,0:T(8,128)(2,1)S(1)} %collective-permute-done.2.refs_1_.refs_4_, bf16[128,4096]{1,0:T(8,128)(2,1)S(1)} %collective-permute-done.refs_2_.refs_5_, ...), custom_call_target="tpu_custom_call" | custom-call | flops 1 | bytes 1 | tf_op jit(solution)/shard_map/reduce_own/pallas_call | solution.py:541
  92.6 3.4 %collective-permute-done.13.refs_6_ = bf16[64,4096]{1,0:T(8,128)(2,1)S(1)} collective-permute-done((bf16[64,4096]{1,0:T(8,128)(2,1)S(1)}, bf16[64,4096]{1,0:T(8,128)(2,1)S(1)}, u32[]{:S(2)}, u32[]{:S(2)}) %collective-permute-start.13) | collective-permute-done | bytes 524320 | tf_op jit(solution)/shard_map/ppermute | solution.py:747
  97.6 3.6 %collective-permute-start.19 = (bf16[64,1024]{1,0:T(8,128)(2,1)S(1)}, bf16[64,1024]{1,0:T(8,128)(2,1)S(1)}, u32[]{:S(2)}, u32[]{:S(2)}) collective-permute-start(bf16[64,1024]{1,0:T(8,128)(2,1)S(1)} %get-tuple-element.127), channel_id=1, source_target_pairs={{0,4},{2,6},{4,0},{6,2},{8,12},{10,14},{12,8},{14,10},{1,5},{3,7},... | collective-permute-start | bytes 393224 | tf_op jit(solution)/shard_map/ppermute | solution.py:731
  102.0 2.7 %reduce_taken.1 = (f32[64,128]{1,0:T(8,128)S(1)}, f32[64,128]{1,0:T(8,128)S(1)}, f32[256,128]{1,0:T(8,128)S(1)}) custom-call(bf16[128,4224]{1,0:T(8,128)(2,1)S(1)} %copy-done.1, bf16[128,4224]{1,0:T(8,128)(2,1)S(1)} %collective-permute-done.2.refs_1_.refs_4_, bf16[128,4096]{1,0:T(8,128)(2,1)S(1)} %collective-permute-done.refs_2_.refs_5_, ...), custom_call_target="tpu_custom_call" | custom-call | flops 1 | bytes 1 | tf_op jit(solution)/shard_map/reduce_taken/pallas_call | solution.py:541
  110.2 2.1 %collective-permute-done.20.refs_1_ = bf16[64,1024]{1,0:T(8,128)(2,1)S(1)} collective-permute-done((bf16[64,1024]{1,0:T(8,128)(2,1)S(1)}, bf16[64,1024]{1,0:T(8,128)(2,1)S(1)}, u32[]{:S(2)}, u32[]{:S(2)}) %collective-permute-start.20) | collective-permute-done | bytes 131104 | tf_op jit(solution)/shard_map/ppermute | solution.py:731
  113.6 2.1 %collective-permute-start.22 = (bf16[64,1024]{1,0:T(8,128)(2,1)S(1)}, bf16[64,1024]{1,0:T(8,128)(2,1)S(1)}, u32[]{:S(2)}, u32[]{:S(2)}) collective-permute-start(bf16[64,1024]{1,0:T(8,128)(2,1)S(1)} %get-tuple-element.137), channel_id=1, source_target_pairs={{0,4},{2,6},{4,0},{6,2},{8,12},{10,14},{12,8},{14,10},{1,5},{3,7},... | collective-permute-start | bytes 393224 | tf_op jit(solution)/shard_map/ppermute | solution.py:731
  117.2 2.3 %collective-permute-done.22.refs_4_ = bf16[64,1024]{1,0:T(8,128)(2,1)S(1)} collective-permute-done((bf16[64,1024]{1,0:T(8,128)(2,1)S(1)}, bf16[64,1024]{1,0:T(8,128)(2,1)S(1)}, u32[]{:S(2)}, u32[]{:S(2)}) %collective-permute-start.22) | collective-permute-done | bytes 131104 | tf_op jit(solution)/shard_map/ppermute | solution.py:731
  119.5 2.9 %collective-permute-done.23.refs_5_ = bf16[64,1024]{1,0:T(8,128)(2,1)S(1)} collective-permute-done((bf16[64,1024]{1,0:T(8,128)(2,1)S(1)}, bf16[64,1024]{1,0:T(8,128)(2,1)S(1)}, u32[]{:S(2)}, u32[]{:S(2)}) %collective-permute-start.23) | collective-permute-done | bytes 131104 | tf_op jit(solution)/shard_map/ppermute | solution.py:731
  123.5 1.8 %join.1 = bf16[512,1024]{1,0:T(8,128)(2,1)} custom-call(s32[16]{0:T(128)S(1)} %copy-done.3, f32[512,1024]{1,0:T(8,128)S(1)} %add.14.base_ref, bf16[64,1024]{1,0:T(8,128)(2,1)S(1)} %collective-permute-done.19.refs_0_, bf16[64,1024]{1,0:T(8,128)(2,1)S(1)} %collective-permute-done.20.refs_1_, bf16[64,1024]{1,0:T(8,128)(2,1)S(1)} %get-tuple-element.131.refs_2_, ...), custom_call_target="tpu_custom_call" | custom-call | flops 524288 | bytes 4194304 | tf_op jit(solution)/shard_map/join/pallas_call | solution.py:716
  (76 shorter events, 27.4 us)
Async XLA Ops:
  4.6 27.1 %collective-permute-start.2 = (bf16[128,4224]{1,0:T(8,128)(2,1)}, bf16[128,4224]{1,0:T(8,128)(2,1)S(1)}, u32[]{:S(2)}, u32[]{:S(2)}) collective-permute-start(bf16[128,4224]{1,0:T(8,128)(2,1)} %get-tuple-element.78), channel_id=1, source_target_pairs={{0,2},{2,0},{4,6},{6,4},{8,10},{10,8},{12,14},{14,12},{1,3},{3,1},... | collective-permute-start | bytes 3244040 | tf_op jit(solution)/shard_map/ppermute | solution.py:731
  7.7 27.4 %collective-permute-start = (bf16[128,4096]{1,0:T(8,128)(2,1)}, bf16[128,4096]{1,0:T(8,128)(2,1)S(1)}, u32[]{:S(2)}, u32[]{:S(2)}) collective-permute-start(bf16[128,4096]{1,0:T(8,128)(2,1)} %get-tuple-element.74), channel_id=1, source_target_pairs={{0,4},{1,5},{2,6},{3,7},{12,8},{13,9},{14,10},{15,11},{16,20},{17,... | collective-permute-start | bytes 3145736 | tf_op jit(solution)/shard_map/ppermute | solution.py:747
  9.7 47.9 %collective-permute-start.1 = (bf16[128,4096]{1,0:T(8,128)(2,1)}, bf16[128,4096]{1,0:T(8,128)(2,1)S(1)}, u32[]{:S(2)}, u32[]{:S(2)}) collective-permute-start(bf16[128,4096]{1,0:T(8,128)(2,1)} %get-tuple-element.75), channel_id=1, source_target_pairs={{0,6},{1,7},{2,4},{3,5},{12,10},{13,11},{14,8},{15,9},{16,22},{17,... | collective-permute-start | bytes 3145736 | tf_op jit(solution)/shard_map/ppermute | solution.py:747
  11.8 45.3 %collective-permute-start.4 = (bf16[128,128]{1,0:T(8,128)(2,1)}, bf16[128,128]{1,0:T(8,128)(2,1)S(1)}, u32[]{:S(2)}, u32[]{:S(2)}) collective-permute-start(bf16[128,128]{1,0:T(8,128)(2,1)} %get-tuple-element.84), channel_id=1, source_target_pairs={{0,4},{2,6},{4,0},{6,2},{8,12},{10,14},{12,8},{14,10},{1,5},{3,7},... | collective-permute-start | bytes 98312 | tf_op jit(solution)/shard_map/ppermute | solution.py:731
  12.8 44.9 %collective-permute-start.5 = (bf16[128,128]{1,0:T(8,128)(2,1)}, bf16[128,128]{1,0:T(8,128)(2,1)S(1)}, u32[]{:S(2)}, u32[]{:S(2)}) collective-permute-start(bf16[128,128]{1,0:T(8,128)(2,1)} %get-tuple-element.85), channel_id=1, source_target_pairs={{0,6},{2,4},{4,2},{6,0},{8,14},{10,12},{12,10},{14,8},{1,7},{3,5},... | collective-permute-start | bytes 98312 | tf_op jit(solution)/shard_map/ppermute | solution.py:731
  36.3 21.3 %collective-permute-start.3 = (bf16[64,4224]{1,0:T(8,128)(2,1)S(1)}, bf16[64,4224]{1,0:T(8,128)(2,1)S(1)}, u32[]{:S(2)}, u32[]{:S(2)}) collective-permute-start(bf16[64,4224]{1,0:T(8,128)(2,1)S(1)} %pad_maximum_fusion), channel_id=1, source_target_pairs={{0,16},{1,17},{2,18},{3,19},{12,28},{13,29},{14,30},{15,31},{16,0}... | collective-permute-start | bytes 1622024 | tf_op jit(solution)/shard_map/ppermute | solution.py:747
  50.1 11.6 %collective-permute-start.9 = (bf16[64,4224]{1,0:T(8,128)(2,1)S(1)}, bf16[64,4224]{1,0:T(8,128)(2,1)S(1)}, u32[]{:S(2)}, u32[]{:S(2)}) collective-permute-start(bf16[64,4224]{1,0:T(8,128)(2,1)S(1)} %pad_maximum_fusion.1), channel_id=1, source_target_pairs={{0,16},{1,17},{2,18},{3,19},{12,28},{13,29},{14,30},{15,31},{16,0}... | collective-permute-start | bytes 1622024 | tf_op jit(solution)/shard_map/ppermute | solution.py:747
  57.7 43.5 %collective-permute-start.15 = (f32[512,1024]{1,0:T(8,128)S(1)}, f32[512,1024]{1,0:T(8,128)S(1)}, u32[]{:S(2)}, u32[]{:S(2)}) collective-permute-start(f32[512,1024]{1,0:T(8,128)S(1)} %fusion.2), channel_id=1, source_target_pairs={{0,1},{1,0},{2,3},{3,2},{4,5},{5,4},{6,7},{7,6},{8,9},{9,8},{10,11... | collective-permute-start | bytes 6291464 | tf_op jit(solution)/shard_map/ppermute | solution.py:731
  57.8 14.8 %collective-permute-start.8 = (bf16[64,4096]{1,0:T(8,128)(2,1)S(1)}, bf16[64,4096]{1,0:T(8,128)(2,1)S(1)}, u32[]{:S(2)}, u32[]{:S(2)}) collective-permute-start(bf16[64,4096]{1,0:T(8,128)(2,1)S(1)} %copy-done.8), channel_id=1, source_target_pairs={{4,0},{5,1},{6,2},{7,3},{8,12},{9,13},{10,14},{11,15},{20,16},{21,... | collective-permute-start | bytes 1572872 | tf_op jit(solution)/shard_map/ppermute | solution.py:747
  59.6 25.2 %collective-permute-start.6 = (bf16[64,4096]{1,0:T(8,128)(2,1)S(1)}, bf16[64,4096]{1,0:T(8,128)(2,1)S(1)}, u32[]{:S(2)}, u32[]{:S(2)}) collective-permute-start(bf16[64,4096]{1,0:T(8,128)(2,1)S(1)} %copy-done.7), channel_id=1, source_target_pairs={{4,2},{5,3},{6,0},{7,1},{8,14},{9,15},{10,12},{11,13},{20,18},{21,... | collective-permute-start | bytes 1572872 | tf_op jit(solution)/shard_map/ppermute | solution.py:747
  72.6 15.3 %collective-permute-start.10 = (bf16[64,4224]{1,0:T(8,128)(2,1)S(1)}, bf16[64,4224]{1,0:T(8,128)(2,1)S(1)}, u32[]{:S(2)}, u32[]{:S(2)}) collective-permute-start(bf16[64,4224]{1,0:T(8,128)(2,1)S(1)} %pad_maximum_fusion.2), channel_id=1, source_target_pairs={{0,16},{1,17},{2,18},{3,19},{12,28},{13,29},{14,30},{15,31},{16,0}... | collective-permute-start | bytes 1622024 | tf_op jit(solution)/shard_map/ppermute | solution.py:747
  74.2 21.8 %collective-permute-start.13 = (bf16[64,4096]{1,0:T(8,128)(2,1)S(1)}, bf16[64,4096]{1,0:T(8,128)(2,1)S(1)}, u32[]{:S(2)}, u32[]{:S(2)}) collective-permute-start(bf16[64,4096]{1,0:T(8,128)(2,1)S(1)} %copy-done.6), channel_id=1, source_target_pairs={{4,2},{5,3},{6,0},{7,1},{8,14},{9,15},{10,12},{11,13},{20,18},{21,... | collective-permute-start | bytes 1572872 | tf_op jit(solution)/shard_map/ppermute | solution.py:747
  76.8 20.8 %collective-permute-start.14 = (bf16[64,4224]{1,0:T(8,128)(2,1)S(1)}, bf16[64,4224]{1,0:T(8,128)(2,1)S(1)}, u32[]{:S(2)}, u32[]{:S(2)}) collective-permute-start(bf16[64,4224]{1,0:T(8,128)(2,1)S(1)} %pad_maximum_fusion.3), channel_id=1, source_target_pairs={{0,16},{1,17},{2,18},{3,19},{12,28},{13,29},{14,30},{15,31},{16,0}... | collective-permute-start | bytes 1622024 | tf_op jit(solution)/shard_map/ppermute | solution.py:747
  84.7 21.5 %collective-permute-start.7 = (bf16[64,4096]{1,0:T(8,128)(2,1)S(1)}, bf16[64,4096]{1,0:T(8,128)(2,1)S(1)}, u32[]{:S(2)}, u32[]{:S(2)}) collective-permute-start(bf16[64,4096]{1,0:T(8,128)(2,1)S(1)} %copy-done.5), channel_id=1, source_target_pairs={{4,0},{5,1},{6,2},{7,3},{8,12},{9,13},{10,14},{11,15},{20,16},{21,... | collective-permute-start | bytes 1572872 | tf_op jit(solution)/shard_map/ppermute | solution.py:747
  89.9 1.3 %collective-permute-start.11 = (f32[128,128]{1,0:T(8,128)S(1)}, f32[128,128]{1,0:T(8,128)S(1)}, u32[]{:S(2)}, u32[]{:S(2)}) collective-permute-start(f32[128,128]{1,0:T(8,128)S(1)} %get-tuple-element.106.refs_0_), channel_id=1, source_target_pairs={{0,1},{1,0},{2,3},{3,2},{4,5},{5,4},{6,7},{7,6},{8,9},{9,8},{10,11... | collective-permute-start | bytes 196616 | tf_op jit(solution)/shard_map/ppermute | solution.py:731
  91.2 21.4 %collective-permute-start.21 = (bf16[48,4096]{1,0:T(8,128)(2,1)S(1)}, bf16[48,4096]{1,0:T(8,128)(2,1)S(1)}, u32[]{:S(2)}, u32[]{:S(2)}) collective-permute-start(bf16[48,4096]{1,0:T(8,128)(2,1)S(1)} %slice.54), channel_id=1, source_target_pairs={{4,20},{5,21},{6,22},{7,23},{8,24},{9,25},{10,26},{11,27},{20,4},{... | collective-permute-start | bytes 1179656 | tf_op jit(solution)/shard_map/ppermute | solution.py:747
  96.0 10.3 %collective-permute-start.12 = (bf16[64,1024]{1,0:T(8,128)(2,1)S(1)}, bf16[64,1024]{1,0:T(8,128)(2,1)S(1)}, u32[]{:S(2)}, u32[]{:S(2)}) collective-permute-start(bf16[64,1024]{1,0:T(8,128)(2,1)S(1)} %get-tuple-element.109), channel_id=1, source_target_pairs={{0,2},{2,0},{4,6},{6,4},{8,10},{10,8},{12,14},{14,12},{1,3},{3,1},... | collective-permute-start | bytes 393224 | tf_op jit(solution)/shard_map/ppermute | solution.py:731
  97.6 12.6 %collective-permute-start.19 = (bf16[64,1024]{1,0:T(8,128)(2,1)S(1)}, bf16[64,1024]{1,0:T(8,128)(2,1)S(1)}, u32[]{:S(2)}, u32[]{:S(2)}) collective-permute-start(bf16[64,1024]{1,0:T(8,128)(2,1)S(1)} %get-tuple-element.127), channel_id=1, source_target_pairs={{0,4},{2,6},{4,0},{6,2},{8,12},{10,14},{12,8},{14,10},{1,5},{3,7},... | collective-permute-start | bytes 393224 | tf_op jit(solution)/shard_map/ppermute | solution.py:731
  101.2 11.1 %collective-permute-start.20 = (bf16[64,1024]{1,0:T(8,128)(2,1)S(1)}, bf16[64,1024]{1,0:T(8,128)(2,1)S(1)}, u32[]{:S(2)}, u32[]{:S(2)}) collective-permute-start(bf16[64,1024]{1,0:T(8,128)(2,1)S(1)} %get-tuple-element.128), channel_id=1, source_target_pairs={{0,6},{2,4},{4,2},{6,0},{8,14},{10,12},{12,10},{14,8},{1,7},{3,5},... | collective-permute-start | bytes 393224 | tf_op jit(solution)/shard_map/ppermute | solution.py:731
  107.5 4.8 %collective-permute-start.16 = (f32[64,128]{1,0:T(8,128)S(1)}, f32[64,128]{1,0:T(8,128)S(1)}, u32[]{:S(2)}, u32[]{:S(2)}) collective-permute-start(f32[64,128]{1,0:T(8,128)S(1)} %get-tuple-element.133.refs_0_), channel_id=1, source_target_pairs={{0,1},{1,0},{2,3},{3,2},{4,5},{5,4},{6,7},{7,6},{8,9},{9,8},{10,11... | collective-permute-start | bytes 98312 | tf_op jit(solution)/shard_map/ppermute | solution.py:731
  108.7 3.9 %collective-permute-start.18 = (f32[64,128]{1,0:T(8,128)S(1)}, f32[64,128]{1,0:T(8,128)S(1)}, u32[]{:S(2)}, u32[]{:S(2)}) collective-permute-start(f32[64,128]{1,0:T(8,128)S(1)} %add.15.refs_2_), channel_id=1, source_target_pairs={{0,16},{16,0},{1,17},{17,1},{2,18},{18,2},{3,19},{19,3},{4,20},{20... | collective-permute-start | bytes 98312 | tf_op jit(solution)/shard_map/ppermute | solution.py:731
  113.6 5.9 %collective-permute-start.22 = (bf16[64,1024]{1,0:T(8,128)(2,1)S(1)}, bf16[64,1024]{1,0:T(8,128)(2,1)S(1)}, u32[]{:S(2)}, u32[]{:S(2)}) collective-permute-start(bf16[64,1024]{1,0:T(8,128)(2,1)S(1)} %get-tuple-element.137), channel_id=1, source_target_pairs={{0,4},{2,6},{4,0},{6,2},{8,12},{10,14},{12,8},{14,10},{1,5},{3,7},... | collective-permute-start | bytes 393224 | tf_op jit(solution)/shard_map/ppermute | solution.py:731
  115.6 6.8 %collective-permute-start.23 = (bf16[64,1024]{1,0:T(8,128)(2,1)S(1)}, bf16[64,1024]{1,0:T(8,128)(2,1)S(1)}, u32[]{:S(2)}, u32[]{:S(2)}) collective-permute-start(bf16[64,1024]{1,0:T(8,128)(2,1)S(1)} %get-tuple-element.138), channel_id=1, source_target_pairs={{0,6},{2,4},{4,2},{6,0},{8,14},{10,12},{12,10},{14,8},{1,7},{3,5},... | collective-permute-start | bytes 393224 | tf_op jit(solution)/shard_map/ppermute | solution.py:731
  116.6 6.9 %collective-permute-start.24 = (bf16[64,1024]{1,0:T(8,128)(2,1)S(1)}, bf16[64,1024]{1,0:T(8,128)(2,1)S(1)}, u32[]{:S(2)}, u32[]{:S(2)}) collective-permute-start(bf16[64,1024]{1,0:T(8,128)(2,1)S(1)} %get-tuple-element.140), channel_id=1, source_target_pairs={{0,2},{2,0},{4,6},{6,4},{8,10},{10,8},{12,14},{14,12},{1,3},{3,1},... | collective-permute-start | bytes 393224 | tf_op jit(solution)/shard_map/ppermute | solution.py:731
  (14 other events, 202.2 us)

commit v18 on v17

--- a/solution.py
+++ b/solution.py
@@ -91,6 +91,34 @@
     outer = am_outer(plan)
     rows_outer = outer if first_call else jnp.logical_not(outer)
 
+    def copy_in(i, source, stage):
+        return pltpu.make_async_copy(source, stage, in_sems.at[i])
+
+    quarter = x_ref.shape[0] // 4
+    x_in = [
+        copy_in(i, x_ref.at[pl.ds(i * quarter, quarter)], staged.at[pl.ds(i * quarter, quarter)])
+        for i in range(4)
+    ]
+    adapters_in = []
+    for slot in range(slots):
+        source = pl.ds(first, share)
+        stage = pl.ds(slot * share, share)
+        n = len(adapters_in)
+        adapters_in.append(copy_in(n, left_ref.at[slot, source], left.at[stage]))
+        adapters_in.append(copy_in(n + 1, up_ref.at[slot, source], up.at[stage]))
+
+    @pl.when(rows_outer)
+    def _():
+        for copy in x_in:
+            copy.start()
+
+    @pl.when(jnp.logical_not(rows_outer))
+    def _():
+        for copy in adapters_in:
+            copy.start()
+
+    scale = 2**16 // slots + 1
+    assert all(a * scale >> 16 == a // slots for a in range(residency_ref.shape[0]))
     for h in range(plan.replicas):
         count_ref[h] = 0
         for p in range(CAP):
@@ -98,9 +126,10 @@
             slot_ref[h * CAP + p] = 0
     for s in range(ids_ref.shape[0]):
         adapter = ids_ref[s]
-        holder = adapter // slots
-        place = holder * CAP + count_ref[holder]
-        count_ref[holder] = count_ref[holder] + 1
+        holder = (adapter * scale) >> 16
+        count = count_ref[holder]
+        place = holder * CAP + count
+        count_ref[holder] = count + 1
         seg_ref[place] = s
         slot_ref[place] = residency_ref[adapter] - holder * slots
     for d in range(half):
@@ -110,18 +139,12 @@
                     (me ^ (d + kind * half)) * CAP + p
                 ]
 
-    def move(moves, tagged):
-        arrivals = []
-        for source, stage, _ in moves:
-            arrivals.append(pltpu.make_async_copy(source, stage, in_sems.at[len(arrivals)]))
-            arrivals[-1].start()
-        departures = []
-
-        def depart(source, target):
-            departures.append(pltpu.make_async_copy(source, target, sems.at[len(departures)]))
-            departures[-1].start()
-
-        written = [(d, kind) for d, kind, _ in tagged]
+    def segment(d, kind, p):
+        seg = jnp.maximum(seg_out[(kind * half + d) * CAP + p], 0)
+        return pl.ds(pl.multiple_of(seg * SEG, SEG), SEG)
+
+    def write_tags(targets):
+        written = [(d, kind) for d, kind, _ in targets]
         if first_call:
             written += [(d, kind) for d in plan.cross for kind in range(2)]
         for d, kind in written:
@@ -130,57 +153,6 @@
                 tags[d, pl.ds((kind * CAP + p) * SEG, SEG), :] = jnp.full(
                     (SEG, LANES), slot, jnp.float32
                 ).astype(tags.dtype)
-        for d, kind, target in tagged:
-            depart(tags.at[d, pl.ds(kind * PAIR, PAIR)], target.at[:, pl.ds(width, LANES)])
-        for d, tag_out in zip(plan.cross, tag_outs):
-            depart(tags.at[d], tag_out)
-        for arrival, (_, stage, target) in zip(arrivals, moves):
-            arrival.wait()
-            if target is not None:
-                for part, place in target:
-                    depart(part, place)
-        for departure in departures:
-            departure.wait()
-
-    def row_moves(targets):
-        moves = []
-        for d, kind, target in targets:
-            for p in range(CAP):
-                seg = jnp.maximum(seg_out[(kind * half + d) * CAP + p], 0)
-                stage = staged.at[pl.ds(((kind * half + d) * CAP + p) * SEG, SEG)]
-                moves.append(
-                    (
-                        x_ref.at[pl.ds(pl.multiple_of(seg * SEG, SEG), SEG)],
-                        stage,
-                        [(stage, target.at[pl.ds(p * SEG, SEG), pl.ds(0, width)])],
-                    )
-                )
-        return moves
-
-    def adapter_moves(target_of):
-        moves = []
-        for slot in range(slots):
-            span = pl.ds(slot * share, share)
-            source = pl.ds(first, share)
-            moves.append((up_ref.at[slot, source], up.at[span], None))
-            moves.append((left_ref.at[slot, source], left.at[span], None))
-        outs = [
-            (
-                up.at[pl.ds(row, rows)],
-                target_of(plan.left_pieces).at[pl.ds(0, rows), pl.ds(column, plan.features)],
-            )
-            for row, rows, column in plan.up_columns()
-        ]
-        outs += [
-            (
-                left.at[pl.ds(piece * PAIR, rows)],
-                target_of(piece).at[pl.ds(0, rows), pl.ds(0, width)],
-            )
-            for piece, rows in plan.left_spans()
-        ]
-        source, stage, _ = moves[-1]
-        moves[-1] = (source, stage, outs)
-        return moves
 
     near_d = plan.near[1:] if first_call else plan.near[:1]
     near_targets = [
@@ -188,30 +160,79 @@
         for i, d in enumerate(near_d)
         for kind in range(2)
     ]
-    if first_call:
-        cross_targets = [
-            (d, kind, of_wide(blocks, 2 * i + kind))
-            for i, d in enumerate(plan.cross)
-            for kind in range(2)
-        ]
-    else:
-        cross_targets = [
-            (d, kind, plan.late_rows(blocks, i, kind))
-            for i, d in enumerate(plan.cross)
-            for kind in range(2)
-        ]
+    cross_targets = [
+        (
+            d,
+            kind,
+            of_wide(blocks, 2 * i + kind) if first_call else plan.late_rows(blocks, i, kind),
+        )
+        for i, d in enumerate(plan.cross)
+        for kind in range(2)
+    ]
+    departures = []
+
+    def depart(source, target):
+        copy = pltpu.make_async_copy(source, target, sems.at[len(departures)])
+        copy.start()
+        departures.append(copy)
+
+    def depart_tags():
+        for d, kind, target in near_targets:
+            depart(tags.at[d, pl.ds(kind * PAIR, PAIR)], target.at[:, pl.ds(width, LANES)])
+        for d, tag_out in zip(plan.cross, tag_outs):
+            depart(tags.at[d], tag_out)
+
+    def finish():
+        for copy in departures:
+            copy.wait()
+        departures.clear()
 
     @pl.when(rows_outer)
     def _():
-        move(row_moves(cross_targets + near_targets), near_targets)
+        write_tags(near_targets)
+        for copy in x_in:
+            copy.wait()
+        for d, kind, target in cross_targets + near_targets:
+            for p in range(CAP):
+                place = target.at[pl.ds(p * SEG, SEG), pl.ds(0, width)]
+                depart(staged.at[segment(d, kind, p)], place)
+        depart_tags()
+        finish()
 
     @pl.when(jnp.logical_not(rows_outer))
     def _():
-        if first_call:
-            adapters = adapter_moves(lambda piece: of_wide(blocks, piece))
-        else:
-            adapters = adapter_moves(lambda piece: late_adapters(blocks, piece, plan))
-        move(adapters + row_moves(near_targets), near_targets)
+        rows_in = []
+        for d, kind, target in near_targets:
+            for p in range(CAP):
+                stage = staged.at[pl.ds(len(rows_in) * SEG, SEG)]
+                copy = copy_in(
+                    len(adapters_in) + len(rows_in), x_ref.at[segment(d, kind, p)], stage
+                )
+                copy.start()
+                place = target.at[pl.ds(p * SEG, SEG), pl.ds(0, width)]
+                rows_in.append((copy, stage, place))
+        write_tags(near_targets)
+        depart_tags()
+        for slot in range(slots):
+            adapters_in[2 * slot].wait()
+            piece, at = divmod(slot * share, PAIR)
+            unit = (
+                of_wide(blocks, piece) if first_call else late_adapters(blocks, piece, plan)
+            )
+            depart(
+                left.at[pl.ds(slot * share, share)],
+                unit.at[pl.ds(at, share), pl.ds(0, width)],
+            )
+        for slot in range(slots):
+            adapters_in[2 * slot + 1].wait()
+        piece = plan.left_pieces
+        unit = of_wide(blocks, piece) if first_call else late_adapters(blocks, piece, plan)
+        for row, rows, column in plan.up_columns():
+            depart(up.at[pl.ds(row, rows)], unit.at[pl.ds(0, rows), pl.ds(column, plan.features)])
+        for copy, stage, place in rows_in:
+            copy.wait()
+            depart(stage, place)
+        finish()
 
 
 def lay_out(plan, first_call, ids, residency, x, left_rows, ups):

time: 126 us -> 126 us (level)
  starting transfers between devices: 34 us -> 35.3 us
  transfers between devices with their start and end apart: 25 -> 25, of which waited for: 18 -> 17; matrix products, arithmetic and copies ran while one was open for 12% -> 12% of each run, Pallas kernels for 9% -> 9%
where the time goes in v18:
time: 126 us
  waiting for transfers between devices  56.4 us (45%)
  starting transfers between devices  35.3 us (28%)
  Pallas kernels  19.4 us (15%)
  matrix products  12.1 us (10%)
  other arithmetic  1.79 us (1%)
    ppermute x14, waiting for transfers between devices, swap(): return lax.ppermute(value, axis, [(i, i ^ distance) for i in range(count)])  28.4 us
    ppermute x11, waiting for transfers between devices, send(): return lax.ppermute(value, ('groups', 'replica', 'tensor'), pairs)  28 us
    ppermute x14, starting transfers between devices, swap(): return lax.ppermute(value, axis, [(i, i ^ distance) for i in range(count)])  17.8 us
    ppermute x11, starting transfers between devices, send(): return lax.ppermute(value, ('groups', 'replica', 'tensor'), pairs)  17.5 us
    dot_general x2, matrix products, part(): return jnp.dot(rows, columns, preferred_element_type=jnp.float32)  12.1 us
    pallas_call x2, Pallas kernels, lay_out(): pl.pallas_call(functools.partial(lay_kernel, plan, first_call), out_shape...  10.2 us
    pallas_call x4, Pallas kernels, blocks_call(): pl.pallas_call(body, out_shape=out_shape, in_specs=[VMEM] * n_extra + [HB...  6.19 us
  transfers between devices with their start and end apart: 25, of which 17 were waited for; matrix products, arithmetic and copies ran while one was open for 12% of the time, Pallas kernels for 9%

profile of v18, /device:TPU:0, one launch (start us, length us, event | category | flops | bytes accessed | tf_op | source)
XLA Modules:
  0.0 126.1 jit_solution(16259923414372536275)
XLA Ops:
  0.0 5.7 %lay_out_first.1 = (bf16[128,4224]{1,0:T(8,128)(2,1)}, bf16[128,4096]{1,0:T(8,128)(2,1)}, bf16[128,4096]{1,0:T(8,128)(2,1)}, bf16[128,128]{1,0:T(8,128)(2,1)}, bf16[128,128]{1,0:T(8,128)(2,1)}, /*index=5*/s32[16]{0:T(128)}) custom-call(s32[16]{0:T(128)} %ids_ref.2, s32[48]{0:T(128)} %residency_ref.3, bf16[512,4096]{1,0:T(8,128)(2,1)} %x_ref.3, ...), custom_call_target="tpu_custom_call" | custom-call | bytes 2097152 | tf_op jit(solution)/shard_map/lay_out_first/pallas_call | solution.py:246
  5.7 3.0 %collective-permute-start.2 = (bf16[128,4224]{1,0:T(8,128)(2,1)}, bf16[128,4224]{1,0:T(8,128)(2,1)S(1)}, u32[]{:S(2)}, u32[]{:S(2)}) collective-permute-start(bf16[128,4224]{1,0:T(8,128)(2,1)} %get-tuple-element.78), channel_id=1, source_target_pairs={{0,2},{2,0},{4,6},{6,4},{8,10},{10,8},{12,14},{14,12},{1,3},{3,1},... | collective-permute-start | bytes 3244040 | tf_op jit(solution)/shard_map/ppermute | solution.py:752
  9.2 3.6 %collective-permute-start.1 = (bf16[128,4096]{1,0:T(8,128)(2,1)}, bf16[128,4096]{1,0:T(8,128)(2,1)S(1)}, u32[]{:S(2)}, u32[]{:S(2)}) collective-permute-start(bf16[128,4096]{1,0:T(8,128)(2,1)} %get-tuple-element.75), channel_id=1, source_target_pairs={{0,6},{1,7},{2,4},{3,5},{12,10},{13,11},{14,8},{15,9},{16,22},{17,... | collective-permute-start | bytes 3145736 | tf_op jit(solution)/shard_map/ppermute | solution.py:768
  12.9 2.9 %collective-permute-start.5 = (bf16[128,128]{1,0:T(8,128)(2,1)}, bf16[128,128]{1,0:T(8,128)(2,1)S(1)}, u32[]{:S(2)}, u32[]{:S(2)}) collective-permute-start(bf16[128,128]{1,0:T(8,128)(2,1)} %get-tuple-element.85), channel_id=1, source_target_pairs={{0,6},{2,4},{4,2},{6,0},{8,14},{10,12},{12,10},{14,8},{1,7},{3,5},... | collective-permute-start | bytes 98312 | tf_op jit(solution)/shard_map/ppermute | solution.py:752
  15.8 4.5 %lay_out_second.1 = (bf16[128,4224]{1,0:T(8,128)(2,1)}, bf16[64,4096]{1,0:T(8,128)(2,1)}, bf16[64,4096]{1,0:T(8,128)(2,1)}, bf16[64,4096]{1,0:T(8,128)(2,1)}, bf16[64,4096]{1,0:T(8,128)(2,1)}, /*index=5*/s32[16]{0:T(128)}) custom-call(s32[16]{0:T(128)} %ids_ref.2, s32[48]{0:T(128)} %residency_ref.3, bf16[512,4096]{1,0:T(8,128)(2,1)} %x_ref.3, ...), custom_call_target="tpu_custom_call" | custom-call | bytes 2097152 | tf_op jit(solution)/shard_map/lay_out_second/pallas_call | solution.py:246
  21.0 11.7 %collective-permute-done.2.refs_1_.refs_4_ = bf16[128,4224]{1,0:T(8,128)(2,1)S(1)} collective-permute-done((bf16[128,4224]{1,0:T(8,128)(2,1)}, bf16[128,4224]{1,0:T(8,128)(2,1)S(1)}, u32[]{:S(2)}, u32[]{:S(2)}) %collective-permute-start.2) | collective-permute-done | bytes 1081376 | tf_op jit(solution)/shard_map/ppermute | solution.py:752
  32.8 3.2 %collective-permute-done.refs_2_.refs_5_ = bf16[128,4096]{1,0:T(8,128)(2,1)S(1)} collective-permute-done((bf16[128,4096]{1,0:T(8,128)(2,1)}, bf16[128,4096]{1,0:T(8,128)(2,1)S(1)}, u32[]{:S(2)}, u32[]{:S(2)}) %collective-permute-start) | collective-permute-done | bytes 1048608 | tf_op jit(solution)/shard_map/ppermute | solution.py:768
  38.8 7.6 %fusion.2 = f32[512,1024]{1,0:T(8,128)S(1)} fusion(bf16[512,4096]{1,0:T(8,128)(2,1)S(1)} %copy-done.4, bf16[4096,2048]{1,0:T(8,128)(2,1)} %param.7, s32[]{:T(128)S(6)} %select_n.26), kind=kOutput, calls=%fused_computation.2 | convolution fusion | flops 4294967296 | bytes 14680068 | tf_op jit(solution)/shard_map/dot_general | solution.py:805
  46.5 4.5 %fusion = f32[512,1024]{1,0:T(8,128)S(1)} fusion(bf16[512,4096]{1,0:T(8,128)(2,1)S(1)} %copy-done.4, bf16[4096,2048]{1,0:T(8,128)(2,1)S(1)} %bitcast.11, s32[]{:T(128)S(6)} %select_n.27), kind=kOutput, calls=%fused_computation | convolution fusion | flops 4294967296 | bytes 14680068 | tf_op jit(solution)/shard_map/dot_general | solution.py:805
  51.7 6.0 %collective-permute-done.4.refs_6_.refs_7_ = bf16[128,128]{1,0:T(8,128)(2,1)S(1)} collective-permute-done((bf16[128,128]{1,0:T(8,128)(2,1)}, bf16[128,128]{1,0:T(8,128)(2,1)S(1)}, u32[]{:S(2)}, u32[]{:S(2)}) %collective-permute-start.4) | collective-permute-done | bytes 32800 | tf_op jit(solution)/shard_map/ppermute | solution.py:752
  58.2 1.7 %collective-permute-start.8 = (bf16[64,4096]{1,0:T(8,128)(2,1)S(1)}, bf16[64,4096]{1,0:T(8,128)(2,1)S(1)}, u32[]{:S(2)}, u32[]{:S(2)}) collective-permute-start(bf16[64,4096]{1,0:T(8,128)(2,1)S(1)} %copy-done.8), channel_id=1, source_target_pairs={{4,0},{5,1},{6,2},{7,3},{8,12},{9,13},{10,14},{11,15},{20,16},{21,... | collective-permute-start | bytes 1572872 | tf_op jit(solution)/shard_map/ppermute | solution.py:768
  60.0 2.6 %collective-permute-start.6 = (bf16[64,4096]{1,0:T(8,128)(2,1)S(1)}, bf16[64,4096]{1,0:T(8,128)(2,1)S(1)}, u32[]{:S(2)}, u32[]{:S(2)}) collective-permute-start(bf16[64,4096]{1,0:T(8,128)(2,1)S(1)} %copy-done.7), channel_id=1, source_target_pairs={{4,2},{5,3},{6,0},{7,1},{8,14},{9,15},{10,12},{11,13},{20,18},{21,... | collective-permute-start | bytes 1572872 | tf_op jit(solution)/shard_map/ppermute | solution.py:768
  62.7 10.3 %collective-permute-done.8.refs_4_.refs_7_ = bf16[64,4096]{1,0:T(8,128)(2,1)S(1)} collective-permute-done((bf16[64,4096]{1,0:T(8,128)(2,1)S(1)}, bf16[64,4096]{1,0:T(8,128)(2,1)S(1)}, u32[]{:S(2)}, u32[]{:S(2)}) %collective-permute-start.8) | collective-permute-done | bytes 524320 | tf_op jit(solution)/shard_map/ppermute | solution.py:768
  74.8 2.4 %collective-permute-start.13 = (bf16[64,4096]{1,0:T(8,128)(2,1)S(1)}, bf16[64,4096]{1,0:T(8,128)(2,1)S(1)}, u32[]{:S(2)}, u32[]{:S(2)}) collective-permute-start(bf16[64,4096]{1,0:T(8,128)(2,1)S(1)} %copy-done.6), channel_id=1, source_target_pairs={{4,2},{5,3},{6,0},{7,1},{8,14},{9,15},{10,12},{11,13},{20,18},{21,... | collective-permute-start | bytes 1572872 | tf_op jit(solution)/shard_map/ppermute | solution.py:768
  77.8 7.5 %collective-permute-done.6.refs_5_ = bf16[64,4096]{1,0:T(8,128)(2,1)S(1)} collective-permute-done((bf16[64,4096]{1,0:T(8,128)(2,1)S(1)}, bf16[64,4096]{1,0:T(8,128)(2,1)S(1)}, u32[]{:S(2)}, u32[]{:S(2)}) %collective-permute-start.6) | collective-permute-done | bytes 524320 | tf_op jit(solution)/shard_map/ppermute | solution.py:768
  88.3 2.0 %reduce_own.1 = (f32[128,128]{1,0:T(8,128)S(1)}, f32[256,128]{1,0:T(8,128)S(1)}) custom-call(bf16[128,4224]{1,0:T(8,128)(2,1)S(1)} %copy-done.1, bf16[128,4224]{1,0:T(8,128)(2,1)S(1)} %collective-permute-done.2.refs_1_.refs_4_, bf16[128,4096]{1,0:T(8,128)(2,1)S(1)} %collective-permute-done.refs_2_.refs_5_, ...), custom_call_target="tpu_custom_call" | custom-call | flops 1 | bytes 1 | tf_op jit(solution)/shard_map/reduce_own/pallas_call | solution.py:562
  93.0 3.6 %collective-permute-done.13.refs_6_ = bf16[64,4096]{1,0:T(8,128)(2,1)S(1)} collective-permute-done((bf16[64,4096]{1,0:T(8,128)(2,1)S(1)}, bf16[64,4096]{1,0:T(8,128)(2,1)S(1)}, u32[]{:S(2)}, u32[]{:S(2)}) %collective-permute-start.13) | collective-permute-done | bytes 524320 | tf_op jit(solution)/shard_map/ppermute | solution.py:768
  98.1 4.2 %collective-permute-start.19 = (bf16[64,1024]{1,0:T(8,128)(2,1)S(1)}, bf16[64,1024]{1,0:T(8,128)(2,1)S(1)}, u32[]{:S(2)}, u32[]{:S(2)}) collective-permute-start(bf16[64,1024]{1,0:T(8,128)(2,1)S(1)} %get-tuple-element.127), channel_id=1, source_target_pairs={{0,4},{2,6},{4,0},{6,2},{8,12},{10,14},{12,8},{14,10},{1,5},{3,7},... | collective-permute-start | bytes 393224 | tf_op jit(solution)/shard_map/ppermute | solution.py:752
  102.9 2.7 %reduce_taken.1 = (f32[64,128]{1,0:T(8,128)S(1)}, f32[64,128]{1,0:T(8,128)S(1)}, f32[256,128]{1,0:T(8,128)S(1)}) custom-call(bf16[128,4224]{1,0:T(8,128)(2,1)S(1)} %copy-done.1, bf16[128,4224]{1,0:T(8,128)(2,1)S(1)} %collective-permute-done.2.refs_1_.refs_4_, bf16[128,4096]{1,0:T(8,128)(2,1)S(1)} %collective-permute-done.refs_2_.refs_5_, ...), custom_call_target="tpu_custom_call" | custom-call | flops 1 | bytes 1 | tf_op jit(solution)/shard_map/reduce_taken/pallas_call | solution.py:562
  110.8 2.1 %collective-permute-done.20.refs_1_ = bf16[64,1024]{1,0:T(8,128)(2,1)S(1)} collective-permute-done((bf16[64,1024]{1,0:T(8,128)(2,1)S(1)}, bf16[64,1024]{1,0:T(8,128)(2,1)S(1)}, u32[]{:S(2)}, u32[]{:S(2)}) %collective-permute-start.20) | collective-permute-done | bytes 131104 | tf_op jit(solution)/shard_map/ppermute | solution.py:752
  114.0 2.7 %collective-permute-start.22 = (bf16[64,1024]{1,0:T(8,128)(2,1)S(1)}, bf16[64,1024]{1,0:T(8,128)(2,1)S(1)}, u32[]{:S(2)}, u32[]{:S(2)}) collective-permute-start(bf16[64,1024]{1,0:T(8,128)(2,1)S(1)} %get-tuple-element.137), channel_id=1, source_target_pairs={{0,4},{2,6},{4,0},{6,2},{8,12},{10,14},{12,8},{14,10},{1,5},{3,7},... | collective-permute-start | bytes 393224 | tf_op jit(solution)/shard_map/ppermute | solution.py:752
  118.2 2.5 %collective-permute-done.22.refs_4_ = bf16[64,1024]{1,0:T(8,128)(2,1)S(1)} collective-permute-done((bf16[64,1024]{1,0:T(8,128)(2,1)S(1)}, bf16[64,1024]{1,0:T(8,128)(2,1)S(1)}, u32[]{:S(2)}, u32[]{:S(2)}) %collective-permute-start.22) | collective-permute-done | bytes 131104 | tf_op jit(solution)/shard_map/ppermute | solution.py:752
  120.7 2.4 %collective-permute-done.23.refs_5_ = bf16[64,1024]{1,0:T(8,128)(2,1)S(1)} collective-permute-done((bf16[64,1024]{1,0:T(8,128)(2,1)S(1)}, bf16[64,1024]{1,0:T(8,128)(2,1)S(1)}, u32[]{:S(2)}, u32[]{:S(2)}) %collective-permute-start.23) | collective-permute-done | bytes 131104 | tf_op jit(solution)/shard_map/ppermute | solution.py:752
  124.3 1.8 %join.1 = bf16[512,1024]{1,0:T(8,128)(2,1)} custom-call(s32[16]{0:T(128)S(1)} %copy-done.3, f32[512,1024]{1,0:T(8,128)S(1)} %add.14.base_ref, bf16[64,1024]{1,0:T(8,128)(2,1)S(1)} %collective-permute-done.19.refs_0_, bf16[64,1024]{1,0:T(8,128)(2,1)S(1)} %collective-permute-done.20.refs_1_, bf16[64,1024]{1,0:T(8,128)(2,1)S(1)} %get-tuple-element.131.refs_2_, ...), custom_call_target="tpu_custom_call" | custom-call | flops 524288 | bytes 4194304 | tf_op jit(solution)/shard_map/join/pallas_call | solution.py:737
  (76 shorter events, 24.3 us)
Async XLA Ops:
  5.7 27.1 %collective-permute-start.2 = (bf16[128,4224]{1,0:T(8,128)(2,1)}, bf16[128,4224]{1,0:T(8,128)(2,1)S(1)}, u32[]{:S(2)}, u32[]{:S(2)}) collective-permute-start(bf16[128,4224]{1,0:T(8,128)(2,1)} %get-tuple-element.78), channel_id=1, source_target_pairs={{0,2},{2,0},{4,6},{6,4},{8,10},{10,8},{12,14},{14,12},{1,3},{3,1},... | collective-permute-start | bytes 3244040 | tf_op jit(solution)/shard_map/ppermute | solution.py:752
  8.7 27.3 %collective-permute-start = (bf16[128,4096]{1,0:T(8,128)(2,1)}, bf16[128,4096]{1,0:T(8,128)(2,1)S(1)}, u32[]{:S(2)}, u32[]{:S(2)}) collective-permute-start(bf16[128,4096]{1,0:T(8,128)(2,1)} %get-tuple-element.74), channel_id=1, source_target_pairs={{0,4},{1,5},{2,6},{3,7},{12,8},{13,9},{14,10},{15,11},{16,20},{17,... | collective-permute-start | bytes 3145736 | tf_op jit(solution)/shard_map/ppermute | solution.py:768
  9.2 48.9 %collective-permute-start.1 = (bf16[128,4096]{1,0:T(8,128)(2,1)}, bf16[128,4096]{1,0:T(8,128)(2,1)S(1)}, u32[]{:S(2)}, u32[]{:S(2)}) collective-permute-start(bf16[128,4096]{1,0:T(8,128)(2,1)} %get-tuple-element.75), channel_id=1, source_target_pairs={{0,6},{1,7},{2,4},{3,5},{12,10},{13,11},{14,8},{15,9},{16,22},{17,... | collective-permute-start | bytes 3145736 | tf_op jit(solution)/shard_map/ppermute | solution.py:768
  12.8 44.9 %collective-permute-start.4 = (bf16[128,128]{1,0:T(8,128)(2,1)}, bf16[128,128]{1,0:T(8,128)(2,1)S(1)}, u32[]{:S(2)}, u32[]{:S(2)}) collective-permute-start(bf16[128,128]{1,0:T(8,128)(2,1)} %get-tuple-element.84), channel_id=1, source_target_pairs={{0,4},{2,6},{4,0},{6,2},{8,12},{10,14},{12,8},{14,10},{1,5},{3,7},... | collective-permute-start | bytes 98312 | tf_op jit(solution)/shard_map/ppermute | solution.py:752
  12.9 45.2 %collective-permute-start.5 = (bf16[128,128]{1,0:T(8,128)(2,1)}, bf16[128,128]{1,0:T(8,128)(2,1)S(1)}, u32[]{:S(2)}, u32[]{:S(2)}) collective-permute-start(bf16[128,128]{1,0:T(8,128)(2,1)} %get-tuple-element.85), channel_id=1, source_target_pairs={{0,6},{2,4},{4,2},{6,0},{8,14},{10,12},{12,10},{14,8},{1,7},{3,5},... | collective-permute-start | bytes 98312 | tf_op jit(solution)/shard_map/ppermute | solution.py:752
  37.2 20.9 %collective-permute-start.3 = (bf16[64,4224]{1,0:T(8,128)(2,1)S(1)}, bf16[64,4224]{1,0:T(8,128)(2,1)S(1)}, u32[]{:S(2)}, u32[]{:S(2)}) collective-permute-start(bf16[64,4224]{1,0:T(8,128)(2,1)S(1)} %pad_maximum_fusion), channel_id=1, source_target_pairs={{0,16},{1,17},{2,18},{3,19},{12,28},{13,29},{14,30},{15,31},{16,0}... | collective-permute-start | bytes 1622024 | tf_op jit(solution)/shard_map/ppermute | solution.py:768
  51.1 11.6 %collective-permute-start.9 = (bf16[64,4224]{1,0:T(8,128)(2,1)S(1)}, bf16[64,4224]{1,0:T(8,128)(2,1)S(1)}, u32[]{:S(2)}, u32[]{:S(2)}) collective-permute-start(bf16[64,4224]{1,0:T(8,128)(2,1)S(1)} %pad_maximum_fusion.1), channel_id=1, source_target_pairs={{0,16},{1,17},{2,18},{3,19},{12,28},{13,29},{14,30},{15,31},{16,0}... | collective-permute-start | bytes 1622024 | tf_op jit(solution)/shard_map/ppermute | solution.py:768
  58.1 44.1 %collective-permute-start.15 = (f32[512,1024]{1,0:T(8,128)S(1)}, f32[512,1024]{1,0:T(8,128)S(1)}, u32[]{:S(2)}, u32[]{:S(2)}) collective-permute-start(f32[512,1024]{1,0:T(8,128)S(1)} %fusion.2), channel_id=1, source_target_pairs={{0,1},{1,0},{2,3},{3,2},{4,5},{5,4},{6,7},{7,6},{8,9},{9,8},{10,11... | collective-permute-start | bytes 6291464 | tf_op jit(solution)/shard_map/ppermute | solution.py:752
  58.2 14.8 %collective-permute-start.8 = (bf16[64,4096]{1,0:T(8,128)(2,1)S(1)}, bf16[64,4096]{1,0:T(8,128)(2,1)S(1)}, u32[]{:S(2)}, u32[]{:S(2)}) collective-permute-start(bf16[64,4096]{1,0:T(8,128)(2,1)S(1)} %copy-done.8), channel_id=1, source_target_pairs={{4,0},{5,1},{6,2},{7,3},{8,12},{9,13},{10,14},{11,15},{20,16},{21,... | collective-permute-start | bytes 1572872 | tf_op jit(solution)/shard_map/ppermute | solution.py:768
  60.0 25.4 %collective-permute-start.6 = (bf16[64,4096]{1,0:T(8,128)(2,1)S(1)}, bf16[64,4096]{1,0:T(8,128)(2,1)S(1)}, u32[]{:S(2)}, u32[]{:S(2)}) collective-permute-start(bf16[64,4096]{1,0:T(8,128)(2,1)S(1)} %copy-done.7), channel_id=1, source_target_pairs={{4,2},{5,3},{6,0},{7,1},{8,14},{9,15},{10,12},{11,13},{20,18},{21,... | collective-permute-start | bytes 1572872 | tf_op jit(solution)/shard_map/ppermute | solution.py:768
  73.1 15.3 %collective-permute-start.10 = (bf16[64,4224]{1,0:T(8,128)(2,1)S(1)}, bf16[64,4224]{1,0:T(8,128)(2,1)S(1)}, u32[]{:S(2)}, u32[]{:S(2)}) collective-permute-start(bf16[64,4224]{1,0:T(8,128)(2,1)S(1)} %pad_maximum_fusion.2), channel_id=1, source_target_pairs={{0,16},{1,17},{2,18},{3,19},{12,28},{13,29},{14,30},{15,31},{16,0}... | collective-permute-start | bytes 1622024 | tf_op jit(solution)/shard_map/ppermute | solution.py:768
  74.8 21.8 %collective-permute-start.13 = (bf16[64,4096]{1,0:T(8,128)(2,1)S(1)}, bf16[64,4096]{1,0:T(8,128)(2,1)S(1)}, u32[]{:S(2)}, u32[]{:S(2)}) collective-permute-start(bf16[64,4096]{1,0:T(8,128)(2,1)S(1)} %copy-done.6), channel_id=1, source_target_pairs={{4,2},{5,3},{6,0},{7,1},{8,14},{9,15},{10,12},{11,13},{20,18},{21,... | collective-permute-start | bytes 1572872 | tf_op jit(solution)/shard_map/ppermute | solution.py:768
  77.2 20.8 %collective-permute-start.14 = (bf16[64,4224]{1,0:T(8,128)(2,1)S(1)}, bf16[64,4224]{1,0:T(8,128)(2,1)S(1)}, u32[]{:S(2)}, u32[]{:S(2)}) collective-permute-start(bf16[64,4224]{1,0:T(8,128)(2,1)S(1)} %pad_maximum_fusion.3), channel_id=1, source_target_pairs={{0,16},{1,17},{2,18},{3,19},{12,28},{13,29},{14,30},{15,31},{16,0}... | collective-permute-start | bytes 1622024 | tf_op jit(solution)/shard_map/ppermute | solution.py:768
  85.4 21.4 %collective-permute-start.7 = (bf16[64,4096]{1,0:T(8,128)(2,1)S(1)}, bf16[64,4096]{1,0:T(8,128)(2,1)S(1)}, u32[]{:S(2)}, u32[]{:S(2)}) collective-permute-start(bf16[64,4096]{1,0:T(8,128)(2,1)S(1)} %copy-done.5), channel_id=1, source_target_pairs={{4,0},{5,1},{6,2},{7,3},{8,12},{9,13},{10,14},{11,15},{20,16},{21,... | collective-permute-start | bytes 1572872 | tf_op jit(solution)/shard_map/ppermute | solution.py:768
  90.4 1.3 %collective-permute-start.11 = (f32[128,128]{1,0:T(8,128)S(1)}, f32[128,128]{1,0:T(8,128)S(1)}, u32[]{:S(2)}, u32[]{:S(2)}) collective-permute-start(f32[128,128]{1,0:T(8,128)S(1)} %get-tuple-element.106.refs_0_), channel_id=1, source_target_pairs={{0,1},{1,0},{2,3},{3,2},{4,5},{5,4},{6,7},{7,6},{8,9},{9,8},{10,11... | collective-permute-start | bytes 196616 | tf_op jit(solution)/shard_map/ppermute | solution.py:752
  91.7 21.4 %collective-permute-start.21 = (bf16[48,4096]{1,0:T(8,128)(2,1)S(1)}, bf16[48,4096]{1,0:T(8,128)(2,1)S(1)}, u32[]{:S(2)}, u32[]{:S(2)}) collective-permute-start(bf16[48,4096]{1,0:T(8,128)(2,1)S(1)} %slice.54), channel_id=1, source_target_pairs={{4,20},{5,21},{6,22},{7,23},{8,24},{9,25},{10,26},{11,27},{20,4},{... | collective-permute-start | bytes 1179656 | tf_op jit(solution)/shard_map/ppermute | solution.py:768
  96.6 10.1 %collective-permute-start.12 = (bf16[64,1024]{1,0:T(8,128)(2,1)S(1)}, bf16[64,1024]{1,0:T(8,128)(2,1)S(1)}, u32[]{:S(2)}, u32[]{:S(2)}) collective-permute-start(bf16[64,1024]{1,0:T(8,128)(2,1)S(1)} %get-tuple-element.109), channel_id=1, source_target_pairs={{0,2},{2,0},{4,6},{6,4},{8,10},{10,8},{12,14},{14,12},{1,3},{3,1},... | collective-permute-start | bytes 393224 | tf_op jit(solution)/shard_map/ppermute | solution.py:752
  98.1 12.8 %collective-permute-start.19 = (bf16[64,1024]{1,0:T(8,128)(2,1)S(1)}, bf16[64,1024]{1,0:T(8,128)(2,1)S(1)}, u32[]{:S(2)}, u32[]{:S(2)}) collective-permute-start(bf16[64,1024]{1,0:T(8,128)(2,1)S(1)} %get-tuple-element.127), channel_id=1, source_target_pairs={{0,4},{2,6},{4,0},{6,2},{8,12},{10,14},{12,8},{14,10},{1,5},{3,7},... | collective-permute-start | bytes 393224 | tf_op jit(solution)/shard_map/ppermute | solution.py:752
  102.3 10.7 %collective-permute-start.20 = (bf16[64,1024]{1,0:T(8,128)(2,1)S(1)}, bf16[64,1024]{1,0:T(8,128)(2,1)S(1)}, u32[]{:S(2)}, u32[]{:S(2)}) collective-permute-start(bf16[64,1024]{1,0:T(8,128)(2,1)S(1)} %get-tuple-element.128), channel_id=1, source_target_pairs={{0,6},{2,4},{4,2},{6,0},{8,14},{10,12},{12,10},{14,8},{1,7},{3,5},... | collective-permute-start | bytes 393224 | tf_op jit(solution)/shard_map/ppermute | solution.py:752
  108.0 5.0 %collective-permute-start.16 = (f32[64,128]{1,0:T(8,128)S(1)}, f32[64,128]{1,0:T(8,128)S(1)}, u32[]{:S(2)}, u32[]{:S(2)}) collective-permute-start(f32[64,128]{1,0:T(8,128)S(1)} %get-tuple-element.133.refs_0_), channel_id=1, source_target_pairs={{0,1},{1,0},{2,3},{3,2},{4,5},{5,4},{6,7},{7,6},{8,9},{9,8},{10,11... | collective-permute-start | bytes 98312 | tf_op jit(solution)/shard_map/ppermute | solution.py:752
  109.2 3.9 %collective-permute-start.18 = (f32[64,128]{1,0:T(8,128)S(1)}, f32[64,128]{1,0:T(8,128)S(1)}, u32[]{:S(2)}, u32[]{:S(2)}) collective-permute-start(f32[64,128]{1,0:T(8,128)S(1)} %add.15.refs_2_), channel_id=1, source_target_pairs={{0,16},{16,0},{1,17},{17,1},{2,18},{18,2},{3,19},{19,3},{4,20},{20... | collective-permute-start | bytes 98312 | tf_op jit(solution)/shard_map/ppermute | solution.py:752
  114.0 6.7 %collective-permute-start.22 = (bf16[64,1024]{1,0:T(8,128)(2,1)S(1)}, bf16[64,1024]{1,0:T(8,128)(2,1)S(1)}, u32[]{:S(2)}, u32[]{:S(2)}) collective-permute-start(bf16[64,1024]{1,0:T(8,128)(2,1)S(1)} %get-tuple-element.137), channel_id=1, source_target_pairs={{0,4},{2,6},{4,0},{6,2},{8,12},{10,14},{12,8},{14,10},{1,5},{3,7},... | collective-permute-start | bytes 393224 | tf_op jit(solution)/shard_map/ppermute | solution.py:752
  116.7 6.5 %collective-permute-start.23 = (bf16[64,1024]{1,0:T(8,128)(2,1)S(1)}, bf16[64,1024]{1,0:T(8,128)(2,1)S(1)}, u32[]{:S(2)}, u32[]{:S(2)}) collective-permute-start(bf16[64,1024]{1,0:T(8,128)(2,1)S(1)} %get-tuple-element.138), channel_id=1, source_target_pairs={{0,6},{2,4},{4,2},{6,0},{8,14},{10,12},{12,10},{14,8},{1,7},{3,5},... | collective-permute-start | bytes 393224 | tf_op jit(solution)/shard_map/ppermute | solution.py:752
  117.4 6.9 %collective-permute-start.24 = (bf16[64,1024]{1,0:T(8,128)(2,1)S(1)}, bf16[64,1024]{1,0:T(8,128)(2,1)S(1)}, u32[]{:S(2)}, u32[]{:S(2)}) collective-permute-start(bf16[64,1024]{1,0:T(8,128)(2,1)S(1)} %get-tuple-element.140), channel_id=1, source_target_pairs={{0,2},{2,0},{4,6},{6,4},{8,10},{10,8},{12,14},{14,12},{1,3},{3,1},... | collective-permute-start | bytes 393224 | tf_op jit(solution)/shard_map/ppermute | solution.py:752
  (14 other events, 201.3 us)

commit v19 on v18

--- a/solution.py
+++ b/solution.py
@@ -94,11 +94,6 @@
     def copy_in(i, source, stage):
         return pltpu.make_async_copy(source, stage, in_sems.at[i])
 
-    quarter = x_ref.shape[0] // 4
-    x_in = [
-        copy_in(i, x_ref.at[pl.ds(i * quarter, quarter)], staged.at[pl.ds(i * quarter, quarter)])
-        for i in range(4)
-    ]
     adapters_in = []
     for slot in range(slots):
         source = pl.ds(first, share)
@@ -106,11 +101,6 @@
         n = len(adapters_in)
         adapters_in.append(copy_in(n, left_ref.at[slot, source], left.at[stage]))
         adapters_in.append(copy_in(n + 1, up_ref.at[slot, source], up.at[stage]))
-
-    @pl.when(rows_outer)
-    def _():
-        for copy in x_in:
-            copy.start()
 
     @pl.when(jnp.logical_not(rows_outer))
     def _():
@@ -187,22 +177,9 @@
             copy.wait()
         departures.clear()
 
-    @pl.when(rows_outer)
-    def _():
-        write_tags(near_targets)
-        for copy in x_in:
-            copy.wait()
-        for d, kind, target in cross_targets + near_targets:
-            for p in range(CAP):
-                place = target.at[pl.ds(p * SEG, SEG), pl.ds(0, width)]
-                depart(staged.at[segment(d, kind, p)], place)
-        depart_tags()
-        finish()
-
-    @pl.when(jnp.logical_not(rows_outer))
-    def _():
+    def start_rows(targets):
         rows_in = []
-        for d, kind, target in near_targets:
+        for d, kind, target in targets:
             for p in range(CAP):
                 stage = staged.at[pl.ds(len(rows_in) * SEG, SEG)]
                 copy = copy_in(
@@ -211,6 +188,24 @@
                 copy.start()
                 place = target.at[pl.ds(p * SEG, SEG), pl.ds(0, width)]
                 rows_in.append((copy, stage, place))
+        return rows_in
+
+    def depart_rows(rows_in):
+        for copy, stage, place in rows_in:
+            copy.wait()
+            depart(stage, place)
+        finish()
+
+    @pl.when(rows_outer)
+    def _():
+        rows_in = start_rows(cross_targets + near_targets)
+        write_tags(near_targets)
+        depart_tags()
+        depart_rows(rows_in)
+
+    @pl.when(jnp.logical_not(rows_outer))
+    def _():
+        rows_in = start_rows(near_targets)
         write_tags(near_targets)
         depart_tags()
         for slot in range(slots):
@@ -229,10 +224,7 @@
         unit = of_wide(blocks, piece) if first_call else late_adapters(blocks, piece, plan)
         for row, rows, column in plan.up_columns():
             depart(up.at[pl.ds(row, rows)], unit.at[pl.ds(0, rows), pl.ds(column, plan.features)])
-        for copy, stage, place in rows_in:
-            copy.wait()
-            depart(stage, place)
-        finish()
+        depart_rows(rows_in)
 
 
 def lay_out(plan, first_call, ids, residency, x, left_rows, ups):
@@ -826,8 +818,8 @@
     across = [across_send(0), across_send(1)]
     tags_in = [swap(tag, "replica", d) for tag, d in zip(tags, plan.cross)]
 
-    wide_in, near, across[0], late, tags_in, base_other, base_mine = lax.optimization_barrier(
-        (wide_in, near, across[0], late, tags_in, base_other, base_mine)
+    wide_in[0], near, across[0], late, base_other, base_mine = lax.optimization_barrier(
+        (wide_in[0], near, across[0], late, base_other, base_mine)
     )
     late_in = []
     for unit, d in enumerate(plan.late_blocks()):
@@ -835,9 +827,13 @@
         if unit < plan.pieces:
             moves.append((plan.outer, 0, half, 0))
         block = late[unit]
-        if unit == 2:
-            late_in[0], across[1], tags_in, block = lax.optimization_barrier(
-                (late_in[0], across[1], tags_in, block)
+        if unit == 1:
+            near, wide_in, tags_in, block = lax.optimization_barrier(
+                (near, wide_in, tags_in, block)
+            )
+        elif unit == 2:
+            late_in[0], wide_in, tags_in, block, base_other = lax.optimization_barrier(
+                (late_in[0], wide_in, tags_in, block, base_other)
             )
         elif unit > 2:
             late_in[unit - 2], block = lax.optimization_barrier((late_in[unit - 2], block))

time: 126 us -> 122 us (0.968)
  waiting for transfers between devices: 56.4 us -> 49.5 us
  starting transfers between devices: 35.3 us -> 38.9 us
    ppermute x11, waiting for transfers between devices: 28 us -> 23.2 us  [send(): return lax.ppermute(value, ('groups', 'replica', 'tensor'), pairs)]
    ppermute x11, starting transfers between devices: 17.5 us -> 20.9 us  [send(): return lax.ppermute(value, ('groups', 'replica', 'tensor'), pairs)]
    ppermute x14, waiting for transfers between devices: 28.4 us -> 26.3 us  [swap(): return lax.ppermute(value, axis, [(i, i ^ distance) for i in range(count)])]
  transfers between devices with their start and end apart: 25 -> 25, of which waited for: 17 -> 16; matrix products, arithmetic and copies ran while one was open for 12% -> 12% of each run, Pallas kernels for 9% -> 9%
where the time goes in v19:
time: 122 us
  waiting for transfers between devices  49.5 us (41%)
  starting transfers between devices  38.9 us (32%)
  Pallas kernels  18.3 us (15%)
  matrix products  12.1 us (10%)
  other arithmetic  1.79 us (1%)
    ppermute x14, waiting for transfers between devices, swap(): return lax.ppermute(value, axis, [(i, i ^ distance) for i in range(count)])  26.3 us
    ppermute x11, waiting for transfers between devices, send(): return lax.ppermute(value, ('groups', 'replica', 'tensor'), pairs)  23.2 us
    ppermute x11, starting transfers between devices, send(): return lax.ppermute(value, ('groups', 'replica', 'tensor'), pairs)  20.9 us
    ppermute x14, starting transfers between devices, swap(): return lax.ppermute(value, axis, [(i, i ^ distance) for i in range(count)])  18 us
    dot_general x2, matrix products, part(): return jnp.dot(rows, columns, preferred_element_type=jnp.float32)  12.1 us
    pallas_call x2, Pallas kernels, lay_out(): pl.pallas_call(functools.partial(lay_kernel, plan, first_call), out_shape...  9.09 us
    pallas_call x4, Pallas kernels, blocks_call(): pl.pallas_call(body, out_shape=out_shape, in_specs=[VMEM] * n_extra + [HB...  6.2 us
  transfers between devices with their start and end apart: 25, of which 16 were waited for; matrix products, arithmetic and copies ran while one was open for 12% of the time, Pallas kernels for 9%

profile of v19, /device:TPU:0, one launch (start us, length us, event | category | flops | bytes accessed | tf_op | source)
XLA Modules:
  0.0 121.8 jit_solution(12338767600162569475)
XLA Ops:
  0.0 4.6 %lay_out_first.1 = (bf16[128,4224]{1,0:T(8,128)(2,1)}, bf16[128,4096]{1,0:T(8,128)(2,1)}, bf16[128,4096]{1,0:T(8,128)(2,1)}, bf16[128,128]{1,0:T(8,128)(2,1)}, bf16[128,128]{1,0:T(8,128)(2,1)}, /*index=5*/s32[16]{0:T(128)}) custom-call(s32[16]{0:T(128)} %ids_ref.2, s32[48]{0:T(128)} %residency_ref.3, bf16[512,4096]{1,0:T(8,128)(2,1)} %x_ref.3, ...), custom_call_target="tpu_custom_call" | custom-call | bytes 2097152 | tf_op jit(solution)/shard_map/lay_out_first/pallas_call | solution.py:238
  4.6 3.0 %collective-permute-start.1 = (bf16[128,4224]{1,0:T(8,128)(2,1)}, bf16[128,4224]{1,0:T(8,128)(2,1)S(1)}, u32[]{:S(2)}, u32[]{:S(2)}) collective-permute-start(bf16[128,4224]{1,0:T(8,128)(2,1)} %get-tuple-element.83), channel_id=1, source_target_pairs={{0,2},{2,0},{4,6},{6,4},{8,10},{10,8},{12,14},{14,12},{1,3},{3,1},... | collective-permute-start | bytes 3244040 | tf_op jit(solution)/shard_map/ppermute | solution.py:744
  9.1 2.6 %collective-permute-start.3 = (bf16[128,4096]{1,0:T(8,128)(2,1)}, bf16[128,4096]{1,0:T(8,128)(2,1)S(1)}, u32[]{:S(2)}, u32[]{:S(2)}) collective-permute-start(bf16[128,4096]{1,0:T(8,128)(2,1)} %get-tuple-element.93), channel_id=1, source_target_pairs={{0,6},{1,7},{2,4},{3,5},{12,10},{13,11},{14,8},{15,9},{16,22},{17,... | collective-permute-start | bytes 3145736 | tf_op jit(solution)/shard_map/ppermute | solution.py:760
  12.2 2.5 %collective-permute-start.5 = (bf16[128,128]{1,0:T(8,128)(2,1)}, bf16[128,128]{1,0:T(8,128)(2,1)S(1)}, u32[]{:S(2)}, u32[]{:S(2)}) collective-permute-start(bf16[128,128]{1,0:T(8,128)(2,1)} %get-tuple-element.95), channel_id=1, source_target_pairs={{0,6},{2,4},{4,2},{6,0},{8,14},{10,12},{12,10},{14,8},{1,7},{3,5},... | collective-permute-start | bytes 98312 | tf_op jit(solution)/shard_map/ppermute | solution.py:744
  14.7 4.5 %lay_out_second.1 = (bf16[128,4224]{1,0:T(8,128)(2,1)}, bf16[64,4096]{1,0:T(8,128)(2,1)}, bf16[64,4096]{1,0:T(8,128)(2,1)}, bf16[64,4096]{1,0:T(8,128)(2,1)}, bf16[64,4096]{1,0:T(8,128)(2,1)}, /*index=5*/s32[16]{0:T(128)}) custom-call(s32[16]{0:T(128)} %ids_ref.2, s32[48]{0:T(128)} %residency_ref.3, bf16[512,4096]{1,0:T(8,128)(2,1)} %x_ref.3, ...), custom_call_target="tpu_custom_call" | custom-call | bytes 2097152 | tf_op jit(solution)/shard_map/lay_out_second/pallas_call | solution.py:238
  20.0 11.7 %collective-permute-done.1.refs_1_.refs_4_ = bf16[128,4224]{1,0:T(8,128)(2,1)S(1)} collective-permute-done((bf16[128,4224]{1,0:T(8,128)(2,1)}, bf16[128,4224]{1,0:T(8,128)(2,1)S(1)}, u32[]{:S(2)}, u32[]{:S(2)}) %collective-permute-start.1) | collective-permute-done | bytes 1081376 | tf_op jit(solution)/shard_map/ppermute | solution.py:744
  31.7 3.2 %collective-permute-done.refs_2_.refs_5_ = bf16[128,4096]{1,0:T(8,128)(2,1)S(1)} collective-permute-done((bf16[128,4096]{1,0:T(8,128)(2,1)}, bf16[128,4096]{1,0:T(8,128)(2,1)S(1)}, u32[]{:S(2)}, u32[]{:S(2)}) %collective-permute-start) | collective-permute-done | bytes 1048608 | tf_op jit(solution)/shard_map/ppermute | solution.py:760
  37.7 7.6 %fusion.2 = f32[512,1024]{1,0:T(8,128)S(1)} fusion(bf16[512,4096]{1,0:T(8,128)(2,1)S(1)} %copy-done.4, bf16[4096,2048]{1,0:T(8,128)(2,1)} %param.7, s32[]{:T(128)S(6)} %select_n.26), kind=kOutput, calls=%fused_computation.2 | convolution fusion | flops 4294967296 | bytes 14680068 | tf_op jit(solution)/shard_map/dot_general | solution.py:797
  45.4 4.5 %fusion = f32[512,1024]{1,0:T(8,128)S(1)} fusion(bf16[512,4096]{1,0:T(8,128)(2,1)S(1)} %copy-done.4, bf16[4096,2048]{1,0:T(8,128)(2,1)S(1)} %bitcast.11, s32[]{:T(128)S(6)} %select_n.27), kind=kOutput, calls=%fused_computation | convolution fusion | flops 4294967296 | bytes 14680068 | tf_op jit(solution)/shard_map/dot_general | solution.py:797
  49.9 1.8 %collective-permute-start.8 = (bf16[64,4096]{1,0:T(8,128)(2,1)S(1)}, bf16[64,4096]{1,0:T(8,128)(2,1)S(1)}, u32[]{:S(2)}, u32[]{:S(2)}) collective-permute-start(bf16[64,4096]{1,0:T(8,128)(2,1)S(1)} %copy-done.8), channel_id=1, source_target_pairs={{4,0},{5,1},{6,2},{7,3},{8,12},{9,13},{10,14},{11,15},{20,16},{21,... | collective-permute-start | bytes 1572872 | tf_op jit(solution)/shard_map/ppermute | solution.py:760
  52.4 4.2 %collective-permute-done.4.refs_6_.refs_7_ = bf16[128,128]{1,0:T(8,128)(2,1)S(1)} collective-permute-done((bf16[128,128]{1,0:T(8,128)(2,1)}, bf16[128,128]{1,0:T(8,128)(2,1)S(1)}, u32[]{:S(2)}, u32[]{:S(2)}) %collective-permute-start.4) | collective-permute-done | bytes 32800 | tf_op jit(solution)/shard_map/ppermute | solution.py:744
  57.1 3.1 %collective-permute-start.6 = (bf16[64,4096]{1,0:T(8,128)(2,1)S(1)}, bf16[64,4096]{1,0:T(8,128)(2,1)S(1)}, u32[]{:S(2)}, u32[]{:S(2)}) collective-permute-start(bf16[64,4096]{1,0:T(8,128)(2,1)S(1)} %copy-done.7), channel_id=1, source_target_pairs={{4,2},{5,3},{6,0},{7,1},{8,14},{9,15},{10,12},{11,13},{20,18},{21,... | collective-permute-start | bytes 1572872 | tf_op jit(solution)/shard_map/ppermute | solution.py:760
  60.3 8.3 %collective-permute-done.8.refs_4_.refs_7_ = bf16[64,4096]{1,0:T(8,128)(2,1)S(1)} collective-permute-done((bf16[64,4096]{1,0:T(8,128)(2,1)S(1)}, bf16[64,4096]{1,0:T(8,128)(2,1)S(1)}, u32[]{:S(2)}, u32[]{:S(2)}) %collective-permute-start.8) | collective-permute-done | bytes 524320 | tf_op jit(solution)/shard_map/ppermute | solution.py:760
  70.3 2.9 %collective-permute-start.13 = (bf16[64,4096]{1,0:T(8,128)(2,1)S(1)}, bf16[64,4096]{1,0:T(8,128)(2,1)S(1)}, u32[]{:S(2)}, u32[]{:S(2)}) collective-permute-start(bf16[64,4096]{1,0:T(8,128)(2,1)S(1)} %copy-done.6), channel_id=1, source_target_pairs={{4,2},{5,3},{6,0},{7,1},{8,14},{9,15},{10,12},{11,13},{20,18},{21,... | collective-permute-start | bytes 1572872 | tf_op jit(solution)/shard_map/ppermute | solution.py:760
  73.2 6.4 %collective-permute-done.6.refs_5_ = bf16[64,4096]{1,0:T(8,128)(2,1)S(1)} collective-permute-done((bf16[64,4096]{1,0:T(8,128)(2,1)S(1)}, bf16[64,4096]{1,0:T(8,128)(2,1)S(1)}, u32[]{:S(2)}, u32[]{:S(2)}) %collective-permute-start.6) | collective-permute-done | bytes 524320 | tf_op jit(solution)/shard_map/ppermute | solution.py:760
  81.2 2.9 %collective-permute-start.7 = (bf16[64,4096]{1,0:T(8,128)(2,1)S(1)}, bf16[64,4096]{1,0:T(8,128)(2,1)S(1)}, u32[]{:S(2)}, u32[]{:S(2)}) collective-permute-start(bf16[64,4096]{1,0:T(8,128)(2,1)S(1)} %copy-done.5), channel_id=1, source_target_pairs={{4,0},{5,1},{6,2},{7,3},{8,12},{9,13},{10,14},{11,15},{20,16},{21,... | collective-permute-start | bytes 1572872 | tf_op jit(solution)/shard_map/ppermute | solution.py:760
  84.2 2.0 %reduce_own.1 = (f32[128,128]{1,0:T(8,128)S(1)}, f32[256,128]{1,0:T(8,128)S(1)}) custom-call(bf16[128,4224]{1,0:T(8,128)(2,1)S(1)} %copy-done.1, bf16[128,4224]{1,0:T(8,128)(2,1)S(1)} %collective-permute-done.1.refs_1_.refs_4_, bf16[128,4096]{1,0:T(8,128)(2,1)S(1)} %collective-permute-done.refs_2_.refs_5_, ...), custom_call_target="tpu_custom_call" | custom-call | flops 1 | bytes 1 | tf_op jit(solution)/shard_map/reduce_own/pallas_call | solution.py:554
  88.9 2.0 %collective-permute-done.13.refs_6_ = bf16[64,4096]{1,0:T(8,128)(2,1)S(1)} collective-permute-done((bf16[64,4096]{1,0:T(8,128)(2,1)S(1)}, bf16[64,4096]{1,0:T(8,128)(2,1)S(1)}, u32[]{:S(2)}, u32[]{:S(2)}) %collective-permute-start.13) | collective-permute-done | bytes 524320 | tf_op jit(solution)/shard_map/ppermute | solution.py:760
  92.5 2.6 %collective-permute-done.14.refs_12_.refs_11_.refs_8_ = bf16[64,4224]{1,0:T(8,128)(2,1)S(1)} collective-permute-done((bf16[64,4224]{1,0:T(8,128)(2,1)S(1)}, bf16[64,4224]{1,0:T(8,128)(2,1)S(1)}, u32[]{:S(2)}, u32[]{:S(2)}) %collective-permute-start.14) | collective-permute-done | bytes 540704 | tf_op jit(solution)/shard_map/ppermute | solution.py:760
  95.1 3.4 %collective-permute-start.19 = (bf16[64,1024]{1,0:T(8,128)(2,1)S(1)}, bf16[64,1024]{1,0:T(8,128)(2,1)S(1)}, u32[]{:S(2)}, u32[]{:S(2)}) collective-permute-start(bf16[64,1024]{1,0:T(8,128)(2,1)S(1)} %get-tuple-element.139), channel_id=1, source_target_pairs={{0,4},{2,6},{4,0},{6,2},{8,12},{10,14},{12,8},{14,10},{1,5},{3,7},... | collective-permute-start | bytes 393224 | tf_op jit(solution)/shard_map/ppermute | solution.py:744
  98.4 2.7 %reduce_taken.1 = (f32[64,128]{1,0:T(8,128)S(1)}, f32[64,128]{1,0:T(8,128)S(1)}, f32[256,128]{1,0:T(8,128)S(1)}) custom-call(bf16[128,4224]{1,0:T(8,128)(2,1)S(1)} %copy-done.1, bf16[128,4224]{1,0:T(8,128)(2,1)S(1)} %collective-permute-done.1.refs_1_.refs_4_, bf16[128,4096]{1,0:T(8,128)(2,1)S(1)} %collective-permute-done.refs_2_.refs_5_, ...), custom_call_target="tpu_custom_call" | custom-call | flops 1 | bytes 1 | tf_op jit(solution)/shard_map/reduce_taken/pallas_call | solution.py:554
  109.5 3.3 %collective-permute-start.22 = (bf16[64,1024]{1,0:T(8,128)(2,1)S(1)}, bf16[64,1024]{1,0:T(8,128)(2,1)S(1)}, u32[]{:S(2)}, u32[]{:S(2)}) collective-permute-start(bf16[64,1024]{1,0:T(8,128)(2,1)S(1)} %get-tuple-element.149), channel_id=1, source_target_pairs={{0,4},{2,6},{4,0},{6,2},{8,12},{10,14},{12,8},{14,10},{1,5},{3,7},... | collective-permute-start | bytes 393224 | tf_op jit(solution)/shard_map/ppermute | solution.py:744
  114.4 2.5 %collective-permute-done.22.refs_4_ = bf16[64,1024]{1,0:T(8,128)(2,1)S(1)} collective-permute-done((bf16[64,1024]{1,0:T(8,128)(2,1)S(1)}, bf16[64,1024]{1,0:T(8,128)(2,1)S(1)}, u32[]{:S(2)}, u32[]{:S(2)}) %collective-permute-start.22) | collective-permute-done | bytes 131104 | tf_op jit(solution)/shard_map/ppermute | solution.py:744
  116.9 1.8 %collective-permute-done.23.refs_5_ = bf16[64,1024]{1,0:T(8,128)(2,1)S(1)} collective-permute-done((bf16[64,1024]{1,0:T(8,128)(2,1)S(1)}, bf16[64,1024]{1,0:T(8,128)(2,1)S(1)}, u32[]{:S(2)}, u32[]{:S(2)}) %collective-permute-start.23) | collective-permute-done | bytes 131104 | tf_op jit(solution)/shard_map/ppermute | solution.py:744
  (76 shorter events, 27.1 us)
Async XLA Ops:
  4.6 27.1 %collective-permute-start.1 = (bf16[128,4224]{1,0:T(8,128)(2,1)}, bf16[128,4224]{1,0:T(8,128)(2,1)S(1)}, u32[]{:S(2)}, u32[]{:S(2)}) collective-permute-start(bf16[128,4224]{1,0:T(8,128)(2,1)} %get-tuple-element.83), channel_id=1, source_target_pairs={{0,2},{2,0},{4,6},{6,4},{8,10},{10,8},{12,14},{14,12},{1,3},{3,1},... | collective-permute-start | bytes 3244040 | tf_op jit(solution)/shard_map/ppermute | solution.py:744
  7.6 27.3 %collective-permute-start = (bf16[128,4096]{1,0:T(8,128)(2,1)}, bf16[128,4096]{1,0:T(8,128)(2,1)S(1)}, u32[]{:S(2)}, u32[]{:S(2)}) collective-permute-start(bf16[128,4096]{1,0:T(8,128)(2,1)} %get-tuple-element.80), channel_id=1, source_target_pairs={{0,4},{1,5},{2,6},{3,7},{12,8},{13,9},{14,10},{15,11},{16,20},{17,... | collective-permute-start | bytes 3145736 | tf_op jit(solution)/shard_map/ppermute | solution.py:760
  9.1 48.0 %collective-permute-start.3 = (bf16[128,4096]{1,0:T(8,128)(2,1)}, bf16[128,4096]{1,0:T(8,128)(2,1)S(1)}, u32[]{:S(2)}, u32[]{:S(2)}) collective-permute-start(bf16[128,4096]{1,0:T(8,128)(2,1)} %get-tuple-element.93), channel_id=1, source_target_pairs={{0,6},{1,7},{2,4},{3,5},{12,10},{13,11},{14,8},{15,9},{16,22},{17,... | collective-permute-start | bytes 3145736 | tf_op jit(solution)/shard_map/ppermute | solution.py:760
  11.7 44.9 %collective-permute-start.4 = (bf16[128,128]{1,0:T(8,128)(2,1)}, bf16[128,128]{1,0:T(8,128)(2,1)S(1)}, u32[]{:S(2)}, u32[]{:S(2)}) collective-permute-start(bf16[128,128]{1,0:T(8,128)(2,1)} %get-tuple-element.94), channel_id=1, source_target_pairs={{0,4},{2,6},{4,0},{6,2},{8,12},{10,14},{12,8},{14,10},{1,5},{3,7},... | collective-permute-start | bytes 98312 | tf_op jit(solution)/shard_map/ppermute | solution.py:744
  12.2 45.0 %collective-permute-start.5 = (bf16[128,128]{1,0:T(8,128)(2,1)}, bf16[128,128]{1,0:T(8,128)(2,1)S(1)}, u32[]{:S(2)}, u32[]{:S(2)}) collective-permute-start(bf16[128,128]{1,0:T(8,128)(2,1)} %get-tuple-element.95), channel_id=1, source_target_pairs={{0,6},{2,4},{4,2},{6,0},{8,14},{10,12},{12,10},{14,8},{1,7},{3,5},... | collective-permute-start | bytes 98312 | tf_op jit(solution)/shard_map/ppermute | solution.py:744
  36.2 13.8 %collective-permute-start.2 = (bf16[64,4224]{1,0:T(8,128)(2,1)S(1)}, bf16[64,4224]{1,0:T(8,128)(2,1)S(1)}, u32[]{:S(2)}, u32[]{:S(2)}) collective-permute-start(bf16[64,4224]{1,0:T(8,128)(2,1)S(1)} %pad_maximum_fusion), channel_id=1, source_target_pairs={{0,16},{1,17},{2,18},{3,19},{12,28},{13,29},{14,30},{15,31},{16,0}... | collective-permute-start | bytes 1622024 | tf_op jit(solution)/shard_map/ppermute | solution.py:760
  49.9 18.6 %collective-permute-start.8 = (bf16[64,4096]{1,0:T(8,128)(2,1)S(1)}, bf16[64,4096]{1,0:T(8,128)(2,1)S(1)}, u32[]{:S(2)}, u32[]{:S(2)}) collective-permute-start(bf16[64,4096]{1,0:T(8,128)(2,1)S(1)} %copy-done.8), channel_id=1, source_target_pairs={{4,0},{5,1},{6,2},{7,3},{8,12},{9,13},{10,14},{11,15},{20,16},{21,... | collective-permute-start | bytes 1572872 | tf_op jit(solution)/shard_map/ppermute | solution.py:760
  51.8 29.4 %collective-permute-start.9 = (bf16[64,4224]{1,0:T(8,128)(2,1)S(1)}, bf16[64,4224]{1,0:T(8,128)(2,1)S(1)}, u32[]{:S(2)}, u32[]{:S(2)}) collective-permute-start(bf16[64,4224]{1,0:T(8,128)(2,1)S(1)} %pad_maximum_fusion.1), channel_id=1, source_target_pairs={{0,16},{1,17},{2,18},{3,19},{12,28},{13,29},{14,30},{15,31},{16,0}... | collective-permute-start | bytes 1622024 | tf_op jit(solution)/shard_map/ppermute | solution.py:760
  57.1 22.5 %collective-permute-start.6 = (bf16[64,4096]{1,0:T(8,128)(2,1)S(1)}, bf16[64,4096]{1,0:T(8,128)(2,1)S(1)}, u32[]{:S(2)}, u32[]{:S(2)}) collective-permute-start(bf16[64,4096]{1,0:T(8,128)(2,1)S(1)} %copy-done.7), channel_id=1, source_target_pairs={{4,2},{5,3},{6,0},{7,1},{8,14},{9,15},{10,12},{11,13},{20,18},{21,... | collective-permute-start | bytes 1572872 | tf_op jit(solution)/shard_map/ppermute | solution.py:760
  68.5 29.9 %collective-permute-start.15 = (f32[512,1024]{1,0:T(8,128)S(1)}, f32[512,1024]{1,0:T(8,128)S(1)}, u32[]{:S(2)}, u32[]{:S(2)}) collective-permute-start(f32[512,1024]{1,0:T(8,128)S(1)} %fusion.2), channel_id=1, source_target_pairs={{0,1},{1,0},{2,3},{3,2},{4,5},{5,4},{6,7},{7,6},{8,9},{9,8},{10,11... | collective-permute-start | bytes 6291464 | tf_op jit(solution)/shard_map/ppermute | solution.py:744
  68.7 15.5 %collective-permute-start.10 = (bf16[64,4224]{1,0:T(8,128)(2,1)S(1)}, bf16[64,4224]{1,0:T(8,128)(2,1)S(1)}, u32[]{:S(2)}, u32[]{:S(2)}) collective-permute-start(bf16[64,4224]{1,0:T(8,128)(2,1)S(1)} %pad_maximum_fusion.2), channel_id=1, source_target_pairs={{0,16},{1,17},{2,18},{3,19},{12,28},{13,29},{14,30},{15,31},{16,0}... | collective-permute-start | bytes 1622024 | tf_op jit(solution)/shard_map/ppermute | solution.py:760
  70.3 20.6 %collective-permute-start.13 = (bf16[64,4096]{1,0:T(8,128)(2,1)S(1)}, bf16[64,4096]{1,0:T(8,128)(2,1)S(1)}, u32[]{:S(2)}, u32[]{:S(2)}) collective-permute-start(bf16[64,4096]{1,0:T(8,128)(2,1)S(1)} %copy-done.6), channel_id=1, source_target_pairs={{4,2},{5,3},{6,0},{7,1},{8,14},{9,15},{10,12},{11,13},{20,18},{21,... | collective-permute-start | bytes 1572872 | tf_op jit(solution)/shard_map/ppermute | solution.py:760
  79.6 15.4 %collective-permute-start.14 = (bf16[64,4224]{1,0:T(8,128)(2,1)S(1)}, bf16[64,4224]{1,0:T(8,128)(2,1)S(1)}, u32[]{:S(2)}, u32[]{:S(2)}) collective-permute-start(bf16[64,4224]{1,0:T(8,128)(2,1)S(1)} %pad_maximum_fusion.3), channel_id=1, source_target_pairs={{0,16},{1,17},{2,18},{3,19},{12,28},{13,29},{14,30},{15,31},{16,0}... | collective-permute-start | bytes 1622024 | tf_op jit(solution)/shard_map/ppermute | solution.py:760
  81.2 21.0 %collective-permute-start.7 = (bf16[64,4096]{1,0:T(8,128)(2,1)S(1)}, bf16[64,4096]{1,0:T(8,128)(2,1)S(1)}, u32[]{:S(2)}, u32[]{:S(2)}) collective-permute-start(bf16[64,4096]{1,0:T(8,128)(2,1)S(1)} %copy-done.5), channel_id=1, source_target_pairs={{4,0},{5,1},{6,2},{7,3},{8,12},{9,13},{10,14},{11,15},{20,16},{21,... | collective-permute-start | bytes 1572872 | tf_op jit(solution)/shard_map/ppermute | solution.py:760
  86.2 1.3 %collective-permute-start.11 = (f32[128,128]{1,0:T(8,128)S(1)}, f32[128,128]{1,0:T(8,128)S(1)}, u32[]{:S(2)}, u32[]{:S(2)}) collective-permute-start(f32[128,128]{1,0:T(8,128)S(1)} %get-tuple-element.118.refs_0_), channel_id=1, source_target_pairs={{0,1},{1,0},{2,3},{3,2},{4,5},{5,4},{6,7},{7,6},{8,9},{9,8},{10,11... | collective-permute-start | bytes 196616 | tf_op jit(solution)/shard_map/ppermute | solution.py:744
  87.6 21.1 %collective-permute-start.21 = (bf16[48,4096]{1,0:T(8,128)(2,1)S(1)}, bf16[48,4096]{1,0:T(8,128)(2,1)S(1)}, u32[]{:S(2)}, u32[]{:S(2)}) collective-permute-start(bf16[48,4096]{1,0:T(8,128)(2,1)S(1)} %slice.54), channel_id=1, source_target_pairs={{4,20},{5,21},{6,22},{7,23},{8,24},{9,25},{10,26},{11,27},{20,4},{... | collective-permute-start | bytes 1179656 | tf_op jit(solution)/shard_map/ppermute | solution.py:760
  90.8 11.4 %collective-permute-start.12 = (bf16[64,1024]{1,0:T(8,128)(2,1)S(1)}, bf16[64,1024]{1,0:T(8,128)(2,1)S(1)}, u32[]{:S(2)}, u32[]{:S(2)}) collective-permute-start(bf16[64,1024]{1,0:T(8,128)(2,1)S(1)} %get-tuple-element.121), channel_id=1, source_target_pairs={{0,2},{2,0},{4,6},{6,4},{8,10},{10,8},{12,14},{14,12},{1,3},{3,1},... | collective-permute-start | bytes 393224 | tf_op jit(solution)/shard_map/ppermute | solution.py:744
  95.1 11.2 %collective-permute-start.19 = (bf16[64,1024]{1,0:T(8,128)(2,1)S(1)}, bf16[64,1024]{1,0:T(8,128)(2,1)S(1)}, u32[]{:S(2)}, u32[]{:S(2)}) collective-permute-start(bf16[64,1024]{1,0:T(8,128)(2,1)S(1)} %get-tuple-element.139), channel_id=1, source_target_pairs={{0,4},{2,6},{4,0},{6,2},{8,12},{10,14},{12,8},{14,10},{1,5},{3,7},... | collective-permute-start | bytes 393224 | tf_op jit(solution)/shard_map/ppermute | solution.py:744
  98.4 9.2 %collective-permute-start.20 = (bf16[64,1024]{1,0:T(8,128)(2,1)S(1)}, bf16[64,1024]{1,0:T(8,128)(2,1)S(1)}, u32[]{:S(2)}, u32[]{:S(2)}) collective-permute-start(bf16[64,1024]{1,0:T(8,128)(2,1)S(1)} %get-tuple-element.140), channel_id=1, source_target_pairs={{0,6},{2,4},{4,2},{6,0},{8,14},{10,12},{12,10},{14,8},{1,7},{3,5},... | collective-permute-start | bytes 393224 | tf_op jit(solution)/shard_map/ppermute | solution.py:744
  103.5 4.1 %collective-permute-start.16 = (f32[64,128]{1,0:T(8,128)S(1)}, f32[64,128]{1,0:T(8,128)S(1)}, u32[]{:S(2)}, u32[]{:S(2)}) collective-permute-start(f32[64,128]{1,0:T(8,128)S(1)} %get-tuple-element.145.refs_0_), channel_id=1, source_target_pairs={{0,1},{1,0},{2,3},{3,2},{4,5},{5,4},{6,7},{7,6},{8,9},{9,8},{10,11... | collective-permute-start | bytes 98312 | tf_op jit(solution)/shard_map/ppermute | solution.py:744
  104.7 3.9 %collective-permute-start.18 = (f32[64,128]{1,0:T(8,128)S(1)}, f32[64,128]{1,0:T(8,128)S(1)}, u32[]{:S(2)}, u32[]{:S(2)}) collective-permute-start(f32[64,128]{1,0:T(8,128)S(1)} %add.15.refs_2_), channel_id=1, source_target_pairs={{0,16},{16,0},{1,17},{17,1},{2,18},{18,2},{3,19},{19,3},{4,20},{20... | collective-permute-start | bytes 98312 | tf_op jit(solution)/shard_map/ppermute | solution.py:744
  109.5 7.4 %collective-permute-start.22 = (bf16[64,1024]{1,0:T(8,128)(2,1)S(1)}, bf16[64,1024]{1,0:T(8,128)(2,1)S(1)}, u32[]{:S(2)}, u32[]{:S(2)}) collective-permute-start(bf16[64,1024]{1,0:T(8,128)(2,1)S(1)} %get-tuple-element.149), channel_id=1, source_target_pairs={{0,4},{2,6},{4,0},{6,2},{8,12},{10,14},{12,8},{14,10},{1,5},{3,7},... | collective-permute-start | bytes 393224 | tf_op jit(solution)/shard_map/ppermute | solution.py:744
  112.9 5.9 %collective-permute-start.23 = (bf16[64,1024]{1,0:T(8,128)(2,1)S(1)}, bf16[64,1024]{1,0:T(8,128)(2,1)S(1)}, u32[]{:S(2)}, u32[]{:S(2)}) collective-permute-start(bf16[64,1024]{1,0:T(8,128)(2,1)S(1)} %get-tuple-element.150), channel_id=1, source_target_pairs={{0,6},{2,4},{4,2},{6,0},{8,14},{10,12},{12,10},{14,8},{1,7},{3,5},... | collective-permute-start | bytes 393224 | tf_op jit(solution)/shard_map/ppermute | solution.py:744
  112.9 7.1 %collective-permute-start.24 = (bf16[64,1024]{1,0:T(8,128)(2,1)S(1)}, bf16[64,1024]{1,0:T(8,128)(2,1)S(1)}, u32[]{:S(2)}, u32[]{:S(2)}) collective-permute-start(bf16[64,1024]{1,0:T(8,128)(2,1)S(1)} %get-tuple-element.152), channel_id=1, source_target_pairs={{0,2},{2,0},{4,6},{6,4},{8,10},{10,8},{12,14},{14,12},{1,3},{3,1},... | collective-permute-start | bytes 393224 | tf_op jit(solution)/shard_map/ppermute | solution.py:744
  (14 other events, 193.7 us)

commit v20 on v19

--- a/solution.py
+++ b/solution.py
@@ -708,35 +708,54 @@
 
 
 def join_kernel(order, seg_ref, base_ref, *refs):
-    deltas, out_ref = refs[:-1], refs[-1]
-    for i in range(len(deltas) * CAP):
-        part = i % CAP
-        k = order[i // CAP] * CAP + part
-
-        @pl.when(seg_ref[k] >= 0)
+    n = len(order)
+    deltas, (out_ref, rows, sems) = refs[:n], refs[-3:]
+
+    def parts():
+        for i in range(n * CAP):
+            seg = seg_ref[order[i // CAP] * CAP + i % CAP]
+            span = pl.ds(pl.multiple_of(jnp.maximum(seg, 0) * SEG, SEG), SEG)
+            place = pl.ds(i * SEG, SEG)
+            yield i, seg, span, pltpu.make_async_copy(
+                rows.at[place], out_ref.at[span], sems.at[i]
+            )
+
+    for i, seg, span, copy in parts():
+
+        @pl.when(seg >= 0)
         def _():
-            span = pl.ds(pl.multiple_of(seg_ref[k] * SEG, SEG), SEG)
+            part = i % CAP
             delta = deltas[i // CAP][part * SEG : (part + 1) * SEG, :]
-            out_ref[span, :] = (base_ref[span, :] + delta.astype(jnp.float32)).astype(
-                out_ref.dtype
-            )
-
-
-def join(plan, seg_of, base, deltas):
+            total = base_ref[span, :] + delta.astype(jnp.float32)
+            rows[i * SEG : (i + 1) * SEG, :] = total.astype(rows.dtype)
+            copy.start()
+
+    for _, seg, _, copy in parts():
+        pl.when(seg >= 0)(copy.wait)
+
+
+def join(plan, seg_of, base, deltas, kind, before=None):
     height, features = base.shape
-    order = [kind * plan.half + d for kind in range(2) for d in plan.cross + plan.near]
+    order = [kind * plan.half + d for d in plan.cross + plan.near]
     deltas = [deltas[i] for i in order]
+    n = len(deltas)
+    more = [] if before is None else [before]
     return pl.pallas_call(
         functools.partial(join_kernel, order),
         out_shape=jax.ShapeDtypeStruct((height, features), jnp.bfloat16),
-        in_specs=[SMEM, VMEM] + [VMEM] * len(deltas),
-        out_specs=VMEM,
+        in_specs=[SMEM, VMEM] + [VMEM] * n + [HBM] * len(more),
+        out_specs=HBM,
+        scratch_shapes=[
+            pltpu.VMEM((n * PAIR, features), jnp.bfloat16),
+            pltpu.SemaphoreType.DMA((n * CAP,)),
+        ],
+        input_output_aliases={2 + n: 0} if more else {},
         compiler_params=params(),
         cost_estimate=pl.CostEstimate(
-            flops=height * features, bytes_accessed=8 * height * features, transcendentals=0
+            flops=height * features, bytes_accessed=4 * height * features, transcendentals=0
         ),
-        name="join",
-    )(seg_of, base, *deltas)
+        name="join_taken" if more else "join_own",
+    )(seg_of, base, *deltas, *more)
 
 
 def swap(value, axis, distance):
@@ -868,7 +887,8 @@
     across_wide = [blocks[plan.left_pieces] for blocks in across]
     terms = expand_taken(plan, pairs, tag, wide_in, late_in[0], across_wide, across_up)
     deltas += [terms[0]] + return_terms(terms)
-    return join(plan, seg_of, base, deltas)
+    own = join(plan, seg_of, base, deltas, 0)
+    return join(plan, seg_of, base, deltas, 1, own)
 
 
 def solution(mesh):

time: 122 us -> 122 us (level)
  waiting for transfers between devices: 49.5 us -> 48.1 us
    ppermute x14, waiting for transfers between devices: 26.3 us -> 24.9 us  [swap(): return lax.ppermute(value, axis, [(i, i ^ distance) for i in range(count)])]
    pallas_call x1 -> x2, Pallas kernels: 1.81 us -> 2.81 us  [join(): pl.pallas_call(functools.partial(join_kernel, order), out_shape=jax.Shape...]
  transfers between devices with their start and end apart: 25 -> 25, of which waited for: 16 -> 16; matrix products, arithmetic and copies ran while one was open for 12% -> 12% of each run, Pallas kernels for 9% -> 10%
where the time goes in v20:
time: 122 us
  waiting for transfers between devices  48.1 us (39%)
  starting transfers between devices  38.9 us (32%)
  Pallas kernels  19.3 us (16%)
  matrix products  12.1 us (10%)
  other arithmetic  1.79 us (1%)
    ppermute x14, waiting for transfers between devices, swap(): return lax.ppermute(value, axis, [(i, i ^ distance) for i in range(count)])  24.9 us
    ppermute x11, waiting for transfers between devices, send(): return lax.ppermute(value, ('groups', 'replica', 'tensor'), pairs)  23.2 us
    ppermute x11, starting transfers between devices, send(): return lax.ppermute(value, ('groups', 'replica', 'tensor'), pairs)  20.9 us
    ppermute x14, starting transfers between devices, swap(): return lax.ppermute(value, axis, [(i, i ^ distance) for i in range(count)])  18 us
    dot_general x2, matrix products, part(): return jnp.dot(rows, columns, preferred_element_type=jnp.float32)  12.1 us
    pallas_call x2, Pallas kernels, lay_out(): pl.pallas_call(functools.partial(lay_kernel, plan, first_call), out_shape...  9.09 us
    pallas_call x4, Pallas kernels, blocks_call(): pl.pallas_call(body, out_shape=out_shape, in_specs=[VMEM] * n_extra + [HB...  6.2 us
    pallas_call x2, Pallas kernels, join(): pl.pallas_call(functools.partial(join_kernel, order), out_shape=jax.Shape...  2.81 us
  transfers between devices with their start and end apart: 25, of which 16 were waited for; matrix products, arithmetic and copies ran while one was open for 12% of the time, Pallas kernels for 10%

profile of v20, /device:TPU:0, one launch (start us, length us, event | category | flops | bytes accessed | tf_op | source)
XLA Modules:
  0.0 121.5 jit_solution(17357800310162583996)
XLA Ops:
  0.0 4.6 %lay_out_first.1 = (bf16[128,4224]{1,0:T(8,128)(2,1)}, bf16[128,4096]{1,0:T(8,128)(2,1)}, bf16[128,4096]{1,0:T(8,128)(2,1)}, bf16[128,128]{1,0:T(8,128)(2,1)}, bf16[128,128]{1,0:T(8,128)(2,1)}, /*index=5*/s32[16]{0:T(128)}) custom-call(s32[16]{0:T(128)} %ids_ref.2, s32[48]{0:T(128)} %residency_ref.3, bf16[512,4096]{1,0:T(8,128)(2,1)} %x_ref.3, ...), custom_call_target="tpu_custom_call" | custom-call | bytes 2097152 | tf_op jit(solution)/shard_map/lay_out_first/pallas_call | solution.py:238
  4.6 3.0 %collective-permute-start.1 = (bf16[128,4224]{1,0:T(8,128)(2,1)}, bf16[128,4224]{1,0:T(8,128)(2,1)S(1)}, u32[]{:S(2)}, u32[]{:S(2)}) collective-permute-start(bf16[128,4224]{1,0:T(8,128)(2,1)} %get-tuple-element.83), channel_id=1, source_target_pairs={{0,2},{2,0},{4,6},{6,4},{8,10},{10,8},{12,14},{14,12},{1,3},{3,1},... | collective-permute-start | bytes 3244040 | tf_op jit(solution)/shard_map/ppermute | solution.py:763
  9.1 2.6 %collective-permute-start.3 = (bf16[128,4096]{1,0:T(8,128)(2,1)}, bf16[128,4096]{1,0:T(8,128)(2,1)S(1)}, u32[]{:S(2)}, u32[]{:S(2)}) collective-permute-start(bf16[128,4096]{1,0:T(8,128)(2,1)} %get-tuple-element.93), channel_id=1, source_target_pairs={{0,6},{1,7},{2,4},{3,5},{12,10},{13,11},{14,8},{15,9},{16,22},{17,... | collective-permute-start | bytes 3145736 | tf_op jit(solution)/shard_map/ppermute | solution.py:779
  12.2 2.5 %collective-permute-start.5 = (bf16[128,128]{1,0:T(8,128)(2,1)}, bf16[128,128]{1,0:T(8,128)(2,1)S(1)}, u32[]{:S(2)}, u32[]{:S(2)}) collective-permute-start(bf16[128,128]{1,0:T(8,128)(2,1)} %get-tuple-element.95), channel_id=1, source_target_pairs={{0,6},{2,4},{4,2},{6,0},{8,14},{10,12},{12,10},{14,8},{1,7},{3,5},... | collective-permute-start | bytes 98312 | tf_op jit(solution)/shard_map/ppermute | solution.py:763
  14.7 4.5 %lay_out_second.1 = (bf16[128,4224]{1,0:T(8,128)(2,1)}, bf16[64,4096]{1,0:T(8,128)(2,1)}, bf16[64,4096]{1,0:T(8,128)(2,1)}, bf16[64,4096]{1,0:T(8,128)(2,1)}, bf16[64,4096]{1,0:T(8,128)(2,1)}, /*index=5*/s32[16]{0:T(128)}) custom-call(s32[16]{0:T(128)} %ids_ref.2, s32[48]{0:T(128)} %residency_ref.3, bf16[512,4096]{1,0:T(8,128)(2,1)} %x_ref.3, ...), custom_call_target="tpu_custom_call" | custom-call | bytes 2097152 | tf_op jit(solution)/shard_map/lay_out_second/pallas_call | solution.py:238
  20.0 11.7 %collective-permute-done.1.refs_1_.refs_4_ = bf16[128,4224]{1,0:T(8,128)(2,1)S(1)} collective-permute-done((bf16[128,4224]{1,0:T(8,128)(2,1)}, bf16[128,4224]{1,0:T(8,128)(2,1)S(1)}, u32[]{:S(2)}, u32[]{:S(2)}) %collective-permute-start.1) | collective-permute-done | bytes 1081376 | tf_op jit(solution)/shard_map/ppermute | solution.py:763
  31.7 3.2 %collective-permute-done.refs_2_.refs_5_ = bf16[128,4096]{1,0:T(8,128)(2,1)S(1)} collective-permute-done((bf16[128,4096]{1,0:T(8,128)(2,1)}, bf16[128,4096]{1,0:T(8,128)(2,1)S(1)}, u32[]{:S(2)}, u32[]{:S(2)}) %collective-permute-start) | collective-permute-done | bytes 1048608 | tf_op jit(solution)/shard_map/ppermute | solution.py:779
  37.7 7.6 %fusion.2 = f32[512,1024]{1,0:T(8,128)S(1)} fusion(bf16[512,4096]{1,0:T(8,128)(2,1)S(1)} %copy-done.4, bf16[4096,2048]{1,0:T(8,128)(2,1)} %param.7, s32[]{:T(128)S(6)} %select_n.26), kind=kOutput, calls=%fused_computation.2 | convolution fusion | flops 4294967296 | bytes 14680068 | tf_op jit(solution)/shard_map/dot_general | solution.py:816
  45.4 4.5 %fusion = f32[512,1024]{1,0:T(8,128)S(1)} fusion(bf16[512,4096]{1,0:T(8,128)(2,1)S(1)} %copy-done.4, bf16[4096,2048]{1,0:T(8,128)(2,1)S(1)} %bitcast.11, s32[]{:T(128)S(6)} %select_n.27), kind=kOutput, calls=%fused_computation | convolution fusion | flops 4294967296 | bytes 14680068 | tf_op jit(solution)/shard_map/dot_general | solution.py:816
  49.9 1.8 %collective-permute-start.8 = (bf16[64,4096]{1,0:T(8,128)(2,1)S(1)}, bf16[64,4096]{1,0:T(8,128)(2,1)S(1)}, u32[]{:S(2)}, u32[]{:S(2)}) collective-permute-start(bf16[64,4096]{1,0:T(8,128)(2,1)S(1)} %copy-done.8), channel_id=1, source_target_pairs={{4,0},{5,1},{6,2},{7,3},{8,12},{9,13},{10,14},{11,15},{20,16},{21,... | collective-permute-start | bytes 1572872 | tf_op jit(solution)/shard_map/ppermute | solution.py:779
  52.4 4.2 %collective-permute-done.4.refs_6_.refs_7_ = bf16[128,128]{1,0:T(8,128)(2,1)S(1)} collective-permute-done((bf16[128,128]{1,0:T(8,128)(2,1)}, bf16[128,128]{1,0:T(8,128)(2,1)S(1)}, u32[]{:S(2)}, u32[]{:S(2)}) %collective-permute-start.4) | collective-permute-done | bytes 32800 | tf_op jit(solution)/shard_map/ppermute | solution.py:763
  57.1 3.1 %collective-permute-start.6 = (bf16[64,4096]{1,0:T(8,128)(2,1)S(1)}, bf16[64,4096]{1,0:T(8,128)(2,1)S(1)}, u32[]{:S(2)}, u32[]{:S(2)}) collective-permute-start(bf16[64,4096]{1,0:T(8,128)(2,1)S(1)} %copy-done.7), channel_id=1, source_target_pairs={{4,2},{5,3},{6,0},{7,1},{8,14},{9,15},{10,12},{11,13},{20,18},{21,... | collective-permute-start | bytes 1572872 | tf_op jit(solution)/shard_map/ppermute | solution.py:779
  60.3 8.3 %collective-permute-done.8.refs_4_.refs_7_ = bf16[64,4096]{1,0:T(8,128)(2,1)S(1)} collective-permute-done((bf16[64,4096]{1,0:T(8,128)(2,1)S(1)}, bf16[64,4096]{1,0:T(8,128)(2,1)S(1)}, u32[]{:S(2)}, u32[]{:S(2)}) %collective-permute-start.8) | collective-permute-done | bytes 524320 | tf_op jit(solution)/shard_map/ppermute | solution.py:779
  70.3 2.9 %collective-permute-start.13 = (bf16[64,4096]{1,0:T(8,128)(2,1)S(1)}, bf16[64,4096]{1,0:T(8,128)(2,1)S(1)}, u32[]{:S(2)}, u32[]{:S(2)}) collective-permute-start(bf16[64,4096]{1,0:T(8,128)(2,1)S(1)} %copy-done.6), channel_id=1, source_target_pairs={{4,2},{5,3},{6,0},{7,1},{8,14},{9,15},{10,12},{11,13},{20,18},{21,... | collective-permute-start | bytes 1572872 | tf_op jit(solution)/shard_map/ppermute | solution.py:779
  73.2 6.4 %collective-permute-done.6.refs_5_ = bf16[64,4096]{1,0:T(8,128)(2,1)S(1)} collective-permute-done((bf16[64,4096]{1,0:T(8,128)(2,1)S(1)}, bf16[64,4096]{1,0:T(8,128)(2,1)S(1)}, u32[]{:S(2)}, u32[]{:S(2)}) %collective-permute-start.6) | collective-permute-done | bytes 524320 | tf_op jit(solution)/shard_map/ppermute | solution.py:779
  81.2 2.9 %collective-permute-start.7 = (bf16[64,4096]{1,0:T(8,128)(2,1)S(1)}, bf16[64,4096]{1,0:T(8,128)(2,1)S(1)}, u32[]{:S(2)}, u32[]{:S(2)}) collective-permute-start(bf16[64,4096]{1,0:T(8,128)(2,1)S(1)} %copy-done.5), channel_id=1, source_target_pairs={{4,0},{5,1},{6,2},{7,3},{8,12},{9,13},{10,14},{11,15},{20,16},{21,... | collective-permute-start | bytes 1572872 | tf_op jit(solution)/shard_map/ppermute | solution.py:779
  84.2 2.0 %reduce_own.1 = (f32[128,128]{1,0:T(8,128)S(1)}, f32[256,128]{1,0:T(8,128)S(1)}) custom-call(bf16[128,4224]{1,0:T(8,128)(2,1)S(1)} %copy-done.1, bf16[128,4224]{1,0:T(8,128)(2,1)S(1)} %collective-permute-done.1.refs_1_.refs_4_, bf16[128,4096]{1,0:T(8,128)(2,1)S(1)} %collective-permute-done.refs_2_.refs_5_, ...), custom_call_target="tpu_custom_call" | custom-call | flops 1 | bytes 1 | tf_op jit(solution)/shard_map/reduce_own/pallas_call | solution.py:554
  88.9 2.0 %collective-permute-done.13.refs_6_ = bf16[64,4096]{1,0:T(8,128)(2,1)S(1)} collective-permute-done((bf16[64,4096]{1,0:T(8,128)(2,1)S(1)}, bf16[64,4096]{1,0:T(8,128)(2,1)S(1)}, u32[]{:S(2)}, u32[]{:S(2)}) %collective-permute-start.13) | collective-permute-done | bytes 524320 | tf_op jit(solution)/shard_map/ppermute | solution.py:779
  90.8 1.6 %collective-permute-start.12 = (bf16[64,1024]{1,0:T(8,128)(2,1)S(1)}, bf16[64,1024]{1,0:T(8,128)(2,1)S(1)}, u32[]{:S(2)}, u32[]{:S(2)}) collective-permute-start(bf16[64,1024]{1,0:T(8,128)(2,1)S(1)} %get-tuple-element.121), channel_id=1, source_target_pairs={{0,2},{2,0},{4,6},{6,4},{8,10},{10,8},{12,14},{14,12},{1,3},{3,1},... | collective-permute-start | bytes 393224 | tf_op jit(solution)/shard_map/ppermute | solution.py:763
  92.5 2.6 %collective-permute-done.14.refs_12_.refs_11_.refs_8_ = bf16[64,4224]{1,0:T(8,128)(2,1)S(1)} collective-permute-done((bf16[64,4224]{1,0:T(8,128)(2,1)S(1)}, bf16[64,4224]{1,0:T(8,128)(2,1)S(1)}, u32[]{:S(2)}, u32[]{:S(2)}) %collective-permute-start.14) | collective-permute-done | bytes 540704 | tf_op jit(solution)/shard_map/ppermute | solution.py:779
  95.1 3.4 %collective-permute-start.19 = (bf16[64,1024]{1,0:T(8,128)(2,1)S(1)}, bf16[64,1024]{1,0:T(8,128)(2,1)S(1)}, u32[]{:S(2)}, u32[]{:S(2)}) collective-permute-start(bf16[64,1024]{1,0:T(8,128)(2,1)S(1)} %get-tuple-element.139), channel_id=1, source_target_pairs={{0,4},{2,6},{4,0},{6,2},{8,12},{10,14},{12,8},{14,10},{1,5},{3,7},... | collective-permute-start | bytes 393224 | tf_op jit(solution)/shard_map/ppermute | solution.py:763
  98.4 2.7 %reduce_taken.1 = (f32[64,128]{1,0:T(8,128)S(1)}, f32[64,128]{1,0:T(8,128)S(1)}, f32[256,128]{1,0:T(8,128)S(1)}) custom-call(bf16[128,4224]{1,0:T(8,128)(2,1)S(1)} %copy-done.1, bf16[128,4224]{1,0:T(8,128)(2,1)S(1)} %collective-permute-done.1.refs_1_.refs_4_, bf16[128,4096]{1,0:T(8,128)(2,1)S(1)} %collective-permute-done.refs_2_.refs_5_, ...), custom_call_target="tpu_custom_call" | custom-call | flops 1 | bytes 1 | tf_op jit(solution)/shard_map/reduce_taken/pallas_call | solution.py:554
  109.5 3.3 %collective-permute-start.22 = (bf16[64,1024]{1,0:T(8,128)(2,1)S(1)}, bf16[64,1024]{1,0:T(8,128)(2,1)S(1)}, u32[]{:S(2)}, u32[]{:S(2)}) collective-permute-start(bf16[64,1024]{1,0:T(8,128)(2,1)S(1)} %get-tuple-element.145), channel_id=1, source_target_pairs={{0,4},{2,6},{4,0},{6,2},{8,12},{10,14},{12,8},{14,10},{1,5},{3,7},... | collective-permute-start | bytes 393224 | tf_op jit(solution)/shard_map/ppermute | solution.py:763
  116.9 1.8 %collective-permute-done.23.refs_1_ = bf16[64,1024]{1,0:T(8,128)(2,1)S(1)} collective-permute-done((bf16[64,1024]{1,0:T(8,128)(2,1)S(1)}, bf16[64,1024]{1,0:T(8,128)(2,1)S(1)}, u32[]{:S(2)}, u32[]{:S(2)}) %collective-permute-start.23) | collective-permute-done | bytes 131104 | tf_op jit(solution)/shard_map/ppermute | solution.py:763
  (77 shorter events, 27.6 us)
Async XLA Ops:
  4.6 27.1 %collective-permute-start.1 = (bf16[128,4224]{1,0:T(8,128)(2,1)}, bf16[128,4224]{1,0:T(8,128)(2,1)S(1)}, u32[]{:S(2)}, u32[]{:S(2)}) collective-permute-start(bf16[128,4224]{1,0:T(8,128)(2,1)} %get-tuple-element.83), channel_id=1, source_target_pairs={{0,2},{2,0},{4,6},{6,4},{8,10},{10,8},{12,14},{14,12},{1,3},{3,1},... | collective-permute-start | bytes 3244040 | tf_op jit(solution)/shard_map/ppermute | solution.py:763
  7.6 27.3 %collective-permute-start = (bf16[128,4096]{1,0:T(8,128)(2,1)}, bf16[128,4096]{1,0:T(8,128)(2,1)S(1)}, u32[]{:S(2)}, u32[]{:S(2)}) collective-permute-start(bf16[128,4096]{1,0:T(8,128)(2,1)} %get-tuple-element.80), channel_id=1, source_target_pairs={{0,4},{1,5},{2,6},{3,7},{12,8},{13,9},{14,10},{15,11},{16,20},{17,... | collective-permute-start | bytes 3145736 | tf_op jit(solution)/shard_map/ppermute | solution.py:779
  9.1 48.0 %collective-permute-start.3 = (bf16[128,4096]{1,0:T(8,128)(2,1)}, bf16[128,4096]{1,0:T(8,128)(2,1)S(1)}, u32[]{:S(2)}, u32[]{:S(2)}) collective-permute-start(bf16[128,4096]{1,0:T(8,128)(2,1)} %get-tuple-element.93), channel_id=1, source_target_pairs={{0,6},{1,7},{2,4},{3,5},{12,10},{13,11},{14,8},{15,9},{16,22},{17,... | collective-permute-start | bytes 3145736 | tf_op jit(solution)/shard_map/ppermute | solution.py:779
  11.7 44.9 %collective-permute-start.4 = (bf16[128,128]{1,0:T(8,128)(2,1)}, bf16[128,128]{1,0:T(8,128)(2,1)S(1)}, u32[]{:S(2)}, u32[]{:S(2)}) collective-permute-start(bf16[128,128]{1,0:T(8,128)(2,1)} %get-tuple-element.94), channel_id=1, source_target_pairs={{0,4},{2,6},{4,0},{6,2},{8,12},{10,14},{12,8},{14,10},{1,5},{3,7},... | collective-permute-start | bytes 98312 | tf_op jit(solution)/shard_map/ppermute | solution.py:763
  12.2 45.0 %collective-permute-start.5 = (bf16[128,128]{1,0:T(8,128)(2,1)}, bf16[128,128]{1,0:T(8,128)(2,1)S(1)}, u32[]{:S(2)}, u32[]{:S(2)}) collective-permute-start(bf16[128,128]{1,0:T(8,128)(2,1)} %get-tuple-element.95), channel_id=1, source_target_pairs={{0,6},{2,4},{4,2},{6,0},{8,14},{10,12},{12,10},{14,8},{1,7},{3,5},... | collective-permute-start | bytes 98312 | tf_op jit(solution)/shard_map/ppermute | solution.py:763
  36.2 13.8 %collective-permute-start.2 = (bf16[64,4224]{1,0:T(8,128)(2,1)S(1)}, bf16[64,4224]{1,0:T(8,128)(2,1)S(1)}, u32[]{:S(2)}, u32[]{:S(2)}) collective-permute-start(bf16[64,4224]{1,0:T(8,128)(2,1)S(1)} %pad_maximum_fusion), channel_id=1, source_target_pairs={{0,16},{1,17},{2,18},{3,19},{12,28},{13,29},{14,30},{15,31},{16,0}... | collective-permute-start | bytes 1622024 | tf_op jit(solution)/shard_map/ppermute | solution.py:779
  49.9 18.6 %collective-permute-start.8 = (bf16[64,4096]{1,0:T(8,128)(2,1)S(1)}, bf16[64,4096]{1,0:T(8,128)(2,1)S(1)}, u32[]{:S(2)}, u32[]{:S(2)}) collective-permute-start(bf16[64,4096]{1,0:T(8,128)(2,1)S(1)} %copy-done.8), channel_id=1, source_target_pairs={{4,0},{5,1},{6,2},{7,3},{8,12},{9,13},{10,14},{11,15},{20,16},{21,... | collective-permute-start | bytes 1572872 | tf_op jit(solution)/shard_map/ppermute | solution.py:779
  51.8 29.4 %collective-permute-start.9 = (bf16[64,4224]{1,0:T(8,128)(2,1)S(1)}, bf16[64,4224]{1,0:T(8,128)(2,1)S(1)}, u32[]{:S(2)}, u32[]{:S(2)}) collective-permute-start(bf16[64,4224]{1,0:T(8,128)(2,1)S(1)} %pad_maximum_fusion.1), channel_id=1, source_target_pairs={{0,16},{1,17},{2,18},{3,19},{12,28},{13,29},{14,30},{15,31},{16,0}... | collective-permute-start | bytes 1622024 | tf_op jit(solution)/shard_map/ppermute | solution.py:779
  57.1 22.5 %collective-permute-start.6 = (bf16[64,4096]{1,0:T(8,128)(2,1)S(1)}, bf16[64,4096]{1,0:T(8,128)(2,1)S(1)}, u32[]{:S(2)}, u32[]{:S(2)}) collective-permute-start(bf16[64,4096]{1,0:T(8,128)(2,1)S(1)} %copy-done.7), channel_id=1, source_target_pairs={{4,2},{5,3},{6,0},{7,1},{8,14},{9,15},{10,12},{11,13},{20,18},{21,... | collective-permute-start | bytes 1572872 | tf_op jit(solution)/shard_map/ppermute | solution.py:779
  68.5 29.9 %collective-permute-start.15 = (f32[512,1024]{1,0:T(8,128)S(1)}, f32[512,1024]{1,0:T(8,128)S(1)}, u32[]{:S(2)}, u32[]{:S(2)}) collective-permute-start(f32[512,1024]{1,0:T(8,128)S(1)} %fusion.2), channel_id=1, source_target_pairs={{0,1},{1,0},{2,3},{3,2},{4,5},{5,4},{6,7},{7,6},{8,9},{9,8},{10,11... | collective-permute-start | bytes 6291464 | tf_op jit(solution)/shard_map/ppermute | solution.py:763
  68.7 15.5 %collective-permute-start.10 = (bf16[64,4224]{1,0:T(8,128)(2,1)S(1)}, bf16[64,4224]{1,0:T(8,128)(2,1)S(1)}, u32[]{:S(2)}, u32[]{:S(2)}) collective-permute-start(bf16[64,4224]{1,0:T(8,128)(2,1)S(1)} %pad_maximum_fusion.2), channel_id=1, source_target_pairs={{0,16},{1,17},{2,18},{3,19},{12,28},{13,29},{14,30},{15,31},{16,0}... | collective-permute-start | bytes 1622024 | tf_op jit(solution)/shard_map/ppermute | solution.py:779
  70.3 20.6 %collective-permute-start.13 = (bf16[64,4096]{1,0:T(8,128)(2,1)S(1)}, bf16[64,4096]{1,0:T(8,128)(2,1)S(1)}, u32[]{:S(2)}, u32[]{:S(2)}) collective-permute-start(bf16[64,4096]{1,0:T(8,128)(2,1)S(1)} %copy-done.6), channel_id=1, source_target_pairs={{4,2},{5,3},{6,0},{7,1},{8,14},{9,15},{10,12},{11,13},{20,18},{21,... | collective-permute-start | bytes 1572872 | tf_op jit(solution)/shard_map/ppermute | solution.py:779
  79.6 15.4 %collective-permute-start.14 = (bf16[64,4224]{1,0:T(8,128)(2,1)S(1)}, bf16[64,4224]{1,0:T(8,128)(2,1)S(1)}, u32[]{:S(2)}, u32[]{:S(2)}) collective-permute-start(bf16[64,4224]{1,0:T(8,128)(2,1)S(1)} %pad_maximum_fusion.3), channel_id=1, source_target_pairs={{0,16},{1,17},{2,18},{3,19},{12,28},{13,29},{14,30},{15,31},{16,0}... | collective-permute-start | bytes 1622024 | tf_op jit(solution)/shard_map/ppermute | solution.py:779
  81.2 21.0 %collective-permute-start.7 = (bf16[64,4096]{1,0:T(8,128)(2,1)S(1)}, bf16[64,4096]{1,0:T(8,128)(2,1)S(1)}, u32[]{:S(2)}, u32[]{:S(2)}) collective-permute-start(bf16[64,4096]{1,0:T(8,128)(2,1)S(1)} %copy-done.5), channel_id=1, source_target_pairs={{4,0},{5,1},{6,2},{7,3},{8,12},{9,13},{10,14},{11,15},{20,16},{21,... | collective-permute-start | bytes 1572872 | tf_op jit(solution)/shard_map/ppermute | solution.py:779
  86.2 1.3 %collective-permute-start.11 = (f32[128,128]{1,0:T(8,128)S(1)}, f32[128,128]{1,0:T(8,128)S(1)}, u32[]{:S(2)}, u32[]{:S(2)}) collective-permute-start(f32[128,128]{1,0:T(8,128)S(1)} %get-tuple-element.118.refs_0_), channel_id=1, source_target_pairs={{0,1},{1,0},{2,3},{3,2},{4,5},{5,4},{6,7},{7,6},{8,9},{9,8},{10,11... | collective-permute-start | bytes 196616 | tf_op jit(solution)/shard_map/ppermute | solution.py:763
  87.6 21.1 %collective-permute-start.21 = (bf16[48,4096]{1,0:T(8,128)(2,1)S(1)}, bf16[48,4096]{1,0:T(8,128)(2,1)S(1)}, u32[]{:S(2)}, u32[]{:S(2)}) collective-permute-start(bf16[48,4096]{1,0:T(8,128)(2,1)S(1)} %slice.54), channel_id=1, source_target_pairs={{4,20},{5,21},{6,22},{7,23},{8,24},{9,25},{10,26},{11,27},{20,4},{... | collective-permute-start | bytes 1179656 | tf_op jit(solution)/shard_map/ppermute | solution.py:779
  90.8 11.4 %collective-permute-start.12 = (bf16[64,1024]{1,0:T(8,128)(2,1)S(1)}, bf16[64,1024]{1,0:T(8,128)(2,1)S(1)}, u32[]{:S(2)}, u32[]{:S(2)}) collective-permute-start(bf16[64,1024]{1,0:T(8,128)(2,1)S(1)} %get-tuple-element.121), channel_id=1, source_target_pairs={{0,2},{2,0},{4,6},{6,4},{8,10},{10,8},{12,14},{14,12},{1,3},{3,1},... | collective-permute-start | bytes 393224 | tf_op jit(solution)/shard_map/ppermute | solution.py:763
  95.1 11.2 %collective-permute-start.19 = (bf16[64,1024]{1,0:T(8,128)(2,1)S(1)}, bf16[64,1024]{1,0:T(8,128)(2,1)S(1)}, u32[]{:S(2)}, u32[]{:S(2)}) collective-permute-start(bf16[64,1024]{1,0:T(8,128)(2,1)S(1)} %get-tuple-element.139), channel_id=1, source_target_pairs={{0,4},{2,6},{4,0},{6,2},{8,12},{10,14},{12,8},{14,10},{1,5},{3,7},... | collective-permute-start | bytes 393224 | tf_op jit(solution)/shard_map/ppermute | solution.py:763
  98.4 9.2 %collective-permute-start.20 = (bf16[64,1024]{1,0:T(8,128)(2,1)S(1)}, bf16[64,1024]{1,0:T(8,128)(2,1)S(1)}, u32[]{:S(2)}, u32[]{:S(2)}) collective-permute-start(bf16[64,1024]{1,0:T(8,128)(2,1)S(1)} %get-tuple-element.140), channel_id=1, source_target_pairs={{0,6},{2,4},{4,2},{6,0},{8,14},{10,12},{12,10},{14,8},{1,7},{3,5},... | collective-permute-start | bytes 393224 | tf_op jit(solution)/shard_map/ppermute | solution.py:763
  103.5 4.1 %collective-permute-start.16 = (f32[64,128]{1,0:T(8,128)S(1)}, f32[64,128]{1,0:T(8,128)S(1)}, u32[]{:S(2)}, u32[]{:S(2)}) collective-permute-start(f32[64,128]{1,0:T(8,128)S(1)} %get-tuple-element.141.refs_0_), channel_id=1, source_target_pairs={{0,1},{1,0},{2,3},{3,2},{4,5},{5,4},{6,7},{7,6},{8,9},{9,8},{10,11... | collective-permute-start | bytes 98312 | tf_op jit(solution)/shard_map/ppermute | solution.py:763
  104.7 3.9 %collective-permute-start.18 = (f32[64,128]{1,0:T(8,128)S(1)}, f32[64,128]{1,0:T(8,128)S(1)}, u32[]{:S(2)}, u32[]{:S(2)}) collective-permute-start(f32[64,128]{1,0:T(8,128)S(1)} %add.15.refs_2_), channel_id=1, source_target_pairs={{0,16},{16,0},{1,17},{17,1},{2,18},{18,2},{3,19},{19,3},{4,20},{20... | collective-permute-start | bytes 98312 | tf_op jit(solution)/shard_map/ppermute | solution.py:763
  109.5 7.4 %collective-permute-start.22 = (bf16[64,1024]{1,0:T(8,128)(2,1)S(1)}, bf16[64,1024]{1,0:T(8,128)(2,1)S(1)}, u32[]{:S(2)}, u32[]{:S(2)}) collective-permute-start(bf16[64,1024]{1,0:T(8,128)(2,1)S(1)} %get-tuple-element.145), channel_id=1, source_target_pairs={{0,4},{2,6},{4,0},{6,2},{8,12},{10,14},{12,8},{14,10},{1,5},{3,7},... | collective-permute-start | bytes 393224 | tf_op jit(solution)/shard_map/ppermute | solution.py:763
  112.9 5.9 %collective-permute-start.23 = (bf16[64,1024]{1,0:T(8,128)(2,1)S(1)}, bf16[64,1024]{1,0:T(8,128)(2,1)S(1)}, u32[]{:S(2)}, u32[]{:S(2)}) collective-permute-start(bf16[64,1024]{1,0:T(8,128)(2,1)S(1)} %get-tuple-element.146), channel_id=1, source_target_pairs={{0,6},{2,4},{4,2},{6,0},{8,14},{10,12},{12,10},{14,8},{1,7},{3,5},... | collective-permute-start | bytes 393224 | tf_op jit(solution)/shard_map/ppermute | solution.py:763
  112.9 7.1 %collective-permute-start.24 = (bf16[64,1024]{1,0:T(8,128)(2,1)S(1)}, bf16[64,1024]{1,0:T(8,128)(2,1)S(1)}, u32[]{:S(2)}, u32[]{:S(2)}) collective-permute-start(bf16[64,1024]{1,0:T(8,128)(2,1)S(1)} %get-tuple-element.148), channel_id=1, source_target_pairs={{0,2},{2,0},{4,6},{6,4},{8,10},{10,8},{12,14},{14,12},{1,3},{3,1},... | collective-permute-start | bytes 393224 | tf_op jit(solution)/shard_map/ppermute | solution.py:763
  (14 other events, 188.2 us)

commit v21 on v20

--- a/solution.py
+++ b/solution.py
@@ -734,9 +734,8 @@
         pl.when(seg >= 0)(copy.wait)
 
 
-def join(plan, seg_of, base, deltas, kind, before=None):
+def join(seg_of, base, deltas, order, name, before=None):
     height, features = base.shape
-    order = [kind * plan.half + d for d in plan.cross + plan.near]
     deltas = [deltas[i] for i in order]
     n = len(deltas)
     more = [] if before is None else [before]
@@ -754,7 +753,7 @@
         cost_estimate=pl.CostEstimate(
             flops=height * features, bytes_accessed=4 * height * features, transcendentals=0
         ),
-        name="join_taken" if more else "join_own",
+        name=name,
     )(seg_of, base, *deltas, *more)
 
 
@@ -887,8 +886,11 @@
     across_wide = [blocks[plan.left_pieces] for blocks in across]
     terms = expand_taken(plan, pairs, tag, wide_in, late_in[0], across_wide, across_up)
     deltas += [terms[0]] + return_terms(terms)
-    own = join(plan, seg_of, base, deltas, 0)
-    return join(plan, seg_of, base, deltas, 1, own)
+    own = [d for d in plan.cross + plan.near] + [half]
+    rows = join(seg_of, base, deltas, own, "join_own")
+    rows = join(seg_of, base, deltas, [half + d for d in plan.cross], "join_cross", rows)
+    last = [half + d for d in plan.near if d]
+    return join(seg_of, base, deltas, last, "join_near", rows)
 
 
 def solution(mesh):

time: 122 us -> 122 us (level)
    ppermute x14, waiting for transfers between devices: 24.9 us -> 23.7 us  [swap(): return lax.ppermute(value, axis, [(i, i ^ distance) for i in range(count)])]
    pallas_call x2 -> x3, Pallas kernels: 2.81 us -> 3.98 us  [join(): pl.pallas_call(functools.partial(join_kernel, order), out_shape=jax.Shape...]
  transfers between devices with their start and end apart: 25 -> 25, of which waited for: 16 -> 15; matrix products, arithmetic and copies ran while one was open for 12% -> 12% of each run, Pallas kernels for 10% -> 11%
where the time goes in v21:
time: 122 us; the launch traced here: 121 us
  waiting for transfers between devices  46.9 us (38%)
  starting transfers between devices  38.9 us (32%)
  Pallas kernels  20.5 us (17%)
  matrix products  12.1 us (10%)
  other arithmetic  1.79 us (1%)
    ppermute x14, waiting for transfers between devices, swap(): return lax.ppermute(value, axis, [(i, i ^ distance) for i in range(count)])  23.7 us
    ppermute x11, waiting for transfers between devices, send(): return lax.ppermute(value, ('groups', 'replica', 'tensor'), pairs)  23.2 us
    ppermute x11, starting transfers between devices, send(): return lax.ppermute(value, ('groups', 'replica', 'tensor'), pairs)  20.9 us
    ppermute x14, starting transfers between devices, swap(): return lax.ppermute(value, axis, [(i, i ^ distance) for i in range(count)])  18 us
    dot_general x2, matrix products, part(): return jnp.dot(rows, columns, preferred_element_type=jnp.float32)  12.1 us
    pallas_call x2, Pallas kernels, lay_out(): pl.pallas_call(functools.partial(lay_kernel, plan, first_call), out_shape...  9.09 us
    pallas_call x4, Pallas kernels, blocks_call(): pl.pallas_call(body, out_shape=out_shape, in_specs=[VMEM] * n_extra + [HB...  6.2 us
    pallas_call x3, Pallas kernels, join(): pl.pallas_call(functools.partial(join_kernel, order), out_shape=jax.Shape...  3.98 us
  transfers between devices with their start and end apart: 25, of which 15 were waited for; matrix products, arithmetic and copies ran while one was open for 12% of the time, Pallas kernels for 11%

profile of v21, /device:TPU:0, one launch (start us, length us, event | category | flops | bytes accessed | tf_op | source)
XLA Modules:
  0.0 121.5 jit_solution(2132294819524962271)
XLA Ops:
  0.0 4.6 %lay_out_first.1 = (bf16[128,4224]{1,0:T(8,128)(2,1)}, bf16[128,4096]{1,0:T(8,128)(2,1)}, bf16[128,4096]{1,0:T(8,128)(2,1)}, bf16[128,128]{1,0:T(8,128)(2,1)}, bf16[128,128]{1,0:T(8,128)(2,1)}, /*index=5*/s32[16]{0:T(128)}) custom-call(s32[16]{0:T(128)} %ids_ref.2, s32[48]{0:T(128)} %residency_ref.3, bf16[512,4096]{1,0:T(8,128)(2,1)} %x_ref.3, ...), custom_call_target="tpu_custom_call" | custom-call | bytes 2097152 | tf_op jit(solution)/shard_map/lay_out_first/pallas_call | solution.py:238
  4.6 3.0 %collective-permute-start.1 = (bf16[128,4224]{1,0:T(8,128)(2,1)}, bf16[128,4224]{1,0:T(8,128)(2,1)S(1)}, u32[]{:S(2)}, u32[]{:S(2)}) collective-permute-start(bf16[128,4224]{1,0:T(8,128)(2,1)} %get-tuple-element.83), channel_id=1, source_target_pairs={{0,2},{2,0},{4,6},{6,4},{8,10},{10,8},{12,14},{14,12},{1,3},{3,1},... | collective-permute-start | bytes 3244040 | tf_op jit(solution)/shard_map/ppermute | solution.py:762
  9.1 2.6 %collective-permute-start.3 = (bf16[128,4096]{1,0:T(8,128)(2,1)}, bf16[128,4096]{1,0:T(8,128)(2,1)S(1)}, u32[]{:S(2)}, u32[]{:S(2)}) collective-permute-start(bf16[128,4096]{1,0:T(8,128)(2,1)} %get-tuple-element.93), channel_id=1, source_target_pairs={{0,6},{1,7},{2,4},{3,5},{12,10},{13,11},{14,8},{15,9},{16,22},{17,... | collective-permute-start | bytes 3145736 | tf_op jit(solution)/shard_map/ppermute | solution.py:778
  12.2 2.5 %collective-permute-start.5 = (bf16[128,128]{1,0:T(8,128)(2,1)}, bf16[128,128]{1,0:T(8,128)(2,1)S(1)}, u32[]{:S(2)}, u32[]{:S(2)}) collective-permute-start(bf16[128,128]{1,0:T(8,128)(2,1)} %get-tuple-element.95), channel_id=1, source_target_pairs={{0,6},{2,4},{4,2},{6,0},{8,14},{10,12},{12,10},{14,8},{1,7},{3,5},... | collective-permute-start | bytes 98312 | tf_op jit(solution)/shard_map/ppermute | solution.py:762
  14.7 4.5 %lay_out_second.1 = (bf16[128,4224]{1,0:T(8,128)(2,1)}, bf16[64,4096]{1,0:T(8,128)(2,1)}, bf16[64,4096]{1,0:T(8,128)(2,1)}, bf16[64,4096]{1,0:T(8,128)(2,1)}, bf16[64,4096]{1,0:T(8,128)(2,1)}, /*index=5*/s32[16]{0:T(128)}) custom-call(s32[16]{0:T(128)} %ids_ref.2, s32[48]{0:T(128)} %residency_ref.3, bf16[512,4096]{1,0:T(8,128)(2,1)} %x_ref.3, ...), custom_call_target="tpu_custom_call" | custom-call | bytes 2097152 | tf_op jit(solution)/shard_map/lay_out_second/pallas_call | solution.py:238
  20.0 11.7 %collective-permute-done.1.refs_1_.refs_4_ = bf16[128,4224]{1,0:T(8,128)(2,1)S(1)} collective-permute-done((bf16[128,4224]{1,0:T(8,128)(2,1)}, bf16[128,4224]{1,0:T(8,128)(2,1)S(1)}, u32[]{:S(2)}, u32[]{:S(2)}) %collective-permute-start.1) | collective-permute-done | bytes 1081376 | tf_op jit(solution)/shard_map/ppermute | solution.py:762
  31.7 3.2 %collective-permute-done.refs_2_.refs_5_ = bf16[128,4096]{1,0:T(8,128)(2,1)S(1)} collective-permute-done((bf16[128,4096]{1,0:T(8,128)(2,1)}, bf16[128,4096]{1,0:T(8,128)(2,1)S(1)}, u32[]{:S(2)}, u32[]{:S(2)}) %collective-permute-start) | collective-permute-done | bytes 1048608 | tf_op jit(solution)/shard_map/ppermute | solution.py:778
  37.7 7.6 %fusion.2 = f32[512,1024]{1,0:T(8,128)S(1)} fusion(bf16[512,4096]{1,0:T(8,128)(2,1)S(1)} %copy-done.4, bf16[4096,2048]{1,0:T(8,128)(2,1)} %param.7, s32[]{:T(128)S(6)} %select_n.26), kind=kOutput, calls=%fused_computation.2 | convolution fusion | flops 4294967296 | bytes 14680068 | tf_op jit(solution)/shard_map/dot_general | solution.py:815
  45.4 4.5 %fusion = f32[512,1024]{1,0:T(8,128)S(1)} fusion(bf16[512,4096]{1,0:T(8,128)(2,1)S(1)} %copy-done.4, bf16[4096,2048]{1,0:T(8,128)(2,1)S(1)} %bitcast.11, s32[]{:T(128)S(6)} %select_n.27), kind=kOutput, calls=%fused_computation | convolution fusion | flops 4294967296 | bytes 14680068 | tf_op jit(solution)/shard_map/dot_general | solution.py:815
  49.9 1.8 %collective-permute-start.8 = (bf16[64,4096]{1,0:T(8,128)(2,1)S(1)}, bf16[64,4096]{1,0:T(8,128)(2,1)S(1)}, u32[]{:S(2)}, u32[]{:S(2)}) collective-permute-start(bf16[64,4096]{1,0:T(8,128)(2,1)S(1)} %copy-done.8), channel_id=1, source_target_pairs={{4,0},{5,1},{6,2},{7,3},{8,12},{9,13},{10,14},{11,15},{20,16},{21,... | collective-permute-start | bytes 1572872 | tf_op jit(solution)/shard_map/ppermute | solution.py:778
  52.4 4.2 %collective-permute-done.4.refs_6_.refs_7_ = bf16[128,128]{1,0:T(8,128)(2,1)S(1)} collective-permute-done((bf16[128,128]{1,0:T(8,128)(2,1)}, bf16[128,128]{1,0:T(8,128)(2,1)S(1)}, u32[]{:S(2)}, u32[]{:S(2)}) %collective-permute-start.4) | collective-permute-done | bytes 32800 | tf_op jit(solution)/shard_map/ppermute | solution.py:762
  57.1 3.1 %collective-permute-start.6 = (bf16[64,4096]{1,0:T(8,128)(2,1)S(1)}, bf16[64,4096]{1,0:T(8,128)(2,1)S(1)}, u32[]{:S(2)}, u32[]{:S(2)}) collective-permute-start(bf16[64,4096]{1,0:T(8,128)(2,1)S(1)} %copy-done.7), channel_id=1, source_target_pairs={{4,2},{5,3},{6,0},{7,1},{8,14},{9,15},{10,12},{11,13},{20,18},{21,... | collective-permute-start | bytes 1572872 | tf_op jit(solution)/shard_map/ppermute | solution.py:778
  60.3 8.3 %collective-permute-done.8.refs_4_.refs_7_ = bf16[64,4096]{1,0:T(8,128)(2,1)S(1)} collective-permute-done((bf16[64,4096]{1,0:T(8,128)(2,1)S(1)}, bf16[64,4096]{1,0:T(8,128)(2,1)S(1)}, u32[]{:S(2)}, u32[]{:S(2)}) %collective-permute-start.8) | collective-permute-done | bytes 524320 | tf_op jit(solution)/shard_map/ppermute | solution.py:778
  70.3 2.9 %collective-permute-start.13 = (bf16[64,4096]{1,0:T(8,128)(2,1)S(1)}, bf16[64,4096]{1,0:T(8,128)(2,1)S(1)}, u32[]{:S(2)}, u32[]{:S(2)}) collective-permute-start(bf16[64,4096]{1,0:T(8,128)(2,1)S(1)} %copy-done.6), channel_id=1, source_target_pairs={{4,2},{5,3},{6,0},{7,1},{8,14},{9,15},{10,12},{11,13},{20,18},{21,... | collective-permute-start | bytes 1572872 | tf_op jit(solution)/shard_map/ppermute | solution.py:778
  73.2 6.4 %collective-permute-done.6.refs_5_ = bf16[64,4096]{1,0:T(8,128)(2,1)S(1)} collective-permute-done((bf16[64,4096]{1,0:T(8,128)(2,1)S(1)}, bf16[64,4096]{1,0:T(8,128)(2,1)S(1)}, u32[]{:S(2)}, u32[]{:S(2)}) %collective-permute-start.6) | collective-permute-done | bytes 524320 | tf_op jit(solution)/shard_map/ppermute | solution.py:778
  81.2 2.9 %collective-permute-start.7 = (bf16[64,4096]{1,0:T(8,128)(2,1)S(1)}, bf16[64,4096]{1,0:T(8,128)(2,1)S(1)}, u32[]{:S(2)}, u32[]{:S(2)}) collective-permute-start(bf16[64,4096]{1,0:T(8,128)(2,1)S(1)} %copy-done.5), channel_id=1, source_target_pairs={{4,0},{5,1},{6,2},{7,3},{8,12},{9,13},{10,14},{11,15},{20,16},{21,... | collective-permute-start | bytes 1572872 | tf_op jit(solution)/shard_map/ppermute | solution.py:778
  84.2 2.0 %reduce_own.1 = (f32[128,128]{1,0:T(8,128)S(1)}, f32[256,128]{1,0:T(8,128)S(1)}) custom-call(bf16[128,4224]{1,0:T(8,128)(2,1)S(1)} %copy-done.1, bf16[128,4224]{1,0:T(8,128)(2,1)S(1)} %collective-permute-done.1.refs_1_.refs_4_, bf16[128,4096]{1,0:T(8,128)(2,1)S(1)} %collective-permute-done.refs_2_.refs_5_, ...), custom_call_target="tpu_custom_call" | custom-call | flops 1 | bytes 1 | tf_op jit(solution)/shard_map/reduce_own/pallas_call | solution.py:554
  88.9 2.0 %collective-permute-done.13.refs_6_ = bf16[64,4096]{1,0:T(8,128)(2,1)S(1)} collective-permute-done((bf16[64,4096]{1,0:T(8,128)(2,1)S(1)}, bf16[64,4096]{1,0:T(8,128)(2,1)S(1)}, u32[]{:S(2)}, u32[]{:S(2)}) %collective-permute-start.13) | collective-permute-done | bytes 524320 | tf_op jit(solution)/shard_map/ppermute | solution.py:778
  90.8 1.6 %collective-permute-start.12 = (bf16[64,1024]{1,0:T(8,128)(2,1)S(1)}, bf16[64,1024]{1,0:T(8,128)(2,1)S(1)}, u32[]{:S(2)}, u32[]{:S(2)}) collective-permute-start(bf16[64,1024]{1,0:T(8,128)(2,1)S(1)} %get-tuple-element.121), channel_id=1, source_target_pairs={{0,2},{2,0},{4,6},{6,4},{8,10},{10,8},{12,14},{14,12},{1,3},{3,1},... | collective-permute-start | bytes 393224 | tf_op jit(solution)/shard_map/ppermute | solution.py:762
  92.5 2.6 %collective-permute-done.14.refs_12_.refs_11_.refs_8_ = bf16[64,4224]{1,0:T(8,128)(2,1)S(1)} collective-permute-done((bf16[64,4224]{1,0:T(8,128)(2,1)S(1)}, bf16[64,4224]{1,0:T(8,128)(2,1)S(1)}, u32[]{:S(2)}, u32[]{:S(2)}) %collective-permute-start.14) | collective-permute-done | bytes 540704 | tf_op jit(solution)/shard_map/ppermute | solution.py:778
  95.1 3.4 %collective-permute-start.19 = (bf16[64,1024]{1,0:T(8,128)(2,1)S(1)}, bf16[64,1024]{1,0:T(8,128)(2,1)S(1)}, u32[]{:S(2)}, u32[]{:S(2)}) collective-permute-start(bf16[64,1024]{1,0:T(8,128)(2,1)S(1)} %get-tuple-element.139), channel_id=1, source_target_pairs={{0,4},{2,6},{4,0},{6,2},{8,12},{10,14},{12,8},{14,10},{1,5},{3,7},... | collective-permute-start | bytes 393224 | tf_op jit(solution)/shard_map/ppermute | solution.py:762
  98.4 2.7 %reduce_taken.1 = (f32[64,128]{1,0:T(8,128)S(1)}, f32[64,128]{1,0:T(8,128)S(1)}, f32[256,128]{1,0:T(8,128)S(1)}) custom-call(bf16[128,4224]{1,0:T(8,128)(2,1)S(1)} %copy-done.1, bf16[128,4224]{1,0:T(8,128)(2,1)S(1)} %collective-permute-done.1.refs_1_.refs_4_, bf16[128,4096]{1,0:T(8,128)(2,1)S(1)} %collective-permute-done.refs_2_.refs_5_, ...), custom_call_target="tpu_custom_call" | custom-call | flops 1 | bytes 1 | tf_op jit(solution)/shard_map/reduce_taken/pallas_call | solution.py:554
  109.5 3.3 %collective-permute-start.23 = (bf16[64,1024]{1,0:T(8,128)(2,1)S(1)}, bf16[64,1024]{1,0:T(8,128)(2,1)S(1)}, u32[]{:S(2)}, u32[]{:S(2)}) collective-permute-start(bf16[64,1024]{1,0:T(8,128)(2,1)S(1)} %get-tuple-element.146), channel_id=1, source_target_pairs={{0,4},{2,6},{4,0},{6,2},{8,12},{10,14},{12,8},{14,10},{1,5},{3,7},... | collective-permute-start | bytes 393224 | tf_op jit(solution)/shard_map/ppermute | solution.py:762
  116.9 1.8 %collective-permute-done.24.refs_1_ = bf16[64,1024]{1,0:T(8,128)(2,1)S(1)} collective-permute-done((bf16[64,1024]{1,0:T(8,128)(2,1)S(1)}, bf16[64,1024]{1,0:T(8,128)(2,1)S(1)}, u32[]{:S(2)}, u32[]{:S(2)}) %collective-permute-start.24) | collective-permute-done | bytes 131104 | tf_op jit(solution)/shard_map/ppermute | solution.py:762
  (78 shorter events, 27.6 us)
Async XLA Ops:
  4.6 27.1 %collective-permute-start.1 = (bf16[128,4224]{1,0:T(8,128)(2,1)}, bf16[128,4224]{1,0:T(8,128)(2,1)S(1)}, u32[]{:S(2)}, u32[]{:S(2)}) collective-permute-start(bf16[128,4224]{1,0:T(8,128)(2,1)} %get-tuple-element.83), channel_id=1, source_target_pairs={{0,2},{2,0},{4,6},{6,4},{8,10},{10,8},{12,14},{14,12},{1,3},{3,1},... | collective-permute-start | bytes 3244040 | tf_op jit(solution)/shard_map/ppermute | solution.py:762
  7.6 27.3 %collective-permute-start = (bf16[128,4096]{1,0:T(8,128)(2,1)}, bf16[128,4096]{1,0:T(8,128)(2,1)S(1)}, u32[]{:S(2)}, u32[]{:S(2)}) collective-permute-start(bf16[128,4096]{1,0:T(8,128)(2,1)} %get-tuple-element.80), channel_id=1, source_target_pairs={{0,4},{1,5},{2,6},{3,7},{12,8},{13,9},{14,10},{15,11},{16,20},{17,... | collective-permute-start | bytes 3145736 | tf_op jit(solution)/shard_map/ppermute | solution.py:778
  9.1 48.0 %collective-permute-start.3 = (bf16[128,4096]{1,0:T(8,128)(2,1)}, bf16[128,4096]{1,0:T(8,128)(2,1)S(1)}, u32[]{:S(2)}, u32[]{:S(2)}) collective-permute-start(bf16[128,4096]{1,0:T(8,128)(2,1)} %get-tuple-element.93), channel_id=1, source_target_pairs={{0,6},{1,7},{2,4},{3,5},{12,10},{13,11},{14,8},{15,9},{16,22},{17,... | collective-permute-start | bytes 3145736 | tf_op jit(solution)/shard_map/ppermute | solution.py:778
  11.7 44.9 %collective-permute-start.4 = (bf16[128,128]{1,0:T(8,128)(2,1)}, bf16[128,128]{1,0:T(8,128)(2,1)S(1)}, u32[]{:S(2)}, u32[]{:S(2)}) collective-permute-start(bf16[128,128]{1,0:T(8,128)(2,1)} %get-tuple-element.94), channel_id=1, source_target_pairs={{0,4},{2,6},{4,0},{6,2},{8,12},{10,14},{12,8},{14,10},{1,5},{3,7},... | collective-permute-start | bytes 98312 | tf_op jit(solution)/shard_map/ppermute | solution.py:762
  12.2 45.0 %collective-permute-start.5 = (bf16[128,128]{1,0:T(8,128)(2,1)}, bf16[128,128]{1,0:T(8,128)(2,1)S(1)}, u32[]{:S(2)}, u32[]{:S(2)}) collective-permute-start(bf16[128,128]{1,0:T(8,128)(2,1)} %get-tuple-element.95), channel_id=1, source_target_pairs={{0,6},{2,4},{4,2},{6,0},{8,14},{10,12},{12,10},{14,8},{1,7},{3,5},... | collective-permute-start | bytes 98312 | tf_op jit(solution)/shard_map/ppermute | solution.py:762
  36.2 13.8 %collective-permute-start.2 = (bf16[64,4224]{1,0:T(8,128)(2,1)S(1)}, bf16[64,4224]{1,0:T(8,128)(2,1)S(1)}, u32[]{:S(2)}, u32[]{:S(2)}) collective-permute-start(bf16[64,4224]{1,0:T(8,128)(2,1)S(1)} %pad_maximum_fusion), channel_id=1, source_target_pairs={{0,16},{1,17},{2,18},{3,19},{12,28},{13,29},{14,30},{15,31},{16,0}... | collective-permute-start | bytes 1622024 | tf_op jit(solution)/shard_map/ppermute | solution.py:778
  49.9 18.6 %collective-permute-start.8 = (bf16[64,4096]{1,0:T(8,128)(2,1)S(1)}, bf16[64,4096]{1,0:T(8,128)(2,1)S(1)}, u32[]{:S(2)}, u32[]{:S(2)}) collective-permute-start(bf16[64,4096]{1,0:T(8,128)(2,1)S(1)} %copy-done.8), channel_id=1, source_target_pairs={{4,0},{5,1},{6,2},{7,3},{8,12},{9,13},{10,14},{11,15},{20,16},{21,... | collective-permute-start | bytes 1572872 | tf_op jit(solution)/shard_map/ppermute | solution.py:778
  51.8 29.4 %collective-permute-start.9 = (bf16[64,4224]{1,0:T(8,128)(2,1)S(1)}, bf16[64,4224]{1,0:T(8,128)(2,1)S(1)}, u32[]{:S(2)}, u32[]{:S(2)}) collective-permute-start(bf16[64,4224]{1,0:T(8,128)(2,1)S(1)} %pad_maximum_fusion.1), channel_id=1, source_target_pairs={{0,16},{1,17},{2,18},{3,19},{12,28},{13,29},{14,30},{15,31},{16,0}... | collective-permute-start | bytes 1622024 | tf_op jit(solution)/shard_map/ppermute | solution.py:778
  57.1 22.5 %collective-permute-start.6 = (bf16[64,4096]{1,0:T(8,128)(2,1)S(1)}, bf16[64,4096]{1,0:T(8,128)(2,1)S(1)}, u32[]{:S(2)}, u32[]{:S(2)}) collective-permute-start(bf16[64,4096]{1,0:T(8,128)(2,1)S(1)} %copy-done.7), channel_id=1, source_target_pairs={{4,2},{5,3},{6,0},{7,1},{8,14},{9,15},{10,12},{11,13},{20,18},{21,... | collective-permute-start | bytes 1572872 | tf_op jit(solution)/shard_map/ppermute | solution.py:778
  68.5 29.9 %collective-permute-start.15 = (f32[512,1024]{1,0:T(8,128)S(1)}, f32[512,1024]{1,0:T(8,128)S(1)}, u32[]{:S(2)}, u32[]{:S(2)}) collective-permute-start(f32[512,1024]{1,0:T(8,128)S(1)} %fusion.2), channel_id=1, source_target_pairs={{0,1},{1,0},{2,3},{3,2},{4,5},{5,4},{6,7},{7,6},{8,9},{9,8},{10,11... | collective-permute-start | bytes 6291464 | tf_op jit(solution)/shard_map/ppermute | solution.py:762
  68.7 15.5 %collective-permute-start.10 = (bf16[64,4224]{1,0:T(8,128)(2,1)S(1)}, bf16[64,4224]{1,0:T(8,128)(2,1)S(1)}, u32[]{:S(2)}, u32[]{:S(2)}) collective-permute-start(bf16[64,4224]{1,0:T(8,128)(2,1)S(1)} %pad_maximum_fusion.2), channel_id=1, source_target_pairs={{0,16},{1,17},{2,18},{3,19},{12,28},{13,29},{14,30},{15,31},{16,0}... | collective-permute-start | bytes 1622024 | tf_op jit(solution)/shard_map/ppermute | solution.py:778
  70.3 20.6 %collective-permute-start.13 = (bf16[64,4096]{1,0:T(8,128)(2,1)S(1)}, bf16[64,4096]{1,0:T(8,128)(2,1)S(1)}, u32[]{:S(2)}, u32[]{:S(2)}) collective-permute-start(bf16[64,4096]{1,0:T(8,128)(2,1)S(1)} %copy-done.6), channel_id=1, source_target_pairs={{4,2},{5,3},{6,0},{7,1},{8,14},{9,15},{10,12},{11,13},{20,18},{21,... | collective-permute-start | bytes 1572872 | tf_op jit(solution)/shard_map/ppermute | solution.py:778
  79.6 15.4 %collective-permute-start.14 = (bf16[64,4224]{1,0:T(8,128)(2,1)S(1)}, bf16[64,4224]{1,0:T(8,128)(2,1)S(1)}, u32[]{:S(2)}, u32[]{:S(2)}) collective-permute-start(bf16[64,4224]{1,0:T(8,128)(2,1)S(1)} %pad_maximum_fusion.3), channel_id=1, source_target_pairs={{0,16},{1,17},{2,18},{3,19},{12,28},{13,29},{14,30},{15,31},{16,0}... | collective-permute-start | bytes 1622024 | tf_op jit(solution)/shard_map/ppermute | solution.py:778
  81.2 21.0 %collective-permute-start.7 = (bf16[64,4096]{1,0:T(8,128)(2,1)S(1)}, bf16[64,4096]{1,0:T(8,128)(2,1)S(1)}, u32[]{:S(2)}, u32[]{:S(2)}) collective-permute-start(bf16[64,4096]{1,0:T(8,128)(2,1)S(1)} %copy-done.5), channel_id=1, source_target_pairs={{4,0},{5,1},{6,2},{7,3},{8,12},{9,13},{10,14},{11,15},{20,16},{21,... | collective-permute-start | bytes 1572872 | tf_op jit(solution)/shard_map/ppermute | solution.py:778
  86.2 1.3 %collective-permute-start.11 = (f32[128,128]{1,0:T(8,128)S(1)}, f32[128,128]{1,0:T(8,128)S(1)}, u32[]{:S(2)}, u32[]{:S(2)}) collective-permute-start(f32[128,128]{1,0:T(8,128)S(1)} %get-tuple-element.118.refs_0_), channel_id=1, source_target_pairs={{0,1},{1,0},{2,3},{3,2},{4,5},{5,4},{6,7},{7,6},{8,9},{9,8},{10,11... | collective-permute-start | bytes 196616 | tf_op jit(solution)/shard_map/ppermute | solution.py:762
  87.6 21.1 %collective-permute-start.21 = (bf16[48,4096]{1,0:T(8,128)(2,1)S(1)}, bf16[48,4096]{1,0:T(8,128)(2,1)S(1)}, u32[]{:S(2)}, u32[]{:S(2)}) collective-permute-start(bf16[48,4096]{1,0:T(8,128)(2,1)S(1)} %slice.54), channel_id=1, source_target_pairs={{4,20},{5,21},{6,22},{7,23},{8,24},{9,25},{10,26},{11,27},{20,4},{... | collective-permute-start | bytes 1179656 | tf_op jit(solution)/shard_map/ppermute | solution.py:778
  90.8 11.4 %collective-permute-start.12 = (bf16[64,1024]{1,0:T(8,128)(2,1)S(1)}, bf16[64,1024]{1,0:T(8,128)(2,1)S(1)}, u32[]{:S(2)}, u32[]{:S(2)}) collective-permute-start(bf16[64,1024]{1,0:T(8,128)(2,1)S(1)} %get-tuple-element.121), channel_id=1, source_target_pairs={{0,2},{2,0},{4,6},{6,4},{8,10},{10,8},{12,14},{14,12},{1,3},{3,1},... | collective-permute-start | bytes 393224 | tf_op jit(solution)/shard_map/ppermute | solution.py:762
  95.1 11.2 %collective-permute-start.19 = (bf16[64,1024]{1,0:T(8,128)(2,1)S(1)}, bf16[64,1024]{1,0:T(8,128)(2,1)S(1)}, u32[]{:S(2)}, u32[]{:S(2)}) collective-permute-start(bf16[64,1024]{1,0:T(8,128)(2,1)S(1)} %get-tuple-element.139), channel_id=1, source_target_pairs={{0,4},{2,6},{4,0},{6,2},{8,12},{10,14},{12,8},{14,10},{1,5},{3,7},... | collective-permute-start | bytes 393224 | tf_op jit(solution)/shard_map/ppermute | solution.py:762
  98.4 9.2 %collective-permute-start.20 = (bf16[64,1024]{1,0:T(8,128)(2,1)S(1)}, bf16[64,1024]{1,0:T(8,128)(2,1)S(1)}, u32[]{:S(2)}, u32[]{:S(2)}) collective-permute-start(bf16[64,1024]{1,0:T(8,128)(2,1)S(1)} %get-tuple-element.140), channel_id=1, source_target_pairs={{0,6},{2,4},{4,2},{6,0},{8,14},{10,12},{12,10},{14,8},{1,7},{3,5},... | collective-permute-start | bytes 393224 | tf_op jit(solution)/shard_map/ppermute | solution.py:762
  103.5 4.1 %collective-permute-start.16 = (f32[64,128]{1,0:T(8,128)S(1)}, f32[64,128]{1,0:T(8,128)S(1)}, u32[]{:S(2)}, u32[]{:S(2)}) collective-permute-start(f32[64,128]{1,0:T(8,128)S(1)} %get-tuple-element.141.refs_0_), channel_id=1, source_target_pairs={{0,1},{1,0},{2,3},{3,2},{4,5},{5,4},{6,7},{7,6},{8,9},{9,8},{10,11... | collective-permute-start | bytes 98312 | tf_op jit(solution)/shard_map/ppermute | solution.py:762
  104.7 3.9 %collective-permute-start.18 = (f32[64,128]{1,0:T(8,128)S(1)}, f32[64,128]{1,0:T(8,128)S(1)}, u32[]{:S(2)}, u32[]{:S(2)}) collective-permute-start(f32[64,128]{1,0:T(8,128)S(1)} %add.15.refs_2_), channel_id=1, source_target_pairs={{0,16},{16,0},{1,17},{17,1},{2,18},{18,2},{3,19},{19,3},{4,20},{20... | collective-permute-start | bytes 98312 | tf_op jit(solution)/shard_map/ppermute | solution.py:762
  109.5 7.4 %collective-permute-start.23 = (bf16[64,1024]{1,0:T(8,128)(2,1)S(1)}, bf16[64,1024]{1,0:T(8,128)(2,1)S(1)}, u32[]{:S(2)}, u32[]{:S(2)}) collective-permute-start(bf16[64,1024]{1,0:T(8,128)(2,1)S(1)} %get-tuple-element.146), channel_id=1, source_target_pairs={{0,4},{2,6},{4,0},{6,2},{8,12},{10,14},{12,8},{14,10},{1,5},{3,7},... | collective-permute-start | bytes 393224 | tf_op jit(solution)/shard_map/ppermute | solution.py:762
  112.9 5.9 %collective-permute-start.24 = (bf16[64,1024]{1,0:T(8,128)(2,1)S(1)}, bf16[64,1024]{1,0:T(8,128)(2,1)S(1)}, u32[]{:S(2)}, u32[]{:S(2)}) collective-permute-start(bf16[64,1024]{1,0:T(8,128)(2,1)S(1)} %get-tuple-element.147), channel_id=1, source_target_pairs={{0,6},{2,4},{4,2},{6,0},{8,14},{10,12},{12,10},{14,8},{1,7},{3,5},... | collective-permute-start | bytes 393224 | tf_op jit(solution)/shard_map/ppermute | solution.py:762
  112.9 7.2 %collective-permute-start.22 = (bf16[64,1024]{1,0:T(8,128)(2,1)S(1)}, bf16[64,1024]{1,0:T(8,128)(2,1)S(1)}, u32[]{:S(2)}, u32[]{:S(2)}) collective-permute-start(bf16[64,1024]{1,0:T(8,128)(2,1)S(1)} %get-tuple-element.145), channel_id=1, source_target_pairs={{0,2},{2,0},{4,6},{6,4},{8,10},{10,8},{12,14},{14,12},{1,3},{3,1},... | collective-permute-start | bytes 393224 | tf_op jit(solution)/shard_map/ppermute | solution.py:762
  (14 other events, 188.2 us)

commit v22 on v21

--- a/solution.py
+++ b/solution.py
@@ -888,7 +888,7 @@
     deltas += [terms[0]] + return_terms(terms)
     own = [d for d in plan.cross + plan.near] + [half]
     rows = join(seg_of, base, deltas, own, "join_own")
-    rows = join(seg_of, base, deltas, [half + d for d in plan.cross], "join_cross", rows)
+    rows = join(seg_of, base, deltas, [half + d for d in plan.cross[::-1]], "join_cross", rows)
     last = [half + d for d in plan.near if d]
     return join(seg_of, base, deltas, last, "join_near", rows)
 

time: 122 us -> 121 us (level)
  no operation moved by 1% of the time
where the time goes in v22:
time: 121 us
  waiting for transfers between devices  46.5 us (38%)
  starting transfers between devices  38.8 us (32%)
  Pallas kernels  20.5 us (17%)
  matrix products  12.1 us (10%)
  other arithmetic  1.79 us (1%)
    ppermute x14, waiting for transfers between devices, swap(): return lax.ppermute(value, axis, [(i, i ^ distance) for i in range(count)])  23.3 us
    ppermute x11, waiting for transfers between devices, send(): return lax.ppermute(value, ('groups', 'replica', 'tensor'), pairs)  23.2 us
    ppermute x11, starting transfers between devices, send(): return lax.ppermute(value, ('groups', 'replica', 'tensor'), pairs)  20.9 us
    ppermute x14, starting transfers between devices, swap(): return lax.ppermute(value, axis, [(i, i ^ distance) for i in range(count)])  17.9 us
    dot_general x2, matrix products, part(): return jnp.dot(rows, columns, preferred_element_type=jnp.float32)  12.1 us
    pallas_call x2, Pallas kernels, lay_out(): pl.pallas_call(functools.partial(lay_kernel, plan, first_call), out_shape...  9.09 us
    pallas_call x4, Pallas kernels, blocks_call(): pl.pallas_call(body, out_shape=out_shape, in_specs=[VMEM] * n_extra + [HB...  6.2 us
    pallas_call x3, Pallas kernels, join(): pl.pallas_call(functools.partial(join_kernel, order), out_shape=jax.Shape...  3.98 us
  transfers between devices with their start and end apart: 25, of which 15 were waited for; matrix products, arithmetic and copies ran while one was open for 12% of the time, Pallas kernels for 11%

profile of v22, /device:TPU:0, one launch (start us, length us, event | category | flops | bytes accessed | tf_op | source)
XLA Modules:
  0.0 121.0 jit_solution(2467742231502222236)
XLA Ops:
  0.0 4.6 %lay_out_first.1 = (bf16[128,4224]{1,0:T(8,128)(2,1)}, bf16[128,4096]{1,0:T(8,128)(2,1)}, bf16[128,4096]{1,0:T(8,128)(2,1)}, bf16[128,128]{1,0:T(8,128)(2,1)}, bf16[128,128]{1,0:T(8,128)(2,1)}, /*index=5*/s32[16]{0:T(128)}) custom-call(s32[16]{0:T(128)} %ids_ref.2, s32[48]{0:T(128)} %residency_ref.3, bf16[512,4096]{1,0:T(8,128)(2,1)} %x_ref.3, ...), custom_call_target="tpu_custom_call" | custom-call | bytes 2097152 | tf_op jit(solution)/shard_map/lay_out_first/pallas_call | solution.py:238
  4.6 3.0 %collective-permute-start.1 = (bf16[128,4224]{1,0:T(8,128)(2,1)}, bf16[128,4224]{1,0:T(8,128)(2,1)S(1)}, u32[]{:S(2)}, u32[]{:S(2)}) collective-permute-start(bf16[128,4224]{1,0:T(8,128)(2,1)} %get-tuple-element.83), channel_id=1, source_target_pairs={{0,2},{2,0},{4,6},{6,4},{8,10},{10,8},{12,14},{14,12},{1,3},{3,1},... | collective-permute-start | bytes 3244040 | tf_op jit(solution)/shard_map/ppermute | solution.py:762
  9.1 2.6 %collective-permute-start.3 = (bf16[128,4096]{1,0:T(8,128)(2,1)}, bf16[128,4096]{1,0:T(8,128)(2,1)S(1)}, u32[]{:S(2)}, u32[]{:S(2)}) collective-permute-start(bf16[128,4096]{1,0:T(8,128)(2,1)} %get-tuple-element.93), channel_id=1, source_target_pairs={{0,6},{1,7},{2,4},{3,5},{12,10},{13,11},{14,8},{15,9},{16,22},{17,... | collective-permute-start | bytes 3145736 | tf_op jit(solution)/shard_map/ppermute | solution.py:778
  12.2 2.5 %collective-permute-start.5 = (bf16[128,128]{1,0:T(8,128)(2,1)}, bf16[128,128]{1,0:T(8,128)(2,1)S(1)}, u32[]{:S(2)}, u32[]{:S(2)}) collective-permute-start(bf16[128,128]{1,0:T(8,128)(2,1)} %get-tuple-element.95), channel_id=1, source_target_pairs={{0,6},{2,4},{4,2},{6,0},{8,14},{10,12},{12,10},{14,8},{1,7},{3,5},... | collective-permute-start | bytes 98312 | tf_op jit(solution)/shard_map/ppermute | solution.py:762
  14.7 4.5 %lay_out_second.1 = (bf16[128,4224]{1,0:T(8,128)(2,1)}, bf16[64,4096]{1,0:T(8,128)(2,1)}, bf16[64,4096]{1,0:T(8,128)(2,1)}, bf16[64,4096]{1,0:T(8,128)(2,1)}, bf16[64,4096]{1,0:T(8,128)(2,1)}, /*index=5*/s32[16]{0:T(128)}) custom-call(s32[16]{0:T(128)} %ids_ref.2, s32[48]{0:T(128)} %residency_ref.3, bf16[512,4096]{1,0:T(8,128)(2,1)} %x_ref.3, ...), custom_call_target="tpu_custom_call" | custom-call | bytes 2097152 | tf_op jit(solution)/shard_map/lay_out_second/pallas_call | solution.py:238
  20.0 11.7 %collective-permute-done.1.refs_1_.refs_4_ = bf16[128,4224]{1,0:T(8,128)(2,1)S(1)} collective-permute-done((bf16[128,4224]{1,0:T(8,128)(2,1)}, bf16[128,4224]{1,0:T(8,128)(2,1)S(1)}, u32[]{:S(2)}, u32[]{:S(2)}) %collective-permute-start.1) | collective-permute-done | bytes 1081376 | tf_op jit(solution)/shard_map/ppermute | solution.py:762
  31.7 3.2 %collective-permute-done.refs_2_.refs_5_ = bf16[128,4096]{1,0:T(8,128)(2,1)S(1)} collective-permute-done((bf16[128,4096]{1,0:T(8,128)(2,1)}, bf16[128,4096]{1,0:T(8,128)(2,1)S(1)}, u32[]{:S(2)}, u32[]{:S(2)}) %collective-permute-start) | collective-permute-done | bytes 1048608 | tf_op jit(solution)/shard_map/ppermute | solution.py:778
  37.7 7.6 %fusion.2 = f32[512,1024]{1,0:T(8,128)S(1)} fusion(bf16[512,4096]{1,0:T(8,128)(2,1)S(1)} %copy-done.4, bf16[4096,2048]{1,0:T(8,128)(2,1)} %param.7, s32[]{:T(128)S(6)} %select_n.26), kind=kOutput, calls=%fused_computation.2 | convolution fusion | flops 4294967296 | bytes 14680068 | tf_op jit(solution)/shard_map/dot_general | solution.py:815
  45.4 4.5 %fusion = f32[512,1024]{1,0:T(8,128)S(1)} fusion(bf16[512,4096]{1,0:T(8,128)(2,1)S(1)} %copy-done.4, bf16[4096,2048]{1,0:T(8,128)(2,1)S(1)} %bitcast.11, s32[]{:T(128)S(6)} %select_n.27), kind=kOutput, calls=%fused_computation | convolution fusion | flops 4294967296 | bytes 14680068 | tf_op jit(solution)/shard_map/dot_general | solution.py:815
  49.9 1.8 %collective-permute-start.8 = (bf16[64,4096]{1,0:T(8,128)(2,1)S(1)}, bf16[64,4096]{1,0:T(8,128)(2,1)S(1)}, u32[]{:S(2)}, u32[]{:S(2)}) collective-permute-start(bf16[64,4096]{1,0:T(8,128)(2,1)S(1)} %copy-done.8), channel_id=1, source_target_pairs={{4,0},{5,1},{6,2},{7,3},{8,12},{9,13},{10,14},{11,15},{20,16},{21,... | collective-permute-start | bytes 1572872 | tf_op jit(solution)/shard_map/ppermute | solution.py:778
  52.4 4.2 %collective-permute-done.4.refs_6_.refs_7_ = bf16[128,128]{1,0:T(8,128)(2,1)S(1)} collective-permute-done((bf16[128,128]{1,0:T(8,128)(2,1)}, bf16[128,128]{1,0:T(8,128)(2,1)S(1)}, u32[]{:S(2)}, u32[]{:S(2)}) %collective-permute-start.4) | collective-permute-done | bytes 32800 | tf_op jit(solution)/shard_map/ppermute | solution.py:762
  57.1 3.1 %collective-permute-start.6 = (bf16[64,4096]{1,0:T(8,128)(2,1)S(1)}, bf16[64,4096]{1,0:T(8,128)(2,1)S(1)}, u32[]{:S(2)}, u32[]{:S(2)}) collective-permute-start(bf16[64,4096]{1,0:T(8,128)(2,1)S(1)} %copy-done.7), channel_id=1, source_target_pairs={{4,2},{5,3},{6,0},{7,1},{8,14},{9,15},{10,12},{11,13},{20,18},{21,... | collective-permute-start | bytes 1572872 | tf_op jit(solution)/shard_map/ppermute | solution.py:778
  60.3 8.3 %collective-permute-done.8.refs_4_.refs_7_ = bf16[64,4096]{1,0:T(8,128)(2,1)S(1)} collective-permute-done((bf16[64,4096]{1,0:T(8,128)(2,1)S(1)}, bf16[64,4096]{1,0:T(8,128)(2,1)S(1)}, u32[]{:S(2)}, u32[]{:S(2)}) %collective-permute-start.8) | collective-permute-done | bytes 524320 | tf_op jit(solution)/shard_map/ppermute | solution.py:778
  70.3 2.9 %collective-permute-start.13 = (bf16[64,4096]{1,0:T(8,128)(2,1)S(1)}, bf16[64,4096]{1,0:T(8,128)(2,1)S(1)}, u32[]{:S(2)}, u32[]{:S(2)}) collective-permute-start(bf16[64,4096]{1,0:T(8,128)(2,1)S(1)} %copy-done.6), channel_id=1, source_target_pairs={{4,2},{5,3},{6,0},{7,1},{8,14},{9,15},{10,12},{11,13},{20,18},{21,... | collective-permute-start | bytes 1572872 | tf_op jit(solution)/shard_map/ppermute | solution.py:778
  73.2 6.4 %collective-permute-done.6.refs_5_ = bf16[64,4096]{1,0:T(8,128)(2,1)S(1)} collective-permute-done((bf16[64,4096]{1,0:T(8,128)(2,1)S(1)}, bf16[64,4096]{1,0:T(8,128)(2,1)S(1)}, u32[]{:S(2)}, u32[]{:S(2)}) %collective-permute-start.6) | collective-permute-done | bytes 524320 | tf_op jit(solution)/shard_map/ppermute | solution.py:778
  81.2 2.9 %collective-permute-start.7 = (bf16[64,4096]{1,0:T(8,128)(2,1)S(1)}, bf16[64,4096]{1,0:T(8,128)(2,1)S(1)}, u32[]{:S(2)}, u32[]{:S(2)}) collective-permute-start(bf16[64,4096]{1,0:T(8,128)(2,1)S(1)} %copy-done.5), channel_id=1, source_target_pairs={{4,0},{5,1},{6,2},{7,3},{8,12},{9,13},{10,14},{11,15},{20,16},{21,... | collective-permute-start | bytes 1572872 | tf_op jit(solution)/shard_map/ppermute | solution.py:778
  84.2 2.0 %reduce_own.1 = (f32[128,128]{1,0:T(8,128)S(1)}, f32[256,128]{1,0:T(8,128)S(1)}) custom-call(bf16[128,4224]{1,0:T(8,128)(2,1)S(1)} %copy-done.1, bf16[128,4224]{1,0:T(8,128)(2,1)S(1)} %collective-permute-done.1.refs_1_.refs_4_, bf16[128,4096]{1,0:T(8,128)(2,1)S(1)} %collective-permute-done.refs_2_.refs_5_, ...), custom_call_target="tpu_custom_call" | custom-call | flops 1 | bytes 1 | tf_op jit(solution)/shard_map/reduce_own/pallas_call | solution.py:554
  88.9 2.0 %collective-permute-done.13.refs_6_ = bf16[64,4096]{1,0:T(8,128)(2,1)S(1)} collective-permute-done((bf16[64,4096]{1,0:T(8,128)(2,1)S(1)}, bf16[64,4096]{1,0:T(8,128)(2,1)S(1)}, u32[]{:S(2)}, u32[]{:S(2)}) %collective-permute-start.13) | collective-permute-done | bytes 524320 | tf_op jit(solution)/shard_map/ppermute | solution.py:778
  90.8 1.6 %collective-permute-start.12 = (bf16[64,1024]{1,0:T(8,128)(2,1)S(1)}, bf16[64,1024]{1,0:T(8,128)(2,1)S(1)}, u32[]{:S(2)}, u32[]{:S(2)}) collective-permute-start(bf16[64,1024]{1,0:T(8,128)(2,1)S(1)} %get-tuple-element.121), channel_id=1, source_target_pairs={{0,2},{2,0},{4,6},{6,4},{8,10},{10,8},{12,14},{14,12},{1,3},{3,1},... | collective-permute-start | bytes 393224 | tf_op jit(solution)/shard_map/ppermute | solution.py:762
  92.5 2.6 %collective-permute-done.14.refs_12_.refs_11_.refs_8_ = bf16[64,4224]{1,0:T(8,128)(2,1)S(1)} collective-permute-done((bf16[64,4224]{1,0:T(8,128)(2,1)S(1)}, bf16[64,4224]{1,0:T(8,128)(2,1)S(1)}, u32[]{:S(2)}, u32[]{:S(2)}) %collective-permute-start.14) | collective-permute-done | bytes 540704 | tf_op jit(solution)/shard_map/ppermute | solution.py:778
  95.1 3.4 %collective-permute-start.19 = (bf16[64,1024]{1,0:T(8,128)(2,1)S(1)}, bf16[64,1024]{1,0:T(8,128)(2,1)S(1)}, u32[]{:S(2)}, u32[]{:S(2)}) collective-permute-start(bf16[64,1024]{1,0:T(8,128)(2,1)S(1)} %get-tuple-element.139), channel_id=1, source_target_pairs={{0,4},{2,6},{4,0},{6,2},{8,12},{10,14},{12,8},{14,10},{1,5},{3,7},... | collective-permute-start | bytes 393224 | tf_op jit(solution)/shard_map/ppermute | solution.py:762
  98.4 2.7 %reduce_taken.1 = (f32[64,128]{1,0:T(8,128)S(1)}, f32[64,128]{1,0:T(8,128)S(1)}, f32[256,128]{1,0:T(8,128)S(1)}) custom-call(bf16[128,4224]{1,0:T(8,128)(2,1)S(1)} %copy-done.1, bf16[128,4224]{1,0:T(8,128)(2,1)S(1)} %collective-permute-done.1.refs_1_.refs_4_, bf16[128,4096]{1,0:T(8,128)(2,1)S(1)} %collective-permute-done.refs_2_.refs_5_, ...), custom_call_target="tpu_custom_call" | custom-call | flops 1 | bytes 1 | tf_op jit(solution)/shard_map/reduce_taken/pallas_call | solution.py:554
  109.5 3.3 %collective-permute-start.23 = (bf16[64,1024]{1,0:T(8,128)(2,1)S(1)}, bf16[64,1024]{1,0:T(8,128)(2,1)S(1)}, u32[]{:S(2)}, u32[]{:S(2)}) collective-permute-start(bf16[64,1024]{1,0:T(8,128)(2,1)S(1)} %get-tuple-element.146), channel_id=1, source_target_pairs={{0,6},{2,4},{4,2},{6,0},{8,14},{10,12},{12,10},{14,8},{1,7},{3,5},... | collective-permute-start | bytes 393224 | tf_op jit(solution)/shard_map/ppermute | solution.py:762
  116.5 1.9 %collective-permute-done.24.refs_1_ = bf16[64,1024]{1,0:T(8,128)(2,1)S(1)} collective-permute-done((bf16[64,1024]{1,0:T(8,128)(2,1)S(1)}, bf16[64,1024]{1,0:T(8,128)(2,1)S(1)}, u32[]{:S(2)}, u32[]{:S(2)}) %collective-permute-start.24) | collective-permute-done | bytes 131104 | tf_op jit(solution)/shard_map/ppermute | solution.py:762
  (78 shorter events, 27.1 us)
Async XLA Ops:
  4.6 27.1 %collective-permute-start.1 = (bf16[128,4224]{1,0:T(8,128)(2,1)}, bf16[128,4224]{1,0:T(8,128)(2,1)S(1)}, u32[]{:S(2)}, u32[]{:S(2)}) collective-permute-start(bf16[128,4224]{1,0:T(8,128)(2,1)} %get-tuple-element.83), channel_id=1, source_target_pairs={{0,2},{2,0},{4,6},{6,4},{8,10},{10,8},{12,14},{14,12},{1,3},{3,1},... | collective-permute-start | bytes 3244040 | tf_op jit(solution)/shard_map/ppermute | solution.py:762
  7.6 27.3 %collective-permute-start = (bf16[128,4096]{1,0:T(8,128)(2,1)}, bf16[128,4096]{1,0:T(8,128)(2,1)S(1)}, u32[]{:S(2)}, u32[]{:S(2)}) collective-permute-start(bf16[128,4096]{1,0:T(8,128)(2,1)} %get-tuple-element.80), channel_id=1, source_target_pairs={{0,4},{1,5},{2,6},{3,7},{12,8},{13,9},{14,10},{15,11},{16,20},{17,... | collective-permute-start | bytes 3145736 | tf_op jit(solution)/shard_map/ppermute | solution.py:778
  9.1 48.0 %collective-permute-start.3 = (bf16[128,4096]{1,0:T(8,128)(2,1)}, bf16[128,4096]{1,0:T(8,128)(2,1)S(1)}, u32[]{:S(2)}, u32[]{:S(2)}) collective-permute-start(bf16[128,4096]{1,0:T(8,128)(2,1)} %get-tuple-element.93), channel_id=1, source_target_pairs={{0,6},{1,7},{2,4},{3,5},{12,10},{13,11},{14,8},{15,9},{16,22},{17,... | collective-permute-start | bytes 3145736 | tf_op jit(solution)/shard_map/ppermute | solution.py:778
  11.7 44.9 %collective-permute-start.4 = (bf16[128,128]{1,0:T(8,128)(2,1)}, bf16[128,128]{1,0:T(8,128)(2,1)S(1)}, u32[]{:S(2)}, u32[]{:S(2)}) collective-permute-start(bf16[128,128]{1,0:T(8,128)(2,1)} %get-tuple-element.94), channel_id=1, source_target_pairs={{0,4},{2,6},{4,0},{6,2},{8,12},{10,14},{12,8},{14,10},{1,5},{3,7},... | collective-permute-start | bytes 98312 | tf_op jit(solution)/shard_map/ppermute | solution.py:762
  12.2 45.0 %collective-permute-start.5 = (bf16[128,128]{1,0:T(8,128)(2,1)}, bf16[128,128]{1,0:T(8,128)(2,1)S(1)}, u32[]{:S(2)}, u32[]{:S(2)}) collective-permute-start(bf16[128,128]{1,0:T(8,128)(2,1)} %get-tuple-element.95), channel_id=1, source_target_pairs={{0,6},{2,4},{4,2},{6,0},{8,14},{10,12},{12,10},{14,8},{1,7},{3,5},... | collective-permute-start | bytes 98312 | tf_op jit(solution)/shard_map/ppermute | solution.py:762
  36.2 13.8 %collective-permute-start.2 = (bf16[64,4224]{1,0:T(8,128)(2,1)S(1)}, bf16[64,4224]{1,0:T(8,128)(2,1)S(1)}, u32[]{:S(2)}, u32[]{:S(2)}) collective-permute-start(bf16[64,4224]{1,0:T(8,128)(2,1)S(1)} %pad_maximum_fusion), channel_id=1, source_target_pairs={{0,16},{1,17},{2,18},{3,19},{12,28},{13,29},{14,30},{15,31},{16,0}... | collective-permute-start | bytes 1622024 | tf_op jit(solution)/shard_map/ppermute | solution.py:778
  49.9 18.6 %collective-permute-start.8 = (bf16[64,4096]{1,0:T(8,128)(2,1)S(1)}, bf16[64,4096]{1,0:T(8,128)(2,1)S(1)}, u32[]{:S(2)}, u32[]{:S(2)}) collective-permute-start(bf16[64,4096]{1,0:T(8,128)(2,1)S(1)} %copy-done.8), channel_id=1, source_target_pairs={{4,0},{5,1},{6,2},{7,3},{8,12},{9,13},{10,14},{11,15},{20,16},{21,... | collective-permute-start | bytes 1572872 | tf_op jit(solution)/shard_map/ppermute | solution.py:778
  51.8 29.4 %collective-permute-start.9 = (bf16[64,4224]{1,0:T(8,128)(2,1)S(1)}, bf16[64,4224]{1,0:T(8,128)(2,1)S(1)}, u32[]{:S(2)}, u32[]{:S(2)}) collective-permute-start(bf16[64,4224]{1,0:T(8,128)(2,1)S(1)} %pad_maximum_fusion.1), channel_id=1, source_target_pairs={{0,16},{1,17},{2,18},{3,19},{12,28},{13,29},{14,30},{15,31},{16,0}... | collective-permute-start | bytes 1622024 | tf_op jit(solution)/shard_map/ppermute | solution.py:778
  57.1 22.5 %collective-permute-start.6 = (bf16[64,4096]{1,0:T(8,128)(2,1)S(1)}, bf16[64,4096]{1,0:T(8,128)(2,1)S(1)}, u32[]{:S(2)}, u32[]{:S(2)}) collective-permute-start(bf16[64,4096]{1,0:T(8,128)(2,1)S(1)} %copy-done.7), channel_id=1, source_target_pairs={{4,2},{5,3},{6,0},{7,1},{8,14},{9,15},{10,12},{11,13},{20,18},{21,... | collective-permute-start | bytes 1572872 | tf_op jit(solution)/shard_map/ppermute | solution.py:778
  68.5 29.9 %collective-permute-start.15 = (f32[512,1024]{1,0:T(8,128)S(1)}, f32[512,1024]{1,0:T(8,128)S(1)}, u32[]{:S(2)}, u32[]{:S(2)}) collective-permute-start(f32[512,1024]{1,0:T(8,128)S(1)} %fusion.2), channel_id=1, source_target_pairs={{0,1},{1,0},{2,3},{3,2},{4,5},{5,4},{6,7},{7,6},{8,9},{9,8},{10,11... | collective-permute-start | bytes 6291464 | tf_op jit(solution)/shard_map/ppermute | solution.py:762
  68.7 15.5 %collective-permute-start.10 = (bf16[64,4224]{1,0:T(8,128)(2,1)S(1)}, bf16[64,4224]{1,0:T(8,128)(2,1)S(1)}, u32[]{:S(2)}, u32[]{:S(2)}) collective-permute-start(bf16[64,4224]{1,0:T(8,128)(2,1)S(1)} %pad_maximum_fusion.2), channel_id=1, source_target_pairs={{0,16},{1,17},{2,18},{3,19},{12,28},{13,29},{14,30},{15,31},{16,0}... | collective-permute-start | bytes 1622024 | tf_op jit(solution)/shard_map/ppermute | solution.py:778
  70.3 20.6 %collective-permute-start.13 = (bf16[64,4096]{1,0:T(8,128)(2,1)S(1)}, bf16[64,4096]{1,0:T(8,128)(2,1)S(1)}, u32[]{:S(2)}, u32[]{:S(2)}) collective-permute-start(bf16[64,4096]{1,0:T(8,128)(2,1)S(1)} %copy-done.6), channel_id=1, source_target_pairs={{4,2},{5,3},{6,0},{7,1},{8,14},{9,15},{10,12},{11,13},{20,18},{21,... | collective-permute-start | bytes 1572872 | tf_op jit(solution)/shard_map/ppermute | solution.py:778
  79.6 15.4 %collective-permute-start.14 = (bf16[64,4224]{1,0:T(8,128)(2,1)S(1)}, bf16[64,4224]{1,0:T(8,128)(2,1)S(1)}, u32[]{:S(2)}, u32[]{:S(2)}) collective-permute-start(bf16[64,4224]{1,0:T(8,128)(2,1)S(1)} %pad_maximum_fusion.3), channel_id=1, source_target_pairs={{0,16},{1,17},{2,18},{3,19},{12,28},{13,29},{14,30},{15,31},{16,0}... | collective-permute-start | bytes 1622024 | tf_op jit(solution)/shard_map/ppermute | solution.py:778
  81.2 21.0 %collective-permute-start.7 = (bf16[64,4096]{1,0:T(8,128)(2,1)S(1)}, bf16[64,4096]{1,0:T(8,128)(2,1)S(1)}, u32[]{:S(2)}, u32[]{:S(2)}) collective-permute-start(bf16[64,4096]{1,0:T(8,128)(2,1)S(1)} %copy-done.5), channel_id=1, source_target_pairs={{4,0},{5,1},{6,2},{7,3},{8,12},{9,13},{10,14},{11,15},{20,16},{21,... | collective-permute-start | bytes 1572872 | tf_op jit(solution)/shard_map/ppermute | solution.py:778
  86.2 1.3 %collective-permute-start.11 = (f32[128,128]{1,0:T(8,128)S(1)}, f32[128,128]{1,0:T(8,128)S(1)}, u32[]{:S(2)}, u32[]{:S(2)}) collective-permute-start(f32[128,128]{1,0:T(8,128)S(1)} %get-tuple-element.118.refs_0_), channel_id=1, source_target_pairs={{0,1},{1,0},{2,3},{3,2},{4,5},{5,4},{6,7},{7,6},{8,9},{9,8},{10,11... | collective-permute-start | bytes 196616 | tf_op jit(solution)/shard_map/ppermute | solution.py:762
  87.6 21.1 %collective-permute-start.21 = (bf16[48,4096]{1,0:T(8,128)(2,1)S(1)}, bf16[48,4096]{1,0:T(8,128)(2,1)S(1)}, u32[]{:S(2)}, u32[]{:S(2)}) collective-permute-start(bf16[48,4096]{1,0:T(8,128)(2,1)S(1)} %slice.54), channel_id=1, source_target_pairs={{4,20},{5,21},{6,22},{7,23},{8,24},{9,25},{10,26},{11,27},{20,4},{... | collective-permute-start | bytes 1179656 | tf_op jit(solution)/shard_map/ppermute | solution.py:778
  90.8 11.4 %collective-permute-start.12 = (bf16[64,1024]{1,0:T(8,128)(2,1)S(1)}, bf16[64,1024]{1,0:T(8,128)(2,1)S(1)}, u32[]{:S(2)}, u32[]{:S(2)}) collective-permute-start(bf16[64,1024]{1,0:T(8,128)(2,1)S(1)} %get-tuple-element.121), channel_id=1, source_target_pairs={{0,2},{2,0},{4,6},{6,4},{8,10},{10,8},{12,14},{14,12},{1,3},{3,1},... | collective-permute-start | bytes 393224 | tf_op jit(solution)/shard_map/ppermute | solution.py:762
  95.1 11.2 %collective-permute-start.19 = (bf16[64,1024]{1,0:T(8,128)(2,1)S(1)}, bf16[64,1024]{1,0:T(8,128)(2,1)S(1)}, u32[]{:S(2)}, u32[]{:S(2)}) collective-permute-start(bf16[64,1024]{1,0:T(8,128)(2,1)S(1)} %get-tuple-element.139), channel_id=1, source_target_pairs={{0,4},{2,6},{4,0},{6,2},{8,12},{10,14},{12,8},{14,10},{1,5},{3,7},... | collective-permute-start | bytes 393224 | tf_op jit(solution)/shard_map/ppermute | solution.py:762
  98.4 9.2 %collective-permute-start.20 = (bf16[64,1024]{1,0:T(8,128)(2,1)S(1)}, bf16[64,1024]{1,0:T(8,128)(2,1)S(1)}, u32[]{:S(2)}, u32[]{:S(2)}) collective-permute-start(bf16[64,1024]{1,0:T(8,128)(2,1)S(1)} %get-tuple-element.140), channel_id=1, source_target_pairs={{0,6},{2,4},{4,2},{6,0},{8,14},{10,12},{12,10},{14,8},{1,7},{3,5},... | collective-permute-start | bytes 393224 | tf_op jit(solution)/shard_map/ppermute | solution.py:762
  103.5 4.1 %collective-permute-start.16 = (f32[64,128]{1,0:T(8,128)S(1)}, f32[64,128]{1,0:T(8,128)S(1)}, u32[]{:S(2)}, u32[]{:S(2)}) collective-permute-start(f32[64,128]{1,0:T(8,128)S(1)} %get-tuple-element.141.refs_0_), channel_id=1, source_target_pairs={{0,1},{1,0},{2,3},{3,2},{4,5},{5,4},{6,7},{7,6},{8,9},{9,8},{10,11... | collective-permute-start | bytes 98312 | tf_op jit(solution)/shard_map/ppermute | solution.py:762
  104.7 3.9 %collective-permute-start.18 = (f32[64,128]{1,0:T(8,128)S(1)}, f32[64,128]{1,0:T(8,128)S(1)}, u32[]{:S(2)}, u32[]{:S(2)}) collective-permute-start(f32[64,128]{1,0:T(8,128)S(1)} %add.15.refs_2_), channel_id=1, source_target_pairs={{0,16},{16,0},{1,17},{17,1},{2,18},{18,2},{3,19},{19,3},{4,20},{20... | collective-permute-start | bytes 98312 | tf_op jit(solution)/shard_map/ppermute | solution.py:762
  109.5 6.9 %collective-permute-start.23 = (bf16[64,1024]{1,0:T(8,128)(2,1)S(1)}, bf16[64,1024]{1,0:T(8,128)(2,1)S(1)}, u32[]{:S(2)}, u32[]{:S(2)}) collective-permute-start(bf16[64,1024]{1,0:T(8,128)(2,1)S(1)} %get-tuple-element.146), channel_id=1, source_target_pairs={{0,6},{2,4},{4,2},{6,0},{8,14},{10,12},{12,10},{14,8},{1,7},{3,5},... | collective-permute-start | bytes 393224 | tf_op jit(solution)/shard_map/ppermute | solution.py:762
  112.8 5.5 %collective-permute-start.24 = (bf16[64,1024]{1,0:T(8,128)(2,1)S(1)}, bf16[64,1024]{1,0:T(8,128)(2,1)S(1)}, u32[]{:S(2)}, u32[]{:S(2)}) collective-permute-start(bf16[64,1024]{1,0:T(8,128)(2,1)S(1)} %get-tuple-element.147), channel_id=1, source_target_pairs={{0,4},{2,6},{4,0},{6,2},{8,12},{10,14},{12,8},{14,10},{1,5},{3,7},... | collective-permute-start | bytes 393224 | tf_op jit(solution)/shard_map/ppermute | solution.py:762
  112.9 6.7 %collective-permute-start.22 = (bf16[64,1024]{1,0:T(8,128)(2,1)S(1)}, bf16[64,1024]{1,0:T(8,128)(2,1)S(1)}, u32[]{:S(2)}, u32[]{:S(2)}) collective-permute-start(bf16[64,1024]{1,0:T(8,128)(2,1)S(1)} %get-tuple-element.145), channel_id=1, source_target_pairs={{0,2},{2,0},{4,6},{6,4},{8,10},{10,8},{12,14},{14,12},{1,3},{3,1},... | collective-permute-start | bytes 393224 | tf_op jit(solution)/shard_map/ppermute | solution.py:762
  (14 other events, 188.1 us)
